TPU v7x, 32 devices: a whole 2x2x4 slice. The times are simulated.
32 devices in a mesh: groups: 2 (over y), row: 4 (over z), col: 4 (over x, core).
Axes of the slice: x: 2, y: 2, z: 4, core: 2. Of those that a mesh axis runs over, the one named last changes fastest.
Arguments:
- tokens: bfloat16 [1280, 8192], P(('groups', 'col'), 'row'), parts along dimension 0, may hold values from -6 to 6
- lengths: int32 [8], P('groups'), parts along dimension 0, may hold values from 1 to 160, 320 in all
- gate_weight: bfloat16 [8192, 14336], P('col', 'row'), may hold values from -0.0625 to 0.0625
- up_weight: bfloat16 [8192, 14336], P('col', 'row'), may hold values from -0.0625 to 0.0625
- down_weight: bfloat16 [14336, 8192], P('col', 'row'), may hold values from -0.046875 to 0.046875
Outputs:
- mixed: bfloat16 [1280, 8192], P(('groups', 'col'), 'row'), parts along dimension 0
There are 2 independent parts, one for each index of `groups`. A program takes and returns all parts, laid end to end along the dimension named above; an argument that names none is the same for every part. Nothing has to cross between parts.
Inputs may be any that keep to these rules, and one draw needn't show every extreme that they name: `lengths`: each packed row uses 1 to 160 slots, all rows together half of the 640 slots, and some row uses all 160.
All inputs are finite; a program needn't handle non-finite values.
Results may differ from a plain program's by a relative error of at most 0.0042.
Values may be sent and summed in bfloat16 or wider, within the bound.
No kernel may reach another device: no remote copies, remote signals or barrier semaphores. Data moves between devices by JAX's collectives and lax.ppermute only.
A program may use at most 448 MiB of HBM per device.

v0:
```python
import jax
import jax.numpy as jnp
from jax import lax
from jax.sharding import PartitionSpec as P


def add_rows(whole, piece):
    return jnp.dot(whole, piece, preferred_element_type=jnp.float32)


def branch_of(source, gate_weight, up_weight, down_weight):
    whole = lax.all_gather(source, "row", axis=1, tiled=True)

    def add_one(piece):
        return add_rows(whole, piece)

    gate = add_one(lax.all_gather(gate_weight, "col", axis=0, tiled=True))
    up = add_one(lax.all_gather(up_weight, "col", axis=0, tiled=True))
    hidden = (jax.nn.silu(gate) * up).astype(jnp.bfloat16)
    hidden_all = lax.all_gather(hidden, "row", axis=1, tiled=True)
    return add_rows(hidden_all, lax.all_gather(down_weight, "col", axis=0, tiled=True))


def per_device(tokens, lengths, gate_weight, up_weight, down_weight):
    slot_count = tokens.shape[0]
    column = lax.axis_index("col")
    own_len = jnp.take(lengths, column)
    branch = branch_of(tokens, gate_weight, up_weight, down_weight)
    valid = jnp.arange(slot_count, dtype=jnp.int32) < own_len
    total = tokens.astype(jnp.float32) + branch
    return jnp.where(valid[:, None], total, jnp.float32(0.0)).astype(jnp.bfloat16)


def solution(mesh):
    in_specs = (
        P(("groups", "col"), "row"),
        P("groups"),
        P("col", "row"),
        P("col", "row"),
        P("col", "row"),
    )
    out_specs = P(("groups", "col"), "row")
    return jax.shard_map(
        per_device, mesh=mesh, in_specs=in_specs, out_specs=out_specs, check_vma=False
    )
```

profile of v0, /device:TPU:0, one launch (start us, length us, event | category | flops | bytes accessed | tf_op | source)
XLA Modules:
  0.0 1226.9 jit_solution(737999675746137176)
XLA Ops:
  6.5 0.0 all-gather.6.cloned.1.call-start
  6.5 0.7 all-gather.6.cloned.1.call-update
  7.3 0.0 all-gather.8.cloned.1.call-start
  7.3 0.7 all-gather.8.cloned.1.call-update
  8.0 0.0 all-gather.10.cloned.1.call-start
  8.1 0.7 all-gather.10.cloned.1.call-update
  8.7 0.0 all-gather.14.cloned.1.call-start
  8.8 0.5 all-gather.14.cloned.1.call-update
  9.3 0.0 all-gather.12.cloned.1.call-start
  9.4 57.1 %all-gather.6.cloned.1.call-done = bf16[160,8192]{1,0:T(8,128)(2,1)} async-done(((bf16[160,2048]{1,0:T(8,128)(2,1)}), bf16[160,8192]{1,0:T(8,128)(2,1)}) %all-gather.6.cloned.1.call-update) | async-done | bytes 2621456 | tf_op jit(solution)/shard_map/all_gather | solution.py:12
  66.4 0.0 copy-start.1
  66.4 346.4 %all-gather.8.cloned.1.call-done = bf16[8192,3584]{1,0:T(8,128)(2,1)} async-done(((bf16[2048,3584]{1,0:T(8,128)(2,1)}), bf16[8192,3584]{1,0:T(8,128)(2,1)}) %all-gather.8.cloned.1.call-update) | async-done | bytes 58720272 | tf_op jit(solution)/shard_map/all_gather | solution.py:17
  412.9 34.2 %fusion.3 = f32[160,3584]{1,0:T(8,128)} fusion(bf16[160,8192]{1,0:T(8,128)(2,1)} %all-gather.6.cloned.1.call-done, bf16[8192,3584]{1,0:T(8,128)(2,1)} %all-gather.8.cloned.1.call-done), kind=kOutput, calls=%fused_computation.6 | convolution fusion | flops 9395240960 | bytes 63635456 | tf_op jit(solution)/shard_map/dot_general | solution.py:8
  447.1 0.0 copy-start.2
  447.1 0.0 copy-start
  447.1 313.4 %all-gather.10.cloned.1.call-done = bf16[8192,3584]{1,0:T(8,128)(2,1)} async-done(((bf16[2048,3584]{1,0:T(8,128)(2,1)}), bf16[8192,3584]{1,0:T(8,128)(2,1)}) %all-gather.10.cloned.1.call-update) | async-done | bytes 58720272 | tf_op jit(solution)/shard_map/all_gather | solution.py:18
  760.5 0.0 copy-done.1
  760.5 33.1 %fusion = bf16[160,3584]{1,0:T(8,128)(2,1)} fusion(bf16[160,8192]{1,0:T(8,128)(2,1)S(1)} %copy-done.1, bf16[8192,3584]{1,0:T(8,128)(2,1)} %all-gather.10.cloned.1.call-done, f32[160,3584]{1,0:T(8,128)} %fusion.3), kind=kOutput, calls=%fused_computation.1 | convolution fusion | flops 9398681600 | bytes 64782336 | tf_op jit(solution)/shard_map/dot_general | solution.py:8
  793.6 0.0 all-gather.12.cloned.1.call-update
  793.6 0.0 copy-done.2
  793.6 0.6 dynamic-slice.2
  794.8 313.1 %all-gather.14.cloned.1.call-done = bf16[14336,2048]{1,0:T(8,128)(2,1)} async-done(((bf16[3584,2048]{1,0:T(8,128)(2,1)}), bf16[14336,2048]{1,0:T(8,128)(2,1)}) %all-gather.14.cloned.1.call-update) | async-done | bytes 58720272 | tf_op jit(solution)/shard_map/all_gather | solution.py:21
  1108.0 88.7 %all-gather.12.cloned.1.call-done = bf16[160,14336]{1,0:T(8,128)(2,1)} async-done(((bf16[160,3584]{1,0:T(8,128)(2,1)}), bf16[160,14336]{1,0:T(8,128)(2,1)}) %all-gather.12.cloned.1.call-update) | async-done | bytes 4587536 | tf_op jit(solution)/shard_map/all_gather | solution.py:20
  1196.7 0.0 copy-done
  1196.7 23.7 %fusion.2 = bf16[160,2048]{1,0:T(8,128)(2,1)} fusion(bf16[160,14336]{1,0:T(8,128)(2,1)} %all-gather.12.cloned.1.call-done, bf16[14336,2048]{1,0:T(8,128)(2,1)} %all-gather.14.cloned.1.call-done, bf16[160,2048]{1,0:T(8,128)(2,1)S(1)} %copy-done, pred[160]{0:T(512)(128)(4,1)S(1)} %iota_compare_fusion), kind=kOutput, calls=%fused_computation.4 | convolution fusion | flops 9396551680 | bytes 64618656 | tf_op jit(solution)/shard_map/dot_general | solution.py:8
  (1 shorter events, 0.0 us)
Async XLA Ops:
  6.5 59.9 %all-gather.6.cloned.1.call-start = ((), (), s32[]{:S(2)}) async-start(), calls=%async_computation | async-start | bytes 3276800 | tf_op jit(solution)/shard_map/all_gather | solution.py:12
  7.3 405.6 %all-gather.8.cloned.1.call-start = ((), (), s32[]{:S(2)}) async-start(), calls=%async_computation.1 | async-start | bytes 73400320 | tf_op jit(solution)/shard_map/all_gather | solution.py:17
  8.0 752.5 %all-gather.10.cloned.1.call-start = ((), (), s32[]{:S(2)}) async-start(), calls=%async_computation.2 | async-start | bytes 73400320 | tf_op jit(solution)/shard_map/all_gather | solution.py:18
  8.7 1099.2 %all-gather.14.cloned.1.call-start = ((), (), s32[]{:S(2)}) async-start(), calls=%async_computation.4 | async-start | bytes 73400320 | tf_op jit(solution)/shard_map/all_gather | solution.py:21
  9.3 1187.3 %all-gather.12.cloned.1.call-start = ((), (), s32[]{:S(2)}) async-start(), calls=%async_computation.3 | async-start | bytes 5734400 | tf_op jit(solution)/shard_map/all_gather | solution.py:20
  66.4 694.1 %copy-start.1 = (bf16[160,8192]{1,0:T(8,128)(2,1)S(1)}, bf16[160,8192]{1,0:T(8,128)(2,1)}, u32[]{:S(2)}) copy-start(bf16[160,8192]{1,0:T(8,128)(2,1)} %all-gather.6.cloned.1.call-done) | copy-start | bytes 7864324
  447.1 346.6 %copy-start.2 = (s32[4]{0:T(128)S(1)}, s32[4]{0:T(128)}, u32[]{:S(2)}) copy-start(s32[4]{0:T(128)} %param.6) | copy-start | bytes 52
  447.1 749.6 %copy-start = (bf16[160,2048]{1,0:T(8,128)(2,1)S(1)}, bf16[160,2048]{1,0:T(8,128)(2,1)}, u32[]{:S(2)}) copy-start(bf16[160,2048]{1,0:T(8,128)(2,1)} %param.5) | copy-start | bytes 1966084
Sparse Core Ops, SparseCore 0:
  8.9 57.4 all-gather.5
  68.0 344.8 all-gather.7
  414.4 345.9 all-gather.9
  761.9 345.9 all-gather.13
  1109.4 87.2 all-gather.11
where the time goes:
time: 1230 us
  waiting for transfers between devices  1120 us (91%)
  matrix products  91.1 us (7%)
  between operations  13.7 us (1%)
    all_gather x1, waiting for transfers between devices, branch_of(): gate = add_one(lax.all_gather(gate_weight, 'col', axis=0, tiled=True))  346 us
    all_gather x1, waiting for transfers between devices, branch_of(): up = add_one(lax.all_gather(up_weight, 'col', axis=0, tiled=True))  313 us
    all_gather x1, waiting for transfers between devices, branch_of(): lax.all_gather(down_weight, 'col', axis=0, tiled=True)  313 us
    dot_general x3, matrix products, add_rows(): return jnp.dot(whole, piece, preferred_element_type=jnp.float32)  91.1 us
    all_gather x1, waiting for transfers between devices, branch_of(): hidden_all = lax.all_gather(hidden, 'row', axis=1, tiled=True)  88.7 us
    all_gather x1, waiting for transfers between devices, branch_of(): whole = lax.all_gather(source, 'row', axis=1, tiled=True)  57.1 us
  transfers between devices with their start and end apart: 5, of which 5 were waited for; matrix products, arithmetic and copies ran while one was open for 6% of the time, Pallas kernels for 0%

commit v1 on v0

v1 whole, which is shorter than its diff:
```python
import jax
import jax.numpy as jnp
from jax import lax
from jax.sharding import PartitionSpec as P

UNIT_CHUNKS = 2


def dot(a, b):
    return jnp.dot(a, b, preferred_element_type=jnp.float32)


def flip(value, axis, bit):
    count = lax.axis_size(axis)
    return lax.ppermute(value, axis, [(i, i ^ bit) for i in range(count)])


def spread(piece, zh, zl, x, k):
    other = flip(piece, "row", 2)
    stay = zh == x
    keep = jnp.where(stay, piece, other)
    send = jnp.where(stay, other, piece)
    pair = jnp.concatenate([keep, flip(send, "col", 2)], axis=0)
    other = flip(pair, "row", 1)
    stay = zl == k
    keep = jnp.where(stay, pair, other)
    send = jnp.where(stay, other, pair)
    return jnp.concatenate([keep, flip(send, "col", 1)], axis=0)


def stationary(tokens, lengths, gate_weight, up_weight, down_weight):
    slots, width = tokens.shape
    units = gate_weight.shape[1]
    c = lax.axis_index("col")
    r = lax.axis_index("row")
    x, k, zh, zl = c // 2, c % 2, r // 2, r % 2
    quarter = slots // 2
    starts = jnp.cumsum(lengths) - lengths
    first = jnp.take(starts, jnp.stack([c, c ^ 1]))
    count = jnp.take(lengths, jnp.stack([c, c ^ 1]))

    slot = jnp.arange(slots, dtype=jnp.int32)
    place = jnp.where(slot[None] < count[:, None], slot[None] + first[:, None], -1)
    inside = jnp.arange(quarter, dtype=jnp.int32)
    mine = jnp.concatenate([inside + quarter * c, inside + quarter * (c ^ 2)])

    sibling = flip(tokens, "col", 1)
    both = jnp.concatenate([tokens, sibling], axis=0)
    pick = (mine[:, None] == place.reshape(-1)[None]).astype(jnp.bfloat16)
    picked = dot(pick, both).astype(jnp.bfloat16)
    own = picked[:quarter] + flip(picked[quarter:], "col", 2)
    full = spread(own, zh, zl, x, k)

    half = 2 * quarter
    step = units // UNIT_CHUNKS
    branch = jnp.zeros((2 * half, down_weight.shape[1]), jnp.float32)
    for i in range(UNIT_CHUNKS):
        part = slice(i * step, (i + 1) * step)
        sums = jnp.stack([dot(full, gate_weight[:, part]), dot(full, up_weight[:, part])])
        sums = sums[:, :half] + flip(sums[:, half:].astype(jnp.bfloat16), "col", 1)
        sums = sums[:, :quarter] + flip(sums[:, quarter:].astype(jnp.bfloat16), "col", 2)
        hidden = (jax.nn.silu(sums[0]) * sums[1]).astype(jnp.bfloat16)
        branch = branch + dot(spread(hidden, zh, zl, x, k), down_weight[part])

    total = branch[:half] + flip(branch[half:].astype(jnp.bfloat16), "col", 1)
    theirs = flip(total.astype(jnp.bfloat16), "col", 2)
    total = total + jnp.concatenate([theirs[quarter:], theirs[:quarter]], axis=0)
    put = place.reshape(-1)[:, None] == mine[None]
    moved = jnp.dot(put.astype(jnp.float32), total, precision=lax.Precision.HIGHEST)
    handled = jnp.any(put, axis=1)
    mixed = jnp.where(handled[:, None], both.astype(jnp.float32) + moved, 0.0).astype(jnp.bfloat16)
    return mixed[:slots] + flip(mixed[slots:], "col", 1)


def general(tokens, lengths, gate_weight, up_weight, down_weight):
    c = lax.axis_index("col")
    slots = tokens.shape[0]
    whole = lax.all_gather(tokens, "row", axis=1, tiled=True)
    whole = lax.all_gather(whole, "col", axis=0, tiled=True)
    depth = gate_weight.shape[0]
    block = lax.dynamic_slice_in_dim(whole, c * depth, depth, axis=1)

    def summed(a, b):
        return lax.psum_scatter(dot(a, b), "col", scatter_dimension=0, tiled=True)

    hidden = (jax.nn.silu(summed(block, gate_weight)) * summed(block, up_weight)).astype(jnp.bfloat16)
    hidden = lax.all_gather(hidden, "row", axis=1, tiled=True)
    hidden = lax.all_gather(hidden, "col", axis=0, tiled=True)
    depth = down_weight.shape[0]
    branch = summed(lax.dynamic_slice_in_dim(hidden, c * depth, depth, axis=1), down_weight)
    valid = jnp.arange(slots, dtype=jnp.int32) < jnp.take(lengths, c)
    total = tokens.astype(jnp.float32) + branch
    return jnp.where(valid[:, None], total, jnp.float32(0.0)).astype(jnp.bfloat16)


def solution(mesh):
    square = mesh.shape["row"] == 4 and mesh.shape["col"] == 4
    in_specs = (
        P(("groups", "col"), "row"),
        P("groups"),
        P("col", "row"),
        P("col", "row"),
        P("col", "row"),
    )
    out_specs = P(("groups", "col"), "row")
    return jax.shard_map(
        stationary if square else general,
        mesh=mesh, in_specs=in_specs, out_specs=out_specs, check_vma=False,
    )
```

time: 1230 us -> 181 us (0.15)
  waiting for transfers between devices: 1120 us -> 122 us
  matrix products: 91.1 us -> 24.1 us
  starting transfers between devices: 0.15 us -> 23.6 us
  between operations: 13.7 us -> 0.36 us
    all_gather x5 -> x0, waiting for transfers between devices: 1120 us -> none  [the longest x1 346 us: branch_of(): gate = add_one(lax.all_gather(gate_weight, 'col', axis=0, tiled=True))]
    ppermute x0 -> x21, waiting for transfers between devices: none -> 122 us  [flip(): return lax.ppermute(value, axis, [(i, i ^ bit) for i in range(count)])]
    dot_general x3 -> x8, matrix products: 91.1 us -> 24.1 us  [the longest x7 22.4 us: dot(): return jnp.dot(a, b, preferred_element_type=jnp.float32)]
    ppermute x0 -> x21, starting transfers between devices: none -> 23.6 us  [flip(): return lax.ppermute(value, axis, [(i, i ^ bit) for i in range(count)])]
  transfers between devices with their start and end apart: 5 -> 21, of which waited for: 5 -> 17; matrix products, arithmetic and copies ran while one was open for 6% -> 10% of each run, Pallas kernels for 0% -> 0%
where the time goes in v1:
time: 181 us
  waiting for transfers between devices  122 us (67%)
  matrix products  24.1 us (13%)
  starting transfers between devices  23.6 us (13%)
  other arithmetic  5.67 us (3%)
  local copies, waits for them, and re-layouts  5.03 us (3%)
    ppermute x21, waiting for transfers between devices, flip(): return lax.ppermute(value, axis, [(i, i ^ bit) for i in range(count)])  122 us
    ppermute x21, starting transfers between devices, flip(): return lax.ppermute(value, axis, [(i, i ^ bit) for i in range(count)])  23.6 us
    dot_general x7, matrix products, dot(): return jnp.dot(a, b, preferred_element_type=jnp.float32)  22.4 us
  transfers between devices with their start and end apart: 21, of which 17 were waited for; matrix products, arithmetic and copies ran while one was open for 10% of the time, Pallas kernels for 0%

profile of v1, /device:TPU:0, one launch (start us, length us, event | category | flops | bytes accessed | tf_op | source)
XLA Modules:
  0.0 180.6 jit_solution(13885626326987340712)
XLA Ops:
  0.0 0.5 collective-permute-start
  0.5 0.8 reduce-window.9
  1.4 0.7 bitcast_subtract_fusion
  2.0 1.3 gather_fusion
  3.3 0.6 gather_fusion.1
  4.1 0.1 select_n.109
  4.3 1.1 constant_dynamic-update-slice_fusion.1
  5.5 0.5 convolution_convert_fusion
  6.1 2.6 %collective-permute-start.1 = (bf16[80,2048]{1,0:T(8,128)(2,1)S(1)}, bf16[80,2048]{1,0:T(8,128)(2,1)S(1)}, u32[]{:S(2)}, u32[]{:S(2)}) collective-permute-start(bf16[80,2048]{1,0:T(8,128)(2,1)S(1)} %slice.114), channel_id=1, source_target_pairs={{0,2},{1,3},{2,0},{3,1},{4,6},{5,7},{6,4},{7,5},{8,10},{9,11},{10,... | collective-permute-start | bytes 983048 | tf_op jit(solution)/shard_map/ppermute | solution.py:15
  8.6 8.4 %collective-permute-done.1 = bf16[80,2048]{1,0:T(8,128)(2,1)S(1)} collective-permute-done((bf16[80,2048]{1,0:T(8,128)(2,1)S(1)}, bf16[80,2048]{1,0:T(8,128)(2,1)S(1)}, u32[]{:S(2)}, u32[]{:S(2)}) %collective-permute-start.1) | collective-permute-done | bytes 327712 | tf_op jit(solution)/shard_map/ppermute | solution.py:15
  17.1 2.9 %collective-permute-start.2 = (bf16[80,2048]{1,0:T(8,128)(2,1)S(1)}, bf16[80,2048]{1,0:T(8,128)(2,1)S(1)}, u32[]{:S(2)}, u32[]{:S(2)}) collective-permute-start(bf16[80,2048]{1,0:T(8,128)(2,1)S(1)} %slice_add_fusion.5), channel_id=1, source_target_pairs={{0,8},{4,12},{8,0},{12,4},{1,9},{5,13},{9,1},{13,5},{2,10},{6,14},... | collective-permute-start | bytes 983048 | tf_op jit(solution)/shard_map/ppermute | solution.py:15
  20.0 14.6 %collective-permute-done.2 = bf16[80,2048]{1,0:T(8,128)(2,1)S(1)} collective-permute-done((bf16[80,2048]{1,0:T(8,128)(2,1)S(1)}, bf16[80,2048]{1,0:T(8,128)(2,1)S(1)}, u32[]{:S(2)}, u32[]{:S(2)}) %collective-permute-start.2) | collective-permute-done | bytes 327712 | tf_op jit(solution)/shard_map/ppermute | solution.py:15
  34.6 1.6 collective-permute-start.3
  36.2 7.1 %collective-permute-done.3 = bf16[80,2048]{1,0:T(8,128)(2,1)S(1)} collective-permute-done((bf16[80,2048]{1,0:T(8,128)(2,1)S(1)}, bf16[80,2048]{1,0:T(8,128)(2,1)S(1)}, u32[]{:S(2)}, u32[]{:S(2)}) %collective-permute-start.3) | collective-permute-done | bytes 327712 | tf_op jit(solution)/shard_map/ppermute | solution.py:15
  43.4 1.7 collective-permute-start.4
  45.2 14.1 %collective-permute-done.4 = bf16[160,2048]{1,0:T(8,128)(2,1)S(1)} collective-permute-done((bf16[160,2048]{1,0:T(8,128)(2,1)S(1)}, bf16[160,2048]{1,0:T(8,128)(2,1)S(1)}, u32[]{:S(2)}, u32[]{:S(2)}) %collective-permute-start.4) | collective-permute-done | bytes 655392 | tf_op jit(solution)/shard_map/ppermute | solution.py:15
  59.2 0.2 broadcast_select_fusion.1
  59.6 2.1 %collective-permute-done.5 = bf16[160,2048]{1,0:T(8,128)(2,1)S(1)} collective-permute-done((bf16[160,2048]{1,0:T(8,128)(2,1)S(1)}, bf16[160,2048]{1,0:T(8,128)(2,1)S(1)}, u32[]{:S(2)}, u32[]{:S(2)}) %collective-permute-start.5) | collective-permute-done | bytes 655392 | tf_op jit(solution)/shard_map/ppermute | solution.py:15
  61.7 5.8 %fusion.21 = f32[1,320,1792]{2,1,0:T(8,128)S(1)} fusion(bf16[2048,3584]{1,0:T(8,128)(2,1)} %param.10, bf16[160,2048]{1,0:T(8,128)(2,1)S(1)} %collective-permute-done.5, bf16[160,2048]{1,0:T(8,128)(2,1)S(1)} %get-tuple-element.6), kind=kOutput, calls=%fused_computation.21 | convolution fusion | flops 2351431680 | bytes 10944512 | tf_op jit(solution)/shard_map/dot_general | solution.py:10
  67.4 1.5 copy-done
  68.9 2.6 %fusion.18 = f32[1,320,1792]{2,1,0:T(8,128)S(1)} fusion(bf16[2048,3584]{1,0:T(8,128)(2,1)S(1)} %copy-done, bf16[160,2048]{1,0:T(8,128)(2,1)S(1)} %collective-permute-done.5, bf16[160,2048]{1,0:T(8,128)(2,1)S(1)} %get-tuple-element.6), kind=kOutput, calls=%fused_computation.20 | convolution fusion | flops 2351431680 | bytes 10944512 | tf_op jit(solution)/shard_map/dot_general | solution.py:10
  71.6 0.1 fusion.31
  71.7 0.2 collective-permute-start.12
  71.9 2.6 %fusion.12 = f32[1,320,1792]{2,1,0:T(8,128)S(1)} fusion(bf16[2048,3584]{1,0:T(8,128)(2,1)S(1)} %copy-done, bf16[160,2048]{1,0:T(8,128)(2,1)S(1)} %collective-permute-done.5, bf16[160,2048]{1,0:T(8,128)(2,1)S(1)} %get-tuple-element.6), kind=kOutput, calls=%fused_computation.18 | convolution fusion | flops 2351431680 | bytes 10944512 | tf_op jit(solution)/shard_map/dot_general | solution.py:10
  74.5 5.7 %fusion.15 = f32[1,320,1792]{2,1,0:T(8,128)S(1)} fusion(bf16[2048,3584]{1,0:T(8,128)(2,1)} %param.10, bf16[160,2048]{1,0:T(8,128)(2,1)S(1)} %collective-permute-done.5, bf16[160,2048]{1,0:T(8,128)(2,1)S(1)} %get-tuple-element.6), kind=kOutput, calls=%fused_computation.19 | convolution fusion | flops 2351431680 | bytes 10944512 | tf_op jit(solution)/shard_map/dot_general | solution.py:10
  80.2 0.1 fusion.32
  80.3 0.4 collective-permute-start.6
  80.8 0.2 fusion.28
  81.0 1.5 collective-permute-start.13
  82.6 0.6 collective-permute-done.6
  83.2 0.2 fusion.30
  83.5 1.6 collective-permute-start.7
  85.1 11.8 %collective-permute-done.13 = bf16[2,80,1792]{2,1,0:T(8,128)(2,1)S(1)} collective-permute-done((bf16[2,80,1792]{2,1,0:T(8,128)(2,1)S(1)}, bf16[2,80,1792]{2,1,0:T(8,128)(2,1)S(1)}, u32[]{:S(2)}, u32[]{:S(2)}) %collective-permute-start.13) | collective-permute-done | bytes 573472 | tf_op jit(solution)/shard_map/ppermute | solution.py:15
  96.9 0.1 slice_add_fusion.1
  97.0 0.2 fusion.49
  97.2 3.5 %collective-permute-start.14 = (bf16[80,1792]{1,0:T(8,128)(2,1)S(1)}, bf16[80,1792]{1,0:T(8,128)(2,1)S(1)}, u32[]{:S(2)}, u32[]{:S(2)}) collective-permute-start(bf16[80,1792]{1,0:T(8,128)(2,1)S(1)} %fusion.49), channel_id=1, source_target_pairs={{0,8},{4,12},{8,0},{12,4},{1,9},{5,13},{9,1},{13,5},{2,10},{6,14},... | collective-permute-start | bytes 860168 | tf_op jit(solution)/shard_map/ppermute | solution.py:15
  100.7 7.7 %collective-permute-done.7 = bf16[2,80,1792]{2,1,0:T(8,128)(2,1)S(1)} collective-permute-done((bf16[2,80,1792]{2,1,0:T(8,128)(2,1)S(1)}, bf16[2,80,1792]{2,1,0:T(8,128)(2,1)S(1)}, u32[]{:S(2)}, u32[]{:S(2)}) %collective-permute-start.7) | collective-permute-done | bytes 573472 | tf_op jit(solution)/shard_map/ppermute | solution.py:15
  108.4 0.1 slice_add_fusion.2
  108.5 3.8 %collective-permute-done.14 = bf16[80,1792]{1,0:T(8,128)(2,1)S(1)} collective-permute-done((bf16[80,1792]{1,0:T(8,128)(2,1)S(1)}, bf16[80,1792]{1,0:T(8,128)(2,1)S(1)}, u32[]{:S(2)}, u32[]{:S(2)}) %collective-permute-start.14) | collective-permute-done | bytes 286752 | tf_op jit(solution)/shard_map/ppermute | solution.py:15
  112.3 0.2 broadcast_select_fusion.9
  112.5 1.6 collective-permute-start.15
  114.1 0.2 fusion.51
  114.4 5.6 %collective-permute-done.15 = bf16[80,1792]{1,0:T(8,128)(2,1)S(1)} collective-permute-done((bf16[80,1792]{1,0:T(8,128)(2,1)S(1)}, bf16[80,1792]{1,0:T(8,128)(2,1)S(1)}, u32[]{:S(2)}, u32[]{:S(2)}) %collective-permute-start.15) | collective-permute-done | bytes 286752 | tf_op jit(solution)/shard_map/ppermute | solution.py:15
  120.1 2.1 %collective-permute-start.16 = (bf16[160,1792]{1,0:T(8,128)(2,1)S(1)}, bf16[160,1792]{1,0:T(8,128)(2,1)S(1)}, u32[]{:S(2)}, u32[]{:S(2)}) collective-permute-start(bf16[160,1792]{1,0:T(8,128)(2,1)S(1)} %pad_maximum_fusion.5), channel_id=1, source_target_pairs={{0,4},{4,0},{8,12},{12,8},{1,5},{5,1},{9,13},{13,9},{2,6},{6,2},{1... | collective-permute-start | bytes 1720328 | tf_op jit(solution)/shard_map/ppermute | solution.py:15
  122.2 6.6 %collective-permute-done.8 = bf16[80,1792]{1,0:T(8,128)(2,1)S(1)} collective-permute-done((bf16[80,1792]{1,0:T(8,128)(2,1)S(1)}, bf16[80,1792]{1,0:T(8,128)(2,1)S(1)}, u32[]{:S(2)}, u32[]{:S(2)}) %collective-permute-start.8) | collective-permute-done | bytes 286752 | tf_op jit(solution)/shard_map/ppermute | solution.py:15
  128.7 0.4 broadcast_select_fusion.11
  129.1 0.5 collective-permute-start.9
  129.6 6.2 %collective-permute-done.9 = bf16[80,1792]{1,0:T(8,128)(2,1)S(1)} collective-permute-done((bf16[80,1792]{1,0:T(8,128)(2,1)S(1)}, bf16[80,1792]{1,0:T(8,128)(2,1)S(1)}, u32[]{:S(2)}, u32[]{:S(2)}) %collective-permute-start.9) | collective-permute-done | bytes 286752 | tf_op jit(solution)/shard_map/ppermute | solution.py:15
  135.9 0.5 collective-permute-start.10
  136.4 3.6 %collective-permute-done.16 = bf16[160,1792]{1,0:T(8,128)(2,1)S(1)} collective-permute-done((bf16[160,1792]{1,0:T(8,128)(2,1)S(1)}, bf16[160,1792]{1,0:T(8,128)(2,1)S(1)}, u32[]{:S(2)}, u32[]{:S(2)}) %collective-permute-start.16) | collective-permute-done | bytes 573472 | tf_op jit(solution)/shard_map/ppermute | solution.py:15
  139.9 0.2 broadcast_select_fusion.3
  140.2 10.4 %collective-permute-done.10 = bf16[160,1792]{1,0:T(8,128)(2,1)S(1)} collective-permute-done((bf16[160,1792]{1,0:T(8,128)(2,1)S(1)}, bf16[160,1792]{1,0:T(8,128)(2,1)S(1)}, u32[]{:S(2)}, u32[]{:S(2)}) %collective-permute-start.10) | collective-permute-done | bytes 573472 | tf_op jit(solution)/shard_map/ppermute | solution.py:15
  150.7 0.2 broadcast_select_fusion.5
  151.0 2.6 %fusion = f32[320,2048]{1,0:T(8,128)S(1)} fusion(bf16[3584,2048]{1,0:T(8,128)(2,1)S(1)} %bitcast.44, bf16[160,1792]{1,0:T(8,128)(2,1)S(1)} %collective-permute-done.17, bf16[160,1792]{1,0:T(8,128)(2,1)S(1)} %get-tuple-element.10), kind=kOutput, calls=%fused_computation.2 | convolution fusion | flops 2351104000 | bytes 11108352 | tf_op jit(solution)/shard_map/dot_general | solution.py:10
  153.6 2.6 %fusion.24 = f32[320,2048]{1,0:T(8,128)S(1)} fusion(f32[320,2048]{1,0:T(8,128)S(1)} %fusion, bf16[3584,2048]{1,0:T(8,128)(2,1)S(1)} %bitcast.44, bf16[160,1792]{1,0:T(8,128)(2,1)S(1)} %collective-permute-done.11, bf16[160,1792]{1,0:T(8,128)(2,1)S(1)} %get-tuple-element.8), kind=kOutput, calls=%fused_computation.22 | convolution fusion | flops 2351759360 | bytes 13729792 | tf_op jit(solution)/shard_map/dot_general | solution.py:10
  156.3 0.5 collective-permute-start.18
  156.8 1.7 collective-permute-done.18
  158.6 0.2 fusion.44
  158.7 1.6 collective-permute-start.19
  160.3 0.1 compare_reduce_fusion
  160.4 15.4 %collective-permute-done.19 = bf16[160,2048]{1,0:T(8,128)(2,1)S(1)} collective-permute-done((bf16[160,2048]{1,0:T(8,128)(2,1)S(1)}, bf16[160,2048]{1,0:T(8,128)(2,1)S(1)}, u32[]{:S(2)}, u32[]{:S(2)}) %collective-permute-start.19) | collective-permute-done | bytes 655392 | tf_op jit(solution)/shard_map/ppermute | solution.py:15
  175.9 1.6 select_convert_fusion
  177.6 2.1 %collective-permute-done.20 = bf16[160,2048]{1,0:T(8,128)(2,1)S(1)} collective-permute-done((bf16[160,2048]{1,0:T(8,128)(2,1)S(1)}, bf16[160,2048]{1,0:T(8,128)(2,1)S(1)}, u32[]{:S(2)}, u32[]{:S(2)}) %collective-permute-start.20) | collective-permute-done | bytes 655392 | tf_op jit(solution)/shard_map/ppermute | solution.py:15
  179.7 0.9 slice_add_fusion.4
  (37 shorter events, 1.3 us)
Async XLA Ops:
  0.0 5.4 %collective-permute-start = (bf16[160,2048]{1,0:T(8,128)(2,1)}, bf16[160,2048]{1,0:T(8,128)(2,1)S(1)}, u32[]{:S(2)}, u32[]{:S(2)}) collective-permute-start(bf16[160,2048]{1,0:T(8,128)(2,1)} %param.7), channel_id=1, source_target_pairs={{0,1},{1,0},{2,3},{3,2},{4,5},{5,4},{6,7},{7,6},{8,9},{9,8},{10,11... | collective-permute-start | bytes 1966088 | tf_op jit(solution)/shard_map/ppermute | solution.py:15
  6.1 10.9 %collective-permute-start.1 = (bf16[80,2048]{1,0:T(8,128)(2,1)S(1)}, bf16[80,2048]{1,0:T(8,128)(2,1)S(1)}, u32[]{:S(2)}, u32[]{:S(2)}) collective-permute-start(bf16[80,2048]{1,0:T(8,128)(2,1)S(1)} %slice.114), channel_id=1, source_target_pairs={{0,2},{1,3},{2,0},{3,1},{4,6},{5,7},{6,4},{7,5},{8,10},{9,11},{10,... | collective-permute-start | bytes 983048 | tf_op jit(solution)/shard_map/ppermute | solution.py:15
  17.1 17.5 %collective-permute-start.2 = (bf16[80,2048]{1,0:T(8,128)(2,1)S(1)}, bf16[80,2048]{1,0:T(8,128)(2,1)S(1)}, u32[]{:S(2)}, u32[]{:S(2)}) collective-permute-start(bf16[80,2048]{1,0:T(8,128)(2,1)S(1)} %slice_add_fusion.5), channel_id=1, source_target_pairs={{0,8},{4,12},{8,0},{12,4},{1,9},{5,13},{9,1},{13,5},{2,10},{6,14},... | collective-permute-start | bytes 983048 | tf_op jit(solution)/shard_map/ppermute | solution.py:15
  34.6 8.7 %collective-permute-start.3 = (bf16[80,2048]{1,0:T(8,128)(2,1)S(1)}, bf16[80,2048]{1,0:T(8,128)(2,1)S(1)}, u32[]{:S(2)}, u32[]{:S(2)}) collective-permute-start(bf16[80,2048]{1,0:T(8,128)(2,1)S(1)} %get-tuple-element.15), channel_id=1, source_target_pairs={{0,2},{1,3},{2,0},{3,1},{4,6},{5,7},{6,4},{7,5},{8,10},{9,11},{10,... | collective-permute-start | bytes 983048 | tf_op jit(solution)/shard_map/ppermute | solution.py:15
  43.4 15.8 %collective-permute-start.4 = (bf16[160,2048]{1,0:T(8,128)(2,1)S(1)}, bf16[160,2048]{1,0:T(8,128)(2,1)S(1)}, u32[]{:S(2)}, u32[]{:S(2)}) collective-permute-start(bf16[160,2048]{1,0:T(8,128)(2,1)S(1)} %pad_maximum_fusion.3), channel_id=1, source_target_pairs={{0,4},{4,0},{8,12},{12,8},{1,5},{5,1},{9,13},{13,9},{2,6},{6,2},{1... | collective-permute-start | bytes 1966088 | tf_op jit(solution)/shard_map/ppermute | solution.py:15
  59.5 2.2 %collective-permute-start.5 = (bf16[160,2048]{1,0:T(8,128)(2,1)S(1)}, bf16[160,2048]{1,0:T(8,128)(2,1)S(1)}, u32[]{:S(2)}, u32[]{:S(2)}) collective-permute-start(bf16[160,2048]{1,0:T(8,128)(2,1)S(1)} %get-tuple-element.7), channel_id=1, source_target_pairs={{0,1},{1,0},{2,3},{3,2},{4,5},{5,4},{6,7},{7,6},{8,9},{9,8},{10,11... | collective-permute-start | bytes 1966088 | tf_op jit(solution)/shard_map/ppermute | solution.py:15
  61.7 7.3 %copy-start = (bf16[2048,3584]{1,0:T(8,128)(2,1)S(1)}, bf16[2048,3584]{1,0:T(8,128)(2,1)}, u32[]{:S(2)}) copy-start(bf16[2048,3584]{1,0:T(8,128)(2,1)} %param.9) | copy-start | bytes 44040196
  71.7 9.1 %collective-permute-start.12 = (bf16[2,160,1792]{2,1,0:T(8,128)(2,1)S(1)}, bf16[2,160,1792]{2,1,0:T(8,128)(2,1)S(1)}, u32[]{:S(2)}, u32[]{:S(2)}) collective-permute-start(bf16[2,160,1792]{2,1,0:T(8,128)(2,1)S(1)} %fusion.31), channel_id=1, source_target_pairs={{0,1},{1,0},{2,3},{3,2},{4,5},{5,4},{6,7},{7,6},{8,9},{9,8},{10,11... | collective-permute-start | bytes 3440648 | tf_op jit(solution)/shard_map/ppermute | solution.py:15
  80.3 2.9 %collective-permute-start.6 = (bf16[2,160,1792]{2,1,0:T(8,128)(2,1)S(1)}, bf16[2,160,1792]{2,1,0:T(8,128)(2,1)S(1)}, u32[]{:S(2)}, u32[]{:S(2)}) collective-permute-start(bf16[2,160,1792]{2,1,0:T(8,128)(2,1)S(1)} %fusion.32), channel_id=1, source_target_pairs={{0,1},{1,0},{2,3},{3,2},{4,5},{5,4},{6,7},{7,6},{8,9},{9,8},{10,11... | collective-permute-start | bytes 3440648 | tf_op jit(solution)/shard_map/ppermute | solution.py:15
  81.0 15.9 %collective-permute-start.13 = (bf16[2,80,1792]{2,1,0:T(8,128)(2,1)S(1)}, bf16[2,80,1792]{2,1,0:T(8,128)(2,1)S(1)}, u32[]{:S(2)}, u32[]{:S(2)}) collective-permute-start(bf16[2,80,1792]{2,1,0:T(8,128)(2,1)S(1)} %slice.201), channel_id=1, source_target_pairs={{0,2},{1,3},{2,0},{3,1},{4,6},{5,7},{6,4},{7,5},{8,10},{9,11},{10,... | collective-permute-start | bytes 1720328 | tf_op jit(solution)/shard_map/ppermute | solution.py:15
  83.2 67.7 %slice-start = ((s8[14680064]{0:T(1024)(128)(4,1)}), s8[4194304]{0:T(1024)(128)(4,1)S(1)}, s32[]{:S(2)}) async-start(s8[14680064]{0:T(1024)(128)(4,1)} %bitcast.43), calls=%async_computation | async-start | bytes 8388608
  83.2 67.8 %slice-start.1 = ((s8[14680064]{0:T(1024)(128)(4,1)}), s8[4194304]{0:T(1024)(128)(4,1)S(1)}, s32[]{:S(2)}) async-start(s8[14680064]{0:T(1024)(128)(4,1)} %bitcast.43), calls=%async_computation.1 | async-start | bytes 8388608
  83.5 24.9 %collective-permute-start.7 = (bf16[2,80,1792]{2,1,0:T(8,128)(2,1)S(1)}, bf16[2,80,1792]{2,1,0:T(8,128)(2,1)S(1)}, u32[]{:S(2)}, u32[]{:S(2)}) collective-permute-start(bf16[2,80,1792]{2,1,0:T(8,128)(2,1)S(1)} %slice.202), channel_id=1, source_target_pairs={{0,2},{1,3},{2,0},{3,1},{4,6},{5,7},{6,4},{7,5},{8,10},{9,11},{10,... | collective-permute-start | bytes 1720328 | tf_op jit(solution)/shard_map/ppermute | solution.py:15
  97.2 53.8 %slice-start.2 = ((s8[14680064]{0:T(1024)(128)(4,1)}), s8[4194304]{0:T(1024)(128)(4,1)S(1)}, s32[]{:S(2)}) async-start(s8[14680064]{0:T(1024)(128)(4,1)} %bitcast.43), calls=%async_computation.2 | async-start | bytes 8388608
  97.2 15.0 %collective-permute-start.14 = (bf16[80,1792]{1,0:T(8,128)(2,1)S(1)}, bf16[80,1792]{1,0:T(8,128)(2,1)S(1)}, u32[]{:S(2)}, u32[]{:S(2)}) collective-permute-start(bf16[80,1792]{1,0:T(8,128)(2,1)S(1)} %fusion.49), channel_id=1, source_target_pairs={{0,8},{4,12},{8,0},{12,4},{1,9},{5,13},{9,1},{13,5},{2,10},{6,14},... | collective-permute-start | bytes 860168 | tf_op jit(solution)/shard_map/ppermute | solution.py:15
  112.5 7.5 %collective-permute-start.15 = (bf16[80,1792]{1,0:T(8,128)(2,1)S(1)}, bf16[80,1792]{1,0:T(8,128)(2,1)S(1)}, u32[]{:S(2)}, u32[]{:S(2)}) collective-permute-start(bf16[80,1792]{1,0:T(8,128)(2,1)S(1)} %get-tuple-element.19), channel_id=1, source_target_pairs={{0,2},{1,3},{2,0},{3,1},{4,6},{5,7},{6,4},{7,5},{8,10},{9,11},{10,... | collective-permute-start | bytes 860168 | tf_op jit(solution)/shard_map/ppermute | solution.py:15
  114.3 14.4 %collective-permute-start.8 = (bf16[80,1792]{1,0:T(8,128)(2,1)S(1)}, bf16[80,1792]{1,0:T(8,128)(2,1)S(1)}, u32[]{:S(2)}, u32[]{:S(2)}) collective-permute-start(bf16[80,1792]{1,0:T(8,128)(2,1)S(1)} %fusion.51), channel_id=1, source_target_pairs={{0,8},{4,12},{8,0},{12,4},{1,9},{5,13},{9,1},{13,5},{2,10},{6,14},... | collective-permute-start | bytes 860168 | tf_op jit(solution)/shard_map/ppermute | solution.py:15
  120.0 30.9 %slice-start.3 = ((s8[14680064]{0:T(1024)(128)(4,1)}), s8[2097152]{0:T(1024)(128)(4,1)S(1)}, s32[]{:S(2)}) async-start(s8[14680064]{0:T(1024)(128)(4,1)} %bitcast.43), calls=%async_computation.3 | async-start | bytes 4194304
  120.1 19.9 %collective-permute-start.16 = (bf16[160,1792]{1,0:T(8,128)(2,1)S(1)}, bf16[160,1792]{1,0:T(8,128)(2,1)S(1)}, u32[]{:S(2)}, u32[]{:S(2)}) collective-permute-start(bf16[160,1792]{1,0:T(8,128)(2,1)S(1)} %pad_maximum_fusion.5), channel_id=1, source_target_pairs={{0,4},{4,0},{8,12},{12,8},{1,5},{5,1},{9,13},{13,9},{2,6},{6,2},{1... | collective-permute-start | bytes 1720328 | tf_op jit(solution)/shard_map/ppermute | solution.py:15
  129.1 6.7 %collective-permute-start.9 = (bf16[80,1792]{1,0:T(8,128)(2,1)S(1)}, bf16[80,1792]{1,0:T(8,128)(2,1)S(1)}, u32[]{:S(2)}, u32[]{:S(2)}) collective-permute-start(bf16[80,1792]{1,0:T(8,128)(2,1)S(1)} %get-tuple-element.17), channel_id=1, source_target_pairs={{0,2},{1,3},{2,0},{3,1},{4,6},{5,7},{6,4},{7,5},{8,10},{9,11},{10,... | collective-permute-start | bytes 860168 | tf_op jit(solution)/shard_map/ppermute | solution.py:15
  135.9 14.8 %collective-permute-start.10 = (bf16[160,1792]{1,0:T(8,128)(2,1)S(1)}, bf16[160,1792]{1,0:T(8,128)(2,1)S(1)}, u32[]{:S(2)}, u32[]{:S(2)}) collective-permute-start(bf16[160,1792]{1,0:T(8,128)(2,1)S(1)} %pad_maximum_fusion.4), channel_id=1, source_target_pairs={{0,4},{4,0},{8,12},{12,8},{1,5},{5,1},{9,13},{13,9},{2,6},{6,2},{1... | collective-permute-start | bytes 1720328 | tf_op jit(solution)/shard_map/ppermute | solution.py:15
  140.1 10.8 %collective-permute-start.17 = (bf16[160,1792]{1,0:T(8,128)(2,1)S(1)}, bf16[160,1792]{1,0:T(8,128)(2,1)S(1)}, u32[]{:S(2)}, u32[]{:S(2)}) collective-permute-start(bf16[160,1792]{1,0:T(8,128)(2,1)S(1)} %get-tuple-element.11), channel_id=1, source_target_pairs={{0,1},{1,0},{2,3},{3,2},{4,5},{5,4},{6,7},{7,6},{8,9},{9,8},{10,11... | collective-permute-start | bytes 1720328 | tf_op jit(solution)/shard_map/ppermute | solution.py:15
  150.8 2.8 %collective-permute-start.11 = (bf16[160,1792]{1,0:T(8,128)(2,1)S(1)}, bf16[160,1792]{1,0:T(8,128)(2,1)S(1)}, u32[]{:S(2)}, u32[]{:S(2)}) collective-permute-start(bf16[160,1792]{1,0:T(8,128)(2,1)S(1)} %get-tuple-element.9), channel_id=1, source_target_pairs={{0,1},{1,0},{2,3},{3,2},{4,5},{5,4},{6,7},{7,6},{8,9},{9,8},{10,11... | collective-permute-start | bytes 1720328 | tf_op jit(solution)/shard_map/ppermute | solution.py:15
  156.3 2.3 %collective-permute-start.18 = (bf16[160,2048]{1,0:T(8,128)(2,1)S(1)}, bf16[160,2048]{1,0:T(8,128)(2,1)S(1)}, u32[]{:S(2)}, u32[]{:S(2)}) collective-permute-start(bf16[160,2048]{1,0:T(8,128)(2,1)S(1)} %slice.200), channel_id=1, source_target_pairs={{0,1},{1,0},{2,3},{3,2},{4,5},{5,4},{6,7},{7,6},{8,9},{9,8},{10,11... | collective-permute-start | bytes 1966088 | tf_op jit(solution)/shard_map/ppermute | solution.py:15
  158.7 17.1 %collective-permute-start.19 = (bf16[160,2048]{1,0:T(8,128)(2,1)S(1)}, bf16[160,2048]{1,0:T(8,128)(2,1)S(1)}, u32[]{:S(2)}, u32[]{:S(2)}) collective-permute-start(bf16[160,2048]{1,0:T(8,128)(2,1)S(1)} %fusion.44), channel_id=1, source_target_pairs={{0,2},{1,3},{2,0},{3,1},{4,6},{5,7},{6,4},{7,5},{8,10},{9,11},{10,... | collective-permute-start | bytes 1966088 | tf_op jit(solution)/shard_map/ppermute | solution.py:15
  177.5 2.2 %collective-permute-start.20 = (bf16[160,2048]{1,0:T(8,128)(2,1)S(1)}, bf16[160,2048]{1,0:T(8,128)(2,1)S(1)}, u32[]{:S(2)}, u32[]{:S(2)}) collective-permute-start(bf16[160,2048]{1,0:T(8,128)(2,1)S(1)} %slice.132), channel_id=1, source_target_pairs={{0,1},{1,0},{2,3},{3,2},{4,5},{5,4},{6,7},{7,6},{8,9},{9,8},{10,11... | collective-permute-start | bytes 1966088 | tf_op jit(solution)/shard_map/ppermute | solution.py:15

commit v2 on v1

--- a/solution.py
+++ b/solution.py
@@ -1,9 +1,13 @@
 import jax
 import jax.numpy as jnp
 from jax import lax
+from jax.experimental import pallas as pl
+from jax.experimental.pallas import tpu as pltpu
 from jax.sharding import PartitionSpec as P
 
 UNIT_CHUNKS = 2
+HALVES = 2
+TILE = 256
 
 
 def dot(a, b):
@@ -28,6 +32,37 @@
     return jnp.concatenate([keep, flip(send, "col", 1)], axis=0)
 
 
+def partial_sums_kernel(full_ref, gate_ref, up_ref, keep_ref, send_ref):
+    half = full_ref.shape[0] // 2
+    for i, weight_ref in enumerate((gate_ref, up_ref)):
+        sums = dot(full_ref[...], weight_ref[...])
+        keep_ref[i] = sums[:half]
+        send_ref[i] = sums[half:].astype(jnp.bfloat16)
+
+
+def partial_sums(full, gate_weight, up_weight, first, units):
+    rows, depth = full.shape
+    half = rows // 2
+    weight = pl.BlockSpec((depth, TILE), lambda j: (0, first // TILE + j))
+    out = pl.BlockSpec((2, half, TILE), lambda j: (0, 0, j))
+    return pl.pallas_call(
+        partial_sums_kernel,
+        grid=(units // TILE,),
+        in_specs=[pl.BlockSpec((rows, depth), lambda j: (0, 0)), weight, weight],
+        out_specs=[out, out],
+        out_shape=[
+            jax.ShapeDtypeStruct((2, half, units), jnp.float32),
+            jax.ShapeDtypeStruct((2, half, units), jnp.bfloat16),
+        ],
+        compiler_params=pltpu.CompilerParams(vmem_limit_bytes=24 * 2**20),
+        cost_estimate=pl.CostEstimate(
+            flops=4 * rows * depth * units,
+            bytes_accessed=4 * depth * units + 6 * rows * units,
+            transcendentals=0,
+        ),
+    )(full, gate_weight, up_weight)
+
+
 def stationary(tokens, lengths, gate_weight, up_weight, down_weight):
     slots, width = tokens.shape
     units = gate_weight.shape[1]
@@ -35,38 +70,50 @@
     r = lax.axis_index("row")
     x, k, zh, zl = c // 2, c % 2, r // 2, r % 2
     quarter = slots // 2
-    starts = jnp.cumsum(lengths) - lengths
-    first = jnp.take(starts, jnp.stack([c, c ^ 1]))
-    count = jnp.take(lengths, jnp.stack([c, c ^ 1]))
+    piece = quarter // HALVES
 
+    rows = jnp.arange(lengths.shape[0], dtype=jnp.int32)
     slot = jnp.arange(slots, dtype=jnp.int32)
-    place = jnp.where(slot[None] < count[:, None], slot[None] + first[:, None], -1)
-    inside = jnp.arange(quarter, dtype=jnp.int32)
-    mine = jnp.concatenate([inside + quarter * c, inside + quarter * (c ^ 2)])
+    places = []
+    for row in (c, c ^ 1):
+        first = jnp.sum(jnp.where(rows < row, lengths, 0))
+        count = jnp.sum(jnp.where(rows == row, lengths, 0))
+        places.append(jnp.where(slot < count, slot + first, -1))
+    place = jnp.concatenate(places)
+    inside = jnp.arange(piece, dtype=jnp.int32)
+    mine = [
+        jnp.concatenate([inside + quarter * c, inside + quarter * (c ^ 2)]) + h * piece
+        for h in range(HALVES)
+    ]
 
-    sibling = flip(tokens, "col", 1)
-    both = jnp.concatenate([tokens, sibling], axis=0)
-    pick = (mine[:, None] == place.reshape(-1)[None]).astype(jnp.bfloat16)
-    picked = dot(pick, both).astype(jnp.bfloat16)
-    own = picked[:quarter] + flip(picked[quarter:], "col", 2)
-    full = spread(own, zh, zl, x, k)
+    both = jnp.concatenate([tokens, flip(tokens, "col", 1)], axis=0)
+    half = 2 * piece
+    step = units // UNIT_CHUNKS
+    totals = []
+    fulls = []
+    for h in range(HALVES):
+        pick = (mine[h][:, None] == place[None]).astype(jnp.bfloat16)
+        picked = dot(pick, both).astype(jnp.bfloat16)
+        own = picked[:piece] + flip(picked[piece:], "col", 2)
+        fulls.append(spread(own, zh, zl, x, k))
+    for h in range(HALVES):
+        full = fulls[h]
+        branch = 0.0
+        for i in range(UNIT_CHUNKS):
+            keep, send = partial_sums(full, gate_weight, up_weight, i * step, step)
+            sums = keep + flip(send, "col", 1)
+            sums = sums[:, :piece] + flip(sums[:, piece:].astype(jnp.bfloat16), "col", 2)
+            hidden = (jax.nn.silu(sums[0]) * sums[1]).astype(jnp.bfloat16)
+            part = slice(i * step, (i + 1) * step)
+            branch = branch + dot(spread(hidden, zh, zl, x, k), down_weight[part])
+        total = branch[:half] + flip(branch[half:].astype(jnp.bfloat16), "col", 1)
+        theirs = flip(total.astype(jnp.bfloat16), "col", 2)
+        totals.append(total + jnp.concatenate([theirs[piece:], theirs[:piece]], axis=0))
 
-    half = 2 * quarter
-    step = units // UNIT_CHUNKS
-    branch = jnp.zeros((2 * half, down_weight.shape[1]), jnp.float32)
-    for i in range(UNIT_CHUNKS):
-        part = slice(i * step, (i + 1) * step)
-        sums = jnp.stack([dot(full, gate_weight[:, part]), dot(full, up_weight[:, part])])
-        sums = sums[:, :half] + flip(sums[:, half:].astype(jnp.bfloat16), "col", 1)
-        sums = sums[:, :quarter] + flip(sums[:, quarter:].astype(jnp.bfloat16), "col", 2)
-        hidden = (jax.nn.silu(sums[0]) * sums[1]).astype(jnp.bfloat16)
-        branch = branch + dot(spread(hidden, zh, zl, x, k), down_weight[part])
-
-    total = branch[:half] + flip(branch[half:].astype(jnp.bfloat16), "col", 1)
-    theirs = flip(total.astype(jnp.bfloat16), "col", 2)
-    total = total + jnp.concatenate([theirs[quarter:], theirs[:quarter]], axis=0)
-    put = place.reshape(-1)[:, None] == mine[None]
-    moved = jnp.dot(put.astype(jnp.float32), total, precision=lax.Precision.HIGHEST)
+    put = place[:, None] == jnp.concatenate(mine)[None]
+    moved = jnp.dot(
+        put.astype(jnp.float32), jnp.concatenate(totals), precision=lax.Precision.HIGHEST
+    )
     handled = jnp.any(put, axis=1)
     mixed = jnp.where(handled[:, None], both.astype(jnp.float32) + moved, 0.0).astype(jnp.bfloat16)
     return mixed[:slots] + flip(mixed[slots:], "col", 1)

time: 181 us -> 182 us (level)
  waiting for transfers between devices: 122 us -> 85.2 us
  Pallas kernels: 0 us -> 30.8 us
  starting transfers between devices: 23.6 us -> 41.8 us
  matrix products: 24.1 us -> 7.93 us
  other arithmetic: 5.67 us -> 7.84 us
    ppermute x21 -> x40, waiting for transfers between devices: 122 us -> 85.2 us  [flip(): return lax.ppermute(value, axis, [(i, i ^ bit) for i in range(count)])]
    pallas_call x0 -> x4, Pallas kernels: none -> 30.8 us  [partial_sums(): pl.pallas_call(partial_sums_kernel, grid=(units // TILE,), in_specs=[pl.B...]
    ppermute x21 -> x40, starting transfers between devices: 23.6 us -> 41.8 us  [flip(): return lax.ppermute(value, axis, [(i, i ^ bit) for i in range(count)])]
    dot_general x7 -> x6, matrix products: 22.4 us -> 6.42 us  [dot(): return jnp.dot(a, b, preferred_element_type=jnp.float32)]
    unnamed x11 -> x19, local copies, waits for them, and re-layouts: 2.65 us -> 6.35 us
    select_n x3 -> x1, other arithmetic: 0.23 us -> 2.47 us  [stationary(): places.append(jnp.where(slot < count, slot + first, -1))]
    gather x2 -> x0, local copies, waits for them, and re-layouts: 1.93 us -> none  [the longest x1 1.29 us: stationary(): count = jnp.take(lengths, jnp.stack([c, c ^ 1]))]
  transfers between devices with their start and end apart: 21 -> 40, of which waited for: 17 -> 23; matrix products, arithmetic and copies ran while one was open for 10% -> 8% of each run, Pallas kernels for 0% -> 17%
where the time goes in v2:
time: 182 us; the launch traced here: 181 us
  waiting for transfers between devices  85.2 us (47%)
  starting transfers between devices  41.8 us (23%)
  Pallas kernels  30.8 us (17%)
  matrix products  7.93 us (4%)
  other arithmetic  7.84 us (4%)
  local copies, waits for them, and re-layouts  6.71 us (4%)
    ppermute x40, waiting for transfers between devices, flip(): return lax.ppermute(value, axis, [(i, i ^ bit) for i in range(count)])  85.2 us
    ppermute x40, starting transfers between devices, flip(): return lax.ppermute(value, axis, [(i, i ^ bit) for i in range(count)])  41.8 us
    pallas_call x4, Pallas kernels, partial_sums(): pl.pallas_call(partial_sums_kernel, grid=(units // TILE,), in_specs=[pl.B...  30.8 us
    dot_general x6, matrix products, dot(): return jnp.dot(a, b, preferred_element_type=jnp.float32)  6.42 us
    unnamed x19, local copies, waits for them, and re-layouts  6.35 us
  transfers between devices with their start and end apart: 40, of which 23 were waited for; matrix products, arithmetic and copies ran while one was open for 8% of the time, Pallas kernels for 17%

profile of v2, /device:TPU:0, one launch (start us, length us, event | category | flops | bytes accessed | tf_op | source)
XLA Modules:
  0.0 180.9 jit_solution(9820190312144753389)
XLA Ops:
  0.0 0.5 collective-permute-start
  0.6 1.4 fusion.51
  2.0 2.5 %compare_select_fusion.1 = (s32[160]{0:T(256)S(1)}, s32[160]{0:T(256)S(1)}) fusion(s32[]{:T(128)} %get-tuple-element.23, s32[]{:T(128)} %get-tuple-element.24, s32[]{:T(128)} %get-tuple-element.22, s32[]{:T(128)} %get-tuple-element.21), kind=kLoop, calls=%fused_computation.114 | loop fusion | flops 960 | bytes 1296 | tf_op jit(solution)/shard_map/jit(_where)/select_n | solution.py:81
  4.6 1.1 constant_dynamic-update-slice_fusion.1
  6.2 2.6 %collective-permute-start.1 = (bf16[40,2048]{1,0:T(8,128)(2,1)S(1)}, bf16[40,2048]{1,0:T(8,128)(2,1)S(1)}, u32[]{:S(2)}, u32[]{:S(2)}) collective-permute-start(bf16[40,2048]{1,0:T(8,128)(2,1)S(1)} %slice.137), channel_id=1, source_target_pairs={{0,2},{1,3},{2,0},{3,1},{4,6},{5,7},{6,4},{7,5},{8,10},{9,11},{10,... | collective-permute-start | bytes 491528 | tf_op jit(solution)/shard_map/ppermute | solution.py:19
  9.4 4.5 %collective-permute-done.1 = bf16[40,2048]{1,0:T(8,128)(2,1)S(1)} collective-permute-done((bf16[40,2048]{1,0:T(8,128)(2,1)S(1)}, bf16[40,2048]{1,0:T(8,128)(2,1)S(1)}, u32[]{:S(2)}, u32[]{:S(2)}) %collective-permute-start.1) | collective-permute-done | bytes 163872 | tf_op jit(solution)/shard_map/ppermute | solution.py:19
  13.9 3.1 %collective-permute-start.2 = (bf16[40,2048]{1,0:T(8,128)(2,1)S(1)}, bf16[40,2048]{1,0:T(8,128)(2,1)S(1)}, u32[]{:S(2)}, u32[]{:S(2)}) collective-permute-start(bf16[40,2048]{1,0:T(8,128)(2,1)S(1)} %slice_add_fusion.8), channel_id=1, source_target_pairs={{0,8},{4,12},{8,0},{12,4},{1,9},{5,13},{9,1},{13,5},{2,10},{6,14},... | collective-permute-start | bytes 491528 | tf_op jit(solution)/shard_map/ppermute | solution.py:19
  17.2 2.9 %collective-permute-start.21 = (bf16[40,2048]{1,0:T(8,128)(2,1)S(1)}, bf16[40,2048]{1,0:T(8,128)(2,1)S(1)}, u32[]{:S(2)}, u32[]{:S(2)}) collective-permute-start(bf16[40,2048]{1,0:T(8,128)(2,1)S(1)} %slice_add_fusion.7), channel_id=1, source_target_pairs={{0,8},{4,12},{8,0},{12,4},{1,9},{5,13},{9,1},{13,5},{2,10},{6,14},... | collective-permute-start | bytes 491528 | tf_op jit(solution)/shard_map/ppermute | solution.py:19
  20.1 8.8 %collective-permute-done.2 = bf16[40,2048]{1,0:T(8,128)(2,1)S(1)} collective-permute-done((bf16[40,2048]{1,0:T(8,128)(2,1)S(1)}, bf16[40,2048]{1,0:T(8,128)(2,1)S(1)}, u32[]{:S(2)}, u32[]{:S(2)}) %collective-permute-start.2) | collective-permute-done | bytes 163872 | tf_op jit(solution)/shard_map/ppermute | solution.py:19
  28.9 1.6 collective-permute-start.3
  30.5 0.7 collective-permute-done.21
  31.3 1.6 collective-permute-start.22
  32.9 3.0 %collective-permute-done.3 = bf16[40,2048]{1,0:T(8,128)(2,1)S(1)} collective-permute-done((bf16[40,2048]{1,0:T(8,128)(2,1)S(1)}, bf16[40,2048]{1,0:T(8,128)(2,1)S(1)}, u32[]{:S(2)}, u32[]{:S(2)}) %collective-permute-start.3) | collective-permute-done | bytes 163872 | tf_op jit(solution)/shard_map/ppermute | solution.py:19
  36.0 1.8 collective-permute-done.22
  38.3 7.9 %collective-permute-done.4 = bf16[80,2048]{1,0:T(8,128)(2,1)S(1)} collective-permute-done((bf16[80,2048]{1,0:T(8,128)(2,1)S(1)}, bf16[80,2048]{1,0:T(8,128)(2,1)S(1)}, u32[]{:S(2)}, u32[]{:S(2)}) %collective-permute-start.4) | collective-permute-done | bytes 327712 | tf_op jit(solution)/shard_map/ppermute | solution.py:19
  46.4 3.3 %collective-permute-done.23 = bf16[80,2048]{1,0:T(8,128)(2,1)S(1)} collective-permute-done((bf16[80,2048]{1,0:T(8,128)(2,1)S(1)}, bf16[80,2048]{1,0:T(8,128)(2,1)S(1)}, u32[]{:S(2)}, u32[]{:S(2)}) %collective-permute-start.23) | collective-permute-done | bytes 327712 | tf_op jit(solution)/shard_map/ppermute | solution.py:19
  50.0 5.2 %copy-done = bf16[2048,3584]{1,0:T(8,128)(2,1)S(1)} copy-done((bf16[2048,3584]{1,0:T(8,128)(2,1)S(1)}, bf16[2048,3584]{1,0:T(8,128)(2,1)}, u32[]{:S(2)}) %copy-start) | copy-done | bytes 14680088
  55.1 7.3 %shard_map.55 = (f32[2,80,1792]{2,1,0:T(8,128)S(1)}, bf16[2,80,1792]{2,1,0:T(8,128)(2,1)S(1)}) custom-call(bf16[160,2048]{1,0:T(8,128)(2,1)S(1)} %pad_maximum_fusion.full_ref, bf16[2048,3584]{1,0:T(8,128)(2,1)S(1)} %copy-done, bf16[2048,3584]{1,0:T(8,128)(2,1)} %up_ref.7), custom_call_target="tpu_custom_call" | custom-call | flops 2348810240 | bytes 16400384 | tf_op jit(solution)/shard_map/pallas_call | solution.py:48
  62.5 0.6 collective-permute-start.6
  63.1 8.6 %shard_map.56 = (f32[2,80,1792]{2,1,0:T(8,128)S(1)}, bf16[2,80,1792]{2,1,0:T(8,128)(2,1)S(1)}) custom-call(bf16[160,2048]{1,0:T(8,128)(2,1)S(1)} %pad_maximum_fusion.full_ref, bf16[2048,3584]{1,0:T(8,128)(2,1)S(1)} %copy-done, bf16[2048,3584]{1,0:T(8,128)(2,1)} %up_ref.7), custom_call_target="tpu_custom_call" | custom-call | flops 2348810240 | bytes 16400384 | tf_op jit(solution)/shard_map/pallas_call | solution.py:48
  71.7 0.6 collective-permute-start.12
  72.3 7.4 %shard_map.57 = (f32[2,80,1792]{2,1,0:T(8,128)S(1)}, bf16[2,80,1792]{2,1,0:T(8,128)(2,1)S(1)}) custom-call(bf16[160,2048]{1,0:T(8,128)(2,1)S(1)} %pad_maximum_fusion.1.full_ref, bf16[2048,3584]{1,0:T(8,128)(2,1)S(1)} %bitcast.59, bf16[2048,3584]{1,0:T(8,128)(2,1)} %up_ref.7), custom_call_target="tpu_custom_call" | custom-call | flops 2348810240 | bytes 16400384 | tf_op jit(solution)/shard_map/pallas_call | solution.py:48
  79.7 7.6 %shard_map.58 = (f32[2,80,1792]{2,1,0:T(8,128)S(1)}, bf16[2,80,1792]{2,1,0:T(8,128)(2,1)S(1)}) custom-call(bf16[160,2048]{1,0:T(8,128)(2,1)S(1)} %pad_maximum_fusion.1.full_ref, bf16[2048,3584]{1,0:T(8,128)(2,1)S(1)} %bitcast.59, bf16[2048,3584]{1,0:T(8,128)(2,1)} %up_ref.7), custom_call_target="tpu_custom_call" | custom-call | flops 2348810240 | bytes 16400384 | tf_op jit(solution)/shard_map/pallas_call | solution.py:48
  87.3 0.5 collective-permute-start.31
  88.0 1.6 collective-permute-start.7
  89.7 0.5 collective-permute-start.13
  90.4 1.6 collective-permute-start.26
  92.2 0.5 collective-permute-start.32
  92.7 5.0 %collective-permute-done.7 = bf16[2,40,1792]{2,1,0:T(8,128)(2,1)S(1)} collective-permute-done((bf16[2,40,1792]{2,1,0:T(8,128)(2,1)S(1)}, bf16[2,40,1792]{2,1,0:T(8,128)(2,1)S(1)}, u32[]{:S(2)}, u32[]{:S(2)}) %collective-permute-start.7) | collective-permute-done | bytes 286752 | tf_op jit(solution)/shard_map/ppermute | solution.py:19
  97.9 2.5 %collective-permute-start.8 = (bf16[40,1792]{1,0:T(8,128)(2,1)S(1)}, bf16[40,1792]{1,0:T(8,128)(2,1)S(1)}, u32[]{:S(2)}, u32[]{:S(2)}) collective-permute-start(bf16[40,1792]{1,0:T(8,128)(2,1)S(1)} %fusion.42), channel_id=1, source_target_pairs={{0,8},{4,12},{8,0},{12,4},{1,9},{5,13},{9,1},{13,5},{2,10},{6,14},... | collective-permute-start | bytes 430088 | tf_op jit(solution)/shard_map/ppermute | solution.py:19
  100.3 3.5 %collective-permute-done.13 = bf16[2,40,1792]{2,1,0:T(8,128)(2,1)S(1)} collective-permute-done((bf16[2,40,1792]{2,1,0:T(8,128)(2,1)S(1)}, bf16[2,40,1792]{2,1,0:T(8,128)(2,1)S(1)}, u32[]{:S(2)}, u32[]{:S(2)}) %collective-permute-start.13) | collective-permute-done | bytes 286752 | tf_op jit(solution)/shard_map/ppermute | solution.py:19
  104.0 2.5 %collective-permute-start.14 = (bf16[40,1792]{1,0:T(8,128)(2,1)S(1)}, bf16[40,1792]{1,0:T(8,128)(2,1)S(1)}, u32[]{:S(2)}, u32[]{:S(2)}) collective-permute-start(bf16[40,1792]{1,0:T(8,128)(2,1)S(1)} %fusion.40), channel_id=1, source_target_pairs={{0,8},{4,12},{8,0},{12,4},{1,9},{5,13},{9,1},{13,5},{2,10},{6,14},... | collective-permute-start | bytes 430088 | tf_op jit(solution)/shard_map/ppermute | solution.py:19
  106.5 3.5 %collective-permute-done.26 = bf16[2,40,1792]{2,1,0:T(8,128)(2,1)S(1)} collective-permute-done((bf16[2,40,1792]{2,1,0:T(8,128)(2,1)S(1)}, bf16[2,40,1792]{2,1,0:T(8,128)(2,1)S(1)}, u32[]{:S(2)}, u32[]{:S(2)}) %collective-permute-start.26) | collective-permute-done | bytes 286752 | tf_op jit(solution)/shard_map/ppermute | solution.py:19
  110.2 2.5 %collective-permute-start.27 = (bf16[40,1792]{1,0:T(8,128)(2,1)S(1)}, bf16[40,1792]{1,0:T(8,128)(2,1)S(1)}, u32[]{:S(2)}, u32[]{:S(2)}) collective-permute-start(bf16[40,1792]{1,0:T(8,128)(2,1)S(1)} %fusion.38), channel_id=1, source_target_pairs={{0,8},{4,12},{8,0},{12,4},{1,9},{5,13},{9,1},{13,5},{2,10},{6,14},... | collective-permute-start | bytes 430088 | tf_op jit(solution)/shard_map/ppermute | solution.py:19
  112.6 2.6 %collective-permute-done.32 = bf16[2,40,1792]{2,1,0:T(8,128)(2,1)S(1)} collective-permute-done((bf16[2,40,1792]{2,1,0:T(8,128)(2,1)S(1)}, bf16[2,40,1792]{2,1,0:T(8,128)(2,1)S(1)}, u32[]{:S(2)}, u32[]{:S(2)}) %collective-permute-start.32) | collective-permute-done | bytes 286752 | tf_op jit(solution)/shard_map/ppermute | solution.py:19
  115.4 2.5 %collective-permute-start.33 = (bf16[40,1792]{1,0:T(8,128)(2,1)S(1)}, bf16[40,1792]{1,0:T(8,128)(2,1)S(1)}, u32[]{:S(2)}, u32[]{:S(2)}) collective-permute-start(bf16[40,1792]{1,0:T(8,128)(2,1)S(1)} %fusion.36), channel_id=1, source_target_pairs={{0,8},{4,12},{8,0},{12,4},{1,9},{5,13},{9,1},{13,5},{2,10},{6,14},... | collective-permute-start | bytes 430088 | tf_op jit(solution)/shard_map/ppermute | solution.py:19
  118.0 1.6 collective-permute-start.9
  119.7 0.6 collective-permute-start.15
  120.5 1.5 collective-permute-start.28
  122.0 2.4 %collective-permute-done.33 = bf16[40,1792]{1,0:T(8,128)(2,1)S(1)} collective-permute-done((bf16[40,1792]{1,0:T(8,128)(2,1)S(1)}, bf16[40,1792]{1,0:T(8,128)(2,1)S(1)}, u32[]{:S(2)}, u32[]{:S(2)}) %collective-permute-start.33) | collective-permute-done | bytes 143392 | tf_op jit(solution)/shard_map/ppermute | solution.py:19
  124.5 1.6 collective-permute-start.34
  126.1 0.5 collective-permute-start.10
  126.6 1.2 collective-permute-done.15
  127.9 1.8 collective-permute-start.16
  129.7 0.7 collective-permute-done.28
  130.4 1.8 collective-permute-start.29
  132.2 1.5 collective-permute-start.35
  133.8 2.2 %collective-permute-done.10 = bf16[80,1792]{1,0:T(8,128)(2,1)S(1)} collective-permute-done((bf16[80,1792]{1,0:T(8,128)(2,1)S(1)}, bf16[80,1792]{1,0:T(8,128)(2,1)S(1)}, u32[]{:S(2)}, u32[]{:S(2)}) %collective-permute-start.10) | collective-permute-done | bytes 286752 | tf_op jit(solution)/shard_map/ppermute | solution.py:19
  136.2 6.0 %collective-permute-done.16 = bf16[80,1792]{1,0:T(8,128)(2,1)S(1)} collective-permute-done((bf16[80,1792]{1,0:T(8,128)(2,1)S(1)}, bf16[80,1792]{1,0:T(8,128)(2,1)S(1)}, u32[]{:S(2)}, u32[]{:S(2)}) %collective-permute-start.16) | collective-permute-done | bytes 286752 | tf_op jit(solution)/shard_map/ppermute | solution.py:19
  142.3 6.0 %collective-permute-done.29 = bf16[80,1792]{1,0:T(8,128)(2,1)S(1)} collective-permute-done((bf16[80,1792]{1,0:T(8,128)(2,1)S(1)}, bf16[80,1792]{1,0:T(8,128)(2,1)S(1)}, u32[]{:S(2)}, u32[]{:S(2)}) %collective-permute-start.29) | collective-permute-done | bytes 286752 | tf_op jit(solution)/shard_map/ppermute | solution.py:19
  148.5 3.7 %collective-permute-done.35 = bf16[80,1792]{1,0:T(8,128)(2,1)S(1)} collective-permute-done((bf16[80,1792]{1,0:T(8,128)(2,1)S(1)}, bf16[80,1792]{1,0:T(8,128)(2,1)S(1)}, u32[]{:S(2)}, u32[]{:S(2)}) %collective-permute-start.35) | collective-permute-done | bytes 286752 | tf_op jit(solution)/shard_map/ppermute | solution.py:19
  152.4 1.4 fusion.2
  153.8 1.4 fusion.8
  155.2 0.5 collective-permute-start.18
  155.8 1.4 fusion
  157.2 1.4 fusion.11
  158.8 0.5 collective-permute-start.19
  159.3 1.1 collective-permute-done.37
  160.4 0.6 collective-permute-start.38
  161.0 8.4 %collective-permute-done.19 = bf16[80,2048]{1,0:T(8,128)(2,1)S(1)} collective-permute-done((bf16[80,2048]{1,0:T(8,128)(2,1)S(1)}, bf16[80,2048]{1,0:T(8,128)(2,1)S(1)}, u32[]{:S(2)}, u32[]{:S(2)}) %collective-permute-start.19) | collective-permute-done | bytes 327712 | tf_op jit(solution)/shard_map/ppermute | solution.py:19
  169.4 6.6 %collective-permute-done.38 = bf16[80,2048]{1,0:T(8,128)(2,1)S(1)} collective-permute-done((bf16[80,2048]{1,0:T(8,128)(2,1)S(1)}, bf16[80,2048]{1,0:T(8,128)(2,1)S(1)}, u32[]{:S(2)}, u32[]{:S(2)}) %collective-permute-start.38) | collective-permute-done | bytes 327712 | tf_op jit(solution)/shard_map/ppermute | solution.py:19
  176.2 1.5 select_convert_fusion
  177.9 2.1 %collective-permute-done.39 = bf16[160,2048]{1,0:T(8,128)(2,1)S(1)} collective-permute-done((bf16[160,2048]{1,0:T(8,128)(2,1)S(1)}, bf16[160,2048]{1,0:T(8,128)(2,1)S(1)}, u32[]{:S(2)}, u32[]{:S(2)}) %collective-permute-start.39) | collective-permute-done | bytes 655392 | tf_op jit(solution)/shard_map/ppermute | solution.py:19
  180.0 0.9 slice_add_fusion
  (106 shorter events, 5.8 us)
Async XLA Ops:
  0.0 5.7 %collective-permute-start = (bf16[160,2048]{1,0:T(8,128)(2,1)}, bf16[160,2048]{1,0:T(8,128)(2,1)S(1)}, u32[]{:S(2)}, u32[]{:S(2)}) collective-permute-start(bf16[160,2048]{1,0:T(8,128)(2,1)} %param.5), channel_id=1, source_target_pairs={{0,1},{1,0},{2,3},{3,2},{4,5},{5,4},{6,7},{7,6},{8,9},{9,8},{10,11... | collective-permute-start | bytes 1966088 | tf_op jit(solution)/shard_map/ppermute | solution.py:19
  6.2 7.6 %collective-permute-start.1 = (bf16[40,2048]{1,0:T(8,128)(2,1)S(1)}, bf16[40,2048]{1,0:T(8,128)(2,1)S(1)}, u32[]{:S(2)}, u32[]{:S(2)}) collective-permute-start(bf16[40,2048]{1,0:T(8,128)(2,1)S(1)} %slice.137), channel_id=1, source_target_pairs={{0,2},{1,3},{2,0},{3,1},{4,6},{5,7},{6,4},{7,5},{8,10},{9,11},{10,... | collective-permute-start | bytes 491528 | tf_op jit(solution)/shard_map/ppermute | solution.py:19
  9.3 7.9 %collective-permute-start.20 = (bf16[40,2048]{1,0:T(8,128)(2,1)S(1)}, bf16[40,2048]{1,0:T(8,128)(2,1)S(1)}, u32[]{:S(2)}, u32[]{:S(2)}) collective-permute-start(bf16[40,2048]{1,0:T(8,128)(2,1)S(1)} %slice.151), channel_id=1, source_target_pairs={{0,2},{1,3},{2,0},{3,1},{4,6},{5,7},{6,4},{7,5},{8,10},{9,11},{10,... | collective-permute-start | bytes 491528 | tf_op jit(solution)/shard_map/ppermute | solution.py:19
  13.9 15.0 %collective-permute-start.2 = (bf16[40,2048]{1,0:T(8,128)(2,1)S(1)}, bf16[40,2048]{1,0:T(8,128)(2,1)S(1)}, u32[]{:S(2)}, u32[]{:S(2)}) collective-permute-start(bf16[40,2048]{1,0:T(8,128)(2,1)S(1)} %slice_add_fusion.8), channel_id=1, source_target_pairs={{0,8},{4,12},{8,0},{12,4},{1,9},{5,13},{9,1},{13,5},{2,10},{6,14},... | collective-permute-start | bytes 491528 | tf_op jit(solution)/shard_map/ppermute | solution.py:19
  17.2 14.0 %collective-permute-start.21 = (bf16[40,2048]{1,0:T(8,128)(2,1)S(1)}, bf16[40,2048]{1,0:T(8,128)(2,1)S(1)}, u32[]{:S(2)}, u32[]{:S(2)}) collective-permute-start(bf16[40,2048]{1,0:T(8,128)(2,1)S(1)} %slice_add_fusion.7), channel_id=1, source_target_pairs={{0,8},{4,12},{8,0},{12,4},{1,9},{5,13},{9,1},{13,5},{2,10},{6,14},... | collective-permute-start | bytes 491528 | tf_op jit(solution)/shard_map/ppermute | solution.py:19
  28.9 6.9 %collective-permute-start.3 = (bf16[40,2048]{1,0:T(8,128)(2,1)S(1)}, bf16[40,2048]{1,0:T(8,128)(2,1)S(1)}, u32[]{:S(2)}, u32[]{:S(2)}) collective-permute-start(bf16[40,2048]{1,0:T(8,128)(2,1)S(1)} %get-tuple-element.42), channel_id=1, source_target_pairs={{0,2},{1,3},{2,0},{3,1},{4,6},{5,7},{6,4},{7,5},{8,10},{9,11},{10,... | collective-permute-start | bytes 491528 | tf_op jit(solution)/shard_map/ppermute | solution.py:19
  31.3 6.6 %collective-permute-start.22 = (bf16[40,2048]{1,0:T(8,128)(2,1)S(1)}, bf16[40,2048]{1,0:T(8,128)(2,1)S(1)}, u32[]{:S(2)}, u32[]{:S(2)}) collective-permute-start(bf16[40,2048]{1,0:T(8,128)(2,1)S(1)} %get-tuple-element.46), channel_id=1, source_target_pairs={{0,2},{1,3},{2,0},{3,1},{4,6},{5,7},{6,4},{7,5},{8,10},{9,11},{10,... | collective-permute-start | bytes 491528 | tf_op jit(solution)/shard_map/ppermute | solution.py:19
  35.8 10.3 %collective-permute-start.4 = (bf16[80,2048]{1,0:T(8,128)(2,1)S(1)}, bf16[80,2048]{1,0:T(8,128)(2,1)S(1)}, u32[]{:S(2)}, u32[]{:S(2)}) collective-permute-start(bf16[80,2048]{1,0:T(8,128)(2,1)S(1)} %pad_maximum_fusion.2), channel_id=1, source_target_pairs={{0,4},{4,0},{8,12},{12,8},{1,5},{5,1},{9,13},{13,9},{2,6},{6,2},{1... | collective-permute-start | bytes 983048 | tf_op jit(solution)/shard_map/ppermute | solution.py:19
  37.9 11.8 %collective-permute-start.23 = (bf16[80,2048]{1,0:T(8,128)(2,1)S(1)}, bf16[80,2048]{1,0:T(8,128)(2,1)S(1)}, u32[]{:S(2)}, u32[]{:S(2)}) collective-permute-start(bf16[80,2048]{1,0:T(8,128)(2,1)S(1)} %pad_maximum_fusion.3), channel_id=1, source_target_pairs={{0,4},{4,0},{8,12},{12,8},{1,5},{5,1},{9,13},{13,9},{2,6},{6,2},{1... | collective-permute-start | bytes 983048 | tf_op jit(solution)/shard_map/ppermute | solution.py:19
  46.3 3.6 %collective-permute-start.5 = (bf16[80,2048]{1,0:T(8,128)(2,1)S(1)}, bf16[80,2048]{1,0:T(8,128)(2,1)S(1)}, u32[]{:S(2)}, u32[]{:S(2)}) collective-permute-start(bf16[80,2048]{1,0:T(8,128)(2,1)S(1)} %get-tuple-element.28), channel_id=1, source_target_pairs={{0,1},{1,0},{2,3},{3,2},{4,5},{5,4},{6,7},{7,6},{8,9},{9,8},{10,11... | collective-permute-start | bytes 983048 | tf_op jit(solution)/shard_map/ppermute | solution.py:19
  49.8 22.4 %collective-permute-start.24 = (bf16[80,2048]{1,0:T(8,128)(2,1)S(1)}, bf16[80,2048]{1,0:T(8,128)(2,1)S(1)}, u32[]{:S(2)}, u32[]{:S(2)}) collective-permute-start(bf16[80,2048]{1,0:T(8,128)(2,1)S(1)} %get-tuple-element.30), channel_id=1, source_target_pairs={{0,1},{1,0},{2,3},{3,2},{4,5},{5,4},{6,7},{7,6},{8,9},{9,8},{10,11... | collective-permute-start | bytes 983048 | tf_op jit(solution)/shard_map/ppermute | solution.py:19
  50.0 5.2 %copy-start = (bf16[2048,3584]{1,0:T(8,128)(2,1)S(1)}, bf16[2048,3584]{1,0:T(8,128)(2,1)}, u32[]{:S(2)}) copy-start(bf16[2048,3584]{1,0:T(8,128)(2,1)} %gate_ref.7) | copy-start | bytes 44040196
  62.5 9.8 %slice-start = ((s8[14680064]{0:T(1024)(128)(4,1)}), s8[4194304]{0:T(1024)(128)(4,1)S(1)}, s32[]{:S(2)}) async-start(s8[14680064]{0:T(1024)(128)(4,1)} %bitcast.58), calls=%async_computation | async-start | bytes 8388608
  62.5 9.8 %slice-start.1 = ((s8[14680064]{0:T(1024)(128)(4,1)}), s8[4194304]{0:T(1024)(128)(4,1)S(1)}, s32[]{:S(2)}) async-start(s8[14680064]{0:T(1024)(128)(4,1)} %bitcast.58), calls=%async_computation.1 | async-start | bytes 8388608
  62.5 9.8 %slice-start.2 = ((s8[14680064]{0:T(1024)(128)(4,1)}), s8[4194304]{0:T(1024)(128)(4,1)S(1)}, s32[]{:S(2)}) async-start(s8[14680064]{0:T(1024)(128)(4,1)} %bitcast.58), calls=%async_computation.2 | async-start | bytes 8388608
  62.5 9.8 %slice-start.3 = ((s8[14680064]{0:T(1024)(128)(4,1)}), s8[2097152]{0:T(1024)(128)(4,1)S(1)}, s32[]{:S(2)}) async-start(s8[14680064]{0:T(1024)(128)(4,1)} %bitcast.58), calls=%async_computation.3 | async-start | bytes 4194304
  62.5 25.3 %collective-permute-start.6 = (bf16[2,80,1792]{2,1,0:T(8,128)(2,1)S(1)}, bf16[2,80,1792]{2,1,0:T(8,128)(2,1)S(1)}, u32[]{:S(2)}, u32[]{:S(2)}) collective-permute-start(bf16[2,80,1792]{2,1,0:T(8,128)(2,1)S(1)} %get-tuple-element.14), channel_id=1, source_target_pairs={{0,1},{1,0},{2,3},{3,2},{4,5},{5,4},{6,7},{7,6},{8,9},{9,8},{10,11... | collective-permute-start | bytes 1720328 | tf_op jit(solution)/shard_map/ppermute | solution.py:19
  71.7 17.9 %collective-permute-start.12 = (bf16[2,80,1792]{2,1,0:T(8,128)(2,1)S(1)}, bf16[2,80,1792]{2,1,0:T(8,128)(2,1)S(1)}, u32[]{:S(2)}, u32[]{:S(2)}) collective-permute-start(bf16[2,80,1792]{2,1,0:T(8,128)(2,1)S(1)} %get-tuple-element.16), channel_id=1, source_target_pairs={{0,1},{1,0},{2,3},{3,2},{4,5},{5,4},{6,7},{7,6},{8,9},{9,8},{10,11... | collective-permute-start | bytes 1720328 | tf_op jit(solution)/shard_map/ppermute | solution.py:19
  87.2 3.0 %collective-permute-start.25 = (bf16[2,80,1792]{2,1,0:T(8,128)(2,1)S(1)}, bf16[2,80,1792]{2,1,0:T(8,128)(2,1)S(1)}, u32[]{:S(2)}, u32[]{:S(2)}) collective-permute-start(bf16[2,80,1792]{2,1,0:T(8,128)(2,1)S(1)} %get-tuple-element.18), channel_id=1, source_target_pairs={{0,1},{1,0},{2,3},{3,2},{4,5},{5,4},{6,7},{7,6},{8,9},{9,8},{10,11... | collective-permute-start | bytes 1720328 | tf_op jit(solution)/shard_map/ppermute | solution.py:19
  87.3 4.7 %collective-permute-start.31 = (bf16[2,80,1792]{2,1,0:T(8,128)(2,1)S(1)}, bf16[2,80,1792]{2,1,0:T(8,128)(2,1)S(1)}, u32[]{:S(2)}, u32[]{:S(2)}) collective-permute-start(bf16[2,80,1792]{2,1,0:T(8,128)(2,1)S(1)} %get-tuple-element.20), channel_id=1, source_target_pairs={{0,1},{1,0},{2,3},{3,2},{4,5},{5,4},{6,7},{7,6},{8,9},{9,8},{10,11... | collective-permute-start | bytes 1720328 | tf_op jit(solution)/shard_map/ppermute | solution.py:19
  88.0 9.8 %collective-permute-start.7 = (bf16[2,40,1792]{2,1,0:T(8,128)(2,1)S(1)}, bf16[2,40,1792]{2,1,0:T(8,128)(2,1)S(1)}, u32[]{:S(2)}, u32[]{:S(2)}) collective-permute-start(bf16[2,40,1792]{2,1,0:T(8,128)(2,1)S(1)} %slice.238), channel_id=1, source_target_pairs={{0,2},{1,3},{2,0},{3,1},{4,6},{5,7},{6,4},{7,5},{8,10},{9,11},{10,... | collective-permute-start | bytes 860168 | tf_op jit(solution)/shard_map/ppermute | solution.py:19
  89.6 62.8 %slice-start.4 = ((s8[14680064]{0:T(1024)(128)(4,1)}), s8[4194304]{0:T(1024)(128)(4,1)S(1)}, s32[]{:S(2)}) async-start(s8[14680064]{0:T(1024)(128)(4,1)} %bitcast.60), calls=%async_computation.4 | async-start | bytes 8388608
  89.7 14.1 %collective-permute-start.13 = (bf16[2,40,1792]{2,1,0:T(8,128)(2,1)S(1)}, bf16[2,40,1792]{2,1,0:T(8,128)(2,1)S(1)}, u32[]{:S(2)}, u32[]{:S(2)}) collective-permute-start(bf16[2,40,1792]{2,1,0:T(8,128)(2,1)S(1)} %slice.237), channel_id=1, source_target_pairs={{0,2},{1,3},{2,0},{3,1},{4,6},{5,7},{6,4},{7,5},{8,10},{9,11},{10,... | collective-permute-start | bytes 860168 | tf_op jit(solution)/shard_map/ppermute | solution.py:19
  90.4 19.6 %collective-permute-start.26 = (bf16[2,40,1792]{2,1,0:T(8,128)(2,1)S(1)}, bf16[2,40,1792]{2,1,0:T(8,128)(2,1)S(1)}, u32[]{:S(2)}, u32[]{:S(2)}) collective-permute-start(bf16[2,40,1792]{2,1,0:T(8,128)(2,1)S(1)} %slice.236), channel_id=1, source_target_pairs={{0,2},{1,3},{2,0},{3,1},{4,6},{5,7},{6,4},{7,5},{8,10},{9,11},{10,... | collective-permute-start | bytes 860168 | tf_op jit(solution)/shard_map/ppermute | solution.py:19
  92.0 60.4 %slice-start.5 = ((s8[14680064]{0:T(1024)(128)(4,1)}), s8[4194304]{0:T(1024)(128)(4,1)S(1)}, s32[]{:S(2)}) async-start(s8[14680064]{0:T(1024)(128)(4,1)} %bitcast.60), calls=%async_computation.5 | async-start | bytes 8388608
  92.2 23.1 %collective-permute-start.32 = (bf16[2,40,1792]{2,1,0:T(8,128)(2,1)S(1)}, bf16[2,40,1792]{2,1,0:T(8,128)(2,1)S(1)}, u32[]{:S(2)}, u32[]{:S(2)}) collective-permute-start(bf16[2,40,1792]{2,1,0:T(8,128)(2,1)S(1)} %slice.235), channel_id=1, source_target_pairs={{0,2},{1,3},{2,0},{3,1},{4,6},{5,7},{6,4},{7,5},{8,10},{9,11},{10,... | collective-permute-start | bytes 860168 | tf_op jit(solution)/shard_map/ppermute | solution.py:19
  97.9 20.0 %collective-permute-start.8 = (bf16[40,1792]{1,0:T(8,128)(2,1)S(1)}, bf16[40,1792]{1,0:T(8,128)(2,1)S(1)}, u32[]{:S(2)}, u32[]{:S(2)}) collective-permute-start(bf16[40,1792]{1,0:T(8,128)(2,1)S(1)} %fusion.42), channel_id=1, source_target_pairs={{0,8},{4,12},{8,0},{12,4},{1,9},{5,13},{9,1},{13,5},{2,10},{6,14},... | collective-permute-start | bytes 430088 | tf_op jit(solution)/shard_map/ppermute | solution.py:19
  104.0 48.4 %slice-start.6 = ((s8[14680064]{0:T(1024)(128)(4,1)}), s8[4194304]{0:T(1024)(128)(4,1)S(1)}, s32[]{:S(2)}) async-start(s8[14680064]{0:T(1024)(128)(4,1)} %bitcast.60), calls=%async_computation.6 | async-start | bytes 8388608
  104.0 15.6 %collective-permute-start.14 = (bf16[40,1792]{1,0:T(8,128)(2,1)S(1)}, bf16[40,1792]{1,0:T(8,128)(2,1)S(1)}, u32[]{:S(2)}, u32[]{:S(2)}) collective-permute-start(bf16[40,1792]{1,0:T(8,128)(2,1)S(1)} %fusion.40), channel_id=1, source_target_pairs={{0,8},{4,12},{8,0},{12,4},{1,9},{5,13},{9,1},{13,5},{2,10},{6,14},... | collective-permute-start | bytes 430088 | tf_op jit(solution)/shard_map/ppermute | solution.py:19
  110.2 10.2 %collective-permute-start.27 = (bf16[40,1792]{1,0:T(8,128)(2,1)S(1)}, bf16[40,1792]{1,0:T(8,128)(2,1)S(1)}, u32[]{:S(2)}, u32[]{:S(2)}) collective-permute-start(bf16[40,1792]{1,0:T(8,128)(2,1)S(1)} %fusion.38), channel_id=1, source_target_pairs={{0,8},{4,12},{8,0},{12,4},{1,9},{5,13},{9,1},{13,5},{2,10},{6,14},... | collective-permute-start | bytes 430088 | tf_op jit(solution)/shard_map/ppermute | solution.py:19
  115.4 8.9 %collective-permute-start.33 = (bf16[40,1792]{1,0:T(8,128)(2,1)S(1)}, bf16[40,1792]{1,0:T(8,128)(2,1)S(1)}, u32[]{:S(2)}, u32[]{:S(2)}) collective-permute-start(bf16[40,1792]{1,0:T(8,128)(2,1)S(1)} %fusion.36), channel_id=1, source_target_pairs={{0,8},{4,12},{8,0},{12,4},{1,9},{5,13},{9,1},{13,5},{2,10},{6,14},... | collective-permute-start | bytes 430088 | tf_op jit(solution)/shard_map/ppermute | solution.py:19
  118.0 8.1 %collective-permute-start.9 = (bf16[40,1792]{1,0:T(8,128)(2,1)S(1)}, bf16[40,1792]{1,0:T(8,128)(2,1)S(1)}, u32[]{:S(2)}, u32[]{:S(2)}) collective-permute-start(bf16[40,1792]{1,0:T(8,128)(2,1)S(1)} %get-tuple-element.48), channel_id=1, source_target_pairs={{0,2},{1,3},{2,0},{3,1},{4,6},{5,7},{6,4},{7,5},{8,10},{9,11},{10,... | collective-permute-start | bytes 430088 | tf_op jit(solution)/shard_map/ppermute | solution.py:19
  119.7 8.2 %collective-permute-start.15 = (bf16[40,1792]{1,0:T(8,128)(2,1)S(1)}, bf16[40,1792]{1,0:T(8,128)(2,1)S(1)}, u32[]{:S(2)}, u32[]{:S(2)}) collective-permute-start(bf16[40,1792]{1,0:T(8,128)(2,1)S(1)} %get-tuple-element.50), channel_id=1, source_target_pairs={{0,2},{1,3},{2,0},{3,1},{4,6},{5,7},{6,4},{7,5},{8,10},{9,11},{10,... | collective-permute-start | bytes 430088 | tf_op jit(solution)/shard_map/ppermute | solution.py:19
  120.4 32.0 %slice-start.7 = ((s8[14680064]{0:T(1024)(128)(4,1)}), s8[2097152]{0:T(1024)(128)(4,1)S(1)}, s32[]{:S(2)}) async-start(s8[14680064]{0:T(1024)(128)(4,1)} %bitcast.60), calls=%async_computation.7 | async-start | bytes 4194304
  120.5 9.9 %collective-permute-start.28 = (bf16[40,1792]{1,0:T(8,128)(2,1)S(1)}, bf16[40,1792]{1,0:T(8,128)(2,1)S(1)}, u32[]{:S(2)}, u32[]{:S(2)}) collective-permute-start(bf16[40,1792]{1,0:T(8,128)(2,1)S(1)} %get-tuple-element.52), channel_id=1, source_target_pairs={{0,2},{1,3},{2,0},{3,1},{4,6},{5,7},{6,4},{7,5},{8,10},{9,11},{10,... | collective-permute-start | bytes 430088 | tf_op jit(solution)/shard_map/ppermute | solution.py:19
  124.5 7.7 %collective-permute-start.34 = (bf16[40,1792]{1,0:T(8,128)(2,1)S(1)}, bf16[40,1792]{1,0:T(8,128)(2,1)S(1)}, u32[]{:S(2)}, u32[]{:S(2)}) collective-permute-start(bf16[40,1792]{1,0:T(8,128)(2,1)S(1)} %get-tuple-element.54), channel_id=1, source_target_pairs={{0,2},{1,3},{2,0},{3,1},{4,6},{5,7},{6,4},{7,5},{8,10},{9,11},{10,... | collective-permute-start | bytes 430088 | tf_op jit(solution)/shard_map/ppermute | solution.py:19
  126.1 9.8 %collective-permute-start.10 = (bf16[80,1792]{1,0:T(8,128)(2,1)S(1)}, bf16[80,1792]{1,0:T(8,128)(2,1)S(1)}, u32[]{:S(2)}, u32[]{:S(2)}) collective-permute-start(bf16[80,1792]{1,0:T(8,128)(2,1)S(1)} %pad_maximum_fusion.4), channel_id=1, source_target_pairs={{0,4},{4,0},{8,12},{12,8},{1,5},{5,1},{9,13},{13,9},{2,6},{6,2},{1... | collective-permute-start | bytes 860168 | tf_op jit(solution)/shard_map/ppermute | solution.py:19
  127.9 14.2 %collective-permute-start.16 = (bf16[80,1792]{1,0:T(8,128)(2,1)S(1)}, bf16[80,1792]{1,0:T(8,128)(2,1)S(1)}, u32[]{:S(2)}, u32[]{:S(2)}) collective-permute-start(bf16[80,1792]{1,0:T(8,128)(2,1)S(1)} %pad_maximum_fusion.5), channel_id=1, source_target_pairs={{0,4},{4,0},{8,12},{12,8},{1,5},{5,1},{9,13},{13,9},{2,6},{6,2},{1... | collective-permute-start | bytes 860168 | tf_op jit(solution)/shard_map/ppermute | solution.py:19
  130.4 17.9 %collective-permute-start.29 = (bf16[80,1792]{1,0:T(8,128)(2,1)S(1)}, bf16[80,1792]{1,0:T(8,128)(2,1)S(1)}, u32[]{:S(2)}, u32[]{:S(2)}) collective-permute-start(bf16[80,1792]{1,0:T(8,128)(2,1)S(1)} %pad_maximum_fusion.6), channel_id=1, source_target_pairs={{0,4},{4,0},{8,12},{12,8},{1,5},{5,1},{9,13},{13,9},{2,6},{6,2},{1... | collective-permute-start | bytes 860168 | tf_op jit(solution)/shard_map/ppermute | solution.py:19
  132.2 19.9 %collective-permute-start.35 = (bf16[80,1792]{1,0:T(8,128)(2,1)S(1)}, bf16[80,1792]{1,0:T(8,128)(2,1)S(1)}, u32[]{:S(2)}, u32[]{:S(2)}) collective-permute-start(bf16[80,1792]{1,0:T(8,128)(2,1)S(1)} %pad_maximum_fusion.7), channel_id=1, source_target_pairs={{0,4},{4,0},{8,12},{12,8},{1,5},{5,1},{9,13},{13,9},{2,6},{6,2},{1... | collective-permute-start | bytes 860168 | tf_op jit(solution)/shard_map/ppermute | solution.py:19
  136.1 17.7 %collective-permute-start.11 = (bf16[80,1792]{1,0:T(8,128)(2,1)S(1)}, bf16[80,1792]{1,0:T(8,128)(2,1)S(1)}, u32[]{:S(2)}, u32[]{:S(2)}) collective-permute-start(bf16[80,1792]{1,0:T(8,128)(2,1)S(1)} %get-tuple-element.32), channel_id=1, source_target_pairs={{0,1},{1,0},{2,3},{3,2},{4,5},{5,4},{6,7},{7,6},{8,9},{9,8},{10,11... | collective-permute-start | bytes 860168 | tf_op jit(solution)/shard_map/ppermute | solution.py:19
  142.2 10.1 %collective-permute-start.17 = (bf16[80,1792]{1,0:T(8,128)(2,1)S(1)}, bf16[80,1792]{1,0:T(8,128)(2,1)S(1)}, u32[]{:S(2)}, u32[]{:S(2)}) collective-permute-start(bf16[80,1792]{1,0:T(8,128)(2,1)S(1)} %get-tuple-element.34), channel_id=1, source_target_pairs={{0,1},{1,0},{2,3},{3,2},{4,5},{5,4},{6,7},{7,6},{8,9},{9,8},{10,11... | collective-permute-start | bytes 860168 | tf_op jit(solution)/shard_map/ppermute | solution.py:19
  148.4 8.8 %collective-permute-start.30 = (bf16[80,1792]{1,0:T(8,128)(2,1)S(1)}, bf16[80,1792]{1,0:T(8,128)(2,1)S(1)}, u32[]{:S(2)}, u32[]{:S(2)}) collective-permute-start(bf16[80,1792]{1,0:T(8,128)(2,1)S(1)} %get-tuple-element.36), channel_id=1, source_target_pairs={{0,1},{1,0},{2,3},{3,2},{4,5},{5,4},{6,7},{7,6},{8,9},{9,8},{10,11... | collective-permute-start | bytes 860168 | tf_op jit(solution)/shard_map/ppermute | solution.py:19
  152.3 3.5 %collective-permute-start.36 = (bf16[80,1792]{1,0:T(8,128)(2,1)S(1)}, bf16[80,1792]{1,0:T(8,128)(2,1)S(1)}, u32[]{:S(2)}, u32[]{:S(2)}) collective-permute-start(bf16[80,1792]{1,0:T(8,128)(2,1)S(1)} %get-tuple-element.38), channel_id=1, source_target_pairs={{0,1},{1,0},{2,3},{3,2},{4,5},{5,4},{6,7},{7,6},{8,9},{9,8},{10,11... | collective-permute-start | bytes 860168 | tf_op jit(solution)/shard_map/ppermute | solution.py:19
  155.2 3.5 %collective-permute-start.18 = (bf16[80,2048]{1,0:T(8,128)(2,1)S(1)}, bf16[80,2048]{1,0:T(8,128)(2,1)S(1)}, u32[]{:S(2)}, u32[]{:S(2)}) collective-permute-start(bf16[80,2048]{1,0:T(8,128)(2,1)S(1)} %slice.234), channel_id=1, source_target_pairs={{0,1},{1,0},{2,3},{3,2},{4,5},{5,4},{6,7},{7,6},{8,9},{9,8},{10,11... | collective-permute-start | bytes 983048 | tf_op jit(solution)/shard_map/ppermute | solution.py:19
  158.6 1.7 collective-permute-start.37
  158.8 10.6 %collective-permute-start.19 = (bf16[80,2048]{1,0:T(8,128)(2,1)S(1)}, bf16[80,2048]{1,0:T(8,128)(2,1)S(1)}, u32[]{:S(2)}, u32[]{:S(2)}) collective-permute-start(bf16[80,2048]{1,0:T(8,128)(2,1)S(1)} %fusion.32), channel_id=1, source_target_pairs={{0,2},{1,3},{2,0},{3,1},{4,6},{5,7},{6,4},{7,5},{8,10},{9,11},{10,... | collective-permute-start | bytes 983048 | tf_op jit(solution)/shard_map/ppermute | solution.py:19
  160.4 15.6 %collective-permute-start.38 = (bf16[80,2048]{1,0:T(8,128)(2,1)S(1)}, bf16[80,2048]{1,0:T(8,128)(2,1)S(1)}, u32[]{:S(2)}, u32[]{:S(2)}) collective-permute-start(bf16[80,2048]{1,0:T(8,128)(2,1)S(1)} %fusion.33), channel_id=1, source_target_pairs={{0,2},{1,3},{2,0},{3,1},{4,6},{5,7},{6,4},{7,5},{8,10},{9,11},{10,... | collective-permute-start | bytes 983048 | tf_op jit(solution)/shard_map/ppermute | solution.py:19
  177.8 2.2 %collective-permute-start.39 = (bf16[160,2048]{1,0:T(8,128)(2,1)S(1)}, bf16[160,2048]{1,0:T(8,128)(2,1)S(1)}, u32[]{:S(2)}, u32[]{:S(2)}) collective-permute-start(bf16[160,2048]{1,0:T(8,128)(2,1)S(1)} %slice.165), channel_id=1, source_target_pairs={{0,1},{1,0},{2,3},{3,2},{4,5},{5,4},{6,7},{7,6},{8,9},{9,8},{10,11... | collective-permute-start | bytes 1966088 | tf_op jit(solution)/shard_map/ppermute | solution.py:19

commit v3 on v1

v3 whole, which is shorter than its diff:
```python
import jax
import jax.numpy as jnp
from jax import lax
from jax.sharding import PartitionSpec as P

UNIT_CHUNKS = 2
HALVES = 2


def dot(a, b):
    return jnp.dot(a, b, preferred_element_type=jnp.float32)


def flip(value, axis, bit):
    count = lax.axis_size(axis)
    return lax.ppermute(value, axis, [(i, i ^ bit) for i in range(count)])


def after(value, *others):
    return lax.optimization_barrier((value, *others))[0]


def stationary(tokens, lengths, gate_weight, up_weight, down_weight):
    slots, width = tokens.shape
    units = gate_weight.shape[1]
    c = lax.axis_index("col")
    r = lax.axis_index("row")
    x, k, zh, zl = c // 2, c % 2, r // 2, r % 2
    quarter = slots // 2
    piece = quarter // HALVES

    rows = jnp.arange(lengths.shape[0], dtype=jnp.int32)
    slot = jnp.arange(slots, dtype=jnp.int32)
    places = []
    for row in (c, c ^ 1):
        first = jnp.sum(jnp.where(rows < row, lengths, 0))
        count = jnp.sum(jnp.where(rows == row, lengths, 0))
        places.append(jnp.where(slot < count, slot + first, -1))
    inside = jnp.arange(piece, dtype=jnp.int32)
    mine = [
        jnp.concatenate([inside + quarter * c, inside + quarter * (c ^ 2)]) + h * piece
        for h in range(HALVES)
    ]

    busy = {}

    def swap(value, axis, bit, depth=1):
        link = (axis, bit) if bit == 1 and axis == "col" else axis
        line = busy.setdefault(link, [])
        if depth and len(line) >= depth:
            value = after(value, line[-depth])
        got = flip(value, axis, bit)
        line.append(got)
        return got

    def steps_of_spread(piece):
        other = swap(piece, "row", 2)
        yield
        stay = zh == x
        keep = jnp.where(stay, piece, other)
        send = jnp.where(stay, other, piece)
        pair = jnp.concatenate([keep, swap(send, "col", 2)], axis=0)
        yield
        other = swap(pair, "row", 1)
        yield
        stay = zl == k
        keep = jnp.where(stay, pair, other)
        send = jnp.where(stay, other, pair)
        yield jnp.concatenate([keep, swap(send, "col", 1, 0)], axis=0)

    sibling = flip(tokens, "col", 1)
    half = 2 * piece
    step = units // UNIT_CHUNKS

    def half_steps(h):
        own_pick = (mine[h][:, None] == places[0][None]).astype(jnp.bfloat16)
        sib_pick = (mine[h][:, None] == places[1][None]).astype(jnp.bfloat16)
        picked = (dot(own_pick, tokens) + dot(sib_pick, sibling)).astype(jnp.bfloat16)
        own = picked[:piece] + swap(picked[piece:], "col", 2)
        yield
        for full in steps_of_spread(own):
            yield full

    def chunk_steps(full, i):
        part = slice(i * step, (i + 1) * step)
        if "sums" in busy:
            full = after(full, busy["sums"])
        gate, up = dot(full, gate_weight[:, part]), dot(full, up_weight[:, part])
        send = jnp.stack([gate[half:], up[half:]]).astype(jnp.bfloat16)
        got = busy["sums"] = swap(send, "col", 1, 0)
        gate, up = gate[:half] + got[0], up[:half] + got[1]
        send = jnp.stack([gate[piece:], up[piece:]]).astype(jnp.bfloat16)
        got = swap(send, "col", 2)
        gate, up = gate[:piece] + got[0], up[:piece] + got[1]
        yield
        hidden = (jax.nn.silu(gate) * up).astype(jnp.bfloat16)
        for whole in steps_of_spread(hidden):
            yield whole

    def run(generators):
        results = [None] * len(generators)
        live = []
        waiting = list(range(len(generators)))
        while live or waiting:
            if waiting:
                live.append(waiting.pop(0))
            for index in list(live):
                try:
                    value = next(generators[index])
                    if value is not None:
                        results[index] = value
                except StopIteration:
                    live.remove(index)
        return results

    fulls = run([half_steps(h) for h in range(HALVES)])
    wholes = run([chunk_steps(fulls[h], i) for h in range(HALVES) for i in range(UNIT_CHUNKS)])
    totals = []
    for h in range(HALVES):
        branch = 0.0
        for i in range(UNIT_CHUNKS):
            branch = branch + dot(wholes[h * UNIT_CHUNKS + i], down_weight[i * step : (i + 1) * step])
        total = branch[:half] + swap(branch[half:].astype(jnp.bfloat16), "col", 1, 0)
        theirs = swap(total.astype(jnp.bfloat16), "col", 2)
        totals.append(total + jnp.concatenate([theirs[piece:], theirs[:piece]], axis=0))

    total = jnp.concatenate(totals)
    mixed = []
    for place, known in zip(places, (tokens, sibling)):
        put = place[:, None] == jnp.concatenate(mine)[None]
        moved = jnp.dot(put.astype(jnp.float32), total, precision=lax.Precision.HIGHEST)
        handled = jnp.any(put, axis=1)[:, None]
        mixed.append(jnp.where(handled, known.astype(jnp.float32) + moved, 0.0).astype(jnp.bfloat16))
    return mixed[0] + flip(mixed[1], "col", 1)


def general(tokens, lengths, gate_weight, up_weight, down_weight):
    c = lax.axis_index("col")
    slots = tokens.shape[0]
    whole = lax.all_gather(tokens, "row", axis=1, tiled=True)
    whole = lax.all_gather(whole, "col", axis=0, tiled=True)
    depth = gate_weight.shape[0]
    block = lax.dynamic_slice_in_dim(whole, c * depth, depth, axis=1)

    def summed(a, b):
        return lax.psum_scatter(dot(a, b), "col", scatter_dimension=0, tiled=True)

    hidden = (jax.nn.silu(summed(block, gate_weight)) * summed(block, up_weight)).astype(jnp.bfloat16)
    hidden = lax.all_gather(hidden, "row", axis=1, tiled=True)
    hidden = lax.all_gather(hidden, "col", axis=0, tiled=True)
    depth = down_weight.shape[0]
    branch = summed(lax.dynamic_slice_in_dim(hidden, c * depth, depth, axis=1), down_weight)
    valid = jnp.arange(slots, dtype=jnp.int32) < jnp.take(lengths, c)
    total = tokens.astype(jnp.float32) + branch
    return jnp.where(valid[:, None], total, jnp.float32(0.0)).astype(jnp.bfloat16)


def solution(mesh):
    square = mesh.shape["row"] == 4 and mesh.shape["col"] == 4
    in_specs = (
        P(("groups", "col"), "row"),
        P("groups"),
        P("col", "row"),
        P("col", "row"),
        P("col", "row"),
    )
    out_specs = P(("groups", "col"), "row")
    return jax.shard_map(
        stationary if square else general,
        mesh=mesh, in_specs=in_specs, out_specs=out_specs, check_vma=False,
    )
```

time: 181 us -> 176 us (0.972)
  waiting for transfers between devices: 122 us -> 110 us
  starting transfers between devices: 23.6 us -> 28.7 us
  local copies, waits for them, and re-layouts: 5.03 us -> 0.59 us
  matrix products: 24.1 us -> 28.5 us
    ppermute x21 -> x40, waiting for transfers between devices: 122 us -> 110 us  [flip(): return lax.ppermute(value, axis, [(i, i ^ bit) for i in range(count)])]
    ppermute x21 -> x40, starting transfers between devices: 23.6 us -> 28.7 us  [flip(): return lax.ppermute(value, axis, [(i, i ^ bit) for i in range(count)])]
    dot_general x7 -> x16, matrix products: 22.4 us -> 25.7 us  [dot(): return jnp.dot(a, b, preferred_element_type=jnp.float32)]
    unnamed x11 -> x20, local copies, waits for them, and re-layouts: 2.65 us -> 0.05 us
    gather x2 -> x0, local copies, waits for them, and re-layouts: 1.93 us -> none  [the longest x1 1.29 us: stationary(): count = jnp.take(lengths, jnp.stack([c, c ^ 1]))]
  transfers between devices with their start and end apart: 21 -> 40, of which waited for: 17 -> 26; matrix products, arithmetic and copies ran while one was open for 10% -> 17% of each run, Pallas kernels for 0% -> 0%
where the time goes in v3:
time: 176 us
  waiting for transfers between devices  110 us (62%)
  starting transfers between devices  28.7 us (16%)
  matrix products  28.5 us (16%)
  other arithmetic  6.93 us (4%)
    ppermute x40, waiting for transfers between devices, flip(): return lax.ppermute(value, axis, [(i, i ^ bit) for i in range(count)])  110 us
    ppermute x40, starting transfers between devices, flip(): return lax.ppermute(value, axis, [(i, i ^ bit) for i in range(count)])  28.7 us
    dot_general x16, matrix products, dot(): return jnp.dot(a, b, preferred_element_type=jnp.float32)  25.7 us
  transfers between devices with their start and end apart: 40, of which 26 were waited for; matrix products, arithmetic and copies ran while one was open for 17% of the time, Pallas kernels for 0%

profile of v3, /device:TPU:0, one launch (start us, length us, event | category | flops | bytes accessed | tf_op | source)
XLA Modules:
  0.0 175.9 jit_solution(9721086306810162287)
XLA Ops:
  0.0 0.5 collective-permute-start
  0.5 1.4 fusion.96
  1.9 2.5 %compare_select_fusion.1 = (s32[160]{0:T(256)S(1)}, s32[160]{0:T(256)S(1)}) fusion(s32[]{:T(128)} %get-tuple-element.64, s32[]{:T(128)} %get-tuple-element.61, s32[]{:T(128)} %get-tuple-element.62, s32[]{:T(128)} %get-tuple-element.63), kind=kLoop, calls=%fused_computation.194 | loop fusion | flops 960 | bytes 1296 | tf_op jit(solution)/shard_map/jit(_where)/select_n | solution.py:38
  4.4 1.4 fusion.84
  6.2 2.6 %collective-permute-start.1 = (bf16[40,2048]{1,0:T(8,128)(2,1)S(1)}, bf16[40,2048]{1,0:T(8,128)(2,1)S(1)}, u32[]{:S(2)}, u32[]{:S(2)}) collective-permute-start(bf16[40,2048]{1,0:T(8,128)(2,1)S(1)} %slice.289), channel_id=1, source_target_pairs={{0,2},{1,3},{2,0},{3,1},{4,6},{5,7},{6,4},{7,5},{8,10},{9,11},{10,... | collective-permute-start | bytes 491528 | tf_op jit(solution)/shard_map/ppermute | solution.py:16
  8.7 0.3 fusion.81
  9.1 4.5 %collective-permute-done.1 = bf16[40,2048]{1,0:T(8,128)(2,1)S(1)} collective-permute-done((bf16[40,2048]{1,0:T(8,128)(2,1)S(1)}, bf16[40,2048]{1,0:T(8,128)(2,1)S(1)}, u32[]{:S(2)}, u32[]{:S(2)}) %collective-permute-start.1) | collective-permute-done | bytes 163872 | tf_op jit(solution)/shard_map/ppermute | solution.py:16
  13.6 2.9 %collective-permute-start.2 = (bf16[40,2048]{1,0:T(8,128)(2,1)S(1)}, bf16[40,2048]{1,0:T(8,128)(2,1)S(1)}, u32[]{:S(2)}, u32[]{:S(2)}) collective-permute-start(bf16[40,2048]{1,0:T(8,128)(2,1)S(1)} %slice_add_fusion.19), channel_id=1, source_target_pairs={{0,8},{4,12},{8,0},{12,4},{1,9},{5,13},{9,1},{13,5},{2,10},{6,14},... | collective-permute-start | bytes 491528 | tf_op jit(solution)/shard_map/ppermute | solution.py:16
  16.8 1.6 collective-permute-start.3
  18.4 5.7 %collective-permute-done.2 = bf16[40,2048]{1,0:T(8,128)(2,1)S(1)} collective-permute-done((bf16[40,2048]{1,0:T(8,128)(2,1)S(1)}, bf16[40,2048]{1,0:T(8,128)(2,1)S(1)}, u32[]{:S(2)}, u32[]{:S(2)}) %collective-permute-start.2) | collective-permute-done | bytes 163872 | tf_op jit(solution)/shard_map/ppermute | solution.py:16
  24.2 1.6 collective-permute-start.4
  25.9 3.7 %collective-permute-done.4 = bf16[40,2048]{1,0:T(8,128)(2,1)S(1)} collective-permute-done((bf16[40,2048]{1,0:T(8,128)(2,1)S(1)}, bf16[40,2048]{1,0:T(8,128)(2,1)S(1)}, u32[]{:S(2)}, u32[]{:S(2)}) %collective-permute-start.4) | collective-permute-done | bytes 163872 | tf_op jit(solution)/shard_map/ppermute | solution.py:16
  29.6 5.7 %collective-permute-done.5 = bf16[40,2048]{1,0:T(8,128)(2,1)S(1)} collective-permute-done((bf16[40,2048]{1,0:T(8,128)(2,1)S(1)}, bf16[40,2048]{1,0:T(8,128)(2,1)S(1)}, u32[]{:S(2)}, u32[]{:S(2)}) %collective-permute-start.5) | collective-permute-done | bytes 163872 | tf_op jit(solution)/shard_map/ppermute | solution.py:16
  35.3 0.6 collective-permute-start.9
  35.9 6.4 %collective-permute-done.6 = bf16[80,2048]{1,0:T(8,128)(2,1)S(1)} collective-permute-done((bf16[80,2048]{1,0:T(8,128)(2,1)S(1)}, bf16[80,2048]{1,0:T(8,128)(2,1)S(1)}, u32[]{:S(2)}, u32[]{:S(2)}) %collective-permute-start.6) | collective-permute-done | bytes 327712 | tf_op jit(solution)/shard_map/ppermute | solution.py:16
  42.9 0.5 collective-permute-start.11
  43.4 0.8 collective-permute-done.7
  44.2 4.6 %fusion.22 = f32[160,1792]{1,0:T(8,128)S(1)} fusion(bf16[2048,3584]{1,0:T(8,128)(2,1)} %param.7, bf16[80,2048]{1,0:T(8,128)(2,1)S(1)} %collective-permute-done.7, bf16[80,2048]{1,0:T(8,128)(2,1)S(1)} %get-tuple-element.67), kind=kOutput, calls=%fused_computation.22 | convolution fusion | flops 1175715840 | bytes 9142272 | tf_op jit(solution)/shard_map/dot_general | solution.py:11
  48.9 1.4 fusion.18
  50.6 2.5 %collective-permute-done.11 = bf16[80,2048]{1,0:T(8,128)(2,1)S(1)} collective-permute-done((bf16[80,2048]{1,0:T(8,128)(2,1)S(1)}, bf16[80,2048]{1,0:T(8,128)(2,1)S(1)}, u32[]{:S(2)}, u32[]{:S(2)}) %collective-permute-start.11) | collective-permute-done | bytes 327712 | tf_op jit(solution)/shard_map/ppermute | solution.py:16
  53.4 1.4 fusion.14
  54.8 1.4 fusion.10
  56.4 0.6 collective-permute-start.10
  57.4 8.3 %collective-permute-done.10 = bf16[2,40,1792]{2,1,0:T(8,128)(2,1)S(1)} collective-permute-done((bf16[2,40,1792]{2,1,0:T(8,128)(2,1)S(1)}, bf16[2,40,1792]{2,1,0:T(8,128)(2,1)S(1)}, u32[]{:S(2)}, u32[]{:S(2)}) %collective-permute-start.10) | collective-permute-done | bytes 286752 | tf_op jit(solution)/shard_map/ppermute | solution.py:16
  65.8 1.9 %collective-permute-start.12 = (bf16[40,1792]{1,0:T(8,128)(2,1)S(1)}, bf16[40,1792]{1,0:T(8,128)(2,1)S(1)}, u32[]{:S(2)}, u32[]{:S(2)}) collective-permute-start(bf16[40,1792]{1,0:T(8,128)(2,1)S(1)} %fusion.65), channel_id=1, source_target_pairs={{0,8},{4,12},{8,0},{12,4},{1,9},{5,13},{9,1},{13,5},{2,10},{6,14},... | collective-permute-start | bytes 430088 | tf_op jit(solution)/shard_map/ppermute | solution.py:16
  67.7 7.5 %collective-permute-done.12 = bf16[40,1792]{1,0:T(8,128)(2,1)S(1)} collective-permute-done((bf16[40,1792]{1,0:T(8,128)(2,1)S(1)}, bf16[40,1792]{1,0:T(8,128)(2,1)S(1)}, u32[]{:S(2)}, u32[]{:S(2)}) %collective-permute-start.12) | collective-permute-done | bytes 143392 | tf_op jit(solution)/shard_map/ppermute | solution.py:16
  75.2 1.4 fusion.20
  76.6 1.4 fusion.16
  78.2 0.6 collective-permute-start.14
  79.0 7.6 %collective-permute-done.14 = bf16[2,40,1792]{2,1,0:T(8,128)(2,1)S(1)} collective-permute-done((bf16[2,40,1792]{2,1,0:T(8,128)(2,1)S(1)}, bf16[2,40,1792]{2,1,0:T(8,128)(2,1)S(1)}, u32[]{:S(2)}, u32[]{:S(2)}) %collective-permute-start.14) | collective-permute-done | bytes 286752 | tf_op jit(solution)/shard_map/ppermute | solution.py:16
  86.7 0.6 collective-permute-start.15
  87.4 4.3 %collective-permute-done.15 = bf16[40,1792]{1,0:T(8,128)(2,1)S(1)} collective-permute-done((bf16[40,1792]{1,0:T(8,128)(2,1)S(1)}, bf16[40,1792]{1,0:T(8,128)(2,1)S(1)}, u32[]{:S(2)}, u32[]{:S(2)}) %collective-permute-start.15) | collective-permute-done | bytes 143392 | tf_op jit(solution)/shard_map/ppermute | solution.py:16
  91.8 3.8 %collective-permute-done.16 = bf16[40,1792]{1,0:T(8,128)(2,1)S(1)} collective-permute-done((bf16[40,1792]{1,0:T(8,128)(2,1)S(1)}, bf16[40,1792]{1,0:T(8,128)(2,1)S(1)}, u32[]{:S(2)}, u32[]{:S(2)}) %collective-permute-start.16) | collective-permute-done | bytes 143392 | tf_op jit(solution)/shard_map/ppermute | solution.py:16
  95.6 1.6 fusion.12
  97.2 1.4 fusion.8
  98.9 1.4 collective-permute-start.21
  100.5 3.0 %collective-permute-done.17 = bf16[80,1792]{1,0:T(8,128)(2,1)S(1)} collective-permute-done((bf16[80,1792]{1,0:T(8,128)(2,1)S(1)}, bf16[80,1792]{1,0:T(8,128)(2,1)S(1)}, u32[]{:S(2)}, u32[]{:S(2)}) %collective-permute-start.17) | collective-permute-done | bytes 286752 | tf_op jit(solution)/shard_map/ppermute | solution.py:16
  103.6 3.2 %collective-permute-done.21 = bf16[2,40,1792]{2,1,0:T(8,128)(2,1)S(1)} collective-permute-done((bf16[2,40,1792]{2,1,0:T(8,128)(2,1)S(1)}, bf16[2,40,1792]{2,1,0:T(8,128)(2,1)S(1)}, u32[]{:S(2)}, u32[]{:S(2)}) %collective-permute-start.21) | collective-permute-done | bytes 286752 | tf_op jit(solution)/shard_map/ppermute | solution.py:16
  106.8 1.2 collective-permute-start.22
  108.1 2.6 %collective-permute-start.23 = (bf16[40,1792]{1,0:T(8,128)(2,1)S(1)}, bf16[40,1792]{1,0:T(8,128)(2,1)S(1)}, u32[]{:S(2)}, u32[]{:S(2)}) collective-permute-start(bf16[40,1792]{1,0:T(8,128)(2,1)S(1)} %fusion.61), channel_id=1, source_target_pairs={{0,8},{4,12},{8,0},{12,4},{1,9},{5,13},{9,1},{13,5},{2,10},{6,14},... | collective-permute-start | bytes 430088 | tf_op jit(solution)/shard_map/ppermute | solution.py:16
  110.7 1.2 collective-permute-done.22
  111.9 3.9 %collective-permute-done.23 = bf16[40,1792]{1,0:T(8,128)(2,1)S(1)} collective-permute-done((bf16[40,1792]{1,0:T(8,128)(2,1)S(1)}, bf16[40,1792]{1,0:T(8,128)(2,1)S(1)}, u32[]{:S(2)}, u32[]{:S(2)}) %collective-permute-start.23) | collective-permute-done | bytes 143392 | tf_op jit(solution)/shard_map/ppermute | solution.py:16
  116.3 0.8 collective-permute-start.28
  117.1 5.4 %collective-permute-done.24 = bf16[80,1792]{1,0:T(8,128)(2,1)S(1)} collective-permute-done((bf16[80,1792]{1,0:T(8,128)(2,1)S(1)}, bf16[80,1792]{1,0:T(8,128)(2,1)S(1)}, u32[]{:S(2)}, u32[]{:S(2)}) %collective-permute-start.24) | collective-permute-done | bytes 286752 | tf_op jit(solution)/shard_map/ppermute | solution.py:16
  122.7 0.3 collective-permute-done.28
  123.0 0.8 collective-permute-start.30
  123.9 2.9 %collective-permute-start.29 = (bf16[40,1792]{1,0:T(8,128)(2,1)S(1)}, bf16[40,1792]{1,0:T(8,128)(2,1)S(1)}, u32[]{:S(2)}, u32[]{:S(2)}) collective-permute-start(bf16[40,1792]{1,0:T(8,128)(2,1)S(1)} %fusion.59), channel_id=1, source_target_pairs={{0,8},{4,12},{8,0},{12,4},{1,9},{5,13},{9,1},{13,5},{2,10},{6,14},... | collective-permute-start | bytes 430088 | tf_op jit(solution)/shard_map/ppermute | solution.py:16
  126.8 4.6 %fusion.2 = f32[160,2048]{1,0:T(8,128)S(1)} fusion(bf16[3584,2048]{1,0:T(8,128)(2,1)} %param.9, bf16[80,1792]{1,0:T(8,128)(2,1)S(1)} %collective-permute-done.25, bf16[80,1792]{1,0:T(8,128)(2,1)S(1)} %get-tuple-element.73), kind=kOutput, calls=%fused_computation.2 | convolution fusion | flops 1175552000 | bytes 9224192 | tf_op jit(solution)/shard_map/dot_general | solution.py:11
  131.4 1.9 %collective-permute-done.29 = bf16[40,1792]{1,0:T(8,128)(2,1)S(1)} collective-permute-done((bf16[40,1792]{1,0:T(8,128)(2,1)S(1)}, bf16[40,1792]{1,0:T(8,128)(2,1)S(1)}, u32[]{:S(2)}, u32[]{:S(2)}) %collective-permute-start.29) | collective-permute-done | bytes 143392 | tf_op jit(solution)/shard_map/ppermute | solution.py:16
  133.4 1.3 collective-permute-start.31
  134.9 1.4 fusion.25
  136.5 2.7 %collective-permute-done.31 = bf16[40,1792]{1,0:T(8,128)(2,1)S(1)} collective-permute-done((bf16[40,1792]{1,0:T(8,128)(2,1)S(1)}, bf16[40,1792]{1,0:T(8,128)(2,1)S(1)}, u32[]{:S(2)}, u32[]{:S(2)}) %collective-permute-start.31) | collective-permute-done | bytes 143392 | tf_op jit(solution)/shard_map/ppermute | solution.py:16
  139.1 4.1 %collective-permute-done.33 = bf16[80,1792]{1,0:T(8,128)(2,1)S(1)} collective-permute-done((bf16[80,1792]{1,0:T(8,128)(2,1)S(1)}, bf16[80,1792]{1,0:T(8,128)(2,1)S(1)}, u32[]{:S(2)}, u32[]{:S(2)}) %collective-permute-start.33) | collective-permute-done | bytes 286752 | tf_op jit(solution)/shard_map/ppermute | solution.py:16
  143.8 7.1 %collective-permute-done.35 = bf16[80,1792]{1,0:T(8,128)(2,1)S(1)} collective-permute-done((bf16[80,1792]{1,0:T(8,128)(2,1)S(1)}, bf16[80,1792]{1,0:T(8,128)(2,1)S(1)}, u32[]{:S(2)}, u32[]{:S(2)}) %collective-permute-start.35) | collective-permute-done | bytes 286752 | tf_op jit(solution)/shard_map/ppermute | solution.py:16
  151.1 0.8 collective-permute-start.32
  151.9 0.7 collective-permute-done.36
  152.6 1.4 fusion
  154.1 1.5 fusion.28
  155.8 5.5 %collective-permute-done.32 = bf16[80,2048]{1,0:T(8,128)(2,1)S(1)} collective-permute-done((bf16[80,2048]{1,0:T(8,128)(2,1)S(1)}, bf16[80,2048]{1,0:T(8,128)(2,1)S(1)}, u32[]{:S(2)}, u32[]{:S(2)}) %collective-permute-start.32) | collective-permute-done | bytes 327712 | tf_op jit(solution)/shard_map/ppermute | solution.py:16
  161.4 0.8 collective-permute-start.38
  162.3 8.5 %collective-permute-done.38 = bf16[80,2048]{1,0:T(8,128)(2,1)S(1)} collective-permute-done((bf16[80,2048]{1,0:T(8,128)(2,1)S(1)}, bf16[80,2048]{1,0:T(8,128)(2,1)S(1)}, u32[]{:S(2)}, u32[]{:S(2)}) %collective-permute-start.38) | collective-permute-done | bytes 327712 | tf_op jit(solution)/shard_map/ppermute | solution.py:16
  171.0 0.9 select_convert_fusion
  172.0 2.1 %collective-permute-done.39 = bf16[160,2048]{1,0:T(8,128)(2,1)S(1)} collective-permute-done((bf16[160,2048]{1,0:T(8,128)(2,1)S(1)}, bf16[160,2048]{1,0:T(8,128)(2,1)S(1)}, u32[]{:S(2)}, u32[]{:S(2)}) %collective-permute-start.39) | collective-permute-done | bytes 655392 | tf_op jit(solution)/shard_map/ppermute | solution.py:16
  174.0 1.9 %fusion.34 = bf16[160,2048]{1,0:T(8,128)(2,1)} fusion(bf16[160,2048]{1,0:T(8,128)(2,1)S(1)} %collective-permute-done.39, bf16[160,2048]{1,0:T(8,128)(2,1)S(1)} %copy-done, f32[80,2048]{1,0:T(8,128)S(1)} %convert_add_fusion, f32[80,2048]{1,0:T(8,128)S(1)} %convert_add_fusion.1, pred[160]{0:T(512)(128)(4,1)S(1)} %get-tuple-element.59, ...), kind=kOutput, calls=%fused_computation.35 | convolution fusion | flops 631137280 | bytes 3278240 | tf_op jit(solution)/shard_map/dot_general | solution.py:131
  (126 shorter events, 6.3 us)
Async XLA Ops:
  0.0 5.8 %collective-permute-start = (bf16[160,2048]{1,0:T(8,128)(2,1)}, bf16[160,2048]{1,0:T(8,128)(2,1)S(1)}, u32[]{:S(2)}, u32[]{:S(2)}) collective-permute-start(bf16[160,2048]{1,0:T(8,128)(2,1)} %param.5), channel_id=1, source_target_pairs={{0,1},{1,0},{2,3},{3,2},{4,5},{5,4},{6,7},{7,6},{8,9},{9,8},{10,11... | collective-permute-start | bytes 1966088 | tf_op jit(solution)/shard_map/ppermute | solution.py:16
  5.8 2.9 %copy-start = (bf16[160,2048]{1,0:T(8,128)(2,1)S(1)}, bf16[160,2048]{1,0:T(8,128)(2,1)}, u32[]{:S(2)}) copy-start(bf16[160,2048]{1,0:T(8,128)(2,1)} %param.5) | copy-start | bytes 1966084
  6.2 7.4 %collective-permute-start.1 = (bf16[40,2048]{1,0:T(8,128)(2,1)S(1)}, bf16[40,2048]{1,0:T(8,128)(2,1)S(1)}, u32[]{:S(2)}, u32[]{:S(2)}) collective-permute-start(bf16[40,2048]{1,0:T(8,128)(2,1)S(1)} %slice.289), channel_id=1, source_target_pairs={{0,2},{1,3},{2,0},{3,1},{4,6},{5,7},{6,4},{7,5},{8,10},{9,11},{10,... | collective-permute-start | bytes 491528 | tf_op jit(solution)/shard_map/ppermute | solution.py:16
  13.6 10.5 %collective-permute-start.2 = (bf16[40,2048]{1,0:T(8,128)(2,1)S(1)}, bf16[40,2048]{1,0:T(8,128)(2,1)S(1)}, u32[]{:S(2)}, u32[]{:S(2)}) collective-permute-start(bf16[40,2048]{1,0:T(8,128)(2,1)S(1)} %slice_add_fusion.19), channel_id=1, source_target_pairs={{0,8},{4,12},{8,0},{12,4},{1,9},{5,13},{9,1},{13,5},{2,10},{6,14},... | collective-permute-start | bytes 491528 | tf_op jit(solution)/shard_map/ppermute | solution.py:16
  16.8 7.3 %collective-permute-start.3 = (bf16[40,2048]{1,0:T(8,128)(2,1)S(1)}, bf16[40,2048]{1,0:T(8,128)(2,1)S(1)}, u32[]{:S(2)}, u32[]{:S(2)}) collective-permute-start(bf16[40,2048]{1,0:T(8,128)(2,1)S(1)} %slice.290), channel_id=1, source_target_pairs={{0,2},{1,3},{2,0},{3,1},{4,6},{5,7},{6,4},{7,5},{8,10},{9,11},{10,... | collective-permute-start | bytes 491528 | tf_op jit(solution)/shard_map/ppermute | solution.py:16
  24.2 5.4 %collective-permute-start.4 = (bf16[40,2048]{1,0:T(8,128)(2,1)S(1)}, bf16[40,2048]{1,0:T(8,128)(2,1)S(1)}, u32[]{:S(2)}, u32[]{:S(2)}) collective-permute-start(bf16[40,2048]{1,0:T(8,128)(2,1)S(1)} %get-tuple-element.33), channel_id=1, source_target_pairs={{0,2},{1,3},{2,0},{3,1},{4,6},{5,7},{6,4},{7,5},{8,10},{9,11},{10,... | collective-permute-start | bytes 491528 | tf_op jit(solution)/shard_map/ppermute | solution.py:16
  25.8 9.5 %collective-permute-start.5 = (bf16[40,2048]{1,0:T(8,128)(2,1)S(1)}, bf16[40,2048]{1,0:T(8,128)(2,1)S(1)}, u32[]{:S(2)}, u32[]{:S(2)}) collective-permute-start(bf16[40,2048]{1,0:T(8,128)(2,1)S(1)} %slice_add_fusion.18), channel_id=1, source_target_pairs={{0,8},{4,12},{8,0},{12,4},{1,9},{5,13},{9,1},{13,5},{2,10},{6,14},... | collective-permute-start | bytes 491528 | tf_op jit(solution)/shard_map/ppermute | solution.py:16
  35.3 7.1 %collective-permute-start.6 = (bf16[80,2048]{1,0:T(8,128)(2,1)S(1)}, bf16[80,2048]{1,0:T(8,128)(2,1)S(1)}, u32[]{:S(2)}, u32[]{:S(2)}) collective-permute-start(bf16[80,2048]{1,0:T(8,128)(2,1)S(1)} %pad_maximum_fusion.11), channel_id=1, source_target_pairs={{0,4},{4,0},{8,12},{12,8},{1,5},{5,1},{9,13},{13,9},{2,6},{6,2},{1... | collective-permute-start | bytes 983048 | tf_op jit(solution)/shard_map/ppermute | solution.py:16
  35.3 13.5 %copy-start.1 = (bf16[2048,3584]{1,0:T(8,128)(2,1)S(1)}, bf16[2048,3584]{1,0:T(8,128)(2,1)}, u32[]{:S(2)}) copy-start(bf16[2048,3584]{1,0:T(8,128)(2,1)} %param.8) | copy-start | bytes 44040196
  35.3 7.5 %collective-permute-start.9 = (bf16[40,2048]{1,0:T(8,128)(2,1)S(1)}, bf16[40,2048]{1,0:T(8,128)(2,1)S(1)}, u32[]{:S(2)}, u32[]{:S(2)}) collective-permute-start(bf16[40,2048]{1,0:T(8,128)(2,1)S(1)} %get-tuple-element.36), channel_id=1, source_target_pairs={{0,2},{1,3},{2,0},{3,1},{4,6},{5,7},{6,4},{7,5},{8,10},{9,11},{10,... | collective-permute-start | bytes 491528 | tf_op jit(solution)/shard_map/ppermute | solution.py:16
  42.5 1.7 collective-permute-start.7
  42.9 10.2 %collective-permute-start.11 = (bf16[80,2048]{1,0:T(8,128)(2,1)S(1)}, bf16[80,2048]{1,0:T(8,128)(2,1)S(1)}, u32[]{:S(2)}, u32[]{:S(2)}) collective-permute-start(bf16[80,2048]{1,0:T(8,128)(2,1)S(1)} %pad_maximum_fusion.12), channel_id=1, source_target_pairs={{0,4},{4,0},{8,12},{12,8},{1,5},{5,1},{9,13},{13,9},{2,6},{6,2},{1... | collective-permute-start | bytes 983048 | tf_op jit(solution)/shard_map/ppermute | solution.py:16
  44.2 9.1 %slice-start = ((s8[14680064]{0:T(1024)(128)(4,1)}), s8[4194304]{0:T(1024)(128)(4,1)S(1)}, s32[]{:S(2)}) async-start(s8[14680064]{0:T(1024)(128)(4,1)} %bitcast.122), calls=%async_computation | async-start | bytes 8388608
  44.2 9.1 %slice-start.1 = ((s8[14680064]{0:T(1024)(128)(4,1)}), s8[4194304]{0:T(1024)(128)(4,1)S(1)}, s32[]{:S(2)}) async-start(s8[14680064]{0:T(1024)(128)(4,1)} %bitcast.122), calls=%async_computation.1 | async-start | bytes 8388608
  48.9 4.5 %slice-start.2 = ((s8[14680064]{0:T(1024)(128)(4,1)}), s8[4194304]{0:T(1024)(128)(4,1)S(1)}, s32[]{:S(2)}) async-start(s8[14680064]{0:T(1024)(128)(4,1)} %bitcast.122), calls=%async_computation.2 | async-start | bytes 8388608
  48.9 4.5 %slice-start.3 = ((s8[14680064]{0:T(1024)(128)(4,1)}), s8[2097152]{0:T(1024)(128)(4,1)S(1)}, s32[]{:S(2)}) async-start(s8[14680064]{0:T(1024)(128)(4,1)} %bitcast.122), calls=%async_computation.3 | async-start | bytes 4194304
  50.4 2.9 %collective-permute-start.8 = (bf16[2,80,1792]{2,1,0:T(8,128)(2,1)S(1)}, bf16[2,80,1792]{2,1,0:T(8,128)(2,1)S(1)}, u32[]{:S(2)}, u32[]{:S(2)}) collective-permute-start(bf16[2,80,1792]{2,1,0:T(8,128)(2,1)S(1)} %pad_maximum_fusion.7), channel_id=1, source_target_pairs={{0,1},{1,0},{2,3},{3,2},{4,5},{5,4},{6,7},{7,6},{8,9},{9,8},{10,11... | collective-permute-start | bytes 1720328 | tf_op jit(solution)/shard_map/ppermute | solution.py:16
  53.2 14.5 %collective-permute-start.19 = (bf16[80,2048]{1,0:T(8,128)(2,1)S(1)}, bf16[80,2048]{1,0:T(8,128)(2,1)S(1)}, u32[]{:S(2)}, u32[]{:S(2)}) collective-permute-start(bf16[80,2048]{1,0:T(8,128)(2,1)S(1)} %get-tuple-element.70), channel_id=1, source_target_pairs={{0,1},{1,0},{2,3},{3,2},{4,5},{5,4},{6,7},{7,6},{8,9},{9,8},{10,11... | collective-permute-start | bytes 983048 | tf_op jit(solution)/shard_map/ppermute | solution.py:16
  56.4 9.3 %collective-permute-start.10 = (bf16[2,40,1792]{2,1,0:T(8,128)(2,1)S(1)}, bf16[2,40,1792]{2,1,0:T(8,128)(2,1)S(1)}, u32[]{:S(2)}, u32[]{:S(2)}) collective-permute-start(bf16[2,40,1792]{2,1,0:T(8,128)(2,1)S(1)} %pad_maximum_fusion.13), channel_id=1, source_target_pairs={{0,2},{1,3},{2,0},{3,1},{4,6},{5,7},{6,4},{7,5},{8,10},{9,11},{10,... | collective-permute-start | bytes 860168 | tf_op jit(solution)/shard_map/ppermute | solution.py:16
  57.1 18.1 %collective-permute-start.13 = (bf16[2,80,1792]{2,1,0:T(8,128)(2,1)S(1)}, bf16[2,80,1792]{2,1,0:T(8,128)(2,1)S(1)}, u32[]{:S(2)}, u32[]{:S(2)}) collective-permute-start(bf16[2,80,1792]{2,1,0:T(8,128)(2,1)S(1)} %pad_maximum_fusion.8), channel_id=1, source_target_pairs={{0,1},{1,0},{2,3},{3,2},{4,5},{5,4},{6,7},{7,6},{8,9},{9,8},{10,11... | collective-permute-start | bytes 1720328 | tf_op jit(solution)/shard_map/ppermute | solution.py:16
  65.8 9.4 %collective-permute-start.12 = (bf16[40,1792]{1,0:T(8,128)(2,1)S(1)}, bf16[40,1792]{1,0:T(8,128)(2,1)S(1)}, u32[]{:S(2)}, u32[]{:S(2)}) collective-permute-start(bf16[40,1792]{1,0:T(8,128)(2,1)S(1)} %fusion.65), channel_id=1, source_target_pairs={{0,8},{4,12},{8,0},{12,4},{1,9},{5,13},{9,1},{13,5},{2,10},{6,14},... | collective-permute-start | bytes 430088 | tf_op jit(solution)/shard_map/ppermute | solution.py:16
  78.2 8.4 %collective-permute-start.14 = (bf16[2,40,1792]{2,1,0:T(8,128)(2,1)S(1)}, bf16[2,40,1792]{2,1,0:T(8,128)(2,1)S(1)}, u32[]{:S(2)}, u32[]{:S(2)}) collective-permute-start(bf16[2,40,1792]{2,1,0:T(8,128)(2,1)S(1)} %pad_maximum_fusion.14), channel_id=1, source_target_pairs={{0,2},{1,3},{2,0},{3,1},{4,6},{5,7},{6,4},{7,5},{8,10},{9,11},{10,... | collective-permute-start | bytes 860168 | tf_op jit(solution)/shard_map/ppermute | solution.py:16
  79.0 16.7 %collective-permute-start.20 = (bf16[2,80,1792]{2,1,0:T(8,128)(2,1)S(1)}, bf16[2,80,1792]{2,1,0:T(8,128)(2,1)S(1)}, u32[]{:S(2)}, u32[]{:S(2)}) collective-permute-start(bf16[2,80,1792]{2,1,0:T(8,128)(2,1)S(1)} %pad_maximum_fusion.9), channel_id=1, source_target_pairs={{0,1},{1,0},{2,3},{3,2},{4,5},{5,4},{6,7},{7,6},{8,9},{9,8},{10,11... | collective-permute-start | bytes 1720328 | tf_op jit(solution)/shard_map/ppermute | solution.py:16
  86.7 5.1 %collective-permute-start.15 = (bf16[40,1792]{1,0:T(8,128)(2,1)S(1)}, bf16[40,1792]{1,0:T(8,128)(2,1)S(1)}, u32[]{:S(2)}, u32[]{:S(2)}) collective-permute-start(bf16[40,1792]{1,0:T(8,128)(2,1)S(1)} %get-tuple-element.42), channel_id=1, source_target_pairs={{0,2},{1,3},{2,0},{3,1},{4,6},{5,7},{6,4},{7,5},{8,10},{9,11},{10,... | collective-permute-start | bytes 430088 | tf_op jit(solution)/shard_map/ppermute | solution.py:16
  87.4 8.2 %collective-permute-start.16 = (bf16[40,1792]{1,0:T(8,128)(2,1)S(1)}, bf16[40,1792]{1,0:T(8,128)(2,1)S(1)}, u32[]{:S(2)}, u32[]{:S(2)}) collective-permute-start(bf16[40,1792]{1,0:T(8,128)(2,1)S(1)} %fusion.63), channel_id=1, source_target_pairs={{0,8},{4,12},{8,0},{12,4},{1,9},{5,13},{9,1},{13,5},{2,10},{6,14},... | collective-permute-start | bytes 430088 | tf_op jit(solution)/shard_map/ppermute | solution.py:16
  95.6 7.9 %collective-permute-start.17 = (bf16[80,1792]{1,0:T(8,128)(2,1)S(1)}, bf16[80,1792]{1,0:T(8,128)(2,1)S(1)}, u32[]{:S(2)}, u32[]{:S(2)}) collective-permute-start(bf16[80,1792]{1,0:T(8,128)(2,1)S(1)} %pad_maximum_fusion.15), channel_id=1, source_target_pairs={{0,4},{4,0},{8,12},{12,8},{1,5},{5,1},{9,13},{13,9},{2,6},{6,2},{1... | collective-permute-start | bytes 860168 | tf_op jit(solution)/shard_map/ppermute | solution.py:16
  97.2 37.6 %slice-start.4 = ((s8[14680064]{0:T(1024)(128)(4,1)}), s8[2097152]{0:T(1024)(128)(4,1)S(1)}, s32[]{:S(2)}) async-start(s8[14680064]{0:T(1024)(128)(4,1)} %bitcast.124), calls=%async_computation.4 | async-start | bytes 4194304
  97.2 37.6 %slice-start.5 = ((s8[14680064]{0:T(1024)(128)(4,1)}), s8[4194304]{0:T(1024)(128)(4,1)S(1)}, s32[]{:S(2)}) async-start(s8[14680064]{0:T(1024)(128)(4,1)} %bitcast.124), calls=%async_computation.5 | async-start | bytes 8388608
  98.9 7.9 %collective-permute-start.21 = (bf16[2,40,1792]{2,1,0:T(8,128)(2,1)S(1)}, bf16[2,40,1792]{2,1,0:T(8,128)(2,1)S(1)}, u32[]{:S(2)}, u32[]{:S(2)}) collective-permute-start(bf16[2,40,1792]{2,1,0:T(8,128)(2,1)S(1)} %pad_maximum_fusion.16), channel_id=1, source_target_pairs={{0,2},{1,3},{2,0},{3,1},{4,6},{5,7},{6,4},{7,5},{8,10},{9,11},{10,... | collective-permute-start | bytes 860168 | tf_op jit(solution)/shard_map/ppermute | solution.py:16
  100.4 15.7 %collective-permute-start.27 = (bf16[2,80,1792]{2,1,0:T(8,128)(2,1)S(1)}, bf16[2,80,1792]{2,1,0:T(8,128)(2,1)S(1)}, u32[]{:S(2)}, u32[]{:S(2)}) collective-permute-start(bf16[2,80,1792]{2,1,0:T(8,128)(2,1)S(1)} %pad_maximum_fusion.10), channel_id=1, source_target_pairs={{0,1},{1,0},{2,3},{3,2},{4,5},{5,4},{6,7},{7,6},{8,9},{9,8},{10,11... | collective-permute-start | bytes 1720328 | tf_op jit(solution)/shard_map/ppermute | solution.py:16
  103.6 31.3 %collective-permute-start.18 = (bf16[80,1792]{1,0:T(8,128)(2,1)S(1)}, bf16[80,1792]{1,0:T(8,128)(2,1)S(1)}, u32[]{:S(2)}, u32[]{:S(2)}) collective-permute-start(bf16[80,1792]{1,0:T(8,128)(2,1)S(1)} %get-tuple-element.72), channel_id=1, source_target_pairs={{0,1},{1,0},{2,3},{3,2},{4,5},{5,4},{6,7},{7,6},{8,9},{9,8},{10,11... | collective-permute-start | bytes 860168 | tf_op jit(solution)/shard_map/ppermute | solution.py:16
  106.8 5.1 %collective-permute-start.22 = (bf16[40,1792]{1,0:T(8,128)(2,1)S(1)}, bf16[40,1792]{1,0:T(8,128)(2,1)S(1)}, u32[]{:S(2)}, u32[]{:S(2)}) collective-permute-start(bf16[40,1792]{1,0:T(8,128)(2,1)S(1)} %get-tuple-element.47), channel_id=1, source_target_pairs={{0,2},{1,3},{2,0},{3,1},{4,6},{5,7},{6,4},{7,5},{8,10},{9,11},{10,... | collective-permute-start | bytes 430088 | tf_op jit(solution)/shard_map/ppermute | solution.py:16
  108.1 7.7 %collective-permute-start.23 = (bf16[40,1792]{1,0:T(8,128)(2,1)S(1)}, bf16[40,1792]{1,0:T(8,128)(2,1)S(1)}, u32[]{:S(2)}, u32[]{:S(2)}) collective-permute-start(bf16[40,1792]{1,0:T(8,128)(2,1)S(1)} %fusion.61), channel_id=1, source_target_pairs={{0,8},{4,12},{8,0},{12,4},{1,9},{5,13},{9,1},{13,5},{2,10},{6,14},... | collective-permute-start | bytes 430088 | tf_op jit(solution)/shard_map/ppermute | solution.py:16
  111.9 23.0 %slice-start.6 = ((s8[14680064]{0:T(1024)(128)(4,1)}), s8[4194304]{0:T(1024)(128)(4,1)S(1)}, s32[]{:S(2)}) async-start(s8[14680064]{0:T(1024)(128)(4,1)} %bitcast.124), calls=%async_computation.6 | async-start | bytes 8388608
  115.8 6.6 %collective-permute-start.24 = (bf16[80,1792]{1,0:T(8,128)(2,1)S(1)}, bf16[80,1792]{1,0:T(8,128)(2,1)S(1)}, u32[]{:S(2)}, u32[]{:S(2)}) collective-permute-start(bf16[80,1792]{1,0:T(8,128)(2,1)S(1)} %pad_maximum_fusion.17), channel_id=1, source_target_pairs={{0,4},{4,0},{8,12},{12,8},{1,5},{5,1},{9,13},{13,9},{2,6},{6,2},{1... | collective-permute-start | bytes 860168 | tf_op jit(solution)/shard_map/ppermute | solution.py:16
  116.3 6.7 %collective-permute-start.28 = (bf16[2,40,1792]{2,1,0:T(8,128)(2,1)S(1)}, bf16[2,40,1792]{2,1,0:T(8,128)(2,1)S(1)}, u32[]{:S(2)}, u32[]{:S(2)}) collective-permute-start(bf16[2,40,1792]{2,1,0:T(8,128)(2,1)S(1)} %pad_maximum_fusion.18), channel_id=1, source_target_pairs={{0,2},{1,3},{2,0},{3,1},{4,6},{5,7},{6,4},{7,5},{8,10},{9,11},{10,... | collective-permute-start | bytes 860168 | tf_op jit(solution)/shard_map/ppermute | solution.py:16
  122.6 4.2 %collective-permute-start.25 = (bf16[80,1792]{1,0:T(8,128)(2,1)S(1)}, bf16[80,1792]{1,0:T(8,128)(2,1)S(1)}, u32[]{:S(2)}, u32[]{:S(2)}) collective-permute-start(bf16[80,1792]{1,0:T(8,128)(2,1)S(1)} %get-tuple-element.74), channel_id=1, source_target_pairs={{0,1},{1,0},{2,3},{3,2},{4,5},{5,4},{6,7},{7,6},{8,9},{9,8},{10,11... | collective-permute-start | bytes 860168 | tf_op jit(solution)/shard_map/ppermute | solution.py:16
  123.0 10.4 %collective-permute-start.30 = (bf16[40,1792]{1,0:T(8,128)(2,1)S(1)}, bf16[40,1792]{1,0:T(8,128)(2,1)S(1)}, u32[]{:S(2)}, u32[]{:S(2)}) collective-permute-start(bf16[40,1792]{1,0:T(8,128)(2,1)S(1)} %get-tuple-element.53), channel_id=1, source_target_pairs={{0,2},{1,3},{2,0},{3,1},{4,6},{5,7},{6,4},{7,5},{8,10},{9,11},{10,... | collective-permute-start | bytes 430088 | tf_op jit(solution)/shard_map/ppermute | solution.py:16
  123.9 9.5 %collective-permute-start.29 = (bf16[40,1792]{1,0:T(8,128)(2,1)S(1)}, bf16[40,1792]{1,0:T(8,128)(2,1)S(1)}, u32[]{:S(2)}, u32[]{:S(2)}) collective-permute-start(bf16[40,1792]{1,0:T(8,128)(2,1)S(1)} %fusion.59), channel_id=1, source_target_pairs={{0,8},{4,12},{8,0},{12,4},{1,9},{5,13},{9,1},{13,5},{2,10},{6,14},... | collective-permute-start | bytes 430088 | tf_op jit(solution)/shard_map/ppermute | solution.py:16
  126.8 8.1 %slice-start.7 = ((s8[14680064]{0:T(1024)(128)(4,1)}), s8[4194304]{0:T(1024)(128)(4,1)S(1)}, s32[]{:S(2)}) async-start(s8[14680064]{0:T(1024)(128)(4,1)} %bitcast.124), calls=%async_computation.7 | async-start | bytes 8388608
  133.4 5.7 %collective-permute-start.31 = (bf16[40,1792]{1,0:T(8,128)(2,1)S(1)}, bf16[40,1792]{1,0:T(8,128)(2,1)S(1)}, u32[]{:S(2)}, u32[]{:S(2)}) collective-permute-start(bf16[40,1792]{1,0:T(8,128)(2,1)S(1)} %get-tuple-element.54), channel_id=1, source_target_pairs={{0,2},{1,3},{2,0},{3,1},{4,6},{5,7},{6,4},{7,5},{8,10},{9,11},{10,... | collective-permute-start | bytes 430088 | tf_op jit(solution)/shard_map/ppermute | solution.py:16
  134.7 8.5 %collective-permute-start.33 = (bf16[80,1792]{1,0:T(8,128)(2,1)S(1)}, bf16[80,1792]{1,0:T(8,128)(2,1)S(1)}, u32[]{:S(2)}, u32[]{:S(2)}) collective-permute-start(bf16[80,1792]{1,0:T(8,128)(2,1)S(1)} %pad_maximum_fusion.19), channel_id=1, source_target_pairs={{0,4},{4,0},{8,12},{12,8},{1,5},{5,1},{9,13},{13,9},{2,6},{6,2},{1... | collective-permute-start | bytes 860168 | tf_op jit(solution)/shard_map/ppermute | solution.py:16
  136.4 14.7 %collective-permute-start.26 = (bf16[80,2048]{1,0:T(8,128)(2,1)S(1)}, bf16[80,2048]{1,0:T(8,128)(2,1)S(1)}, u32[]{:S(2)}, u32[]{:S(2)}) collective-permute-start(bf16[80,2048]{1,0:T(8,128)(2,1)S(1)} %slice.527), channel_id=1, source_target_pairs={{0,1},{1,0},{2,3},{3,2},{4,5},{5,4},{6,7},{7,6},{8,9},{9,8},{10,11... | collective-permute-start | bytes 983048 | tf_op jit(solution)/shard_map/ppermute | solution.py:16
  143.3 7.6 %collective-permute-start.35 = (bf16[80,1792]{1,0:T(8,128)(2,1)S(1)}, bf16[80,1792]{1,0:T(8,128)(2,1)S(1)}, u32[]{:S(2)}, u32[]{:S(2)}) collective-permute-start(bf16[80,1792]{1,0:T(8,128)(2,1)S(1)} %pad_maximum_fusion.20), channel_id=1, source_target_pairs={{0,4},{4,0},{8,12},{12,8},{1,5},{5,1},{9,13},{13,9},{2,6},{6,2},{1... | collective-permute-start | bytes 860168 | tf_op jit(solution)/shard_map/ppermute | solution.py:16
  143.7 10.4 %collective-permute-start.34 = (bf16[80,1792]{1,0:T(8,128)(2,1)S(1)}, bf16[80,1792]{1,0:T(8,128)(2,1)S(1)}, u32[]{:S(2)}, u32[]{:S(2)}) collective-permute-start(bf16[80,1792]{1,0:T(8,128)(2,1)S(1)} %get-tuple-element.76), channel_id=1, source_target_pairs={{0,1},{1,0},{2,3},{3,2},{4,5},{5,4},{6,7},{7,6},{8,9},{9,8},{10,11... | collective-permute-start | bytes 860168 | tf_op jit(solution)/shard_map/ppermute | solution.py:16
  151.0 1.6 collective-permute-start.36
  151.1 10.2 %collective-permute-start.32 = (bf16[80,2048]{1,0:T(8,128)(2,1)S(1)}, bf16[80,2048]{1,0:T(8,128)(2,1)S(1)}, u32[]{:S(2)}, u32[]{:S(2)}) collective-permute-start(bf16[80,2048]{1,0:T(8,128)(2,1)S(1)} %fusion.48), channel_id=1, source_target_pairs={{0,2},{1,3},{2,0},{3,1},{4,6},{5,7},{6,4},{7,5},{8,10},{9,11},{10,... | collective-permute-start | bytes 983048 | tf_op jit(solution)/shard_map/ppermute | solution.py:16
  155.6 5.8 %collective-permute-start.37 = (bf16[80,2048]{1,0:T(8,128)(2,1)S(1)}, bf16[80,2048]{1,0:T(8,128)(2,1)S(1)}, u32[]{:S(2)}, u32[]{:S(2)}) collective-permute-start(bf16[80,2048]{1,0:T(8,128)(2,1)S(1)} %slice.526), channel_id=1, source_target_pairs={{0,1},{1,0},{2,3},{3,2},{4,5},{5,4},{6,7},{7,6},{8,9},{9,8},{10,11... | collective-permute-start | bytes 983048 | tf_op jit(solution)/shard_map/ppermute | solution.py:16
  161.4 9.4 %collective-permute-start.38 = (bf16[80,2048]{1,0:T(8,128)(2,1)S(1)}, bf16[80,2048]{1,0:T(8,128)(2,1)S(1)}, u32[]{:S(2)}, u32[]{:S(2)}) collective-permute-start(bf16[80,2048]{1,0:T(8,128)(2,1)S(1)} %fusion.49), channel_id=1, source_target_pairs={{0,2},{1,3},{2,0},{3,1},{4,6},{5,7},{6,4},{7,5},{8,10},{9,11},{10,... | collective-permute-start | bytes 983048 | tf_op jit(solution)/shard_map/ppermute | solution.py:16
  171.9 2.2 %collective-permute-start.39 = (bf16[160,2048]{1,0:T(8,128)(2,1)S(1)}, bf16[160,2048]{1,0:T(8,128)(2,1)S(1)}, u32[]{:S(2)}, u32[]{:S(2)}) collective-permute-start(bf16[160,2048]{1,0:T(8,128)(2,1)S(1)} %select_convert_fusion), channel_id=1, source_target_pairs={{0,1},{1,0},{2,3},{3,2},{4,5},{5,4},{6,7},{7,6},{8,9},{9,8},{10,11... | collective-permute-start | bytes 1966088 | tf_op jit(solution)/shard_map/ppermute | solution.py:16

commit v4 on v3

v4 whole, which is shorter than its diff:
```python
import jax
import jax.numpy as jnp
from jax import lax
from jax.sharding import PartitionSpec as P

UNIT_CHUNKS = 2
HALVES = 2
ORDER = (
    "t0 t0 t1 t0 t1 t0 c00 c01 c00 c01 "
    "t1 t1 c10 c11 c00 c10 c01 c11 c00 "
    "c10 c01 c11 c00 c10 c01 b0 c11 "
    "b0 c10 c11 b1 b0 b1 b1"
)


def dot(a, b):
    return jnp.dot(a, b, preferred_element_type=jnp.float32)


def flip(value, axis, bit):
    count = lax.axis_size(axis)
    return lax.ppermute(value, axis, [(i, i ^ bit) for i in range(count)])


def stationary(tokens, lengths, gate_weight, up_weight, down_weight):
    slots, width = tokens.shape
    units = gate_weight.shape[1]
    col_count = lax.axis_size("col")
    c = lax.axis_index("col")
    r = lax.axis_index("row")
    x, k, zh, zl = c // 2, c % 2, r // 2, r % 2
    quarter = slots // 2
    piece = quarter // HALVES
    half = 2 * piece
    step = units // UNIT_CHUNKS

    rows = jnp.arange(lengths.shape[0], dtype=jnp.int32)
    slot = jnp.arange(slots, dtype=jnp.int32)
    places = []
    for row in (c, c ^ 1):
        first = jnp.sum(jnp.where(rows < row, lengths, 0))
        count = jnp.sum(jnp.where(rows == row, lengths, 0))
        places.append(jnp.where(slot < count, slot + first, -1))
    inside = jnp.arange(piece, dtype=jnp.int32)
    mine = [
        jnp.concatenate([inside + quarter * c, inside + quarter * (c ^ 2)]) + h * piece
        for h in range(HALVES)
    ]

    devices = [(i // col_count, i % col_count) for i in range(lax.axis_size("row") * col_count)]

    def move(value, where_to):
        pairs = []
        for i, (row, col) in enumerate(devices):
            to = where_to(row // 2, row % 2, col // 2, col % 2)
            if to is not None:
                to_zh, to_zl, to_x, to_k = to
                pairs.append((i, (to_zh * 2 + to_zl) * col_count + to_x * 2 + to_k))
        return lax.ppermute(value, ("row", "col"), pairs)

    def one_step(value, stay, first_to, second_to):
        first, second = move(value, first_to), move(value, second_to)

        def finish(value):
            return jnp.concatenate(
                [jnp.where(stay, value, first), jnp.where(stay, first, second)], axis=0
            )

        return finish

    def to_columns(value):
        return one_step(
            value,
            zh == x,
            lambda zh, zl, x, k: (1 - zh, zl, x, k) if x == zh else (zh, zl, 1 - x, k),
            lambda zh, zl, x, k: None if x == zh else (1 - zh, zl, 1 - x, k),
        )

    def to_cores(value):
        return one_step(
            value,
            zl == k,
            lambda zh, zl, x, k: (zh, 1 - zl, x, k) if k == zl else (zh, zl, x, 1 - k),
            lambda zh, zl, x, k: None if k == zl else (zh, 1 - zl, x, 1 - k),
        )

    sibling = flip(tokens, "col", 1)
    last = []

    def ordered(value):
        if last:
            value = lax.optimization_barrier((value, last[-1]))[0]
        return value

    def issued(value):
        last.append(value)
        return value

    def spread_steps(value):
        finish = to_columns(value)
        yield
        pair = issued(finish(ordered(value)))
        finish = to_cores(pair)
        yield
        whole = issued(finish(ordered(pair)))
        return whole

    def half_steps(h):
        own_pick = (mine[h][:, None] == places[0][None]).astype(jnp.bfloat16)
        sib_pick = (mine[h][:, None] == places[1][None]).astype(jnp.bfloat16)
        picked = dot(own_pick, tokens) + dot(ordered(sib_pick), sibling)
        picked = issued(picked.astype(jnp.bfloat16))
        got = flip(picked[piece:], "col", 2)
        yield
        own = issued(ordered(picked[:piece]) + got)
        return (yield from spread_steps(own))

    def chunk_steps(full, i):
        part = slice(i * step, (i + 1) * step)
        full = ordered(full)
        gate, up = dot(full, gate_weight[:, part]), dot(full, up_weight[:, part])
        send = issued(jnp.stack([gate[half:], up[half:]]).astype(jnp.bfloat16))
        got = flip(send, "col", 1)
        yield
        got = ordered(got)
        gate, up = gate[:half] + got[0], up[:half] + got[1]
        send = issued(jnp.stack([gate[piece:], up[piece:]]).astype(jnp.bfloat16))
        got = flip(send, "col", 2)
        yield
        got = ordered(got)
        gate, up = gate[:piece] + got[0], up[:piece] + got[1]
        hidden = issued((jax.nn.silu(gate) * up).astype(jnp.bfloat16))
        whole = yield from spread_steps(hidden)
        return issued(dot(ordered(whole), down_weight[part]))

    def branch_steps(parts):
        branch = issued(sum(parts[1:], parts[0]))
        got = flip(branch[half:].astype(jnp.bfloat16), "col", 1)
        yield
        total = issued(branch[:half] + ordered(got))
        got = flip(total.astype(jnp.bfloat16), "col", 2)
        yield
        got = ordered(got)
        return issued(total + jnp.concatenate([got[piece:], got[:piece]], axis=0))

    chains, results = {}, {}

    def advance(name):
        if name not in chains:
            kind, rest = name[0], name[1:]
            if kind == "t":
                chains[name] = half_steps(int(rest))
            elif kind == "c":
                chains[name] = chunk_steps(results["t" + rest[0]], int(rest[1]))
            else:
                parts = [results["c" + rest + str(i)] for i in range(UNIT_CHUNKS)]
                chains[name] = branch_steps(parts)
        try:
            next(chains[name])
        except StopIteration as stop:
            results[name] = stop.value

    for name in ORDER.split():
        advance(name)

    total = jnp.concatenate([results["b" + str(h)] for h in range(HALVES)])
    mixed = []
    for place, known in zip(places, (tokens, sibling)):
        put = place[:, None] == jnp.concatenate(mine)[None]
        moved = jnp.dot(put.astype(jnp.float32), total, precision=lax.Precision.HIGHEST)
        handled = jnp.any(put, axis=1)[:, None]
        mixed.append(jnp.where(handled, known.astype(jnp.float32) + moved, 0.0).astype(jnp.bfloat16))
    return mixed[0] + flip(mixed[1], "col", 1)


def general(tokens, lengths, gate_weight, up_weight, down_weight):
    c = lax.axis_index("col")
    slots = tokens.shape[0]
    whole = lax.all_gather(tokens, "row", axis=1, tiled=True)
    whole = lax.all_gather(whole, "col", axis=0, tiled=True)
    depth = gate_weight.shape[0]
    block = lax.dynamic_slice_in_dim(whole, c * depth, depth, axis=1)

    def summed(a, b):
        return lax.psum_scatter(dot(a, b), "col", scatter_dimension=0, tiled=True)

    hidden = (jax.nn.silu(summed(block, gate_weight)) * summed(block, up_weight)).astype(jnp.bfloat16)
    hidden = lax.all_gather(hidden, "row", axis=1, tiled=True)
    hidden = lax.all_gather(hidden, "col", axis=0, tiled=True)
    depth = down_weight.shape[0]
    branch = summed(lax.dynamic_slice_in_dim(hidden, c * depth, depth, axis=1), down_weight)
    valid = jnp.arange(slots, dtype=jnp.int32) < jnp.take(lengths, c)
    total = tokens.astype(jnp.float32) + branch
    return jnp.where(valid[:, None], total, jnp.float32(0.0)).astype(jnp.bfloat16)


def solution(mesh):
    square = mesh.shape["row"] == 4 and mesh.shape["col"] == 4
    in_specs = (
        P(("groups", "col"), "row"),
        P("groups"),
        P("col", "row"),
        P("col", "row"),
        P("col", "row"),
    )
    out_specs = P(("groups", "col"), "row")
    return jax.shard_map(
        stationary if square else general,
        mesh=mesh, in_specs=in_specs, out_specs=out_specs, check_vma=False,
    )
```

time: 176 us -> 155 us (0.88)
  waiting for transfers between devices: 110 us -> 39.3 us
  starting transfers between devices: 28.7 us -> 71.4 us
  matrix products: 28.5 us -> 34.1 us
    ppermute x40 -> x16, waiting for transfers between devices: 110 us -> 29.6 us  [flip(): return lax.ppermute(value, axis, [(i, i ^ bit) for i in range(count)])]
    ppermute x0 -> x24, starting transfers between devices: none -> 37.2 us  [move(): return lax.ppermute(value, ('row', 'col'), pairs)]
    ppermute x0 -> x24, waiting for transfers between devices: none -> 9.68 us  [move(): return lax.ppermute(value, ('row', 'col'), pairs)]
    dot_general x16, matrix products: 25.7 us -> 32.3 us  [dot(): return jnp.dot(a, b, preferred_element_type=jnp.float32)]
    ppermute x40 -> x16, starting transfers between devices: 28.7 us -> 34.2 us  [flip(): return lax.ppermute(value, axis, [(i, i ^ bit) for i in range(count)])]
  transfers between devices with their start and end apart: 40 -> 40, of which waited for: 26 -> 12; matrix products, arithmetic and copies ran while one was open for 17% -> 26% of each run, Pallas kernels for 0% -> 0%
where the time goes in v4:
time: 155 us
  starting transfers between devices  71.4 us (46%)
  waiting for transfers between devices  39.3 us (25%)
  matrix products  34.1 us (22%)
  other arithmetic  8.01 us (5%)
    ppermute x24, starting transfers between devices, move(): return lax.ppermute(value, ('row', 'col'), pairs)  37.2 us
    ppermute x16, starting transfers between devices, flip(): return lax.ppermute(value, axis, [(i, i ^ bit) for i in range(count)])  34.2 us
    dot_general x16, matrix products, dot(): return jnp.dot(a, b, preferred_element_type=jnp.float32)  32.3 us
    ppermute x16, waiting for transfers between devices, flip(): return lax.ppermute(value, axis, [(i, i ^ bit) for i in range(count)])  29.6 us
    ppermute x24, waiting for transfers between devices, move(): return lax.ppermute(value, ('row', 'col'), pairs)  9.68 us
  transfers between devices with their start and end apart: 40, of which 12 were waited for; matrix products, arithmetic and copies ran while one was open for 26% of the time, Pallas kernels for 0%

profile of v4, /device:TPU:0, one launch (start us, length us, event | category | flops | bytes accessed | tf_op | source)
XLA Modules:
  0.0 154.7 jit_solution(10512808505458799331)
XLA Ops:
  0.0 0.5 collective-permute-start
  0.5 1.4 fusion.78
  1.9 2.5 %compare_select_fusion.1 = (s32[160]{0:T(256)S(1)}, s32[160]{0:T(256)S(1)}) fusion(s32[]{:T(128)} %get-tuple-element.72, s32[]{:T(128)} %get-tuple-element.69, s32[]{:T(128)} %get-tuple-element.70, s32[]{:T(128)} %get-tuple-element.71), kind=kLoop, calls=%fused_computation.163 | loop fusion | flops 960 | bytes 1296 | tf_op jit(solution)/shard_map/jit(_where)/select_n | solution.py:43
  4.5 1.4 fusion.68
  6.5 2.6 %collective-permute-start.1 = (bf16[40,2048]{1,0:T(8,128)(2,1)S(1)}, bf16[40,2048]{1,0:T(8,128)(2,1)S(1)}, u32[]{:S(2)}, u32[]{:S(2)}) collective-permute-start(bf16[40,2048]{1,0:T(8,128)(2,1)S(1)} %get-tuple-element.97), channel_id=1, source_target_pairs={{0,2},{1,3},{2,0},{3,1},{4,6},{5,7},{6,4},{7,5},{8,10},{9,11},{10,... | collective-permute-start | bytes 491528 | tf_op jit(solution)/shard_map/ppermute | solution.py:22
  9.2 4.7 %collective-permute-done.1 = bf16[40,2048]{1,0:T(8,128)(2,1)S(1)} collective-permute-done((bf16[40,2048]{1,0:T(8,128)(2,1)S(1)}, bf16[40,2048]{1,0:T(8,128)(2,1)S(1)}, u32[]{:S(2)}, u32[]{:S(2)}) %collective-permute-start.1) | collective-permute-done | bytes 163872 | tf_op jit(solution)/shard_map/ppermute | solution.py:22
  14.0 2.9 %collective-permute-start.2 = (bf16[40,2048]{1,0:T(8,128)(2,1)S(1)}, bf16[40,2048]{1,0:T(8,128)(2,1)S(1)}, u32[]{:S(2)}, u32[]{:S(2)}) collective-permute-start(bf16[40,2048]{1,0:T(8,128)(2,1)S(1)} %add.180), channel_id=1, source_target_pairs={{0,8},{1,9},{2,0},{3,1},{4,12},{5,13},{6,4},{7,5},{8,10},{9,11},{1... | collective-permute-start | bytes 491528 | tf_op jit(solution)/shard_map/ppermute | solution.py:59
  16.9 0.7 collective-permute-start.3
  17.8 2.4 %collective-permute-done.2 = bf16[40,2048]{1,0:T(8,128)(2,1)S(1)} collective-permute-done((bf16[40,2048]{1,0:T(8,128)(2,1)S(1)}, bf16[40,2048]{1,0:T(8,128)(2,1)S(1)}, u32[]{:S(2)}, u32[]{:S(2)}) %collective-permute-start.2) | collective-permute-done | bytes 163872 | tf_op jit(solution)/shard_map/ppermute | solution.py:59
  20.3 5.0 %collective-permute-start.5 = (bf16[80,2048]{1,0:T(8,128)(2,1)S(1)}, bf16[80,2048]{1,0:T(8,128)(2,1)S(1)}, u32[]{:S(2)}, u32[]{:S(2)}) collective-permute-start(bf16[80,2048]{1,0:T(8,128)(2,1)S(1)} %pad_maximum_fusion.15), channel_id=1, source_target_pairs={{0,4},{1,0},{2,6},{3,2},{4,5},{5,1},{6,7},{7,3},{8,12},{9,8},{10,1... | collective-permute-start | bytes 983048 | tf_op jit(solution)/shard_map/ppermute | solution.py:59
  25.3 0.7 collective-permute-start.6
  26.0 4.7 %collective-permute-start.4 = (bf16[40,2048]{1,0:T(8,128)(2,1)S(1)}, bf16[40,2048]{1,0:T(8,128)(2,1)S(1)}, u32[]{:S(2)}, u32[]{:S(2)}) collective-permute-start(bf16[40,2048]{1,0:T(8,128)(2,1)S(1)} %get-tuple-element.95), channel_id=1, source_target_pairs={{0,2},{1,3},{2,0},{3,1},{4,6},{5,7},{6,4},{7,5},{8,10},{9,11},{10,... | collective-permute-start | bytes 491528 | tf_op jit(solution)/shard_map/ppermute | solution.py:22
  30.6 4.4 %collective-permute-done.4 = bf16[40,2048]{1,0:T(8,128)(2,1)S(1)} collective-permute-done((bf16[40,2048]{1,0:T(8,128)(2,1)S(1)}, bf16[40,2048]{1,0:T(8,128)(2,1)S(1)}, u32[]{:S(2)}, u32[]{:S(2)}) %collective-permute-start.4) | collective-permute-done | bytes 163872 | tf_op jit(solution)/shard_map/ppermute | solution.py:22
  35.1 5.3 %collective-permute-start.10 = (bf16[40,2048]{1,0:T(8,128)(2,1)S(1)}, bf16[40,2048]{1,0:T(8,128)(2,1)S(1)}, u32[]{:S(2)}, u32[]{:S(2)}) collective-permute-start(bf16[40,2048]{1,0:T(8,128)(2,1)S(1)} %add.182), channel_id=1, source_target_pairs={{0,8},{1,9},{2,0},{3,1},{4,12},{5,13},{6,4},{7,5},{8,10},{9,11},{1... | collective-permute-start | bytes 491528 | tf_op jit(solution)/shard_map/ppermute | solution.py:59
  40.4 0.7 collective-permute-start.11
  41.2 4.6 %fusion.22 = f32[160,1792]{1,0:T(8,128)S(1)} fusion(bf16[160,2048]{1,0:T(8,128)(2,1)S(1)} %pad_maximum_fusion.5, bf16[2048,3584]{1,0:T(8,128)(2,1)} %param.7), kind=kOutput, calls=%fused_computation.22 | convolution fusion | flops 1174405120 | bytes 9142272 | tf_op jit(solution)/shard_map/dot_general | solution.py:17
  45.9 5.3 %fusion.18 = f32[160,1792]{1,0:T(8,128)S(1)} fusion(bf16[160,2048]{1,0:T(8,128)(2,1)S(1)} %pad_maximum_fusion.5, bf16[2048,3584]{1,0:T(8,128)(2,1)} %param.8), kind=kOutput, calls=%fused_computation.18 | convolution fusion | flops 1174405120 | bytes 9142272 | tf_op jit(solution)/shard_map/dot_general | solution.py:17
  51.3 1.4 fusion.14
  52.7 4.6 %fusion.10 = f32[160,1792]{1,0:T(8,128)S(1)} fusion(bf16[160,2048]{1,0:T(8,128)(2,1)S(1)} %pad_maximum_fusion.5, bf16[2048,3584]{1,0:T(8,128)(2,1)} %param.8), kind=kOutput, calls=%fused_computation.10 | convolution fusion | flops 1174405120 | bytes 9142272 | tf_op jit(solution)/shard_map/dot_general | solution.py:17
  57.5 0.6 collective-permute-start.9
  58.1 1.3 collective-permute-done.7
  59.6 0.6 collective-permute-done.9
  60.5 1.0 collective-permute-start.13
  61.5 2.8 %collective-permute-start.8 = (bf16[2,40,1792]{2,1,0:T(8,128)(2,1)S(1)}, bf16[2,40,1792]{2,1,0:T(8,128)(2,1)S(1)}, u32[]{:S(2)}, u32[]{:S(2)}) collective-permute-start(bf16[2,40,1792]{2,1,0:T(8,128)(2,1)S(1)} %pad_maximum_fusion.17), channel_id=1, source_target_pairs={{0,2},{1,3},{2,0},{3,1},{4,6},{5,7},{6,4},{7,5},{8,10},{9,11},{10,... | collective-permute-start | bytes 860168 | tf_op jit(solution)/shard_map/ppermute | solution.py:22
  64.4 2.4 %collective-permute-done.12 = bf16[80,2048]{1,0:T(8,128)(2,1)S(1)} collective-permute-done((bf16[80,2048]{1,0:T(8,128)(2,1)S(1)}, bf16[80,2048]{1,0:T(8,128)(2,1)S(1)}, u32[]{:S(2)}, u32[]{:S(2)}) %collective-permute-start.12) | collective-permute-done | bytes 327712 | tf_op jit(solution)/shard_map/ppermute | solution.py:59
  67.0 1.4 fusion.20
  68.6 1.4 fusion.16
  70.1 1.4 fusion.12
  71.5 1.4 fusion.8
  72.9 3.6 %collective-permute-start.16 = (bf16[2,80,1792]{2,1,0:T(8,128)(2,1)S(1)}, bf16[2,80,1792]{2,1,0:T(8,128)(2,1)S(1)}, u32[]{:S(2)}, u32[]{:S(2)}) collective-permute-start(bf16[2,80,1792]{2,1,0:T(8,128)(2,1)S(1)} %pad_maximum_fusion.9), channel_id=1, source_target_pairs={{0,1},{1,0},{2,3},{3,2},{4,5},{5,4},{6,7},{7,6},{8,9},{9,8},{10,11... | collective-permute-start | bytes 1720328 | tf_op jit(solution)/shard_map/ppermute | solution.py:22
  76.8 3.3 %collective-permute-start.17 = (bf16[40,1792]{1,0:T(8,128)(2,1)S(1)}, bf16[40,1792]{1,0:T(8,128)(2,1)S(1)}, u32[]{:S(2)}, u32[]{:S(2)}) collective-permute-start(bf16[40,1792]{1,0:T(8,128)(2,1)S(1)} %fusion.50), channel_id=1, source_target_pairs={{0,8},{1,9},{2,0},{3,1},{4,12},{5,13},{6,4},{7,5},{8,10},{9,11},{1... | collective-permute-start | bytes 430088 | tf_op jit(solution)/shard_map/ppermute | solution.py:59
  80.2 0.7 collective-permute-start.18
  81.0 2.8 %collective-permute-start.20 = (bf16[2,40,1792]{2,1,0:T(8,128)(2,1)S(1)}, bf16[2,40,1792]{2,1,0:T(8,128)(2,1)S(1)}, u32[]{:S(2)}, u32[]{:S(2)}) collective-permute-start(bf16[2,40,1792]{2,1,0:T(8,128)(2,1)S(1)} %pad_maximum_fusion.19), channel_id=1, source_target_pairs={{0,2},{1,3},{2,0},{3,1},{4,6},{5,7},{6,4},{7,5},{8,10},{9,11},{10,... | collective-permute-start | bytes 860168 | tf_op jit(solution)/shard_map/ppermute | solution.py:22
  84.0 0.4 collective-permute-start.21
  84.4 0.8 collective-permute-start.22
  85.5 7.6 %collective-permute-start.19 = (bf16[2,40,1792]{2,1,0:T(8,128)(2,1)S(1)}, bf16[2,40,1792]{2,1,0:T(8,128)(2,1)S(1)}, u32[]{:S(2)}, u32[]{:S(2)}) collective-permute-start(bf16[2,40,1792]{2,1,0:T(8,128)(2,1)S(1)} %pad_maximum_fusion.20), channel_id=1, source_target_pairs={{0,2},{1,3},{2,0},{3,1},{4,6},{5,7},{6,4},{7,5},{8,10},{9,11},{10,... | collective-permute-start | bytes 860168 | tf_op jit(solution)/shard_map/ppermute | solution.py:22
  93.2 3.4 %collective-permute-done.20 = bf16[2,40,1792]{2,1,0:T(8,128)(2,1)S(1)} collective-permute-done((bf16[2,40,1792]{2,1,0:T(8,128)(2,1)S(1)}, bf16[2,40,1792]{2,1,0:T(8,128)(2,1)S(1)}, u32[]{:S(2)}, u32[]{:S(2)}) %collective-permute-start.20) | collective-permute-done | bytes 286752 | tf_op jit(solution)/shard_map/ppermute | solution.py:22
  96.6 0.7 collective-permute-start.24
  97.4 2.7 %collective-permute-start.25 = (bf16[40,1792]{1,0:T(8,128)(2,1)S(1)}, bf16[40,1792]{1,0:T(8,128)(2,1)S(1)}, u32[]{:S(2)}, u32[]{:S(2)}) collective-permute-start(bf16[40,1792]{1,0:T(8,128)(2,1)S(1)} %fusion.46), channel_id=1, source_target_pairs={{0,8},{1,9},{2,0},{3,1},{4,12},{5,13},{6,4},{7,5},{8,10},{9,11},{1... | collective-permute-start | bytes 430088 | tf_op jit(solution)/shard_map/ppermute | solution.py:59
  100.2 0.7 collective-permute-start.26
  100.9 1.5 collective-permute-done.19
  102.4 1.4 collective-permute-start.27
  103.9 0.7 collective-permute-start.28
  104.6 3.1 %collective-permute-start.30 = (bf16[40,1792]{1,0:T(8,128)(2,1)S(1)}, bf16[40,1792]{1,0:T(8,128)(2,1)S(1)}, u32[]{:S(2)}, u32[]{:S(2)}) collective-permute-start(bf16[40,1792]{1,0:T(8,128)(2,1)S(1)} %fusion.44), channel_id=1, source_target_pairs={{0,8},{1,9},{2,0},{3,1},{4,12},{5,13},{6,4},{7,5},{8,10},{9,11},{1... | collective-permute-start | bytes 430088 | tf_op jit(solution)/shard_map/ppermute | solution.py:59
  107.9 4.6 %fusion.6 = f32[160,2048]{1,0:T(8,128)S(1)} fusion(bf16[160,1792]{1,0:T(8,128)(2,1)S(1)} %pad_maximum_fusion.11, bf16[3584,2048]{1,0:T(8,128)(2,1)} %param.9), kind=kOutput, calls=%fused_computation.6 | convolution fusion | flops 1174405120 | bytes 9224192 | tf_op jit(solution)/shard_map/dot_general | solution.py:17
  112.5 0.7 collective-permute-start.31
  113.3 2.8 %collective-permute-start.33 = (bf16[80,1792]{1,0:T(8,128)(2,1)S(1)}, bf16[80,1792]{1,0:T(8,128)(2,1)S(1)}, u32[]{:S(2)}, u32[]{:S(2)}) collective-permute-start(bf16[80,1792]{1,0:T(8,128)(2,1)S(1)} %pad_maximum_fusion.23), channel_id=1, source_target_pairs={{0,4},{1,0},{2,6},{3,2},{4,5},{5,1},{6,7},{7,3},{8,12},{9,8},{10,1... | collective-permute-start | bytes 860168 | tf_op jit(solution)/shard_map/ppermute | solution.py:59
  116.0 0.7 collective-permute-start.34
  116.9 1.4 fusion.25
  118.3 1.4 collective-permute-start.29
  119.8 1.4 collective-permute-start.35
  121.2 0.9 collective-permute-start.36
  122.4 1.4 fusion.4
  123.7 4.8 %collective-permute-done.35 = bf16[80,1792]{1,0:T(8,128)(2,1)S(1)} collective-permute-done((bf16[80,1792]{1,0:T(8,128)(2,1)S(1)}, bf16[80,1792]{1,0:T(8,128)(2,1)S(1)}, u32[]{:S(2)}, u32[]{:S(2)}) %collective-permute-start.35) | collective-permute-done | bytes 286752 | tf_op jit(solution)/shard_map/ppermute | solution.py:59
  128.6 3.3 %collective-permute-start.32 = (bf16[80,2048]{1,0:T(8,128)(2,1)S(1)}, bf16[80,2048]{1,0:T(8,128)(2,1)S(1)}, u32[]{:S(2)}, u32[]{:S(2)}) collective-permute-start(bf16[80,2048]{1,0:T(8,128)(2,1)S(1)} %get-tuple-element.75), channel_id=1, source_target_pairs={{0,2},{1,3},{2,0},{3,1},{4,6},{5,7},{6,4},{7,5},{8,10},{9,11},{10,... | collective-permute-start | bytes 983048 | tf_op jit(solution)/shard_map/ppermute | solution.py:22
  131.9 1.4 fusion.28
  133.3 1.5 collective-permute-start.37
  134.8 4.4 %collective-permute-done.32 = bf16[80,2048]{1,0:T(8,128)(2,1)S(1)} collective-permute-done((bf16[80,2048]{1,0:T(8,128)(2,1)S(1)}, bf16[80,2048]{1,0:T(8,128)(2,1)S(1)}, u32[]{:S(2)}, u32[]{:S(2)}) %collective-permute-start.32) | collective-permute-done | bytes 327712 | tf_op jit(solution)/shard_map/ppermute | solution.py:22
  139.5 2.5 %collective-permute-start.38 = (bf16[80,2048]{1,0:T(8,128)(2,1)S(1)}, bf16[80,2048]{1,0:T(8,128)(2,1)S(1)}, u32[]{:S(2)}, u32[]{:S(2)}) collective-permute-start(bf16[80,2048]{1,0:T(8,128)(2,1)S(1)} %get-tuple-element.73), channel_id=1, source_target_pairs={{0,2},{1,3},{2,0},{3,1},{4,6},{5,7},{6,4},{7,5},{8,10},{9,11},{10,... | collective-permute-start | bytes 983048 | tf_op jit(solution)/shard_map/ppermute | solution.py:22
  142.3 8.1 %collective-permute-done.38 = bf16[80,2048]{1,0:T(8,128)(2,1)S(1)} collective-permute-done((bf16[80,2048]{1,0:T(8,128)(2,1)S(1)}, bf16[80,2048]{1,0:T(8,128)(2,1)S(1)}, u32[]{:S(2)}, u32[]{:S(2)}) %collective-permute-start.38) | collective-permute-done | bytes 327712 | tf_op jit(solution)/shard_map/ppermute | solution.py:22
  150.5 0.9 select_convert_fusion
  151.5 0.9 fusion.31
  152.4 1.2 collective-permute-done.39
  153.6 1.0 add.211
  (139 shorter events, 5.2 us)
Async XLA Ops:
  0.0 5.9 %copy-start = (bf16[160,2048]{1,0:T(8,128)(2,1)S(1)}, bf16[160,2048]{1,0:T(8,128)(2,1)}, u32[]{:S(2)}) copy-start(bf16[160,2048]{1,0:T(8,128)(2,1)} %param.5) | copy-start | bytes 1966084
  0.0 6.2 %collective-permute-start = (bf16[160,2048]{1,0:T(8,128)(2,1)}, bf16[160,2048]{1,0:T(8,128)(2,1)S(1)}, u32[]{:S(2)}, u32[]{:S(2)}) collective-permute-start(bf16[160,2048]{1,0:T(8,128)(2,1)} %param.5), channel_id=1, source_target_pairs={{0,1},{1,0},{2,3},{3,2},{4,5},{5,4},{6,7},{7,6},{8,9},{9,8},{10,11... | collective-permute-start | bytes 1966088 | tf_op jit(solution)/shard_map/ppermute | solution.py:22
  6.5 7.4 %collective-permute-start.1 = (bf16[40,2048]{1,0:T(8,128)(2,1)S(1)}, bf16[40,2048]{1,0:T(8,128)(2,1)S(1)}, u32[]{:S(2)}, u32[]{:S(2)}) collective-permute-start(bf16[40,2048]{1,0:T(8,128)(2,1)S(1)} %get-tuple-element.97), channel_id=1, source_target_pairs={{0,2},{1,3},{2,0},{3,1},{4,6},{5,7},{6,4},{7,5},{8,10},{9,11},{10,... | collective-permute-start | bytes 491528 | tf_op jit(solution)/shard_map/ppermute | solution.py:22
  14.0 6.2 %collective-permute-start.2 = (bf16[40,2048]{1,0:T(8,128)(2,1)S(1)}, bf16[40,2048]{1,0:T(8,128)(2,1)S(1)}, u32[]{:S(2)}, u32[]{:S(2)}) collective-permute-start(bf16[40,2048]{1,0:T(8,128)(2,1)S(1)} %add.180), channel_id=1, source_target_pairs={{0,8},{1,9},{2,0},{3,1},{4,12},{5,13},{6,4},{7,5},{8,10},{9,11},{1... | collective-permute-start | bytes 491528 | tf_op jit(solution)/shard_map/ppermute | solution.py:59
  16.9 3.3 %collective-permute-start.3 = (bf16[40,2048]{1,0:T(8,128)(2,1)S(1)}, bf16[40,2048]{1,0:T(8,128)(2,1)S(1)}, u32[]{:S(2)}, u32[]{:S(2)}) collective-permute-start(bf16[40,2048]{1,0:T(8,128)(2,1)S(1)} %add.180), channel_id=1, source_target_pairs={{2,8},{3,9},{6,12},{7,13},{8,2},{9,3},{12,6},{13,7},{18,24},{19,25... | collective-permute-start | bytes 491528 | tf_op jit(solution)/shard_map/ppermute | solution.py:59
  20.3 20.8 %collective-permute-start.5 = (bf16[80,2048]{1,0:T(8,128)(2,1)S(1)}, bf16[80,2048]{1,0:T(8,128)(2,1)S(1)}, u32[]{:S(2)}, u32[]{:S(2)}) collective-permute-start(bf16[80,2048]{1,0:T(8,128)(2,1)S(1)} %pad_maximum_fusion.15), channel_id=1, source_target_pairs={{0,4},{1,0},{2,6},{3,2},{4,5},{5,1},{6,7},{7,3},{8,12},{9,8},{10,1... | collective-permute-start | bytes 983048 | tf_op jit(solution)/shard_map/ppermute | solution.py:59
  25.3 15.8 %collective-permute-start.6 = (bf16[80,2048]{1,0:T(8,128)(2,1)S(1)}, bf16[80,2048]{1,0:T(8,128)(2,1)S(1)}, u32[]{:S(2)}, u32[]{:S(2)}) collective-permute-start(bf16[80,2048]{1,0:T(8,128)(2,1)S(1)} %pad_maximum_fusion.15), channel_id=1, source_target_pairs={{1,4},{3,6},{4,1},{6,3},{9,12},{11,14},{12,9},{14,11},{17,20},{19,... | collective-permute-start | bytes 983048 | tf_op jit(solution)/shard_map/ppermute | solution.py:59
  26.0 9.1 %collective-permute-start.4 = (bf16[40,2048]{1,0:T(8,128)(2,1)S(1)}, bf16[40,2048]{1,0:T(8,128)(2,1)S(1)}, u32[]{:S(2)}, u32[]{:S(2)}) collective-permute-start(bf16[40,2048]{1,0:T(8,128)(2,1)S(1)} %get-tuple-element.95), channel_id=1, source_target_pairs={{0,2},{1,3},{2,0},{3,1},{4,6},{5,7},{6,4},{7,5},{8,10},{9,11},{10,... | collective-permute-start | bytes 491528 | tf_op jit(solution)/shard_map/ppermute | solution.py:22
  35.1 25.3 %collective-permute-start.10 = (bf16[40,2048]{1,0:T(8,128)(2,1)S(1)}, bf16[40,2048]{1,0:T(8,128)(2,1)S(1)}, u32[]{:S(2)}, u32[]{:S(2)}) collective-permute-start(bf16[40,2048]{1,0:T(8,128)(2,1)S(1)} %add.182), channel_id=1, source_target_pairs={{0,8},{1,9},{2,0},{3,1},{4,12},{5,13},{6,4},{7,5},{8,10},{9,11},{1... | collective-permute-start | bytes 491528 | tf_op jit(solution)/shard_map/ppermute | solution.py:59
  40.4 20.0 %collective-permute-start.11 = (bf16[40,2048]{1,0:T(8,128)(2,1)S(1)}, bf16[40,2048]{1,0:T(8,128)(2,1)S(1)}, u32[]{:S(2)}, u32[]{:S(2)}) collective-permute-start(bf16[40,2048]{1,0:T(8,128)(2,1)S(1)} %add.182), channel_id=1, source_target_pairs={{2,8},{3,9},{6,12},{7,13},{8,2},{9,3},{12,6},{13,7},{18,24},{19,25... | collective-permute-start | bytes 491528 | tf_op jit(solution)/shard_map/ppermute | solution.py:59
  41.1 10.2 %slice-start = ((s8[14680064]{0:T(1024)(128)(4,1)}), s8[4194304]{0:T(1024)(128)(4,1)S(1)}, s32[]{:S(2)}) async-start(s8[14680064]{0:T(1024)(128)(4,1)} %bitcast.97), calls=%async_computation | async-start | bytes 8388608
  41.2 10.1 %slice-start.1 = ((s8[14680064]{0:T(1024)(128)(4,1)}), s8[4194304]{0:T(1024)(128)(4,1)S(1)}, s32[]{:S(2)}) async-start(s8[14680064]{0:T(1024)(128)(4,1)} %bitcast.97), calls=%async_computation.1 | async-start | bytes 8388608
  41.2 10.1 %slice-start.2 = ((s8[14680064]{0:T(1024)(128)(4,1)}), s8[4194304]{0:T(1024)(128)(4,1)S(1)}, s32[]{:S(2)}) async-start(s8[14680064]{0:T(1024)(128)(4,1)} %bitcast.97), calls=%async_computation.2 | async-start | bytes 8388608
  45.9 5.4 %slice-start.3 = ((s8[14680064]{0:T(1024)(128)(4,1)}), s8[2097152]{0:T(1024)(128)(4,1)S(1)}, s32[]{:S(2)}) async-start(s8[14680064]{0:T(1024)(128)(4,1)} %bitcast.97), calls=%async_computation.3 | async-start | bytes 4194304
  52.7 15.7 %slice-start.4 = ((s8[14680064]{0:T(1024)(128)(4,1)}), s8[4194304]{0:T(1024)(128)(4,1)S(1)}, s32[]{:S(2)}) async-start(s8[14680064]{0:T(1024)(128)(4,1)} %bitcast.99), calls=%async_computation.4 | async-start | bytes 8388608
  52.7 15.7 %slice-start.5 = ((s8[14680064]{0:T(1024)(128)(4,1)}), s8[4194304]{0:T(1024)(128)(4,1)S(1)}, s32[]{:S(2)}) async-start(s8[14680064]{0:T(1024)(128)(4,1)} %bitcast.99), calls=%async_computation.5 | async-start | bytes 8388608
  57.3 2.0 %collective-permute-start.7 = (bf16[2,80,1792]{2,1,0:T(8,128)(2,1)S(1)}, bf16[2,80,1792]{2,1,0:T(8,128)(2,1)S(1)}, u32[]{:S(2)}, u32[]{:S(2)}) collective-permute-start(bf16[2,80,1792]{2,1,0:T(8,128)(2,1)S(1)} %pad_maximum_fusion.7), channel_id=1, source_target_pairs={{0,1},{1,0},{2,3},{3,2},{4,5},{5,4},{6,7},{7,6},{8,9},{9,8},{10,11... | collective-permute-start | bytes 1720328 | tf_op jit(solution)/shard_map/ppermute | solution.py:22
  57.5 2.6 %collective-permute-start.9 = (bf16[2,80,1792]{2,1,0:T(8,128)(2,1)S(1)}, bf16[2,80,1792]{2,1,0:T(8,128)(2,1)S(1)}, u32[]{:S(2)}, u32[]{:S(2)}) collective-permute-start(bf16[2,80,1792]{2,1,0:T(8,128)(2,1)S(1)} %pad_maximum_fusion.8), channel_id=1, source_target_pairs={{0,1},{1,0},{2,3},{3,2},{4,5},{5,4},{6,7},{7,6},{8,9},{9,8},{10,11... | collective-permute-start | bytes 1720328 | tf_op jit(solution)/shard_map/ppermute | solution.py:22
  59.5 8.9 %slice-start.6 = ((s8[14680064]{0:T(1024)(128)(4,1)}), s8[4194304]{0:T(1024)(128)(4,1)S(1)}, s32[]{:S(2)}) async-start(s8[14680064]{0:T(1024)(128)(4,1)} %bitcast.99), calls=%async_computation.6 | async-start | bytes 8388608
  60.5 6.4 %collective-permute-start.12 = (bf16[80,2048]{1,0:T(8,128)(2,1)S(1)}, bf16[80,2048]{1,0:T(8,128)(2,1)S(1)}, u32[]{:S(2)}, u32[]{:S(2)}) collective-permute-start(bf16[80,2048]{1,0:T(8,128)(2,1)S(1)} %pad_maximum_fusion.16), channel_id=1, source_target_pairs={{0,4},{1,0},{2,6},{3,2},{4,5},{5,1},{6,7},{7,3},{8,12},{9,8},{10,1... | collective-permute-start | bytes 983048 | tf_op jit(solution)/shard_map/ppermute | solution.py:59
  60.5 6.3 %collective-permute-start.13 = (bf16[80,2048]{1,0:T(8,128)(2,1)S(1)}, bf16[80,2048]{1,0:T(8,128)(2,1)S(1)}, u32[]{:S(2)}, u32[]{:S(2)}) collective-permute-start(bf16[80,2048]{1,0:T(8,128)(2,1)S(1)} %pad_maximum_fusion.16), channel_id=1, source_target_pairs={{1,4},{3,6},{4,1},{6,3},{9,12},{11,14},{12,9},{14,11},{17,20},{19,... | collective-permute-start | bytes 983048 | tf_op jit(solution)/shard_map/ppermute | solution.py:59
  61.5 15.2 %collective-permute-start.8 = (bf16[2,40,1792]{2,1,0:T(8,128)(2,1)S(1)}, bf16[2,40,1792]{2,1,0:T(8,128)(2,1)S(1)}, u32[]{:S(2)}, u32[]{:S(2)}) collective-permute-start(bf16[2,40,1792]{2,1,0:T(8,128)(2,1)S(1)} %pad_maximum_fusion.17), channel_id=1, source_target_pairs={{0,2},{1,3},{2,0},{3,1},{4,6},{5,7},{6,4},{7,5},{8,10},{9,11},{10,... | collective-permute-start | bytes 860168 | tf_op jit(solution)/shard_map/ppermute | solution.py:22
  64.3 19.5 %collective-permute-start.15 = (bf16[2,40,1792]{2,1,0:T(8,128)(2,1)S(1)}, bf16[2,40,1792]{2,1,0:T(8,128)(2,1)S(1)}, u32[]{:S(2)}, u32[]{:S(2)}) collective-permute-start(bf16[2,40,1792]{2,1,0:T(8,128)(2,1)S(1)} %pad_maximum_fusion.18), channel_id=1, source_target_pairs={{0,2},{1,3},{2,0},{3,1},{4,6},{5,7},{6,4},{7,5},{8,10},{9,11},{10,... | collective-permute-start | bytes 860168 | tf_op jit(solution)/shard_map/ppermute | solution.py:22
  67.0 1.6 %slice-start.7 = ((s8[14680064]{0:T(1024)(128)(4,1)}), s8[2097152]{0:T(1024)(128)(4,1)S(1)}, s32[]{:S(2)}) async-start(s8[14680064]{0:T(1024)(128)(4,1)} %bitcast.99), calls=%async_computation.7 | async-start | bytes 4194304
  72.9 7.9 %collective-permute-start.16 = (bf16[2,80,1792]{2,1,0:T(8,128)(2,1)S(1)}, bf16[2,80,1792]{2,1,0:T(8,128)(2,1)S(1)}, u32[]{:S(2)}, u32[]{:S(2)}) collective-permute-start(bf16[2,80,1792]{2,1,0:T(8,128)(2,1)S(1)} %pad_maximum_fusion.9), channel_id=1, source_target_pairs={{0,1},{1,0},{2,3},{3,2},{4,5},{5,4},{6,7},{7,6},{8,9},{9,8},{10,11... | collective-permute-start | bytes 1720328 | tf_op jit(solution)/shard_map/ppermute | solution.py:22
  76.6 7.8 %collective-permute-start.14 = (bf16[2,80,1792]{2,1,0:T(8,128)(2,1)S(1)}, bf16[2,80,1792]{2,1,0:T(8,128)(2,1)S(1)}, u32[]{:S(2)}, u32[]{:S(2)}) collective-permute-start(bf16[2,80,1792]{2,1,0:T(8,128)(2,1)S(1)} %pad_maximum_fusion.10), channel_id=1, source_target_pairs={{0,1},{1,0},{2,3},{3,2},{4,5},{5,4},{6,7},{7,6},{8,9},{9,8},{10,11... | collective-permute-start | bytes 1720328 | tf_op jit(solution)/shard_map/ppermute | solution.py:22
  76.8 8.6 %collective-permute-start.17 = (bf16[40,1792]{1,0:T(8,128)(2,1)S(1)}, bf16[40,1792]{1,0:T(8,128)(2,1)S(1)}, u32[]{:S(2)}, u32[]{:S(2)}) collective-permute-start(bf16[40,1792]{1,0:T(8,128)(2,1)S(1)} %fusion.50), channel_id=1, source_target_pairs={{0,8},{1,9},{2,0},{3,1},{4,12},{5,13},{6,4},{7,5},{8,10},{9,11},{1... | collective-permute-start | bytes 430088 | tf_op jit(solution)/shard_map/ppermute | solution.py:59
  80.2 12.9 %collective-permute-start.18 = (bf16[40,1792]{1,0:T(8,128)(2,1)S(1)}, bf16[40,1792]{1,0:T(8,128)(2,1)S(1)}, u32[]{:S(2)}, u32[]{:S(2)}) collective-permute-start(bf16[40,1792]{1,0:T(8,128)(2,1)S(1)} %fusion.50), channel_id=1, source_target_pairs={{2,8},{3,9},{6,12},{7,13},{8,2},{9,3},{12,6},{13,7},{18,24},{19,25... | collective-permute-start | bytes 430088 | tf_op jit(solution)/shard_map/ppermute | solution.py:59
  80.8 36.0 %slice-start.8 = ((s8[14680064]{0:T(1024)(128)(4,1)}), s8[4194304]{0:T(1024)(128)(4,1)S(1)}, s32[]{:S(2)}) async-start(s8[14680064]{0:T(1024)(128)(4,1)} %bitcast.101), calls=%async_computation.8 | async-start | bytes 8388608
  81.0 15.6 %collective-permute-start.20 = (bf16[2,40,1792]{2,1,0:T(8,128)(2,1)S(1)}, bf16[2,40,1792]{2,1,0:T(8,128)(2,1)S(1)}, u32[]{:S(2)}, u32[]{:S(2)}) collective-permute-start(bf16[2,40,1792]{2,1,0:T(8,128)(2,1)S(1)} %pad_maximum_fusion.19), channel_id=1, source_target_pairs={{0,2},{1,3},{2,0},{3,1},{4,6},{5,7},{6,4},{7,5},{8,10},{9,11},{10,... | collective-permute-start | bytes 860168 | tf_op jit(solution)/shard_map/ppermute | solution.py:22
  83.9 32.9 %slice-start.9 = ((s8[14680064]{0:T(1024)(128)(4,1)}), s8[4194304]{0:T(1024)(128)(4,1)S(1)}, s32[]{:S(2)}) async-start(s8[14680064]{0:T(1024)(128)(4,1)} %bitcast.101), calls=%async_computation.9 | async-start | bytes 8388608
  84.0 13.5 %collective-permute-start.21 = (bf16[40,1792]{1,0:T(8,128)(2,1)S(1)}, bf16[40,1792]{1,0:T(8,128)(2,1)S(1)}, u32[]{:S(2)}, u32[]{:S(2)}) collective-permute-start(bf16[40,1792]{1,0:T(8,128)(2,1)S(1)} %fusion.48), channel_id=1, source_target_pairs={{0,8},{1,9},{2,0},{3,1},{4,12},{5,13},{6,4},{7,5},{8,10},{9,11},{1... | collective-permute-start | bytes 430088 | tf_op jit(solution)/shard_map/ppermute | solution.py:59
  84.4 15.8 %collective-permute-start.22 = (bf16[40,1792]{1,0:T(8,128)(2,1)S(1)}, bf16[40,1792]{1,0:T(8,128)(2,1)S(1)}, u32[]{:S(2)}, u32[]{:S(2)}) collective-permute-start(bf16[40,1792]{1,0:T(8,128)(2,1)S(1)} %fusion.48), channel_id=1, source_target_pairs={{2,8},{3,9},{6,12},{7,13},{8,2},{9,3},{12,6},{13,7},{18,24},{19,25... | collective-permute-start | bytes 430088 | tf_op jit(solution)/shard_map/ppermute | solution.py:59
  85.5 16.9 %collective-permute-start.19 = (bf16[2,40,1792]{2,1,0:T(8,128)(2,1)S(1)}, bf16[2,40,1792]{2,1,0:T(8,128)(2,1)S(1)}, u32[]{:S(2)}, u32[]{:S(2)}) collective-permute-start(bf16[2,40,1792]{2,1,0:T(8,128)(2,1)S(1)} %pad_maximum_fusion.20), channel_id=1, source_target_pairs={{0,2},{1,3},{2,0},{3,1},{4,6},{5,7},{6,4},{7,5},{8,10},{9,11},{10,... | collective-permute-start | bytes 860168 | tf_op jit(solution)/shard_map/ppermute | solution.py:22
  93.2 10.8 %collective-permute-start.23 = (bf16[80,1792]{1,0:T(8,128)(2,1)S(1)}, bf16[80,1792]{1,0:T(8,128)(2,1)S(1)}, u32[]{:S(2)}, u32[]{:S(2)}) collective-permute-start(bf16[80,1792]{1,0:T(8,128)(2,1)S(1)} %pad_maximum_fusion.21), channel_id=1, source_target_pairs={{0,4},{1,0},{2,6},{3,2},{4,5},{5,1},{6,7},{7,3},{8,12},{9,8},{10,1... | collective-permute-start | bytes 860168 | tf_op jit(solution)/shard_map/ppermute | solution.py:59
  96.6 8.0 %collective-permute-start.24 = (bf16[80,1792]{1,0:T(8,128)(2,1)S(1)}, bf16[80,1792]{1,0:T(8,128)(2,1)S(1)}, u32[]{:S(2)}, u32[]{:S(2)}) collective-permute-start(bf16[80,1792]{1,0:T(8,128)(2,1)S(1)} %pad_maximum_fusion.21), channel_id=1, source_target_pairs={{1,4},{3,6},{4,1},{6,3},{9,12},{11,14},{12,9},{14,11},{17,20},{19,... | collective-permute-start | bytes 860168 | tf_op jit(solution)/shard_map/ppermute | solution.py:59
  97.4 15.1 %collective-permute-start.25 = (bf16[40,1792]{1,0:T(8,128)(2,1)S(1)}, bf16[40,1792]{1,0:T(8,128)(2,1)S(1)}, u32[]{:S(2)}, u32[]{:S(2)}) collective-permute-start(bf16[40,1792]{1,0:T(8,128)(2,1)S(1)} %fusion.46), channel_id=1, source_target_pairs={{0,8},{1,9},{2,0},{3,1},{4,12},{5,13},{6,4},{7,5},{8,10},{9,11},{1... | collective-permute-start | bytes 430088 | tf_op jit(solution)/shard_map/ppermute | solution.py:59
  100.2 13.0 %collective-permute-start.26 = (bf16[40,1792]{1,0:T(8,128)(2,1)S(1)}, bf16[40,1792]{1,0:T(8,128)(2,1)S(1)}, u32[]{:S(2)}, u32[]{:S(2)}) collective-permute-start(bf16[40,1792]{1,0:T(8,128)(2,1)S(1)} %fusion.46), channel_id=1, source_target_pairs={{2,8},{3,9},{6,12},{7,13},{8,2},{9,3},{12,6},{13,7},{18,24},{19,25... | collective-permute-start | bytes 430088 | tf_op jit(solution)/shard_map/ppermute | solution.py:59
  102.4 13.7 %collective-permute-start.27 = (bf16[80,1792]{1,0:T(8,128)(2,1)S(1)}, bf16[80,1792]{1,0:T(8,128)(2,1)S(1)}, u32[]{:S(2)}, u32[]{:S(2)}) collective-permute-start(bf16[80,1792]{1,0:T(8,128)(2,1)S(1)} %pad_maximum_fusion.22), channel_id=1, source_target_pairs={{0,4},{1,0},{2,6},{3,2},{4,5},{5,1},{6,7},{7,3},{8,12},{9,8},{10,1... | collective-permute-start | bytes 860168 | tf_op jit(solution)/shard_map/ppermute | solution.py:59
  103.9 12.8 %collective-permute-start.28 = (bf16[80,1792]{1,0:T(8,128)(2,1)S(1)}, bf16[80,1792]{1,0:T(8,128)(2,1)S(1)}, u32[]{:S(2)}, u32[]{:S(2)}) collective-permute-start(bf16[80,1792]{1,0:T(8,128)(2,1)S(1)} %pad_maximum_fusion.22), channel_id=1, source_target_pairs={{1,4},{3,6},{4,1},{6,3},{9,12},{11,14},{12,9},{14,11},{17,20},{19,... | collective-permute-start | bytes 860168 | tf_op jit(solution)/shard_map/ppermute | solution.py:59
  104.6 15.1 %collective-permute-start.30 = (bf16[40,1792]{1,0:T(8,128)(2,1)S(1)}, bf16[40,1792]{1,0:T(8,128)(2,1)S(1)}, u32[]{:S(2)}, u32[]{:S(2)}) collective-permute-start(bf16[40,1792]{1,0:T(8,128)(2,1)S(1)} %fusion.44), channel_id=1, source_target_pairs={{0,8},{1,9},{2,0},{3,1},{4,12},{5,13},{6,4},{7,5},{8,10},{9,11},{1... | collective-permute-start | bytes 430088 | tf_op jit(solution)/shard_map/ppermute | solution.py:59
  107.8 9.1 %slice-start.10 = ((s8[14680064]{0:T(1024)(128)(4,1)}), s8[4194304]{0:T(1024)(128)(4,1)S(1)}, s32[]{:S(2)}) async-start(s8[14680064]{0:T(1024)(128)(4,1)} %bitcast.101), calls=%async_computation.10 | async-start | bytes 8388608
  107.8 9.0 %slice-start.11 = ((s8[14680064]{0:T(1024)(128)(4,1)}), s8[2097152]{0:T(1024)(128)(4,1)S(1)}, s32[]{:S(2)}) async-start(s8[14680064]{0:T(1024)(128)(4,1)} %bitcast.101), calls=%async_computation.11 | async-start | bytes 4194304
  112.5 7.2 %collective-permute-start.31 = (bf16[40,1792]{1,0:T(8,128)(2,1)S(1)}, bf16[40,1792]{1,0:T(8,128)(2,1)S(1)}, u32[]{:S(2)}, u32[]{:S(2)}) collective-permute-start(bf16[40,1792]{1,0:T(8,128)(2,1)S(1)} %fusion.44), channel_id=1, source_target_pairs={{2,8},{3,9},{6,12},{7,13},{8,2},{9,3},{12,6},{13,7},{18,24},{19,25... | collective-permute-start | bytes 430088 | tf_op jit(solution)/shard_map/ppermute | solution.py:59
  113.3 9.0 %collective-permute-start.33 = (bf16[80,1792]{1,0:T(8,128)(2,1)S(1)}, bf16[80,1792]{1,0:T(8,128)(2,1)S(1)}, u32[]{:S(2)}, u32[]{:S(2)}) collective-permute-start(bf16[80,1792]{1,0:T(8,128)(2,1)S(1)} %pad_maximum_fusion.23), channel_id=1, source_target_pairs={{0,4},{1,0},{2,6},{3,2},{4,5},{5,1},{6,7},{7,3},{8,12},{9,8},{10,1... | collective-permute-start | bytes 860168 | tf_op jit(solution)/shard_map/ppermute | solution.py:59
  116.0 6.2 %collective-permute-start.34 = (bf16[80,1792]{1,0:T(8,128)(2,1)S(1)}, bf16[80,1792]{1,0:T(8,128)(2,1)S(1)}, u32[]{:S(2)}, u32[]{:S(2)}) collective-permute-start(bf16[80,1792]{1,0:T(8,128)(2,1)S(1)} %pad_maximum_fusion.23), channel_id=1, source_target_pairs={{1,4},{3,6},{4,1},{6,3},{9,12},{11,14},{12,9},{14,11},{17,20},{19,... | collective-permute-start | bytes 860168 | tf_op jit(solution)/shard_map/ppermute | solution.py:59
  118.3 3.8 %collective-permute-start.29 = (bf16[80,2048]{1,0:T(8,128)(2,1)S(1)}, bf16[80,2048]{1,0:T(8,128)(2,1)S(1)}, u32[]{:S(2)}, u32[]{:S(2)}) collective-permute-start(bf16[80,2048]{1,0:T(8,128)(2,1)S(1)} %slice.465), channel_id=1, source_target_pairs={{0,1},{1,0},{2,3},{3,2},{4,5},{5,4},{6,7},{7,6},{8,9},{9,8},{10,11... | collective-permute-start | bytes 983048 | tf_op jit(solution)/shard_map/ppermute | solution.py:22
  119.8 8.7 %collective-permute-start.35 = (bf16[80,1792]{1,0:T(8,128)(2,1)S(1)}, bf16[80,1792]{1,0:T(8,128)(2,1)S(1)}, u32[]{:S(2)}, u32[]{:S(2)}) collective-permute-start(bf16[80,1792]{1,0:T(8,128)(2,1)S(1)} %pad_maximum_fusion.24), channel_id=1, source_target_pairs={{0,4},{1,0},{2,6},{3,2},{4,5},{5,1},{6,7},{7,3},{8,12},{9,8},{10,1... | collective-permute-start | bytes 860168 | tf_op jit(solution)/shard_map/ppermute | solution.py:59
  121.2 7.3 %collective-permute-start.36 = (bf16[80,1792]{1,0:T(8,128)(2,1)S(1)}, bf16[80,1792]{1,0:T(8,128)(2,1)S(1)}, u32[]{:S(2)}, u32[]{:S(2)}) collective-permute-start(bf16[80,1792]{1,0:T(8,128)(2,1)S(1)} %pad_maximum_fusion.24), channel_id=1, source_target_pairs={{1,4},{3,6},{4,1},{6,3},{9,12},{11,14},{12,9},{14,11},{17,20},{19,... | collective-permute-start | bytes 860168 | tf_op jit(solution)/shard_map/ppermute | solution.py:59
  128.6 10.7 %collective-permute-start.32 = (bf16[80,2048]{1,0:T(8,128)(2,1)S(1)}, bf16[80,2048]{1,0:T(8,128)(2,1)S(1)}, u32[]{:S(2)}, u32[]{:S(2)}) collective-permute-start(bf16[80,2048]{1,0:T(8,128)(2,1)S(1)} %get-tuple-element.75), channel_id=1, source_target_pairs={{0,2},{1,3},{2,0},{3,1},{4,6},{5,7},{6,4},{7,5},{8,10},{9,11},{10,... | collective-permute-start | bytes 983048 | tf_op jit(solution)/shard_map/ppermute | solution.py:22
  133.3 6.0 %collective-permute-start.37 = (bf16[80,2048]{1,0:T(8,128)(2,1)S(1)}, bf16[80,2048]{1,0:T(8,128)(2,1)S(1)}, u32[]{:S(2)}, u32[]{:S(2)}) collective-permute-start(bf16[80,2048]{1,0:T(8,128)(2,1)S(1)} %slice.464), channel_id=1, source_target_pairs={{0,1},{1,0},{2,3},{3,2},{4,5},{5,4},{6,7},{7,6},{8,9},{9,8},{10,11... | collective-permute-start | bytes 983048 | tf_op jit(solution)/shard_map/ppermute | solution.py:22
  139.5 11.0 %collective-permute-start.38 = (bf16[80,2048]{1,0:T(8,128)(2,1)S(1)}, bf16[80,2048]{1,0:T(8,128)(2,1)S(1)}, u32[]{:S(2)}, u32[]{:S(2)}) collective-permute-start(bf16[80,2048]{1,0:T(8,128)(2,1)S(1)} %get-tuple-element.73), channel_id=1, source_target_pairs={{0,2},{1,3},{2,0},{3,1},{4,6},{5,7},{6,4},{7,5},{8,10},{9,11},{10,... | collective-permute-start | bytes 983048 | tf_op jit(solution)/shard_map/ppermute | solution.py:22
  151.4 2.2 %collective-permute-start.39 = (bf16[160,2048]{1,0:T(8,128)(2,1)S(1)}, bf16[160,2048]{1,0:T(8,128)(2,1)S(1)}, u32[]{:S(2)}, u32[]{:S(2)}) collective-permute-start(bf16[160,2048]{1,0:T(8,128)(2,1)S(1)} %select_convert_fusion), channel_id=1, source_target_pairs={{0,1},{1,0},{2,3},{3,2},{4,5},{5,4},{6,7},{7,6},{8,9},{9,8},{10,11... | collective-permute-start | bytes 1966088 | tf_op jit(solution)/shard_map/ppermute | solution.py:22

commit v5 on v4

--- a/solution.py
+++ b/solution.py
@@ -1,15 +1,24 @@
+import functools
+
 import jax
 import jax.numpy as jnp
 from jax import lax
+from jax.experimental import pallas as pl
+from jax.experimental.pallas import tpu as pltpu
 from jax.sharding import PartitionSpec as P
 
 UNIT_CHUNKS = 2
 HALVES = 2
 ORDER = (
-    "t0 t0 t1 t0 t1 t0 c00 c01 c00 c01 "
-    "t1 t1 c10 c11 c00 c10 c01 c11 c00 "
-    "c10 c01 c11 c00 c10 c01 b0 c11 "
-    "b0 c10 c11 b1 b0 b1 b1"
+    "p t0 w0a t0",
+    "t1 t0 c00 c00",
+    "w1a c01 c01 t1",
+    "t1 c00 c11 c01",
+    "w0b c10 c11 c00",
+    "c10 c01 c11 c00",
+    "c10 c11 c01 b0",
+    "c10 c11 b0 c10",
+    "b1 b1 b0 b1",
 )
 
 
@@ -20,6 +29,41 @@
 def flip(value, axis, bit):
     count = lax.axis_size(axis)
     return lax.ppermute(value, axis, [(i, i ^ bit) for i in range(count)])
+
+
+def pull_kernel(first, units, tick_ref, gate_ref, up_ref, gate_here, up_here, done_ref, sems):
+    del tick_ref
+    columns = pl.ds(first, units)
+    copies = [
+        pltpu.make_async_copy(source.at[:, columns], here, sems.at[i])
+        for i, (source, here) in enumerate(((gate_ref, gate_here), (up_ref, up_here)))
+    ]
+    for copy in copies:
+        copy.start()
+    for copy in copies:
+        copy.wait()
+    done_ref[...] = jnp.zeros_like(done_ref)
+
+
+def pull(gate_weight, up_weight, first, units, tick):
+    far = pl.BlockSpec(memory_space=pltpu.HBM)
+    near = pl.BlockSpec(memory_space=pltpu.VMEM)
+    here = pltpu.VMEM((gate_weight.shape[0], units), gate_weight.dtype)
+    return pl.pallas_call(
+        functools.partial(pull_kernel, first, units),
+        in_specs=[pl.BlockSpec(memory_space=pltpu.SMEM), far, far],
+        out_specs=[near, near, near],
+        out_shape=[here, here, jax.ShapeDtypeStruct((8, 128), jnp.float32)],
+        scratch_shapes=[pltpu.SemaphoreType.DMA((2,))],
+        compiler_params=pltpu.CompilerParams(
+            vmem_limit_bytes=4 * gate_weight.shape[0] * units + 2**20
+        ),
+        cost_estimate=pl.CostEstimate(flops=0, bytes_accessed=0, transcendentals=0),
+    )(
+        tick,
+        pltpu.with_memory_space_constraint(gate_weight, pltpu.HBM),
+        pltpu.with_memory_space_constraint(up_weight, pltpu.HBM),
+    )
 
 
 def stationary(tokens, lengths, gate_weight, up_weight, down_weight):
@@ -105,20 +149,35 @@
         whole = issued(finish(ordered(pair)))
         return whole
 
+    picked = {}
+
+    def pick_steps():
+        own = jnp.concatenate(mine)[:, None] == places[0][None]
+        sib = jnp.concatenate(mine)[:, None] == places[1][None]
+        rows = dot(own.astype(jnp.bfloat16), tokens) + dot(sib.astype(jnp.bfloat16), sibling)
+        rows = issued(rows.astype(jnp.bfloat16)).reshape(HALVES, 2, piece, width)
+        picked["got"] = flip(rows[:, 1], "col", 2)
+        picked["rows"] = rows[:, 0]
+        return None
+        yield
+
     def half_steps(h):
-        own_pick = (mine[h][:, None] == places[0][None]).astype(jnp.bfloat16)
-        sib_pick = (mine[h][:, None] == places[1][None]).astype(jnp.bfloat16)
-        picked = dot(own_pick, tokens) + dot(ordered(sib_pick), sibling)
-        picked = issued(picked.astype(jnp.bfloat16))
-        got = flip(picked[piece:], "col", 2)
-        yield
-        own = issued(ordered(picked[:piece]) + got)
+        own = issued(ordered(picked["rows"][h]) + picked["got"][h])
         return (yield from spread_steps(own))
+
+    weights = {}
+
+    def pull_steps(i):
+        gate, up, done = pull(gate_weight, up_weight, i * step, step, ordered(lengths))
+        weights[i] = gate, up
+        issued(done)
+        return None
+        yield
 
     def chunk_steps(full, i):
         part = slice(i * step, (i + 1) * step)
         full = ordered(full)
-        gate, up = dot(full, gate_weight[:, part]), dot(full, up_weight[:, part])
+        gate, up = (dot(full, weight) for weight in weights[i])
         send = issued(jnp.stack([gate[half:], up[half:]]).astype(jnp.bfloat16))
         got = flip(send, "col", 1)
         yield
@@ -148,7 +207,11 @@
     def advance(name):
         if name not in chains:
             kind, rest = name[0], name[1:]
-            if kind == "t":
+            if kind == "p":
+                chains[name] = pick_steps()
+            elif kind == "w":
+                chains[name] = pull_steps(int(rest[0]))
+            elif kind == "t":
                 chains[name] = half_steps(int(rest))
             elif kind == "c":
                 chains[name] = chunk_steps(results["t" + rest[0]], int(rest[1]))
@@ -160,8 +223,9 @@
         except StopIteration as stop:
             results[name] = stop.value
 
-    for name in ORDER.split():
-        advance(name)
+    for line in ORDER:
+        for name in line.split():
+            advance(name)
 
     total = jnp.concatenate([results["b" + str(h)] for h in range(HALVES)])
     mixed = []

time: 155 us -> 171 us (1.10)
  Pallas kernels: 0 us -> 19.3 us
  matrix products: 34.1 us -> 20.5 us
  waiting for transfers between devices: 39.3 us -> 47.8 us
  starting transfers between devices: 71.4 us -> 73.8 us
    pallas_call x0 -> x3, Pallas kernels: none -> 19.3 us  [pull(): pl.pallas_call(functools.partial(pull_kernel, first, units), in_specs=[pl...]
    dot_general x16 -> x14, matrix products: 32.3 us -> 18.7 us  [dot(): return jnp.dot(a, b, preferred_element_type=jnp.float32)]
    ppermute x24, starting transfers between devices: 37.2 us -> 49.7 us  [move(): return lax.ppermute(value, ('row', 'col'), pairs)]
    ppermute x16 -> x15, starting transfers between devices: 34.2 us -> 24.1 us  [flip(): return lax.ppermute(value, axis, [(i, i ^ bit) for i in range(count)])]
    ppermute x24, waiting for transfers between devices: 9.68 us -> 17.4 us  [move(): return lax.ppermute(value, ('row', 'col'), pairs)]
    ppermute x16 -> x15, waiting for transfers between devices: 29.6 us -> 30.4 us  [flip(): return lax.ppermute(value, axis, [(i, i ^ bit) for i in range(count)])]
  transfers between devices with their start and end apart: 40 -> 39, of which waited for: 12 -> 13; matrix products, arithmetic and copies ran while one was open for 26% -> 11% of each run, Pallas kernels for 0% -> 8%
where the time goes in v5:
time: 171 us
  starting transfers between devices  73.8 us (43%)
  waiting for transfers between devices  47.8 us (28%)
  matrix products  20.5 us (12%)
  Pallas kernels  19.3 us (11%)
  other arithmetic  7.77 us (5%)
    ppermute x24, starting transfers between devices, move(): return lax.ppermute(value, ('row', 'col'), pairs)  49.7 us
    ppermute x15, waiting for transfers between devices, flip(): return lax.ppermute(value, axis, [(i, i ^ bit) for i in range(count)])  30.4 us
    ppermute x15, starting transfers between devices, flip(): return lax.ppermute(value, axis, [(i, i ^ bit) for i in range(count)])  24.1 us
    pallas_call x3, Pallas kernels, pull(): pl.pallas_call(functools.partial(pull_kernel, first, units), in_specs=[pl...  19.3 us
    dot_general x14, matrix products, dot(): return jnp.dot(a, b, preferred_element_type=jnp.float32)  18.7 us
    ppermute x24, waiting for transfers between devices, move(): return lax.ppermute(value, ('row', 'col'), pairs)  17.4 us
  transfers between devices with their start and end apart: 39, of which 13 were waited for; matrix products, arithmetic and copies ran while one was open for 11% of the time, Pallas kernels for 8%

profile of v5, /device:TPU:0, one launch (start us, length us, event | category | flops | bytes accessed | tf_op | source)
XLA Modules:
  0.0 170.8 jit_solution(6021846770985940513)
XLA Ops:
  0.6 1.4 fusion.59
  2.0 2.4 %compare_select_fusion.1 = (s32[160]{0:T(256)S(1)}, s32[160]{0:T(256)S(1)}) fusion(s32[]{:T(128)} %get-tuple-element.80, s32[]{:T(128)} %get-tuple-element.79, s32[]{:T(128)} %get-tuple-element.81, s32[]{:T(128)} %get-tuple-element.82), kind=kLoop, calls=%fused_computation.147 | loop fusion | flops 960 | bytes 1296 | tf_op jit(solution)/shard_map/jit(_where)/select_n | solution.py:87
  4.4 1.5 fusion.39
  6.3 2.6 %collective-permute-start.1 = (bf16[2,40,2048]{2,1,0:T(8,128)(2,1)S(1)}, bf16[2,40,2048]{2,1,0:T(8,128)(2,1)S(1)}, u32[]{:S(2)}, u32[]{:S(2)}) collective-permute-start(bf16[2,40,2048]{2,1,0:T(8,128)(2,1)S(1)} %slice_bitcast_fusion), channel_id=1, source_target_pairs={{0,2},{1,3},{2,0},{3,1},{4,6},{5,7},{6,4},{7,5},{8,10},{9,11},{10,... | collective-permute-start | bytes 983048 | tf_op jit(solution)/shard_map/ppermute | solution.py:31
  8.9 8.4 %collective-permute-done.1 = bf16[2,40,2048]{2,1,0:T(8,128)(2,1)S(1)} collective-permute-done((bf16[2,40,2048]{2,1,0:T(8,128)(2,1)S(1)}, bf16[2,40,2048]{2,1,0:T(8,128)(2,1)S(1)}, u32[]{:S(2)}, u32[]{:S(2)}) %collective-permute-start.1) | collective-permute-done | bytes 327712 | tf_op jit(solution)/shard_map/ppermute | solution.py:31
  17.3 2.9 %collective-permute-start.2 = (bf16[40,2048]{1,0:T(8,128)(2,1)S(1)}, bf16[40,2048]{1,0:T(8,128)(2,1)S(1)}, u32[]{:S(2)}, u32[]{:S(2)}) collective-permute-start(bf16[40,2048]{1,0:T(8,128)(2,1)S(1)} %fusion.37), channel_id=1, source_target_pairs={{0,8},{1,9},{2,0},{3,1},{4,12},{5,13},{6,4},{7,5},{8,10},{9,11},{1... | collective-permute-start | bytes 491528 | tf_op jit(solution)/shard_map/ppermute | solution.py:103
  20.2 0.7 collective-permute-start.3
  20.9 6.4 %shard_map.55 = (bf16[2048,1792]{1,0:T(8,128)(2,1)S(1)}, bf16[2048,1792]{1,0:T(8,128)(2,1)S(1)}, f32[8,128]{1,0:T(8,128)}) custom-call(s32[4]{0:T(128)S(1)} %copy-done, bf16[2048,3584]{1,0:T(8,128)(2,1)} %gate_ref.5, bf16[2048,3584]{1,0:T(8,128)(2,1)} %up_ref.5), custom_call_target="tpu_custom_call" | custom-call | tf_op jit(solution)/shard_map/pallas_call | solution.py:52
  27.4 1.6 collective-permute-start.4
  29.1 0.7 collective-permute-start.5
  29.8 6.0 %collective-permute-done.4 = bf16[80,2048]{1,0:T(8,128)(2,1)S(1)} collective-permute-done((bf16[80,2048]{1,0:T(8,128)(2,1)S(1)}, bf16[80,2048]{1,0:T(8,128)(2,1)S(1)}, u32[]{:S(2)}, u32[]{:S(2)}) %collective-permute-start.4) | collective-permute-done | bytes 327712 | tf_op jit(solution)/shard_map/ppermute | solution.py:103
  35.9 1.4 fusion.68
  37.3 1.4 fusion.67
  38.8 2.0 %collective-permute-start.6 = (bf16[2,80,1792]{2,1,0:T(8,128)(2,1)S(1)}, bf16[2,80,1792]{2,1,0:T(8,128)(2,1)S(1)}, u32[]{:S(2)}, u32[]{:S(2)}) collective-permute-start(bf16[2,80,1792]{2,1,0:T(8,128)(2,1)S(1)} %pad_maximum_fusion.7), channel_id=1, source_target_pairs={{0,1},{1,0},{2,3},{3,2},{4,5},{5,4},{6,7},{7,6},{8,9},{9,8},{10,11... | collective-permute-start | bytes 1720328 | tf_op jit(solution)/shard_map/ppermute | solution.py:31
  40.8 1.6 collective-permute-done.6
  42.6 6.4 %shard_map.56 = (bf16[2048,1792]{1,0:T(8,128)(2,1)S(1)}, bf16[2048,1792]{1,0:T(8,128)(2,1)S(1)}, f32[8,128]{1,0:T(8,128)}) custom-call(s32[4]{0:T(128)S(1)} %copy-done, bf16[2048,3584]{1,0:T(8,128)(2,1)} %gate_ref.5, bf16[2048,3584]{1,0:T(8,128)(2,1)} %up_ref.5), custom_call_target="tpu_custom_call" | custom-call | tf_op jit(solution)/shard_map/pallas_call | solution.py:52
  49.1 1.4 fusion.70
  50.5 1.4 fusion.69
  52.4 0.7 collective-permute-start.10
  53.1 7.9 %collective-permute-start.9 = (bf16[40,2048]{1,0:T(8,128)(2,1)S(1)}, bf16[40,2048]{1,0:T(8,128)(2,1)S(1)}, u32[]{:S(2)}, u32[]{:S(2)}) collective-permute-start(bf16[40,2048]{1,0:T(8,128)(2,1)S(1)} %fusion.36), channel_id=1, source_target_pairs={{0,8},{1,9},{2,0},{3,1},{4,12},{5,13},{6,4},{7,5},{8,10},{9,11},{1... | collective-permute-start | bytes 491528 | tf_op jit(solution)/shard_map/ppermute | solution.py:103
  61.2 5.4 %collective-permute-done.9 = bf16[40,2048]{1,0:T(8,128)(2,1)S(1)} collective-permute-done((bf16[40,2048]{1,0:T(8,128)(2,1)S(1)}, bf16[40,2048]{1,0:T(8,128)(2,1)S(1)}, u32[]{:S(2)}, u32[]{:S(2)}) %collective-permute-start.9) | collective-permute-done | bytes 163872 | tf_op jit(solution)/shard_map/ppermute | solution.py:103
  66.8 3.1 %collective-permute-start.11 = (bf16[80,2048]{1,0:T(8,128)(2,1)S(1)}, bf16[80,2048]{1,0:T(8,128)(2,1)S(1)}, u32[]{:S(2)}, u32[]{:S(2)}) collective-permute-start(bf16[80,2048]{1,0:T(8,128)(2,1)S(1)} %pad_maximum_fusion.16), channel_id=1, source_target_pairs={{0,4},{1,0},{2,6},{3,2},{4,5},{5,1},{6,7},{7,3},{8,12},{9,8},{10,1... | collective-permute-start | bytes 983048 | tf_op jit(solution)/shard_map/ppermute | solution.py:103
  69.9 0.7 collective-permute-start.12
  70.6 3.2 %collective-permute-start.7 = (bf16[2,40,1792]{2,1,0:T(8,128)(2,1)S(1)}, bf16[2,40,1792]{2,1,0:T(8,128)(2,1)S(1)}, u32[]{:S(2)}, u32[]{:S(2)}) collective-permute-start(bf16[2,40,1792]{2,1,0:T(8,128)(2,1)S(1)} %pad_maximum_fusion.17), channel_id=1, source_target_pairs={{0,2},{1,3},{2,0},{3,1},{4,6},{5,7},{6,4},{7,5},{8,10},{9,11},{10,... | collective-permute-start | bytes 860168 | tf_op jit(solution)/shard_map/ppermute | solution.py:31
  73.8 2.8 %collective-permute-done.11 = bf16[80,2048]{1,0:T(8,128)(2,1)S(1)} collective-permute-done((bf16[80,2048]{1,0:T(8,128)(2,1)S(1)}, bf16[80,2048]{1,0:T(8,128)(2,1)S(1)}, u32[]{:S(2)}, u32[]{:S(2)}) %collective-permute-start.11) | collective-permute-done | bytes 327712 | tf_op jit(solution)/shard_map/ppermute | solution.py:103
  76.7 3.6 %collective-permute-done.7 = bf16[2,40,1792]{2,1,0:T(8,128)(2,1)S(1)} collective-permute-done((bf16[2,40,1792]{2,1,0:T(8,128)(2,1)S(1)}, bf16[2,40,1792]{2,1,0:T(8,128)(2,1)S(1)}, u32[]{:S(2)}, u32[]{:S(2)}) %collective-permute-start.7) | collective-permute-done | bytes 286752 | tf_op jit(solution)/shard_map/ppermute | solution.py:31
  80.5 1.4 fusion.72
  81.9 1.4 fusion.71
  83.3 3.8 %collective-permute-start.15 = (bf16[40,1792]{1,0:T(8,128)(2,1)S(1)}, bf16[40,1792]{1,0:T(8,128)(2,1)S(1)}, u32[]{:S(2)}, u32[]{:S(2)}) collective-permute-start(bf16[40,1792]{1,0:T(8,128)(2,1)S(1)} %fusion.33), channel_id=1, source_target_pairs={{0,8},{1,9},{2,0},{3,1},{4,12},{5,13},{6,4},{7,5},{8,10},{9,11},{1... | collective-permute-start | bytes 430088 | tf_op jit(solution)/shard_map/ppermute | solution.py:103
  87.2 0.7 collective-permute-start.16
  88.0 0.6 collective-permute-start.13
  88.7 3.0 %collective-permute-start.19 = (bf16[40,1792]{1,0:T(8,128)(2,1)S(1)}, bf16[40,1792]{1,0:T(8,128)(2,1)S(1)}, u32[]{:S(2)}, u32[]{:S(2)}) collective-permute-start(bf16[40,1792]{1,0:T(8,128)(2,1)S(1)} %fusion.31), channel_id=1, source_target_pairs={{0,8},{1,9},{2,0},{3,1},{4,12},{5,13},{6,4},{7,5},{8,10},{9,11},{1... | collective-permute-start | bytes 430088 | tf_op jit(solution)/shard_map/ppermute | solution.py:103
  91.7 0.8 collective-permute-start.20
  92.5 6.4 %shard_map.57 = (bf16[2048,1792]{1,0:T(8,128)(2,1)S(1)}, bf16[2048,1792]{1,0:T(8,128)(2,1)S(1)}, f32[8,128]{1,0:T(8,128)}) custom-call(s32[4]{0:T(128)S(1)} %copy-done, bf16[2048,3584]{1,0:T(8,128)(2,1)} %gate_ref.5, bf16[2048,3584]{1,0:T(8,128)(2,1)} %up_ref.5), custom_call_target="tpu_custom_call" | custom-call | tf_op jit(solution)/shard_map/pallas_call | solution.py:52
  99.0 1.4 fusion.73
  100.4 1.4 fusion.74
  102.3 2.8 %collective-permute-start.17 = (bf16[2,40,1792]{2,1,0:T(8,128)(2,1)S(1)}, bf16[2,40,1792]{2,1,0:T(8,128)(2,1)S(1)}, u32[]{:S(2)}, u32[]{:S(2)}) collective-permute-start(bf16[2,40,1792]{2,1,0:T(8,128)(2,1)S(1)} %pad_maximum_fusion.19), channel_id=1, source_target_pairs={{0,2},{1,3},{2,0},{3,1},{4,6},{5,7},{6,4},{7,5},{8,10},{9,11},{10,... | collective-permute-start | bytes 860168 | tf_op jit(solution)/shard_map/ppermute | solution.py:31
  105.1 3.1 %collective-permute-start.21 = (bf16[80,1792]{1,0:T(8,128)(2,1)S(1)}, bf16[80,1792]{1,0:T(8,128)(2,1)S(1)}, u32[]{:S(2)}, u32[]{:S(2)}) collective-permute-start(bf16[80,1792]{1,0:T(8,128)(2,1)S(1)} %pad_maximum_fusion.20), channel_id=1, source_target_pairs={{0,4},{1,0},{2,6},{3,2},{4,5},{5,1},{6,7},{7,3},{8,12},{9,8},{10,1... | collective-permute-start | bytes 860168 | tf_op jit(solution)/shard_map/ppermute | solution.py:103
  108.2 0.7 collective-permute-start.22
  109.3 2.8 %collective-permute-start.26 = (bf16[80,1792]{1,0:T(8,128)(2,1)S(1)}, bf16[80,1792]{1,0:T(8,128)(2,1)S(1)}, u32[]{:S(2)}, u32[]{:S(2)}) collective-permute-start(bf16[80,1792]{1,0:T(8,128)(2,1)S(1)} %pad_maximum_fusion.22), channel_id=1, source_target_pairs={{0,4},{1,0},{2,6},{3,2},{4,5},{5,1},{6,7},{7,3},{8,12},{9,8},{10,1... | collective-permute-start | bytes 860168 | tf_op jit(solution)/shard_map/ppermute | solution.py:103
  112.5 0.7 collective-permute-start.27
  113.8 2.5 %collective-permute-start.24 = (bf16[40,1792]{1,0:T(8,128)(2,1)S(1)}, bf16[40,1792]{1,0:T(8,128)(2,1)S(1)}, u32[]{:S(2)}, u32[]{:S(2)}) collective-permute-start(bf16[40,1792]{1,0:T(8,128)(2,1)S(1)} %fusion.29), channel_id=1, source_target_pairs={{0,8},{1,9},{2,0},{3,1},{4,12},{5,13},{6,4},{7,5},{8,10},{9,11},{1... | collective-permute-start | bytes 430088 | tf_op jit(solution)/shard_map/ppermute | solution.py:103
  116.2 0.7 collective-permute-start.25
  117.1 1.4 fusion.6
  118.6 3.2 %collective-permute-start.29 = (bf16[40,1792]{1,0:T(8,128)(2,1)S(1)}, bf16[40,1792]{1,0:T(8,128)(2,1)S(1)}, u32[]{:S(2)}, u32[]{:S(2)}) collective-permute-start(bf16[40,1792]{1,0:T(8,128)(2,1)S(1)} %fusion.27), channel_id=1, source_target_pairs={{0,8},{1,9},{2,0},{3,1},{4,12},{5,13},{6,4},{7,5},{8,10},{9,11},{1... | collective-permute-start | bytes 430088 | tf_op jit(solution)/shard_map/ppermute | solution.py:103
  122.0 0.7 collective-permute-start.30
  122.7 3.9 %collective-permute-start.31 = (bf16[80,1792]{1,0:T(8,128)(2,1)S(1)}, bf16[80,1792]{1,0:T(8,128)(2,1)S(1)}, u32[]{:S(2)}, u32[]{:S(2)}) collective-permute-start(bf16[80,1792]{1,0:T(8,128)(2,1)S(1)} %pad_maximum_fusion.23), channel_id=1, source_target_pairs={{0,4},{1,0},{2,6},{3,2},{4,5},{5,1},{6,7},{7,3},{8,12},{9,8},{10,1... | collective-permute-start | bytes 860168 | tf_op jit(solution)/shard_map/ppermute | solution.py:103
  126.7 0.7 collective-permute-start.32
  127.4 1.5 fusion.12
  129.1 3.5 %collective-permute-start.34 = (bf16[80,1792]{1,0:T(8,128)(2,1)S(1)}, bf16[80,1792]{1,0:T(8,128)(2,1)S(1)}, u32[]{:S(2)}, u32[]{:S(2)}) collective-permute-start(bf16[80,1792]{1,0:T(8,128)(2,1)S(1)} %pad_maximum_fusion.24), channel_id=1, source_target_pairs={{0,4},{1,0},{2,6},{3,2},{4,5},{5,1},{6,7},{7,3},{8,12},{9,8},{10,1... | collective-permute-start | bytes 860168 | tf_op jit(solution)/shard_map/ppermute | solution.py:103
  132.6 0.9 collective-permute-start.35
  133.5 1.4 collective-permute-start.28
  135.0 1.4 fusion
  136.5 2.5 %collective-permute-done.34 = bf16[80,1792]{1,0:T(8,128)(2,1)S(1)} collective-permute-done((bf16[80,1792]{1,0:T(8,128)(2,1)S(1)}, bf16[80,1792]{1,0:T(8,128)(2,1)S(1)}, u32[]{:S(2)}, u32[]{:S(2)}) %collective-permute-start.34) | collective-permute-done | bytes 286752 | tf_op jit(solution)/shard_map/ppermute | solution.py:103
  139.1 1.5 fusion.9
  140.6 5.9 %collective-permute-start.36 = (bf16[80,2048]{1,0:T(8,128)(2,1)S(1)}, bf16[80,2048]{1,0:T(8,128)(2,1)S(1)}, u32[]{:S(2)}, u32[]{:S(2)}) collective-permute-start(bf16[80,2048]{1,0:T(8,128)(2,1)S(1)} %slice.447), channel_id=1, source_target_pairs={{0,1},{1,0},{2,3},{3,2},{4,5},{5,4},{6,7},{7,6},{8,9},{9,8},{10,11... | collective-permute-start | bytes 983048 | tf_op jit(solution)/shard_map/ppermute | solution.py:31
  146.8 2.7 %collective-permute-start.33 = (bf16[80,2048]{1,0:T(8,128)(2,1)S(1)}, bf16[80,2048]{1,0:T(8,128)(2,1)S(1)}, u32[]{:S(2)}, u32[]{:S(2)}) collective-permute-start(bf16[80,2048]{1,0:T(8,128)(2,1)S(1)} %get-tuple-element.83), channel_id=1, source_target_pairs={{0,2},{1,3},{2,0},{3,1},{4,6},{5,7},{6,4},{7,5},{8,10},{9,11},{10,... | collective-permute-start | bytes 983048 | tf_op jit(solution)/shard_map/ppermute | solution.py:31
  149.6 7.8 %collective-permute-done.33 = bf16[80,2048]{1,0:T(8,128)(2,1)S(1)} collective-permute-done((bf16[80,2048]{1,0:T(8,128)(2,1)S(1)}, bf16[80,2048]{1,0:T(8,128)(2,1)S(1)}, u32[]{:S(2)}, u32[]{:S(2)}) %collective-permute-start.33) | collective-permute-done | bytes 327712 | tf_op jit(solution)/shard_map/ppermute | solution.py:31
  157.4 1.8 %collective-permute-start.37 = (bf16[80,2048]{1,0:T(8,128)(2,1)S(1)}, bf16[80,2048]{1,0:T(8,128)(2,1)S(1)}, u32[]{:S(2)}, u32[]{:S(2)}) collective-permute-start(bf16[80,2048]{1,0:T(8,128)(2,1)S(1)} %get-tuple-element.85), channel_id=1, source_target_pairs={{0,2},{1,3},{2,0},{3,1},{4,6},{5,7},{6,4},{7,5},{8,10},{9,11},{10,... | collective-permute-start | bytes 983048 | tf_op jit(solution)/shard_map/ppermute | solution.py:31
  159.3 7.3 %collective-permute-done.37 = bf16[80,2048]{1,0:T(8,128)(2,1)S(1)} collective-permute-done((bf16[80,2048]{1,0:T(8,128)(2,1)S(1)}, bf16[80,2048]{1,0:T(8,128)(2,1)S(1)}, u32[]{:S(2)}, u32[]{:S(2)}) %collective-permute-start.37) | collective-permute-done | bytes 327712 | tf_op jit(solution)/shard_map/ppermute | solution.py:31
  166.7 0.9 select_convert_fusion
  167.8 0.9 fusion.15
  168.7 1.1 collective-permute-done.38
  169.8 1.0 add.199
  (121 shorter events, 6.4 us)
Async XLA Ops:
  0.0 5.9 %collective-permute-start = (bf16[160,2048]{1,0:T(8,128)(2,1)}, bf16[160,2048]{1,0:T(8,128)(2,1)S(1)}, u32[]{:S(2)}, u32[]{:S(2)}) collective-permute-start(bf16[160,2048]{1,0:T(8,128)(2,1)} %param.5), channel_id=1, source_target_pairs={{0,1},{1,0},{2,3},{3,2},{4,5},{5,4},{6,7},{7,6},{8,9},{9,8},{10,11... | collective-permute-start | bytes 1966088 | tf_op jit(solution)/shard_map/ppermute | solution.py:31
  6.3 14.6 %copy-start = (s32[4]{0:T(128)S(1)}, s32[4]{0:T(128)}, u32[]{:S(2)}) copy-start(s32[4]{0:T(128)} %tick_ref.2) | copy-start | bytes 52
  6.3 10.9 %collective-permute-start.1 = (bf16[2,40,2048]{2,1,0:T(8,128)(2,1)S(1)}, bf16[2,40,2048]{2,1,0:T(8,128)(2,1)S(1)}, u32[]{:S(2)}, u32[]{:S(2)}) collective-permute-start(bf16[2,40,2048]{2,1,0:T(8,128)(2,1)S(1)} %slice_bitcast_fusion), channel_id=1, source_target_pairs={{0,2},{1,3},{2,0},{3,1},{4,6},{5,7},{6,4},{7,5},{8,10},{9,11},{10,... | collective-permute-start | bytes 983048 | tf_op jit(solution)/shard_map/ppermute | solution.py:31
  17.3 10.1 %collective-permute-start.2 = (bf16[40,2048]{1,0:T(8,128)(2,1)S(1)}, bf16[40,2048]{1,0:T(8,128)(2,1)S(1)}, u32[]{:S(2)}, u32[]{:S(2)}) collective-permute-start(bf16[40,2048]{1,0:T(8,128)(2,1)S(1)} %fusion.37), channel_id=1, source_target_pairs={{0,8},{1,9},{2,0},{3,1},{4,12},{5,13},{6,4},{7,5},{8,10},{9,11},{1... | collective-permute-start | bytes 491528 | tf_op jit(solution)/shard_map/ppermute | solution.py:103
  20.2 7.2 %collective-permute-start.3 = (bf16[40,2048]{1,0:T(8,128)(2,1)S(1)}, bf16[40,2048]{1,0:T(8,128)(2,1)S(1)}, u32[]{:S(2)}, u32[]{:S(2)}) collective-permute-start(bf16[40,2048]{1,0:T(8,128)(2,1)S(1)} %fusion.37), channel_id=1, source_target_pairs={{2,8},{3,9},{6,12},{7,13},{8,2},{9,3},{12,6},{13,7},{18,24},{19,25... | collective-permute-start | bytes 491528 | tf_op jit(solution)/shard_map/ppermute | solution.py:103
  27.4 8.4 %collective-permute-start.4 = (bf16[80,2048]{1,0:T(8,128)(2,1)S(1)}, bf16[80,2048]{1,0:T(8,128)(2,1)S(1)}, u32[]{:S(2)}, u32[]{:S(2)}) collective-permute-start(bf16[80,2048]{1,0:T(8,128)(2,1)S(1)} %pad_maximum_fusion.15), channel_id=1, source_target_pairs={{0,4},{1,0},{2,6},{3,2},{4,5},{5,1},{6,7},{7,3},{8,12},{9,8},{10,1... | collective-permute-start | bytes 983048 | tf_op jit(solution)/shard_map/ppermute | solution.py:103
  29.1 6.7 %collective-permute-start.5 = (bf16[80,2048]{1,0:T(8,128)(2,1)S(1)}, bf16[80,2048]{1,0:T(8,128)(2,1)S(1)}, u32[]{:S(2)}, u32[]{:S(2)}) collective-permute-start(bf16[80,2048]{1,0:T(8,128)(2,1)S(1)} %pad_maximum_fusion.15), channel_id=1, source_target_pairs={{1,4},{3,6},{4,1},{6,3},{9,12},{11,14},{12,9},{14,11},{17,20},{19,... | collective-permute-start | bytes 983048 | tf_op jit(solution)/shard_map/ppermute | solution.py:103
  38.8 3.6 %collective-permute-start.6 = (bf16[2,80,1792]{2,1,0:T(8,128)(2,1)S(1)}, bf16[2,80,1792]{2,1,0:T(8,128)(2,1)S(1)}, u32[]{:S(2)}, u32[]{:S(2)}) collective-permute-start(bf16[2,80,1792]{2,1,0:T(8,128)(2,1)S(1)} %pad_maximum_fusion.7), channel_id=1, source_target_pairs={{0,1},{1,0},{2,3},{3,2},{4,5},{5,4},{6,7},{7,6},{8,9},{9,8},{10,11... | collective-permute-start | bytes 1720328 | tf_op jit(solution)/shard_map/ppermute | solution.py:31
  52.0 9.0 %collective-permute-start.8 = (bf16[2,80,1792]{2,1,0:T(8,128)(2,1)S(1)}, bf16[2,80,1792]{2,1,0:T(8,128)(2,1)S(1)}, u32[]{:S(2)}, u32[]{:S(2)}) collective-permute-start(bf16[2,80,1792]{2,1,0:T(8,128)(2,1)S(1)} %pad_maximum_fusion.8), channel_id=1, source_target_pairs={{0,1},{1,0},{2,3},{3,2},{4,5},{5,4},{6,7},{7,6},{8,9},{9,8},{10,11... | collective-permute-start | bytes 1720328 | tf_op jit(solution)/shard_map/ppermute | solution.py:31
  52.4 8.8 %collective-permute-start.10 = (bf16[40,2048]{1,0:T(8,128)(2,1)S(1)}, bf16[40,2048]{1,0:T(8,128)(2,1)S(1)}, u32[]{:S(2)}, u32[]{:S(2)}) collective-permute-start(bf16[40,2048]{1,0:T(8,128)(2,1)S(1)} %fusion.36), channel_id=1, source_target_pairs={{2,8},{3,9},{6,12},{7,13},{8,2},{9,3},{12,6},{13,7},{18,24},{19,25... | collective-permute-start | bytes 491528 | tf_op jit(solution)/shard_map/ppermute | solution.py:103
  53.1 13.6 %collective-permute-start.9 = (bf16[40,2048]{1,0:T(8,128)(2,1)S(1)}, bf16[40,2048]{1,0:T(8,128)(2,1)S(1)}, u32[]{:S(2)}, u32[]{:S(2)}) collective-permute-start(bf16[40,2048]{1,0:T(8,128)(2,1)S(1)} %fusion.36), channel_id=1, source_target_pairs={{0,8},{1,9},{2,0},{3,1},{4,12},{5,13},{6,4},{7,5},{8,10},{9,11},{1... | collective-permute-start | bytes 491528 | tf_op jit(solution)/shard_map/ppermute | solution.py:103
  66.8 9.9 %collective-permute-start.11 = (bf16[80,2048]{1,0:T(8,128)(2,1)S(1)}, bf16[80,2048]{1,0:T(8,128)(2,1)S(1)}, u32[]{:S(2)}, u32[]{:S(2)}) collective-permute-start(bf16[80,2048]{1,0:T(8,128)(2,1)S(1)} %pad_maximum_fusion.16), channel_id=1, source_target_pairs={{0,4},{1,0},{2,6},{3,2},{4,5},{5,1},{6,7},{7,3},{8,12},{9,8},{10,1... | collective-permute-start | bytes 983048 | tf_op jit(solution)/shard_map/ppermute | solution.py:103
  69.9 6.7 %collective-permute-start.12 = (bf16[80,2048]{1,0:T(8,128)(2,1)S(1)}, bf16[80,2048]{1,0:T(8,128)(2,1)S(1)}, u32[]{:S(2)}, u32[]{:S(2)}) collective-permute-start(bf16[80,2048]{1,0:T(8,128)(2,1)S(1)} %pad_maximum_fusion.16), channel_id=1, source_target_pairs={{1,4},{3,6},{4,1},{6,3},{9,12},{11,14},{12,9},{14,11},{17,20},{19,... | collective-permute-start | bytes 983048 | tf_op jit(solution)/shard_map/ppermute | solution.py:103
  70.6 9.8 %collective-permute-start.7 = (bf16[2,40,1792]{2,1,0:T(8,128)(2,1)S(1)}, bf16[2,40,1792]{2,1,0:T(8,128)(2,1)S(1)}, u32[]{:S(2)}, u32[]{:S(2)}) collective-permute-start(bf16[2,40,1792]{2,1,0:T(8,128)(2,1)S(1)} %pad_maximum_fusion.17), channel_id=1, source_target_pairs={{0,2},{1,3},{2,0},{3,1},{4,6},{5,7},{6,4},{7,5},{8,10},{9,11},{10,... | collective-permute-start | bytes 860168 | tf_op jit(solution)/shard_map/ppermute | solution.py:31
  73.7 14.8 %collective-permute-start.14 = (bf16[2,40,1792]{2,1,0:T(8,128)(2,1)S(1)}, bf16[2,40,1792]{2,1,0:T(8,128)(2,1)S(1)}, u32[]{:S(2)}, u32[]{:S(2)}) collective-permute-start(bf16[2,40,1792]{2,1,0:T(8,128)(2,1)S(1)} %pad_maximum_fusion.18), channel_id=1, source_target_pairs={{0,2},{1,3},{2,0},{3,1},{4,6},{5,7},{6,4},{7,5},{8,10},{9,11},{10,... | collective-permute-start | bytes 860168 | tf_op jit(solution)/shard_map/ppermute | solution.py:31
  83.3 18.9 %collective-permute-start.15 = (bf16[40,1792]{1,0:T(8,128)(2,1)S(1)}, bf16[40,1792]{1,0:T(8,128)(2,1)S(1)}, u32[]{:S(2)}, u32[]{:S(2)}) collective-permute-start(bf16[40,1792]{1,0:T(8,128)(2,1)S(1)} %fusion.33), channel_id=1, source_target_pairs={{0,8},{1,9},{2,0},{3,1},{4,12},{5,13},{6,4},{7,5},{8,10},{9,11},{1... | collective-permute-start | bytes 430088 | tf_op jit(solution)/shard_map/ppermute | solution.py:103
  87.2 17.9 %collective-permute-start.16 = (bf16[40,1792]{1,0:T(8,128)(2,1)S(1)}, bf16[40,1792]{1,0:T(8,128)(2,1)S(1)}, u32[]{:S(2)}, u32[]{:S(2)}) collective-permute-start(bf16[40,1792]{1,0:T(8,128)(2,1)S(1)} %fusion.33), channel_id=1, source_target_pairs={{2,8},{3,9},{6,12},{7,13},{8,2},{9,3},{12,6},{13,7},{18,24},{19,25... | collective-permute-start | bytes 430088 | tf_op jit(solution)/shard_map/ppermute | solution.py:103
  88.0 14.0 %collective-permute-start.13 = (bf16[2,80,1792]{2,1,0:T(8,128)(2,1)S(1)}, bf16[2,80,1792]{2,1,0:T(8,128)(2,1)S(1)}, u32[]{:S(2)}, u32[]{:S(2)}) collective-permute-start(bf16[2,80,1792]{2,1,0:T(8,128)(2,1)S(1)} %pad_maximum_fusion.9), channel_id=1, source_target_pairs={{0,1},{1,0},{2,3},{3,2},{4,5},{5,4},{6,7},{7,6},{8,9},{9,8},{10,11... | collective-permute-start | bytes 1720328 | tf_op jit(solution)/shard_map/ppermute | solution.py:31
  88.7 20.4 %collective-permute-start.19 = (bf16[40,1792]{1,0:T(8,128)(2,1)S(1)}, bf16[40,1792]{1,0:T(8,128)(2,1)S(1)}, u32[]{:S(2)}, u32[]{:S(2)}) collective-permute-start(bf16[40,1792]{1,0:T(8,128)(2,1)S(1)} %fusion.31), channel_id=1, source_target_pairs={{0,8},{1,9},{2,0},{3,1},{4,12},{5,13},{6,4},{7,5},{8,10},{9,11},{1... | collective-permute-start | bytes 430088 | tf_op jit(solution)/shard_map/ppermute | solution.py:103
  91.7 17.5 %collective-permute-start.20 = (bf16[40,1792]{1,0:T(8,128)(2,1)S(1)}, bf16[40,1792]{1,0:T(8,128)(2,1)S(1)}, u32[]{:S(2)}, u32[]{:S(2)}) collective-permute-start(bf16[40,1792]{1,0:T(8,128)(2,1)S(1)} %fusion.31), channel_id=1, source_target_pairs={{2,8},{3,9},{6,12},{7,13},{8,2},{9,3},{12,6},{13,7},{18,24},{19,25... | collective-permute-start | bytes 430088 | tf_op jit(solution)/shard_map/ppermute | solution.py:103
  100.4 16.6 %slice-start = ((s8[14680064]{0:T(1024)(128)(4,1)}), s8[2097152]{0:T(1024)(128)(4,1)S(1)}, s32[]{:S(2)}) async-start(s8[14680064]{0:T(1024)(128)(4,1)} %bitcast.121), calls=%async_computation | async-start | bytes 4194304
  100.4 16.6 %slice-start.1 = ((s8[14680064]{0:T(1024)(128)(4,1)}), s8[4194304]{0:T(1024)(128)(4,1)S(1)}, s32[]{:S(2)}) async-start(s8[14680064]{0:T(1024)(128)(4,1)} %bitcast.121), calls=%async_computation.1 | async-start | bytes 8388608
  100.4 16.6 %slice-start.2 = ((s8[14680064]{0:T(1024)(128)(4,1)}), s8[4194304]{0:T(1024)(128)(4,1)S(1)}, s32[]{:S(2)}) async-start(s8[14680064]{0:T(1024)(128)(4,1)} %bitcast.121), calls=%async_computation.2 | async-start | bytes 8388608
  102.0 6.3 %collective-permute-start.18 = (bf16[2,80,1792]{2,1,0:T(8,128)(2,1)S(1)}, bf16[2,80,1792]{2,1,0:T(8,128)(2,1)S(1)}, u32[]{:S(2)}, u32[]{:S(2)}) collective-permute-start(bf16[2,80,1792]{2,1,0:T(8,128)(2,1)S(1)} %pad_maximum_fusion.10), channel_id=1, source_target_pairs={{0,1},{1,0},{2,3},{3,2},{4,5},{5,4},{6,7},{7,6},{8,9},{9,8},{10,11... | collective-permute-start | bytes 1720328 | tf_op jit(solution)/shard_map/ppermute | solution.py:31
  102.3 10.3 %collective-permute-start.17 = (bf16[2,40,1792]{2,1,0:T(8,128)(2,1)S(1)}, bf16[2,40,1792]{2,1,0:T(8,128)(2,1)S(1)}, u32[]{:S(2)}, u32[]{:S(2)}) collective-permute-start(bf16[2,40,1792]{2,1,0:T(8,128)(2,1)S(1)} %pad_maximum_fusion.19), channel_id=1, source_target_pairs={{0,2},{1,3},{2,0},{3,1},{4,6},{5,7},{6,4},{7,5},{8,10},{9,11},{10,... | collective-permute-start | bytes 860168 | tf_op jit(solution)/shard_map/ppermute | solution.py:31
  105.1 12.0 %slice-start.3 = ((s8[14680064]{0:T(1024)(128)(4,1)}), s8[4194304]{0:T(1024)(128)(4,1)S(1)}, s32[]{:S(2)}) async-start(s8[14680064]{0:T(1024)(128)(4,1)} %bitcast.121), calls=%async_computation.3 | async-start | bytes 8388608
  105.1 8.7 %collective-permute-start.21 = (bf16[80,1792]{1,0:T(8,128)(2,1)S(1)}, bf16[80,1792]{1,0:T(8,128)(2,1)S(1)}, u32[]{:S(2)}, u32[]{:S(2)}) collective-permute-start(bf16[80,1792]{1,0:T(8,128)(2,1)S(1)} %pad_maximum_fusion.20), channel_id=1, source_target_pairs={{0,4},{1,0},{2,6},{3,2},{4,5},{5,1},{6,7},{7,3},{8,12},{9,8},{10,1... | collective-permute-start | bytes 860168 | tf_op jit(solution)/shard_map/ppermute | solution.py:103
  108.2 8.0 %collective-permute-start.22 = (bf16[80,1792]{1,0:T(8,128)(2,1)S(1)}, bf16[80,1792]{1,0:T(8,128)(2,1)S(1)}, u32[]{:S(2)}, u32[]{:S(2)}) collective-permute-start(bf16[80,1792]{1,0:T(8,128)(2,1)S(1)} %pad_maximum_fusion.20), channel_id=1, source_target_pairs={{1,4},{3,6},{4,1},{6,3},{9,12},{11,14},{12,9},{14,11},{17,20},{19,... | collective-permute-start | bytes 860168 | tf_op jit(solution)/shard_map/ppermute | solution.py:103
  109.1 9.3 %collective-permute-start.23 = (bf16[2,40,1792]{2,1,0:T(8,128)(2,1)S(1)}, bf16[2,40,1792]{2,1,0:T(8,128)(2,1)S(1)}, u32[]{:S(2)}, u32[]{:S(2)}) collective-permute-start(bf16[2,40,1792]{2,1,0:T(8,128)(2,1)S(1)} %pad_maximum_fusion.21), channel_id=1, source_target_pairs={{0,2},{1,3},{2,0},{3,1},{4,6},{5,7},{6,4},{7,5},{8,10},{9,11},{10,... | collective-permute-start | bytes 860168 | tf_op jit(solution)/shard_map/ppermute | solution.py:31
  109.3 17.4 %collective-permute-start.26 = (bf16[80,1792]{1,0:T(8,128)(2,1)S(1)}, bf16[80,1792]{1,0:T(8,128)(2,1)S(1)}, u32[]{:S(2)}, u32[]{:S(2)}) collective-permute-start(bf16[80,1792]{1,0:T(8,128)(2,1)S(1)} %pad_maximum_fusion.22), channel_id=1, source_target_pairs={{0,4},{1,0},{2,6},{3,2},{4,5},{5,1},{6,7},{7,3},{8,12},{9,8},{10,1... | collective-permute-start | bytes 860168 | tf_op jit(solution)/shard_map/ppermute | solution.py:103
  112.5 14.8 %collective-permute-start.27 = (bf16[80,1792]{1,0:T(8,128)(2,1)S(1)}, bf16[80,1792]{1,0:T(8,128)(2,1)S(1)}, u32[]{:S(2)}, u32[]{:S(2)}) collective-permute-start(bf16[80,1792]{1,0:T(8,128)(2,1)S(1)} %pad_maximum_fusion.22), channel_id=1, source_target_pairs={{1,4},{3,6},{4,1},{6,3},{9,12},{11,14},{12,9},{14,11},{17,20},{19,... | collective-permute-start | bytes 860168 | tf_op jit(solution)/shard_map/ppermute | solution.py:103
  113.8 8.2 %collective-permute-start.24 = (bf16[40,1792]{1,0:T(8,128)(2,1)S(1)}, bf16[40,1792]{1,0:T(8,128)(2,1)S(1)}, u32[]{:S(2)}, u32[]{:S(2)}) collective-permute-start(bf16[40,1792]{1,0:T(8,128)(2,1)S(1)} %fusion.29), channel_id=1, source_target_pairs={{0,8},{1,9},{2,0},{3,1},{4,12},{5,13},{6,4},{7,5},{8,10},{9,11},{1... | collective-permute-start | bytes 430088 | tf_op jit(solution)/shard_map/ppermute | solution.py:103
  116.2 6.4 %collective-permute-start.25 = (bf16[40,1792]{1,0:T(8,128)(2,1)S(1)}, bf16[40,1792]{1,0:T(8,128)(2,1)S(1)}, u32[]{:S(2)}, u32[]{:S(2)}) collective-permute-start(bf16[40,1792]{1,0:T(8,128)(2,1)S(1)} %fusion.29), channel_id=1, source_target_pairs={{2,8},{3,9},{6,12},{7,13},{8,2},{9,3},{12,6},{13,7},{18,24},{19,25... | collective-permute-start | bytes 430088 | tf_op jit(solution)/shard_map/ppermute | solution.py:103
  118.6 10.4 %collective-permute-start.29 = (bf16[40,1792]{1,0:T(8,128)(2,1)S(1)}, bf16[40,1792]{1,0:T(8,128)(2,1)S(1)}, u32[]{:S(2)}, u32[]{:S(2)}) collective-permute-start(bf16[40,1792]{1,0:T(8,128)(2,1)S(1)} %fusion.27), channel_id=1, source_target_pairs={{0,8},{1,9},{2,0},{3,1},{4,12},{5,13},{6,4},{7,5},{8,10},{9,11},{1... | collective-permute-start | bytes 430088 | tf_op jit(solution)/shard_map/ppermute | solution.py:103
  122.0 7.0 %collective-permute-start.30 = (bf16[40,1792]{1,0:T(8,128)(2,1)S(1)}, bf16[40,1792]{1,0:T(8,128)(2,1)S(1)}, u32[]{:S(2)}, u32[]{:S(2)}) collective-permute-start(bf16[40,1792]{1,0:T(8,128)(2,1)S(1)} %fusion.27), channel_id=1, source_target_pairs={{2,8},{3,9},{6,12},{7,13},{8,2},{9,3},{12,6},{13,7},{18,24},{19,25... | collective-permute-start | bytes 430088 | tf_op jit(solution)/shard_map/ppermute | solution.py:103
  122.7 12.2 %collective-permute-start.31 = (bf16[80,1792]{1,0:T(8,128)(2,1)S(1)}, bf16[80,1792]{1,0:T(8,128)(2,1)S(1)}, u32[]{:S(2)}, u32[]{:S(2)}) collective-permute-start(bf16[80,1792]{1,0:T(8,128)(2,1)S(1)} %pad_maximum_fusion.23), channel_id=1, source_target_pairs={{0,4},{1,0},{2,6},{3,2},{4,5},{5,1},{6,7},{7,3},{8,12},{9,8},{10,1... | collective-permute-start | bytes 860168 | tf_op jit(solution)/shard_map/ppermute | solution.py:103
  126.7 8.3 %collective-permute-start.32 = (bf16[80,1792]{1,0:T(8,128)(2,1)S(1)}, bf16[80,1792]{1,0:T(8,128)(2,1)S(1)}, u32[]{:S(2)}, u32[]{:S(2)}) collective-permute-start(bf16[80,1792]{1,0:T(8,128)(2,1)S(1)} %pad_maximum_fusion.23), channel_id=1, source_target_pairs={{1,4},{3,6},{4,1},{6,3},{9,12},{11,14},{12,9},{14,11},{17,20},{19,... | collective-permute-start | bytes 860168 | tf_op jit(solution)/shard_map/ppermute | solution.py:103
  129.1 9.9 %collective-permute-start.34 = (bf16[80,1792]{1,0:T(8,128)(2,1)S(1)}, bf16[80,1792]{1,0:T(8,128)(2,1)S(1)}, u32[]{:S(2)}, u32[]{:S(2)}) collective-permute-start(bf16[80,1792]{1,0:T(8,128)(2,1)S(1)} %pad_maximum_fusion.24), channel_id=1, source_target_pairs={{0,4},{1,0},{2,6},{3,2},{4,5},{5,1},{6,7},{7,3},{8,12},{9,8},{10,1... | collective-permute-start | bytes 860168 | tf_op jit(solution)/shard_map/ppermute | solution.py:103
  132.6 6.4 %collective-permute-start.35 = (bf16[80,1792]{1,0:T(8,128)(2,1)S(1)}, bf16[80,1792]{1,0:T(8,128)(2,1)S(1)}, u32[]{:S(2)}, u32[]{:S(2)}) collective-permute-start(bf16[80,1792]{1,0:T(8,128)(2,1)S(1)} %pad_maximum_fusion.24), channel_id=1, source_target_pairs={{1,4},{3,6},{4,1},{6,3},{9,12},{11,14},{12,9},{14,11},{17,20},{19,... | collective-permute-start | bytes 860168 | tf_op jit(solution)/shard_map/ppermute | solution.py:103
  133.5 2.9 %collective-permute-start.28 = (bf16[80,2048]{1,0:T(8,128)(2,1)S(1)}, bf16[80,2048]{1,0:T(8,128)(2,1)S(1)}, u32[]{:S(2)}, u32[]{:S(2)}) collective-permute-start(bf16[80,2048]{1,0:T(8,128)(2,1)S(1)} %slice.448), channel_id=1, source_target_pairs={{0,1},{1,0},{2,3},{3,2},{4,5},{5,4},{6,7},{7,6},{8,9},{9,8},{10,11... | collective-permute-start | bytes 983048 | tf_op jit(solution)/shard_map/ppermute | solution.py:31
  140.6 8.9 %collective-permute-start.36 = (bf16[80,2048]{1,0:T(8,128)(2,1)S(1)}, bf16[80,2048]{1,0:T(8,128)(2,1)S(1)}, u32[]{:S(2)}, u32[]{:S(2)}) collective-permute-start(bf16[80,2048]{1,0:T(8,128)(2,1)S(1)} %slice.447), channel_id=1, source_target_pairs={{0,1},{1,0},{2,3},{3,2},{4,5},{5,4},{6,7},{7,6},{8,9},{9,8},{10,11... | collective-permute-start | bytes 983048 | tf_op jit(solution)/shard_map/ppermute | solution.py:31
  146.8 10.6 %collective-permute-start.33 = (bf16[80,2048]{1,0:T(8,128)(2,1)S(1)}, bf16[80,2048]{1,0:T(8,128)(2,1)S(1)}, u32[]{:S(2)}, u32[]{:S(2)}) collective-permute-start(bf16[80,2048]{1,0:T(8,128)(2,1)S(1)} %get-tuple-element.83), channel_id=1, source_target_pairs={{0,2},{1,3},{2,0},{3,1},{4,6},{5,7},{6,4},{7,5},{8,10},{9,11},{10,... | collective-permute-start | bytes 983048 | tf_op jit(solution)/shard_map/ppermute | solution.py:31
  157.4 9.2 %collective-permute-start.37 = (bf16[80,2048]{1,0:T(8,128)(2,1)S(1)}, bf16[80,2048]{1,0:T(8,128)(2,1)S(1)}, u32[]{:S(2)}, u32[]{:S(2)}) collective-permute-start(bf16[80,2048]{1,0:T(8,128)(2,1)S(1)} %get-tuple-element.85), channel_id=1, source_target_pairs={{0,2},{1,3},{2,0},{3,1},{4,6},{5,7},{6,4},{7,5},{8,10},{9,11},{10,... | collective-permute-start | bytes 983048 | tf_op jit(solution)/shard_map/ppermute | solution.py:31
  166.7 1.1 copy-start.1
  167.6 2.2 %collective-permute-start.38 = (bf16[160,2048]{1,0:T(8,128)(2,1)S(1)}, bf16[160,2048]{1,0:T(8,128)(2,1)S(1)}, u32[]{:S(2)}, u32[]{:S(2)}) collective-permute-start(bf16[160,2048]{1,0:T(8,128)(2,1)S(1)} %select_convert_fusion), channel_id=1, source_target_pairs={{0,1},{1,0},{2,3},{3,2},{4,5},{5,4},{6,7},{7,6},{8,9},{9,8},{10,11... | collective-permute-start | bytes 1966088 | tf_op jit(solution)/shard_map/ppermute | solution.py:31

commit v6 on v4

--- a/solution.py
+++ b/solution.py
@@ -5,12 +5,23 @@
 
 UNIT_CHUNKS = 2
 HALVES = 2
-ORDER = (
-    "t0 t0 t1 t0 t1 t0 c00 c01 c00 c01 "
-    "t1 t1 c10 c11 c00 c10 c01 c11 c00 "
-    "c10 c01 c11 c00 c10 c01 b0 c11 "
-    "b0 c10 c11 b1 b0 b1 b1"
-)
+EDGES = {
+    "t1.add": ["t0.columns"],
+    "c00.dots": ["t1.columns"],
+    "t1.cores": ["c01.dots"],
+    "c01.dots": ["c00.sum"],
+    "c10.dots": ["c01.cores_swapped"],
+    "c11.dots": ["c10.cores_swapped"],
+    "c00.hidden": ["c01.sum"],
+    "c01.hidden": ["c10.sum"],
+    "c10.hidden": ["c11.sum"],
+    "c00.columns": ["c01.hidden"],
+    "c01.columns": ["c10.hidden"],
+    "c10.columns": ["c11.hidden"],
+    "c00.cores": ["c01.columns"],
+    "c01.cores": ["c10.columns"],
+    "c10.cores": ["c11.columns"],
+}
 
 
 def dot(a, b):
@@ -85,83 +96,96 @@
         )
 
     sibling = flip(tokens, "col", 1)
-    last = []
-
-    def ordered(value):
-        if last:
-            value = lax.optimization_barrier((value, last[-1]))[0]
+    seen = {}
+
+    def ordered(step, value):
+        for name in EDGES.get(step, ()):
+            while name not in seen:
+                advance(name.split(".")[0])
+        others = [seen[name] for name in EDGES.get(step, ())]
+        return lax.optimization_barrier((value, *others))[0] if others else value
+
+    def issued(step, value):
+        seen[step] = value
         return value
 
-    def issued(value):
-        last.append(value)
-        return value
-
-    def spread_steps(value):
+    def spread_steps(name, value):
         finish = to_columns(value)
         yield
-        pair = issued(finish(ordered(value)))
+        pair = issued(name + ".columns", finish(ordered(name + ".columns", value)))
         finish = to_cores(pair)
         yield
-        whole = issued(finish(ordered(pair)))
-        return whole
-
-    def half_steps(h):
-        own_pick = (mine[h][:, None] == places[0][None]).astype(jnp.bfloat16)
-        sib_pick = (mine[h][:, None] == places[1][None]).astype(jnp.bfloat16)
-        picked = dot(own_pick, tokens) + dot(ordered(sib_pick), sibling)
-        picked = issued(picked.astype(jnp.bfloat16))
-        got = flip(picked[piece:], "col", 2)
-        yield
-        own = issued(ordered(picked[:piece]) + got)
-        return (yield from spread_steps(own))
-
-    def chunk_steps(full, i):
+        return issued(name + ".cores", finish(ordered(name + ".cores", pair)))
+
+    picked = {}
+
+    def pick_steps():
+        own = jnp.concatenate(mine)[:, None] == places[0][None]
+        sib = jnp.concatenate(mine)[:, None] == places[1][None]
+        rows = dot(own.astype(jnp.bfloat16), tokens) + dot(sib.astype(jnp.bfloat16), sibling)
+        rows = rows.astype(jnp.bfloat16).reshape(HALVES, 2, piece, width)
+        picked["got"] = flip(rows[:, 1], "col", 2)
+        picked["rows"] = rows[:, 0]
+        return None
+        yield
+
+    def half_steps(name, h):
+        own = ordered(name + ".add", picked["rows"][h]) + picked["got"][h]
+        own = issued(name + ".add", own)
+        return (yield from spread_steps(name, own))
+
+    def chunk_steps(name, h, i):
+        full = result("t" + str(h))
         part = slice(i * step, (i + 1) * step)
-        full = ordered(full)
+        full = ordered(name + ".dots", full)
         gate, up = dot(full, gate_weight[:, part]), dot(full, up_weight[:, part])
-        send = issued(jnp.stack([gate[half:], up[half:]]).astype(jnp.bfloat16))
-        got = flip(send, "col", 1)
-        yield
-        got = ordered(got)
+        send = issued(name + ".dots", jnp.stack([gate[half:], up[half:]]).astype(jnp.bfloat16))
+        got = issued(name + ".cores_swapped", flip(send, "col", 1))
+        yield
+        got = ordered(name + ".sum", got)
         gate, up = gate[:half] + got[0], up[:half] + got[1]
-        send = issued(jnp.stack([gate[piece:], up[piece:]]).astype(jnp.bfloat16))
+        send = issued(name + ".sum", jnp.stack([gate[piece:], up[piece:]]).astype(jnp.bfloat16))
         got = flip(send, "col", 2)
         yield
-        got = ordered(got)
+        got = ordered(name + ".hidden", got)
         gate, up = gate[:piece] + got[0], up[:piece] + got[1]
-        hidden = issued((jax.nn.silu(gate) * up).astype(jnp.bfloat16))
-        whole = yield from spread_steps(hidden)
-        return issued(dot(ordered(whole), down_weight[part]))
-
-    def branch_steps(parts):
-        branch = issued(sum(parts[1:], parts[0]))
+        hidden = issued(name + ".hidden", (jax.nn.silu(gate) * up).astype(jnp.bfloat16))
+        whole = yield from spread_steps(name, hidden)
+        whole = ordered(name + ".down", whole)
+        return issued(name + ".down", dot(whole, down_weight[part]))
+
+    def branch_steps(name, h):
+        parts = [result("c" + str(h) + str(i)) for i in range(UNIT_CHUNKS)]
+        branch = issued(name + ".branch", sum(parts[1:], parts[0]))
         got = flip(branch[half:].astype(jnp.bfloat16), "col", 1)
         yield
-        total = issued(branch[:half] + ordered(got))
+        total = issued(name + ".total", branch[:half] + ordered(name + ".total", got))
         got = flip(total.astype(jnp.bfloat16), "col", 2)
         yield
-        got = ordered(got)
-        return issued(total + jnp.concatenate([got[piece:], got[:piece]], axis=0))
-
-    chains, results = {}, {}
+        got = ordered(name + ".all", got)
+        return issued(name + ".all", total + jnp.concatenate([got[piece:], got[:piece]], axis=0))
+
+    chains, results = {"p": pick_steps()}, {}
+    for h in range(HALVES):
+        chains["t" + str(h)] = half_steps("t" + str(h), h)
+        for i in range(UNIT_CHUNKS):
+            chains["c" + str(h) + str(i)] = chunk_steps("c" + str(h) + str(i), h, i)
+        chains["b" + str(h)] = branch_steps("b" + str(h), h)
 
     def advance(name):
-        if name not in chains:
-            kind, rest = name[0], name[1:]
-            if kind == "t":
-                chains[name] = half_steps(int(rest))
-            elif kind == "c":
-                chains[name] = chunk_steps(results["t" + rest[0]], int(rest[1]))
-            else:
-                parts = [results["c" + rest + str(i)] for i in range(UNIT_CHUNKS)]
-                chains[name] = branch_steps(parts)
         try:
             next(chains[name])
         except StopIteration as stop:
             results[name] = stop.value
 
-    for name in ORDER.split():
-        advance(name)
+    def result(name):
+        while name not in results:
+            advance(name)
+        return results[name]
+
+    result("p")
+    for h in range(HALVES):
+        result("b" + str(h))
 
     total = jnp.concatenate([results["b" + str(h)] for h in range(HALVES)])
     mixed = []

time: 155 us -> 170 us (1.097)
  waiting for transfers between devices: 39.3 us -> 58.1 us
  matrix products: 34.1 us -> 31.5 us
  local copies, waits for them, and re-layouts: 0.81 us -> 3.01 us
  starting transfers between devices: 71.4 us -> 69.3 us
    ppermute x16 -> x15, waiting for transfers between devices: 29.6 us -> 47.8 us  [flip(): return lax.ppermute(value, axis, [(i, i ^ bit) for i in range(count)])]
    dot_general x16 -> x14, matrix products: 32.3 us -> 28.7 us  [dot(): return jnp.dot(a, b, preferred_element_type=jnp.float32)]
    ppermute x16 -> x15, starting transfers between devices: 34.2 us -> 31 us  [flip(): return lax.ppermute(value, axis, [(i, i ^ bit) for i in range(count)])]
    unnamed x26 -> x28, local copies, waits for them, and re-layouts: 0.24 us -> 2.46 us
  transfers between devices with their start and end apart: 40 -> 39, of which waited for: 12 -> 12; matrix products, arithmetic and copies ran while one was open for 26% -> 17% of each run, Pallas kernels for 0% -> 0%
where the time goes in v6:
time: 170 us
  starting transfers between devices  69.3 us (41%)
  waiting for transfers between devices  58.1 us (34%)
  matrix products  31.5 us (19%)
  other arithmetic  6.93 us (4%)
  local copies, waits for them, and re-layouts  3.01 us (2%)
    ppermute x15, waiting for transfers between devices, flip(): return lax.ppermute(value, axis, [(i, i ^ bit) for i in range(count)])  47.8 us
    ppermute x24, starting transfers between devices, move(): return lax.ppermute(value, ('row', 'col'), pairs)  38.2 us
    ppermute x15, starting transfers between devices, flip(): return lax.ppermute(value, axis, [(i, i ^ bit) for i in range(count)])  31 us
    dot_general x14, matrix products, dot(): return jnp.dot(a, b, preferred_element_type=jnp.float32)  28.7 us
    ppermute x24, waiting for transfers between devices, move(): return lax.ppermute(value, ('row', 'col'), pairs)  10.2 us
  transfers between devices with their start and end apart: 39, of which 12 were waited for; matrix products, arithmetic and copies ran while one was open for 17% of the time, Pallas kernels for 0%

profile of v6, /device:TPU:0, one launch (start us, length us, event | category | flops | bytes accessed | tf_op | source)
XLA Modules:
  0.0 169.8 jit_solution(9441280281630400493)
XLA Ops:
  0.0 0.5 collective-permute-start
  0.6 1.4 fusion.90
  2.0 2.5 %compare_select_fusion.1 = (s32[160]{0:T(256)S(1)}, s32[160]{0:T(256)S(1)}) fusion(s32[]{:T(128)} %get-tuple-element.40, s32[]{:T(128)} %get-tuple-element.37, s32[]{:T(128)} %get-tuple-element.38, s32[]{:T(128)} %get-tuple-element.39), kind=kLoop, calls=%fused_computation.184 | loop fusion | flops 960 | bytes 1296 | tf_op jit(solution)/shard_map/jit(_where)/select_n | solution.py:54
  4.5 1.5 fusion.70
  6.4 2.6 %collective-permute-start.1 = (bf16[2,40,2048]{2,1,0:T(8,128)(2,1)S(1)}, bf16[2,40,2048]{2,1,0:T(8,128)(2,1)S(1)}, u32[]{:S(2)}, u32[]{:S(2)}) collective-permute-start(bf16[2,40,2048]{2,1,0:T(8,128)(2,1)S(1)} %slice_bitcast_fusion), channel_id=1, source_target_pairs={{0,2},{1,3},{2,0},{3,1},{4,6},{5,7},{6,4},{7,5},{8,10},{9,11},{10,... | collective-permute-start | bytes 983048 | tf_op jit(solution)/shard_map/ppermute | solution.py:33
  9.0 8.4 %collective-permute-done.1 = bf16[2,40,2048]{2,1,0:T(8,128)(2,1)S(1)} collective-permute-done((bf16[2,40,2048]{2,1,0:T(8,128)(2,1)S(1)}, bf16[2,40,2048]{2,1,0:T(8,128)(2,1)S(1)}, u32[]{:S(2)}, u32[]{:S(2)}) %collective-permute-start.1) | collective-permute-done | bytes 327712 | tf_op jit(solution)/shard_map/ppermute | solution.py:33
  17.4 2.9 %collective-permute-start.2 = (bf16[40,2048]{1,0:T(8,128)(2,1)S(1)}, bf16[40,2048]{1,0:T(8,128)(2,1)S(1)}, u32[]{:S(2)}, u32[]{:S(2)}) collective-permute-start(bf16[40,2048]{1,0:T(8,128)(2,1)S(1)} %fusion.68), channel_id=1, source_target_pairs={{0,8},{1,9},{2,0},{3,1},{4,12},{5,13},{6,4},{7,5},{8,10},{9,11},{1... | collective-permute-start | bytes 491528 | tf_op jit(solution)/shard_map/ppermute | solution.py:70
  20.3 0.7 collective-permute-start.3
  21.0 2.7 %collective-permute-done.2 = bf16[40,2048]{1,0:T(8,128)(2,1)S(1)} collective-permute-done((bf16[40,2048]{1,0:T(8,128)(2,1)S(1)}, bf16[40,2048]{1,0:T(8,128)(2,1)S(1)}, u32[]{:S(2)}, u32[]{:S(2)}) %collective-permute-start.2) | collective-permute-done | bytes 163872 | tf_op jit(solution)/shard_map/ppermute | solution.py:70
  23.8 7.5 %collective-permute-start.6 = (bf16[40,2048]{1,0:T(8,128)(2,1)S(1)}, bf16[40,2048]{1,0:T(8,128)(2,1)S(1)}, u32[]{:S(2)}, u32[]{:S(2)}) collective-permute-start(bf16[40,2048]{1,0:T(8,128)(2,1)S(1)} %fusion.67), channel_id=1, source_target_pairs={{0,8},{1,9},{2,0},{3,1},{4,12},{5,13},{6,4},{7,5},{8,10},{9,11},{1... | collective-permute-start | bytes 491528 | tf_op jit(solution)/shard_map/ppermute | solution.py:70
  31.2 0.7 collective-permute-start.7
  31.9 4.9 %collective-permute-start.4 = (bf16[80,2048]{1,0:T(8,128)(2,1)S(1)}, bf16[80,2048]{1,0:T(8,128)(2,1)S(1)}, u32[]{:S(2)}, u32[]{:S(2)}) collective-permute-start(bf16[80,2048]{1,0:T(8,128)(2,1)S(1)} %pad_maximum_fusion.11), channel_id=1, source_target_pairs={{0,4},{1,0},{2,6},{3,2},{4,5},{5,1},{6,7},{7,3},{8,12},{9,8},{10,1... | collective-permute-start | bytes 983048 | tf_op jit(solution)/shard_map/ppermute | solution.py:70
  36.9 0.7 collective-permute-start.5
  37.6 6.0 %collective-permute-done.4 = bf16[80,2048]{1,0:T(8,128)(2,1)S(1)} collective-permute-done((bf16[80,2048]{1,0:T(8,128)(2,1)S(1)}, bf16[80,2048]{1,0:T(8,128)(2,1)S(1)}, u32[]{:S(2)}, u32[]{:S(2)}) %collective-permute-start.4) | collective-permute-done | bytes 327712 | tf_op jit(solution)/shard_map/ppermute | solution.py:70
  43.8 4.6 %fusion.22 = f32[160,1792]{1,0:T(8,128)S(1)} fusion(bf16[160,2048]{1,0:T(8,128)(2,1)S(1)} %pad_maximum_fusion.5, bf16[2048,3584]{1,0:T(8,128)(2,1)} %param.7), kind=kOutput, calls=%fused_computation.22 | convolution fusion | flops 1174405120 | bytes 9142272 | tf_op jit(solution)/shard_map/dot_general | solution.py:28
  48.5 2.4 %copy-done.1 = bf16[2048,3584]{1,0:T(8,128)(2,1)S(1)} copy-done((bf16[2048,3584]{1,0:T(8,128)(2,1)S(1)}, bf16[2048,3584]{1,0:T(8,128)(2,1)}, u32[]{:S(2)}) %copy-start.1) | copy-done | bytes 14680088
  50.9 1.4 fusion.18
  52.4 3.2 %collective-permute-start.8 = (bf16[2,80,1792]{2,1,0:T(8,128)(2,1)S(1)}, bf16[2,80,1792]{2,1,0:T(8,128)(2,1)S(1)}, u32[]{:S(2)}, u32[]{:S(2)}) collective-permute-start(bf16[2,80,1792]{2,1,0:T(8,128)(2,1)S(1)} %pad_maximum_fusion.7), channel_id=1, source_target_pairs={{0,1},{1,0},{2,3},{3,2},{4,5},{5,4},{6,7},{7,6},{8,9},{9,8},{10,11... | collective-permute-start | bytes 1720328 | tf_op jit(solution)/shard_map/ppermute | solution.py:33
  55.8 0.8 collective-permute-start.12
  56.6 0.7 collective-permute-start.13
  57.6 1.4 fusion.14
  59.0 5.1 %fusion.10 = f32[160,1792]{1,0:T(8,128)S(1)} fusion(bf16[160,2048]{1,0:T(8,128)(2,1)S(1)} %pad_maximum_fusion.5, bf16[2048,3584]{1,0:T(8,128)(2,1)} %param.8), kind=kOutput, calls=%fused_computation.10 | convolution fusion | flops 1174405120 | bytes 9142272 | tf_op jit(solution)/shard_map/dot_general | solution.py:28
  64.1 2.8 %collective-permute-start.9 = (bf16[2,40,1792]{2,1,0:T(8,128)(2,1)S(1)}, bf16[2,40,1792]{2,1,0:T(8,128)(2,1)S(1)}, u32[]{:S(2)}, u32[]{:S(2)}) collective-permute-start(bf16[2,40,1792]{2,1,0:T(8,128)(2,1)S(1)} %pad_maximum_fusion.13), channel_id=1, source_target_pairs={{0,2},{1,3},{2,0},{3,1},{4,6},{5,7},{6,4},{7,5},{8,10},{9,11},{10,... | collective-permute-start | bytes 860168 | tf_op jit(solution)/shard_map/ppermute | solution.py:33
  67.0 1.9 %collective-permute-start.10 = (bf16[2,80,1792]{2,1,0:T(8,128)(2,1)S(1)}, bf16[2,80,1792]{2,1,0:T(8,128)(2,1)S(1)}, u32[]{:S(2)}, u32[]{:S(2)}) collective-permute-start(bf16[2,80,1792]{2,1,0:T(8,128)(2,1)S(1)} %pad_maximum_fusion.8), channel_id=1, source_target_pairs={{0,1},{1,0},{2,3},{3,2},{4,5},{5,4},{6,7},{7,6},{8,9},{9,8},{10,11... | collective-permute-start | bytes 1720328 | tf_op jit(solution)/shard_map/ppermute | solution.py:33
  69.1 1.5 collective-permute-done.10
  70.5 1.4 fusion.20
  72.0 1.4 fusion.16
  74.3 1.3 collective-permute-start.15
  75.6 0.8 collective-permute-start.16
  76.4 3.7 %collective-permute-start.11 = (bf16[2,40,1792]{2,1,0:T(8,128)(2,1)S(1)}, bf16[2,40,1792]{2,1,0:T(8,128)(2,1)S(1)}, u32[]{:S(2)}, u32[]{:S(2)}) collective-permute-start(bf16[2,40,1792]{2,1,0:T(8,128)(2,1)S(1)} %pad_maximum_fusion.14), channel_id=1, source_target_pairs={{0,2},{1,3},{2,0},{3,1},{4,6},{5,7},{6,4},{7,5},{8,10},{9,11},{10,... | collective-permute-start | bytes 860168 | tf_op jit(solution)/shard_map/ppermute | solution.py:33
  80.1 1.4 fusion.12
  81.5 1.4 fusion.8
  83.1 6.7 %collective-permute-done.11 = bf16[2,40,1792]{2,1,0:T(8,128)(2,1)S(1)} collective-permute-done((bf16[2,40,1792]{2,1,0:T(8,128)(2,1)S(1)}, bf16[2,40,1792]{2,1,0:T(8,128)(2,1)S(1)}, u32[]{:S(2)}, u32[]{:S(2)}) %collective-permute-start.11) | collective-permute-done | bytes 286752 | tf_op jit(solution)/shard_map/ppermute | solution.py:33
  90.4 0.8 collective-permute-start.22
  91.2 3.0 %collective-permute-start.19 = (bf16[40,1792]{1,0:T(8,128)(2,1)S(1)}, bf16[40,1792]{1,0:T(8,128)(2,1)S(1)}, u32[]{:S(2)}, u32[]{:S(2)}) collective-permute-start(bf16[40,1792]{1,0:T(8,128)(2,1)S(1)} %fusion.62), channel_id=1, source_target_pairs={{0,8},{1,9},{2,0},{3,1},{4,12},{5,13},{6,4},{7,5},{8,10},{9,11},{1... | collective-permute-start | bytes 430088 | tf_op jit(solution)/shard_map/ppermute | solution.py:70
  94.2 0.7 collective-permute-start.20
  94.9 2.8 %collective-permute-start.17 = (bf16[2,40,1792]{2,1,0:T(8,128)(2,1)S(1)}, bf16[2,40,1792]{2,1,0:T(8,128)(2,1)S(1)}, u32[]{:S(2)}, u32[]{:S(2)}) collective-permute-start(bf16[2,40,1792]{2,1,0:T(8,128)(2,1)S(1)} %pad_maximum_fusion.15), channel_id=1, source_target_pairs={{0,2},{1,3},{2,0},{3,1},{4,6},{5,7},{6,4},{7,5},{8,10},{9,11},{10,... | collective-permute-start | bytes 860168 | tf_op jit(solution)/shard_map/ppermute | solution.py:33
  97.9 9.8 %collective-permute-done.17 = bf16[2,40,1792]{2,1,0:T(8,128)(2,1)S(1)} collective-permute-done((bf16[2,40,1792]{2,1,0:T(8,128)(2,1)S(1)}, bf16[2,40,1792]{2,1,0:T(8,128)(2,1)S(1)}, u32[]{:S(2)}, u32[]{:S(2)}) %collective-permute-start.17) | collective-permute-done | bytes 286752 | tf_op jit(solution)/shard_map/ppermute | solution.py:33
  108.0 0.9 collective-permute-start.26
  108.9 0.8 collective-permute-start.27
  109.7 3.1 %collective-permute-start.24 = (bf16[40,1792]{1,0:T(8,128)(2,1)S(1)}, bf16[40,1792]{1,0:T(8,128)(2,1)S(1)}, u32[]{:S(2)}, u32[]{:S(2)}) collective-permute-start(bf16[40,1792]{1,0:T(8,128)(2,1)S(1)} %fusion.60), channel_id=1, source_target_pairs={{0,8},{1,9},{2,0},{3,1},{4,12},{5,13},{6,4},{7,5},{8,10},{9,11},{1... | collective-permute-start | bytes 430088 | tf_op jit(solution)/shard_map/ppermute | solution.py:70
  112.8 0.7 collective-permute-start.25
  113.5 2.8 %collective-permute-start.23 = (bf16[2,40,1792]{2,1,0:T(8,128)(2,1)S(1)}, bf16[2,40,1792]{2,1,0:T(8,128)(2,1)S(1)}, u32[]{:S(2)}, u32[]{:S(2)}) collective-permute-start(bf16[2,40,1792]{2,1,0:T(8,128)(2,1)S(1)} %pad_maximum_fusion.17), channel_id=1, source_target_pairs={{0,2},{1,3},{2,0},{3,1},{4,6},{5,7},{6,4},{7,5},{8,10},{9,11},{10,... | collective-permute-start | bytes 860168 | tf_op jit(solution)/shard_map/ppermute | solution.py:33
  116.3 10.0 %collective-permute-done.23 = bf16[2,40,1792]{2,1,0:T(8,128)(2,1)S(1)} collective-permute-done((bf16[2,40,1792]{2,1,0:T(8,128)(2,1)S(1)}, bf16[2,40,1792]{2,1,0:T(8,128)(2,1)S(1)}, u32[]{:S(2)}, u32[]{:S(2)}) %collective-permute-start.23) | collective-permute-done | bytes 286752 | tf_op jit(solution)/shard_map/ppermute | solution.py:33
  126.6 0.7 collective-permute-start.33
  127.2 3.0 %collective-permute-start.30 = (bf16[40,1792]{1,0:T(8,128)(2,1)S(1)}, bf16[40,1792]{1,0:T(8,128)(2,1)S(1)}, u32[]{:S(2)}, u32[]{:S(2)}) collective-permute-start(bf16[40,1792]{1,0:T(8,128)(2,1)S(1)} %fusion.58), channel_id=1, source_target_pairs={{0,8},{1,9},{2,0},{3,1},{4,12},{5,13},{6,4},{7,5},{8,10},{9,11},{1... | collective-permute-start | bytes 430088 | tf_op jit(solution)/shard_map/ppermute | solution.py:70
  130.3 0.7 collective-permute-start.31
  131.0 4.6 %fusion.2 = f32[160,2048]{1,0:T(8,128)S(1)} fusion(bf16[3584,2048]{1,0:T(8,128)(2,1)} %param.9, bf16[80,1792]{1,0:T(8,128)(2,1)S(1)} %get-tuple-element.60, bf16[80,1792]{1,0:T(8,128)(2,1)S(1)} %get-tuple-element.59), kind=kOutput, calls=%fused_computation.2 | convolution fusion | flops 1175552000 | bytes 9224192 | tf_op jit(solution)/shard_map/dot_general | solution.py:28
  135.7 1.4 fusion.25
  137.2 1.5 collective-permute-start.28
  138.7 2.0 %collective-permute-start.34 = (bf16[80,1792]{1,0:T(8,128)(2,1)S(1)}, bf16[80,1792]{1,0:T(8,128)(2,1)S(1)}, u32[]{:S(2)}, u32[]{:S(2)}) collective-permute-start(bf16[80,1792]{1,0:T(8,128)(2,1)S(1)} %pad_maximum_fusion.20), channel_id=1, source_target_pairs={{0,4},{1,0},{2,6},{3,2},{4,5},{5,1},{6,7},{7,3},{8,12},{9,8},{10,1... | collective-permute-start | bytes 860168 | tf_op jit(solution)/shard_map/ppermute | solution.py:70
  140.7 0.9 collective-permute-start.35
  141.8 2.8 %collective-permute-start.29 = (bf16[80,2048]{1,0:T(8,128)(2,1)S(1)}, bf16[80,2048]{1,0:T(8,128)(2,1)S(1)}, u32[]{:S(2)}, u32[]{:S(2)}) collective-permute-start(bf16[80,2048]{1,0:T(8,128)(2,1)S(1)} %fusion.47), channel_id=1, source_target_pairs={{0,2},{1,3},{2,0},{3,1},{4,6},{5,7},{6,4},{7,5},{8,10},{9,11},{10,... | collective-permute-start | bytes 983048 | tf_op jit(solution)/shard_map/ppermute | solution.py:33
  144.6 1.5 collective-permute-done.34
  146.2 1.4 fusion
  147.6 1.4 fusion.28
  149.1 2.3 %collective-permute-start.36 = (bf16[80,2048]{1,0:T(8,128)(2,1)S(1)}, bf16[80,2048]{1,0:T(8,128)(2,1)S(1)}, u32[]{:S(2)}, u32[]{:S(2)}) collective-permute-start(bf16[80,2048]{1,0:T(8,128)(2,1)S(1)} %slice.527), channel_id=1, source_target_pairs={{0,1},{1,0},{2,3},{3,2},{4,5},{5,4},{6,7},{7,6},{8,9},{9,8},{10,11... | collective-permute-start | bytes 983048 | tf_op jit(solution)/shard_map/ppermute | solution.py:33
  151.4 0.6 collective-permute-done.29
  152.0 0.6 collective-permute-done.36
  152.7 3.7 %collective-permute-start.37 = (bf16[80,2048]{1,0:T(8,128)(2,1)S(1)}, bf16[80,2048]{1,0:T(8,128)(2,1)S(1)}, u32[]{:S(2)}, u32[]{:S(2)}) collective-permute-start(bf16[80,2048]{1,0:T(8,128)(2,1)S(1)} %fusion.48), channel_id=1, source_target_pairs={{0,2},{1,3},{2,0},{3,1},{4,6},{5,7},{6,4},{7,5},{8,10},{9,11},{10,... | collective-permute-start | bytes 983048 | tf_op jit(solution)/shard_map/ppermute | solution.py:33
  156.6 8.1 %collective-permute-done.37 = bf16[80,2048]{1,0:T(8,128)(2,1)S(1)} collective-permute-done((bf16[80,2048]{1,0:T(8,128)(2,1)S(1)}, bf16[80,2048]{1,0:T(8,128)(2,1)S(1)}, u32[]{:S(2)}, u32[]{:S(2)}) %collective-permute-start.37) | collective-permute-done | bytes 327712 | tf_op jit(solution)/shard_map/ppermute | solution.py:33
  164.9 0.9 select_convert_fusion
  165.9 2.1 %collective-permute-done.38 = bf16[160,2048]{1,0:T(8,128)(2,1)S(1)} collective-permute-done((bf16[160,2048]{1,0:T(8,128)(2,1)S(1)}, bf16[160,2048]{1,0:T(8,128)(2,1)S(1)}, u32[]{:S(2)}, u32[]{:S(2)}) %collective-permute-start.38) | collective-permute-done | bytes 655392 | tf_op jit(solution)/shard_map/ppermute | solution.py:33
  168.0 1.9 %fusion.33 = bf16[160,2048]{1,0:T(8,128)(2,1)} fusion(bf16[160,2048]{1,0:T(8,128)(2,1)S(1)} %collective-permute-done.38, bf16[160,2048]{1,0:T(8,128)(2,1)S(1)} %copy-done, f32[80,2048]{1,0:T(8,128)S(1)} %convert_add_fusion, f32[80,2048]{1,0:T(8,128)S(1)} %convert_add_fusion.1, pred[160]{0:T(512)(128)(4,1)S(1)} %get-tuple-element.35, ...), kind=kOutput, calls=%fused_computation.33 | convolution fusion | flops 631137280 | bytes 3278240 | tf_op jit(solution)/shard_map/dot_general | solution.py:194
  (131 shorter events, 4.8 us)
Async XLA Ops:
  0.0 6.0 %collective-permute-start = (bf16[160,2048]{1,0:T(8,128)(2,1)}, bf16[160,2048]{1,0:T(8,128)(2,1)S(1)}, u32[]{:S(2)}, u32[]{:S(2)}) collective-permute-start(bf16[160,2048]{1,0:T(8,128)(2,1)} %param.5), channel_id=1, source_target_pairs={{0,1},{1,0},{2,3},{3,2},{4,5},{5,4},{6,7},{7,6},{8,9},{9,8},{10,11... | collective-permute-start | bytes 1966088 | tf_op jit(solution)/shard_map/ppermute | solution.py:33
  6.4 10.9 %collective-permute-start.1 = (bf16[2,40,2048]{2,1,0:T(8,128)(2,1)S(1)}, bf16[2,40,2048]{2,1,0:T(8,128)(2,1)S(1)}, u32[]{:S(2)}, u32[]{:S(2)}) collective-permute-start(bf16[2,40,2048]{2,1,0:T(8,128)(2,1)S(1)} %slice_bitcast_fusion), channel_id=1, source_target_pairs={{0,2},{1,3},{2,0},{3,1},{4,6},{5,7},{6,4},{7,5},{8,10},{9,11},{10,... | collective-permute-start | bytes 983048 | tf_op jit(solution)/shard_map/ppermute | solution.py:33
  17.4 6.3 %collective-permute-start.2 = (bf16[40,2048]{1,0:T(8,128)(2,1)S(1)}, bf16[40,2048]{1,0:T(8,128)(2,1)S(1)}, u32[]{:S(2)}, u32[]{:S(2)}) collective-permute-start(bf16[40,2048]{1,0:T(8,128)(2,1)S(1)} %fusion.68), channel_id=1, source_target_pairs={{0,8},{1,9},{2,0},{3,1},{4,12},{5,13},{6,4},{7,5},{8,10},{9,11},{1... | collective-permute-start | bytes 491528 | tf_op jit(solution)/shard_map/ppermute | solution.py:70
  20.3 3.4 %collective-permute-start.3 = (bf16[40,2048]{1,0:T(8,128)(2,1)S(1)}, bf16[40,2048]{1,0:T(8,128)(2,1)S(1)}, u32[]{:S(2)}, u32[]{:S(2)}) collective-permute-start(bf16[40,2048]{1,0:T(8,128)(2,1)S(1)} %fusion.68), channel_id=1, source_target_pairs={{2,8},{3,9},{6,12},{7,13},{8,2},{9,3},{12,6},{13,7},{18,24},{19,25... | collective-permute-start | bytes 491528 | tf_op jit(solution)/shard_map/ppermute | solution.py:70
  23.8 13.8 %collective-permute-start.6 = (bf16[40,2048]{1,0:T(8,128)(2,1)S(1)}, bf16[40,2048]{1,0:T(8,128)(2,1)S(1)}, u32[]{:S(2)}, u32[]{:S(2)}) collective-permute-start(bf16[40,2048]{1,0:T(8,128)(2,1)S(1)} %fusion.67), channel_id=1, source_target_pairs={{0,8},{1,9},{2,0},{3,1},{4,12},{5,13},{6,4},{7,5},{8,10},{9,11},{1... | collective-permute-start | bytes 491528 | tf_op jit(solution)/shard_map/ppermute | solution.py:70
  31.2 6.3 %collective-permute-start.7 = (bf16[40,2048]{1,0:T(8,128)(2,1)S(1)}, bf16[40,2048]{1,0:T(8,128)(2,1)S(1)}, u32[]{:S(2)}, u32[]{:S(2)}) collective-permute-start(bf16[40,2048]{1,0:T(8,128)(2,1)S(1)} %fusion.67), channel_id=1, source_target_pairs={{2,8},{3,9},{6,12},{7,13},{8,2},{9,3},{12,6},{13,7},{18,24},{19,25... | collective-permute-start | bytes 491528 | tf_op jit(solution)/shard_map/ppermute | solution.py:70
  31.9 11.7 %collective-permute-start.4 = (bf16[80,2048]{1,0:T(8,128)(2,1)S(1)}, bf16[80,2048]{1,0:T(8,128)(2,1)S(1)}, u32[]{:S(2)}, u32[]{:S(2)}) collective-permute-start(bf16[80,2048]{1,0:T(8,128)(2,1)S(1)} %pad_maximum_fusion.11), channel_id=1, source_target_pairs={{0,4},{1,0},{2,6},{3,2},{4,5},{5,1},{6,7},{7,3},{8,12},{9,8},{10,1... | collective-permute-start | bytes 983048 | tf_op jit(solution)/shard_map/ppermute | solution.py:70
  36.9 6.7 %collective-permute-start.5 = (bf16[80,2048]{1,0:T(8,128)(2,1)S(1)}, bf16[80,2048]{1,0:T(8,128)(2,1)S(1)}, u32[]{:S(2)}, u32[]{:S(2)}) collective-permute-start(bf16[80,2048]{1,0:T(8,128)(2,1)S(1)} %pad_maximum_fusion.11), channel_id=1, source_target_pairs={{1,4},{3,6},{4,1},{6,3},{9,12},{11,14},{12,9},{14,11},{17,20},{19,... | collective-permute-start | bytes 983048 | tf_op jit(solution)/shard_map/ppermute | solution.py:70
  43.6 7.3 %copy-start.1 = (bf16[2048,3584]{1,0:T(8,128)(2,1)S(1)}, bf16[2048,3584]{1,0:T(8,128)(2,1)}, u32[]{:S(2)}) copy-start(bf16[2048,3584]{1,0:T(8,128)(2,1)} %param.8) | copy-start | bytes 44040196
  43.8 13.7 %slice-start = ((s8[14680064]{0:T(1024)(128)(4,1)}), s8[4194304]{0:T(1024)(128)(4,1)S(1)}, s32[]{:S(2)}) async-start(s8[14680064]{0:T(1024)(128)(4,1)} %bitcast.132), calls=%async_computation | async-start | bytes 8388608
  43.8 13.7 %slice-start.1 = ((s8[14680064]{0:T(1024)(128)(4,1)}), s8[4194304]{0:T(1024)(128)(4,1)S(1)}, s32[]{:S(2)}) async-start(s8[14680064]{0:T(1024)(128)(4,1)} %bitcast.132), calls=%async_computation.1 | async-start | bytes 8388608
  50.9 6.7 %slice-start.2 = ((s8[14680064]{0:T(1024)(128)(4,1)}), s8[4194304]{0:T(1024)(128)(4,1)S(1)}, s32[]{:S(2)}) async-start(s8[14680064]{0:T(1024)(128)(4,1)} %bitcast.132), calls=%async_computation.2 | async-start | bytes 8388608
  50.9 6.7 %slice-start.3 = ((s8[14680064]{0:T(1024)(128)(4,1)}), s8[2097152]{0:T(1024)(128)(4,1)S(1)}, s32[]{:S(2)}) async-start(s8[14680064]{0:T(1024)(128)(4,1)} %bitcast.132), calls=%async_computation.3 | async-start | bytes 4194304
  52.4 4.9 %collective-permute-start.8 = (bf16[2,80,1792]{2,1,0:T(8,128)(2,1)S(1)}, bf16[2,80,1792]{2,1,0:T(8,128)(2,1)S(1)}, u32[]{:S(2)}, u32[]{:S(2)}) collective-permute-start(bf16[2,80,1792]{2,1,0:T(8,128)(2,1)S(1)} %pad_maximum_fusion.7), channel_id=1, source_target_pairs={{0,1},{1,0},{2,3},{3,2},{4,5},{5,4},{6,7},{7,6},{8,9},{9,8},{10,11... | collective-permute-start | bytes 1720328 | tf_op jit(solution)/shard_map/ppermute | solution.py:33
  55.8 13.1 %collective-permute-start.12 = (bf16[80,2048]{1,0:T(8,128)(2,1)S(1)}, bf16[80,2048]{1,0:T(8,128)(2,1)S(1)}, u32[]{:S(2)}, u32[]{:S(2)}) collective-permute-start(bf16[80,2048]{1,0:T(8,128)(2,1)S(1)} %pad_maximum_fusion.12), channel_id=1, source_target_pairs={{0,4},{1,0},{2,6},{3,2},{4,5},{5,1},{6,7},{7,3},{8,12},{9,8},{10,1... | collective-permute-start | bytes 983048 | tf_op jit(solution)/shard_map/ppermute | solution.py:70
  56.6 12.3 %collective-permute-start.13 = (bf16[80,2048]{1,0:T(8,128)(2,1)S(1)}, bf16[80,2048]{1,0:T(8,128)(2,1)S(1)}, u32[]{:S(2)}, u32[]{:S(2)}) collective-permute-start(bf16[80,2048]{1,0:T(8,128)(2,1)S(1)} %pad_maximum_fusion.12), channel_id=1, source_target_pairs={{1,4},{3,6},{4,1},{6,3},{9,12},{11,14},{12,9},{14,11},{17,20},{19,... | collective-permute-start | bytes 983048 | tf_op jit(solution)/shard_map/ppermute | solution.py:70
  57.6 14.4 %slice-start.4 = ((s8[14680064]{0:T(1024)(128)(4,1)}), s8[4194304]{0:T(1024)(128)(4,1)S(1)}, s32[]{:S(2)}) async-start(s8[14680064]{0:T(1024)(128)(4,1)} %bitcast.134), calls=%async_computation.4 | async-start | bytes 8388608
  57.6 14.4 %slice-start.5 = ((s8[14680064]{0:T(1024)(128)(4,1)}), s8[4194304]{0:T(1024)(128)(4,1)S(1)}, s32[]{:S(2)}) async-start(s8[14680064]{0:T(1024)(128)(4,1)} %bitcast.134), calls=%async_computation.5 | async-start | bytes 8388608
  59.0 13.0 %slice-start.6 = ((s8[14680064]{0:T(1024)(128)(4,1)}), s8[4194304]{0:T(1024)(128)(4,1)S(1)}, s32[]{:S(2)}) async-start(s8[14680064]{0:T(1024)(128)(4,1)} %bitcast.134), calls=%async_computation.6 | async-start | bytes 8388608
  64.1 10.0 %collective-permute-start.9 = (bf16[2,40,1792]{2,1,0:T(8,128)(2,1)S(1)}, bf16[2,40,1792]{2,1,0:T(8,128)(2,1)S(1)}, u32[]{:S(2)}, u32[]{:S(2)}) collective-permute-start(bf16[2,40,1792]{2,1,0:T(8,128)(2,1)S(1)} %pad_maximum_fusion.13), channel_id=1, source_target_pairs={{0,2},{1,3},{2,0},{3,1},{4,6},{5,7},{6,4},{7,5},{8,10},{9,11},{10,... | collective-permute-start | bytes 860168 | tf_op jit(solution)/shard_map/ppermute | solution.py:33
  67.0 3.5 %collective-permute-start.10 = (bf16[2,80,1792]{2,1,0:T(8,128)(2,1)S(1)}, bf16[2,80,1792]{2,1,0:T(8,128)(2,1)S(1)}, u32[]{:S(2)}, u32[]{:S(2)}) collective-permute-start(bf16[2,80,1792]{2,1,0:T(8,128)(2,1)S(1)} %pad_maximum_fusion.8), channel_id=1, source_target_pairs={{0,1},{1,0},{2,3},{3,2},{4,5},{5,4},{6,7},{7,6},{8,9},{9,8},{10,11... | collective-permute-start | bytes 1720328 | tf_op jit(solution)/shard_map/ppermute | solution.py:33
  69.1 2.9 %slice-start.7 = ((s8[14680064]{0:T(1024)(128)(4,1)}), s8[2097152]{0:T(1024)(128)(4,1)S(1)}, s32[]{:S(2)}) async-start(s8[14680064]{0:T(1024)(128)(4,1)} %bitcast.134), calls=%async_computation.7 | async-start | bytes 4194304
  73.7 6.5 %collective-permute-start.14 = (bf16[2,80,1792]{2,1,0:T(8,128)(2,1)S(1)}, bf16[2,80,1792]{2,1,0:T(8,128)(2,1)S(1)}, u32[]{:S(2)}, u32[]{:S(2)}) collective-permute-start(bf16[2,80,1792]{2,1,0:T(8,128)(2,1)S(1)} %pad_maximum_fusion.9), channel_id=1, source_target_pairs={{0,1},{1,0},{2,3},{3,2},{4,5},{5,4},{6,7},{7,6},{8,9},{9,8},{10,11... | collective-permute-start | bytes 1720328 | tf_op jit(solution)/shard_map/ppermute | solution.py:33
  74.3 16.0 %collective-permute-start.15 = (bf16[40,1792]{1,0:T(8,128)(2,1)S(1)}, bf16[40,1792]{1,0:T(8,128)(2,1)S(1)}, u32[]{:S(2)}, u32[]{:S(2)}) collective-permute-start(bf16[40,1792]{1,0:T(8,128)(2,1)S(1)} %fusion.64), channel_id=1, source_target_pairs={{0,8},{1,9},{2,0},{3,1},{4,12},{5,13},{6,4},{7,5},{8,10},{9,11},{1... | collective-permute-start | bytes 430088 | tf_op jit(solution)/shard_map/ppermute | solution.py:70
  75.6 14.6 %collective-permute-start.16 = (bf16[40,1792]{1,0:T(8,128)(2,1)S(1)}, bf16[40,1792]{1,0:T(8,128)(2,1)S(1)}, u32[]{:S(2)}, u32[]{:S(2)}) collective-permute-start(bf16[40,1792]{1,0:T(8,128)(2,1)S(1)} %fusion.64), channel_id=1, source_target_pairs={{2,8},{3,9},{6,12},{7,13},{8,2},{9,3},{12,6},{13,7},{18,24},{19,25... | collective-permute-start | bytes 430088 | tf_op jit(solution)/shard_map/ppermute | solution.py:70
  76.4 13.4 %collective-permute-start.11 = (bf16[2,40,1792]{2,1,0:T(8,128)(2,1)S(1)}, bf16[2,40,1792]{2,1,0:T(8,128)(2,1)S(1)}, u32[]{:S(2)}, u32[]{:S(2)}) collective-permute-start(bf16[2,40,1792]{2,1,0:T(8,128)(2,1)S(1)} %pad_maximum_fusion.14), channel_id=1, source_target_pairs={{0,2},{1,3},{2,0},{3,1},{4,6},{5,7},{6,4},{7,5},{8,10},{9,11},{10,... | collective-permute-start | bytes 860168 | tf_op jit(solution)/shard_map/ppermute | solution.py:33
  82.9 52.7 %slice-start.8 = ((s8[14680064]{0:T(1024)(128)(4,1)}), s8[4194304]{0:T(1024)(128)(4,1)S(1)}, s32[]{:S(2)}) async-start(s8[14680064]{0:T(1024)(128)(4,1)} %bitcast.136), calls=%async_computation.8 | async-start | bytes 8388608
  90.1 45.5 %slice-start.9 = ((s8[14680064]{0:T(1024)(128)(4,1)}), s8[4194304]{0:T(1024)(128)(4,1)S(1)}, s32[]{:S(2)}) async-start(s8[14680064]{0:T(1024)(128)(4,1)} %bitcast.136), calls=%async_computation.9 | async-start | bytes 8388608
  90.1 4.7 %collective-permute-start.18 = (bf16[2,80,1792]{2,1,0:T(8,128)(2,1)S(1)}, bf16[2,80,1792]{2,1,0:T(8,128)(2,1)S(1)}, u32[]{:S(2)}, u32[]{:S(2)}) collective-permute-start(bf16[2,80,1792]{2,1,0:T(8,128)(2,1)S(1)} %pad_maximum_fusion.10), channel_id=1, source_target_pairs={{0,1},{1,0},{2,3},{3,2},{4,5},{5,4},{6,7},{7,6},{8,9},{9,8},{10,11... | collective-permute-start | bytes 1720328 | tf_op jit(solution)/shard_map/ppermute | solution.py:33
  90.3 22.5 %collective-permute-start.21 = (bf16[80,1792]{1,0:T(8,128)(2,1)S(1)}, bf16[80,1792]{1,0:T(8,128)(2,1)S(1)}, u32[]{:S(2)}, u32[]{:S(2)}) collective-permute-start(bf16[80,1792]{1,0:T(8,128)(2,1)S(1)} %pad_maximum_fusion.16), channel_id=1, source_target_pairs={{0,4},{1,0},{2,6},{3,2},{4,5},{5,1},{6,7},{7,3},{8,12},{9,8},{10,1... | collective-permute-start | bytes 860168 | tf_op jit(solution)/shard_map/ppermute | solution.py:70
  90.4 23.1 %collective-permute-start.22 = (bf16[80,1792]{1,0:T(8,128)(2,1)S(1)}, bf16[80,1792]{1,0:T(8,128)(2,1)S(1)}, u32[]{:S(2)}, u32[]{:S(2)}) collective-permute-start(bf16[80,1792]{1,0:T(8,128)(2,1)S(1)} %pad_maximum_fusion.16), channel_id=1, source_target_pairs={{1,4},{3,6},{4,1},{6,3},{9,12},{11,14},{12,9},{14,11},{17,20},{19,... | collective-permute-start | bytes 860168 | tf_op jit(solution)/shard_map/ppermute | solution.py:70
  91.2 16.7 %collective-permute-start.19 = (bf16[40,1792]{1,0:T(8,128)(2,1)S(1)}, bf16[40,1792]{1,0:T(8,128)(2,1)S(1)}, u32[]{:S(2)}, u32[]{:S(2)}) collective-permute-start(bf16[40,1792]{1,0:T(8,128)(2,1)S(1)} %fusion.62), channel_id=1, source_target_pairs={{0,8},{1,9},{2,0},{3,1},{4,12},{5,13},{6,4},{7,5},{8,10},{9,11},{1... | collective-permute-start | bytes 430088 | tf_op jit(solution)/shard_map/ppermute | solution.py:70
  94.2 13.7 %collective-permute-start.20 = (bf16[40,1792]{1,0:T(8,128)(2,1)S(1)}, bf16[40,1792]{1,0:T(8,128)(2,1)S(1)}, u32[]{:S(2)}, u32[]{:S(2)}) collective-permute-start(bf16[40,1792]{1,0:T(8,128)(2,1)S(1)} %fusion.62), channel_id=1, source_target_pairs={{2,8},{3,9},{6,12},{7,13},{8,2},{9,3},{12,6},{13,7},{18,24},{19,25... | collective-permute-start | bytes 430088 | tf_op jit(solution)/shard_map/ppermute | solution.py:70
  94.9 12.9 %collective-permute-start.17 = (bf16[2,40,1792]{2,1,0:T(8,128)(2,1)S(1)}, bf16[2,40,1792]{2,1,0:T(8,128)(2,1)S(1)}, u32[]{:S(2)}, u32[]{:S(2)}) collective-permute-start(bf16[2,40,1792]{2,1,0:T(8,128)(2,1)S(1)} %pad_maximum_fusion.15), channel_id=1, source_target_pairs={{0,2},{1,3},{2,0},{3,1},{4,6},{5,7},{6,4},{7,5},{8,10},{9,11},{10,... | collective-permute-start | bytes 860168 | tf_op jit(solution)/shard_map/ppermute | solution.py:33
  108.0 27.7 %slice-start.10 = ((s8[14680064]{0:T(1024)(128)(4,1)}), s8[4194304]{0:T(1024)(128)(4,1)S(1)}, s32[]{:S(2)}) async-start(s8[14680064]{0:T(1024)(128)(4,1)} %bitcast.136), calls=%async_computation.10 | async-start | bytes 8388608
  108.0 22.3 %collective-permute-start.26 = (bf16[80,1792]{1,0:T(8,128)(2,1)S(1)}, bf16[80,1792]{1,0:T(8,128)(2,1)S(1)}, u32[]{:S(2)}, u32[]{:S(2)}) collective-permute-start(bf16[80,1792]{1,0:T(8,128)(2,1)S(1)} %pad_maximum_fusion.18), channel_id=1, source_target_pairs={{0,4},{1,0},{2,6},{3,2},{4,5},{5,1},{6,7},{7,3},{8,12},{9,8},{10,1... | collective-permute-start | bytes 860168 | tf_op jit(solution)/shard_map/ppermute | solution.py:70
  108.9 22.0 %collective-permute-start.27 = (bf16[80,1792]{1,0:T(8,128)(2,1)S(1)}, bf16[80,1792]{1,0:T(8,128)(2,1)S(1)}, u32[]{:S(2)}, u32[]{:S(2)}) collective-permute-start(bf16[80,1792]{1,0:T(8,128)(2,1)S(1)} %pad_maximum_fusion.18), channel_id=1, source_target_pairs={{1,4},{3,6},{4,1},{6,3},{9,12},{11,14},{12,9},{14,11},{17,20},{19,... | collective-permute-start | bytes 860168 | tf_op jit(solution)/shard_map/ppermute | solution.py:70
  109.7 16.7 %collective-permute-start.24 = (bf16[40,1792]{1,0:T(8,128)(2,1)S(1)}, bf16[40,1792]{1,0:T(8,128)(2,1)S(1)}, u32[]{:S(2)}, u32[]{:S(2)}) collective-permute-start(bf16[40,1792]{1,0:T(8,128)(2,1)S(1)} %fusion.60), channel_id=1, source_target_pairs={{0,8},{1,9},{2,0},{3,1},{4,12},{5,13},{6,4},{7,5},{8,10},{9,11},{1... | collective-permute-start | bytes 430088 | tf_op jit(solution)/shard_map/ppermute | solution.py:70
  112.8 13.6 %collective-permute-start.25 = (bf16[40,1792]{1,0:T(8,128)(2,1)S(1)}, bf16[40,1792]{1,0:T(8,128)(2,1)S(1)}, u32[]{:S(2)}, u32[]{:S(2)}) collective-permute-start(bf16[40,1792]{1,0:T(8,128)(2,1)S(1)} %fusion.60), channel_id=1, source_target_pairs={{2,8},{3,9},{6,12},{7,13},{8,2},{9,3},{12,6},{13,7},{18,24},{19,25... | collective-permute-start | bytes 430088 | tf_op jit(solution)/shard_map/ppermute | solution.py:70
  113.5 12.8 %collective-permute-start.23 = (bf16[2,40,1792]{2,1,0:T(8,128)(2,1)S(1)}, bf16[2,40,1792]{2,1,0:T(8,128)(2,1)S(1)}, u32[]{:S(2)}, u32[]{:S(2)}) collective-permute-start(bf16[2,40,1792]{2,1,0:T(8,128)(2,1)S(1)} %pad_maximum_fusion.17), channel_id=1, source_target_pairs={{0,2},{1,3},{2,0},{3,1},{4,6},{5,7},{6,4},{7,5},{8,10},{9,11},{10,... | collective-permute-start | bytes 860168 | tf_op jit(solution)/shard_map/ppermute | solution.py:33
  126.5 15.2 %collective-permute-start.32 = (bf16[80,1792]{1,0:T(8,128)(2,1)S(1)}, bf16[80,1792]{1,0:T(8,128)(2,1)S(1)}, u32[]{:S(2)}, u32[]{:S(2)}) collective-permute-start(bf16[80,1792]{1,0:T(8,128)(2,1)S(1)} %pad_maximum_fusion.19), channel_id=1, source_target_pairs={{0,4},{1,0},{2,6},{3,2},{4,5},{5,1},{6,7},{7,3},{8,12},{9,8},{10,1... | collective-permute-start | bytes 860168 | tf_op jit(solution)/shard_map/ppermute | solution.py:70
  126.6 15.1 %collective-permute-start.33 = (bf16[80,1792]{1,0:T(8,128)(2,1)S(1)}, bf16[80,1792]{1,0:T(8,128)(2,1)S(1)}, u32[]{:S(2)}, u32[]{:S(2)}) collective-permute-start(bf16[80,1792]{1,0:T(8,128)(2,1)S(1)} %pad_maximum_fusion.19), channel_id=1, source_target_pairs={{1,4},{3,6},{4,1},{6,3},{9,12},{11,14},{12,9},{14,11},{17,20},{19,... | collective-permute-start | bytes 860168 | tf_op jit(solution)/shard_map/ppermute | solution.py:70
  127.2 11.4 %collective-permute-start.30 = (bf16[40,1792]{1,0:T(8,128)(2,1)S(1)}, bf16[40,1792]{1,0:T(8,128)(2,1)S(1)}, u32[]{:S(2)}, u32[]{:S(2)}) collective-permute-start(bf16[40,1792]{1,0:T(8,128)(2,1)S(1)} %fusion.58), channel_id=1, source_target_pairs={{0,8},{1,9},{2,0},{3,1},{4,12},{5,13},{6,4},{7,5},{8,10},{9,11},{1... | collective-permute-start | bytes 430088 | tf_op jit(solution)/shard_map/ppermute | solution.py:70
  130.3 8.4 %collective-permute-start.31 = (bf16[40,1792]{1,0:T(8,128)(2,1)S(1)}, bf16[40,1792]{1,0:T(8,128)(2,1)S(1)}, u32[]{:S(2)}, u32[]{:S(2)}) collective-permute-start(bf16[40,1792]{1,0:T(8,128)(2,1)S(1)} %fusion.58), channel_id=1, source_target_pairs={{2,8},{3,9},{6,12},{7,13},{8,2},{9,3},{12,6},{13,7},{18,24},{19,25... | collective-permute-start | bytes 430088 | tf_op jit(solution)/shard_map/ppermute | solution.py:70
  131.0 4.7 %slice-start.11 = ((s8[14680064]{0:T(1024)(128)(4,1)}), s8[2097152]{0:T(1024)(128)(4,1)S(1)}, s32[]{:S(2)}) async-start(s8[14680064]{0:T(1024)(128)(4,1)} %bitcast.136), calls=%async_computation.11 | async-start | bytes 4194304
  137.2 4.6 %collective-permute-start.28 = (bf16[80,2048]{1,0:T(8,128)(2,1)S(1)}, bf16[80,2048]{1,0:T(8,128)(2,1)S(1)}, u32[]{:S(2)}, u32[]{:S(2)}) collective-permute-start(bf16[80,2048]{1,0:T(8,128)(2,1)S(1)} %slice.528), channel_id=1, source_target_pairs={{0,1},{1,0},{2,3},{3,2},{4,5},{5,4},{6,7},{7,6},{8,9},{9,8},{10,11... | collective-permute-start | bytes 983048 | tf_op jit(solution)/shard_map/ppermute | solution.py:33
  138.7 7.4 %collective-permute-start.34 = (bf16[80,1792]{1,0:T(8,128)(2,1)S(1)}, bf16[80,1792]{1,0:T(8,128)(2,1)S(1)}, u32[]{:S(2)}, u32[]{:S(2)}) collective-permute-start(bf16[80,1792]{1,0:T(8,128)(2,1)S(1)} %pad_maximum_fusion.20), channel_id=1, source_target_pairs={{0,4},{1,0},{2,6},{3,2},{4,5},{5,1},{6,7},{7,3},{8,12},{9,8},{10,1... | collective-permute-start | bytes 860168 | tf_op jit(solution)/shard_map/ppermute | solution.py:70
  140.7 5.4 %collective-permute-start.35 = (bf16[80,1792]{1,0:T(8,128)(2,1)S(1)}, bf16[80,1792]{1,0:T(8,128)(2,1)S(1)}, u32[]{:S(2)}, u32[]{:S(2)}) collective-permute-start(bf16[80,1792]{1,0:T(8,128)(2,1)S(1)} %pad_maximum_fusion.20), channel_id=1, source_target_pairs={{1,4},{3,6},{4,1},{6,3},{9,12},{11,14},{12,9},{14,11},{17,20},{19,... | collective-permute-start | bytes 860168 | tf_op jit(solution)/shard_map/ppermute | solution.py:70
  141.8 10.2 %collective-permute-start.29 = (bf16[80,2048]{1,0:T(8,128)(2,1)S(1)}, bf16[80,2048]{1,0:T(8,128)(2,1)S(1)}, u32[]{:S(2)}, u32[]{:S(2)}) collective-permute-start(bf16[80,2048]{1,0:T(8,128)(2,1)S(1)} %fusion.47), channel_id=1, source_target_pairs={{0,2},{1,3},{2,0},{3,1},{4,6},{5,7},{6,4},{7,5},{8,10},{9,11},{10,... | collective-permute-start | bytes 983048 | tf_op jit(solution)/shard_map/ppermute | solution.py:33
  149.1 3.5 %collective-permute-start.36 = (bf16[80,2048]{1,0:T(8,128)(2,1)S(1)}, bf16[80,2048]{1,0:T(8,128)(2,1)S(1)}, u32[]{:S(2)}, u32[]{:S(2)}) collective-permute-start(bf16[80,2048]{1,0:T(8,128)(2,1)S(1)} %slice.527), channel_id=1, source_target_pairs={{0,1},{1,0},{2,3},{3,2},{4,5},{5,4},{6,7},{7,6},{8,9},{9,8},{10,11... | collective-permute-start | bytes 983048 | tf_op jit(solution)/shard_map/ppermute | solution.py:33
  152.7 12.0 %collective-permute-start.37 = (bf16[80,2048]{1,0:T(8,128)(2,1)S(1)}, bf16[80,2048]{1,0:T(8,128)(2,1)S(1)}, u32[]{:S(2)}, u32[]{:S(2)}) collective-permute-start(bf16[80,2048]{1,0:T(8,128)(2,1)S(1)} %fusion.48), channel_id=1, source_target_pairs={{0,2},{1,3},{2,0},{3,1},{4,6},{5,7},{6,4},{7,5},{8,10},{9,11},{10,... | collective-permute-start | bytes 983048 | tf_op jit(solution)/shard_map/ppermute | solution.py:33
  164.9 3.1 %copy-start = (bf16[160,2048]{1,0:T(8,128)(2,1)S(1)}, bf16[160,2048]{1,0:T(8,128)(2,1)}, u32[]{:S(2)}) copy-start(bf16[160,2048]{1,0:T(8,128)(2,1)} %param.5) | copy-start | bytes 1966084
  165.8 2.2 %collective-permute-start.38 = (bf16[160,2048]{1,0:T(8,128)(2,1)S(1)}, bf16[160,2048]{1,0:T(8,128)(2,1)S(1)}, u32[]{:S(2)}, u32[]{:S(2)}) collective-permute-start(bf16[160,2048]{1,0:T(8,128)(2,1)S(1)} %select_convert_fusion), channel_id=1, source_target_pairs={{0,1},{1,0},{2,3},{3,2},{4,5},{5,4},{6,7},{7,6},{8,9},{9,8},{10,11... | collective-permute-start | bytes 1966088 | tf_op jit(solution)/shard_map/ppermute | solution.py:33

commit v7 on v6

--- a/solution.py
+++ b/solution.py
@@ -6,21 +6,10 @@
 UNIT_CHUNKS = 2
 HALVES = 2
 EDGES = {
-    "t1.add": ["t0.columns"],
-    "c00.dots": ["t1.columns"],
-    "t1.cores": ["c01.dots"],
+    "t1.add": ["t0.halves"],
     "c01.dots": ["c00.sum"],
-    "c10.dots": ["c01.cores_swapped"],
-    "c11.dots": ["c10.cores_swapped"],
-    "c00.hidden": ["c01.sum"],
-    "c01.hidden": ["c10.sum"],
-    "c10.hidden": ["c11.sum"],
-    "c00.columns": ["c01.hidden"],
-    "c01.columns": ["c10.hidden"],
-    "c10.columns": ["c11.hidden"],
-    "c00.cores": ["c01.columns"],
-    "c01.cores": ["c10.columns"],
-    "c10.cores": ["c11.columns"],
+    "c10.dots": ["c01.sum"],
+    "c11.dots": ["c10.sum"],
 }
 
 
@@ -79,14 +68,6 @@
 
         return finish
 
-    def to_columns(value):
-        return one_step(
-            value,
-            zh == x,
-            lambda zh, zl, x, k: (1 - zh, zl, x, k) if x == zh else (zh, zl, 1 - x, k),
-            lambda zh, zl, x, k: None if x == zh else (1 - zh, zl, 1 - x, k),
-        )
-
     def to_cores(value):
         return one_step(
             value,
@@ -109,10 +90,21 @@
         seen[step] = value
         return value
 
+    def swap_x(value):
+        pairs = [[i, i ^ 2] for i in range(col_count) if not i & 2]
+        both = lax.all_gather(value, "col", axis_index_groups=pairs)
+        return lax.dynamic_index_in_dim(both, 1 - x, keepdims=False)
+
     def spread_steps(name, value):
-        finish = to_columns(value)
-        yield
-        pair = issued(name + ".columns", finish(ordered(name + ".columns", value)))
+        other = flip(value, "row", 2)
+        yield
+        other = ordered(name + ".halves", other)
+        keep = jnp.where(zh == x, value, other)
+        send = issued(name + ".halves", jnp.where(zh == x, other, value))
+        got = swap_x(send)
+        yield
+        got = ordered(name + ".columns", got)
+        pair = issued(name + ".columns", jnp.concatenate([keep, got], axis=0))
         finish = to_cores(pair)
         yield
         return issued(name + ".cores", finish(ordered(name + ".cores", pair)))
@@ -124,7 +116,7 @@
         sib = jnp.concatenate(mine)[:, None] == places[1][None]
         rows = dot(own.astype(jnp.bfloat16), tokens) + dot(sib.astype(jnp.bfloat16), sibling)
         rows = rows.astype(jnp.bfloat16).reshape(HALVES, 2, piece, width)
-        picked["got"] = flip(rows[:, 1], "col", 2)
+        picked["got"] = swap_x(rows[:, 1])
         picked["rows"] = rows[:, 0]
         return None
         yield
@@ -145,7 +137,7 @@
         got = ordered(name + ".sum", got)
         gate, up = gate[:half] + got[0], up[:half] + got[1]
         send = issued(name + ".sum", jnp.stack([gate[piece:], up[piece:]]).astype(jnp.bfloat16))
-        got = flip(send, "col", 2)
+        got = swap_x(send)
         yield
         got = ordered(name + ".hidden", got)
         gate, up = gate[:piece] + got[0], up[:piece] + got[1]
@@ -160,7 +152,7 @@
         got = flip(branch[half:].astype(jnp.bfloat16), "col", 1)
         yield
         total = issued(name + ".total", branch[:half] + ordered(name + ".total", got))
-        got = flip(total.astype(jnp.bfloat16), "col", 2)
+        got = swap_x(total.astype(jnp.bfloat16))
         yield
         got = ordered(name + ".all", got)
         return issued(name + ".all", total + jnp.concatenate([got[piece:], got[:piece]], axis=0))

time: 170 us -> 199 us (1.17)
  blocking collectives: 0 us -> 107 us
  waiting for transfers between devices: 58.1 us -> 13.9 us
  starting transfers between devices: 69.3 us -> 32.1 us
  matrix products: 31.5 us -> 33.8 us
    all_gather x0 -> x13, blocking collectives: none -> 107 us  [swap_x(): both = lax.all_gather(value, 'col', axis_index_groups=pairs)]
    ppermute x15 -> x14, waiting for transfers between devices: 47.8 us -> 13.5 us  [flip(): return lax.ppermute(value, axis, [(i, i ^ bit) for i in range(count)])]
    ppermute x24 -> x12, starting transfers between devices: 38.2 us -> 14.6 us  [move(): return lax.ppermute(value, ('row', 'col'), pairs)]
    ppermute x15 -> x14, starting transfers between devices: 31 us -> 17.5 us  [flip(): return lax.ppermute(value, axis, [(i, i ^ bit) for i in range(count)])]
    ppermute x24 -> x12, waiting for transfers between devices: 10.2 us -> 0.32 us  [move(): return lax.ppermute(value, ('row', 'col'), pairs)]
    dot_general x14, matrix products: 28.7 us -> 31.1 us  [dot(): return jnp.dot(a, b, preferred_element_type=jnp.float32)]
  transfers between devices with their start and end apart: 39 -> 26, of which waited for: 12 -> 4; matrix products, arithmetic and copies ran while one was open for 17% -> 19% of each run, Pallas kernels for 0% -> 0%
where the time goes in v7:
time: 199 us; the launch traced here: 198 us
  blocking collectives  107 us (54%)
  matrix products  33.8 us (17%)
  starting transfers between devices  32.1 us (16%)
  waiting for transfers between devices  13.9 us (7%)
  other arithmetic  7.17 us (4%)
  local copies, waits for them, and re-layouts  3.08 us (2%)
    all_gather x13, blocking collectives, swap_x(): both = lax.all_gather(value, 'col', axis_index_groups=pairs)  107 us
    dot_general x14, matrix products, dot(): return jnp.dot(a, b, preferred_element_type=jnp.float32)  31.1 us
    ppermute x14, starting transfers between devices, flip(): return lax.ppermute(value, axis, [(i, i ^ bit) for i in range(count)])  17.5 us
    ppermute x12, starting transfers between devices, move(): return lax.ppermute(value, ('row', 'col'), pairs)  14.6 us
    ppermute x14, waiting for transfers between devices, flip(): return lax.ppermute(value, axis, [(i, i ^ bit) for i in range(count)])  13.5 us
  transfers between devices with their start and end apart: 26, of which 4 were waited for; matrix products, arithmetic and copies ran while one was open for 19% of the time, Pallas kernels for 0%

profile of v7, /device:TPU:0, one launch (start us, length us, event | category | flops | bytes accessed | tf_op | source)
XLA Modules:
  0.0 198.2 jit_solution(4386542690618375742)
XLA Ops:
  0.0 0.5 collective-permute-start
  0.6 1.4 fusion.90
  2.0 2.5 %compare_select_fusion.1 = (s32[160]{0:T(256)S(1)}, s32[160]{0:T(256)S(1)}) fusion(s32[]{:T(128)} %get-tuple-element.12, s32[]{:T(128)} %get-tuple-element.9, s32[]{:T(128)} %get-tuple-element.10, s32[]{:T(128)} %get-tuple-element.11), kind=kLoop, calls=%fused_computation.198 | loop fusion | flops 960 | bytes 1296 | tf_op jit(solution)/shard_map/jit(_where)/select_n | solution.py:43
  4.5 1.5 fusion.70
  6.0 0.4 fusion.32
  6.4 11.5 %all-gather = bf16[4,1,40,2048]{3,2,1,0:T(8,128)(2,1)S(1)} all-gather(bf16[2,1,40,2048]{3,2,1,0:T(8,128)(2,1)S(1)} %slice.324), channel_id=2, replica_groups={{0,2},{1,3},{4,6},{5,7},{8,10},{9,11},{12,14},{13,15},{16,18},{17,19},{..., dimensions={0}, use_global_device_ids=true | all-gather | bytes 983040 | tf_op jit(solution)/shard_map/all_gather | solution.py:95
  17.9 2.9 %collective-permute-start.1 = (bf16[40,2048]{1,0:T(8,128)(2,1)S(1)}, bf16[40,2048]{1,0:T(8,128)(2,1)S(1)}, u32[]{:S(2)}, u32[]{:S(2)}) collective-permute-start(bf16[40,2048]{1,0:T(8,128)(2,1)S(1)} %get-tuple-element.17), channel_id=1, source_target_pairs={{0,8},{4,12},{8,0},{12,4},{1,9},{5,13},{9,1},{13,5},{2,10},{6,14},... | collective-permute-start | bytes 491528 | tf_op jit(solution)/shard_map/ppermute | solution.py:22
  20.8 0.2 compare_reduce_fusion.1
  21.1 7.4 %collective-permute-done.1 = bf16[40,2048]{1,0:T(8,128)(2,1)S(1)} collective-permute-done((bf16[40,2048]{1,0:T(8,128)(2,1)S(1)}, bf16[40,2048]{1,0:T(8,128)(2,1)S(1)}, u32[]{:S(2)}, u32[]{:S(2)}) %collective-permute-start.1) | collective-permute-done | bytes 163872 | tf_op jit(solution)/shard_map/ppermute | solution.py:22
  28.5 6.0 %all-gather.1 = bf16[80,2048]{1,0:T(8,128)(2,1)S(1)} all-gather(bf16[40,2048]{1,0:T(8,128)(2,1)S(1)} %get-tuple-element.30), channel_id=3, replica_groups={{0,2},{1,3},{4,6},{5,7},{8,10},{9,11},{12,14},{13,15},{16,18},{17,19},{..., dimensions={0}, use_global_device_ids=true | all-gather | bytes 491520 | tf_op jit(solution)/shard_map/all_gather | solution.py:95
  34.6 4.9 %collective-permute-start.2 = (bf16[80,2048]{1,0:T(8,128)(2,1)S(1)}, bf16[80,2048]{1,0:T(8,128)(2,1)S(1)}, u32[]{:S(2)}, u32[]{:S(2)}) collective-permute-start(bf16[80,2048]{1,0:T(8,128)(2,1)S(1)} %pad_maximum_fusion.11), channel_id=1, source_target_pairs={{0,4},{1,0},{2,6},{3,2},{4,5},{5,1},{6,7},{7,3},{8,12},{9,8},{10,1... | collective-permute-start | bytes 983048 | tf_op jit(solution)/shard_map/ppermute | solution.py:59
  39.6 0.7 collective-permute-start.3
  40.3 4.1 %collective-permute-done.13 = bf16[40,2048]{1,0:T(8,128)(2,1)S(1)} collective-permute-done((bf16[40,2048]{1,0:T(8,128)(2,1)S(1)}, bf16[40,2048]{1,0:T(8,128)(2,1)S(1)}, u32[]{:S(2)}, u32[]{:S(2)}) %collective-permute-start.13) | collective-permute-done | bytes 163872 | tf_op jit(solution)/shard_map/ppermute | solution.py:22
  44.4 6.0 %all-gather.5 = bf16[80,2048]{1,0:T(8,128)(2,1)S(1)} all-gather(bf16[40,2048]{1,0:T(8,128)(2,1)S(1)} %get-tuple-element.34), channel_id=7, replica_groups={{0,2},{1,3},{4,6},{5,7},{8,10},{9,11},{12,14},{13,15},{16,18},{17,19},{..., dimensions={0}, use_global_device_ids=true | all-gather | bytes 491520 | tf_op jit(solution)/shard_map/all_gather | solution.py:95
  50.4 0.4 collective-permute-start.14
  50.8 0.7 collective-permute-start.15
  51.5 0.1 broadcast_select_fusion.3
  51.7 4.6 %fusion.18 = f32[160,1792]{1,0:T(8,128)S(1)} fusion(bf16[2048,3584]{1,0:T(8,128)(2,1)} %param.8, bf16[80,2048]{1,0:T(8,128)(2,1)S(1)} %get-tuple-element.28, bf16[80,2048]{1,0:T(8,128)(2,1)S(1)} %get-tuple-element.27), kind=kOutput, calls=%fused_computation.18 | convolution fusion | flops 1175715840 | bytes 9142272 | tf_op jit(solution)/shard_map/dot_general | solution.py:17
  56.3 2.4 %copy-done.1 = bf16[2048,3584]{1,0:T(8,128)(2,1)S(1)} copy-done((bf16[2048,3584]{1,0:T(8,128)(2,1)S(1)}, bf16[2048,3584]{1,0:T(8,128)(2,1)}, u32[]{:S(2)}) %copy-start.1) | copy-done | bytes 14680088
  58.7 1.4 fusion.22
  60.1 1.4 fusion.10
  61.5 4.5 %fusion.6 = f32[160,1792]{1,0:T(8,128)S(1)} fusion(bf16[160,2048]{1,0:T(8,128)(2,1)S(1)} %pad_maximum_fusion.5, bf16[2048,3584]{1,0:T(8,128)(2,1)} %param.8), kind=kOutput, calls=%fused_computation.6 | convolution fusion | flops 1174405120 | bytes 9142272 | tf_op jit(solution)/shard_map/dot_general | solution.py:17
  66.1 1.5 collective-permute-start.4
  67.9 0.1 broadcast_select_fusion.1
  68.1 1.4 fusion.20
  69.5 4.5 %fusion.16 = f32[160,1792]{1,0:T(8,128)S(1)} fusion(bf16[160,2048]{1,0:T(8,128)(2,1)S(1)} %pad_maximum_fusion.6, bf16[2048,3584]{1,0:T(8,128)(2,1)} %param.8), kind=kOutput, calls=%fused_computation.16 | convolution fusion | flops 1174405120 | bytes 9142272 | tf_op jit(solution)/shard_map/dot_general | solution.py:17
  74.0 1.4 fusion.8
  75.4 4.5 %fusion.4 = f32[160,1792]{1,0:T(8,128)S(1)} fusion(bf16[160,2048]{1,0:T(8,128)(2,1)S(1)} %pad_maximum_fusion.6, bf16[2048,3584]{1,0:T(8,128)(2,1)} %param.8), kind=kOutput, calls=%fused_computation.4 | convolution fusion | flops 1174405120 | bytes 9142272 | tf_op jit(solution)/shard_map/dot_general | solution.py:17
  80.0 0.5 collective-permute-start.16
  81.0 10.0 %all_gather.70 = bf16[2,2,40,1792]{3,2,1,0:T(8,128)(2,1)S(1)} all-gather(bf16[1,2,40,1792]{3,2,1,0:T(8,128)(2,1)S(1)} %pad_maximum_fusion.13), channel_id=1, replica_groups={{0,2},{1,3},{4,6},{5,7},{8,10},{9,11},{12,14},{13,15},{16,18},{17,19},{..., dimensions={0}, use_global_device_ids=true | all-gather | bytes 860160 | tf_op jit(solution)/shard_map/all_gather | solution.py:95
  91.1 1.3 collective-permute-start.5
  92.6 9.0 %all_gather.73 = bf16[2,2,40,1792]{3,2,1,0:T(8,128)(2,1)S(1)} all-gather(bf16[1,2,40,1792]{3,2,1,0:T(8,128)(2,1)S(1)} %pad_maximum_fusion.15), channel_id=1, replica_groups={{0,2},{1,3},{4,6},{5,7},{8,10},{9,11},{12,14},{13,15},{16,18},{17,19},{..., dimensions={0}, use_global_device_ids=true | all-gather | bytes 860160 | tf_op jit(solution)/shard_map/all_gather | solution.py:95
  101.5 0.1 fusion.62
  101.7 1.7 collective-permute-start.9
  103.4 5.8 %all-gather.2 = bf16[80,1792]{1,0:T(8,128)(2,1)S(1)} all-gather(bf16[40,1792]{1,0:T(8,128)(2,1)S(1)} %get-tuple-element.38), channel_id=4, replica_groups={{0,2},{1,3},{4,6},{5,7},{8,10},{9,11},{12,14},{13,15},{16,18},{17,19},{..., dimensions={0}, use_global_device_ids=true | all-gather | bytes 430080 | tf_op jit(solution)/shard_map/all_gather | solution.py:95
  109.2 1.2 collective-permute-start.6
  110.4 0.7 collective-permute-start.7
  111.1 7.0 %all-gather.3 = bf16[80,1792]{1,0:T(8,128)(2,1)S(1)} all-gather(bf16[40,1792]{1,0:T(8,128)(2,1)S(1)} %get-tuple-element.42), channel_id=5, replica_groups={{0,2},{1,3},{4,6},{5,7},{8,10},{9,11},{12,14},{13,15},{16,18},{17,19},{..., dimensions={0}, use_global_device_ids=true | all-gather | bytes 430080 | tf_op jit(solution)/shard_map/all_gather | solution.py:95
  118.2 1.0 collective-permute-start.10
  119.2 1.0 collective-permute-start.11
  120.4 10.1 %all_gather.80 = bf16[2,2,40,1792]{3,2,1,0:T(8,128)(2,1)S(1)} all-gather(bf16[1,2,40,1792]{3,2,1,0:T(8,128)(2,1)S(1)} %pad_maximum_fusion.17), channel_id=1, replica_groups={{0,2},{1,3},{4,6},{5,7},{8,10},{9,11},{12,14},{13,15},{16,18},{17,19},{..., dimensions={0}, use_global_device_ids=true | all-gather | bytes 860160 | tf_op jit(solution)/shard_map/all_gather | solution.py:95
  130.7 1.1 collective-permute-start.17
  131.8 0.1 slice_add_fusion.3
  132.0 9.5 %all_gather.83 = bf16[2,2,40,1792]{3,2,1,0:T(8,128)(2,1)S(1)} all-gather(bf16[1,2,40,1792]{3,2,1,0:T(8,128)(2,1)S(1)} %pad_maximum_fusion.19), channel_id=1, replica_groups={{0,2},{1,3},{4,6},{5,7},{8,10},{9,11},{12,14},{13,15},{16,18},{17,19},{..., dimensions={0}, use_global_device_ids=true | all-gather | bytes 860160 | tf_op jit(solution)/shard_map/all_gather | solution.py:95
  141.7 1.8 collective-permute-start.21
  143.5 5.8 %all-gather.6 = bf16[80,1792]{1,0:T(8,128)(2,1)S(1)} all-gather(bf16[40,1792]{1,0:T(8,128)(2,1)S(1)} %get-tuple-element.46), channel_id=8, replica_groups={{0,2},{1,3},{4,6},{5,7},{8,10},{9,11},{12,14},{13,15},{16,18},{17,19},{..., dimensions={0}, use_global_device_ids=true | all-gather | bytes 430080 | tf_op jit(solution)/shard_map/all_gather | solution.py:95
  149.4 6.8 %all-gather.7 = bf16[80,1792]{1,0:T(8,128)(2,1)S(1)} all-gather(bf16[40,1792]{1,0:T(8,128)(2,1)S(1)} %get-tuple-element.50), channel_id=9, replica_groups={{0,2},{1,3},{4,6},{5,7},{8,10},{9,11},{12,14},{13,15},{16,18},{17,19},{..., dimensions={0}, use_global_device_ids=true | all-gather | bytes 430080 | tf_op jit(solution)/shard_map/all_gather | solution.py:95
  156.3 0.7 collective-permute-start.19
  157.0 2.6 %collective-permute-start.22 = (bf16[80,1792]{1,0:T(8,128)(2,1)S(1)}, bf16[80,1792]{1,0:T(8,128)(2,1)S(1)}, u32[]{:S(2)}, u32[]{:S(2)}) collective-permute-start(bf16[80,1792]{1,0:T(8,128)(2,1)S(1)} %pad_maximum_fusion.20), channel_id=1, source_target_pairs={{0,4},{1,0},{2,6},{3,2},{4,5},{5,1},{6,7},{7,3},{8,12},{9,8},{10,1... | collective-permute-start | bytes 860168 | tf_op jit(solution)/shard_map/ppermute | solution.py:59
  159.8 1.4 fusion.2
  161.2 0.7 collective-permute-start.23
  162.1 1.4 fusion.25
  163.5 1.4 collective-permute-start.12
  165.0 0.3 collective-permute-done.22
  165.3 0.1 broadcast_select_fusion.5
  165.4 1.4 fusion
  166.8 0.1 broadcast_select_fusion.7
  167.0 1.5 fusion.28
  168.5 4.5 %collective-permute-start.24 = (bf16[80,2048]{1,0:T(8,128)(2,1)S(1)}, bf16[80,2048]{1,0:T(8,128)(2,1)S(1)}, u32[]{:S(2)}, u32[]{:S(2)}) collective-permute-start(bf16[80,2048]{1,0:T(8,128)(2,1)S(1)} %slice.524), channel_id=1, source_target_pairs={{0,1},{1,0},{2,3},{3,2},{4,5},{5,4},{6,7},{7,6},{8,9},{9,8},{10,11... | collective-permute-start | bytes 983048 | tf_op jit(solution)/shard_map/ppermute | solution.py:22
  173.0 10.3 %all-gather.4 = bf16[160,2048]{1,0:T(8,128)(2,1)S(1)} all-gather(bf16[80,2048]{1,0:T(8,128)(2,1)S(1)} %fusion.47), channel_id=6, replica_groups={{0,2},{1,3},{4,6},{5,7},{8,10},{9,11},{12,14},{13,15},{16,18},{17,19},{..., dimensions={0}, use_global_device_ids=true | all-gather | bytes 983040 | tf_op jit(solution)/shard_map/all_gather | solution.py:95
  183.6 9.5 %all-gather.8 = bf16[160,2048]{1,0:T(8,128)(2,1)S(1)} all-gather(bf16[80,2048]{1,0:T(8,128)(2,1)S(1)} %fusion.48), channel_id=10, replica_groups={{0,2},{1,3},{4,6},{5,7},{8,10},{9,11},{12,14},{13,15},{16,18},{17,19},{..., dimensions={0}, use_global_device_ids=true | all-gather | bytes 983040 | tf_op jit(solution)/shard_map/all_gather | solution.py:95
  193.2 0.9 select_convert_fusion
  194.2 2.1 %collective-permute-done.25 = bf16[160,2048]{1,0:T(8,128)(2,1)S(1)} collective-permute-done((bf16[160,2048]{1,0:T(8,128)(2,1)S(1)}, bf16[160,2048]{1,0:T(8,128)(2,1)S(1)}, u32[]{:S(2)}, u32[]{:S(2)}) %collective-permute-start.25) | collective-permute-done | bytes 655392 | tf_op jit(solution)/shard_map/ppermute | solution.py:22
  196.3 1.8 fusion.33
  (105 shorter events, 3.3 us)
Async XLA Ops:
  0.0 5.9 %collective-permute-start = (bf16[160,2048]{1,0:T(8,128)(2,1)}, bf16[160,2048]{1,0:T(8,128)(2,1)S(1)}, u32[]{:S(2)}, u32[]{:S(2)}) collective-permute-start(bf16[160,2048]{1,0:T(8,128)(2,1)} %param.5), channel_id=1, source_target_pairs={{0,1},{1,0},{2,3},{3,2},{4,5},{5,4},{6,7},{7,6},{8,9},{9,8},{10,11... | collective-permute-start | bytes 1966088 | tf_op jit(solution)/shard_map/ppermute | solution.py:22
  17.9 10.5 %collective-permute-start.1 = (bf16[40,2048]{1,0:T(8,128)(2,1)S(1)}, bf16[40,2048]{1,0:T(8,128)(2,1)S(1)}, u32[]{:S(2)}, u32[]{:S(2)}) collective-permute-start(bf16[40,2048]{1,0:T(8,128)(2,1)S(1)} %get-tuple-element.17), channel_id=1, source_target_pairs={{0,8},{4,12},{8,0},{12,4},{1,9},{5,13},{9,1},{13,5},{2,10},{6,14},... | collective-permute-start | bytes 491528 | tf_op jit(solution)/shard_map/ppermute | solution.py:22
  34.5 9.8 %collective-permute-start.13 = (bf16[40,2048]{1,0:T(8,128)(2,1)S(1)}, bf16[40,2048]{1,0:T(8,128)(2,1)S(1)}, u32[]{:S(2)}, u32[]{:S(2)}) collective-permute-start(bf16[40,2048]{1,0:T(8,128)(2,1)S(1)} %fusion.67), channel_id=1, source_target_pairs={{0,8},{4,12},{8,0},{12,4},{1,9},{5,13},{9,1},{13,5},{2,10},{6,14},... | collective-permute-start | bytes 491528 | tf_op jit(solution)/shard_map/ppermute | solution.py:22
  34.6 16.8 %collective-permute-start.2 = (bf16[80,2048]{1,0:T(8,128)(2,1)S(1)}, bf16[80,2048]{1,0:T(8,128)(2,1)S(1)}, u32[]{:S(2)}, u32[]{:S(2)}) collective-permute-start(bf16[80,2048]{1,0:T(8,128)(2,1)S(1)} %pad_maximum_fusion.11), channel_id=1, source_target_pairs={{0,4},{1,0},{2,6},{3,2},{4,5},{5,1},{6,7},{7,3},{8,12},{9,8},{10,1... | collective-permute-start | bytes 983048 | tf_op jit(solution)/shard_map/ppermute | solution.py:59
  39.6 11.9 %collective-permute-start.3 = (bf16[80,2048]{1,0:T(8,128)(2,1)S(1)}, bf16[80,2048]{1,0:T(8,128)(2,1)S(1)}, u32[]{:S(2)}, u32[]{:S(2)}) collective-permute-start(bf16[80,2048]{1,0:T(8,128)(2,1)S(1)} %pad_maximum_fusion.11), channel_id=1, source_target_pairs={{1,4},{3,6},{4,1},{6,3},{9,12},{11,14},{12,9},{14,11},{17,20},{19,... | collective-permute-start | bytes 983048 | tf_op jit(solution)/shard_map/ppermute | solution.py:59
  50.4 17.5 %collective-permute-start.14 = (bf16[80,2048]{1,0:T(8,128)(2,1)S(1)}, bf16[80,2048]{1,0:T(8,128)(2,1)S(1)}, u32[]{:S(2)}, u32[]{:S(2)}) collective-permute-start(bf16[80,2048]{1,0:T(8,128)(2,1)S(1)} %pad_maximum_fusion.12), channel_id=1, source_target_pairs={{0,4},{1,0},{2,6},{3,2},{4,5},{5,1},{6,7},{7,3},{8,12},{9,8},{10,1... | collective-permute-start | bytes 983048 | tf_op jit(solution)/shard_map/ppermute | solution.py:59
  50.8 17.1 %collective-permute-start.15 = (bf16[80,2048]{1,0:T(8,128)(2,1)S(1)}, bf16[80,2048]{1,0:T(8,128)(2,1)S(1)}, u32[]{:S(2)}, u32[]{:S(2)}) collective-permute-start(bf16[80,2048]{1,0:T(8,128)(2,1)S(1)} %pad_maximum_fusion.12), channel_id=1, source_target_pairs={{1,4},{3,6},{4,1},{6,3},{9,12},{11,14},{12,9},{14,11},{17,20},{19,... | collective-permute-start | bytes 983048 | tf_op jit(solution)/shard_map/ppermute | solution.py:59
  51.5 7.3 %copy-start.1 = (bf16[2048,3584]{1,0:T(8,128)(2,1)S(1)}, bf16[2048,3584]{1,0:T(8,128)(2,1)}, u32[]{:S(2)}) copy-start(bf16[2048,3584]{1,0:T(8,128)(2,1)} %param.7) | copy-start | bytes 44040196
  66.1 14.7 %collective-permute-start.4 = (bf16[2,80,1792]{2,1,0:T(8,128)(2,1)S(1)}, bf16[2,80,1792]{2,1,0:T(8,128)(2,1)S(1)}, u32[]{:S(2)}, u32[]{:S(2)}) collective-permute-start(bf16[2,80,1792]{2,1,0:T(8,128)(2,1)S(1)} %pad_maximum_fusion.7), channel_id=1, source_target_pairs={{0,1},{1,0},{2,3},{3,2},{4,5},{5,4},{6,7},{7,6},{8,9},{9,8},{10,11... | collective-permute-start | bytes 1720328 | tf_op jit(solution)/shard_map/ppermute | solution.py:22
  67.8 24.6 %collective-permute-start.8 = (bf16[2,80,1792]{2,1,0:T(8,128)(2,1)S(1)}, bf16[2,80,1792]{2,1,0:T(8,128)(2,1)S(1)}, u32[]{:S(2)}, u32[]{:S(2)}) collective-permute-start(bf16[2,80,1792]{2,1,0:T(8,128)(2,1)S(1)} %pad_maximum_fusion.8), channel_id=1, source_target_pairs={{0,1},{1,0},{2,3},{3,2},{4,5},{5,4},{6,7},{7,6},{8,9},{9,8},{10,11... | collective-permute-start | bytes 1720328 | tf_op jit(solution)/shard_map/ppermute | solution.py:22
  80.0 39.2 %collective-permute-start.16 = (bf16[2,80,1792]{2,1,0:T(8,128)(2,1)S(1)}, bf16[2,80,1792]{2,1,0:T(8,128)(2,1)S(1)}, u32[]{:S(2)}, u32[]{:S(2)}) collective-permute-start(bf16[2,80,1792]{2,1,0:T(8,128)(2,1)S(1)} %pad_maximum_fusion.9), channel_id=1, source_target_pairs={{0,1},{1,0},{2,3},{3,2},{4,5},{5,4},{6,7},{7,6},{8,9},{9,8},{10,11... | collective-permute-start | bytes 1720328 | tf_op jit(solution)/shard_map/ppermute | solution.py:22
  80.7 50.0 %collective-permute-start.20 = (bf16[2,80,1792]{2,1,0:T(8,128)(2,1)S(1)}, bf16[2,80,1792]{2,1,0:T(8,128)(2,1)S(1)}, u32[]{:S(2)}, u32[]{:S(2)}) collective-permute-start(bf16[2,80,1792]{2,1,0:T(8,128)(2,1)S(1)} %pad_maximum_fusion.10), channel_id=1, source_target_pairs={{0,1},{1,0},{2,3},{3,2},{4,5},{5,4},{6,7},{7,6},{8,9},{9,8},{10,11... | collective-permute-start | bytes 1720328 | tf_op jit(solution)/shard_map/ppermute | solution.py:22
  80.8 79.0 %slice-start = ((s8[14680064]{0:T(1024)(128)(4,1)}), s8[2097152]{0:T(1024)(128)(4,1)S(1)}, s32[]{:S(2)}) async-start(s8[14680064]{0:T(1024)(128)(4,1)} %bitcast.170), calls=%async_computation | async-start | bytes 4194304
  91.1 68.7 %slice-start.1 = ((s8[14680064]{0:T(1024)(128)(4,1)}), s8[4194304]{0:T(1024)(128)(4,1)S(1)}, s32[]{:S(2)}) async-start(s8[14680064]{0:T(1024)(128)(4,1)} %bitcast.170), calls=%async_computation.1 | async-start | bytes 8388608
  91.1 12.2 %collective-permute-start.5 = (bf16[40,1792]{1,0:T(8,128)(2,1)S(1)}, bf16[40,1792]{1,0:T(8,128)(2,1)S(1)}, u32[]{:S(2)}, u32[]{:S(2)}) collective-permute-start(bf16[40,1792]{1,0:T(8,128)(2,1)S(1)} %fusion.64), channel_id=1, source_target_pairs={{0,8},{4,12},{8,0},{12,4},{1,9},{5,13},{9,1},{13,5},{2,10},{6,14},... | collective-permute-start | bytes 430088 | tf_op jit(solution)/shard_map/ppermute | solution.py:22
  101.7 9.4 %collective-permute-start.9 = (bf16[40,1792]{1,0:T(8,128)(2,1)S(1)}, bf16[40,1792]{1,0:T(8,128)(2,1)S(1)}, u32[]{:S(2)}, u32[]{:S(2)}) collective-permute-start(bf16[40,1792]{1,0:T(8,128)(2,1)S(1)} %fusion.62), channel_id=1, source_target_pairs={{0,8},{4,12},{8,0},{12,4},{1,9},{5,13},{9,1},{13,5},{2,10},{6,14},... | collective-permute-start | bytes 430088 | tf_op jit(solution)/shard_map/ppermute | solution.py:22
  109.2 52.0 %collective-permute-start.6 = (bf16[80,1792]{1,0:T(8,128)(2,1)S(1)}, bf16[80,1792]{1,0:T(8,128)(2,1)S(1)}, u32[]{:S(2)}, u32[]{:S(2)}) collective-permute-start(bf16[80,1792]{1,0:T(8,128)(2,1)S(1)} %pad_maximum_fusion.14), channel_id=1, source_target_pairs={{0,4},{1,0},{2,6},{3,2},{4,5},{5,1},{6,7},{7,3},{8,12},{9,8},{10,1... | collective-permute-start | bytes 860168 | tf_op jit(solution)/shard_map/ppermute | solution.py:59
  110.4 51.5 %collective-permute-start.7 = (bf16[80,1792]{1,0:T(8,128)(2,1)S(1)}, bf16[80,1792]{1,0:T(8,128)(2,1)S(1)}, u32[]{:S(2)}, u32[]{:S(2)}) collective-permute-start(bf16[80,1792]{1,0:T(8,128)(2,1)S(1)} %pad_maximum_fusion.14), channel_id=1, source_target_pairs={{1,4},{3,6},{4,1},{6,3},{9,12},{11,14},{12,9},{14,11},{17,20},{19,... | collective-permute-start | bytes 860168 | tf_op jit(solution)/shard_map/ppermute | solution.py:59
  118.2 41.6 %slice-start.2 = ((s8[14680064]{0:T(1024)(128)(4,1)}), s8[4194304]{0:T(1024)(128)(4,1)S(1)}, s32[]{:S(2)}) async-start(s8[14680064]{0:T(1024)(128)(4,1)} %bitcast.170), calls=%async_computation.2 | async-start | bytes 8388608
  118.2 38.1 %collective-permute-start.10 = (bf16[80,1792]{1,0:T(8,128)(2,1)S(1)}, bf16[80,1792]{1,0:T(8,128)(2,1)S(1)}, u32[]{:S(2)}, u32[]{:S(2)}) collective-permute-start(bf16[80,1792]{1,0:T(8,128)(2,1)S(1)} %pad_maximum_fusion.16), channel_id=1, source_target_pairs={{0,4},{1,0},{2,6},{3,2},{4,5},{5,1},{6,7},{7,3},{8,12},{9,8},{10,1... | collective-permute-start | bytes 860168 | tf_op jit(solution)/shard_map/ppermute | solution.py:59
  119.2 37.8 %collective-permute-start.11 = (bf16[80,1792]{1,0:T(8,128)(2,1)S(1)}, bf16[80,1792]{1,0:T(8,128)(2,1)S(1)}, u32[]{:S(2)}, u32[]{:S(2)}) collective-permute-start(bf16[80,1792]{1,0:T(8,128)(2,1)S(1)} %pad_maximum_fusion.16), channel_id=1, source_target_pairs={{1,4},{3,6},{4,1},{6,3},{9,12},{11,14},{12,9},{14,11},{17,20},{19,... | collective-permute-start | bytes 860168 | tf_op jit(solution)/shard_map/ppermute | solution.py:59
  130.7 11.0 %collective-permute-start.17 = (bf16[40,1792]{1,0:T(8,128)(2,1)S(1)}, bf16[40,1792]{1,0:T(8,128)(2,1)S(1)}, u32[]{:S(2)}, u32[]{:S(2)}) collective-permute-start(bf16[40,1792]{1,0:T(8,128)(2,1)S(1)} %fusion.60), channel_id=1, source_target_pairs={{0,8},{4,12},{8,0},{12,4},{1,9},{5,13},{9,1},{13,5},{2,10},{6,14},... | collective-permute-start | bytes 430088 | tf_op jit(solution)/shard_map/ppermute | solution.py:22
  131.9 27.9 %slice-start.3 = ((s8[14680064]{0:T(1024)(128)(4,1)}), s8[4194304]{0:T(1024)(128)(4,1)S(1)}, s32[]{:S(2)}) async-start(s8[14680064]{0:T(1024)(128)(4,1)} %bitcast.170), calls=%async_computation.3 | async-start | bytes 8388608
  141.7 7.7 %collective-permute-start.21 = (bf16[40,1792]{1,0:T(8,128)(2,1)S(1)}, bf16[40,1792]{1,0:T(8,128)(2,1)S(1)}, u32[]{:S(2)}, u32[]{:S(2)}) collective-permute-start(bf16[40,1792]{1,0:T(8,128)(2,1)S(1)} %fusion.58), channel_id=1, source_target_pairs={{0,8},{4,12},{8,0},{12,4},{1,9},{5,13},{9,1},{13,5},{2,10},{6,14},... | collective-permute-start | bytes 430088 | tf_op jit(solution)/shard_map/ppermute | solution.py:22
  149.3 17.5 %collective-permute-start.18 = (bf16[80,1792]{1,0:T(8,128)(2,1)S(1)}, bf16[80,1792]{1,0:T(8,128)(2,1)S(1)}, u32[]{:S(2)}, u32[]{:S(2)}) collective-permute-start(bf16[80,1792]{1,0:T(8,128)(2,1)S(1)} %pad_maximum_fusion.18), channel_id=1, source_target_pairs={{0,4},{1,0},{2,6},{3,2},{4,5},{5,1},{6,7},{7,3},{8,12},{9,8},{10,1... | collective-permute-start | bytes 860168 | tf_op jit(solution)/shard_map/ppermute | solution.py:59
  156.3 10.5 %collective-permute-start.19 = (bf16[80,1792]{1,0:T(8,128)(2,1)S(1)}, bf16[80,1792]{1,0:T(8,128)(2,1)S(1)}, u32[]{:S(2)}, u32[]{:S(2)}) collective-permute-start(bf16[80,1792]{1,0:T(8,128)(2,1)S(1)} %pad_maximum_fusion.18), channel_id=1, source_target_pairs={{1,4},{3,6},{4,1},{6,3},{9,12},{11,14},{12,9},{14,11},{17,20},{19,... | collective-permute-start | bytes 860168 | tf_op jit(solution)/shard_map/ppermute | solution.py:59
  157.0 8.2 %collective-permute-start.22 = (bf16[80,1792]{1,0:T(8,128)(2,1)S(1)}, bf16[80,1792]{1,0:T(8,128)(2,1)S(1)}, u32[]{:S(2)}, u32[]{:S(2)}) collective-permute-start(bf16[80,1792]{1,0:T(8,128)(2,1)S(1)} %pad_maximum_fusion.20), channel_id=1, source_target_pairs={{0,4},{1,0},{2,6},{3,2},{4,5},{5,1},{6,7},{7,3},{8,12},{9,8},{10,1... | collective-permute-start | bytes 860168 | tf_op jit(solution)/shard_map/ppermute | solution.py:59
  161.2 4.0 %collective-permute-start.23 = (bf16[80,1792]{1,0:T(8,128)(2,1)S(1)}, bf16[80,1792]{1,0:T(8,128)(2,1)S(1)}, u32[]{:S(2)}, u32[]{:S(2)}) collective-permute-start(bf16[80,1792]{1,0:T(8,128)(2,1)S(1)} %pad_maximum_fusion.20), channel_id=1, source_target_pairs={{1,4},{3,6},{4,1},{6,3},{9,12},{11,14},{12,9},{14,11},{17,20},{19,... | collective-permute-start | bytes 860168 | tf_op jit(solution)/shard_map/ppermute | solution.py:59
  163.5 9.4 %collective-permute-start.12 = (bf16[80,2048]{1,0:T(8,128)(2,1)S(1)}, bf16[80,2048]{1,0:T(8,128)(2,1)S(1)}, u32[]{:S(2)}, u32[]{:S(2)}) collective-permute-start(bf16[80,2048]{1,0:T(8,128)(2,1)S(1)} %slice.525), channel_id=1, source_target_pairs={{0,1},{1,0},{2,3},{3,2},{4,5},{5,4},{6,7},{7,6},{8,9},{9,8},{10,11... | collective-permute-start | bytes 983048 | tf_op jit(solution)/shard_map/ppermute | solution.py:22
  168.5 15.0 %collective-permute-start.24 = (bf16[80,2048]{1,0:T(8,128)(2,1)S(1)}, bf16[80,2048]{1,0:T(8,128)(2,1)S(1)}, u32[]{:S(2)}, u32[]{:S(2)}) collective-permute-start(bf16[80,2048]{1,0:T(8,128)(2,1)S(1)} %slice.524), channel_id=1, source_target_pairs={{0,1},{1,0},{2,3},{3,2},{4,5},{5,4},{6,7},{7,6},{8,9},{9,8},{10,11... | collective-permute-start | bytes 983048 | tf_op jit(solution)/shard_map/ppermute | solution.py:22
  193.2 3.1 %copy-start = (bf16[160,2048]{1,0:T(8,128)(2,1)S(1)}, bf16[160,2048]{1,0:T(8,128)(2,1)}, u32[]{:S(2)}) copy-start(bf16[160,2048]{1,0:T(8,128)(2,1)} %param.5) | copy-start | bytes 1966084
  194.2 2.2 %collective-permute-start.25 = (bf16[160,2048]{1,0:T(8,128)(2,1)S(1)}, bf16[160,2048]{1,0:T(8,128)(2,1)S(1)}, u32[]{:S(2)}, u32[]{:S(2)}) collective-permute-start(bf16[160,2048]{1,0:T(8,128)(2,1)S(1)} %select_convert_fusion), channel_id=1, source_target_pairs={{0,1},{1,0},{2,3},{3,2},{4,5},{5,4},{6,7},{7,6},{8,9},{9,8},{10,11... | collective-permute-start | bytes 1966088 | tf_op jit(solution)/shard_map/ppermute | solution.py:22

commit v8 on v7

--- a/solution.py
+++ b/solution.py
@@ -1,15 +1,29 @@
+import functools
+
 import jax
 import jax.numpy as jnp
 from jax import lax
+from jax.experimental import pallas as pl
+from jax.experimental.pallas import tpu as pltpu
 from jax.sharding import PartitionSpec as P
 
-UNIT_CHUNKS = 2
 HALVES = 2
+PARTS = ((14, 14), (18, 10))
 EDGES = {
+    "w.pull": ["t0.add"],
+    "t0.halves": ["w.pull"],
     "t1.add": ["t0.halves"],
+    "t1.halves": ["t0.columns"],
+    "c00.dots": ["t1.columns"],
     "c01.dots": ["c00.sum"],
-    "c10.dots": ["c01.sum"],
+    "t1.cores": ["c01.sum"],
+    "c00.hidden": ["c01.sum"],
+    "c01.hidden": ["c10.sum"],
     "c11.dots": ["c10.sum"],
+    "c00.halves": ["c01.hidden"],
+    "c10.hidden": ["c11.sum"],
+    "c01.halves": ["c10.hidden"],
+    "c10.halves": ["c11.hidden"],
 }
 
 
@@ -20,6 +34,41 @@
 def flip(value, axis, bit):
     count = lax.axis_size(axis)
     return lax.ppermute(value, axis, [(i, i ^ bit) for i in range(count)])
+
+
+def pull_kernel(first, end, tick_ref, gate_ref, up_ref, gate_here, up_here, done_ref, sems):
+    del tick_ref
+    columns = pl.ds(first, end - first)
+    copies = [
+        pltpu.make_async_copy(source.at[:, columns], here, sems.at[i])
+        for i, (source, here) in enumerate(((gate_ref, gate_here), (up_ref, up_here)))
+    ]
+    for copy in copies:
+        copy.start()
+    for copy in copies:
+        copy.wait()
+    done_ref[...] = jnp.zeros_like(done_ref)
+
+
+def pull(gate_weight, up_weight, first, end, tick):
+    far = pl.BlockSpec(memory_space=pltpu.HBM)
+    near = pl.BlockSpec(memory_space=pltpu.VMEM)
+    here = pltpu.VMEM((gate_weight.shape[0], end - first), gate_weight.dtype)
+    return pl.pallas_call(
+        functools.partial(pull_kernel, first, end),
+        in_specs=[pl.BlockSpec(memory_space=pltpu.SMEM), far, far],
+        out_specs=[near, near, near],
+        out_shape=[here, here, jax.ShapeDtypeStruct((8, 128), jnp.float32)],
+        scratch_shapes=[pltpu.SemaphoreType.DMA((2,))],
+        compiler_params=pltpu.CompilerParams(
+            vmem_limit_bytes=4 * gate_weight.shape[0] * (end - first) + 2**20
+        ),
+        cost_estimate=pl.CostEstimate(flops=0, bytes_accessed=0, transcendentals=0),
+    )(
+        tick,
+        pltpu.with_memory_space_constraint(gate_weight, pltpu.HBM),
+        pltpu.with_memory_space_constraint(up_weight, pltpu.HBM),
+    )
 
 
 def stationary(tokens, lengths, gate_weight, up_weight, down_weight):
@@ -32,7 +81,12 @@
     quarter = slots // 2
     piece = quarter // HALVES
     half = 2 * piece
-    step = units // UNIT_CHUNKS
+    spans = []
+    for sizes in PARTS:
+        ends = [0]
+        for size in sizes:
+            ends.append(ends[-1] + units * size // sum(sizes))
+        spans.append(list(zip(ends[:-1], ends[1:])))
 
     rows = jnp.arange(lengths.shape[0], dtype=jnp.int32)
     slot = jnp.arange(slots, dtype=jnp.int32)
@@ -91,9 +145,7 @@
         return value
 
     def swap_x(value):
-        pairs = [[i, i ^ 2] for i in range(col_count) if not i & 2]
-        both = lax.all_gather(value, "col", axis_index_groups=pairs)
-        return lax.dynamic_index_in_dim(both, 1 - x, keepdims=False)
+        return flip(value, "col", 2)
 
     def spread_steps(name, value):
         other = flip(value, "row", 2)
@@ -121,16 +173,28 @@
         return None
         yield
 
+    pulled = []
+
+    def pull_steps():
+        tick = ordered("w.pull", lengths)
+        *both, done = pull(gate_weight, up_weight, *spans[0][0], tick)
+        pulled.extend(both)
+        issued("w.pull", done)
+        return None
+        yield
+
     def half_steps(name, h):
-        own = ordered(name + ".add", picked["rows"][h]) + picked["got"][h]
-        own = issued(name + ".add", own)
+        own = issued(name + ".add", ordered(name + ".add", picked["rows"][h]) + picked["got"][h])
         return (yield from spread_steps(name, own))
 
     def chunk_steps(name, h, i):
         full = result("t" + str(h))
-        part = slice(i * step, (i + 1) * step)
+        part = slice(*spans[h][i])
         full = ordered(name + ".dots", full)
-        gate, up = dot(full, gate_weight[:, part]), dot(full, up_weight[:, part])
+        if (h, i) == (0, 0):
+            gate, up = dot(full, pulled[0]), dot(full, pulled[1])
+        else:
+            gate, up = dot(full, gate_weight[:, part]), dot(full, up_weight[:, part])
         send = issued(name + ".dots", jnp.stack([gate[half:], up[half:]]).astype(jnp.bfloat16))
         got = issued(name + ".cores_swapped", flip(send, "col", 1))
         yield
@@ -147,7 +211,7 @@
         return issued(name + ".down", dot(whole, down_weight[part]))
 
     def branch_steps(name, h):
-        parts = [result("c" + str(h) + str(i)) for i in range(UNIT_CHUNKS)]
+        parts = [result("c" + str(h) + str(i)) for i in range(len(spans[h]))]
         branch = issued(name + ".branch", sum(parts[1:], parts[0]))
         got = flip(branch[half:].astype(jnp.bfloat16), "col", 1)
         yield
@@ -157,10 +221,10 @@
         got = ordered(name + ".all", got)
         return issued(name + ".all", total + jnp.concatenate([got[piece:], got[:piece]], axis=0))
 
-    chains, results = {"p": pick_steps()}, {}
+    chains, results = {"p": pick_steps(), "w": pull_steps()}, {}
     for h in range(HALVES):
         chains["t" + str(h)] = half_steps("t" + str(h), h)
-        for i in range(UNIT_CHUNKS):
+        for i in range(len(spans[h])):
             chains["c" + str(h) + str(i)] = chunk_steps("c" + str(h) + str(i), h, i)
         chains["b" + str(h)] = branch_steps("b" + str(h), h)
 
@@ -176,6 +240,7 @@
         return results[name]
 
     result("p")
+    result("w")
     for h in range(HALVES):
         result("b" + str(h))
 

time: 199 us -> 161 us (0.81)
  blocking collectives: 107 us -> 0 us
  waiting for transfers between devices: 13.9 us -> 75.6 us
  matrix products: 33.8 us -> 24.4 us
  starting transfers between devices: 32.1 us -> 41.5 us
  Pallas kernels: 0 us -> 6.43 us
  other arithmetic: 7.17 us -> 9.33 us
    all_gather x13 -> x0, blocking collectives: 107 us -> none  [swap_x(): both = lax.all_gather(value, 'col', axis_index_groups=pairs)]
    ppermute x14 -> x27, waiting for transfers between devices: 13.5 us -> 72.7 us  [flip(): return lax.ppermute(value, axis, [(i, i ^ bit) for i in range(count)])]
    ppermute x14 -> x27, starting transfers between devices: 17.5 us -> 30.8 us  [flip(): return lax.ppermute(value, axis, [(i, i ^ bit) for i in range(count)])]
    dot_general x14, matrix products: 31.1 us -> 21.6 us  [dot(): return jnp.dot(a, b, preferred_element_type=jnp.float32)]
    pallas_call x0 -> x1, Pallas kernels: none -> 6.43 us  [pull(): pl.pallas_call(functools.partial(pull_kernel, first, end), in_specs=[pl.B...]
    ppermute x12, starting transfers between devices: 14.6 us -> 10.7 us  [move(): return lax.ppermute(value, ('row', 'col'), pairs)]
    ppermute x12, waiting for transfers between devices: 0.32 us -> 2.92 us  [move(): return lax.ppermute(value, ('row', 'col'), pairs)]
  transfers between devices with their start and end apart: 26 -> 39, of which waited for: 4 -> 17; matrix products, arithmetic and copies ran while one was open for 19% -> 15% of each run, Pallas kernels for 0% -> 4%
where the time goes in v8:
time: 161 us; the launch traced here: 160 us
  waiting for transfers between devices  75.6 us (47%)
  starting transfers between devices  41.5 us (26%)
  matrix products  24.4 us (15%)
  other arithmetic  9.33 us (6%)
  Pallas kernels  6.43 us (4%)
  local copies, waits for them, and re-layouts  2.14 us (1%)
    ppermute x27, waiting for transfers between devices, flip(): return lax.ppermute(value, axis, [(i, i ^ bit) for i in range(count)])  72.7 us
    ppermute x27, starting transfers between devices, flip(): return lax.ppermute(value, axis, [(i, i ^ bit) for i in range(count)])  30.8 us
    dot_general x14, matrix products, dot(): return jnp.dot(a, b, preferred_element_type=jnp.float32)  21.6 us
    ppermute x12, starting transfers between devices, move(): return lax.ppermute(value, ('row', 'col'), pairs)  10.7 us
    pallas_call x1, Pallas kernels, pull(): pl.pallas_call(functools.partial(pull_kernel, first, end), in_specs=[pl.B...  6.43 us
  transfers between devices with their start and end apart: 39, of which 17 were waited for; matrix products, arithmetic and copies ran while one was open for 15% of the time, Pallas kernels for 4%

profile of v8, /device:TPU:0, one launch (start us, length us, event | category | flops | bytes accessed | tf_op | source)
XLA Modules:
  0.0 160.4 jit_solution(12126361266603937668)
XLA Ops:
  0.6 1.4 fusion.86
  2.0 2.5 %compare_select_fusion.1 = (s32[160]{0:T(256)S(1)}, s32[160]{0:T(256)S(1)}) fusion(s32[]{:T(128)} %get-tuple-element.40, s32[]{:T(128)} %get-tuple-element.37, s32[]{:T(128)} %get-tuple-element.38, s32[]{:T(128)} %get-tuple-element.39), kind=kLoop, calls=%fused_computation.180 | loop fusion | flops 960 | bytes 1296 | tf_op jit(solution)/shard_map/jit(_where)/select_n | solution.py:97
  4.4 1.5 fusion.68
  6.8 2.6 %collective-permute-start.1 = (bf16[2,40,2048]{2,1,0:T(8,128)(2,1)S(1)}, bf16[2,40,2048]{2,1,0:T(8,128)(2,1)S(1)}, u32[]{:S(2)}, u32[]{:S(2)}) collective-permute-start(bf16[2,40,2048]{2,1,0:T(8,128)(2,1)S(1)} %slice_bitcast_fusion.2), channel_id=1, source_target_pairs={{0,2},{1,3},{2,0},{3,1},{4,6},{5,7},{6,4},{7,5},{8,10},{9,11},{10,... | collective-permute-start | bytes 983048 | tf_op jit(solution)/shard_map/ppermute | solution.py:36
  9.3 8.4 %collective-permute-done.1 = bf16[2,40,2048]{2,1,0:T(8,128)(2,1)S(1)} collective-permute-done((bf16[2,40,2048]{2,1,0:T(8,128)(2,1)S(1)}, bf16[2,40,2048]{2,1,0:T(8,128)(2,1)S(1)}, u32[]{:S(2)}, u32[]{:S(2)}) %collective-permute-start.1) | collective-permute-done | bytes 327712 | tf_op jit(solution)/shard_map/ppermute | solution.py:36
  17.7 2.9 %collective-permute-start.2 = (bf16[40,2048]{1,0:T(8,128)(2,1)S(1)}, bf16[40,2048]{1,0:T(8,128)(2,1)S(1)}, u32[]{:S(2)}, u32[]{:S(2)}) collective-permute-start(bf16[40,2048]{1,0:T(8,128)(2,1)S(1)} %fusion.66), channel_id=1, source_target_pairs={{0,8},{4,12},{8,0},{12,4},{1,9},{5,13},{9,1},{13,5},{2,10},{6,14},... | collective-permute-start | bytes 491528 | tf_op jit(solution)/shard_map/ppermute | solution.py:36
  20.7 7.6 %collective-permute-done.2 = bf16[40,2048]{1,0:T(8,128)(2,1)S(1)} collective-permute-done((bf16[40,2048]{1,0:T(8,128)(2,1)S(1)}, bf16[40,2048]{1,0:T(8,128)(2,1)S(1)}, u32[]{:S(2)}, u32[]{:S(2)}) %collective-permute-start.2) | collective-permute-done | bytes 163872 | tf_op jit(solution)/shard_map/ppermute | solution.py:36
  28.3 1.6 collective-permute-start.3
  30.0 3.7 %collective-permute-done.3 = bf16[40,2048]{1,0:T(8,128)(2,1)S(1)} collective-permute-done((bf16[40,2048]{1,0:T(8,128)(2,1)S(1)}, bf16[40,2048]{1,0:T(8,128)(2,1)S(1)}, u32[]{:S(2)}, u32[]{:S(2)}) %collective-permute-start.3) | collective-permute-done | bytes 163872 | tf_op jit(solution)/shard_map/ppermute | solution.py:36
  33.7 5.7 %collective-permute-done.6 = bf16[40,2048]{1,0:T(8,128)(2,1)S(1)} collective-permute-done((bf16[40,2048]{1,0:T(8,128)(2,1)S(1)}, bf16[40,2048]{1,0:T(8,128)(2,1)S(1)}, u32[]{:S(2)}, u32[]{:S(2)}) %collective-permute-start.6) | collective-permute-done | bytes 163872 | tf_op jit(solution)/shard_map/ppermute | solution.py:36
  39.9 0.7 collective-permute-start.5
  40.6 6.4 %shard_map.55 = (bf16[2048,1792]{1,0:T(8,128)(2,1)S(1)}, bf16[2048,1792]{1,0:T(8,128)(2,1)S(1)}, f32[8,128]{1,0:T(8,128)}) custom-call(s32[4]{0:T(128)S(1)} %copy-done, bf16[2048,3584]{1,0:T(8,128)(2,1)} %gate_ref.1, bf16[2048,3584]{1,0:T(8,128)(2,1)} %up_ref.1), custom_call_target="tpu_custom_call" | custom-call | tf_op jit(solution)/shard_map/pallas_call | solution.py:57
  47.4 1.4 fusion.96
  48.8 1.4 fusion.97
  50.4 1.8 %collective-permute-start.8 = (bf16[2,80,1792]{2,1,0:T(8,128)(2,1)S(1)}, bf16[2,80,1792]{2,1,0:T(8,128)(2,1)S(1)}, u32[]{:S(2)}, u32[]{:S(2)}) collective-permute-start(bf16[2,80,1792]{2,1,0:T(8,128)(2,1)S(1)} %pad_maximum_fusion.8), channel_id=1, source_target_pairs={{0,1},{1,0},{2,3},{3,2},{4,5},{5,4},{6,7},{7,6},{8,9},{9,8},{10,11... | collective-permute-start | bytes 1720328 | tf_op jit(solution)/shard_map/ppermute | solution.py:36
  52.2 1.6 %collective-permute-done.8 = bf16[2,80,1792]{2,1,0:T(8,128)(2,1)S(1)} collective-permute-done((bf16[2,80,1792]{2,1,0:T(8,128)(2,1)S(1)}, bf16[2,80,1792]{2,1,0:T(8,128)(2,1)S(1)}, u32[]{:S(2)}, u32[]{:S(2)}) %collective-permute-start.8) | collective-permute-done | bytes 573472 | tf_op jit(solution)/shard_map/ppermute | solution.py:36
  54.0 0.7 pad_maximum_fusion.15
  54.7 1.4 fusion.12
  56.1 1.0 slice-done.7
  57.2 1.4 fusion.10
  58.7 1.8 %collective-permute-start.10 = (bf16[2,80,1792]{2,1,0:T(8,128)(2,1)S(1)}, bf16[2,80,1792]{2,1,0:T(8,128)(2,1)S(1)}, u32[]{:S(2)}, u32[]{:S(2)}) collective-permute-start(bf16[2,80,1792]{2,1,0:T(8,128)(2,1)S(1)} %pad_maximum_fusion.9), channel_id=1, source_target_pairs={{0,1},{1,0},{2,3},{3,2},{4,5},{5,4},{6,7},{7,6},{8,9},{9,8},{10,11... | collective-permute-start | bytes 1720328 | tf_op jit(solution)/shard_map/ppermute | solution.py:36
  60.4 1.7 %collective-permute-start.13 = (bf16[80,2048]{1,0:T(8,128)(2,1)S(1)}, bf16[80,2048]{1,0:T(8,128)(2,1)S(1)}, u32[]{:S(2)}, u32[]{:S(2)}) collective-permute-start(bf16[80,2048]{1,0:T(8,128)(2,1)S(1)} %pad_maximum_fusion.14), channel_id=1, source_target_pairs={{0,4},{1,0},{2,6},{3,2},{4,5},{5,1},{6,7},{7,3},{8,12},{9,8},{10,1... | collective-permute-start | bytes 983048 | tf_op jit(solution)/shard_map/ppermute | solution.py:113
  62.2 0.8 collective-permute-start.14
  63.0 1.6 %collective-permute-start.9 = (bf16[2,40,1792]{2,1,0:T(8,128)(2,1)}, bf16[2,40,1792]{2,1,0:T(8,128)(2,1)}, u32[]{:S(2)}, u32[]{:S(2)}) collective-permute-start(bf16[2,40,1792]{2,1,0:T(8,128)(2,1)} %pad_maximum_fusion.15), channel_id=1, source_target_pairs={{0,2},{1,3},{2,0},{3,1},{4,6},{5,7},{6,4},{7,5},{8,10},{9,11},{10,... | collective-permute-start | bytes 860168 | tf_op jit(solution)/shard_map/ppermute | solution.py:36
  64.8 0.8 pad_maximum_fusion.16
  65.6 2.9 %collective-permute-done.13 = bf16[80,2048]{1,0:T(8,128)(2,1)S(1)} collective-permute-done((bf16[80,2048]{1,0:T(8,128)(2,1)S(1)}, bf16[80,2048]{1,0:T(8,128)(2,1)S(1)}, u32[]{:S(2)}, u32[]{:S(2)}) %collective-permute-start.13) | collective-permute-done | bytes 327712 | tf_op jit(solution)/shard_map/ppermute | solution.py:113
  68.5 1.7 %fusion.4 = f32[160,2304]{1,0:T(8,128)S(1)} fusion(bf16[2048,3584]{1,0:T(8,128)(2,1)S(1)} %bitcast.130, bf16[80,2048]{1,0:T(8,128)(2,1)S(1)} %get-tuple-element.58, bf16[80,2048]{1,0:T(8,128)(2,1)S(1)} %get-tuple-element.57), kind=kOutput, calls=%fused_computation.4 | convolution fusion | flops 1511260160 | bytes 11567104 | tf_op jit(solution)/shard_map/dot_general | solution.py:31
  70.2 1.7 %fusion.2 = f32[160,2304]{1,0:T(8,128)S(1)} fusion(bf16[2048,3584]{1,0:T(8,128)(2,1)S(1)} %bitcast.132, bf16[80,2048]{1,0:T(8,128)(2,1)S(1)} %get-tuple-element.58, bf16[80,2048]{1,0:T(8,128)(2,1)S(1)} %get-tuple-element.57), kind=kOutput, calls=%fused_computation.2 | convolution fusion | flops 1511260160 | bytes 11567104 | tf_op jit(solution)/shard_map/dot_general | solution.py:31
  72.1 2.3 %collective-permute-start.15 = (bf16[2,80,2304]{2,1,0:T(8,128)(2,1)S(1)}, bf16[2,80,2304]{2,1,0:T(8,128)(2,1)S(1)}, u32[]{:S(2)}, u32[]{:S(2)}) collective-permute-start(bf16[2,80,2304]{2,1,0:T(8,128)(2,1)S(1)} %pad_maximum_fusion.5), channel_id=1, source_target_pairs={{0,1},{1,0},{2,3},{3,2},{4,5},{5,4},{6,7},{7,6},{8,9},{9,8},{10,11... | collective-permute-start | bytes 2211848 | tf_op jit(solution)/shard_map/ppermute | solution.py:36
  74.4 1.6 collective-permute-start.12
  76.0 1.1 fusion.56
  77.1 1.8 %collective-permute-start.11 = (bf16[40,1792]{1,0:T(8,128)(2,1)S(1)}, bf16[40,1792]{1,0:T(8,128)(2,1)S(1)}, u32[]{:S(2)}, u32[]{:S(2)}) collective-permute-start(bf16[40,1792]{1,0:T(8,128)(2,1)S(1)} %fusion.56), channel_id=1, source_target_pairs={{0,8},{4,12},{8,0},{12,4},{1,9},{5,13},{9,1},{13,5},{2,10},{6,14},... | collective-permute-start | bytes 430088 | tf_op jit(solution)/shard_map/ppermute | solution.py:36
  79.2 1.0 fusion.18
  80.3 1.0 fusion.16
  81.6 2.2 %collective-permute-done.12 = bf16[2,40,1792]{2,1,0:T(8,128)(2,1)S(1)} collective-permute-done((bf16[2,40,1792]{2,1,0:T(8,128)(2,1)S(1)}, bf16[2,40,1792]{2,1,0:T(8,128)(2,1)S(1)}, u32[]{:S(2)}, u32[]{:S(2)}) %collective-permute-start.12) | collective-permute-done | bytes 286752 | tf_op jit(solution)/shard_map/ppermute | solution.py:36
  84.0 3.3 %collective-permute-done.11 = bf16[40,1792]{1,0:T(8,128)(2,1)S(1)} collective-permute-done((bf16[40,1792]{1,0:T(8,128)(2,1)S(1)}, bf16[40,1792]{1,0:T(8,128)(2,1)S(1)}, u32[]{:S(2)}, u32[]{:S(2)}) %collective-permute-start.11) | collective-permute-done | bytes 143392 | tf_op jit(solution)/shard_map/ppermute | solution.py:36
  88.0 1.6 %collective-permute-start.20 = (bf16[2,40,2304]{2,1,0:T(8,128)(2,1)S(1)}, bf16[2,40,2304]{2,1,0:T(8,128)(2,1)S(1)}, u32[]{:S(2)}, u32[]{:S(2)}) collective-permute-start(bf16[2,40,2304]{2,1,0:T(8,128)(2,1)S(1)} %pad_maximum_fusion.11), channel_id=1, source_target_pairs={{0,2},{1,3},{2,0},{3,1},{4,6},{5,7},{6,4},{7,5},{8,10},{9,11},{10,... | collective-permute-start | bytes 1105928 | tf_op jit(solution)/shard_map/ppermute | solution.py:36
  89.7 4.3 %collective-permute-done.16 = bf16[40,1792]{1,0:T(8,128)(2,1)S(1)} collective-permute-done((bf16[40,1792]{1,0:T(8,128)(2,1)S(1)}, bf16[40,1792]{1,0:T(8,128)(2,1)S(1)}, u32[]{:S(2)}, u32[]{:S(2)}) %collective-permute-start.16) | collective-permute-done | bytes 143392 | tf_op jit(solution)/shard_map/ppermute | solution.py:36
  94.1 0.7 collective-permute-start.18
  95.5 6.2 %collective-permute-done.20 = bf16[2,40,2304]{2,1,0:T(8,128)(2,1)S(1)} collective-permute-done((bf16[2,40,2304]{2,1,0:T(8,128)(2,1)S(1)}, bf16[2,40,2304]{2,1,0:T(8,128)(2,1)S(1)}, u32[]{:S(2)}, u32[]{:S(2)}) %collective-permute-start.20) | collective-permute-done | bytes 368672 | tf_op jit(solution)/shard_map/ppermute | solution.py:36
  102.6 5.4 %collective-permute-done.22 = bf16[40,1792]{1,0:T(8,128)(2,1)S(1)} collective-permute-done((bf16[40,1792]{1,0:T(8,128)(2,1)S(1)}, bf16[40,1792]{1,0:T(8,128)(2,1)S(1)}, u32[]{:S(2)}, u32[]{:S(2)}) %collective-permute-start.22) | collective-permute-done | bytes 143392 | tf_op jit(solution)/shard_map/ppermute | solution.py:36
  108.0 2.5 %collective-permute-start.23 = (bf16[80,1792]{1,0:T(8,128)(2,1)S(1)}, bf16[80,1792]{1,0:T(8,128)(2,1)S(1)}, u32[]{:S(2)}, u32[]{:S(2)}) collective-permute-start(bf16[80,1792]{1,0:T(8,128)(2,1)S(1)} %pad_maximum_fusion.18), channel_id=1, source_target_pairs={{0,4},{1,0},{2,6},{3,2},{4,5},{5,1},{6,7},{7,3},{8,12},{9,8},{10,1... | collective-permute-start | bytes 860168 | tf_op jit(solution)/shard_map/ppermute | solution.py:113
  110.5 0.7 collective-permute-start.24
  111.3 1.2 collective-permute-start.32
  113.1 5.5 %collective-permute-done.32 = bf16[40,1280]{1,0:T(8,128)(2,1)S(1)} collective-permute-done((bf16[40,1280]{1,0:T(8,128)(2,1)S(1)}, bf16[40,1280]{1,0:T(8,128)(2,1)S(1)}, u32[]{:S(2)}, u32[]{:S(2)}) %collective-permute-start.32) | collective-permute-done | bytes 102432 | tf_op jit(solution)/shard_map/ppermute | solution.py:36
  119.2 0.8 collective-permute-done.29
  120.0 1.1 collective-permute-start.30
  121.1 0.7 collective-permute-start.31
  121.8 2.2 %collective-permute-done.33 = bf16[40,1280]{1,0:T(8,128)(2,1)S(1)} collective-permute-done((bf16[40,1280]{1,0:T(8,128)(2,1)S(1)}, bf16[40,1280]{1,0:T(8,128)(2,1)S(1)}, u32[]{:S(2)}, u32[]{:S(2)}) %collective-permute-start.33) | collective-permute-done | bytes 102432 | tf_op jit(solution)/shard_map/ppermute | solution.py:36
  124.0 0.8 collective-permute-start.34
  124.8 0.9 collective-permute-start.35
  125.9 4.6 %fusion.6 = f32[160,2048]{1,0:T(8,128)S(1)} fusion(bf16[3584,2048]{1,0:T(8,128)(2,1)} %param.9, bf16[80,1792]{1,0:T(8,128)(2,1)S(1)} %get-tuple-element.70, bf16[80,1792]{1,0:T(8,128)(2,1)S(1)} %get-tuple-element.69), kind=kOutput, calls=%fused_computation.6 | convolution fusion | flops 1175552000 | bytes 9224192 | tf_op jit(solution)/shard_map/dot_general | solution.py:31
  130.6 1.4 fusion.21
  132.1 1.4 collective-permute-start.25
  133.6 1.1 fusion.14
  134.9 1.8 %fusion.24 = f32[160,2048]{1,0:T(8,128)S(1)} fusion(f32[160,2048]{1,0:T(8,128)S(1)} %fusion.14, bf16[3584,2048]{1,0:T(8,128)(2,1)S(1)} %bitcast.137, bf16[80,2304]{1,0:T(8,128)(2,1)S(1)} %get-tuple-element.50, bf16[80,2304]{1,0:T(8,128)(2,1)S(1)} %get-tuple-element.49), kind=kOutput, calls=%fused_computation.24 | convolution fusion | flops 1511751680 | bytes 12795904 | tf_op jit(solution)/shard_map/dot_general | solution.py:31
  136.7 1.7 %collective-permute-start.36 = (bf16[80,2048]{1,0:T(8,128)(2,1)S(1)}, bf16[80,2048]{1,0:T(8,128)(2,1)S(1)}, u32[]{:S(2)}, u32[]{:S(2)}) collective-permute-start(bf16[80,2048]{1,0:T(8,128)(2,1)S(1)} %slice.533), channel_id=1, source_target_pairs={{0,1},{1,0},{2,3},{3,2},{4,5},{5,4},{6,7},{7,6},{8,9},{9,8},{10,11... | collective-permute-start | bytes 983048 | tf_op jit(solution)/shard_map/ppermute | solution.py:36
  138.5 1.6 collective-permute-start.26
  140.2 1.2 collective-permute-start.37
  141.4 7.8 %collective-permute-done.26 = bf16[80,2048]{1,0:T(8,128)(2,1)S(1)} collective-permute-done((bf16[80,2048]{1,0:T(8,128)(2,1)S(1)}, bf16[80,2048]{1,0:T(8,128)(2,1)S(1)}, u32[]{:S(2)}, u32[]{:S(2)}) %collective-permute-start.26) | collective-permute-done | bytes 327712 | tf_op jit(solution)/shard_map/ppermute | solution.py:36
  149.3 5.9 %collective-permute-done.37 = bf16[80,2048]{1,0:T(8,128)(2,1)S(1)} collective-permute-done((bf16[80,2048]{1,0:T(8,128)(2,1)S(1)}, bf16[80,2048]{1,0:T(8,128)(2,1)S(1)}, u32[]{:S(2)}, u32[]{:S(2)}) %collective-permute-start.37) | collective-permute-done | bytes 327712 | tf_op jit(solution)/shard_map/ppermute | solution.py:36
  155.4 0.9 select_convert_fusion
  156.4 2.1 %collective-permute-done.38 = bf16[160,2048]{1,0:T(8,128)(2,1)S(1)} collective-permute-done((bf16[160,2048]{1,0:T(8,128)(2,1)S(1)}, bf16[160,2048]{1,0:T(8,128)(2,1)S(1)}, u32[]{:S(2)}, u32[]{:S(2)}) %collective-permute-start.38) | collective-permute-done | bytes 655392 | tf_op jit(solution)/shard_map/ppermute | solution.py:36
  158.5 1.9 %fusion.29 = bf16[160,2048]{1,0:T(8,128)(2,1)} fusion(bf16[160,2048]{1,0:T(8,128)(2,1)S(1)} %collective-permute-done.38, bf16[160,2048]{1,0:T(8,128)(2,1)S(1)} %copy-done.1, f32[80,2048]{1,0:T(8,128)S(1)} %convert_add_fusion, f32[80,2048]{1,0:T(8,128)S(1)} %convert_add_fusion.1, pred[160]{0:T(512)(128)(4,1)S(1)} %get-tuple-element.35, ...), kind=kOutput, calls=%fused_computation.29 | convolution fusion | flops 631137280 | bytes 3278240 | tf_op jit(solution)/shard_map/dot_general | solution.py:251
  (138 shorter events, 8.6 us)
Async XLA Ops:
  0.0 5.9 %collective-permute-start = (bf16[160,2048]{1,0:T(8,128)(2,1)}, bf16[160,2048]{1,0:T(8,128)(2,1)S(1)}, u32[]{:S(2)}, u32[]{:S(2)}) collective-permute-start(bf16[160,2048]{1,0:T(8,128)(2,1)} %param.5), channel_id=1, source_target_pairs={{0,1},{1,0},{2,3},{3,2},{4,5},{5,4},{6,7},{7,6},{8,9},{9,8},{10,11... | collective-permute-start | bytes 1966088 | tf_op jit(solution)/shard_map/ppermute | solution.py:36
  5.9 0.8 copy-start.2
  6.8 10.9 %collective-permute-start.1 = (bf16[2,40,2048]{2,1,0:T(8,128)(2,1)S(1)}, bf16[2,40,2048]{2,1,0:T(8,128)(2,1)S(1)}, u32[]{:S(2)}, u32[]{:S(2)}) collective-permute-start(bf16[2,40,2048]{2,1,0:T(8,128)(2,1)S(1)} %slice_bitcast_fusion.2), channel_id=1, source_target_pairs={{0,2},{1,3},{2,0},{3,1},{4,6},{5,7},{6,4},{7,5},{8,10},{9,11},{10,... | collective-permute-start | bytes 983048 | tf_op jit(solution)/shard_map/ppermute | solution.py:36
  17.7 10.5 %collective-permute-start.2 = (bf16[40,2048]{1,0:T(8,128)(2,1)S(1)}, bf16[40,2048]{1,0:T(8,128)(2,1)S(1)}, u32[]{:S(2)}, u32[]{:S(2)}) collective-permute-start(bf16[40,2048]{1,0:T(8,128)(2,1)S(1)} %fusion.66), channel_id=1, source_target_pairs={{0,8},{4,12},{8,0},{12,4},{1,9},{5,13},{9,1},{13,5},{2,10},{6,14},... | collective-permute-start | bytes 491528 | tf_op jit(solution)/shard_map/ppermute | solution.py:36
  20.6 20.0 %copy-start = (s32[4]{0:T(128)S(1)}, s32[4]{0:T(128)}, u32[]{:S(2)}) copy-start(s32[4]{0:T(128)} %tick_ref) | copy-start | bytes 52
  28.3 5.4 %collective-permute-start.3 = (bf16[40,2048]{1,0:T(8,128)(2,1)S(1)}, bf16[40,2048]{1,0:T(8,128)(2,1)S(1)}, u32[]{:S(2)}, u32[]{:S(2)}) collective-permute-start(bf16[40,2048]{1,0:T(8,128)(2,1)S(1)} %get-tuple-element.64), channel_id=1, source_target_pairs={{0,2},{1,3},{2,0},{3,1},{4,6},{5,7},{6,4},{7,5},{8,10},{9,11},{10,... | collective-permute-start | bytes 491528 | tf_op jit(solution)/shard_map/ppermute | solution.py:36
  29.9 9.5 %collective-permute-start.6 = (bf16[40,2048]{1,0:T(8,128)(2,1)S(1)}, bf16[40,2048]{1,0:T(8,128)(2,1)S(1)}, u32[]{:S(2)}, u32[]{:S(2)}) collective-permute-start(bf16[40,2048]{1,0:T(8,128)(2,1)S(1)} %fusion.65), channel_id=1, source_target_pairs={{0,8},{4,12},{8,0},{12,4},{1,9},{5,13},{9,1},{13,5},{2,10},{6,14},... | collective-permute-start | bytes 491528 | tf_op jit(solution)/shard_map/ppermute | solution.py:36
  39.4 7.7 %collective-permute-start.7 = (bf16[40,2048]{1,0:T(8,128)(2,1)S(1)}, bf16[40,2048]{1,0:T(8,128)(2,1)S(1)}, u32[]{:S(2)}, u32[]{:S(2)}) collective-permute-start(bf16[40,2048]{1,0:T(8,128)(2,1)S(1)} %get-tuple-element.62), channel_id=1, source_target_pairs={{0,2},{1,3},{2,0},{3,1},{4,6},{5,7},{6,4},{7,5},{8,10},{9,11},{10,... | collective-permute-start | bytes 491528 | tf_op jit(solution)/shard_map/ppermute | solution.py:36
  39.9 7.2 %collective-permute-start.4 = (bf16[80,2048]{1,0:T(8,128)(2,1)S(1)}, bf16[80,2048]{1,0:T(8,128)(2,1)S(1)}, u32[]{:S(2)}, u32[]{:S(2)}) collective-permute-start(bf16[80,2048]{1,0:T(8,128)(2,1)S(1)} %pad_maximum_fusion.13), channel_id=1, source_target_pairs={{0,4},{1,0},{2,6},{3,2},{4,5},{5,1},{6,7},{7,3},{8,12},{9,8},{10,1... | collective-permute-start | bytes 983048 | tf_op jit(solution)/shard_map/ppermute | solution.py:113
  39.9 7.2 %collective-permute-start.5 = (bf16[80,2048]{1,0:T(8,128)(2,1)S(1)}, bf16[80,2048]{1,0:T(8,128)(2,1)S(1)}, u32[]{:S(2)}, u32[]{:S(2)}) collective-permute-start(bf16[80,2048]{1,0:T(8,128)(2,1)S(1)} %pad_maximum_fusion.13), channel_id=1, source_target_pairs={{1,4},{3,6},{4,1},{6,3},{9,12},{11,14},{12,9},{14,11},{17,20},{19,... | collective-permute-start | bytes 983048 | tf_op jit(solution)/shard_map/ppermute | solution.py:113
  47.4 7.4 %slice-start = ((s8[14680064]{0:T(1024)(128)(4,1)}), s8[4194304]{0:T(1024)(128)(4,1)S(1)}, s32[]{:S(2)}) async-start(s8[14680064]{0:T(1024)(128)(4,1)} %bitcast.129), calls=%async_computation | async-start | bytes 8388608
  47.4 7.3 %slice-start.1 = ((s8[14680064]{0:T(1024)(128)(4,1)}), s8[4194304]{0:T(1024)(128)(4,1)S(1)}, s32[]{:S(2)}) async-start(s8[14680064]{0:T(1024)(128)(4,1)} %bitcast.129), calls=%async_computation.1 | async-start | bytes 8388608
  48.8 5.9 %slice-start.2 = ((s8[14680064]{0:T(1024)(128)(4,1)}), s8[4194304]{0:T(1024)(128)(4,1)S(1)}, s32[]{:S(2)}) async-start(s8[14680064]{0:T(1024)(128)(4,1)} %bitcast.129), calls=%async_computation.2 | async-start | bytes 8388608
  48.8 5.9 %slice-start.3 = ((s8[14680064]{0:T(1024)(128)(4,1)}), s8[2097152]{0:T(1024)(128)(4,1)S(1)}, s32[]{:S(2)}) async-start(s8[14680064]{0:T(1024)(128)(4,1)} %bitcast.129), calls=%async_computation.3 | async-start | bytes 4194304
  48.8 7.3 %slice-start.4 = ((s8[14680064]{0:T(1024)(128)(4,1)}), s8[4194304]{0:T(1024)(128)(4,1)S(1)}, s32[]{:S(2)}) async-start(s8[14680064]{0:T(1024)(128)(4,1)} %bitcast.131), calls=%async_computation.4 | async-start | bytes 8388608
  48.8 7.3 %slice-start.5 = ((s8[14680064]{0:T(1024)(128)(4,1)}), s8[2097152]{0:T(1024)(128)(4,1)S(1)}, s32[]{:S(2)}) async-start(s8[14680064]{0:T(1024)(128)(4,1)} %bitcast.131), calls=%async_computation.5 | async-start | bytes 4194304
  50.3 5.8 %slice-start.6 = ((s8[14680064]{0:T(1024)(128)(4,1)}), s8[4194304]{0:T(1024)(128)(4,1)S(1)}, s32[]{:S(2)}) async-start(s8[14680064]{0:T(1024)(128)(4,1)} %bitcast.131), calls=%async_computation.6 | async-start | bytes 8388608
  50.4 3.4 %collective-permute-start.8 = (bf16[2,80,1792]{2,1,0:T(8,128)(2,1)S(1)}, bf16[2,80,1792]{2,1,0:T(8,128)(2,1)S(1)}, u32[]{:S(2)}, u32[]{:S(2)}) collective-permute-start(bf16[2,80,1792]{2,1,0:T(8,128)(2,1)S(1)} %pad_maximum_fusion.8), channel_id=1, source_target_pairs={{0,1},{1,0},{2,3},{3,2},{4,5},{5,4},{6,7},{7,6},{8,9},{9,8},{10,11... | collective-permute-start | bytes 1720328 | tf_op jit(solution)/shard_map/ppermute | solution.py:36
  54.7 2.4 %slice-start.7 = ((s8[14680064]{0:T(1024)(128)(4,1)}), s8[4194304]{0:T(1024)(128)(4,1)S(1)}, s32[]{:S(2)}) async-start(s8[14680064]{0:T(1024)(128)(4,1)} %bitcast.131), calls=%async_computation.7 | async-start | bytes 8388608
  58.7 6.0 %collective-permute-start.10 = (bf16[2,80,1792]{2,1,0:T(8,128)(2,1)S(1)}, bf16[2,80,1792]{2,1,0:T(8,128)(2,1)S(1)}, u32[]{:S(2)}, u32[]{:S(2)}) collective-permute-start(bf16[2,80,1792]{2,1,0:T(8,128)(2,1)S(1)} %pad_maximum_fusion.9), channel_id=1, source_target_pairs={{0,1},{1,0},{2,3},{3,2},{4,5},{5,4},{6,7},{7,6},{8,9},{9,8},{10,11... | collective-permute-start | bytes 1720328 | tf_op jit(solution)/shard_map/ppermute | solution.py:36
  60.4 8.0 %collective-permute-start.13 = (bf16[80,2048]{1,0:T(8,128)(2,1)S(1)}, bf16[80,2048]{1,0:T(8,128)(2,1)S(1)}, u32[]{:S(2)}, u32[]{:S(2)}) collective-permute-start(bf16[80,2048]{1,0:T(8,128)(2,1)S(1)} %pad_maximum_fusion.14), channel_id=1, source_target_pairs={{0,4},{1,0},{2,6},{3,2},{4,5},{5,1},{6,7},{7,3},{8,12},{9,8},{10,1... | collective-permute-start | bytes 983048 | tf_op jit(solution)/shard_map/ppermute | solution.py:113
  62.2 6.3 %collective-permute-start.14 = (bf16[80,2048]{1,0:T(8,128)(2,1)S(1)}, bf16[80,2048]{1,0:T(8,128)(2,1)S(1)}, u32[]{:S(2)}, u32[]{:S(2)}) collective-permute-start(bf16[80,2048]{1,0:T(8,128)(2,1)S(1)} %pad_maximum_fusion.14), channel_id=1, source_target_pairs={{1,4},{3,6},{4,1},{6,3},{9,12},{11,14},{12,9},{14,11},{17,20},{19,... | collective-permute-start | bytes 983048 | tf_op jit(solution)/shard_map/ppermute | solution.py:113
  63.0 13.0 %collective-permute-start.9 = (bf16[2,40,1792]{2,1,0:T(8,128)(2,1)}, bf16[2,40,1792]{2,1,0:T(8,128)(2,1)}, u32[]{:S(2)}, u32[]{:S(2)}) collective-permute-start(bf16[2,40,1792]{2,1,0:T(8,128)(2,1)} %pad_maximum_fusion.15), channel_id=1, source_target_pairs={{0,2},{1,3},{2,0},{3,1},{4,6},{5,7},{6,4},{7,5},{8,10},{9,11},{10,... | collective-permute-start | bytes 860168 | tf_op jit(solution)/shard_map/ppermute | solution.py:36
  71.9 2.5 %copy-start.4 = (bf16[2,40,1792]{2,1,0:T(8,128)(2,1)S(1)}, bf16[2,40,1792]{2,1,0:T(8,128)(2,1)}, u32[]{:S(2)}) copy-start(bf16[2,40,1792]{2,1,0:T(8,128)(2,1)} %pad_maximum_fusion.16) | copy-start | bytes 860164
  72.1 6.9 %collective-permute-start.15 = (bf16[2,80,2304]{2,1,0:T(8,128)(2,1)S(1)}, bf16[2,80,2304]{2,1,0:T(8,128)(2,1)S(1)}, u32[]{:S(2)}, u32[]{:S(2)}) collective-permute-start(bf16[2,80,2304]{2,1,0:T(8,128)(2,1)S(1)} %pad_maximum_fusion.5), channel_id=1, source_target_pairs={{0,1},{1,0},{2,3},{3,2},{4,5},{5,4},{6,7},{7,6},{8,9},{9,8},{10,11... | collective-permute-start | bytes 2211848 | tf_op jit(solution)/shard_map/ppermute | solution.py:36
  74.4 9.4 %collective-permute-start.12 = (bf16[2,40,1792]{2,1,0:T(8,128)(2,1)S(1)}, bf16[2,40,1792]{2,1,0:T(8,128)(2,1)S(1)}, u32[]{:S(2)}, u32[]{:S(2)}) collective-permute-start(bf16[2,40,1792]{2,1,0:T(8,128)(2,1)S(1)} %copy-done.4), channel_id=1, source_target_pairs={{0,2},{1,3},{2,0},{3,1},{4,6},{5,7},{6,4},{7,5},{8,10},{9,11},{10,... | collective-permute-start | bytes 860168 | tf_op jit(solution)/shard_map/ppermute | solution.py:36
  77.1 10.1 %collective-permute-start.11 = (bf16[40,1792]{1,0:T(8,128)(2,1)S(1)}, bf16[40,1792]{1,0:T(8,128)(2,1)S(1)}, u32[]{:S(2)}, u32[]{:S(2)}) collective-permute-start(bf16[40,1792]{1,0:T(8,128)(2,1)S(1)} %fusion.56), channel_id=1, source_target_pairs={{0,8},{4,12},{8,0},{12,4},{1,9},{5,13},{9,1},{13,5},{2,10},{6,14},... | collective-permute-start | bytes 430088 | tf_op jit(solution)/shard_map/ppermute | solution.py:36
  80.3 50.3 %slice-start.8 = ((s8[14680064]{0:T(1024)(128)(4,1)}), s8[4194304]{0:T(1024)(128)(4,1)S(1)}, s32[]{:S(2)}) async-start(s8[14680064]{0:T(1024)(128)(4,1)} %bitcast.136), calls=%async_computation.8 | async-start | bytes 8388608
  81.3 49.2 %slice-start.9 = ((s8[14680064]{0:T(1024)(128)(4,1)}), s8[4194304]{0:T(1024)(128)(4,1)S(1)}, s32[]{:S(2)}) async-start(s8[14680064]{0:T(1024)(128)(4,1)} %bitcast.136), calls=%async_computation.9 | async-start | bytes 8388608
  81.4 13.4 %collective-permute-start.21 = (bf16[2,80,1280]{2,1,0:T(8,128)(2,1)S(1)}, bf16[2,80,1280]{2,1,0:T(8,128)(2,1)S(1)}, u32[]{:S(2)}, u32[]{:S(2)}) collective-permute-start(bf16[2,80,1280]{2,1,0:T(8,128)(2,1)S(1)} %pad_maximum_fusion.10), channel_id=1, source_target_pairs={{0,1},{1,0},{2,3},{3,2},{4,5},{5,4},{6,7},{7,6},{8,9},{9,8},{10,11... | collective-permute-start | bytes 1228808 | tf_op jit(solution)/shard_map/ppermute | solution.py:36
  87.2 6.7 %collective-permute-start.16 = (bf16[40,1792]{1,0:T(8,128)(2,1)S(1)}, bf16[40,1792]{1,0:T(8,128)(2,1)S(1)}, u32[]{:S(2)}, u32[]{:S(2)}) collective-permute-start(bf16[40,1792]{1,0:T(8,128)(2,1)S(1)} %get-tuple-element.68), channel_id=1, source_target_pairs={{0,2},{1,3},{2,0},{3,1},{4,6},{5,7},{6,4},{7,5},{8,10},{9,11},{10,... | collective-permute-start | bytes 430088 | tf_op jit(solution)/shard_map/ppermute | solution.py:36
  88.0 13.6 %collective-permute-start.20 = (bf16[2,40,2304]{2,1,0:T(8,128)(2,1)S(1)}, bf16[2,40,2304]{2,1,0:T(8,128)(2,1)S(1)}, u32[]{:S(2)}, u32[]{:S(2)}) collective-permute-start(bf16[2,40,2304]{2,1,0:T(8,128)(2,1)S(1)} %pad_maximum_fusion.11), channel_id=1, source_target_pairs={{0,2},{1,3},{2,0},{3,1},{4,6},{5,7},{6,4},{7,5},{8,10},{9,11},{10,... | collective-permute-start | bytes 1105928 | tf_op jit(solution)/shard_map/ppermute | solution.py:36
  89.6 12.2 %collective-permute-start.19 = (bf16[40,1792]{1,0:T(8,128)(2,1)S(1)}, bf16[40,1792]{1,0:T(8,128)(2,1)S(1)}, u32[]{:S(2)}, u32[]{:S(2)}) collective-permute-start(bf16[40,1792]{1,0:T(8,128)(2,1)S(1)} %fusion.54), channel_id=1, source_target_pairs={{0,8},{4,12},{8,0},{12,4},{1,9},{5,13},{9,1},{13,5},{2,10},{6,14},... | collective-permute-start | bytes 430088 | tf_op jit(solution)/shard_map/ppermute | solution.py:36
  94.0 8.4 %collective-permute-start.17 = (bf16[80,1792]{1,0:T(8,128)(2,1)S(1)}, bf16[80,1792]{1,0:T(8,128)(2,1)S(1)}, u32[]{:S(2)}, u32[]{:S(2)}) collective-permute-start(bf16[80,1792]{1,0:T(8,128)(2,1)S(1)} %pad_maximum_fusion.17), channel_id=1, source_target_pairs={{0,4},{1,0},{2,6},{3,2},{4,5},{5,1},{6,7},{7,3},{8,12},{9,8},{10,1... | collective-permute-start | bytes 860168 | tf_op jit(solution)/shard_map/ppermute | solution.py:113
  94.1 8.4 %collective-permute-start.18 = (bf16[80,1792]{1,0:T(8,128)(2,1)S(1)}, bf16[80,1792]{1,0:T(8,128)(2,1)S(1)}, u32[]{:S(2)}, u32[]{:S(2)}) collective-permute-start(bf16[80,1792]{1,0:T(8,128)(2,1)S(1)} %pad_maximum_fusion.17), channel_id=1, source_target_pairs={{1,4},{3,6},{4,1},{6,3},{9,12},{11,14},{12,9},{14,11},{17,20},{19,... | collective-permute-start | bytes 860168 | tf_op jit(solution)/shard_map/ppermute | solution.py:113
  94.9 16.3 %collective-permute-start.28 = (bf16[2,40,1280]{2,1,0:T(8,128)(2,1)S(1)}, bf16[2,40,1280]{2,1,0:T(8,128)(2,1)S(1)}, u32[]{:S(2)}, u32[]{:S(2)}) collective-permute-start(bf16[2,40,1280]{2,1,0:T(8,128)(2,1)S(1)} %pad_maximum_fusion.19), channel_id=1, source_target_pairs={{0,2},{1,3},{2,0},{3,1},{4,6},{5,7},{6,4},{7,5},{8,10},{9,11},{10,... | collective-permute-start | bytes 614408 | tf_op jit(solution)/shard_map/ppermute | solution.py:36
  101.8 10.7 %collective-permute-start.27 = (bf16[40,2304]{1,0:T(8,128)(2,1)S(1)}, bf16[40,2304]{1,0:T(8,128)(2,1)S(1)}, u32[]{:S(2)}, u32[]{:S(2)}) collective-permute-start(bf16[40,2304]{1,0:T(8,128)(2,1)S(1)} %fusion.48), channel_id=1, source_target_pairs={{0,8},{4,12},{8,0},{12,4},{1,9},{5,13},{9,1},{13,5},{2,10},{6,14},... | collective-permute-start | bytes 552968 | tf_op jit(solution)/shard_map/ppermute | solution.py:36
  101.9 28.6 %slice-start.10 = ((s8[14680064]{0:T(1024)(128)(4,1)}), s8[4194304]{0:T(1024)(128)(4,1)S(1)}, s32[]{:S(2)}) async-start(s8[14680064]{0:T(1024)(128)(4,1)} %bitcast.136), calls=%async_computation.10 | async-start | bytes 8388608
  101.9 6.1 %collective-permute-start.22 = (bf16[40,1792]{1,0:T(8,128)(2,1)S(1)}, bf16[40,1792]{1,0:T(8,128)(2,1)S(1)}, u32[]{:S(2)}, u32[]{:S(2)}) collective-permute-start(bf16[40,1792]{1,0:T(8,128)(2,1)S(1)} %get-tuple-element.72), channel_id=1, source_target_pairs={{0,2},{1,3},{2,0},{3,1},{4,6},{5,7},{6,4},{7,5},{8,10},{9,11},{10,... | collective-permute-start | bytes 430088 | tf_op jit(solution)/shard_map/ppermute | solution.py:36
  108.0 16.8 %collective-permute-start.23 = (bf16[80,1792]{1,0:T(8,128)(2,1)S(1)}, bf16[80,1792]{1,0:T(8,128)(2,1)S(1)}, u32[]{:S(2)}, u32[]{:S(2)}) collective-permute-start(bf16[80,1792]{1,0:T(8,128)(2,1)S(1)} %pad_maximum_fusion.18), channel_id=1, source_target_pairs={{0,4},{1,0},{2,6},{3,2},{4,5},{5,1},{6,7},{7,3},{8,12},{9,8},{10,1... | collective-permute-start | bytes 860168 | tf_op jit(solution)/shard_map/ppermute | solution.py:113
  110.5 15.2 %collective-permute-start.24 = (bf16[80,1792]{1,0:T(8,128)(2,1)S(1)}, bf16[80,1792]{1,0:T(8,128)(2,1)S(1)}, u32[]{:S(2)}, u32[]{:S(2)}) collective-permute-start(bf16[80,1792]{1,0:T(8,128)(2,1)S(1)} %pad_maximum_fusion.18), channel_id=1, source_target_pairs={{1,4},{3,6},{4,1},{6,3},{9,12},{11,14},{12,9},{14,11},{17,20},{19,... | collective-permute-start | bytes 860168 | tf_op jit(solution)/shard_map/ppermute | solution.py:113
  111.3 7.3 %collective-permute-start.32 = (bf16[40,1280]{1,0:T(8,128)(2,1)S(1)}, bf16[40,1280]{1,0:T(8,128)(2,1)S(1)}, u32[]{:S(2)}, u32[]{:S(2)}) collective-permute-start(bf16[40,1280]{1,0:T(8,128)(2,1)S(1)} %fusion.62), channel_id=1, source_target_pairs={{0,8},{4,12},{8,0},{12,4},{1,9},{5,13},{9,1},{13,5},{2,10},{6,14},... | collective-permute-start | bytes 307208 | tf_op jit(solution)/shard_map/ppermute | solution.py:36
  112.5 7.5 %collective-permute-start.29 = (bf16[40,2304]{1,0:T(8,128)(2,1)S(1)}, bf16[40,2304]{1,0:T(8,128)(2,1)S(1)}, u32[]{:S(2)}, u32[]{:S(2)}) collective-permute-start(bf16[40,2304]{1,0:T(8,128)(2,1)S(1)} %get-tuple-element.52), channel_id=1, source_target_pairs={{0,2},{1,3},{2,0},{3,1},{4,6},{5,7},{6,4},{7,5},{8,10},{9,11},{10,... | collective-permute-start | bytes 552968 | tf_op jit(solution)/shard_map/ppermute | solution.py:36
  118.6 5.4 %collective-permute-start.33 = (bf16[40,1280]{1,0:T(8,128)(2,1)S(1)}, bf16[40,1280]{1,0:T(8,128)(2,1)S(1)}, u32[]{:S(2)}, u32[]{:S(2)}) collective-permute-start(bf16[40,1280]{1,0:T(8,128)(2,1)S(1)} %get-tuple-element.76), channel_id=1, source_target_pairs={{0,2},{1,3},{2,0},{3,1},{4,6},{5,7},{6,4},{7,5},{8,10},{9,11},{10,... | collective-permute-start | bytes 307208 | tf_op jit(solution)/shard_map/ppermute | solution.py:36
  120.0 14.7 %collective-permute-start.30 = (bf16[80,2304]{1,0:T(8,128)(2,1)S(1)}, bf16[80,2304]{1,0:T(8,128)(2,1)S(1)}, u32[]{:S(2)}, u32[]{:S(2)}) collective-permute-start(bf16[80,2304]{1,0:T(8,128)(2,1)S(1)} %pad_maximum_fusion.12), channel_id=1, source_target_pairs={{0,4},{1,0},{2,6},{3,2},{4,5},{5,1},{6,7},{7,3},{8,12},{9,8},{10,1... | collective-permute-start | bytes 1105928 | tf_op jit(solution)/shard_map/ppermute | solution.py:113
  121.1 13.6 %collective-permute-start.31 = (bf16[80,2304]{1,0:T(8,128)(2,1)S(1)}, bf16[80,2304]{1,0:T(8,128)(2,1)S(1)}, u32[]{:S(2)}, u32[]{:S(2)}) collective-permute-start(bf16[80,2304]{1,0:T(8,128)(2,1)S(1)} %pad_maximum_fusion.12), channel_id=1, source_target_pairs={{1,4},{3,6},{4,1},{6,3},{9,12},{11,14},{12,9},{14,11},{17,20},{19,... | collective-permute-start | bytes 1105928 | tf_op jit(solution)/shard_map/ppermute | solution.py:113
  124.0 9.5 %collective-permute-start.34 = (bf16[80,1280]{1,0:T(8,128)(2,1)S(1)}, bf16[80,1280]{1,0:T(8,128)(2,1)S(1)}, u32[]{:S(2)}, u32[]{:S(2)}) collective-permute-start(bf16[80,1280]{1,0:T(8,128)(2,1)S(1)} %pad_maximum_fusion.20), channel_id=1, source_target_pairs={{0,4},{1,0},{2,6},{3,2},{4,5},{5,1},{6,7},{7,3},{8,12},{9,8},{10,1... | collective-permute-start | bytes 614408 | tf_op jit(solution)/shard_map/ppermute | solution.py:113
  124.8 8.7 %collective-permute-start.35 = (bf16[80,1280]{1,0:T(8,128)(2,1)S(1)}, bf16[80,1280]{1,0:T(8,128)(2,1)S(1)}, u32[]{:S(2)}, u32[]{:S(2)}) collective-permute-start(bf16[80,1280]{1,0:T(8,128)(2,1)S(1)} %pad_maximum_fusion.20), channel_id=1, source_target_pairs={{1,4},{3,6},{4,1},{6,3},{9,12},{11,14},{12,9},{14,11},{17,20},{19,... | collective-permute-start | bytes 614408 | tf_op jit(solution)/shard_map/ppermute | solution.py:113
  125.9 4.7 %slice-start.11 = ((s8[14680064]{0:T(1024)(128)(4,1)}), s8[2097152]{0:T(1024)(128)(4,1)S(1)}, s32[]{:S(2)}) async-start(s8[14680064]{0:T(1024)(128)(4,1)} %bitcast.136), calls=%async_computation.11 | async-start | bytes 4194304
  132.1 6.4 %collective-permute-start.25 = (bf16[80,2048]{1,0:T(8,128)(2,1)S(1)}, bf16[80,2048]{1,0:T(8,128)(2,1)S(1)}, u32[]{:S(2)}, u32[]{:S(2)}) collective-permute-start(bf16[80,2048]{1,0:T(8,128)(2,1)S(1)} %slice.534), channel_id=1, source_target_pairs={{0,1},{1,0},{2,3},{3,2},{4,5},{5,4},{6,7},{7,6},{8,9},{9,8},{10,11... | collective-permute-start | bytes 983048 | tf_op jit(solution)/shard_map/ppermute | solution.py:36
  136.7 3.4 %collective-permute-start.36 = (bf16[80,2048]{1,0:T(8,128)(2,1)S(1)}, bf16[80,2048]{1,0:T(8,128)(2,1)S(1)}, u32[]{:S(2)}, u32[]{:S(2)}) collective-permute-start(bf16[80,2048]{1,0:T(8,128)(2,1)S(1)} %slice.533), channel_id=1, source_target_pairs={{0,1},{1,0},{2,3},{3,2},{4,5},{5,4},{6,7},{7,6},{8,9},{9,8},{10,11... | collective-permute-start | bytes 983048 | tf_op jit(solution)/shard_map/ppermute | solution.py:36
  138.5 10.6 %collective-permute-start.26 = (bf16[80,2048]{1,0:T(8,128)(2,1)S(1)}, bf16[80,2048]{1,0:T(8,128)(2,1)S(1)}, u32[]{:S(2)}, u32[]{:S(2)}) collective-permute-start(bf16[80,2048]{1,0:T(8,128)(2,1)S(1)} %fusion.40), channel_id=1, source_target_pairs={{0,2},{1,3},{2,0},{3,1},{4,6},{5,7},{6,4},{7,5},{8,10},{9,11},{10,... | collective-permute-start | bytes 983048 | tf_op jit(solution)/shard_map/ppermute | solution.py:36
  140.2 15.1 %collective-permute-start.37 = (bf16[80,2048]{1,0:T(8,128)(2,1)S(1)}, bf16[80,2048]{1,0:T(8,128)(2,1)S(1)}, u32[]{:S(2)}, u32[]{:S(2)}) collective-permute-start(bf16[80,2048]{1,0:T(8,128)(2,1)S(1)} %fusion.41), channel_id=1, source_target_pairs={{0,2},{1,3},{2,0},{3,1},{4,6},{5,7},{6,4},{7,5},{8,10},{9,11},{10,... | collective-permute-start | bytes 983048 | tf_op jit(solution)/shard_map/ppermute | solution.py:36
  149.3 6.1 %copy-start.3 = (bf16[160,2048]{1,0:T(8,128)(2,1)S(1)}, bf16[160,2048]{1,0:T(8,128)(2,1)}, u32[]{:S(2)}) copy-start(bf16[160,2048]{1,0:T(8,128)(2,1)} %copy-done.2) | copy-start | bytes 1966084
  155.4 3.1 %copy-start.1 = (bf16[160,2048]{1,0:T(8,128)(2,1)S(1)}, bf16[160,2048]{1,0:T(8,128)(2,1)}, u32[]{:S(2)}) copy-start(bf16[160,2048]{1,0:T(8,128)(2,1)} %param.5) | copy-start | bytes 1966084
  156.3 2.2 %collective-permute-start.38 = (bf16[160,2048]{1,0:T(8,128)(2,1)S(1)}, bf16[160,2048]{1,0:T(8,128)(2,1)S(1)}, u32[]{:S(2)}, u32[]{:S(2)}) collective-permute-start(bf16[160,2048]{1,0:T(8,128)(2,1)S(1)} %select_convert_fusion), channel_id=1, source_target_pairs={{0,1},{1,0},{2,3},{3,2},{4,5},{5,4},{6,7},{7,6},{8,9},{9,8},{10,11... | collective-permute-start | bytes 1966088 | tf_op jit(solution)/shard_map/ppermute | solution.py:36

commit v9 on v8

--- a/solution.py
+++ b/solution.py
@@ -12,18 +12,23 @@
 EDGES = {
     "w.pull": ["t0.add"],
     "t0.halves": ["w.pull"],
+    "t1.pick": ["t0.add"],
     "t1.add": ["t0.halves"],
     "t1.halves": ["t0.columns"],
-    "c00.dots": ["t1.columns"],
-    "c01.dots": ["c00.sum"],
-    "t1.cores": ["c01.sum"],
+    "c01.dots": ["c00.dots"],
+    "c00.sum": ["c01.dots"],
+    "t1.columns": ["c01.sum"],
     "c00.hidden": ["c01.sum"],
-    "c01.hidden": ["c10.sum"],
-    "c11.dots": ["c10.sum"],
-    "c00.halves": ["c01.hidden"],
+    "t1.cores": ["c00.hidden"],
+    "c01.hidden": ["c10.dots"],
+    "c10.sum": ["c01.hidden"],
+    "c11.dots": ["c00.halves"],
+    "c00.halves": ["c10.sum"],
     "c10.hidden": ["c11.sum"],
-    "c01.halves": ["c10.hidden"],
+    "c01.halves": ["c11.sum"],
     "c10.halves": ["c11.hidden"],
+    "c10.cores": ["b0.all"],
+    "c11.cores": ["b0.total"],
 }
 
 
@@ -36,7 +41,7 @@
     return lax.ppermute(value, axis, [(i, i ^ bit) for i in range(count)])
 
 
-def pull_kernel(first, end, tick_ref, gate_ref, up_ref, gate_here, up_here, done_ref, sems):
+def pull_kernel(first, end, tick_ref, gate_ref, up_ref, gate_here, up_here, sems):
     del tick_ref
     columns = pl.ds(first, end - first)
     copies = [
@@ -47,7 +52,6 @@
         copy.start()
     for copy in copies:
         copy.wait()
-    done_ref[...] = jnp.zeros_like(done_ref)
 
 
 def pull(gate_weight, up_weight, first, end, tick):
@@ -57,8 +61,8 @@
     return pl.pallas_call(
         functools.partial(pull_kernel, first, end),
         in_specs=[pl.BlockSpec(memory_space=pltpu.SMEM), far, far],
-        out_specs=[near, near, near],
-        out_shape=[here, here, jax.ShapeDtypeStruct((8, 128), jnp.float32)],
+        out_specs=[near, near],
+        out_shape=[here, here],
         scratch_shapes=[pltpu.SemaphoreType.DMA((2,))],
         compiler_params=pltpu.CompilerParams(
             vmem_limit_bytes=4 * gate_weight.shape[0] * (end - first) + 2**20
@@ -161,30 +165,27 @@
         yield
         return issued(name + ".cores", finish(ordered(name + ".cores", pair)))
 
-    picked = {}
-
-    def pick_steps():
-        own = jnp.concatenate(mine)[:, None] == places[0][None]
-        sib = jnp.concatenate(mine)[:, None] == places[1][None]
-        rows = dot(own.astype(jnp.bfloat16), tokens) + dot(sib.astype(jnp.bfloat16), sibling)
-        rows = rows.astype(jnp.bfloat16).reshape(HALVES, 2, piece, width)
-        picked["got"] = swap_x(rows[:, 1])
-        picked["rows"] = rows[:, 0]
-        return None
-        yield
+    def pick_steps(name, h):
+        own = mine[h][:, None] == places[0][None]
+        sib = mine[h][:, None] == places[1][None]
+        rows = dot(own.astype(jnp.bfloat16), tokens)
+        rows = rows + dot(ordered(name + ".pick", sib).astype(jnp.bfloat16), sibling)
+        rows = issued(name + ".pick", rows.astype(jnp.bfloat16))
+        got = swap_x(rows[piece:])
+        yield
+        return issued(name + ".add", ordered(name + ".add", rows[:piece]) + got)
 
     pulled = []
 
     def pull_steps():
         tick = ordered("w.pull", lengths)
-        *both, done = pull(gate_weight, up_weight, *spans[0][0], tick)
-        pulled.extend(both)
-        issued("w.pull", done)
+        pulled.extend(pull(gate_weight, up_weight, *spans[0][0], tick))
+        issued("w.pull", pulled[0])
         return None
         yield
 
     def half_steps(name, h):
-        own = issued(name + ".add", ordered(name + ".add", picked["rows"][h]) + picked["got"][h])
+        own = yield from pick_steps(name, h)
         return (yield from spread_steps(name, own))
 
     def chunk_steps(name, h, i):
@@ -221,7 +222,7 @@
         got = ordered(name + ".all", got)
         return issued(name + ".all", total + jnp.concatenate([got[piece:], got[:piece]], axis=0))
 
-    chains, results = {"p": pick_steps(), "w": pull_steps()}, {}
+    chains, results = {"w": pull_steps()}, {}
     for h in range(HALVES):
         chains["t" + str(h)] = half_steps("t" + str(h), h)
         for i in range(len(spans[h])):
@@ -239,7 +240,6 @@
             advance(name)
         return results[name]
 
-    result("p")
     result("w")
     for h in range(HALVES):
         result("b" + str(h))

time: 161 us -> 174 us (1.081)
  local copies, waits for them, and re-layouts: 2.14 us -> 11.5 us
  starting transfers between devices: 41.5 us -> 49.4 us
  waiting for transfers between devices: 75.6 us -> 69.1 us
  matrix products: 24.4 us -> 29.5 us
  other arithmetic: 9.33 us -> 7.04 us
    ppermute x27 -> x28, waiting for transfers between devices: 72.7 us -> 52.8 us  [flip(): return lax.ppermute(value, axis, [(i, i ^ bit) for i in range(count)])]
    ppermute x12, waiting for transfers between devices: 2.92 us -> 16.3 us  [move(): return lax.ppermute(value, ('row', 'col'), pairs)]
    ppermute x12, starting transfers between devices: 10.7 us -> 21.7 us  [move(): return lax.ppermute(value, ('row', 'col'), pairs)]
    unnamed x34 -> x38, local copies, waits for them, and re-layouts: 1.59 us -> 9.8 us
    dot_general x14 -> x16, matrix products: 21.6 us -> 26.7 us  [dot(): return jnp.dot(a, b, preferred_element_type=jnp.float32)]
    ppermute x27 -> x28, starting transfers between devices: 30.8 us -> 27.7 us  [flip(): return lax.ppermute(value, axis, [(i, i ^ bit) for i in range(count)])]
  transfers between devices with their start and end apart: 39 -> 40, of which waited for: 17 -> 17; matrix products, arithmetic and copies ran while one was open for 15% -> 18% of each run, Pallas kernels for 4% -> 4%
where the time goes in v9:
time: 174 us; the launch traced here: 173 us
  waiting for transfers between devices  69.1 us (40%)
  starting transfers between devices  49.4 us (28%)
  matrix products  29.5 us (17%)
  local copies, waits for them, and re-layouts  11.5 us (7%)
  other arithmetic  7.04 us (4%)
  Pallas kernels  6.08 us (3%)
    ppermute x28, waiting for transfers between devices, flip(): return lax.ppermute(value, axis, [(i, i ^ bit) for i in range(count)])  52.8 us
    ppermute x28, starting transfers between devices, flip(): return lax.ppermute(value, axis, [(i, i ^ bit) for i in range(count)])  27.7 us
    dot_general x16, matrix products, dot(): return jnp.dot(a, b, preferred_element_type=jnp.float32)  26.7 us
    ppermute x12, starting transfers between devices, move(): return lax.ppermute(value, ('row', 'col'), pairs)  21.7 us
    ppermute x12, waiting for transfers between devices, move(): return lax.ppermute(value, ('row', 'col'), pairs)  16.3 us
    unnamed x38, local copies, waits for them, and re-layouts  9.8 us
    pallas_call x1, Pallas kernels, pull(): pl.pallas_call(functools.partial(pull_kernel, first, end), in_specs=[pl.B...  6.08 us
  transfers between devices with their start and end apart: 40, of which 17 were waited for; matrix products, arithmetic and copies ran while one was open for 18% of the time, Pallas kernels for 4%

profile of v9, /device:TPU:0, one launch (start us, length us, event | category | flops | bytes accessed | tf_op | source)
XLA Modules:
  0.0 173.4 jit_solution(17462503255333701475)
XLA Ops:
  0.5 1.4 fusion.88
  1.9 2.5 %compare_select_fusion.1 = (s32[160]{0:T(256)S(1)}, s32[160]{0:T(256)S(1)}) fusion(s32[]{:T(128)} %get-tuple-element.52, s32[]{:T(128)} %get-tuple-element.49, s32[]{:T(128)} %get-tuple-element.50, s32[]{:T(128)} %get-tuple-element.51), kind=kLoop, calls=%fused_computation.176 | loop fusion | flops 960 | bytes 1296 | tf_op jit(solution)/shard_map/jit(_where)/select_n | solution.py:101
  4.4 1.4 fusion.75
  6.5 2.6 %collective-permute-start.1 = (bf16[40,2048]{1,0:T(8,128)(2,1)S(1)}, bf16[40,2048]{1,0:T(8,128)(2,1)S(1)}, u32[]{:S(2)}, u32[]{:S(2)}) collective-permute-start(bf16[40,2048]{1,0:T(8,128)(2,1)S(1)} %slice.299), channel_id=1, source_target_pairs={{0,2},{1,3},{2,0},{3,1},{4,6},{5,7},{6,4},{7,5},{8,10},{9,11},{10,... | collective-permute-start | bytes 491528 | tf_op jit(solution)/shard_map/ppermute | solution.py:41
  9.2 4.7 %collective-permute-done.1 = bf16[40,2048]{1,0:T(8,128)(2,1)S(1)} collective-permute-done((bf16[40,2048]{1,0:T(8,128)(2,1)S(1)}, bf16[40,2048]{1,0:T(8,128)(2,1)S(1)}, u32[]{:S(2)}, u32[]{:S(2)}) %collective-permute-start.1) | collective-permute-done | bytes 163872 | tf_op jit(solution)/shard_map/ppermute | solution.py:41
  13.9 2.9 %collective-permute-start.2 = (bf16[40,2048]{1,0:T(8,128)(2,1)S(1)}, bf16[40,2048]{1,0:T(8,128)(2,1)S(1)}, u32[]{:S(2)}, u32[]{:S(2)}) collective-permute-start(bf16[40,2048]{1,0:T(8,128)(2,1)S(1)} %slice_add_fusion.18), channel_id=1, source_target_pairs={{0,8},{4,12},{8,0},{12,4},{1,9},{5,13},{9,1},{13,5},{2,10},{6,14},... | collective-permute-start | bytes 491528 | tf_op jit(solution)/shard_map/ppermute | solution.py:41
  17.1 1.6 collective-permute-start.10
  18.7 6.1 %shard_map.55 = (bf16[2048,1792]{1,0:T(8,128)(2,1)S(1)}, bf16[2048,1792]{1,0:T(8,128)(2,1)S(1)}) custom-call(s32[4]{0:T(128)S(1)} %copy-done, bf16[2048,3584]{1,0:T(8,128)(2,1)} %gate_ref.1, bf16[2048,3584]{1,0:T(8,128)(2,1)} %up_ref.1), custom_call_target="tpu_custom_call" | custom-call | tf_op jit(solution)/shard_map/pallas_call | solution.py:61
  24.8 2.9 %copy-done.1 = bf16[2048,1792]{1,0:T(8,128)(2,1)} copy-done((bf16[2048,1792]{1,0:T(8,128)(2,1)}, bf16[2048,1792]{1,0:T(8,128)(2,1)S(1)}, u32[]{:S(2)}) %copy-start.1) | copy-done | bytes 7340056
  27.7 3.0 %copy-done.2 = bf16[2048,1792]{1,0:T(8,128)(2,1)} copy-done((bf16[2048,1792]{1,0:T(8,128)(2,1)}, bf16[2048,1792]{1,0:T(8,128)(2,1)S(1)}, u32[]{:S(2)}) %copy-start.2) | copy-done | bytes 7340056
  31.5 4.6 %collective-permute-done.3 = bf16[40,2048]{1,0:T(8,128)(2,1)S(1)} collective-permute-done((bf16[40,2048]{1,0:T(8,128)(2,1)S(1)}, bf16[40,2048]{1,0:T(8,128)(2,1)S(1)}, u32[]{:S(2)}, u32[]{:S(2)}) %collective-permute-start.3) | collective-permute-done | bytes 163872 | tf_op jit(solution)/shard_map/ppermute | solution.py:41
  36.1 0.8 collective-permute-start.5
  36.9 3.0 %collective-permute-start.4 = (bf16[80,2048]{1,0:T(8,128)(2,1)S(1)}, bf16[80,2048]{1,0:T(8,128)(2,1)S(1)}, u32[]{:S(2)}, u32[]{:S(2)}) collective-permute-start(bf16[80,2048]{1,0:T(8,128)(2,1)S(1)} %pad_maximum_fusion.13), channel_id=1, source_target_pairs={{0,4},{1,0},{2,6},{3,2},{4,5},{5,1},{6,7},{7,3},{8,12},{9,8},{10,1... | collective-permute-start | bytes 983048 | tf_op jit(solution)/shard_map/ppermute | solution.py:117
  40.8 1.6 collective-permute-start.12
  42.4 5.0 %collective-permute-done.4 = bf16[80,2048]{1,0:T(8,128)(2,1)S(1)} collective-permute-done((bf16[80,2048]{1,0:T(8,128)(2,1)S(1)}, bf16[80,2048]{1,0:T(8,128)(2,1)S(1)}, u32[]{:S(2)}, u32[]{:S(2)}) %collective-permute-start.4) | collective-permute-done | bytes 327712 | tf_op jit(solution)/shard_map/ppermute | solution.py:117
  47.6 4.6 %fusion.97 = f32[160,1792]{1,0:T(8,128)S(1)} fusion(bf16[2048,1792]{1,0:T(8,128)(2,1)} %copy-done.2, bf16[80,2048]{1,0:T(8,128)(2,1)S(1)} %get-tuple-element.78, bf16[80,2048]{1,0:T(8,128)(2,1)S(1)} %get-tuple-element.77), kind=kOutput, calls=%fused_computation.197 | convolution fusion | flops 1175715840 | bytes 9142272 | tf_op jit(solution)/shard_map/dot_general | solution.py:36
  52.7 1.4 fusion.96
  54.3 0.9 collective-permute-start.6
  55.2 2.4 %slice-done.4 = s8[4194304]{0:T(1024)(128)(4,1)S(1)} async-done(((s8[14680064]{0:T(1024)(128)(4,1)}), s8[4194304]{0:T(1024)(128)(4,1)S(1)}, s32[]{:S(2)}) %slice-start.4) | async-done | bytes 4194328
  58.2 1.4 fusion.10
  60.0 1.4 fusion.12
  61.6 0.9 collective-permute-start.8
  62.7 0.9 collective-permute-start.7
  64.4 0.9 collective-permute-start.16
  66.0 3.2 %collective-permute-start.13 = (bf16[80,2048]{1,0:T(8,128)(2,1)S(1)}, bf16[80,2048]{1,0:T(8,128)(2,1)S(1)}, u32[]{:S(2)}, u32[]{:S(2)}) collective-permute-start(bf16[80,2048]{1,0:T(8,128)(2,1)S(1)} %pad_maximum_fusion.14), channel_id=1, source_target_pairs={{0,4},{1,0},{2,6},{3,2},{4,5},{5,1},{6,7},{7,3},{8,12},{9,8},{10,1... | collective-permute-start | bytes 983048 | tf_op jit(solution)/shard_map/ppermute | solution.py:117
  69.2 3.3 %collective-permute-done.7 = bf16[2,40,1792]{2,1,0:T(8,128)(2,1)S(1)} collective-permute-done((bf16[2,40,1792]{2,1,0:T(8,128)(2,1)S(1)}, bf16[2,40,1792]{2,1,0:T(8,128)(2,1)S(1)}, u32[]{:S(2)}, u32[]{:S(2)}) %collective-permute-start.7) | collective-permute-done | bytes 286752 | tf_op jit(solution)/shard_map/ppermute | solution.py:41
  72.6 3.8 %collective-permute-done.13 = bf16[80,2048]{1,0:T(8,128)(2,1)S(1)} collective-permute-done((bf16[80,2048]{1,0:T(8,128)(2,1)S(1)}, bf16[80,2048]{1,0:T(8,128)(2,1)S(1)}, u32[]{:S(2)}, u32[]{:S(2)}) %collective-permute-start.13) | collective-permute-done | bytes 327712 | tf_op jit(solution)/shard_map/ppermute | solution.py:117
  76.5 1.7 fusion.4
  78.2 2.9 %fusion.2 = f32[160,2304]{1,0:T(8,128)} fusion(bf16[2048,3584]{1,0:T(8,128)(2,1)S(1)} %bitcast.106, bf16[80,2048]{1,0:T(8,128)(2,1)S(1)} %get-tuple-element.74, bf16[80,2048]{1,0:T(8,128)(2,1)S(1)} %get-tuple-element.73), kind=kOutput, calls=%fused_computation.2 | convolution fusion | flops 1511260160 | bytes 11567104 | tf_op jit(solution)/shard_map/dot_general | solution.py:36
  81.2 1.2 fusion.46
  82.4 1.2 collective-permute-start.15
  84.4 1.1 collective-permute-done.15
  85.7 7.6 %collective-permute-done.9 = bf16[40,1792]{1,0:T(8,128)(2,1)S(1)} collective-permute-done((bf16[40,1792]{1,0:T(8,128)(2,1)S(1)}, bf16[40,1792]{1,0:T(8,128)(2,1)S(1)}, u32[]{:S(2)}, u32[]{:S(2)}) %collective-permute-start.9) | collective-permute-done | bytes 143392 | tf_op jit(solution)/shard_map/ppermute | solution.py:41
  93.4 1.0 fusion.16
  94.5 1.0 fusion.18
  95.7 1.2 collective-permute-start.17
  97.0 0.8 collective-permute-start.27
  97.8 4.5 %collective-permute-done.17 = bf16[40,1792]{1,0:T(8,128)(2,1)S(1)} collective-permute-done((bf16[40,1792]{1,0:T(8,128)(2,1)S(1)}, bf16[40,1792]{1,0:T(8,128)(2,1)S(1)}, u32[]{:S(2)}, u32[]{:S(2)}) %collective-permute-start.17) | collective-permute-done | bytes 143392 | tf_op jit(solution)/shard_map/ppermute | solution.py:41
  103.0 2.1 %collective-permute-start.18 = (bf16[80,1792]{1,0:T(8,128)(2,1)S(1)}, bf16[80,1792]{1,0:T(8,128)(2,1)S(1)}, u32[]{:S(2)}, u32[]{:S(2)}) collective-permute-start(bf16[80,1792]{1,0:T(8,128)(2,1)S(1)} %pad_maximum_fusion.17), channel_id=1, source_target_pairs={{0,4},{1,0},{2,6},{3,2},{4,5},{5,1},{6,7},{7,3},{8,12},{9,8},{10,1... | collective-permute-start | bytes 860168 | tf_op jit(solution)/shard_map/ppermute | solution.py:117
  105.3 1.2 collective-permute-start.29
  106.6 3.6 %collective-permute-done.27 = bf16[2,40,2304]{2,1,0:T(8,128)(2,1)S(1)} collective-permute-done((bf16[2,40,2304]{2,1,0:T(8,128)(2,1)S(1)}, bf16[2,40,2304]{2,1,0:T(8,128)(2,1)S(1)}, u32[]{:S(2)}, u32[]{:S(2)}) %collective-permute-start.27) | collective-permute-done | bytes 368672 | tf_op jit(solution)/shard_map/ppermute | solution.py:41
  110.4 1.2 collective-permute-start.22
  112.3 5.0 %collective-permute-done.22 = bf16[40,1792]{1,0:T(8,128)(2,1)S(1)} collective-permute-done((bf16[40,1792]{1,0:T(8,128)(2,1)S(1)}, bf16[40,1792]{1,0:T(8,128)(2,1)S(1)}, u32[]{:S(2)}, u32[]{:S(2)}) %collective-permute-start.22) | collective-permute-done | bytes 143392 | tf_op jit(solution)/shard_map/ppermute | solution.py:41
  118.0 2.6 %collective-permute-start.23 = (bf16[80,1792]{1,0:T(8,128)(2,1)S(1)}, bf16[80,1792]{1,0:T(8,128)(2,1)S(1)}, u32[]{:S(2)}, u32[]{:S(2)}) collective-permute-start(bf16[80,1792]{1,0:T(8,128)(2,1)S(1)} %pad_maximum_fusion.18), channel_id=1, source_target_pairs={{0,4},{1,0},{2,6},{3,2},{4,5},{5,1},{6,7},{7,3},{8,12},{9,8},{10,1... | collective-permute-start | bytes 860168 | tf_op jit(solution)/shard_map/ppermute | solution.py:117
  120.6 0.8 collective-permute-start.33
  121.5 1.0 collective-permute-start.30
  122.5 5.0 %collective-permute-done.33 = bf16[40,1280]{1,0:T(8,128)(2,1)S(1)} collective-permute-done((bf16[40,1280]{1,0:T(8,128)(2,1)S(1)}, bf16[40,1280]{1,0:T(8,128)(2,1)S(1)}, u32[]{:S(2)}, u32[]{:S(2)}) %collective-permute-start.33) | collective-permute-done | bytes 102432 | tf_op jit(solution)/shard_map/ppermute | solution.py:41
  127.6 1.2 collective-permute-start.34
  129.0 4.6 %fusion.6 = f32[160,2048]{1,0:T(8,128)S(1)} fusion(bf16[3584,2048]{1,0:T(8,128)(2,1)} %param.9, bf16[80,1792]{1,0:T(8,128)(2,1)S(1)} %get-tuple-element.88, bf16[80,1792]{1,0:T(8,128)(2,1)S(1)} %get-tuple-element.87), kind=kOutput, calls=%fused_computation.6 | convolution fusion | flops 1175552000 | bytes 9224192 | tf_op jit(solution)/shard_map/dot_general | solution.py:36
  133.7 1.5 fusion.21
  135.2 0.9 collective-permute-start.25
  136.8 3.3 %collective-permute-start.31 = (bf16[80,2304]{1,0:T(8,128)(2,1)S(1)}, bf16[80,2304]{1,0:T(8,128)(2,1)S(1)}, u32[]{:S(2)}, u32[]{:S(2)}) collective-permute-start(bf16[80,2304]{1,0:T(8,128)(2,1)S(1)} %pad_maximum_fusion.12), channel_id=1, source_target_pairs={{0,4},{1,0},{2,6},{3,2},{4,5},{5,1},{6,7},{7,3},{8,12},{9,8},{10,1... | collective-permute-start | bytes 1105928 | tf_op jit(solution)/shard_map/ppermute | solution.py:117
  140.8 3.3 %collective-permute-start.35 = (bf16[80,1280]{1,0:T(8,128)(2,1)S(1)}, bf16[80,1280]{1,0:T(8,128)(2,1)S(1)}, u32[]{:S(2)}, u32[]{:S(2)}) collective-permute-start(bf16[80,1280]{1,0:T(8,128)(2,1)S(1)} %pad_maximum_fusion.20), channel_id=1, source_target_pairs={{0,4},{1,0},{2,6},{3,2},{4,5},{5,1},{6,7},{7,3},{8,12},{9,8},{10,1... | collective-permute-start | bytes 614408 | tf_op jit(solution)/shard_map/ppermute | solution.py:117
  144.2 1.1 collective-permute-start.26
  145.3 7.5 %collective-permute-done.35 = bf16[80,1280]{1,0:T(8,128)(2,1)S(1)} collective-permute-done((bf16[80,1280]{1,0:T(8,128)(2,1)S(1)}, bf16[80,1280]{1,0:T(8,128)(2,1)S(1)}, u32[]{:S(2)}, u32[]{:S(2)}) %collective-permute-start.35) | collective-permute-done | bytes 204832 | tf_op jit(solution)/shard_map/ppermute | solution.py:117
  152.8 1.0 fusion.14
  154.1 1.8 %fusion.24 = f32[160,2048]{1,0:T(8,128)S(1)} fusion(f32[160,2048]{1,0:T(8,128)S(1)} %fusion.14, bf16[3584,2048]{1,0:T(8,128)(2,1)S(1)} %bitcast.110, bf16[80,2304]{1,0:T(8,128)(2,1)S(1)} %get-tuple-element.66, bf16[80,2304]{1,0:T(8,128)(2,1)S(1)} %get-tuple-element.65), kind=kOutput, calls=%fused_computation.23 | convolution fusion | flops 1511751680 | bytes 12795904 | tf_op jit(solution)/shard_map/dot_general | solution.py:36
  156.0 0.9 collective-permute-start.37
  156.9 1.3 collective-permute-done.37
  158.3 1.2 collective-permute-start.38
  159.7 8.6 %collective-permute-done.38 = bf16[80,2048]{1,0:T(8,128)(2,1)S(1)} collective-permute-done((bf16[80,2048]{1,0:T(8,128)(2,1)S(1)}, bf16[80,2048]{1,0:T(8,128)(2,1)S(1)}, u32[]{:S(2)}, u32[]{:S(2)}) %collective-permute-start.38) | collective-permute-done | bytes 327712 | tf_op jit(solution)/shard_map/ppermute | solution.py:41
  168.5 0.9 select_convert_fusion
  169.5 2.1 %collective-permute-done.39 = bf16[160,2048]{1,0:T(8,128)(2,1)S(1)} collective-permute-done((bf16[160,2048]{1,0:T(8,128)(2,1)S(1)}, bf16[160,2048]{1,0:T(8,128)(2,1)S(1)}, u32[]{:S(2)}, u32[]{:S(2)}) %collective-permute-start.39) | collective-permute-done | bytes 655392 | tf_op jit(solution)/shard_map/ppermute | solution.py:41
  171.5 1.8 %fusion.30 = bf16[160,2048]{1,0:T(8,128)(2,1)} fusion(bf16[160,2048]{1,0:T(8,128)(2,1)S(1)} %collective-permute-done.39, bf16[160,2048]{1,0:T(8,128)(2,1)S(1)} %copy-done.3, f32[80,2048]{1,0:T(8,128)S(1)} %convert_add_fusion, f32[80,2048]{1,0:T(8,128)S(1)} %convert_add_fusion.1, pred[160]{0:T(512)(128)(4,1)S(1)} %get-tuple-element.47, ...), kind=kOutput, calls=%fused_computation.31 | convolution fusion | flops 631137280 | bytes 3278240 | tf_op jit(solution)/shard_map/dot_general | solution.py:251
  (148 shorter events, 13.0 us)
Async XLA Ops:
  0.0 5.8 %copy-start.3 = (bf16[160,2048]{1,0:T(8,128)(2,1)S(1)}, bf16[160,2048]{1,0:T(8,128)(2,1)}, u32[]{:S(2)}) copy-start(bf16[160,2048]{1,0:T(8,128)(2,1)} %param.5) | copy-start | bytes 1966084
  0.0 6.1 %collective-permute-start = (bf16[160,2048]{1,0:T(8,128)(2,1)}, bf16[160,2048]{1,0:T(8,128)(2,1)S(1)}, u32[]{:S(2)}, u32[]{:S(2)}) collective-permute-start(bf16[160,2048]{1,0:T(8,128)(2,1)} %param.5), channel_id=1, source_target_pairs={{0,1},{1,0},{2,3},{3,2},{4,5},{5,4},{6,7},{7,6},{8,9},{9,8},{10,11... | collective-permute-start | bytes 1966088 | tf_op jit(solution)/shard_map/ppermute | solution.py:41
  6.5 7.4 %collective-permute-start.1 = (bf16[40,2048]{1,0:T(8,128)(2,1)S(1)}, bf16[40,2048]{1,0:T(8,128)(2,1)S(1)}, u32[]{:S(2)}, u32[]{:S(2)}) collective-permute-start(bf16[40,2048]{1,0:T(8,128)(2,1)S(1)} %slice.299), channel_id=1, source_target_pairs={{0,2},{1,3},{2,0},{3,1},{4,6},{5,7},{6,4},{7,5},{8,10},{9,11},{10,... | collective-permute-start | bytes 491528 | tf_op jit(solution)/shard_map/ppermute | solution.py:41
  9.2 9.5 %copy-start = (s32[4]{0:T(128)S(1)}, s32[4]{0:T(128)}, u32[]{:S(2)}) copy-start(s32[4]{0:T(128)} %tick_ref) | copy-start | bytes 52
  13.9 16.8 %collective-permute-start.2 = (bf16[40,2048]{1,0:T(8,128)(2,1)S(1)}, bf16[40,2048]{1,0:T(8,128)(2,1)S(1)}, u32[]{:S(2)}, u32[]{:S(2)}) collective-permute-start(bf16[40,2048]{1,0:T(8,128)(2,1)S(1)} %slice_add_fusion.18), channel_id=1, source_target_pairs={{0,8},{4,12},{8,0},{12,4},{1,9},{5,13},{9,1},{13,5},{2,10},{6,14},... | collective-permute-start | bytes 491528 | tf_op jit(solution)/shard_map/ppermute | solution.py:41
  17.1 14.2 %collective-permute-start.10 = (bf16[40,2048]{1,0:T(8,128)(2,1)S(1)}, bf16[40,2048]{1,0:T(8,128)(2,1)S(1)}, u32[]{:S(2)}, u32[]{:S(2)}) collective-permute-start(bf16[40,2048]{1,0:T(8,128)(2,1)S(1)} %get-tuple-element.81), channel_id=1, source_target_pairs={{0,2},{1,3},{2,0},{3,1},{4,6},{5,7},{6,4},{7,5},{8,10},{9,11},{10,... | collective-permute-start | bytes 491528 | tf_op jit(solution)/shard_map/ppermute | solution.py:41
  24.7 2.9 %copy-start.1 = (bf16[2048,1792]{1,0:T(8,128)(2,1)}, bf16[2048,1792]{1,0:T(8,128)(2,1)S(1)}, u32[]{:S(2)}) copy-start(bf16[2048,1792]{1,0:T(8,128)(2,1)S(1)} %get-tuple-element.29) | copy-start | bytes 22020100
  27.7 3.0 %copy-start.2 = (bf16[2048,1792]{1,0:T(8,128)(2,1)}, bf16[2048,1792]{1,0:T(8,128)(2,1)S(1)}, u32[]{:S(2)}) copy-start(bf16[2048,1792]{1,0:T(8,128)(2,1)S(1)} %get-tuple-element.27) | copy-start | bytes 22020100
  30.7 5.4 %collective-permute-start.3 = (bf16[40,2048]{1,0:T(8,128)(2,1)S(1)}, bf16[40,2048]{1,0:T(8,128)(2,1)S(1)}, u32[]{:S(2)}, u32[]{:S(2)}) collective-permute-start(bf16[40,2048]{1,0:T(8,128)(2,1)S(1)} %get-tuple-element.80), channel_id=1, source_target_pairs={{0,2},{1,3},{2,0},{3,1},{4,6},{5,7},{6,4},{7,5},{8,10},{9,11},{10,... | collective-permute-start | bytes 491528 | tf_op jit(solution)/shard_map/ppermute | solution.py:41
  31.4 9.4 %collective-permute-start.11 = (bf16[40,2048]{1,0:T(8,128)(2,1)S(1)}, bf16[40,2048]{1,0:T(8,128)(2,1)S(1)}, u32[]{:S(2)}, u32[]{:S(2)}) collective-permute-start(bf16[40,2048]{1,0:T(8,128)(2,1)S(1)} %add.191), channel_id=1, source_target_pairs={{0,8},{4,12},{8,0},{12,4},{1,9},{5,13},{9,1},{13,5},{2,10},{6,14},... | collective-permute-start | bytes 491528 | tf_op jit(solution)/shard_map/ppermute | solution.py:41
  36.1 23.6 %slice-start.6 = ((s8[14680064]{0:T(1024)(128)(4,1)}), s8[4194304]{0:T(1024)(128)(4,1)S(1)}, s32[]{:S(2)}) async-start(s8[14680064]{0:T(1024)(128)(4,1)} %bitcast.107), calls=%async_computation.6 | async-start | bytes 8388608
  36.1 6.2 %collective-permute-start.5 = (bf16[80,2048]{1,0:T(8,128)(2,1)S(1)}, bf16[80,2048]{1,0:T(8,128)(2,1)S(1)}, u32[]{:S(2)}, u32[]{:S(2)}) collective-permute-start(bf16[80,2048]{1,0:T(8,128)(2,1)S(1)} %pad_maximum_fusion.13), channel_id=1, source_target_pairs={{1,4},{3,6},{4,1},{6,3},{9,12},{11,14},{12,9},{14,11},{17,20},{19,... | collective-permute-start | bytes 983048 | tf_op jit(solution)/shard_map/ppermute | solution.py:117
  36.9 10.4 %collective-permute-start.4 = (bf16[80,2048]{1,0:T(8,128)(2,1)S(1)}, bf16[80,2048]{1,0:T(8,128)(2,1)S(1)}, u32[]{:S(2)}, u32[]{:S(2)}) collective-permute-start(bf16[80,2048]{1,0:T(8,128)(2,1)S(1)} %pad_maximum_fusion.13), channel_id=1, source_target_pairs={{0,4},{1,0},{2,6},{3,2},{4,5},{5,1},{6,7},{7,3},{8,12},{9,8},{10,1... | collective-permute-start | bytes 983048 | tf_op jit(solution)/shard_map/ppermute | solution.py:117
  40.8 24.5 %collective-permute-start.12 = (bf16[40,2048]{1,0:T(8,128)(2,1)S(1)}, bf16[40,2048]{1,0:T(8,128)(2,1)S(1)}, u32[]{:S(2)}, u32[]{:S(2)}) collective-permute-start(bf16[40,2048]{1,0:T(8,128)(2,1)S(1)} %get-tuple-element.76), channel_id=1, source_target_pairs={{0,2},{1,3},{2,0},{3,1},{4,6},{5,7},{6,4},{7,5},{8,10},{9,11},{10,... | collective-permute-start | bytes 491528 | tf_op jit(solution)/shard_map/ppermute | solution.py:41
  47.4 4.9 %slice-start = ((s8[7340032]{0:T(1024)(128)(4,1)}), s8[4194304]{0:T(1024)(128)(4,1)S(1)}, s32[]{:S(2)}) async-start(s8[7340032]{0:T(1024)(128)(4,1)} %bitcast.103), calls=%async_computation | async-start | bytes 8388608
  47.5 5.1 %slice-start.1 = ((s8[7340032]{0:T(1024)(128)(4,1)}), s8[3145728]{0:T(1024)(128)(4,1)S(1)}, s32[]{:S(2)}) async-start(s8[7340032]{0:T(1024)(128)(4,1)} %bitcast.103), calls=%async_computation.1 | async-start | bytes 6291456
  47.6 7.6 %slice-start.2 = ((s8[14680064]{0:T(1024)(128)(4,1)}), s8[4194304]{0:T(1024)(128)(4,1)S(1)}, s32[]{:S(2)}) async-start(s8[14680064]{0:T(1024)(128)(4,1)} %bitcast.105), calls=%async_computation.2 | async-start | bytes 8388608
  47.6 7.6 %slice-start.3 = ((s8[14680064]{0:T(1024)(128)(4,1)}), s8[4194304]{0:T(1024)(128)(4,1)S(1)}, s32[]{:S(2)}) async-start(s8[14680064]{0:T(1024)(128)(4,1)} %bitcast.105), calls=%async_computation.3 | async-start | bytes 8388608
  47.6 12.1 %slice-start.7 = ((s8[14680064]{0:T(1024)(128)(4,1)}), s8[4194304]{0:T(1024)(128)(4,1)S(1)}, s32[]{:S(2)}) async-start(s8[14680064]{0:T(1024)(128)(4,1)} %bitcast.107), calls=%async_computation.7 | async-start | bytes 8388608
  52.7 5.0 %slice-start.4 = ((s8[14680064]{0:T(1024)(128)(4,1)}), s8[4194304]{0:T(1024)(128)(4,1)S(1)}, s32[]{:S(2)}) async-start(s8[14680064]{0:T(1024)(128)(4,1)} %bitcast.105), calls=%async_computation.4 | async-start | bytes 8388608
  52.7 5.6 %slice-start.5 = ((s8[14680064]{0:T(1024)(128)(4,1)}), s8[2097152]{0:T(1024)(128)(4,1)S(1)}, s32[]{:S(2)}) async-start(s8[14680064]{0:T(1024)(128)(4,1)} %bitcast.105), calls=%async_computation.5 | async-start | bytes 4194304
  52.7 7.0 %slice-start.8 = ((s8[14680064]{0:T(1024)(128)(4,1)}), s8[4194304]{0:T(1024)(128)(4,1)S(1)}, s32[]{:S(2)}) async-start(s8[14680064]{0:T(1024)(128)(4,1)} %bitcast.107), calls=%async_computation.8 | async-start | bytes 8388608
  54.2 5.8 %slice-start.9 = ((s8[14680064]{0:T(1024)(128)(4,1)}), s8[2097152]{0:T(1024)(128)(4,1)S(1)}, s32[]{:S(2)}) async-start(s8[14680064]{0:T(1024)(128)(4,1)} %bitcast.107), calls=%async_computation.9 | async-start | bytes 4194304
  54.3 8.3 %collective-permute-start.6 = (bf16[2,80,1792]{2,1,0:T(8,128)(2,1)S(1)}, bf16[2,80,1792]{2,1,0:T(8,128)(2,1)S(1)}, u32[]{:S(2)}, u32[]{:S(2)}) collective-permute-start(bf16[2,80,1792]{2,1,0:T(8,128)(2,1)S(1)} %pad_maximum_fusion.8), channel_id=1, source_target_pairs={{0,1},{1,0},{2,3},{3,2},{4,5},{5,4},{6,7},{7,6},{8,9},{9,8},{10,11... | collective-permute-start | bytes 1720328 | tf_op jit(solution)/shard_map/ppermute | solution.py:41
  61.6 2.5 %collective-permute-start.8 = (bf16[2,80,1792]{2,1,0:T(8,128)(2,1)S(1)}, bf16[2,80,1792]{2,1,0:T(8,128)(2,1)S(1)}, u32[]{:S(2)}, u32[]{:S(2)}) collective-permute-start(bf16[2,80,1792]{2,1,0:T(8,128)(2,1)S(1)} %pad_maximum_fusion.9), channel_id=1, source_target_pairs={{0,1},{1,0},{2,3},{3,2},{4,5},{5,4},{6,7},{7,6},{8,9},{9,8},{10,11... | collective-permute-start | bytes 1720328 | tf_op jit(solution)/shard_map/ppermute | solution.py:41
  62.7 9.8 %collective-permute-start.7 = (bf16[2,40,1792]{2,1,0:T(8,128)(2,1)S(1)}, bf16[2,40,1792]{2,1,0:T(8,128)(2,1)S(1)}, u32[]{:S(2)}, u32[]{:S(2)}) collective-permute-start(bf16[2,40,1792]{2,1,0:T(8,128)(2,1)S(1)} %pad_maximum_fusion.15), channel_id=1, source_target_pairs={{0,2},{1,3},{2,0},{3,1},{4,6},{5,7},{6,4},{7,5},{8,10},{9,11},{10,... | collective-permute-start | bytes 860168 | tf_op jit(solution)/shard_map/ppermute | solution.py:41
  64.4 19.8 %collective-permute-start.16 = (bf16[2,40,1792]{2,1,0:T(8,128)(2,1)S(1)}, bf16[2,40,1792]{2,1,0:T(8,128)(2,1)S(1)}, u32[]{:S(2)}, u32[]{:S(2)}) collective-permute-start(bf16[2,40,1792]{2,1,0:T(8,128)(2,1)S(1)} %pad_maximum_fusion.16), channel_id=1, source_target_pairs={{0,2},{1,3},{2,0},{3,1},{4,6},{5,7},{6,4},{7,5},{8,10},{9,11},{10,... | collective-permute-start | bytes 860168 | tf_op jit(solution)/shard_map/ppermute | solution.py:41
  65.3 7.3 %collective-permute-start.14 = (bf16[80,2048]{1,0:T(8,128)(2,1)S(1)}, bf16[80,2048]{1,0:T(8,128)(2,1)S(1)}, u32[]{:S(2)}, u32[]{:S(2)}) collective-permute-start(bf16[80,2048]{1,0:T(8,128)(2,1)S(1)} %pad_maximum_fusion.14), channel_id=1, source_target_pairs={{1,4},{3,6},{4,1},{6,3},{9,12},{11,14},{12,9},{14,11},{17,20},{19,... | collective-permute-start | bytes 983048 | tf_op jit(solution)/shard_map/ppermute | solution.py:117
  66.0 10.4 %collective-permute-start.13 = (bf16[80,2048]{1,0:T(8,128)(2,1)S(1)}, bf16[80,2048]{1,0:T(8,128)(2,1)S(1)}, u32[]{:S(2)}, u32[]{:S(2)}) collective-permute-start(bf16[80,2048]{1,0:T(8,128)(2,1)S(1)} %pad_maximum_fusion.14), channel_id=1, source_target_pairs={{0,4},{1,0},{2,6},{3,2},{4,5},{5,1},{6,7},{7,3},{8,12},{9,8},{10,1... | collective-permute-start | bytes 983048 | tf_op jit(solution)/shard_map/ppermute | solution.py:117
  82.4 3.1 %copy-start.4 = (f32[160,2304]{1,0:T(8,128)S(1)}, f32[160,2304]{1,0:T(8,128)}, u32[]{:S(2)}) copy-start(f32[160,2304]{1,0:T(8,128)} %fusion.2) | copy-start | bytes 4423684
  82.4 3.1 %collective-permute-start.15 = (bf16[2,80,2304]{2,1,0:T(8,128)(2,1)S(1)}, bf16[2,80,2304]{2,1,0:T(8,128)(2,1)S(1)}, u32[]{:S(2)}, u32[]{:S(2)}) collective-permute-start(bf16[2,80,2304]{2,1,0:T(8,128)(2,1)S(1)} %pad_maximum_fusion.5), channel_id=1, source_target_pairs={{0,1},{1,0},{2,3},{3,2},{4,5},{5,4},{6,7},{7,6},{8,9},{9,8},{10,11... | collective-permute-start | bytes 2211848 | tf_op jit(solution)/shard_map/ppermute | solution.py:41
  83.6 9.7 %collective-permute-start.9 = (bf16[40,1792]{1,0:T(8,128)(2,1)S(1)}, bf16[40,1792]{1,0:T(8,128)(2,1)S(1)}, u32[]{:S(2)}, u32[]{:S(2)}) collective-permute-start(bf16[40,1792]{1,0:T(8,128)(2,1)S(1)} %fusion.56), channel_id=1, source_target_pairs={{0,8},{4,12},{8,0},{12,4},{1,9},{5,13},{9,1},{13,5},{2,10},{6,14},... | collective-permute-start | bytes 430088 | tf_op jit(solution)/shard_map/ppermute | solution.py:41
  94.4 39.2 %slice-start.10 = ((s8[14680064]{0:T(1024)(128)(4,1)}), s8[2097152]{0:T(1024)(128)(4,1)S(1)}, s32[]{:S(2)}) async-start(s8[14680064]{0:T(1024)(128)(4,1)} %bitcast.109), calls=%async_computation.10 | async-start | bytes 4194304
  94.5 39.2 %slice-start.11 = ((s8[14680064]{0:T(1024)(128)(4,1)}), s8[4194304]{0:T(1024)(128)(4,1)S(1)}, s32[]{:S(2)}) async-start(s8[14680064]{0:T(1024)(128)(4,1)} %bitcast.109), calls=%async_computation.11 | async-start | bytes 8388608
  95.6 9.6 %collective-permute-start.21 = (bf16[2,80,1280]{2,1,0:T(8,128)(2,1)S(1)}, bf16[2,80,1280]{2,1,0:T(8,128)(2,1)S(1)}, u32[]{:S(2)}, u32[]{:S(2)}) collective-permute-start(bf16[2,80,1280]{2,1,0:T(8,128)(2,1)S(1)} %pad_maximum_fusion.10), channel_id=1, source_target_pairs={{0,1},{1,0},{2,3},{3,2},{4,5},{5,4},{6,7},{7,6},{8,9},{9,8},{10,11... | collective-permute-start | bytes 1228808 | tf_op jit(solution)/shard_map/ppermute | solution.py:41
  95.7 6.6 %collective-permute-start.17 = (bf16[40,1792]{1,0:T(8,128)(2,1)S(1)}, bf16[40,1792]{1,0:T(8,128)(2,1)S(1)}, u32[]{:S(2)}, u32[]{:S(2)}) collective-permute-start(bf16[40,1792]{1,0:T(8,128)(2,1)S(1)} %get-tuple-element.86), channel_id=1, source_target_pairs={{0,2},{1,3},{2,0},{3,1},{4,6},{5,7},{6,4},{7,5},{8,10},{9,11},{10,... | collective-permute-start | bytes 430088 | tf_op jit(solution)/shard_map/ppermute | solution.py:41
  97.0 13.4 %collective-permute-start.20 = (bf16[40,1792]{1,0:T(8,128)(2,1)S(1)}, bf16[40,1792]{1,0:T(8,128)(2,1)S(1)}, u32[]{:S(2)}, u32[]{:S(2)}) collective-permute-start(bf16[40,1792]{1,0:T(8,128)(2,1)S(1)} %fusion.54), channel_id=1, source_target_pairs={{0,8},{4,12},{8,0},{12,4},{1,9},{5,13},{9,1},{13,5},{2,10},{6,14},... | collective-permute-start | bytes 430088 | tf_op jit(solution)/shard_map/ppermute | solution.py:41
  97.0 13.3 %collective-permute-start.27 = (bf16[2,40,2304]{2,1,0:T(8,128)(2,1)S(1)}, bf16[2,40,2304]{2,1,0:T(8,128)(2,1)S(1)}, u32[]{:S(2)}, u32[]{:S(2)}) collective-permute-start(bf16[2,40,2304]{2,1,0:T(8,128)(2,1)S(1)} %pad_maximum_fusion.11), channel_id=1, source_target_pairs={{0,2},{1,3},{2,0},{3,1},{4,6},{5,7},{6,4},{7,5},{8,10},{9,11},{10,... | collective-permute-start | bytes 1105928 | tf_op jit(solution)/shard_map/ppermute | solution.py:41
  102.4 9.8 %collective-permute-start.19 = (bf16[80,1792]{1,0:T(8,128)(2,1)S(1)}, bf16[80,1792]{1,0:T(8,128)(2,1)S(1)}, u32[]{:S(2)}, u32[]{:S(2)}) collective-permute-start(bf16[80,1792]{1,0:T(8,128)(2,1)S(1)} %pad_maximum_fusion.17), channel_id=1, source_target_pairs={{1,4},{3,6},{4,1},{6,3},{9,12},{11,14},{12,9},{14,11},{17,20},{19,... | collective-permute-start | bytes 860168 | tf_op jit(solution)/shard_map/ppermute | solution.py:117
  103.0 9.1 %collective-permute-start.18 = (bf16[80,1792]{1,0:T(8,128)(2,1)S(1)}, bf16[80,1792]{1,0:T(8,128)(2,1)S(1)}, u32[]{:S(2)}, u32[]{:S(2)}) collective-permute-start(bf16[80,1792]{1,0:T(8,128)(2,1)S(1)} %pad_maximum_fusion.17), channel_id=1, source_target_pairs={{0,4},{1,0},{2,6},{3,2},{4,5},{5,1},{6,7},{7,3},{8,12},{9,8},{10,1... | collective-permute-start | bytes 860168 | tf_op jit(solution)/shard_map/ppermute | solution.py:117
  105.3 15.2 %collective-permute-start.29 = (bf16[2,40,1280]{2,1,0:T(8,128)(2,1)S(1)}, bf16[2,40,1280]{2,1,0:T(8,128)(2,1)S(1)}, u32[]{:S(2)}, u32[]{:S(2)}) collective-permute-start(bf16[2,40,1280]{2,1,0:T(8,128)(2,1)S(1)} %pad_maximum_fusion.19), channel_id=1, source_target_pairs={{0,2},{1,3},{2,0},{3,1},{4,6},{5,7},{6,4},{7,5},{8,10},{9,11},{10,... | collective-permute-start | bytes 614408 | tf_op jit(solution)/shard_map/ppermute | solution.py:41
  110.4 23.2 %slice-start.12 = ((s8[14680064]{0:T(1024)(128)(4,1)}), s8[4194304]{0:T(1024)(128)(4,1)S(1)}, s32[]{:S(2)}) async-start(s8[14680064]{0:T(1024)(128)(4,1)} %bitcast.109), calls=%async_computation.12 | async-start | bytes 8388608
  110.4 6.8 %collective-permute-start.22 = (bf16[40,1792]{1,0:T(8,128)(2,1)S(1)}, bf16[40,1792]{1,0:T(8,128)(2,1)S(1)}, u32[]{:S(2)}, u32[]{:S(2)}) collective-permute-start(bf16[40,1792]{1,0:T(8,128)(2,1)S(1)} %get-tuple-element.90), channel_id=1, source_target_pairs={{0,2},{1,3},{2,0},{3,1},{4,6},{5,7},{6,4},{7,5},{8,10},{9,11},{10,... | collective-permute-start | bytes 430088 | tf_op jit(solution)/shard_map/ppermute | solution.py:41
  111.7 9.8 %collective-permute-start.28 = (bf16[40,2304]{1,0:T(8,128)(2,1)S(1)}, bf16[40,2304]{1,0:T(8,128)(2,1)S(1)}, u32[]{:S(2)}, u32[]{:S(2)}) collective-permute-start(bf16[40,2304]{1,0:T(8,128)(2,1)S(1)} %fusion.48), channel_id=1, source_target_pairs={{0,8},{4,12},{8,0},{12,4},{1,9},{5,13},{9,1},{13,5},{2,10},{6,14},... | collective-permute-start | bytes 552968 | tf_op jit(solution)/shard_map/ppermute | solution.py:41
  117.3 11.6 %collective-permute-start.24 = (bf16[80,1792]{1,0:T(8,128)(2,1)S(1)}, bf16[80,1792]{1,0:T(8,128)(2,1)S(1)}, u32[]{:S(2)}, u32[]{:S(2)}) collective-permute-start(bf16[80,1792]{1,0:T(8,128)(2,1)S(1)} %pad_maximum_fusion.18), channel_id=1, source_target_pairs={{1,4},{3,6},{4,1},{6,3},{9,12},{11,14},{12,9},{14,11},{17,20},{19,... | collective-permute-start | bytes 860168 | tf_op jit(solution)/shard_map/ppermute | solution.py:117
  118.0 10.9 %collective-permute-start.23 = (bf16[80,1792]{1,0:T(8,128)(2,1)S(1)}, bf16[80,1792]{1,0:T(8,128)(2,1)S(1)}, u32[]{:S(2)}, u32[]{:S(2)}) collective-permute-start(bf16[80,1792]{1,0:T(8,128)(2,1)S(1)} %pad_maximum_fusion.18), channel_id=1, source_target_pairs={{0,4},{1,0},{2,6},{3,2},{4,5},{5,1},{6,7},{7,3},{8,12},{9,8},{10,1... | collective-permute-start | bytes 860168 | tf_op jit(solution)/shard_map/ppermute | solution.py:117
  120.6 6.9 %collective-permute-start.33 = (bf16[40,1280]{1,0:T(8,128)(2,1)S(1)}, bf16[40,1280]{1,0:T(8,128)(2,1)S(1)}, u32[]{:S(2)}, u32[]{:S(2)}) collective-permute-start(bf16[40,1280]{1,0:T(8,128)(2,1)S(1)} %fusion.62), channel_id=1, source_target_pairs={{0,8},{4,12},{8,0},{12,4},{1,9},{5,13},{9,1},{13,5},{2,10},{6,14},... | collective-permute-start | bytes 307208 | tf_op jit(solution)/shard_map/ppermute | solution.py:41
  121.5 14.6 %collective-permute-start.30 = (bf16[40,2304]{1,0:T(8,128)(2,1)S(1)}, bf16[40,2304]{1,0:T(8,128)(2,1)S(1)}, u32[]{:S(2)}, u32[]{:S(2)}) collective-permute-start(bf16[40,2304]{1,0:T(8,128)(2,1)S(1)} %get-tuple-element.68), channel_id=1, source_target_pairs={{0,2},{1,3},{2,0},{3,1},{4,6},{5,7},{6,4},{7,5},{8,10},{9,11},{10,... | collective-permute-start | bytes 552968 | tf_op jit(solution)/shard_map/ppermute | solution.py:41
  127.6 12.5 %collective-permute-start.34 = (bf16[40,1280]{1,0:T(8,128)(2,1)S(1)}, bf16[40,1280]{1,0:T(8,128)(2,1)S(1)}, u32[]{:S(2)}, u32[]{:S(2)}) collective-permute-start(bf16[40,1280]{1,0:T(8,128)(2,1)S(1)} %get-tuple-element.94), channel_id=1, source_target_pairs={{0,2},{1,3},{2,0},{3,1},{4,6},{5,7},{6,4},{7,5},{8,10},{9,11},{10,... | collective-permute-start | bytes 307208 | tf_op jit(solution)/shard_map/ppermute | solution.py:41
  129.0 4.7 %slice-start.13 = ((s8[14680064]{0:T(1024)(128)(4,1)}), s8[4194304]{0:T(1024)(128)(4,1)S(1)}, s32[]{:S(2)}) async-start(s8[14680064]{0:T(1024)(128)(4,1)} %bitcast.109), calls=%async_computation.13 | async-start | bytes 8388608
  135.2 8.9 %collective-permute-start.25 = (bf16[80,2048]{1,0:T(8,128)(2,1)S(1)}, bf16[80,2048]{1,0:T(8,128)(2,1)S(1)}, u32[]{:S(2)}, u32[]{:S(2)}) collective-permute-start(bf16[80,2048]{1,0:T(8,128)(2,1)S(1)} %slice.498), channel_id=1, source_target_pairs={{0,1},{1,0},{2,3},{3,2},{4,5},{5,4},{6,7},{7,6},{8,9},{9,8},{10,11... | collective-permute-start | bytes 983048 | tf_op jit(solution)/shard_map/ppermute | solution.py:41
  136.1 17.9 %collective-permute-start.32 = (bf16[80,2304]{1,0:T(8,128)(2,1)S(1)}, bf16[80,2304]{1,0:T(8,128)(2,1)S(1)}, u32[]{:S(2)}, u32[]{:S(2)}) collective-permute-start(bf16[80,2304]{1,0:T(8,128)(2,1)S(1)} %pad_maximum_fusion.12), channel_id=1, source_target_pairs={{1,4},{3,6},{4,1},{6,3},{9,12},{11,14},{12,9},{14,11},{17,20},{19,... | collective-permute-start | bytes 1105928 | tf_op jit(solution)/shard_map/ppermute | solution.py:117
  136.8 17.2 %collective-permute-start.31 = (bf16[80,2304]{1,0:T(8,128)(2,1)S(1)}, bf16[80,2304]{1,0:T(8,128)(2,1)S(1)}, u32[]{:S(2)}, u32[]{:S(2)}) collective-permute-start(bf16[80,2304]{1,0:T(8,128)(2,1)S(1)} %pad_maximum_fusion.12), channel_id=1, source_target_pairs={{0,4},{1,0},{2,6},{3,2},{4,5},{5,1},{6,7},{7,3},{8,12},{9,8},{10,1... | collective-permute-start | bytes 1105928 | tf_op jit(solution)/shard_map/ppermute | solution.py:117
  140.1 5.2 %collective-permute-start.36 = (bf16[80,1280]{1,0:T(8,128)(2,1)S(1)}, bf16[80,1280]{1,0:T(8,128)(2,1)S(1)}, u32[]{:S(2)}, u32[]{:S(2)}) collective-permute-start(bf16[80,1280]{1,0:T(8,128)(2,1)S(1)} %pad_maximum_fusion.20), channel_id=1, source_target_pairs={{1,4},{3,6},{4,1},{6,3},{9,12},{11,14},{12,9},{14,11},{17,20},{19,... | collective-permute-start | bytes 614408 | tf_op jit(solution)/shard_map/ppermute | solution.py:117
  140.8 12.0 %collective-permute-start.35 = (bf16[80,1280]{1,0:T(8,128)(2,1)S(1)}, bf16[80,1280]{1,0:T(8,128)(2,1)S(1)}, u32[]{:S(2)}, u32[]{:S(2)}) collective-permute-start(bf16[80,1280]{1,0:T(8,128)(2,1)S(1)} %pad_maximum_fusion.20), channel_id=1, source_target_pairs={{0,4},{1,0},{2,6},{3,2},{4,5},{5,1},{6,7},{7,3},{8,12},{9,8},{10,1... | collective-permute-start | bytes 614408 | tf_op jit(solution)/shard_map/ppermute | solution.py:117
  144.2 9.7 %collective-permute-start.26 = (bf16[80,2048]{1,0:T(8,128)(2,1)S(1)}, bf16[80,2048]{1,0:T(8,128)(2,1)S(1)}, u32[]{:S(2)}, u32[]{:S(2)}) collective-permute-start(bf16[80,2048]{1,0:T(8,128)(2,1)S(1)} %get-tuple-element.53), channel_id=1, source_target_pairs={{0,2},{1,3},{2,0},{3,1},{4,6},{5,7},{6,4},{7,5},{8,10},{9,11},{10,... | collective-permute-start | bytes 983048 | tf_op jit(solution)/shard_map/ppermute | solution.py:41
  156.0 2.2 %collective-permute-start.37 = (bf16[80,2048]{1,0:T(8,128)(2,1)S(1)}, bf16[80,2048]{1,0:T(8,128)(2,1)S(1)}, u32[]{:S(2)}, u32[]{:S(2)}) collective-permute-start(bf16[80,2048]{1,0:T(8,128)(2,1)S(1)} %slice.497), channel_id=1, source_target_pairs={{0,1},{1,0},{2,3},{3,2},{4,5},{5,4},{6,7},{7,6},{8,9},{9,8},{10,11... | collective-permute-start | bytes 983048 | tf_op jit(solution)/shard_map/ppermute | solution.py:41
  158.3 10.1 %collective-permute-start.38 = (bf16[80,2048]{1,0:T(8,128)(2,1)S(1)}, bf16[80,2048]{1,0:T(8,128)(2,1)S(1)}, u32[]{:S(2)}, u32[]{:S(2)}) collective-permute-start(bf16[80,2048]{1,0:T(8,128)(2,1)S(1)} %fusion.41), channel_id=1, source_target_pairs={{0,2},{1,3},{2,0},{3,1},{4,6},{5,7},{6,4},{7,5},{8,10},{9,11},{10,... | collective-permute-start | bytes 983048 | tf_op jit(solution)/shard_map/ppermute | solution.py:41
  169.4 2.2 %collective-permute-start.39 = (bf16[160,2048]{1,0:T(8,128)(2,1)S(1)}, bf16[160,2048]{1,0:T(8,128)(2,1)S(1)}, u32[]{:S(2)}, u32[]{:S(2)}) collective-permute-start(bf16[160,2048]{1,0:T(8,128)(2,1)S(1)} %select_convert_fusion), channel_id=1, source_target_pairs={{0,1},{1,0},{2,3},{3,2},{4,5},{5,4},{6,7},{7,6},{8,9},{9,8},{10,11... | collective-permute-start | bytes 1966088 | tf_op jit(solution)/shard_map/ppermute | solution.py:41

commit v10 on v9

--- a/solution.py
+++ b/solution.py
@@ -1,5 +1,3 @@
-import functools
-
 import jax
 import jax.numpy as jnp
 from jax import lax
@@ -10,8 +8,10 @@
 HALVES = 2
 PARTS = ((14, 14), (18, 10))
 EDGES = {
-    "w.pull": ["t0.add"],
-    "t0.halves": ["w.pull"],
+    "g.pull": ["t0.add"],
+    "t0.halves": ["g.pull"],
+    "u.pull": ["t0.columns"],
+    "t0.cores": ["u.pull"],
     "t1.pick": ["t0.add"],
     "t1.add": ["t0.halves"],
     "t1.halves": ["t0.columns"],
@@ -22,11 +22,13 @@
     "t1.cores": ["c00.hidden"],
     "c01.hidden": ["c10.dots"],
     "c10.sum": ["c01.hidden"],
-    "c11.dots": ["c00.halves"],
+    "c11.dots": ["c10.sum"],
     "c00.halves": ["c10.sum"],
     "c10.hidden": ["c11.sum"],
     "c01.halves": ["c11.sum"],
     "c10.halves": ["c11.hidden"],
+    "c01.cores": ["c10.columns", "c11.columns"],
+    "c00.down": ["c01.cores"],
     "c10.cores": ["b0.all"],
     "c11.cores": ["b0.total"],
 }
@@ -41,38 +43,26 @@
     return lax.ppermute(value, axis, [(i, i ^ bit) for i in range(count)])
 
 
-def pull_kernel(first, end, tick_ref, gate_ref, up_ref, gate_here, up_here, sems):
+def pull_kernel(tick_ref, weight_ref, here_ref, sem):
     del tick_ref
-    columns = pl.ds(first, end - first)
-    copies = [
-        pltpu.make_async_copy(source.at[:, columns], here, sems.at[i])
-        for i, (source, here) in enumerate(((gate_ref, gate_here), (up_ref, up_here)))
-    ]
-    for copy in copies:
-        copy.start()
-    for copy in copies:
-        copy.wait()
-
-
-def pull(gate_weight, up_weight, first, end, tick):
-    far = pl.BlockSpec(memory_space=pltpu.HBM)
-    near = pl.BlockSpec(memory_space=pltpu.VMEM)
-    here = pltpu.VMEM((gate_weight.shape[0], end - first), gate_weight.dtype)
+    copy = pltpu.make_async_copy(weight_ref, here_ref, sem)
+    copy.start()
+    copy.wait()
+
+
+def pull(weight, tick):
     return pl.pallas_call(
-        functools.partial(pull_kernel, first, end),
-        in_specs=[pl.BlockSpec(memory_space=pltpu.SMEM), far, far],
-        out_specs=[near, near],
-        out_shape=[here, here],
-        scratch_shapes=[pltpu.SemaphoreType.DMA((2,))],
-        compiler_params=pltpu.CompilerParams(
-            vmem_limit_bytes=4 * gate_weight.shape[0] * (end - first) + 2**20
-        ),
+        pull_kernel,
+        in_specs=[
+            pl.BlockSpec(memory_space=pltpu.SMEM),
+            pl.BlockSpec(memory_space=pltpu.HBM),
+        ],
+        out_specs=pl.BlockSpec(memory_space=pltpu.VMEM),
+        out_shape=pltpu.VMEM(weight.shape, weight.dtype),
+        scratch_shapes=[pltpu.SemaphoreType.DMA],
+        compiler_params=pltpu.CompilerParams(vmem_limit_bytes=2 * weight.size + 2**20),
         cost_estimate=pl.CostEstimate(flops=0, bytes_accessed=0, transcendentals=0),
-    )(
-        tick,
-        pltpu.with_memory_space_constraint(gate_weight, pltpu.HBM),
-        pltpu.with_memory_space_constraint(up_weight, pltpu.HBM),
-    )
+    )(tick, pltpu.with_memory_space_constraint(weight, pltpu.HBM))
 
 
 def stationary(tokens, lengths, gate_weight, up_weight, down_weight):
@@ -175,12 +165,10 @@
         yield
         return issued(name + ".add", ordered(name + ".add", rows[:piece]) + got)
 
-    pulled = []
-
-    def pull_steps():
-        tick = ordered("w.pull", lengths)
-        pulled.extend(pull(gate_weight, up_weight, *spans[0][0], tick))
-        issued("w.pull", pulled[0])
+    pulled = {}
+
+    def pull_steps(name, weight):
+        pulled[name] = issued(name + ".pull", pull(weight, ordered(name + ".pull", lengths)))
         return None
         yield
 
@@ -192,10 +180,9 @@
         full = result("t" + str(h))
         part = slice(*spans[h][i])
         full = ordered(name + ".dots", full)
-        if (h, i) == (0, 0):
-            gate, up = dot(full, pulled[0]), dot(full, pulled[1])
-        else:
-            gate, up = dot(full, gate_weight[:, part]), dot(full, up_weight[:, part])
+        result("g")
+        result("u")
+        gate, up = dot(full, pulled["g"][:, part]), dot(full, pulled["u"][:, part])
         send = issued(name + ".dots", jnp.stack([gate[half:], up[half:]]).astype(jnp.bfloat16))
         got = issued(name + ".cores_swapped", flip(send, "col", 1))
         yield
@@ -222,7 +209,8 @@
         got = ordered(name + ".all", got)
         return issued(name + ".all", total + jnp.concatenate([got[piece:], got[:piece]], axis=0))
 
-    chains, results = {"w": pull_steps()}, {}
+    chains = {"g": pull_steps("g", gate_weight), "u": pull_steps("u", up_weight)}
+    results = {}
     for h in range(HALVES):
         chains["t" + str(h)] = half_steps("t" + str(h), h)
         for i in range(len(spans[h])):
@@ -240,7 +228,6 @@
             advance(name)
         return results[name]
 
-    result("w")
     for h in range(HALVES):
         result("b" + str(h))
 

time: 174 us -> 165 us (0.948)
  waiting for transfers between devices: 69.1 us -> 59.4 us
  Pallas kernels: 6.08 us -> 12.2 us
  matrix products: 29.5 us -> 26 us
  local copies, waits for them, and re-layouts: 11.5 us -> 8.03 us
  starting transfers between devices: 49.4 us -> 51.5 us
    pallas_call x1 -> x2, Pallas kernels: 6.08 us -> 12.2 us  [pull(): pl.pallas_call(pull_kernel, in_specs=[pl.BlockSpec(memory_space=pltpu.SME...]
    ppermute x12, waiting for transfers between devices: 16.3 us -> 10.5 us  [move(): return lax.ppermute(value, ('row', 'col'), pairs)]
    ppermute x28, waiting for transfers between devices: 52.8 us -> 48.9 us  [flip(): return lax.ppermute(value, axis, [(i, i ^ bit) for i in range(count)])]
    dot_general x16, matrix products: 26.7 us -> 23.2 us  [dot(): return jnp.dot(a, b, preferred_element_type=jnp.float32)]
    unnamed x38 -> x24, local copies, waits for them, and re-layouts: 9.8 us -> 6.36 us
  transfers between devices with their start and end apart: 40 -> 40, of which waited for: 17 -> 15; matrix products, arithmetic and copies ran while one was open for 18% -> 17% of each run, Pallas kernels for 4% -> 7%
where the time goes in v10:
time: 165 us
  waiting for transfers between devices  59.4 us (36%)
  starting transfers between devices  51.5 us (31%)
  matrix products  26 us (16%)
  Pallas kernels  12.2 us (7%)
  local copies, waits for them, and re-layouts  8.03 us (5%)
  other arithmetic  6.94 us (4%)
    ppermute x28, waiting for transfers between devices, flip(): return lax.ppermute(value, axis, [(i, i ^ bit) for i in range(count)])  48.9 us
    ppermute x28, starting transfers between devices, flip(): return lax.ppermute(value, axis, [(i, i ^ bit) for i in range(count)])  28.3 us
    dot_general x16, matrix products, dot(): return jnp.dot(a, b, preferred_element_type=jnp.float32)  23.2 us
    ppermute x12, starting transfers between devices, move(): return lax.ppermute(value, ('row', 'col'), pairs)  23.1 us
    pallas_call x2, Pallas kernels, pull(): pl.pallas_call(pull_kernel, in_specs=[pl.BlockSpec(memory_space=pltpu.SME...  12.2 us
    ppermute x12, waiting for transfers between devices, move(): return lax.ppermute(value, ('row', 'col'), pairs)  10.5 us
    unnamed x24, local copies, waits for them, and re-layouts  6.36 us
  transfers between devices with their start and end apart: 40, of which 15 were waited for; matrix products, arithmetic and copies ran while one was open for 17% of the time, Pallas kernels for 7%

profile of v10, /device:TPU:0, one launch (start us, length us, event | category | flops | bytes accessed | tf_op | source)
XLA Modules:
  0.0 164.9 jit_solution(10509858581142346769)
XLA Ops:
  0.5 1.4 fusion.86
  1.9 2.5 %compare_select_fusion.1 = (s32[160]{0:T(256)S(1)}, s32[160]{0:T(256)S(1)}) fusion(s32[]{:T(128)} %get-tuple-element.54, s32[]{:T(128)} %get-tuple-element.53, s32[]{:T(128)} %get-tuple-element.55, s32[]{:T(128)} %get-tuple-element.56), kind=kLoop, calls=%fused_computation.176 | loop fusion | flops 960 | bytes 1296 | tf_op jit(solution)/shard_map/jit(_where)/select_n | solution.py:91
  4.5 1.4 fusion.73
  6.5 2.6 %collective-permute-start.1 = (bf16[40,2048]{1,0:T(8,128)(2,1)S(1)}, bf16[40,2048]{1,0:T(8,128)(2,1)S(1)}, u32[]{:S(2)}, u32[]{:S(2)}) collective-permute-start(bf16[40,2048]{1,0:T(8,128)(2,1)S(1)} %slice.307), channel_id=1, source_target_pairs={{0,2},{1,3},{2,0},{3,1},{4,6},{5,7},{6,4},{7,5},{8,10},{9,11},{10,... | collective-permute-start | bytes 491528 | tf_op jit(solution)/shard_map/ppermute | solution.py:43
  9.2 4.7 %collective-permute-done.1 = bf16[40,2048]{1,0:T(8,128)(2,1)S(1)} collective-permute-done((bf16[40,2048]{1,0:T(8,128)(2,1)S(1)}, bf16[40,2048]{1,0:T(8,128)(2,1)S(1)}, u32[]{:S(2)}, u32[]{:S(2)}) %collective-permute-start.1) | collective-permute-done | bytes 163872 | tf_op jit(solution)/shard_map/ppermute | solution.py:43
  13.9 2.9 %collective-permute-start.2 = (bf16[40,2048]{1,0:T(8,128)(2,1)S(1)}, bf16[40,2048]{1,0:T(8,128)(2,1)S(1)}, u32[]{:S(2)}, u32[]{:S(2)}) collective-permute-start(bf16[40,2048]{1,0:T(8,128)(2,1)S(1)} %slice_add_fusion.18), channel_id=1, source_target_pairs={{0,8},{4,12},{8,0},{12,4},{1,9},{5,13},{9,1},{13,5},{2,10},{6,14},... | collective-permute-start | bytes 491528 | tf_op jit(solution)/shard_map/ppermute | solution.py:43
  17.1 1.6 collective-permute-start.10
  18.7 5.7 %shard_map.55 = bf16[2048,3584]{1,0:T(8,128)(2,1)S(1)} custom-call(s32[4]{0:T(128)S(1)} %copy-done.1, bf16[2048,3584]{1,0:T(8,128)(2,1)} %weight_ref.2), custom_call_target="tpu_custom_call" | custom-call | tf_op jit(solution)/shard_map/pallas_call | solution.py:54
  24.4 5.2 %copy-done = bf16[2048,3584]{1,0:T(8,128)(2,1)} copy-done((bf16[2048,3584]{1,0:T(8,128)(2,1)}, bf16[2048,3584]{1,0:T(8,128)(2,1)S(1)}, u32[]{:S(2)}) %copy-start) | copy-done | bytes 14680088
  30.4 4.6 %collective-permute-done.3 = bf16[40,2048]{1,0:T(8,128)(2,1)S(1)} collective-permute-done((bf16[40,2048]{1,0:T(8,128)(2,1)S(1)}, bf16[40,2048]{1,0:T(8,128)(2,1)S(1)}, u32[]{:S(2)}, u32[]{:S(2)}) %collective-permute-start.3) | collective-permute-done | bytes 163872 | tf_op jit(solution)/shard_map/ppermute | solution.py:43
  35.0 0.7 collective-permute-start.5
  35.7 2.9 %collective-permute-start.4 = (bf16[80,2048]{1,0:T(8,128)(2,1)S(1)}, bf16[80,2048]{1,0:T(8,128)(2,1)S(1)}, u32[]{:S(2)}, u32[]{:S(2)}) collective-permute-start(bf16[80,2048]{1,0:T(8,128)(2,1)S(1)} %pad_maximum_fusion.15), channel_id=1, source_target_pairs={{0,4},{1,0},{2,6},{3,2},{4,5},{5,1},{6,7},{7,3},{8,12},{9,8},{10,1... | collective-permute-start | bytes 983048 | tf_op jit(solution)/shard_map/ppermute | solution.py:107
  38.6 1.1 collective-permute-done.11
  39.7 1.6 collective-permute-start.12
  41.4 6.5 %shard_map.56 = bf16[2048,3584]{1,0:T(8,128)(2,1)S(1)} custom-call(s32[4]{0:T(128)S(1)} %copy-done.1, bf16[2048,3584]{1,0:T(8,128)(2,1)} %weight_ref.3), custom_call_target="tpu_custom_call" | custom-call | tf_op jit(solution)/shard_map/pallas_call | solution.py:54
  49.1 1.4 fusion.12
  50.5 1.4 fusion.10
  52.1 1.4 fusion.6
  53.5 1.4 fusion.8
  55.8 1.6 collective-permute-start.7
  57.6 1.4 collective-permute-start.16
  59.1 0.7 collective-permute-start.14
  59.8 3.2 %collective-permute-start.13 = (bf16[80,2048]{1,0:T(8,128)(2,1)S(1)}, bf16[80,2048]{1,0:T(8,128)(2,1)S(1)}, u32[]{:S(2)}, u32[]{:S(2)}) collective-permute-start(bf16[80,2048]{1,0:T(8,128)(2,1)S(1)} %pad_maximum_fusion.16), channel_id=1, source_target_pairs={{0,4},{1,0},{2,6},{3,2},{4,5},{5,1},{6,7},{7,3},{8,12},{9,8},{10,1... | collective-permute-start | bytes 983048 | tf_op jit(solution)/shard_map/ppermute | solution.py:107
  63.0 2.6 %collective-permute-done.7 = bf16[2,40,1792]{2,1,0:T(8,128)(2,1)S(1)} collective-permute-done((bf16[2,40,1792]{2,1,0:T(8,128)(2,1)S(1)}, bf16[2,40,1792]{2,1,0:T(8,128)(2,1)S(1)}, u32[]{:S(2)}, u32[]{:S(2)}) %collective-permute-start.7) | collective-permute-done | bytes 286752 | tf_op jit(solution)/shard_map/ppermute | solution.py:43
  65.7 2.8 %collective-permute-done.13 = bf16[80,2048]{1,0:T(8,128)(2,1)S(1)} collective-permute-done((bf16[80,2048]{1,0:T(8,128)(2,1)S(1)}, bf16[80,2048]{1,0:T(8,128)(2,1)S(1)}, u32[]{:S(2)}, u32[]{:S(2)}) %collective-permute-start.13) | collective-permute-done | bytes 327712 | tf_op jit(solution)/shard_map/ppermute | solution.py:107
  68.5 1.7 %fusion.2 = f32[160,2304]{1,0:T(8,128)S(1)} fusion(bf16[2048,3584]{1,0:T(8,128)(2,1)S(1)} %bitcast.103, bf16[80,2048]{1,0:T(8,128)(2,1)S(1)} %get-tuple-element.78, bf16[80,2048]{1,0:T(8,128)(2,1)S(1)} %get-tuple-element.77), kind=kOutput, calls=%fused_computation.2 | convolution fusion | flops 1511260160 | bytes 11567104 | tf_op jit(solution)/shard_map/dot_general | solution.py:38
  70.3 2.9 %fusion = f32[160,2304]{1,0:T(8,128)} fusion(bf16[2048,3584]{1,0:T(8,128)(2,1)S(1)} %shard_map.56, bf16[80,2048]{1,0:T(8,128)(2,1)S(1)} %get-tuple-element.78, bf16[80,2048]{1,0:T(8,128)(2,1)S(1)} %get-tuple-element.77), kind=kOutput, calls=%fused_computation | convolution fusion | flops 1511260160 | bytes 11567104 | tf_op jit(solution)/shard_map/dot_general | solution.py:38
  73.1 1.2 fusion.44
  74.4 2.5 %collective-permute-start.15 = (bf16[2,80,2304]{2,1,0:T(8,128)(2,1)S(1)}, bf16[2,80,2304]{2,1,0:T(8,128)(2,1)S(1)}, u32[]{:S(2)}, u32[]{:S(2)}) collective-permute-start(bf16[2,80,2304]{2,1,0:T(8,128)(2,1)S(1)} %pad_maximum_fusion.5), channel_id=1, source_target_pairs={{0,1},{1,0},{2,3},{3,2},{4,5},{5,4},{6,7},{7,6},{8,9},{9,8},{10,11... | collective-permute-start | bytes 2211848 | tf_op jit(solution)/shard_map/ppermute | solution.py:43
  77.4 1.3 collective-permute-done.15
  79.0 1.1 fusion.18
  80.0 1.0 fusion.20
  81.1 5.4 %collective-permute-done.9 = bf16[40,1792]{1,0:T(8,128)(2,1)S(1)} collective-permute-done((bf16[40,1792]{1,0:T(8,128)(2,1)S(1)}, bf16[40,1792]{1,0:T(8,128)(2,1)S(1)}, u32[]{:S(2)}, u32[]{:S(2)}) %collective-permute-start.9) | collective-permute-done | bytes 143392 | tf_op jit(solution)/shard_map/ppermute | solution.py:43
  86.8 1.1 collective-permute-start.17
  87.8 1.0 collective-permute-start.23
  88.9 4.5 %collective-permute-done.17 = bf16[40,1792]{1,0:T(8,128)(2,1)S(1)} collective-permute-done((bf16[40,1792]{1,0:T(8,128)(2,1)S(1)}, bf16[40,1792]{1,0:T(8,128)(2,1)S(1)}, u32[]{:S(2)}, u32[]{:S(2)}) %collective-permute-start.17) | collective-permute-done | bytes 143392 | tf_op jit(solution)/shard_map/ppermute | solution.py:43
  93.4 0.7 collective-permute-start.19
  94.1 2.2 %collective-permute-start.18 = (bf16[80,1792]{1,0:T(8,128)(2,1)S(1)}, bf16[80,1792]{1,0:T(8,128)(2,1)S(1)}, u32[]{:S(2)}, u32[]{:S(2)}) collective-permute-start(bf16[80,1792]{1,0:T(8,128)(2,1)S(1)} %pad_maximum_fusion.19), channel_id=1, source_target_pairs={{0,4},{1,0},{2,6},{3,2},{4,5},{5,1},{6,7},{7,3},{8,12},{9,8},{10,1... | collective-permute-start | bytes 860168 | tf_op jit(solution)/shard_map/ppermute | solution.py:107
  96.5 1.1 collective-permute-start.25
  97.6 3.7 %collective-permute-done.23 = bf16[2,40,2304]{2,1,0:T(8,128)(2,1)S(1)} collective-permute-done((bf16[2,40,2304]{2,1,0:T(8,128)(2,1)S(1)}, bf16[2,40,2304]{2,1,0:T(8,128)(2,1)S(1)}, u32[]{:S(2)}, u32[]{:S(2)}) %collective-permute-start.23) | collective-permute-done | bytes 368672 | tf_op jit(solution)/shard_map/ppermute | solution.py:43
  101.5 1.1 collective-permute-start.22
  102.5 1.0 collective-permute-start.24
  103.7 4.6 %fusion.16 = f32[160,2048]{1,0:T(8,128)S(1)} fusion(bf16[160,1792]{1,0:T(8,128)(2,1)S(1)} %pad_maximum_fusion.10, bf16[3584,2048]{1,0:T(8,128)(2,1)} %param.9), kind=kOutput, calls=%fused_computation.16 | convolution fusion | flops 1174405120 | bytes 9224192 | tf_op jit(solution)/shard_map/dot_general | solution.py:38
  109.1 3.0 %collective-permute-start.29 = (bf16[80,1792]{1,0:T(8,128)(2,1)S(1)}, bf16[80,1792]{1,0:T(8,128)(2,1)S(1)}, u32[]{:S(2)}, u32[]{:S(2)}) collective-permute-start(bf16[80,1792]{1,0:T(8,128)(2,1)S(1)} %pad_maximum_fusion.20), channel_id=1, source_target_pairs={{0,4},{1,0},{2,6},{3,2},{4,5},{5,1},{6,7},{7,3},{8,12},{9,8},{10,1... | collective-permute-start | bytes 860168 | tf_op jit(solution)/shard_map/ppermute | solution.py:107
  112.1 1.5 collective-permute-start.27
  113.6 1.0 collective-permute-start.26
  114.6 5.3 %collective-permute-done.27 = bf16[40,1280]{1,0:T(8,128)(2,1)S(1)} collective-permute-done((bf16[40,1280]{1,0:T(8,128)(2,1)S(1)}, bf16[40,1280]{1,0:T(8,128)(2,1)S(1)}, u32[]{:S(2)}, u32[]{:S(2)}) %collective-permute-start.27) | collective-permute-done | bytes 102432 | tf_op jit(solution)/shard_map/ppermute | solution.py:43
  119.9 1.2 collective-permute-start.28
  121.2 3.5 %collective-permute-done.28 = bf16[40,1280]{1,0:T(8,128)(2,1)S(1)} collective-permute-done((bf16[40,1280]{1,0:T(8,128)(2,1)S(1)}, bf16[40,1280]{1,0:T(8,128)(2,1)S(1)}, u32[]{:S(2)}, u32[]{:S(2)}) %collective-permute-start.28) | collective-permute-done | bytes 102432 | tf_op jit(solution)/shard_map/ppermute | solution.py:43
  124.8 1.4 fusion.25
  126.4 0.7 collective-permute-start.34
  127.1 4.5 %collective-permute-start.33 = (bf16[80,2304]{1,0:T(8,128)(2,1)S(1)}, bf16[80,2304]{1,0:T(8,128)(2,1)S(1)}, u32[]{:S(2)}, u32[]{:S(2)}) collective-permute-start(bf16[80,2304]{1,0:T(8,128)(2,1)S(1)} %pad_maximum_fusion.14), channel_id=1, source_target_pairs={{0,4},{1,0},{2,6},{3,2},{4,5},{5,1},{6,7},{7,3},{8,12},{9,8},{10,1... | collective-permute-start | bytes 1105928 | tf_op jit(solution)/shard_map/ppermute | solution.py:107
  132.3 3.3 %collective-permute-start.35 = (bf16[80,1280]{1,0:T(8,128)(2,1)S(1)}, bf16[80,1280]{1,0:T(8,128)(2,1)S(1)}, u32[]{:S(2)}, u32[]{:S(2)}) collective-permute-start(bf16[80,1280]{1,0:T(8,128)(2,1)S(1)} %pad_maximum_fusion.22), channel_id=1, source_target_pairs={{0,4},{1,0},{2,6},{3,2},{4,5},{5,1},{6,7},{7,3},{8,12},{9,8},{10,1... | collective-permute-start | bytes 614408 | tf_op jit(solution)/shard_map/ppermute | solution.py:107
  135.7 1.0 collective-permute-start.32
  136.7 7.7 %collective-permute-done.35 = bf16[80,1280]{1,0:T(8,128)(2,1)S(1)} collective-permute-done((bf16[80,1280]{1,0:T(8,128)(2,1)S(1)}, bf16[80,1280]{1,0:T(8,128)(2,1)S(1)}, u32[]{:S(2)}, u32[]{:S(2)}) %collective-permute-start.35) | collective-permute-done | bytes 204832 | tf_op jit(solution)/shard_map/ppermute | solution.py:107
  144.4 1.0 fusion.22
  145.6 1.8 %fusion.28 = f32[160,2048]{1,0:T(8,128)S(1)} fusion(f32[160,2048]{1,0:T(8,128)S(1)} %fusion.22, bf16[3584,2048]{1,0:T(8,128)(2,1)S(1)} %bitcast.105, bf16[80,2304]{1,0:T(8,128)(2,1)S(1)} %get-tuple-element.70, bf16[80,2304]{1,0:T(8,128)(2,1)S(1)} %get-tuple-element.69), kind=kOutput, calls=%fused_computation.27 | convolution fusion | flops 1511751680 | bytes 12795904 | tf_op jit(solution)/shard_map/dot_general | solution.py:38
  147.5 0.9 collective-permute-start.37
  148.4 1.3 collective-permute-done.37
  149.7 1.0 collective-permute-start.38
  151.1 8.7 %collective-permute-done.38 = bf16[80,2048]{1,0:T(8,128)(2,1)S(1)} collective-permute-done((bf16[80,2048]{1,0:T(8,128)(2,1)S(1)}, bf16[80,2048]{1,0:T(8,128)(2,1)S(1)}, u32[]{:S(2)}, u32[]{:S(2)}) %collective-permute-start.38) | collective-permute-done | bytes 327712 | tf_op jit(solution)/shard_map/ppermute | solution.py:43
  160.0 0.9 select_convert_fusion
  160.9 2.1 %collective-permute-done.39 = bf16[160,2048]{1,0:T(8,128)(2,1)S(1)} collective-permute-done((bf16[160,2048]{1,0:T(8,128)(2,1)S(1)}, bf16[160,2048]{1,0:T(8,128)(2,1)S(1)}, u32[]{:S(2)}, u32[]{:S(2)}) %collective-permute-start.39) | collective-permute-done | bytes 655392 | tf_op jit(solution)/shard_map/ppermute | solution.py:43
  163.0 1.8 %fusion.34 = bf16[160,2048]{1,0:T(8,128)(2,1)} fusion(bf16[160,2048]{1,0:T(8,128)(2,1)S(1)} %collective-permute-done.39, bf16[160,2048]{1,0:T(8,128)(2,1)S(1)} %copy-done.2, f32[80,2048]{1,0:T(8,128)S(1)} %convert_add_fusion, f32[80,2048]{1,0:T(8,128)S(1)} %convert_add_fusion.1, pred[160]{0:T(512)(128)(4,1)S(1)} %get-tuple-element.51, ...), kind=kOutput, calls=%fused_computation.35 | convolution fusion | flops 631137280 | bytes 3278240 | tf_op jit(solution)/shard_map/dot_general | solution.py:238
  (134 shorter events, 9.4 us)
Async XLA Ops:
  0.0 5.8 %copy-start.2 = (bf16[160,2048]{1,0:T(8,128)(2,1)S(1)}, bf16[160,2048]{1,0:T(8,128)(2,1)}, u32[]{:S(2)}) copy-start(bf16[160,2048]{1,0:T(8,128)(2,1)} %param.5) | copy-start | bytes 1966084
  0.0 6.2 %collective-permute-start = (bf16[160,2048]{1,0:T(8,128)(2,1)}, bf16[160,2048]{1,0:T(8,128)(2,1)S(1)}, u32[]{:S(2)}, u32[]{:S(2)}) collective-permute-start(bf16[160,2048]{1,0:T(8,128)(2,1)} %param.5), channel_id=1, source_target_pairs={{0,1},{1,0},{2,3},{3,2},{4,5},{5,4},{6,7},{7,6},{8,9},{9,8},{10,11... | collective-permute-start | bytes 1966088 | tf_op jit(solution)/shard_map/ppermute | solution.py:43
  6.5 7.4 %collective-permute-start.1 = (bf16[40,2048]{1,0:T(8,128)(2,1)S(1)}, bf16[40,2048]{1,0:T(8,128)(2,1)S(1)}, u32[]{:S(2)}, u32[]{:S(2)}) collective-permute-start(bf16[40,2048]{1,0:T(8,128)(2,1)S(1)} %slice.307), channel_id=1, source_target_pairs={{0,2},{1,3},{2,0},{3,1},{4,6},{5,7},{6,4},{7,5},{8,10},{9,11},{10,... | collective-permute-start | bytes 491528 | tf_op jit(solution)/shard_map/ppermute | solution.py:43
  9.2 9.5 %copy-start.1 = (s32[4]{0:T(128)S(1)}, s32[4]{0:T(128)}, u32[]{:S(2)}) copy-start(s32[4]{0:T(128)} %tick_ref.1) | copy-start | bytes 52
  13.9 15.7 %collective-permute-start.2 = (bf16[40,2048]{1,0:T(8,128)(2,1)S(1)}, bf16[40,2048]{1,0:T(8,128)(2,1)S(1)}, u32[]{:S(2)}, u32[]{:S(2)}) collective-permute-start(bf16[40,2048]{1,0:T(8,128)(2,1)S(1)} %slice_add_fusion.18), channel_id=1, source_target_pairs={{0,8},{4,12},{8,0},{12,4},{1,9},{5,13},{9,1},{13,5},{2,10},{6,14},... | collective-permute-start | bytes 491528 | tf_op jit(solution)/shard_map/ppermute | solution.py:43
  17.1 13.1 %collective-permute-start.10 = (bf16[40,2048]{1,0:T(8,128)(2,1)S(1)}, bf16[40,2048]{1,0:T(8,128)(2,1)S(1)}, u32[]{:S(2)}, u32[]{:S(2)}) collective-permute-start(bf16[40,2048]{1,0:T(8,128)(2,1)S(1)} %get-tuple-element.85), channel_id=1, source_target_pairs={{0,2},{1,3},{2,0},{3,1},{4,6},{5,7},{6,4},{7,5},{8,10},{9,11},{10,... | collective-permute-start | bytes 491528 | tf_op jit(solution)/shard_map/ppermute | solution.py:43
  24.4 5.2 %copy-start = (bf16[2048,3584]{1,0:T(8,128)(2,1)}, bf16[2048,3584]{1,0:T(8,128)(2,1)S(1)}, u32[]{:S(2)}) copy-start(bf16[2048,3584]{1,0:T(8,128)(2,1)S(1)} %shard_map.55) | copy-start | bytes 44040196
  29.6 5.4 %collective-permute-start.3 = (bf16[40,2048]{1,0:T(8,128)(2,1)S(1)}, bf16[40,2048]{1,0:T(8,128)(2,1)S(1)}, u32[]{:S(2)}, u32[]{:S(2)}) collective-permute-start(bf16[40,2048]{1,0:T(8,128)(2,1)S(1)} %get-tuple-element.84), channel_id=1, source_target_pairs={{0,2},{1,3},{2,0},{3,1},{4,6},{5,7},{6,4},{7,5},{8,10},{9,11},{10,... | collective-permute-start | bytes 491528 | tf_op jit(solution)/shard_map/ppermute | solution.py:43
  30.3 9.4 %collective-permute-start.11 = (bf16[40,2048]{1,0:T(8,128)(2,1)S(1)}, bf16[40,2048]{1,0:T(8,128)(2,1)S(1)}, u32[]{:S(2)}, u32[]{:S(2)}) collective-permute-start(bf16[40,2048]{1,0:T(8,128)(2,1)S(1)} %add.191), channel_id=1, source_target_pairs={{0,8},{4,12},{8,0},{12,4},{1,9},{5,13},{9,1},{13,5},{2,10},{6,14},... | collective-permute-start | bytes 491528 | tf_op jit(solution)/shard_map/ppermute | solution.py:43
  35.0 12.8 %collective-permute-start.5 = (bf16[80,2048]{1,0:T(8,128)(2,1)S(1)}, bf16[80,2048]{1,0:T(8,128)(2,1)S(1)}, u32[]{:S(2)}, u32[]{:S(2)}) collective-permute-start(bf16[80,2048]{1,0:T(8,128)(2,1)S(1)} %pad_maximum_fusion.15), channel_id=1, source_target_pairs={{1,4},{3,6},{4,1},{6,3},{9,12},{11,14},{12,9},{14,11},{17,20},{19,... | collective-permute-start | bytes 983048 | tf_op jit(solution)/shard_map/ppermute | solution.py:107
  35.7 12.1 %collective-permute-start.4 = (bf16[80,2048]{1,0:T(8,128)(2,1)S(1)}, bf16[80,2048]{1,0:T(8,128)(2,1)S(1)}, u32[]{:S(2)}, u32[]{:S(2)}) collective-permute-start(bf16[80,2048]{1,0:T(8,128)(2,1)S(1)} %pad_maximum_fusion.15), channel_id=1, source_target_pairs={{0,4},{1,0},{2,6},{3,2},{4,5},{5,1},{6,7},{7,3},{8,12},{9,8},{10,1... | collective-permute-start | bytes 983048 | tf_op jit(solution)/shard_map/ppermute | solution.py:107
  39.7 8.3 %slice-start = ((s8[14680064]{0:T(1024)(128)(4,1)}), s8[4194304]{0:T(1024)(128)(4,1)S(1)}, s32[]{:S(2)}) async-start(s8[14680064]{0:T(1024)(128)(4,1)} %bitcast.102), calls=%async_computation | async-start | bytes 8388608
  39.7 8.3 %slice-start.1 = ((s8[14680064]{0:T(1024)(128)(4,1)}), s8[4194304]{0:T(1024)(128)(4,1)S(1)}, s32[]{:S(2)}) async-start(s8[14680064]{0:T(1024)(128)(4,1)} %bitcast.102), calls=%async_computation.1 | async-start | bytes 8388608
  39.7 8.8 %slice-start.2 = ((s8[14680064]{0:T(1024)(128)(4,1)}), s8[4194304]{0:T(1024)(128)(4,1)S(1)}, s32[]{:S(2)}) async-start(s8[14680064]{0:T(1024)(128)(4,1)} %bitcast.102), calls=%async_computation.2 | async-start | bytes 8388608
  39.7 9.4 %slice-start.3 = ((s8[14680064]{0:T(1024)(128)(4,1)}), s8[2097152]{0:T(1024)(128)(4,1)S(1)}, s32[]{:S(2)}) async-start(s8[14680064]{0:T(1024)(128)(4,1)} %bitcast.102), calls=%async_computation.3 | async-start | bytes 4194304
  39.7 19.3 %collective-permute-start.12 = (bf16[40,2048]{1,0:T(8,128)(2,1)S(1)}, bf16[40,2048]{1,0:T(8,128)(2,1)S(1)}, u32[]{:S(2)}, u32[]{:S(2)}) collective-permute-start(bf16[40,2048]{1,0:T(8,128)(2,1)S(1)} %get-tuple-element.80), channel_id=1, source_target_pairs={{0,2},{1,3},{2,0},{3,1},{4,6},{5,7},{6,4},{7,5},{8,10},{9,11},{10,... | collective-permute-start | bytes 491528 | tf_op jit(solution)/shard_map/ppermute | solution.py:43
  52.0 3.6 %collective-permute-start.6 = (bf16[2,80,1792]{2,1,0:T(8,128)(2,1)S(1)}, bf16[2,80,1792]{2,1,0:T(8,128)(2,1)S(1)}, u32[]{:S(2)}, u32[]{:S(2)}) collective-permute-start(bf16[2,80,1792]{2,1,0:T(8,128)(2,1)S(1)} %pad_maximum_fusion.8), channel_id=1, source_target_pairs={{0,1},{1,0},{2,3},{3,2},{4,5},{5,4},{6,7},{7,6},{8,9},{9,8},{10,11... | collective-permute-start | bytes 1720328 | tf_op jit(solution)/shard_map/ppermute | solution.py:43
  55.0 2.4 %collective-permute-start.8 = (bf16[2,80,1792]{2,1,0:T(8,128)(2,1)S(1)}, bf16[2,80,1792]{2,1,0:T(8,128)(2,1)S(1)}, u32[]{:S(2)}, u32[]{:S(2)}) collective-permute-start(bf16[2,80,1792]{2,1,0:T(8,128)(2,1)S(1)} %pad_maximum_fusion.9), channel_id=1, source_target_pairs={{0,1},{1,0},{2,3},{3,2},{4,5},{5,4},{6,7},{7,6},{8,9},{9,8},{10,11... | collective-permute-start | bytes 1720328 | tf_op jit(solution)/shard_map/ppermute | solution.py:43
  55.8 9.8 %collective-permute-start.7 = (bf16[2,40,1792]{2,1,0:T(8,128)(2,1)S(1)}, bf16[2,40,1792]{2,1,0:T(8,128)(2,1)S(1)}, u32[]{:S(2)}, u32[]{:S(2)}) collective-permute-start(bf16[2,40,1792]{2,1,0:T(8,128)(2,1)S(1)} %pad_maximum_fusion.17), channel_id=1, source_target_pairs={{0,2},{1,3},{2,0},{3,1},{4,6},{5,7},{6,4},{7,5},{8,10},{9,11},{10,... | collective-permute-start | bytes 860168 | tf_op jit(solution)/shard_map/ppermute | solution.py:43
  57.6 19.6 %collective-permute-start.16 = (bf16[2,40,1792]{2,1,0:T(8,128)(2,1)S(1)}, bf16[2,40,1792]{2,1,0:T(8,128)(2,1)S(1)}, u32[]{:S(2)}, u32[]{:S(2)}) collective-permute-start(bf16[2,40,1792]{2,1,0:T(8,128)(2,1)S(1)} %pad_maximum_fusion.18), channel_id=1, source_target_pairs={{0,2},{1,3},{2,0},{3,1},{4,6},{5,7},{6,4},{7,5},{8,10},{9,11},{10,... | collective-permute-start | bytes 860168 | tf_op jit(solution)/shard_map/ppermute | solution.py:43
  59.1 6.6 %collective-permute-start.14 = (bf16[80,2048]{1,0:T(8,128)(2,1)S(1)}, bf16[80,2048]{1,0:T(8,128)(2,1)S(1)}, u32[]{:S(2)}, u32[]{:S(2)}) collective-permute-start(bf16[80,2048]{1,0:T(8,128)(2,1)S(1)} %pad_maximum_fusion.16), channel_id=1, source_target_pairs={{1,4},{3,6},{4,1},{6,3},{9,12},{11,14},{12,9},{14,11},{17,20},{19,... | collective-permute-start | bytes 983048 | tf_op jit(solution)/shard_map/ppermute | solution.py:107
  59.8 8.7 %collective-permute-start.13 = (bf16[80,2048]{1,0:T(8,128)(2,1)S(1)}, bf16[80,2048]{1,0:T(8,128)(2,1)S(1)}, u32[]{:S(2)}, u32[]{:S(2)}) collective-permute-start(bf16[80,2048]{1,0:T(8,128)(2,1)S(1)} %pad_maximum_fusion.16), channel_id=1, source_target_pairs={{0,4},{1,0},{2,6},{3,2},{4,5},{5,1},{6,7},{7,3},{8,12},{9,8},{10,1... | collective-permute-start | bytes 983048 | tf_op jit(solution)/shard_map/ppermute | solution.py:107
  74.4 4.3 %copy-start.3 = (f32[160,2304]{1,0:T(8,128)S(1)}, f32[160,2304]{1,0:T(8,128)}, u32[]{:S(2)}) copy-start(f32[160,2304]{1,0:T(8,128)} %fusion) | copy-start | bytes 4423684
  74.4 4.3 %collective-permute-start.15 = (bf16[2,80,2304]{2,1,0:T(8,128)(2,1)S(1)}, bf16[2,80,2304]{2,1,0:T(8,128)(2,1)S(1)}, u32[]{:S(2)}, u32[]{:S(2)}) collective-permute-start(bf16[2,80,2304]{2,1,0:T(8,128)(2,1)S(1)} %pad_maximum_fusion.5), channel_id=1, source_target_pairs={{0,1},{1,0},{2,3},{3,2},{4,5},{5,4},{6,7},{7,6},{8,9},{9,8},{10,11... | collective-permute-start | bytes 2211848 | tf_op jit(solution)/shard_map/ppermute | solution.py:43
  76.9 9.7 %collective-permute-start.9 = (bf16[40,1792]{1,0:T(8,128)(2,1)S(1)}, bf16[40,1792]{1,0:T(8,128)(2,1)S(1)}, u32[]{:S(2)}, u32[]{:S(2)}) collective-permute-start(bf16[40,1792]{1,0:T(8,128)(2,1)S(1)} %fusion.54), channel_id=1, source_target_pairs={{0,8},{4,12},{8,0},{12,4},{1,9},{5,13},{9,1},{13,5},{2,10},{6,14},... | collective-permute-start | bytes 430088 | tf_op jit(solution)/shard_map/ppermute | solution.py:43
  80.0 44.8 %slice-start.4 = ((s8[14680064]{0:T(1024)(128)(4,1)}), s8[2097152]{0:T(1024)(128)(4,1)S(1)}, s32[]{:S(2)}) async-start(s8[14680064]{0:T(1024)(128)(4,1)} %bitcast.104), calls=%async_computation.4 | async-start | bytes 4194304
  81.1 43.7 %slice-start.5 = ((s8[14680064]{0:T(1024)(128)(4,1)}), s8[4194304]{0:T(1024)(128)(4,1)S(1)}, s32[]{:S(2)}) async-start(s8[14680064]{0:T(1024)(128)(4,1)} %bitcast.104), calls=%async_computation.5 | async-start | bytes 8388608
  86.7 9.7 %collective-permute-start.21 = (bf16[2,80,1280]{2,1,0:T(8,128)(2,1)S(1)}, bf16[2,80,1280]{2,1,0:T(8,128)(2,1)S(1)}, u32[]{:S(2)}, u32[]{:S(2)}) collective-permute-start(bf16[2,80,1280]{2,1,0:T(8,128)(2,1)S(1)} %pad_maximum_fusion.12), channel_id=1, source_target_pairs={{0,1},{1,0},{2,3},{3,2},{4,5},{5,4},{6,7},{7,6},{8,9},{9,8},{10,11... | collective-permute-start | bytes 1228808 | tf_op jit(solution)/shard_map/ppermute | solution.py:43
  86.8 6.6 %collective-permute-start.17 = (bf16[40,1792]{1,0:T(8,128)(2,1)S(1)}, bf16[40,1792]{1,0:T(8,128)(2,1)S(1)}, u32[]{:S(2)}, u32[]{:S(2)}) collective-permute-start(bf16[40,1792]{1,0:T(8,128)(2,1)S(1)} %get-tuple-element.94), channel_id=1, source_target_pairs={{0,2},{1,3},{2,0},{3,1},{4,6},{5,7},{6,4},{7,5},{8,10},{9,11},{10,... | collective-permute-start | bytes 430088 | tf_op jit(solution)/shard_map/ppermute | solution.py:43
  87.8 13.6 %collective-permute-start.20 = (bf16[40,1792]{1,0:T(8,128)(2,1)S(1)}, bf16[40,1792]{1,0:T(8,128)(2,1)S(1)}, u32[]{:S(2)}, u32[]{:S(2)}) collective-permute-start(bf16[40,1792]{1,0:T(8,128)(2,1)S(1)} %fusion.52), channel_id=1, source_target_pairs={{0,8},{4,12},{8,0},{12,4},{1,9},{5,13},{9,1},{13,5},{2,10},{6,14},... | collective-permute-start | bytes 430088 | tf_op jit(solution)/shard_map/ppermute | solution.py:43
  87.8 13.5 %collective-permute-start.23 = (bf16[2,40,2304]{2,1,0:T(8,128)(2,1)S(1)}, bf16[2,40,2304]{2,1,0:T(8,128)(2,1)S(1)}, u32[]{:S(2)}, u32[]{:S(2)}) collective-permute-start(bf16[2,40,2304]{2,1,0:T(8,128)(2,1)S(1)} %pad_maximum_fusion.13), channel_id=1, source_target_pairs={{0,2},{1,3},{2,0},{3,1},{4,6},{5,7},{6,4},{7,5},{8,10},{9,11},{10,... | collective-permute-start | bytes 1105928 | tf_op jit(solution)/shard_map/ppermute | solution.py:43
  93.4 10.1 %collective-permute-start.19 = (bf16[80,1792]{1,0:T(8,128)(2,1)S(1)}, bf16[80,1792]{1,0:T(8,128)(2,1)S(1)}, u32[]{:S(2)}, u32[]{:S(2)}) collective-permute-start(bf16[80,1792]{1,0:T(8,128)(2,1)S(1)} %pad_maximum_fusion.19), channel_id=1, source_target_pairs={{1,4},{3,6},{4,1},{6,3},{9,12},{11,14},{12,9},{14,11},{17,20},{19,... | collective-permute-start | bytes 860168 | tf_op jit(solution)/shard_map/ppermute | solution.py:107
  94.1 9.4 %collective-permute-start.18 = (bf16[80,1792]{1,0:T(8,128)(2,1)S(1)}, bf16[80,1792]{1,0:T(8,128)(2,1)S(1)}, u32[]{:S(2)}, u32[]{:S(2)}) collective-permute-start(bf16[80,1792]{1,0:T(8,128)(2,1)S(1)} %pad_maximum_fusion.19), channel_id=1, source_target_pairs={{0,4},{1,0},{2,6},{3,2},{4,5},{5,1},{6,7},{7,3},{8,12},{9,8},{10,1... | collective-permute-start | bytes 860168 | tf_op jit(solution)/shard_map/ppermute | solution.py:107
  96.5 15.5 %collective-permute-start.25 = (bf16[2,40,1280]{2,1,0:T(8,128)(2,1)S(1)}, bf16[2,40,1280]{2,1,0:T(8,128)(2,1)S(1)}, u32[]{:S(2)}, u32[]{:S(2)}) collective-permute-start(bf16[2,40,1280]{2,1,0:T(8,128)(2,1)S(1)} %pad_maximum_fusion.21), channel_id=1, source_target_pairs={{0,2},{1,3},{2,0},{3,1},{4,6},{5,7},{6,4},{7,5},{8,10},{9,11},{10,... | collective-permute-start | bytes 614408 | tf_op jit(solution)/shard_map/ppermute | solution.py:43
  101.5 6.9 %collective-permute-start.22 = (bf16[40,1792]{1,0:T(8,128)(2,1)S(1)}, bf16[40,1792]{1,0:T(8,128)(2,1)S(1)}, u32[]{:S(2)}, u32[]{:S(2)}) collective-permute-start(bf16[40,1792]{1,0:T(8,128)(2,1)S(1)} %get-tuple-element.90), channel_id=1, source_target_pairs={{0,2},{1,3},{2,0},{3,1},{4,6},{5,7},{6,4},{7,5},{8,10},{9,11},{10,... | collective-permute-start | bytes 430088 | tf_op jit(solution)/shard_map/ppermute | solution.py:43
  102.5 11.1 %collective-permute-start.24 = (bf16[40,2304]{1,0:T(8,128)(2,1)S(1)}, bf16[40,2304]{1,0:T(8,128)(2,1)S(1)}, u32[]{:S(2)}, u32[]{:S(2)}) collective-permute-start(bf16[40,2304]{1,0:T(8,128)(2,1)S(1)} %fusion.46), channel_id=1, source_target_pairs={{0,8},{4,12},{8,0},{12,4},{1,9},{5,13},{9,1},{13,5},{2,10},{6,14},... | collective-permute-start | bytes 552968 | tf_op jit(solution)/shard_map/ppermute | solution.py:43
  103.7 21.1 %slice-start.6 = ((s8[14680064]{0:T(1024)(128)(4,1)}), s8[4194304]{0:T(1024)(128)(4,1)S(1)}, s32[]{:S(2)}) async-start(s8[14680064]{0:T(1024)(128)(4,1)} %bitcast.104), calls=%async_computation.6 | async-start | bytes 8388608
  103.7 21.1 %slice-start.7 = ((s8[14680064]{0:T(1024)(128)(4,1)}), s8[4194304]{0:T(1024)(128)(4,1)S(1)}, s32[]{:S(2)}) async-start(s8[14680064]{0:T(1024)(128)(4,1)} %bitcast.104), calls=%async_computation.7 | async-start | bytes 8388608
  108.4 16.3 %collective-permute-start.30 = (bf16[80,1792]{1,0:T(8,128)(2,1)S(1)}, bf16[80,1792]{1,0:T(8,128)(2,1)S(1)}, u32[]{:S(2)}, u32[]{:S(2)}) collective-permute-start(bf16[80,1792]{1,0:T(8,128)(2,1)S(1)} %pad_maximum_fusion.20), channel_id=1, source_target_pairs={{1,4},{3,6},{4,1},{6,3},{9,12},{11,14},{12,9},{14,11},{17,20},{19,... | collective-permute-start | bytes 860168 | tf_op jit(solution)/shard_map/ppermute | solution.py:107
  109.1 15.7 %collective-permute-start.29 = (bf16[80,1792]{1,0:T(8,128)(2,1)S(1)}, bf16[80,1792]{1,0:T(8,128)(2,1)S(1)}, u32[]{:S(2)}, u32[]{:S(2)}) collective-permute-start(bf16[80,1792]{1,0:T(8,128)(2,1)S(1)} %pad_maximum_fusion.20), channel_id=1, source_target_pairs={{0,4},{1,0},{2,6},{3,2},{4,5},{5,1},{6,7},{7,3},{8,12},{9,8},{10,1... | collective-permute-start | bytes 860168 | tf_op jit(solution)/shard_map/ppermute | solution.py:107
  112.1 7.8 %collective-permute-start.27 = (bf16[40,1280]{1,0:T(8,128)(2,1)S(1)}, bf16[40,1280]{1,0:T(8,128)(2,1)S(1)}, u32[]{:S(2)}, u32[]{:S(2)}) collective-permute-start(bf16[40,1280]{1,0:T(8,128)(2,1)S(1)} %fusion.60), channel_id=1, source_target_pairs={{0,8},{4,12},{8,0},{12,4},{1,9},{5,13},{9,1},{13,5},{2,10},{6,14},... | collective-permute-start | bytes 307208 | tf_op jit(solution)/shard_map/ppermute | solution.py:43
  113.6 7.5 %collective-permute-start.26 = (bf16[40,2304]{1,0:T(8,128)(2,1)S(1)}, bf16[40,2304]{1,0:T(8,128)(2,1)S(1)}, u32[]{:S(2)}, u32[]{:S(2)}) collective-permute-start(bf16[40,2304]{1,0:T(8,128)(2,1)S(1)} %get-tuple-element.72), channel_id=1, source_target_pairs={{0,2},{1,3},{2,0},{3,1},{4,6},{5,7},{6,4},{7,5},{8,10},{9,11},{10,... | collective-permute-start | bytes 552968 | tf_op jit(solution)/shard_map/ppermute | solution.py:43
  119.9 4.7 %collective-permute-start.28 = (bf16[40,1280]{1,0:T(8,128)(2,1)S(1)}, bf16[40,1280]{1,0:T(8,128)(2,1)S(1)}, u32[]{:S(2)}, u32[]{:S(2)}) collective-permute-start(bf16[40,1280]{1,0:T(8,128)(2,1)S(1)} %get-tuple-element.98), channel_id=1, source_target_pairs={{0,2},{1,3},{2,0},{3,1},{4,6},{5,7},{6,4},{7,5},{8,10},{9,11},{10,... | collective-permute-start | bytes 307208 | tf_op jit(solution)/shard_map/ppermute | solution.py:43
  126.3 9.3 %collective-permute-start.31 = (bf16[80,2048]{1,0:T(8,128)(2,1)S(1)}, bf16[80,2048]{1,0:T(8,128)(2,1)S(1)}, u32[]{:S(2)}, u32[]{:S(2)}) collective-permute-start(bf16[80,2048]{1,0:T(8,128)(2,1)S(1)} %slice.518), channel_id=1, source_target_pairs={{0,1},{1,0},{2,3},{3,2},{4,5},{5,4},{6,7},{7,6},{8,9},{9,8},{10,11... | collective-permute-start | bytes 983048 | tf_op jit(solution)/shard_map/ppermute | solution.py:43
  126.4 19.2 %collective-permute-start.34 = (bf16[80,2304]{1,0:T(8,128)(2,1)S(1)}, bf16[80,2304]{1,0:T(8,128)(2,1)S(1)}, u32[]{:S(2)}, u32[]{:S(2)}) collective-permute-start(bf16[80,2304]{1,0:T(8,128)(2,1)S(1)} %pad_maximum_fusion.14), channel_id=1, source_target_pairs={{1,4},{3,6},{4,1},{6,3},{9,12},{11,14},{12,9},{14,11},{17,20},{19,... | collective-permute-start | bytes 1105928 | tf_op jit(solution)/shard_map/ppermute | solution.py:107
  127.1 18.5 %collective-permute-start.33 = (bf16[80,2304]{1,0:T(8,128)(2,1)S(1)}, bf16[80,2304]{1,0:T(8,128)(2,1)S(1)}, u32[]{:S(2)}, u32[]{:S(2)}) collective-permute-start(bf16[80,2304]{1,0:T(8,128)(2,1)S(1)} %pad_maximum_fusion.14), channel_id=1, source_target_pairs={{0,4},{1,0},{2,6},{3,2},{4,5},{5,1},{6,7},{7,3},{8,12},{9,8},{10,1... | collective-permute-start | bytes 1105928 | tf_op jit(solution)/shard_map/ppermute | solution.py:107
  131.6 5.0 %collective-permute-start.36 = (bf16[80,1280]{1,0:T(8,128)(2,1)S(1)}, bf16[80,1280]{1,0:T(8,128)(2,1)S(1)}, u32[]{:S(2)}, u32[]{:S(2)}) collective-permute-start(bf16[80,1280]{1,0:T(8,128)(2,1)S(1)} %pad_maximum_fusion.22), channel_id=1, source_target_pairs={{1,4},{3,6},{4,1},{6,3},{9,12},{11,14},{12,9},{14,11},{17,20},{19,... | collective-permute-start | bytes 614408 | tf_op jit(solution)/shard_map/ppermute | solution.py:107
  132.3 12.0 %collective-permute-start.35 = (bf16[80,1280]{1,0:T(8,128)(2,1)S(1)}, bf16[80,1280]{1,0:T(8,128)(2,1)S(1)}, u32[]{:S(2)}, u32[]{:S(2)}) collective-permute-start(bf16[80,1280]{1,0:T(8,128)(2,1)S(1)} %pad_maximum_fusion.22), channel_id=1, source_target_pairs={{0,4},{1,0},{2,6},{3,2},{4,5},{5,1},{6,7},{7,3},{8,12},{9,8},{10,1... | collective-permute-start | bytes 614408 | tf_op jit(solution)/shard_map/ppermute | solution.py:107
  135.7 9.7 %collective-permute-start.32 = (bf16[80,2048]{1,0:T(8,128)(2,1)S(1)}, bf16[80,2048]{1,0:T(8,128)(2,1)S(1)}, u32[]{:S(2)}, u32[]{:S(2)}) collective-permute-start(bf16[80,2048]{1,0:T(8,128)(2,1)S(1)} %get-tuple-element.57), channel_id=1, source_target_pairs={{0,2},{1,3},{2,0},{3,1},{4,6},{5,7},{6,4},{7,5},{8,10},{9,11},{10,... | collective-permute-start | bytes 983048 | tf_op jit(solution)/shard_map/ppermute | solution.py:43
  147.5 2.2 %collective-permute-start.37 = (bf16[80,2048]{1,0:T(8,128)(2,1)S(1)}, bf16[80,2048]{1,0:T(8,128)(2,1)S(1)}, u32[]{:S(2)}, u32[]{:S(2)}) collective-permute-start(bf16[80,2048]{1,0:T(8,128)(2,1)S(1)} %slice.517), channel_id=1, source_target_pairs={{0,1},{1,0},{2,3},{3,2},{4,5},{5,4},{6,7},{7,6},{8,9},{9,8},{10,11... | collective-permute-start | bytes 983048 | tf_op jit(solution)/shard_map/ppermute | solution.py:43
  149.7 10.1 %collective-permute-start.38 = (bf16[80,2048]{1,0:T(8,128)(2,1)S(1)}, bf16[80,2048]{1,0:T(8,128)(2,1)S(1)}, u32[]{:S(2)}, u32[]{:S(2)}) collective-permute-start(bf16[80,2048]{1,0:T(8,128)(2,1)S(1)} %fusion.39), channel_id=1, source_target_pairs={{0,2},{1,3},{2,0},{3,1},{4,6},{5,7},{6,4},{7,5},{8,10},{9,11},{10,... | collective-permute-start | bytes 983048 | tf_op jit(solution)/shard_map/ppermute | solution.py:43
  160.9 2.2 %collective-permute-start.39 = (bf16[160,2048]{1,0:T(8,128)(2,1)S(1)}, bf16[160,2048]{1,0:T(8,128)(2,1)S(1)}, u32[]{:S(2)}, u32[]{:S(2)}) collective-permute-start(bf16[160,2048]{1,0:T(8,128)(2,1)S(1)} %select_convert_fusion), channel_id=1, source_target_pairs={{0,1},{1,0},{2,3},{3,2},{4,5},{5,4},{6,7},{7,6},{8,9},{9,8},{10,11... | collective-permute-start | bytes 1966088 | tf_op jit(solution)/shard_map/ppermute | solution.py:43

commit v11 on v10

--- a/solution.py
+++ b/solution.py
@@ -8,26 +8,29 @@
 HALVES = 2
 PARTS = ((14, 14), (18, 10))
 EDGES = {
-    "g.pull": ["t0.add"],
-    "t0.halves": ["g.pull"],
     "u.pull": ["t0.columns"],
     "t0.cores": ["u.pull"],
-    "t1.pick": ["t0.add"],
     "t1.add": ["t0.halves"],
-    "t1.halves": ["t0.columns"],
+    "t1.halves": ["t0.cores"],
     "c01.dots": ["c00.dots"],
     "c00.sum": ["c01.dots"],
     "t1.columns": ["c01.sum"],
     "c00.hidden": ["c01.sum"],
     "t1.cores": ["c00.hidden"],
-    "c01.hidden": ["c10.dots"],
+    "c11.dots": ["c10.dots"],
+    "c01.hidden": ["c11.dots"],
     "c10.sum": ["c01.hidden"],
-    "c11.dots": ["c10.sum"],
     "c00.halves": ["c10.sum"],
-    "c10.hidden": ["c11.sum"],
+    "c11.sum": ["c00.halves"],
     "c01.halves": ["c11.sum"],
+    "c00.columns": ["c01.halves"],
+    "c10.hidden": ["c00.columns"],
+    "c01.columns": ["c10.hidden"],
+    "c11.hidden": ["c01.columns"],
     "c10.halves": ["c11.hidden"],
-    "c01.cores": ["c10.columns", "c11.columns"],
+    "c00.cores": ["c10.halves"],
+    "c11.halves": ["c00.cores"],
+    "c01.cores": ["c10.columns"],
     "c00.down": ["c01.cores"],
     "c10.cores": ["b0.all"],
     "c11.cores": ["b0.total"],
@@ -82,13 +85,12 @@
             ends.append(ends[-1] + units * size // sum(sizes))
         spans.append(list(zip(ends[:-1], ends[1:])))
 
-    rows = jnp.arange(lengths.shape[0], dtype=jnp.int32)
-    slot = jnp.arange(slots, dtype=jnp.int32)
-    places = []
-    for row in (c, c ^ 1):
-        first = jnp.sum(jnp.where(rows < row, lengths, 0))
-        count = jnp.sum(jnp.where(rows == row, lengths, 0))
-        places.append(jnp.where(slot < count, slot + first, -1))
+    rows = jnp.arange(lengths.shape[0], dtype=jnp.int32)[None]
+    slot = jnp.arange(slots, dtype=jnp.int32)[None]
+    here = (c ^ jnp.arange(2, dtype=jnp.int32))[:, None]
+    first = jnp.sum(jnp.where(rows < here, lengths[None], 0), axis=1, keepdims=True)
+    count = jnp.sum(jnp.where(rows == here, lengths[None], 0), axis=1, keepdims=True)
+    places = jnp.where(slot < count, slot + first, -1)
     inside = jnp.arange(piece, dtype=jnp.int32)
     mine = [
         jnp.concatenate([inside + quarter * c, inside + quarter * (c ^ 2)]) + h * piece
@@ -155,15 +157,17 @@
         yield
         return issued(name + ".cores", finish(ordered(name + ".cores", pair)))
 
-    def pick_steps(name, h):
-        own = mine[h][:, None] == places[0][None]
-        sib = mine[h][:, None] == places[1][None]
-        rows = dot(own.astype(jnp.bfloat16), tokens)
-        rows = rows + dot(ordered(name + ".pick", sib).astype(jnp.bfloat16), sibling)
-        rows = issued(name + ".pick", rows.astype(jnp.bfloat16))
-        got = swap_x(rows[piece:])
-        yield
-        return issued(name + ".add", ordered(name + ".add", rows[:piece]) + got)
+    picked = {}
+
+    def pick_steps():
+        own = jnp.concatenate(mine)[:, None] == places[0][None]
+        sib = jnp.concatenate(mine)[:, None] == places[1][None]
+        rows = dot(own.astype(jnp.bfloat16), tokens) + dot(sib.astype(jnp.bfloat16), sibling)
+        rows = rows.astype(jnp.bfloat16).reshape(HALVES, 2, piece, width)
+        picked["got"] = swap_x(rows[:, 1])
+        picked["rows"] = rows[:, 0]
+        return None
+        yield
 
     pulled = {}
 
@@ -173,16 +177,15 @@
         yield
 
     def half_steps(name, h):
-        own = yield from pick_steps(name, h)
+        own = issued(name + ".add", ordered(name + ".add", picked["rows"][h]) + picked["got"][h])
         return (yield from spread_steps(name, own))
 
     def chunk_steps(name, h, i):
         full = result("t" + str(h))
         part = slice(*spans[h][i])
         full = ordered(name + ".dots", full)
-        result("g")
         result("u")
-        gate, up = dot(full, pulled["g"][:, part]), dot(full, pulled["u"][:, part])
+        gate, up = dot(full, gate_weight[:, part]), dot(full, pulled["u"][:, part])
         send = issued(name + ".dots", jnp.stack([gate[half:], up[half:]]).astype(jnp.bfloat16))
         got = issued(name + ".cores_swapped", flip(send, "col", 1))
         yield
@@ -209,7 +212,7 @@
         got = ordered(name + ".all", got)
         return issued(name + ".all", total + jnp.concatenate([got[piece:], got[:piece]], axis=0))
 
-    chains = {"g": pull_steps("g", gate_weight), "u": pull_steps("u", up_weight)}
+    chains = {"p": pick_steps(), "u": pull_steps("u", up_weight)}
     results = {}
     for h in range(HALVES):
         chains["t" + str(h)] = half_steps("t" + str(h), h)
@@ -228,6 +231,7 @@
             advance(name)
         return results[name]
 
+    result("p")
     for h in range(HALVES):
         result("b" + str(h))
 

time: 165 us -> 167 us (1.012)
  starting transfers between devices: 51.5 us -> 61.8 us
  Pallas kernels: 12.2 us -> 5.99 us
  local copies, waits for them, and re-layouts: 8.03 us -> 2.71 us
  waiting for transfers between devices: 59.4 us -> 64.4 us
  other arithmetic: 6.94 us -> 3.77 us
    ppermute x28 -> x27, waiting for transfers between devices: 48.9 us -> 61.3 us  [flip(): return lax.ppermute(value, axis, [(i, i ^ bit) for i in range(count)])]
    ppermute x28 -> x27, starting transfers between devices: 28.3 us -> 39.9 us  [flip(): return lax.ppermute(value, axis, [(i, i ^ bit) for i in range(count)])]
    ppermute x12, waiting for transfers between devices: 10.5 us -> 3.07 us  [move(): return lax.ppermute(value, ('row', 'col'), pairs)]
    pallas_call x2 -> x1, Pallas kernels: 12.2 us -> 5.99 us  [pull(): pl.pallas_call(pull_kernel, in_specs=[pl.BlockSpec(memory_space=pltpu.SME...]
    unnamed x24 -> x20, local copies, waits for them, and re-layouts: 6.36 us -> 2.15 us
    select_n x1, other arithmetic: 2.52 us -> 0.08 us  [stationary(): places = jnp.where(slot < count, slot + first, -1)]
    dot_general x16 -> x14, matrix products: 23.2 us -> 24.7 us  [dot(): return jnp.dot(a, b, preferred_element_type=jnp.float32)]
  transfers between devices with their start and end apart: 40 -> 39, of which waited for: 15 -> 17; matrix products, arithmetic and copies ran while one was open for 17% -> 16% of each run, Pallas kernels for 7% -> 4%
where the time goes in v11:
time: 167 us
  waiting for transfers between devices  64.4 us (39%)
  starting transfers between devices  61.8 us (37%)
  matrix products  27.4 us (16%)
  Pallas kernels  5.99 us (4%)
  other arithmetic  3.77 us (2%)
  local copies, waits for them, and re-layouts  2.71 us (2%)
    ppermute x27, waiting for transfers between devices, flip(): return lax.ppermute(value, axis, [(i, i ^ bit) for i in range(count)])  61.3 us
    ppermute x27, starting transfers between devices, flip(): return lax.ppermute(value, axis, [(i, i ^ bit) for i in range(count)])  39.9 us
    dot_general x14, matrix products, dot(): return jnp.dot(a, b, preferred_element_type=jnp.float32)  24.7 us
    ppermute x12, starting transfers between devices, move(): return lax.ppermute(value, ('row', 'col'), pairs)  21.9 us
    pallas_call x1, Pallas kernels, pull(): pl.pallas_call(pull_kernel, in_specs=[pl.BlockSpec(memory_space=pltpu.SME...  5.99 us
  transfers between devices with their start and end apart: 39, of which 17 were waited for; matrix products, arithmetic and copies ran while one was open for 16% of the time, Pallas kernels for 4%

profile of v11, /device:TPU:0, one launch (start us, length us, event | category | flops | bytes accessed | tf_op | source)
XLA Modules:
  0.0 166.9 jit_solution(13669489600018871138)
XLA Ops:
  0.5 0.9 fusion.81
  1.6 1.5 fusion.65
  3.5 2.6 %collective-permute-start.1 = (bf16[2,40,2048]{2,1,0:T(8,128)(2,1)S(1)}, bf16[2,40,2048]{2,1,0:T(8,128)(2,1)S(1)}, u32[]{:S(2)}, u32[]{:S(2)}) collective-permute-start(bf16[2,40,2048]{2,1,0:T(8,128)(2,1)S(1)} %slice_bitcast_fusion), channel_id=1, source_target_pairs={{0,2},{1,3},{2,0},{3,1},{4,6},{5,7},{6,4},{7,5},{8,10},{9,11},{10,... | collective-permute-start | bytes 983048 | tf_op jit(solution)/shard_map/ppermute | solution.py:46
  6.0 8.4 %collective-permute-done.1 = bf16[2,40,2048]{2,1,0:T(8,128)(2,1)S(1)} collective-permute-done((bf16[2,40,2048]{2,1,0:T(8,128)(2,1)S(1)}, bf16[2,40,2048]{2,1,0:T(8,128)(2,1)S(1)}, u32[]{:S(2)}, u32[]{:S(2)}) %collective-permute-start.1) | collective-permute-done | bytes 327712 | tf_op jit(solution)/shard_map/ppermute | solution.py:46
  14.4 2.9 %collective-permute-start.2 = (bf16[40,2048]{1,0:T(8,128)(2,1)S(1)}, bf16[40,2048]{1,0:T(8,128)(2,1)S(1)}, u32[]{:S(2)}, u32[]{:S(2)}) collective-permute-start(bf16[40,2048]{1,0:T(8,128)(2,1)S(1)} %fusion.63), channel_id=1, source_target_pairs={{0,8},{4,12},{8,0},{12,4},{1,9},{5,13},{9,1},{13,5},{2,10},{6,14},... | collective-permute-start | bytes 491528 | tf_op jit(solution)/shard_map/ppermute | solution.py:46
  17.3 7.6 %collective-permute-done.2 = bf16[40,2048]{1,0:T(8,128)(2,1)S(1)} collective-permute-done((bf16[40,2048]{1,0:T(8,128)(2,1)S(1)}, bf16[40,2048]{1,0:T(8,128)(2,1)S(1)}, u32[]{:S(2)}, u32[]{:S(2)}) %collective-permute-start.2) | collective-permute-done | bytes 163872 | tf_op jit(solution)/shard_map/ppermute | solution.py:46
  24.9 1.6 collective-permute-start.3
  26.6 3.8 %collective-permute-done.3 = bf16[40,2048]{1,0:T(8,128)(2,1)S(1)} collective-permute-done((bf16[40,2048]{1,0:T(8,128)(2,1)S(1)}, bf16[40,2048]{1,0:T(8,128)(2,1)S(1)}, u32[]{:S(2)}, u32[]{:S(2)}) %collective-permute-start.3) | collective-permute-done | bytes 163872 | tf_op jit(solution)/shard_map/ppermute | solution.py:46
  30.4 0.7 collective-permute-start.5
  31.0 2.8 %collective-permute-start.4 = (bf16[80,2048]{1,0:T(8,128)(2,1)S(1)}, bf16[80,2048]{1,0:T(8,128)(2,1)S(1)}, u32[]{:S(2)}, u32[]{:S(2)}) collective-permute-start(bf16[80,2048]{1,0:T(8,128)(2,1)S(1)} %pad_maximum_fusion.15), channel_id=1, source_target_pairs={{0,4},{1,0},{2,6},{3,2},{4,5},{5,1},{6,7},{7,3},{8,12},{9,8},{10,1... | collective-permute-start | bytes 983048 | tf_op jit(solution)/shard_map/ppermute | solution.py:109
  33.9 3.4 %collective-permute-start.10 = (bf16[40,2048]{1,0:T(8,128)(2,1)S(1)}, bf16[40,2048]{1,0:T(8,128)(2,1)S(1)}, u32[]{:S(2)}, u32[]{:S(2)}) collective-permute-start(bf16[40,2048]{1,0:T(8,128)(2,1)S(1)} %fusion.62), channel_id=1, source_target_pairs={{0,8},{4,12},{8,0},{12,4},{1,9},{5,13},{9,1},{13,5},{2,10},{6,14},... | collective-permute-start | bytes 491528 | tf_op jit(solution)/shard_map/ppermute | solution.py:46
  37.3 6.0 %shard_map.55 = bf16[2048,3584]{1,0:T(8,128)(2,1)S(1)} custom-call(s32[4]{0:T(128)S(1)} %copy-done, bf16[2048,3584]{1,0:T(8,128)(2,1)} %weight_ref.1), custom_call_target="tpu_custom_call" | custom-call | tf_op jit(solution)/shard_map/pallas_call | solution.py:57
  43.5 1.4 fusion.8
  45.0 1.2 slice-done.2
  46.2 0.8 slice-done.3
  47.0 1.4 fusion.16
  49.0 1.3 fusion.6
  50.4 1.4 fusion.14
  51.8 1.6 collective-permute-start.11
  54.4 1.1 collective-permute-done.8
  56.3 2.6 %collective-permute-done.11 = bf16[40,2048]{1,0:T(8,128)(2,1)S(1)} collective-permute-done((bf16[40,2048]{1,0:T(8,128)(2,1)S(1)}, bf16[40,2048]{1,0:T(8,128)(2,1)S(1)}, u32[]{:S(2)}, u32[]{:S(2)}) %collective-permute-start.11) | collective-permute-done | bytes 163872 | tf_op jit(solution)/shard_map/ppermute | solution.py:46
  58.9 0.7 collective-permute-start.13
  59.6 2.6 %collective-permute-start.12 = (bf16[80,2048]{1,0:T(8,128)(2,1)S(1)}, bf16[80,2048]{1,0:T(8,128)(2,1)S(1)}, u32[]{:S(2)}, u32[]{:S(2)}) collective-permute-start(bf16[80,2048]{1,0:T(8,128)(2,1)S(1)} %pad_maximum_fusion.16), channel_id=1, source_target_pairs={{0,4},{1,0},{2,6},{3,2},{4,5},{5,1},{6,7},{7,3},{8,12},{9,8},{10,1... | collective-permute-start | bytes 983048 | tf_op jit(solution)/shard_map/ppermute | solution.py:109
  62.2 2.8 %collective-permute-done.7 = bf16[2,40,1792]{2,1,0:T(8,128)(2,1)S(1)} collective-permute-done((bf16[2,40,1792]{2,1,0:T(8,128)(2,1)S(1)}, bf16[2,40,1792]{2,1,0:T(8,128)(2,1)S(1)}, u32[]{:S(2)}, u32[]{:S(2)}) %collective-permute-start.7) | collective-permute-done | bytes 286752 | tf_op jit(solution)/shard_map/ppermute | solution.py:46
  65.2 2.5 %collective-permute-start.9 = (bf16[40,1792]{1,0:T(8,128)(2,1)S(1)}, bf16[40,1792]{1,0:T(8,128)(2,1)S(1)}, u32[]{:S(2)}, u32[]{:S(2)}) collective-permute-start(bf16[40,1792]{1,0:T(8,128)(2,1)S(1)} %fusion.53), channel_id=1, source_target_pairs={{0,8},{4,12},{8,0},{12,4},{1,9},{5,13},{9,1},{13,5},{2,10},{6,14},... | collective-permute-start | bytes 430088 | tf_op jit(solution)/shard_map/ppermute | solution.py:46
  67.7 2.7 %collective-permute-done.12 = bf16[80,2048]{1,0:T(8,128)(2,1)S(1)} collective-permute-done((bf16[80,2048]{1,0:T(8,128)(2,1)S(1)}, bf16[80,2048]{1,0:T(8,128)(2,1)S(1)}, u32[]{:S(2)}, u32[]{:S(2)}) %collective-permute-start.12) | collective-permute-done | bytes 327712 | tf_op jit(solution)/shard_map/ppermute | solution.py:109
  70.4 5.4 %fusion.4 = f32[160,2304]{1,0:T(8,128)S(1)} fusion(bf16[2048,3584]{1,0:T(8,128)(2,1)} %param.7, bf16[80,2048]{1,0:T(8,128)(2,1)S(1)} %get-tuple-element.80, bf16[80,2048]{1,0:T(8,128)(2,1)S(1)} %get-tuple-element.79), kind=kOutput, calls=%fused_computation.4 | convolution fusion | flops 1511260160 | bytes 11567104 | tf_op jit(solution)/shard_map/dot_general | solution.py:41
  75.8 1.7 %fusion = f32[160,2304]{1,0:T(8,128)S(1)} fusion(bf16[2048,3584]{1,0:T(8,128)(2,1)S(1)} %shard_map.55, bf16[80,2048]{1,0:T(8,128)(2,1)S(1)} %get-tuple-element.80, bf16[80,2048]{1,0:T(8,128)(2,1)S(1)} %get-tuple-element.79), kind=kOutput, calls=%fused_computation | convolution fusion | flops 1511260160 | bytes 11567104 | tf_op jit(solution)/shard_map/dot_general | solution.py:41
  77.7 1.0 fusion.18
  78.8 3.7 %fusion.22 = f32[160,1280]{1,0:T(8,128)S(1)} fusion(bf16[160,2048]{1,0:T(8,128)(2,1)S(1)} %pad_maximum_fusion.7, bf16[2048,3584]{1,0:T(8,128)(2,1)} %param.7), kind=kOutput, calls=%fused_computation.22 | convolution fusion | flops 838860800 | bytes 6717440 | tf_op jit(solution)/shard_map/dot_general | solution.py:41
  82.4 3.2 %collective-permute-start.14 = (bf16[2,80,2304]{2,1,0:T(8,128)(2,1)S(1)}, bf16[2,80,2304]{2,1,0:T(8,128)(2,1)S(1)}, u32[]{:S(2)}, u32[]{:S(2)}) collective-permute-start(bf16[2,80,2304]{2,1,0:T(8,128)(2,1)S(1)} %pad_maximum_fusion.5), channel_id=1, source_target_pairs={{0,1},{1,0},{2,3},{3,2},{4,5},{5,4},{6,7},{7,6},{8,9},{9,8},{10,11... | collective-permute-start | bytes 2211848 | tf_op jit(solution)/shard_map/ppermute | solution.py:46
  85.9 2.5 %collective-permute-start.17 = (bf16[40,1792]{1,0:T(8,128)(2,1)S(1)}, bf16[40,1792]{1,0:T(8,128)(2,1)S(1)}, u32[]{:S(2)}, u32[]{:S(2)}) collective-permute-start(bf16[40,1792]{1,0:T(8,128)(2,1)S(1)} %fusion.51), channel_id=1, source_target_pairs={{0,8},{4,12},{8,0},{12,4},{1,9},{5,13},{9,1},{13,5},{2,10},{6,14},... | collective-permute-start | bytes 430088 | tf_op jit(solution)/shard_map/ppermute | solution.py:46
  88.7 1.6 collective-permute-start.19
  91.1 1.6 collective-permute-start.21
  92.6 3.5 %collective-permute-done.17 = bf16[40,1792]{1,0:T(8,128)(2,1)S(1)} collective-permute-done((bf16[40,1792]{1,0:T(8,128)(2,1)S(1)}, bf16[40,1792]{1,0:T(8,128)(2,1)S(1)}, u32[]{:S(2)}, u32[]{:S(2)}) %collective-permute-start.17) | collective-permute-done | bytes 143392 | tf_op jit(solution)/shard_map/ppermute | solution.py:46
  96.1 1.6 collective-permute-start.22
  97.7 5.6 %collective-permute-done.16 = bf16[40,1792]{1,0:T(8,128)(2,1)S(1)} collective-permute-done((bf16[40,1792]{1,0:T(8,128)(2,1)S(1)}, bf16[40,1792]{1,0:T(8,128)(2,1)S(1)}, u32[]{:S(2)}, u32[]{:S(2)}) %collective-permute-start.16) | collective-permute-done | bytes 143392 | tf_op jit(solution)/shard_map/ppermute | solution.py:46
  103.3 0.7 collective-permute-start.24
  104.0 3.2 %collective-permute-start.23 = (bf16[80,1792]{1,0:T(8,128)(2,1)S(1)}, bf16[80,1792]{1,0:T(8,128)(2,1)S(1)}, u32[]{:S(2)}, u32[]{:S(2)}) collective-permute-start(bf16[80,1792]{1,0:T(8,128)(2,1)S(1)} %pad_maximum_fusion.19), channel_id=1, source_target_pairs={{0,4},{1,0},{2,6},{3,2},{4,5},{5,1},{6,7},{7,3},{8,12},{9,8},{10,1... | collective-permute-start | bytes 860168 | tf_op jit(solution)/shard_map/ppermute | solution.py:109
  107.3 1.3 collective-permute-start.20
  108.7 1.3 collective-permute-done.22
  110.0 0.7 collective-permute-start.27
  110.7 2.7 %collective-permute-start.26 = (bf16[80,1792]{1,0:T(8,128)(2,1)S(1)}, bf16[80,1792]{1,0:T(8,128)(2,1)S(1)}, u32[]{:S(2)}, u32[]{:S(2)}) collective-permute-start(bf16[80,1792]{1,0:T(8,128)(2,1)S(1)} %pad_maximum_fusion.20), channel_id=1, source_target_pairs={{0,4},{1,0},{2,6},{3,2},{4,5},{5,1},{6,7},{7,3},{8,12},{9,8},{10,1... | collective-permute-start | bytes 860168 | tf_op jit(solution)/shard_map/ppermute | solution.py:109
  113.5 4.8 %collective-permute-done.20 = bf16[40,2304]{1,0:T(8,128)(2,1)S(1)} collective-permute-done((bf16[40,2304]{1,0:T(8,128)(2,1)S(1)}, bf16[40,2304]{1,0:T(8,128)(2,1)S(1)}, u32[]{:S(2)}, u32[]{:S(2)}) %collective-permute-start.20) | collective-permute-done | bytes 184352 | tf_op jit(solution)/shard_map/ppermute | solution.py:46
  118.3 3.4 %collective-permute-start.32 = (bf16[40,1280]{1,0:T(8,128)(2,1)S(1)}, bf16[40,1280]{1,0:T(8,128)(2,1)S(1)}, u32[]{:S(2)}, u32[]{:S(2)}) collective-permute-start(bf16[40,1280]{1,0:T(8,128)(2,1)S(1)} %fusion.59), channel_id=1, source_target_pairs={{0,8},{4,12},{8,0},{12,4},{1,9},{5,13},{9,1},{13,5},{2,10},{6,14},... | collective-permute-start | bytes 307208 | tf_op jit(solution)/shard_map/ppermute | solution.py:46
  121.7 1.6 collective-permute-start.25
  123.4 2.6 %collective-permute-done.32 = bf16[40,1280]{1,0:T(8,128)(2,1)S(1)} collective-permute-done((bf16[40,1280]{1,0:T(8,128)(2,1)S(1)}, bf16[40,1280]{1,0:T(8,128)(2,1)S(1)}, u32[]{:S(2)}, u32[]{:S(2)}) %collective-permute-start.32) | collective-permute-done | bytes 102432 | tf_op jit(solution)/shard_map/ppermute | solution.py:46
  126.0 1.6 collective-permute-start.33
  127.6 1.4 fusion.12
  129.1 1.4 fusion.25
  130.8 0.7 collective-permute-start.35
  131.5 3.4 %collective-permute-start.34 = (bf16[80,1280]{1,0:T(8,128)(2,1)S(1)}, bf16[80,1280]{1,0:T(8,128)(2,1)S(1)}, u32[]{:S(2)}, u32[]{:S(2)}) collective-permute-start(bf16[80,1280]{1,0:T(8,128)(2,1)S(1)} %pad_maximum_fusion.22), channel_id=1, source_target_pairs={{0,4},{1,0},{2,6},{3,2},{4,5},{5,1},{6,7},{7,3},{8,12},{9,8},{10,1... | collective-permute-start | bytes 614408 | tf_op jit(solution)/shard_map/ppermute | solution.py:109
  135.5 3.2 %collective-permute-start.30 = (bf16[80,2304]{1,0:T(8,128)(2,1)S(1)}, bf16[80,2304]{1,0:T(8,128)(2,1)S(1)}, u32[]{:S(2)}, u32[]{:S(2)}) collective-permute-start(bf16[80,2304]{1,0:T(8,128)(2,1)S(1)} %pad_maximum_fusion.14), channel_id=1, source_target_pairs={{0,4},{1,0},{2,6},{3,2},{4,5},{5,1},{6,7},{7,3},{8,12},{9,8},{10,1... | collective-permute-start | bytes 1105928 | tf_op jit(solution)/shard_map/ppermute | solution.py:109
  138.8 1.6 collective-permute-start.29
  140.4 1.0 fusion.20
  141.5 5.5 %collective-permute-done.29 = bf16[80,2048]{1,0:T(8,128)(2,1)S(1)} collective-permute-done((bf16[80,2048]{1,0:T(8,128)(2,1)S(1)}, bf16[80,2048]{1,0:T(8,128)(2,1)S(1)}, u32[]{:S(2)}, u32[]{:S(2)}) %collective-permute-start.29) | collective-permute-done | bytes 327712 | tf_op jit(solution)/shard_map/ppermute | solution.py:46
  147.6 1.8 %fusion.28 = f32[160,2048]{1,0:T(8,128)S(1)} fusion(f32[160,2048]{1,0:T(8,128)S(1)} %fusion.20, bf16[3584,2048]{1,0:T(8,128)(2,1)S(1)} %bitcast.124, bf16[80,2304]{1,0:T(8,128)(2,1)S(1)} %get-tuple-element.72, bf16[80,2304]{1,0:T(8,128)(2,1)S(1)} %get-tuple-element.71), kind=kOutput, calls=%fused_computation.28 | convolution fusion | flops 1511751680 | bytes 12795904 | tf_op jit(solution)/shard_map/dot_general | solution.py:41
  149.4 1.0 collective-permute-start.36
  150.4 1.3 collective-permute-done.36
  151.7 1.5 collective-permute-start.37
  153.5 8.3 %collective-permute-done.37 = bf16[80,2048]{1,0:T(8,128)(2,1)S(1)} collective-permute-done((bf16[80,2048]{1,0:T(8,128)(2,1)S(1)}, bf16[80,2048]{1,0:T(8,128)(2,1)S(1)}, u32[]{:S(2)}, u32[]{:S(2)}) %collective-permute-start.37) | collective-permute-done | bytes 327712 | tf_op jit(solution)/shard_map/ppermute | solution.py:46
  161.9 0.9 select_convert_fusion
  162.9 2.1 %collective-permute-done.38 = bf16[160,2048]{1,0:T(8,128)(2,1)S(1)} collective-permute-done((bf16[160,2048]{1,0:T(8,128)(2,1)S(1)}, bf16[160,2048]{1,0:T(8,128)(2,1)S(1)}, u32[]{:S(2)}, u32[]{:S(2)}) %collective-permute-start.38) | collective-permute-done | bytes 655392 | tf_op jit(solution)/shard_map/ppermute | solution.py:46
  165.0 1.9 %fusion.33 = bf16[160,2048]{1,0:T(8,128)(2,1)} fusion(bf16[160,2048]{1,0:T(8,128)(2,1)S(1)} %collective-permute-done.38, bf16[160,2048]{1,0:T(8,128)(2,1)S(1)} %copy-done.1, f32[80,2048]{1,0:T(8,128)S(1)} %convert_add_fusion, f32[80,2048]{1,0:T(8,128)S(1)} %convert_add_fusion.1, pred[160]{0:T(512)(128)(4,1)S(1)} %get-tuple-element.57, ...), kind=kOutput, calls=%fused_computation.33 | convolution fusion | flops 631137280 | bytes 3278240 | tf_op jit(solution)/shard_map/dot_general | solution.py:242
  (126 shorter events, 8.2 us)
Async XLA Ops:
  0.0 3.0 %collective-permute-start = (bf16[160,2048]{1,0:T(8,128)(2,1)}, bf16[160,2048]{1,0:T(8,128)(2,1)S(1)}, u32[]{:S(2)}, u32[]{:S(2)}) collective-permute-start(bf16[160,2048]{1,0:T(8,128)(2,1)} %param.5), channel_id=1, source_target_pairs={{0,1},{1,0},{2,3},{3,2},{4,5},{5,4},{6,7},{7,6},{8,9},{9,8},{10,11... | collective-permute-start | bytes 1966088 | tf_op jit(solution)/shard_map/ppermute | solution.py:46
  3.5 33.9 %copy-start = (s32[4]{0:T(128)S(1)}, s32[4]{0:T(128)}, u32[]{:S(2)}) copy-start(s32[4]{0:T(128)} %tick_ref) | copy-start | bytes 52
  3.5 10.9 %collective-permute-start.1 = (bf16[2,40,2048]{2,1,0:T(8,128)(2,1)S(1)}, bf16[2,40,2048]{2,1,0:T(8,128)(2,1)S(1)}, u32[]{:S(2)}, u32[]{:S(2)}) collective-permute-start(bf16[2,40,2048]{2,1,0:T(8,128)(2,1)S(1)} %slice_bitcast_fusion), channel_id=1, source_target_pairs={{0,2},{1,3},{2,0},{3,1},{4,6},{5,7},{6,4},{7,5},{8,10},{9,11},{10,... | collective-permute-start | bytes 983048 | tf_op jit(solution)/shard_map/ppermute | solution.py:46
  14.4 10.5 %collective-permute-start.2 = (bf16[40,2048]{1,0:T(8,128)(2,1)S(1)}, bf16[40,2048]{1,0:T(8,128)(2,1)S(1)}, u32[]{:S(2)}, u32[]{:S(2)}) collective-permute-start(bf16[40,2048]{1,0:T(8,128)(2,1)S(1)} %fusion.63), channel_id=1, source_target_pairs={{0,8},{4,12},{8,0},{12,4},{1,9},{5,13},{9,1},{13,5},{2,10},{6,14},... | collective-permute-start | bytes 491528 | tf_op jit(solution)/shard_map/ppermute | solution.py:46
  24.9 5.4 %collective-permute-start.3 = (bf16[40,2048]{1,0:T(8,128)(2,1)S(1)}, bf16[40,2048]{1,0:T(8,128)(2,1)S(1)}, u32[]{:S(2)}, u32[]{:S(2)}) collective-permute-start(bf16[40,2048]{1,0:T(8,128)(2,1)S(1)} %get-tuple-element.86), channel_id=1, source_target_pairs={{0,2},{1,3},{2,0},{3,1},{4,6},{5,7},{6,4},{7,5},{8,10},{9,11},{10,... | collective-permute-start | bytes 491528 | tf_op jit(solution)/shard_map/ppermute | solution.py:46
  30.4 13.0 %collective-permute-start.5 = (bf16[80,2048]{1,0:T(8,128)(2,1)S(1)}, bf16[80,2048]{1,0:T(8,128)(2,1)S(1)}, u32[]{:S(2)}, u32[]{:S(2)}) collective-permute-start(bf16[80,2048]{1,0:T(8,128)(2,1)S(1)} %pad_maximum_fusion.15), channel_id=1, source_target_pairs={{1,4},{3,6},{4,1},{6,3},{9,12},{11,14},{12,9},{14,11},{17,20},{19,... | collective-permute-start | bytes 983048 | tf_op jit(solution)/shard_map/ppermute | solution.py:109
  31.0 12.3 %collective-permute-start.4 = (bf16[80,2048]{1,0:T(8,128)(2,1)S(1)}, bf16[80,2048]{1,0:T(8,128)(2,1)S(1)}, u32[]{:S(2)}, u32[]{:S(2)}) collective-permute-start(bf16[80,2048]{1,0:T(8,128)(2,1)S(1)} %pad_maximum_fusion.15), channel_id=1, source_target_pairs={{0,4},{1,0},{2,6},{3,2},{4,5},{5,1},{6,7},{7,3},{8,12},{9,8},{10,1... | collective-permute-start | bytes 983048 | tf_op jit(solution)/shard_map/ppermute | solution.py:109
  33.9 17.9 %collective-permute-start.10 = (bf16[40,2048]{1,0:T(8,128)(2,1)S(1)}, bf16[40,2048]{1,0:T(8,128)(2,1)S(1)}, u32[]{:S(2)}, u32[]{:S(2)}) collective-permute-start(bf16[40,2048]{1,0:T(8,128)(2,1)S(1)} %fusion.62), channel_id=1, source_target_pairs={{0,8},{4,12},{8,0},{12,4},{1,9},{5,13},{9,1},{13,5},{2,10},{6,14},... | collective-permute-start | bytes 491528 | tf_op jit(solution)/shard_map/ppermute | solution.py:46
  37.3 7.5 %slice-start = ((s8[14680064]{0:T(1024)(128)(4,1)}), s8[4194304]{0:T(1024)(128)(4,1)S(1)}, s32[]{:S(2)}) async-start(s8[14680064]{0:T(1024)(128)(4,1)} %bitcast.121), calls=%async_computation | async-start | bytes 8388608
  37.3 7.6 %slice-start.1 = ((s8[14680064]{0:T(1024)(128)(4,1)}), s8[4194304]{0:T(1024)(128)(4,1)S(1)}, s32[]{:S(2)}) async-start(s8[14680064]{0:T(1024)(128)(4,1)} %bitcast.121), calls=%async_computation.1 | async-start | bytes 8388608
  37.3 8.8 %slice-start.2 = ((s8[14680064]{0:T(1024)(128)(4,1)}), s8[4194304]{0:T(1024)(128)(4,1)S(1)}, s32[]{:S(2)}) async-start(s8[14680064]{0:T(1024)(128)(4,1)} %bitcast.121), calls=%async_computation.2 | async-start | bytes 8388608
  43.5 3.5 %slice-start.3 = ((s8[14680064]{0:T(1024)(128)(4,1)}), s8[2097152]{0:T(1024)(128)(4,1)S(1)}, s32[]{:S(2)}) async-start(s8[14680064]{0:T(1024)(128)(4,1)} %bitcast.121), calls=%async_computation.3 | async-start | bytes 4194304
  48.5 5.1 %collective-permute-start.6 = (bf16[2,80,1792]{2,1,0:T(8,128)(2,1)S(1)}, bf16[2,80,1792]{2,1,0:T(8,128)(2,1)S(1)}, u32[]{:S(2)}, u32[]{:S(2)}) collective-permute-start(bf16[2,80,1792]{2,1,0:T(8,128)(2,1)S(1)} %pad_maximum_fusion.8), channel_id=1, source_target_pairs={{0,1},{1,0},{2,3},{3,2},{4,5},{5,4},{6,7},{7,6},{8,9},{9,8},{10,11... | collective-permute-start | bytes 1720328 | tf_op jit(solution)/shard_map/ppermute | solution.py:46
  51.8 7.1 %collective-permute-start.11 = (bf16[40,2048]{1,0:T(8,128)(2,1)S(1)}, bf16[40,2048]{1,0:T(8,128)(2,1)S(1)}, u32[]{:S(2)}, u32[]{:S(2)}) collective-permute-start(bf16[40,2048]{1,0:T(8,128)(2,1)S(1)} %get-tuple-element.82), channel_id=1, source_target_pairs={{0,2},{1,3},{2,0},{3,1},{4,6},{5,7},{6,4},{7,5},{8,10},{9,11},{10,... | collective-permute-start | bytes 491528 | tf_op jit(solution)/shard_map/ppermute | solution.py:46
  53.5 2.0 %collective-permute-start.8 = (bf16[2,80,1792]{2,1,0:T(8,128)(2,1)S(1)}, bf16[2,80,1792]{2,1,0:T(8,128)(2,1)S(1)}, u32[]{:S(2)}, u32[]{:S(2)}) collective-permute-start(bf16[2,80,1792]{2,1,0:T(8,128)(2,1)S(1)} %pad_maximum_fusion.9), channel_id=1, source_target_pairs={{0,1},{1,0},{2,3},{3,2},{4,5},{5,4},{6,7},{7,6},{8,9},{9,8},{10,11... | collective-permute-start | bytes 1720328 | tf_op jit(solution)/shard_map/ppermute | solution.py:46
  53.8 11.3 %collective-permute-start.7 = (bf16[2,40,1792]{2,1,0:T(8,128)(2,1)S(1)}, bf16[2,40,1792]{2,1,0:T(8,128)(2,1)S(1)}, u32[]{:S(2)}, u32[]{:S(2)}) collective-permute-start(bf16[2,40,1792]{2,1,0:T(8,128)(2,1)S(1)} %pad_maximum_fusion.17), channel_id=1, source_target_pairs={{0,2},{1,3},{2,0},{3,1},{4,6},{5,7},{6,4},{7,5},{8,10},{9,11},{10,... | collective-permute-start | bytes 860168 | tf_op jit(solution)/shard_map/ppermute | solution.py:46
  55.7 30.1 %collective-permute-start.15 = (bf16[2,40,1792]{2,1,0:T(8,128)(2,1)S(1)}, bf16[2,40,1792]{2,1,0:T(8,128)(2,1)S(1)}, u32[]{:S(2)}, u32[]{:S(2)}) collective-permute-start(bf16[2,40,1792]{2,1,0:T(8,128)(2,1)S(1)} %pad_maximum_fusion.18), channel_id=1, source_target_pairs={{0,2},{1,3},{2,0},{3,1},{4,6},{5,7},{6,4},{7,5},{8,10},{9,11},{10,... | collective-permute-start | bytes 860168 | tf_op jit(solution)/shard_map/ppermute | solution.py:46
  58.9 8.7 %collective-permute-start.13 = (bf16[80,2048]{1,0:T(8,128)(2,1)S(1)}, bf16[80,2048]{1,0:T(8,128)(2,1)S(1)}, u32[]{:S(2)}, u32[]{:S(2)}) collective-permute-start(bf16[80,2048]{1,0:T(8,128)(2,1)S(1)} %pad_maximum_fusion.16), channel_id=1, source_target_pairs={{1,4},{3,6},{4,1},{6,3},{9,12},{11,14},{12,9},{14,11},{17,20},{19,... | collective-permute-start | bytes 983048 | tf_op jit(solution)/shard_map/ppermute | solution.py:109
  59.6 10.7 %collective-permute-start.12 = (bf16[80,2048]{1,0:T(8,128)(2,1)S(1)}, bf16[80,2048]{1,0:T(8,128)(2,1)S(1)}, u32[]{:S(2)}, u32[]{:S(2)}) collective-permute-start(bf16[80,2048]{1,0:T(8,128)(2,1)S(1)} %pad_maximum_fusion.16), channel_id=1, source_target_pairs={{0,4},{1,0},{2,6},{3,2},{4,5},{5,1},{6,7},{7,3},{8,12},{9,8},{10,1... | collective-permute-start | bytes 983048 | tf_op jit(solution)/shard_map/ppermute | solution.py:109
  65.2 25.1 %collective-permute-start.9 = (bf16[40,1792]{1,0:T(8,128)(2,1)S(1)}, bf16[40,1792]{1,0:T(8,128)(2,1)S(1)}, u32[]{:S(2)}, u32[]{:S(2)}) collective-permute-start(bf16[40,1792]{1,0:T(8,128)(2,1)S(1)} %fusion.53), channel_id=1, source_target_pairs={{0,8},{4,12},{8,0},{12,4},{1,9},{5,13},{9,1},{13,5},{2,10},{6,14},... | collective-permute-start | bytes 430088 | tf_op jit(solution)/shard_map/ppermute | solution.py:46
  77.7 49.9 %slice-start.4 = ((s8[14680064]{0:T(1024)(128)(4,1)}), s8[2097152]{0:T(1024)(128)(4,1)S(1)}, s32[]{:S(2)}) async-start(s8[14680064]{0:T(1024)(128)(4,1)} %bitcast.123), calls=%async_computation.4 | async-start | bytes 4194304
  78.7 48.9 %slice-start.5 = ((s8[14680064]{0:T(1024)(128)(4,1)}), s8[4194304]{0:T(1024)(128)(4,1)S(1)}, s32[]{:S(2)}) async-start(s8[14680064]{0:T(1024)(128)(4,1)} %bitcast.123), calls=%async_computation.5 | async-start | bytes 8388608
  82.4 6.0 %collective-permute-start.14 = (bf16[2,80,2304]{2,1,0:T(8,128)(2,1)S(1)}, bf16[2,80,2304]{2,1,0:T(8,128)(2,1)S(1)}, u32[]{:S(2)}, u32[]{:S(2)}) collective-permute-start(bf16[2,80,2304]{2,1,0:T(8,128)(2,1)S(1)} %pad_maximum_fusion.5), channel_id=1, source_target_pairs={{0,1},{1,0},{2,3},{3,2},{4,5},{5,4},{6,7},{7,6},{8,9},{9,8},{10,11... | collective-permute-start | bytes 2211848 | tf_op jit(solution)/shard_map/ppermute | solution.py:46
  85.6 41.9 %slice-start.6 = ((s8[14680064]{0:T(1024)(128)(4,1)}), s8[4194304]{0:T(1024)(128)(4,1)S(1)}, s32[]{:S(2)}) async-start(s8[14680064]{0:T(1024)(128)(4,1)} %bitcast.123), calls=%async_computation.6 | async-start | bytes 8388608
  85.7 5.2 %collective-permute-start.18 = (bf16[2,80,1280]{2,1,0:T(8,128)(2,1)S(1)}, bf16[2,80,1280]{2,1,0:T(8,128)(2,1)S(1)}, u32[]{:S(2)}, u32[]{:S(2)}) collective-permute-start(bf16[2,80,1280]{2,1,0:T(8,128)(2,1)S(1)} %pad_maximum_fusion.12), channel_id=1, source_target_pairs={{0,1},{1,0},{2,3},{3,2},{4,5},{5,4},{6,7},{7,6},{8,9},{9,8},{10,11... | collective-permute-start | bytes 1228808 | tf_op jit(solution)/shard_map/ppermute | solution.py:46
  85.9 10.2 %collective-permute-start.17 = (bf16[40,1792]{1,0:T(8,128)(2,1)S(1)}, bf16[40,1792]{1,0:T(8,128)(2,1)S(1)}, u32[]{:S(2)}, u32[]{:S(2)}) collective-permute-start(bf16[40,1792]{1,0:T(8,128)(2,1)S(1)} %fusion.51), channel_id=1, source_target_pairs={{0,8},{4,12},{8,0},{12,4},{1,9},{5,13},{9,1},{13,5},{2,10},{6,14},... | collective-permute-start | bytes 430088 | tf_op jit(solution)/shard_map/ppermute | solution.py:46
  88.7 18.5 %collective-permute-start.19 = (bf16[2,40,2304]{2,1,0:T(8,128)(2,1)S(1)}, bf16[2,40,2304]{2,1,0:T(8,128)(2,1)S(1)}, u32[]{:S(2)}, u32[]{:S(2)}) collective-permute-start(bf16[2,40,2304]{2,1,0:T(8,128)(2,1)S(1)} %pad_maximum_fusion.13), channel_id=1, source_target_pairs={{0,2},{1,3},{2,0},{3,1},{4,6},{5,7},{6,4},{7,5},{8,10},{9,11},{10,... | collective-permute-start | bytes 1105928 | tf_op jit(solution)/shard_map/ppermute | solution.py:46
  90.3 37.3 %slice-start.7 = ((s8[14680064]{0:T(1024)(128)(4,1)}), s8[4194304]{0:T(1024)(128)(4,1)S(1)}, s32[]{:S(2)}) async-start(s8[14680064]{0:T(1024)(128)(4,1)} %bitcast.123), calls=%async_computation.7 | async-start | bytes 8388608
  90.3 13.0 %collective-permute-start.16 = (bf16[40,1792]{1,0:T(8,128)(2,1)S(1)}, bf16[40,1792]{1,0:T(8,128)(2,1)S(1)}, u32[]{:S(2)}, u32[]{:S(2)}) collective-permute-start(bf16[40,1792]{1,0:T(8,128)(2,1)S(1)} %get-tuple-element.94), channel_id=1, source_target_pairs={{0,2},{1,3},{2,0},{3,1},{4,6},{5,7},{6,4},{7,5},{8,10},{9,11},{10,... | collective-permute-start | bytes 430088 | tf_op jit(solution)/shard_map/ppermute | solution.py:46
  91.1 19.7 %collective-permute-start.21 = (bf16[2,40,1280]{2,1,0:T(8,128)(2,1)S(1)}, bf16[2,40,1280]{2,1,0:T(8,128)(2,1)S(1)}, u32[]{:S(2)}, u32[]{:S(2)}) collective-permute-start(bf16[2,40,1280]{2,1,0:T(8,128)(2,1)S(1)} %pad_maximum_fusion.21), channel_id=1, source_target_pairs={{0,2},{1,3},{2,0},{3,1},{4,6},{5,7},{6,4},{7,5},{8,10},{9,11},{10,... | collective-permute-start | bytes 614408 | tf_op jit(solution)/shard_map/ppermute | solution.py:46
  96.1 13.9 %collective-permute-start.22 = (bf16[40,1792]{1,0:T(8,128)(2,1)S(1)}, bf16[40,1792]{1,0:T(8,128)(2,1)S(1)}, u32[]{:S(2)}, u32[]{:S(2)}) collective-permute-start(bf16[40,1792]{1,0:T(8,128)(2,1)S(1)} %get-tuple-element.92), channel_id=1, source_target_pairs={{0,2},{1,3},{2,0},{3,1},{4,6},{5,7},{6,4},{7,5},{8,10},{9,11},{10,... | collective-permute-start | bytes 430088 | tf_op jit(solution)/shard_map/ppermute | solution.py:46
  103.3 18.4 %collective-permute-start.24 = (bf16[80,1792]{1,0:T(8,128)(2,1)S(1)}, bf16[80,1792]{1,0:T(8,128)(2,1)S(1)}, u32[]{:S(2)}, u32[]{:S(2)}) collective-permute-start(bf16[80,1792]{1,0:T(8,128)(2,1)S(1)} %pad_maximum_fusion.19), channel_id=1, source_target_pairs={{1,4},{3,6},{4,1},{6,3},{9,12},{11,14},{12,9},{14,11},{17,20},{19,... | collective-permute-start | bytes 860168 | tf_op jit(solution)/shard_map/ppermute | solution.py:109
  104.0 19.3 %collective-permute-start.23 = (bf16[80,1792]{1,0:T(8,128)(2,1)S(1)}, bf16[80,1792]{1,0:T(8,128)(2,1)S(1)}, u32[]{:S(2)}, u32[]{:S(2)}) collective-permute-start(bf16[80,1792]{1,0:T(8,128)(2,1)S(1)} %pad_maximum_fusion.19), channel_id=1, source_target_pairs={{0,4},{1,0},{2,6},{3,2},{4,5},{5,1},{6,7},{7,3},{8,12},{9,8},{10,1... | collective-permute-start | bytes 860168 | tf_op jit(solution)/shard_map/ppermute | solution.py:109
  107.3 11.0 %collective-permute-start.20 = (bf16[40,2304]{1,0:T(8,128)(2,1)S(1)}, bf16[40,2304]{1,0:T(8,128)(2,1)S(1)}, u32[]{:S(2)}, u32[]{:S(2)}) collective-permute-start(bf16[40,2304]{1,0:T(8,128)(2,1)S(1)} %fusion.45), channel_id=1, source_target_pairs={{0,8},{4,12},{8,0},{12,4},{1,9},{5,13},{9,1},{13,5},{2,10},{6,14},... | collective-permute-start | bytes 552968 | tf_op jit(solution)/shard_map/ppermute | solution.py:46
  110.0 19.0 %collective-permute-start.27 = (bf16[80,1792]{1,0:T(8,128)(2,1)S(1)}, bf16[80,1792]{1,0:T(8,128)(2,1)S(1)}, u32[]{:S(2)}, u32[]{:S(2)}) collective-permute-start(bf16[80,1792]{1,0:T(8,128)(2,1)S(1)} %pad_maximum_fusion.20), channel_id=1, source_target_pairs={{1,4},{3,6},{4,1},{6,3},{9,12},{11,14},{12,9},{14,11},{17,20},{19,... | collective-permute-start | bytes 860168 | tf_op jit(solution)/shard_map/ppermute | solution.py:109
  110.7 18.4 %collective-permute-start.26 = (bf16[80,1792]{1,0:T(8,128)(2,1)S(1)}, bf16[80,1792]{1,0:T(8,128)(2,1)S(1)}, u32[]{:S(2)}, u32[]{:S(2)}) collective-permute-start(bf16[80,1792]{1,0:T(8,128)(2,1)S(1)} %pad_maximum_fusion.20), channel_id=1, source_target_pairs={{0,4},{1,0},{2,6},{3,2},{4,5},{5,1},{6,7},{7,3},{8,12},{9,8},{10,1... | collective-permute-start | bytes 860168 | tf_op jit(solution)/shard_map/ppermute | solution.py:109
  118.3 7.7 %collective-permute-start.32 = (bf16[40,1280]{1,0:T(8,128)(2,1)S(1)}, bf16[40,1280]{1,0:T(8,128)(2,1)S(1)}, u32[]{:S(2)}, u32[]{:S(2)}) collective-permute-start(bf16[40,1280]{1,0:T(8,128)(2,1)S(1)} %fusion.59), channel_id=1, source_target_pairs={{0,8},{4,12},{8,0},{12,4},{1,9},{5,13},{9,1},{13,5},{2,10},{6,14},... | collective-permute-start | bytes 307208 | tf_op jit(solution)/shard_map/ppermute | solution.py:46
  121.7 7.3 %collective-permute-start.25 = (bf16[40,2304]{1,0:T(8,128)(2,1)S(1)}, bf16[40,2304]{1,0:T(8,128)(2,1)S(1)}, u32[]{:S(2)}, u32[]{:S(2)}) collective-permute-start(bf16[40,2304]{1,0:T(8,128)(2,1)S(1)} %get-tuple-element.74), channel_id=1, source_target_pairs={{0,2},{1,3},{2,0},{3,1},{4,6},{5,7},{6,4},{7,5},{8,10},{9,11},{10,... | collective-permute-start | bytes 552968 | tf_op jit(solution)/shard_map/ppermute | solution.py:46
  126.0 4.7 %collective-permute-start.33 = (bf16[40,1280]{1,0:T(8,128)(2,1)S(1)}, bf16[40,1280]{1,0:T(8,128)(2,1)S(1)}, u32[]{:S(2)}, u32[]{:S(2)}) collective-permute-start(bf16[40,1280]{1,0:T(8,128)(2,1)S(1)} %get-tuple-element.98), channel_id=1, source_target_pairs={{0,2},{1,3},{2,0},{3,1},{4,6},{5,7},{6,4},{7,5},{8,10},{9,11},{10,... | collective-permute-start | bytes 307208 | tf_op jit(solution)/shard_map/ppermute | solution.py:46
  130.6 8.1 %collective-permute-start.28 = (bf16[80,2048]{1,0:T(8,128)(2,1)S(1)}, bf16[80,2048]{1,0:T(8,128)(2,1)S(1)}, u32[]{:S(2)}, u32[]{:S(2)}) collective-permute-start(bf16[80,2048]{1,0:T(8,128)(2,1)S(1)} %slice.528), channel_id=1, source_target_pairs={{0,1},{1,0},{2,3},{3,2},{4,5},{5,4},{6,7},{7,6},{8,9},{9,8},{10,11... | collective-permute-start | bytes 983048 | tf_op jit(solution)/shard_map/ppermute | solution.py:46
  130.8 9.6 %collective-permute-start.35 = (bf16[80,1280]{1,0:T(8,128)(2,1)S(1)}, bf16[80,1280]{1,0:T(8,128)(2,1)S(1)}, u32[]{:S(2)}, u32[]{:S(2)}) collective-permute-start(bf16[80,1280]{1,0:T(8,128)(2,1)S(1)} %pad_maximum_fusion.22), channel_id=1, source_target_pairs={{1,4},{3,6},{4,1},{6,3},{9,12},{11,14},{12,9},{14,11},{17,20},{19,... | collective-permute-start | bytes 614408 | tf_op jit(solution)/shard_map/ppermute | solution.py:109
  131.5 8.9 %collective-permute-start.34 = (bf16[80,1280]{1,0:T(8,128)(2,1)S(1)}, bf16[80,1280]{1,0:T(8,128)(2,1)S(1)}, u32[]{:S(2)}, u32[]{:S(2)}) collective-permute-start(bf16[80,1280]{1,0:T(8,128)(2,1)S(1)} %pad_maximum_fusion.22), channel_id=1, source_target_pairs={{0,4},{1,0},{2,6},{3,2},{4,5},{5,1},{6,7},{7,3},{8,12},{9,8},{10,1... | collective-permute-start | bytes 614408 | tf_op jit(solution)/shard_map/ppermute | solution.py:109
  134.8 12.2 %collective-permute-start.31 = (bf16[80,2304]{1,0:T(8,128)(2,1)S(1)}, bf16[80,2304]{1,0:T(8,128)(2,1)S(1)}, u32[]{:S(2)}, u32[]{:S(2)}) collective-permute-start(bf16[80,2304]{1,0:T(8,128)(2,1)S(1)} %pad_maximum_fusion.14), channel_id=1, source_target_pairs={{1,4},{3,6},{4,1},{6,3},{9,12},{11,14},{12,9},{14,11},{17,20},{19,... | collective-permute-start | bytes 1105928 | tf_op jit(solution)/shard_map/ppermute | solution.py:109
  135.5 11.9 %collective-permute-start.30 = (bf16[80,2304]{1,0:T(8,128)(2,1)S(1)}, bf16[80,2304]{1,0:T(8,128)(2,1)S(1)}, u32[]{:S(2)}, u32[]{:S(2)}) collective-permute-start(bf16[80,2304]{1,0:T(8,128)(2,1)S(1)} %pad_maximum_fusion.14), channel_id=1, source_target_pairs={{0,4},{1,0},{2,6},{3,2},{4,5},{5,1},{6,7},{7,3},{8,12},{9,8},{10,1... | collective-permute-start | bytes 1105928 | tf_op jit(solution)/shard_map/ppermute | solution.py:109
  138.8 8.2 %collective-permute-start.29 = (bf16[80,2048]{1,0:T(8,128)(2,1)S(1)}, bf16[80,2048]{1,0:T(8,128)(2,1)S(1)}, u32[]{:S(2)}, u32[]{:S(2)}) collective-permute-start(bf16[80,2048]{1,0:T(8,128)(2,1)S(1)} %get-tuple-element.61), channel_id=1, source_target_pairs={{0,2},{1,3},{2,0},{3,1},{4,6},{5,7},{6,4},{7,5},{8,10},{9,11},{10,... | collective-permute-start | bytes 983048 | tf_op jit(solution)/shard_map/ppermute | solution.py:46
  149.4 2.3 %collective-permute-start.36 = (bf16[80,2048]{1,0:T(8,128)(2,1)S(1)}, bf16[80,2048]{1,0:T(8,128)(2,1)S(1)}, u32[]{:S(2)}, u32[]{:S(2)}) collective-permute-start(bf16[80,2048]{1,0:T(8,128)(2,1)S(1)} %slice.527), channel_id=1, source_target_pairs={{0,1},{1,0},{2,3},{3,2},{4,5},{5,4},{6,7},{7,6},{8,9},{9,8},{10,11... | collective-permute-start | bytes 983048 | tf_op jit(solution)/shard_map/ppermute | solution.py:46
  151.7 10.1 %collective-permute-start.37 = (bf16[80,2048]{1,0:T(8,128)(2,1)S(1)}, bf16[80,2048]{1,0:T(8,128)(2,1)S(1)}, u32[]{:S(2)}, u32[]{:S(2)}) collective-permute-start(bf16[80,2048]{1,0:T(8,128)(2,1)S(1)} %fusion.38), channel_id=1, source_target_pairs={{0,2},{1,3},{2,0},{3,1},{4,6},{5,7},{6,4},{7,5},{8,10},{9,11},{10,... | collective-permute-start | bytes 983048 | tf_op jit(solution)/shard_map/ppermute | solution.py:46
  161.9 3.1 %copy-start.1 = (bf16[160,2048]{1,0:T(8,128)(2,1)S(1)}, bf16[160,2048]{1,0:T(8,128)(2,1)}, u32[]{:S(2)}) copy-start(bf16[160,2048]{1,0:T(8,128)(2,1)} %param.5) | copy-start | bytes 1966084
  162.9 2.2 %collective-permute-start.38 = (bf16[160,2048]{1,0:T(8,128)(2,1)S(1)}, bf16[160,2048]{1,0:T(8,128)(2,1)S(1)}, u32[]{:S(2)}, u32[]{:S(2)}) collective-permute-start(bf16[160,2048]{1,0:T(8,128)(2,1)S(1)} %select_convert_fusion), channel_id=1, source_target_pairs={{0,1},{1,0},{2,3},{3,2},{4,5},{5,4},{6,7},{7,6},{8,9},{9,8},{10,11... | collective-permute-start | bytes 1966088 | tf_op jit(solution)/shard_map/ppermute | solution.py:46

commit v12 on v9

--- a/solution.py
+++ b/solution.py
@@ -10,23 +10,29 @@
 HALVES = 2
 PARTS = ((14, 14), (18, 10))
 EDGES = {
-    "w.pull": ["t0.add"],
-    "t0.halves": ["w.pull"],
-    "t1.pick": ["t0.add"],
+    "w.pull": ["t0.columns"],
     "t1.add": ["t0.halves"],
     "t1.halves": ["t0.columns"],
+    "c00.dots": ["t1.columns"],
     "c01.dots": ["c00.dots"],
     "c00.sum": ["c01.dots"],
-    "t1.columns": ["c01.sum"],
     "c00.hidden": ["c01.sum"],
     "t1.cores": ["c00.hidden"],
-    "c01.hidden": ["c10.dots"],
+    "c11.dots": ["c10.dots"],
+    "c01.hidden": ["c11.dots"],
     "c10.sum": ["c01.hidden"],
-    "c11.dots": ["c00.halves"],
     "c00.halves": ["c10.sum"],
-    "c10.hidden": ["c11.sum"],
+    "c11.sum": ["c00.halves"],
     "c01.halves": ["c11.sum"],
+    "c00.columns": ["c01.halves"],
+    "c10.hidden": ["c00.columns"],
+    "c01.columns": ["c10.hidden"],
+    "c11.hidden": ["c01.columns"],
     "c10.halves": ["c11.hidden"],
+    "c00.cores": ["c10.halves"],
+    "c01.cores": ["c10.halves"],
+    "c11.halves": ["c01.down"],
+    "b0.total": ["c11.halves"],
     "c10.cores": ["b0.all"],
     "c11.cores": ["b0.total"],
 }
@@ -92,13 +98,12 @@
             ends.append(ends[-1] + units * size // sum(sizes))
         spans.append(list(zip(ends[:-1], ends[1:])))
 
-    rows = jnp.arange(lengths.shape[0], dtype=jnp.int32)
-    slot = jnp.arange(slots, dtype=jnp.int32)
-    places = []
-    for row in (c, c ^ 1):
-        first = jnp.sum(jnp.where(rows < row, lengths, 0))
-        count = jnp.sum(jnp.where(rows == row, lengths, 0))
-        places.append(jnp.where(slot < count, slot + first, -1))
+    rows = jnp.arange(lengths.shape[0], dtype=jnp.int32)[None]
+    slot = jnp.arange(slots, dtype=jnp.int32)[None]
+    here = (c ^ jnp.arange(2, dtype=jnp.int32))[:, None]
+    first = jnp.sum(jnp.where(rows < here, lengths[None], 0), axis=1, keepdims=True)
+    count = jnp.sum(jnp.where(rows == here, lengths[None], 0), axis=1, keepdims=True)
+    places = jnp.where(slot < count, slot + first, -1)
     inside = jnp.arange(piece, dtype=jnp.int32)
     mine = [
         jnp.concatenate([inside + quarter * c, inside + quarter * (c ^ 2)]) + h * piece
@@ -165,15 +170,17 @@
         yield
         return issued(name + ".cores", finish(ordered(name + ".cores", pair)))
 
-    def pick_steps(name, h):
-        own = mine[h][:, None] == places[0][None]
-        sib = mine[h][:, None] == places[1][None]
-        rows = dot(own.astype(jnp.bfloat16), tokens)
-        rows = rows + dot(ordered(name + ".pick", sib).astype(jnp.bfloat16), sibling)
-        rows = issued(name + ".pick", rows.astype(jnp.bfloat16))
-        got = swap_x(rows[piece:])
-        yield
-        return issued(name + ".add", ordered(name + ".add", rows[:piece]) + got)
+    picked = {}
+
+    def pick_steps():
+        own = jnp.concatenate(mine)[:, None] == places[0][None]
+        sib = jnp.concatenate(mine)[:, None] == places[1][None]
+        rows = dot(own.astype(jnp.bfloat16), tokens) + dot(sib.astype(jnp.bfloat16), sibling)
+        rows = rows.astype(jnp.bfloat16).reshape(HALVES, 2, piece, width)
+        picked["got"] = swap_x(rows[:, 1])
+        picked["rows"] = rows[:, 0]
+        return None
+        yield
 
     pulled = []
 
@@ -185,7 +192,7 @@
         yield
 
     def half_steps(name, h):
-        own = yield from pick_steps(name, h)
+        own = issued(name + ".add", ordered(name + ".add", picked["rows"][h]) + picked["got"][h])
         return (yield from spread_steps(name, own))
 
     def chunk_steps(name, h, i):
@@ -193,6 +200,7 @@
         part = slice(*spans[h][i])
         full = ordered(name + ".dots", full)
         if (h, i) == (0, 0):
+            result("w")
             gate, up = dot(full, pulled[0]), dot(full, pulled[1])
         else:
             gate, up = dot(full, gate_weight[:, part]), dot(full, up_weight[:, part])
@@ -222,7 +230,8 @@
         got = ordered(name + ".all", got)
         return issued(name + ".all", total + jnp.concatenate([got[piece:], got[:piece]], axis=0))
 
-    chains, results = {"w": pull_steps()}, {}
+    chains = {"p": pick_steps(), "w": pull_steps()}
+    results = {}
     for h in range(HALVES):
         chains["t" + str(h)] = half_steps("t" + str(h), h)
         for i in range(len(spans[h])):
@@ -240,7 +249,7 @@
             advance(name)
         return results[name]
 
-    result("w")
+    result("p")
     for h in range(HALVES):
         result("b" + str(h))
 

time: 174 us -> 160 us (0.920)
  local copies, waits for them, and re-layouts: 11.5 us -> 1.1 us
  other arithmetic: 7.04 us -> 5.16 us
    ppermute x12, starting transfers between devices: 21.7 us -> 11.3 us  [move(): return lax.ppermute(value, ('row', 'col'), pairs)]
    ppermute x28 -> x27, waiting for transfers between devices: 52.8 us -> 62.1 us  [flip(): return lax.ppermute(value, axis, [(i, i ^ bit) for i in range(count)])]
    ppermute x28 -> x27, starting transfers between devices: 27.7 us -> 37 us  [flip(): return lax.ppermute(value, axis, [(i, i ^ bit) for i in range(count)])]
    unnamed x38 -> x32, local copies, waits for them, and re-layouts: 9.8 us -> 0.55 us
    ppermute x12, waiting for transfers between devices: 16.3 us -> 7.48 us  [move(): return lax.ppermute(value, ('row', 'col'), pairs)]
    select_n x1, other arithmetic: 2.53 us -> 0.08 us  [stationary(): places = jnp.where(slot < count, slot + first, -1)]
    dot_general x16 -> x14, matrix products: 26.7 us -> 25.6 us  [dot(): return jnp.dot(a, b, preferred_element_type=jnp.float32)]
  transfers between devices with their start and end apart: 40 -> 39, of which waited for: 17 -> 16; matrix products, arithmetic and copies ran while one was open for 18% -> 18% of each run, Pallas kernels for 4% -> 4%
where the time goes in v12:
time: 160 us; the launch traced here: 159 us
  waiting for transfers between devices  69.6 us (43%)
  starting transfers between devices  48.3 us (30%)
  matrix products  28.4 us (18%)
  Pallas kernels  5.84 us (4%)
  other arithmetic  5.16 us (3%)
    ppermute x27, waiting for transfers between devices, flip(): return lax.ppermute(value, axis, [(i, i ^ bit) for i in range(count)])  62.1 us
    ppermute x27, starting transfers between devices, flip(): return lax.ppermute(value, axis, [(i, i ^ bit) for i in range(count)])  37 us
    dot_general x14, matrix products, dot(): return jnp.dot(a, b, preferred_element_type=jnp.float32)  25.6 us
    ppermute x12, starting transfers between devices, move(): return lax.ppermute(value, ('row', 'col'), pairs)  11.3 us
    ppermute x12, waiting for transfers between devices, move(): return lax.ppermute(value, ('row', 'col'), pairs)  7.48 us
    pallas_call x1, Pallas kernels, pull(): pl.pallas_call(functools.partial(pull_kernel, first, end), in_specs=[pl.B...  5.84 us
  transfers between devices with their start and end apart: 39, of which 16 were waited for; matrix products, arithmetic and copies ran while one was open for 18% of the time, Pallas kernels for 4%

profile of v12, /device:TPU:0, one launch (start us, length us, event | category | flops | bytes accessed | tf_op | source)
XLA Modules:
  0.0 159.4 jit_solution(8100818096227162631)
XLA Ops:
  0.5 0.9 fusion.83
  1.6 1.5 fusion.67
  3.9 2.6 %collective-permute-start.1 = (bf16[2,40,2048]{2,1,0:T(8,128)(2,1)S(1)}, bf16[2,40,2048]{2,1,0:T(8,128)(2,1)S(1)}, u32[]{:S(2)}, u32[]{:S(2)}) collective-permute-start(bf16[2,40,2048]{2,1,0:T(8,128)(2,1)S(1)} %slice_bitcast_fusion), channel_id=1, source_target_pairs={{0,2},{1,3},{2,0},{3,1},{4,6},{5,7},{6,4},{7,5},{8,10},{9,11},{10,... | collective-permute-start | bytes 983048 | tf_op jit(solution)/shard_map/ppermute | solution.py:47
  6.5 8.4 %collective-permute-done.1 = bf16[2,40,2048]{2,1,0:T(8,128)(2,1)S(1)} collective-permute-done((bf16[2,40,2048]{2,1,0:T(8,128)(2,1)S(1)}, bf16[2,40,2048]{2,1,0:T(8,128)(2,1)S(1)}, u32[]{:S(2)}, u32[]{:S(2)}) %collective-permute-start.1) | collective-permute-done | bytes 327712 | tf_op jit(solution)/shard_map/ppermute | solution.py:47
  14.9 2.9 %collective-permute-start.2 = (bf16[40,2048]{1,0:T(8,128)(2,1)S(1)}, bf16[40,2048]{1,0:T(8,128)(2,1)S(1)}, u32[]{:S(2)}, u32[]{:S(2)}) collective-permute-start(bf16[40,2048]{1,0:T(8,128)(2,1)S(1)} %fusion.65), channel_id=1, source_target_pairs={{0,8},{4,12},{8,0},{12,4},{1,9},{5,13},{9,1},{13,5},{2,10},{6,14},... | collective-permute-start | bytes 491528 | tf_op jit(solution)/shard_map/ppermute | solution.py:47
  17.8 7.6 %collective-permute-done.2 = bf16[40,2048]{1,0:T(8,128)(2,1)S(1)} collective-permute-done((bf16[40,2048]{1,0:T(8,128)(2,1)S(1)}, bf16[40,2048]{1,0:T(8,128)(2,1)S(1)}, u32[]{:S(2)}, u32[]{:S(2)}) %collective-permute-start.2) | collective-permute-done | bytes 163872 | tf_op jit(solution)/shard_map/ppermute | solution.py:47
  25.4 1.6 collective-permute-start.3
  27.1 3.7 %collective-permute-done.3 = bf16[40,2048]{1,0:T(8,128)(2,1)S(1)} collective-permute-done((bf16[40,2048]{1,0:T(8,128)(2,1)S(1)}, bf16[40,2048]{1,0:T(8,128)(2,1)S(1)}, u32[]{:S(2)}, u32[]{:S(2)}) %collective-permute-start.3) | collective-permute-done | bytes 163872 | tf_op jit(solution)/shard_map/ppermute | solution.py:47
  30.8 5.7 %collective-permute-done.6 = bf16[40,2048]{1,0:T(8,128)(2,1)S(1)} collective-permute-done((bf16[40,2048]{1,0:T(8,128)(2,1)S(1)}, bf16[40,2048]{1,0:T(8,128)(2,1)S(1)}, u32[]{:S(2)}, u32[]{:S(2)}) %collective-permute-start.6) | collective-permute-done | bytes 163872 | tf_op jit(solution)/shard_map/ppermute | solution.py:47
  36.5 0.5 collective-permute-start.7
  37.1 0.7 collective-permute-start.5
  37.8 5.8 %shard_map.55 = (bf16[2048,1792]{1,0:T(8,128)(2,1)S(1)}, bf16[2048,1792]{1,0:T(8,128)(2,1)S(1)}) custom-call(s32[4]{0:T(128)S(1)} %copy-done, bf16[2048,3584]{1,0:T(8,128)(2,1)} %gate_ref.1, bf16[2048,3584]{1,0:T(8,128)(2,1)} %up_ref.1), custom_call_target="tpu_custom_call" | custom-call | tf_op jit(solution)/shard_map/pallas_call | solution.py:67
  43.7 3.4 %collective-permute-start.12 = (bf16[80,2048]{1,0:T(8,128)(2,1)S(1)}, bf16[80,2048]{1,0:T(8,128)(2,1)S(1)}, u32[]{:S(2)}, u32[]{:S(2)}) collective-permute-start(bf16[80,2048]{1,0:T(8,128)(2,1)S(1)} %pad_maximum_fusion.14), channel_id=1, source_target_pairs={{0,4},{1,0},{2,6},{3,2},{4,5},{5,1},{6,7},{7,3},{8,12},{9,8},{10,1... | collective-permute-start | bytes 983048 | tf_op jit(solution)/shard_map/ppermute | solution.py:122
  47.1 0.7 collective-permute-start.13
  48.0 1.4 fusion.95
  49.5 1.4 fusion.96
  51.0 1.4 collective-permute-start.8
  52.5 5.2 %fusion.10 = f32[160,1792]{1,0:T(8,128)S(1)} fusion(bf16[160,2048]{1,0:T(8,128)(2,1)S(1)} %pad_maximum_fusion.6, bf16[2048,3584]{1,0:T(8,128)(2,1)} %up_ref.1), kind=kOutput, calls=%fused_computation.10 | convolution fusion | flops 1174405120 | bytes 9142272 | tf_op jit(solution)/shard_map/dot_general | solution.py:42
  57.8 1.4 fusion.12
  59.3 0.6 collective-permute-start.10
  60.2 1.6 %collective-permute-start.9 = (bf16[2,40,1792]{2,1,0:T(8,128)(2,1)S(1)}, bf16[2,40,1792]{2,1,0:T(8,128)(2,1)S(1)}, u32[]{:S(2)}, u32[]{:S(2)}) collective-permute-start(bf16[2,40,1792]{2,1,0:T(8,128)(2,1)S(1)} %pad_maximum_fusion.15), channel_id=1, source_target_pairs={{0,2},{1,3},{2,0},{3,1},{4,6},{5,7},{6,4},{7,5},{8,10},{9,11},{10,... | collective-permute-start | bytes 860168 | tf_op jit(solution)/shard_map/ppermute | solution.py:47
  62.1 1.4 collective-permute-start.15
  63.5 6.5 %collective-permute-done.9 = bf16[2,40,1792]{2,1,0:T(8,128)(2,1)S(1)} collective-permute-done((bf16[2,40,1792]{2,1,0:T(8,128)(2,1)S(1)}, bf16[2,40,1792]{2,1,0:T(8,128)(2,1)S(1)}, u32[]{:S(2)}, u32[]{:S(2)}) %collective-permute-start.9) | collective-permute-done | bytes 286752 | tf_op jit(solution)/shard_map/ppermute | solution.py:47
  70.3 1.7 %fusion.2 = f32[160,2304]{1,0:T(8,128)S(1)} fusion(bf16[2048,3584]{1,0:T(8,128)(2,1)S(1)} %bitcast.118, bf16[80,2048]{1,0:T(8,128)(2,1)S(1)} %get-tuple-element.82, bf16[80,2048]{1,0:T(8,128)(2,1)S(1)} %get-tuple-element.81), kind=kOutput, calls=%fused_computation.2 | convolution fusion | flops 1511260160 | bytes 11567104 | tf_op jit(solution)/shard_map/dot_general | solution.py:42
  72.0 1.7 %fusion.4 = f32[160,2304]{1,0:T(8,128)S(1)} fusion(bf16[2048,3584]{1,0:T(8,128)(2,1)S(1)} %bitcast.116, bf16[80,2048]{1,0:T(8,128)(2,1)S(1)} %get-tuple-element.82, bf16[80,2048]{1,0:T(8,128)(2,1)S(1)} %get-tuple-element.81), kind=kOutput, calls=%fused_computation.4 | convolution fusion | flops 1511260160 | bytes 11567104 | tf_op jit(solution)/shard_map/dot_general | solution.py:42
  73.9 1.1 fusion.18
  74.9 1.1 fusion.16
  76.3 0.6 collective-permute-start.18
  76.8 1.4 fusion.53
  78.3 2.9 %collective-permute-start.17 = (bf16[40,1792]{1,0:T(8,128)(2,1)S(1)}, bf16[40,1792]{1,0:T(8,128)(2,1)S(1)}, u32[]{:S(2)}, u32[]{:S(2)}) collective-permute-start(bf16[40,1792]{1,0:T(8,128)(2,1)S(1)} %fusion.53), channel_id=1, source_target_pairs={{0,8},{4,12},{8,0},{12,4},{1,9},{5,13},{9,1},{13,5},{2,10},{6,14},... | collective-permute-start | bytes 430088 | tf_op jit(solution)/shard_map/ppermute | solution.py:47
  81.4 1.6 %collective-permute-start.19 = (bf16[2,40,2304]{2,1,0:T(8,128)(2,1)S(1)}, bf16[2,40,2304]{2,1,0:T(8,128)(2,1)S(1)}, u32[]{:S(2)}, u32[]{:S(2)}) collective-permute-start(bf16[2,40,2304]{2,1,0:T(8,128)(2,1)S(1)} %pad_maximum_fusion.11), channel_id=1, source_target_pairs={{0,2},{1,3},{2,0},{3,1},{4,6},{5,7},{6,4},{7,5},{8,10},{9,11},{10,... | collective-permute-start | bytes 1105928 | tf_op jit(solution)/shard_map/ppermute | solution.py:47
  83.1 4.5 %collective-permute-done.11 = bf16[40,1792]{1,0:T(8,128)(2,1)S(1)} collective-permute-done((bf16[40,1792]{1,0:T(8,128)(2,1)S(1)}, bf16[40,1792]{1,0:T(8,128)(2,1)S(1)}, u32[]{:S(2)}, u32[]{:S(2)}) %collective-permute-start.11) | collective-permute-done | bytes 143392 | tf_op jit(solution)/shard_map/ppermute | solution.py:47
  87.6 1.6 %collective-permute-start.16 = (bf16[40,1792]{1,0:T(8,128)(2,1)S(1)}, bf16[40,1792]{1,0:T(8,128)(2,1)S(1)}, u32[]{:S(2)}, u32[]{:S(2)}) collective-permute-start(bf16[40,1792]{1,0:T(8,128)(2,1)S(1)} %get-tuple-element.96), channel_id=1, source_target_pairs={{0,2},{1,3},{2,0},{3,1},{4,6},{5,7},{6,4},{7,5},{8,10},{9,11},{10,... | collective-permute-start | bytes 430088 | tf_op jit(solution)/shard_map/ppermute | solution.py:47
  89.4 0.5 collective-permute-start.21
  90.1 1.6 %collective-permute-start.22 = (bf16[40,1792]{1,0:T(8,128)(2,1)S(1)}, bf16[40,1792]{1,0:T(8,128)(2,1)S(1)}, u32[]{:S(2)}, u32[]{:S(2)}) collective-permute-start(bf16[40,1792]{1,0:T(8,128)(2,1)S(1)} %get-tuple-element.94), channel_id=1, source_target_pairs={{0,2},{1,3},{2,0},{3,1},{4,6},{5,7},{6,4},{7,5},{8,10},{9,11},{10,... | collective-permute-start | bytes 430088 | tf_op jit(solution)/shard_map/ppermute | solution.py:47
  91.7 4.3 %collective-permute-done.16 = bf16[40,1792]{1,0:T(8,128)(2,1)S(1)} collective-permute-done((bf16[40,1792]{1,0:T(8,128)(2,1)S(1)}, bf16[40,1792]{1,0:T(8,128)(2,1)S(1)}, u32[]{:S(2)}, u32[]{:S(2)}) %collective-permute-start.16) | collective-permute-done | bytes 143392 | tf_op jit(solution)/shard_map/ppermute | solution.py:47
  96.2 0.9 collective-permute-start.24
  97.2 1.1 collective-permute-start.20
  98.3 3.8 %collective-permute-done.22 = bf16[40,1792]{1,0:T(8,128)(2,1)S(1)} collective-permute-done((bf16[40,1792]{1,0:T(8,128)(2,1)S(1)}, bf16[40,1792]{1,0:T(8,128)(2,1)S(1)}, u32[]{:S(2)}, u32[]{:S(2)}) %collective-permute-start.22) | collective-permute-done | bytes 143392 | tf_op jit(solution)/shard_map/ppermute | solution.py:47
  102.2 0.7 collective-permute-start.26
  103.0 2.7 %collective-permute-done.20 = bf16[40,2304]{1,0:T(8,128)(2,1)S(1)} collective-permute-done((bf16[40,2304]{1,0:T(8,128)(2,1)S(1)}, bf16[40,2304]{1,0:T(8,128)(2,1)S(1)}, u32[]{:S(2)}, u32[]{:S(2)}) %collective-permute-start.20) | collective-permute-done | bytes 184352 | tf_op jit(solution)/shard_map/ppermute | solution.py:47
  105.7 3.4 %collective-permute-start.28 = (bf16[40,1280]{1,0:T(8,128)(2,1)S(1)}, bf16[40,1280]{1,0:T(8,128)(2,1)S(1)}, u32[]{:S(2)}, u32[]{:S(2)}) collective-permute-start(bf16[40,1280]{1,0:T(8,128)(2,1)S(1)} %fusion.61), channel_id=1, source_target_pairs={{0,8},{4,12},{8,0},{12,4},{1,9},{5,13},{9,1},{13,5},{2,10},{6,14},... | collective-permute-start | bytes 307208 | tf_op jit(solution)/shard_map/ppermute | solution.py:47
  109.1 1.6 %collective-permute-start.30 = (bf16[40,2304]{1,0:T(8,128)(2,1)S(1)}, bf16[40,2304]{1,0:T(8,128)(2,1)S(1)}, u32[]{:S(2)}, u32[]{:S(2)}) collective-permute-start(bf16[40,2304]{1,0:T(8,128)(2,1)S(1)} %get-tuple-element.76), channel_id=1, source_target_pairs={{0,2},{1,3},{2,0},{3,1},{4,6},{5,7},{6,4},{7,5},{8,10},{9,11},{10,... | collective-permute-start | bytes 552968 | tf_op jit(solution)/shard_map/ppermute | solution.py:47
  110.8 0.9 collective-permute-done.25
  111.8 4.6 %fusion.6 = f32[160,2048]{1,0:T(8,128)S(1)} fusion(bf16[3584,2048]{1,0:T(8,128)(2,1)} %param.9, bf16[80,1792]{1,0:T(8,128)(2,1)S(1)} %get-tuple-element.92, bf16[80,1792]{1,0:T(8,128)(2,1)S(1)} %get-tuple-element.91), kind=kOutput, calls=%fused_computation.6 | convolution fusion | flops 1175552000 | bytes 9224192 | tf_op jit(solution)/shard_map/dot_general | solution.py:42
  116.5 1.6 %collective-permute-start.33 = (bf16[40,1280]{1,0:T(8,128)(2,1)S(1)}, bf16[40,1280]{1,0:T(8,128)(2,1)S(1)}, u32[]{:S(2)}, u32[]{:S(2)}) collective-permute-start(bf16[40,1280]{1,0:T(8,128)(2,1)S(1)} %get-tuple-element.100), channel_id=1, source_target_pairs={{0,2},{1,3},{2,0},{3,1},{4,6},{5,7},{6,4},{7,5},{8,10},{9,11},{10,... | collective-permute-start | bytes 307208 | tf_op jit(solution)/shard_map/ppermute | solution.py:47
  118.1 1.4 fusion.21
  119.6 5.0 %collective-permute-start.27 = (bf16[80,2048]{1,0:T(8,128)(2,1)S(1)}, bf16[80,2048]{1,0:T(8,128)(2,1)S(1)}, u32[]{:S(2)}, u32[]{:S(2)}) collective-permute-start(bf16[80,2048]{1,0:T(8,128)(2,1)S(1)} %slice.512), channel_id=1, source_target_pairs={{0,1},{1,0},{2,3},{3,2},{4,5},{5,4},{6,7},{7,6},{8,9},{9,8},{10,11... | collective-permute-start | bytes 983048 | tf_op jit(solution)/shard_map/ppermute | solution.py:47
  124.6 0.5 collective-permute-start.31
  125.1 0.7 collective-permute-start.32
  125.8 3.0 %collective-permute-start.34 = (bf16[80,1280]{1,0:T(8,128)(2,1)S(1)}, bf16[80,1280]{1,0:T(8,128)(2,1)S(1)}, u32[]{:S(2)}, u32[]{:S(2)}) collective-permute-start(bf16[80,1280]{1,0:T(8,128)(2,1)S(1)} %pad_maximum_fusion.20), channel_id=1, source_target_pairs={{0,4},{1,0},{2,6},{3,2},{4,5},{5,1},{6,7},{7,3},{8,12},{9,8},{10,1... | collective-permute-start | bytes 614408 | tf_op jit(solution)/shard_map/ppermute | solution.py:122
  128.8 0.7 collective-permute-start.35
  129.6 0.5 collective-permute-start.29
  130.1 6.5 %collective-permute-done.34 = bf16[80,1280]{1,0:T(8,128)(2,1)S(1)} collective-permute-done((bf16[80,1280]{1,0:T(8,128)(2,1)S(1)}, bf16[80,1280]{1,0:T(8,128)(2,1)S(1)}, u32[]{:S(2)}, u32[]{:S(2)}) %collective-permute-start.34) | collective-permute-done | bytes 204832 | tf_op jit(solution)/shard_map/ppermute | solution.py:122
  136.7 1.0 fusion.14
  137.7 2.2 %collective-permute-done.29 = bf16[80,2048]{1,0:T(8,128)(2,1)S(1)} collective-permute-done((bf16[80,2048]{1,0:T(8,128)(2,1)S(1)}, bf16[80,2048]{1,0:T(8,128)(2,1)S(1)}, u32[]{:S(2)}, u32[]{:S(2)}) %collective-permute-start.29) | collective-permute-done | bytes 327712 | tf_op jit(solution)/shard_map/ppermute | solution.py:47
  140.1 1.8 %fusion.24 = f32[160,2048]{1,0:T(8,128)S(1)} fusion(f32[160,2048]{1,0:T(8,128)S(1)} %fusion.14, bf16[3584,2048]{1,0:T(8,128)(2,1)S(1)} %bitcast.129, bf16[80,2304]{1,0:T(8,128)(2,1)S(1)} %get-tuple-element.74, bf16[80,2304]{1,0:T(8,128)(2,1)S(1)} %get-tuple-element.73), kind=kOutput, calls=%fused_computation.24 | convolution fusion | flops 1511751680 | bytes 12795904 | tf_op jit(solution)/shard_map/dot_general | solution.py:42
  141.9 0.9 collective-permute-start.36
  142.8 1.3 collective-permute-done.36
  144.2 0.5 collective-permute-start.37
  145.0 9.3 %collective-permute-done.37 = bf16[80,2048]{1,0:T(8,128)(2,1)S(1)} collective-permute-done((bf16[80,2048]{1,0:T(8,128)(2,1)S(1)}, bf16[80,2048]{1,0:T(8,128)(2,1)S(1)}, u32[]{:S(2)}, u32[]{:S(2)}) %collective-permute-start.37) | collective-permute-done | bytes 327712 | tf_op jit(solution)/shard_map/ppermute | solution.py:47
  154.4 0.9 select_convert_fusion
  155.4 2.1 %collective-permute-done.38 = bf16[160,2048]{1,0:T(8,128)(2,1)S(1)} collective-permute-done((bf16[160,2048]{1,0:T(8,128)(2,1)S(1)}, bf16[160,2048]{1,0:T(8,128)(2,1)S(1)}, u32[]{:S(2)}, u32[]{:S(2)}) %collective-permute-start.38) | collective-permute-done | bytes 655392 | tf_op jit(solution)/shard_map/ppermute | solution.py:47
  157.5 1.9 %fusion.29 = bf16[160,2048]{1,0:T(8,128)(2,1)} fusion(bf16[160,2048]{1,0:T(8,128)(2,1)S(1)} %collective-permute-done.38, bf16[160,2048]{1,0:T(8,128)(2,1)S(1)} %copy-done.1, f32[80,2048]{1,0:T(8,128)S(1)} %convert_add_fusion, f32[80,2048]{1,0:T(8,128)S(1)} %convert_add_fusion.1, pred[160]{0:T(512)(128)(4,1)S(1)} %get-tuple-element.59, ...), kind=kOutput, calls=%fused_computation.29 | convolution fusion | flops 631137280 | bytes 3278240 | tf_op jit(solution)/shard_map/dot_general | solution.py:260
  (138 shorter events, 5.5 us)
Async XLA Ops:
  0.0 3.0 %collective-permute-start = (bf16[160,2048]{1,0:T(8,128)(2,1)}, bf16[160,2048]{1,0:T(8,128)(2,1)S(1)}, u32[]{:S(2)}, u32[]{:S(2)}) collective-permute-start(bf16[160,2048]{1,0:T(8,128)(2,1)} %param.5), channel_id=1, source_target_pairs={{0,1},{1,0},{2,3},{3,2},{4,5},{5,4},{6,7},{7,6},{8,9},{9,8},{10,11... | collective-permute-start | bytes 1966088 | tf_op jit(solution)/shard_map/ppermute | solution.py:47
  3.0 0.8 copy-start.2
  3.9 10.9 %collective-permute-start.1 = (bf16[2,40,2048]{2,1,0:T(8,128)(2,1)S(1)}, bf16[2,40,2048]{2,1,0:T(8,128)(2,1)S(1)}, u32[]{:S(2)}, u32[]{:S(2)}) collective-permute-start(bf16[2,40,2048]{2,1,0:T(8,128)(2,1)S(1)} %slice_bitcast_fusion), channel_id=1, source_target_pairs={{0,2},{1,3},{2,0},{3,1},{4,6},{5,7},{6,4},{7,5},{8,10},{9,11},{10,... | collective-permute-start | bytes 983048 | tf_op jit(solution)/shard_map/ppermute | solution.py:47
  14.9 10.5 %collective-permute-start.2 = (bf16[40,2048]{1,0:T(8,128)(2,1)S(1)}, bf16[40,2048]{1,0:T(8,128)(2,1)S(1)}, u32[]{:S(2)}, u32[]{:S(2)}) collective-permute-start(bf16[40,2048]{1,0:T(8,128)(2,1)S(1)} %fusion.65), channel_id=1, source_target_pairs={{0,8},{4,12},{8,0},{12,4},{1,9},{5,13},{9,1},{13,5},{2,10},{6,14},... | collective-permute-start | bytes 491528 | tf_op jit(solution)/shard_map/ppermute | solution.py:47
  17.8 20.0 %copy-start = (s32[4]{0:T(128)S(1)}, s32[4]{0:T(128)}, u32[]{:S(2)}) copy-start(s32[4]{0:T(128)} %tick_ref) | copy-start | bytes 52
  25.4 5.4 %collective-permute-start.3 = (bf16[40,2048]{1,0:T(8,128)(2,1)S(1)}, bf16[40,2048]{1,0:T(8,128)(2,1)S(1)}, u32[]{:S(2)}, u32[]{:S(2)}) collective-permute-start(bf16[40,2048]{1,0:T(8,128)(2,1)S(1)} %get-tuple-element.88), channel_id=1, source_target_pairs={{0,2},{1,3},{2,0},{3,1},{4,6},{5,7},{6,4},{7,5},{8,10},{9,11},{10,... | collective-permute-start | bytes 491528 | tf_op jit(solution)/shard_map/ppermute | solution.py:47
  27.0 9.5 %collective-permute-start.6 = (bf16[40,2048]{1,0:T(8,128)(2,1)S(1)}, bf16[40,2048]{1,0:T(8,128)(2,1)S(1)}, u32[]{:S(2)}, u32[]{:S(2)}) collective-permute-start(bf16[40,2048]{1,0:T(8,128)(2,1)S(1)} %fusion.64), channel_id=1, source_target_pairs={{0,8},{4,12},{8,0},{12,4},{1,9},{5,13},{9,1},{13,5},{2,10},{6,14},... | collective-permute-start | bytes 491528 | tf_op jit(solution)/shard_map/ppermute | solution.py:47
  36.5 7.1 %collective-permute-start.7 = (bf16[40,2048]{1,0:T(8,128)(2,1)S(1)}, bf16[40,2048]{1,0:T(8,128)(2,1)S(1)}, u32[]{:S(2)}, u32[]{:S(2)}) collective-permute-start(bf16[40,2048]{1,0:T(8,128)(2,1)S(1)} %get-tuple-element.86), channel_id=1, source_target_pairs={{0,2},{1,3},{2,0},{3,1},{4,6},{5,7},{6,4},{7,5},{8,10},{9,11},{10,... | collective-permute-start | bytes 491528 | tf_op jit(solution)/shard_map/ppermute | solution.py:47
  37.1 10.7 %collective-permute-start.4 = (bf16[80,2048]{1,0:T(8,128)(2,1)S(1)}, bf16[80,2048]{1,0:T(8,128)(2,1)S(1)}, u32[]{:S(2)}, u32[]{:S(2)}) collective-permute-start(bf16[80,2048]{1,0:T(8,128)(2,1)S(1)} %pad_maximum_fusion.13), channel_id=1, source_target_pairs={{0,4},{1,0},{2,6},{3,2},{4,5},{5,1},{6,7},{7,3},{8,12},{9,8},{10,1... | collective-permute-start | bytes 983048 | tf_op jit(solution)/shard_map/ppermute | solution.py:122
  37.1 10.7 %collective-permute-start.5 = (bf16[80,2048]{1,0:T(8,128)(2,1)S(1)}, bf16[80,2048]{1,0:T(8,128)(2,1)S(1)}, u32[]{:S(2)}, u32[]{:S(2)}) collective-permute-start(bf16[80,2048]{1,0:T(8,128)(2,1)S(1)} %pad_maximum_fusion.13), channel_id=1, source_target_pairs={{1,4},{3,6},{4,1},{6,3},{9,12},{11,14},{12,9},{14,11},{17,20},{19,... | collective-permute-start | bytes 983048 | tf_op jit(solution)/shard_map/ppermute | solution.py:122
  43.7 26.4 %collective-permute-start.12 = (bf16[80,2048]{1,0:T(8,128)(2,1)S(1)}, bf16[80,2048]{1,0:T(8,128)(2,1)S(1)}, u32[]{:S(2)}, u32[]{:S(2)}) collective-permute-start(bf16[80,2048]{1,0:T(8,128)(2,1)S(1)} %pad_maximum_fusion.14), channel_id=1, source_target_pairs={{0,4},{1,0},{2,6},{3,2},{4,5},{5,1},{6,7},{7,3},{8,12},{9,8},{10,1... | collective-permute-start | bytes 983048 | tf_op jit(solution)/shard_map/ppermute | solution.py:122
  47.1 23.0 %collective-permute-start.13 = (bf16[80,2048]{1,0:T(8,128)(2,1)S(1)}, bf16[80,2048]{1,0:T(8,128)(2,1)S(1)}, u32[]{:S(2)}, u32[]{:S(2)}) collective-permute-start(bf16[80,2048]{1,0:T(8,128)(2,1)S(1)} %pad_maximum_fusion.14), channel_id=1, source_target_pairs={{1,4},{3,6},{4,1},{6,3},{9,12},{11,14},{12,9},{14,11},{17,20},{19,... | collective-permute-start | bytes 983048 | tf_op jit(solution)/shard_map/ppermute | solution.py:122
  49.4 8.3 %slice-start = ((s8[14680064]{0:T(1024)(128)(4,1)}), s8[4194304]{0:T(1024)(128)(4,1)S(1)}, s32[]{:S(2)}) async-start(s8[14680064]{0:T(1024)(128)(4,1)} %bitcast.115), calls=%async_computation | async-start | bytes 8388608
  49.4 8.3 %slice-start.1 = ((s8[14680064]{0:T(1024)(128)(4,1)}), s8[4194304]{0:T(1024)(128)(4,1)S(1)}, s32[]{:S(2)}) async-start(s8[14680064]{0:T(1024)(128)(4,1)} %bitcast.115), calls=%async_computation.1 | async-start | bytes 8388608
  49.5 8.3 %slice-start.2 = ((s8[14680064]{0:T(1024)(128)(4,1)}), s8[4194304]{0:T(1024)(128)(4,1)S(1)}, s32[]{:S(2)}) async-start(s8[14680064]{0:T(1024)(128)(4,1)} %bitcast.115), calls=%async_computation.2 | async-start | bytes 8388608
  51.0 6.7 %slice-start.3 = ((s8[14680064]{0:T(1024)(128)(4,1)}), s8[2097152]{0:T(1024)(128)(4,1)S(1)}, s32[]{:S(2)}) async-start(s8[14680064]{0:T(1024)(128)(4,1)} %bitcast.115), calls=%async_computation.3 | async-start | bytes 4194304
  51.0 8.9 %collective-permute-start.8 = (bf16[2,80,1792]{2,1,0:T(8,128)(2,1)S(1)}, bf16[2,80,1792]{2,1,0:T(8,128)(2,1)S(1)}, u32[]{:S(2)}, u32[]{:S(2)}) collective-permute-start(bf16[2,80,1792]{2,1,0:T(8,128)(2,1)S(1)} %pad_maximum_fusion.8), channel_id=1, source_target_pairs={{0,1},{1,0},{2,3},{3,2},{4,5},{5,4},{6,7},{7,6},{8,9},{9,8},{10,11... | collective-permute-start | bytes 1720328 | tf_op jit(solution)/shard_map/ppermute | solution.py:47
  52.5 17.8 %slice-start.4 = ((s8[14680064]{0:T(1024)(128)(4,1)}), s8[4194304]{0:T(1024)(128)(4,1)S(1)}, s32[]{:S(2)}) async-start(s8[14680064]{0:T(1024)(128)(4,1)} %bitcast.117), calls=%async_computation.4 | async-start | bytes 8388608
  52.5 17.8 %slice-start.5 = ((s8[14680064]{0:T(1024)(128)(4,1)}), s8[2097152]{0:T(1024)(128)(4,1)S(1)}, s32[]{:S(2)}) async-start(s8[14680064]{0:T(1024)(128)(4,1)} %bitcast.117), calls=%async_computation.5 | async-start | bytes 4194304
  57.8 12.5 %slice-start.6 = ((s8[14680064]{0:T(1024)(128)(4,1)}), s8[4194304]{0:T(1024)(128)(4,1)S(1)}, s32[]{:S(2)}) async-start(s8[14680064]{0:T(1024)(128)(4,1)} %bitcast.117), calls=%async_computation.6 | async-start | bytes 8388608
  59.3 10.9 %slice-start.7 = ((s8[14680064]{0:T(1024)(128)(4,1)}), s8[4194304]{0:T(1024)(128)(4,1)S(1)}, s32[]{:S(2)}) async-start(s8[14680064]{0:T(1024)(128)(4,1)} %bitcast.117), calls=%async_computation.7 | async-start | bytes 8388608
  59.3 2.5 %collective-permute-start.10 = (bf16[2,80,1792]{2,1,0:T(8,128)(2,1)S(1)}, bf16[2,80,1792]{2,1,0:T(8,128)(2,1)S(1)}, u32[]{:S(2)}, u32[]{:S(2)}) collective-permute-start(bf16[2,80,1792]{2,1,0:T(8,128)(2,1)S(1)} %pad_maximum_fusion.9), channel_id=1, source_target_pairs={{0,1},{1,0},{2,3},{3,2},{4,5},{5,4},{6,7},{7,6},{8,9},{9,8},{10,11... | collective-permute-start | bytes 1720328 | tf_op jit(solution)/shard_map/ppermute | solution.py:47
  60.2 9.8 %collective-permute-start.9 = (bf16[2,40,1792]{2,1,0:T(8,128)(2,1)S(1)}, bf16[2,40,1792]{2,1,0:T(8,128)(2,1)S(1)}, u32[]{:S(2)}, u32[]{:S(2)}) collective-permute-start(bf16[2,40,1792]{2,1,0:T(8,128)(2,1)S(1)} %pad_maximum_fusion.15), channel_id=1, source_target_pairs={{0,2},{1,3},{2,0},{3,1},{4,6},{5,7},{6,4},{7,5},{8,10},{9,11},{10,... | collective-permute-start | bytes 860168 | tf_op jit(solution)/shard_map/ppermute | solution.py:47
  62.1 14.8 %collective-permute-start.15 = (bf16[2,40,1792]{2,1,0:T(8,128)(2,1)S(1)}, bf16[2,40,1792]{2,1,0:T(8,128)(2,1)}, u32[]{:S(2)}, u32[]{:S(2)}) collective-permute-start(bf16[2,40,1792]{2,1,0:T(8,128)(2,1)S(1)} %pad_maximum_fusion.16), channel_id=1, source_target_pairs={{0,2},{1,3},{2,0},{3,1},{4,6},{5,7},{6,4},{7,5},{8,10},{9,11},{10,... | collective-permute-start | bytes 860168 | tf_op jit(solution)/shard_map/ppermute | solution.py:47
  76.0 11.6 %collective-permute-start.11 = (bf16[40,1792]{1,0:T(8,128)(2,1)S(1)}, bf16[40,1792]{1,0:T(8,128)(2,1)S(1)}, u32[]{:S(2)}, u32[]{:S(2)}) collective-permute-start(bf16[40,1792]{1,0:T(8,128)(2,1)S(1)} %fusion.55), channel_id=1, source_target_pairs={{0,8},{4,12},{8,0},{12,4},{1,9},{5,13},{9,1},{13,5},{2,10},{6,14},... | collective-permute-start | bytes 430088 | tf_op jit(solution)/shard_map/ppermute | solution.py:47
  76.1 5.1 %collective-permute-start.14 = (bf16[2,80,2304]{2,1,0:T(8,128)(2,1)S(1)}, bf16[2,80,2304]{2,1,0:T(8,128)(2,1)S(1)}, u32[]{:S(2)}, u32[]{:S(2)}) collective-permute-start(bf16[2,80,2304]{2,1,0:T(8,128)(2,1)S(1)} %pad_maximum_fusion.5), channel_id=1, source_target_pairs={{0,1},{1,0},{2,3},{3,2},{4,5},{5,4},{6,7},{7,6},{8,9},{9,8},{10,11... | collective-permute-start | bytes 2211848 | tf_op jit(solution)/shard_map/ppermute | solution.py:47
  76.2 41.9 %slice-start.8 = ((s8[14680064]{0:T(1024)(128)(4,1)}), s8[4194304]{0:T(1024)(128)(4,1)S(1)}, s32[]{:S(2)}) async-start(s8[14680064]{0:T(1024)(128)(4,1)} %bitcast.128), calls=%async_computation.8 | async-start | bytes 8388608
  76.3 12.9 %collective-permute-start.18 = (bf16[2,80,1280]{2,1,0:T(8,128)(2,1)S(1)}, bf16[2,80,1280]{2,1,0:T(8,128)(2,1)S(1)}, u32[]{:S(2)}, u32[]{:S(2)}) collective-permute-start(bf16[2,80,1280]{2,1,0:T(8,128)(2,1)S(1)} %pad_maximum_fusion.10), channel_id=1, source_target_pairs={{0,1},{1,0},{2,3},{3,2},{4,5},{5,4},{6,7},{7,6},{8,9},{9,8},{10,11... | collective-permute-start | bytes 1228808 | tf_op jit(solution)/shard_map/ppermute | solution.py:47
  78.3 11.8 %collective-permute-start.17 = (bf16[40,1792]{1,0:T(8,128)(2,1)S(1)}, bf16[40,1792]{1,0:T(8,128)(2,1)S(1)}, u32[]{:S(2)}, u32[]{:S(2)}) collective-permute-start(bf16[40,1792]{1,0:T(8,128)(2,1)S(1)} %fusion.53), channel_id=1, source_target_pairs={{0,8},{4,12},{8,0},{12,4},{1,9},{5,13},{9,1},{13,5},{2,10},{6,14},... | collective-permute-start | bytes 430088 | tf_op jit(solution)/shard_map/ppermute | solution.py:47
  81.4 36.7 %slice-start.9 = ((s8[14680064]{0:T(1024)(128)(4,1)}), s8[4194304]{0:T(1024)(128)(4,1)S(1)}, s32[]{:S(2)}) async-start(s8[14680064]{0:T(1024)(128)(4,1)} %bitcast.128), calls=%async_computation.9 | async-start | bytes 8388608
  81.4 15.6 %collective-permute-start.19 = (bf16[2,40,2304]{2,1,0:T(8,128)(2,1)S(1)}, bf16[2,40,2304]{2,1,0:T(8,128)(2,1)S(1)}, u32[]{:S(2)}, u32[]{:S(2)}) collective-permute-start(bf16[2,40,2304]{2,1,0:T(8,128)(2,1)S(1)} %pad_maximum_fusion.11), channel_id=1, source_target_pairs={{0,2},{1,3},{2,0},{3,1},{4,6},{5,7},{6,4},{7,5},{8,10},{9,11},{10,... | collective-permute-start | bytes 1105928 | tf_op jit(solution)/shard_map/ppermute | solution.py:47
  87.6 8.5 %collective-permute-start.16 = (bf16[40,1792]{1,0:T(8,128)(2,1)S(1)}, bf16[40,1792]{1,0:T(8,128)(2,1)S(1)}, u32[]{:S(2)}, u32[]{:S(2)}) collective-permute-start(bf16[40,1792]{1,0:T(8,128)(2,1)S(1)} %get-tuple-element.96), channel_id=1, source_target_pairs={{0,2},{1,3},{2,0},{3,1},{4,6},{5,7},{6,4},{7,5},{8,10},{9,11},{10,... | collective-permute-start | bytes 430088 | tf_op jit(solution)/shard_map/ppermute | solution.py:47
  89.4 12.8 %collective-permute-start.21 = (bf16[2,40,1280]{2,1,0:T(8,128)(2,1)S(1)}, bf16[2,40,1280]{2,1,0:T(8,128)(2,1)S(1)}, u32[]{:S(2)}, u32[]{:S(2)}) collective-permute-start(bf16[2,40,1280]{2,1,0:T(8,128)(2,1)S(1)} %pad_maximum_fusion.19), channel_id=1, source_target_pairs={{0,2},{1,3},{2,0},{3,1},{4,6},{5,7},{6,4},{7,5},{8,10},{9,11},{10,... | collective-permute-start | bytes 614408 | tf_op jit(solution)/shard_map/ppermute | solution.py:47
  90.1 12.0 %collective-permute-start.22 = (bf16[40,1792]{1,0:T(8,128)(2,1)S(1)}, bf16[40,1792]{1,0:T(8,128)(2,1)S(1)}, u32[]{:S(2)}, u32[]{:S(2)}) collective-permute-start(bf16[40,1792]{1,0:T(8,128)(2,1)S(1)} %get-tuple-element.94), channel_id=1, source_target_pairs={{0,2},{1,3},{2,0},{3,1},{4,6},{5,7},{6,4},{7,5},{8,10},{9,11},{10,... | collective-permute-start | bytes 430088 | tf_op jit(solution)/shard_map/ppermute | solution.py:47
  96.1 13.0 %collective-permute-start.23 = (bf16[80,1792]{1,0:T(8,128)(2,1)S(1)}, bf16[80,1792]{1,0:T(8,128)(2,1)S(1)}, u32[]{:S(2)}, u32[]{:S(2)}) collective-permute-start(bf16[80,1792]{1,0:T(8,128)(2,1)S(1)} %pad_maximum_fusion.17), channel_id=1, source_target_pairs={{0,4},{1,0},{2,6},{3,2},{4,5},{5,1},{6,7},{7,3},{8,12},{9,8},{10,1... | collective-permute-start | bytes 860168 | tf_op jit(solution)/shard_map/ppermute | solution.py:122
  96.2 14.5 %collective-permute-start.24 = (bf16[80,1792]{1,0:T(8,128)(2,1)S(1)}, bf16[80,1792]{1,0:T(8,128)(2,1)S(1)}, u32[]{:S(2)}, u32[]{:S(2)}) collective-permute-start(bf16[80,1792]{1,0:T(8,128)(2,1)S(1)} %pad_maximum_fusion.17), channel_id=1, source_target_pairs={{1,4},{3,6},{4,1},{6,3},{9,12},{11,14},{12,9},{14,11},{17,20},{19,... | collective-permute-start | bytes 860168 | tf_op jit(solution)/shard_map/ppermute | solution.py:122
  97.2 8.5 %collective-permute-start.20 = (bf16[40,2304]{1,0:T(8,128)(2,1)S(1)}, bf16[40,2304]{1,0:T(8,128)(2,1)S(1)}, u32[]{:S(2)}, u32[]{:S(2)}) collective-permute-start(bf16[40,2304]{1,0:T(8,128)(2,1)S(1)} %fusion.47), channel_id=1, source_target_pairs={{0,8},{4,12},{8,0},{12,4},{1,9},{5,13},{9,1},{13,5},{2,10},{6,14},... | collective-permute-start | bytes 552968 | tf_op jit(solution)/shard_map/ppermute | solution.py:47
  102.1 9.6 %collective-permute-start.25 = (bf16[80,1792]{1,0:T(8,128)(2,1)S(1)}, bf16[80,1792]{1,0:T(8,128)(2,1)S(1)}, u32[]{:S(2)}, u32[]{:S(2)}) collective-permute-start(bf16[80,1792]{1,0:T(8,128)(2,1)S(1)} %pad_maximum_fusion.18), channel_id=1, source_target_pairs={{0,4},{1,0},{2,6},{3,2},{4,5},{5,1},{6,7},{7,3},{8,12},{9,8},{10,1... | collective-permute-start | bytes 860168 | tf_op jit(solution)/shard_map/ppermute | solution.py:122
  102.2 9.5 %collective-permute-start.26 = (bf16[80,1792]{1,0:T(8,128)(2,1)S(1)}, bf16[80,1792]{1,0:T(8,128)(2,1)S(1)}, u32[]{:S(2)}, u32[]{:S(2)}) collective-permute-start(bf16[80,1792]{1,0:T(8,128)(2,1)S(1)} %pad_maximum_fusion.18), channel_id=1, source_target_pairs={{1,4},{3,6},{4,1},{6,3},{9,12},{11,14},{12,9},{14,11},{17,20},{19,... | collective-permute-start | bytes 860168 | tf_op jit(solution)/shard_map/ppermute | solution.py:122
  103.0 15.1 %slice-start.10 = ((s8[14680064]{0:T(1024)(128)(4,1)}), s8[4194304]{0:T(1024)(128)(4,1)S(1)}, s32[]{:S(2)}) async-start(s8[14680064]{0:T(1024)(128)(4,1)} %bitcast.128), calls=%async_computation.10 | async-start | bytes 8388608
  105.7 10.7 %collective-permute-start.28 = (bf16[40,1280]{1,0:T(8,128)(2,1)S(1)}, bf16[40,1280]{1,0:T(8,128)(2,1)S(1)}, u32[]{:S(2)}, u32[]{:S(2)}) collective-permute-start(bf16[40,1280]{1,0:T(8,128)(2,1)S(1)} %fusion.61), channel_id=1, source_target_pairs={{0,8},{4,12},{8,0},{12,4},{1,9},{5,13},{9,1},{13,5},{2,10},{6,14},... | collective-permute-start | bytes 307208 | tf_op jit(solution)/shard_map/ppermute | solution.py:47
  109.1 15.4 %collective-permute-start.30 = (bf16[40,2304]{1,0:T(8,128)(2,1)S(1)}, bf16[40,2304]{1,0:T(8,128)(2,1)S(1)}, u32[]{:S(2)}, u32[]{:S(2)}) collective-permute-start(bf16[40,2304]{1,0:T(8,128)(2,1)S(1)} %get-tuple-element.76), channel_id=1, source_target_pairs={{0,2},{1,3},{2,0},{3,1},{4,6},{5,7},{6,4},{7,5},{8,10},{9,11},{10,... | collective-permute-start | bytes 552968 | tf_op jit(solution)/shard_map/ppermute | solution.py:47
  111.8 6.3 %slice-start.11 = ((s8[14680064]{0:T(1024)(128)(4,1)}), s8[2097152]{0:T(1024)(128)(4,1)S(1)}, s32[]{:S(2)}) async-start(s8[14680064]{0:T(1024)(128)(4,1)} %bitcast.128), calls=%async_computation.11 | async-start | bytes 4194304
  116.5 9.3 %collective-permute-start.33 = (bf16[40,1280]{1,0:T(8,128)(2,1)S(1)}, bf16[40,1280]{1,0:T(8,128)(2,1)S(1)}, u32[]{:S(2)}, u32[]{:S(2)}) collective-permute-start(bf16[40,1280]{1,0:T(8,128)(2,1)S(1)} %get-tuple-element.100), channel_id=1, source_target_pairs={{0,2},{1,3},{2,0},{3,1},{4,6},{5,7},{6,4},{7,5},{8,10},{9,11},{10,... | collective-permute-start | bytes 307208 | tf_op jit(solution)/shard_map/ppermute | solution.py:47
  119.6 9.9 %collective-permute-start.27 = (bf16[80,2048]{1,0:T(8,128)(2,1)S(1)}, bf16[80,2048]{1,0:T(8,128)(2,1)S(1)}, u32[]{:S(2)}, u32[]{:S(2)}) collective-permute-start(bf16[80,2048]{1,0:T(8,128)(2,1)S(1)} %slice.512), channel_id=1, source_target_pairs={{0,1},{1,0},{2,3},{3,2},{4,5},{5,4},{6,7},{7,6},{8,9},{9,8},{10,11... | collective-permute-start | bytes 983048 | tf_op jit(solution)/shard_map/ppermute | solution.py:47
  124.6 15.4 %collective-permute-start.31 = (bf16[80,2304]{1,0:T(8,128)(2,1)S(1)}, bf16[80,2304]{1,0:T(8,128)(2,1)S(1)}, u32[]{:S(2)}, u32[]{:S(2)}) collective-permute-start(bf16[80,2304]{1,0:T(8,128)(2,1)S(1)} %pad_maximum_fusion.12), channel_id=1, source_target_pairs={{0,4},{1,0},{2,6},{3,2},{4,5},{5,1},{6,7},{7,3},{8,12},{9,8},{10,1... | collective-permute-start | bytes 1105928 | tf_op jit(solution)/shard_map/ppermute | solution.py:122
  125.1 14.9 %collective-permute-start.32 = (bf16[80,2304]{1,0:T(8,128)(2,1)S(1)}, bf16[80,2304]{1,0:T(8,128)(2,1)S(1)}, u32[]{:S(2)}, u32[]{:S(2)}) collective-permute-start(bf16[80,2304]{1,0:T(8,128)(2,1)S(1)} %pad_maximum_fusion.12), channel_id=1, source_target_pairs={{1,4},{3,6},{4,1},{6,3},{9,12},{11,14},{12,9},{14,11},{17,20},{19,... | collective-permute-start | bytes 1105928 | tf_op jit(solution)/shard_map/ppermute | solution.py:122
  125.8 10.8 %collective-permute-start.34 = (bf16[80,1280]{1,0:T(8,128)(2,1)S(1)}, bf16[80,1280]{1,0:T(8,128)(2,1)S(1)}, u32[]{:S(2)}, u32[]{:S(2)}) collective-permute-start(bf16[80,1280]{1,0:T(8,128)(2,1)S(1)} %pad_maximum_fusion.20), channel_id=1, source_target_pairs={{0,4},{1,0},{2,6},{3,2},{4,5},{5,1},{6,7},{7,3},{8,12},{9,8},{10,1... | collective-permute-start | bytes 614408 | tf_op jit(solution)/shard_map/ppermute | solution.py:122
  128.8 7.8 %collective-permute-start.35 = (bf16[80,1280]{1,0:T(8,128)(2,1)S(1)}, bf16[80,1280]{1,0:T(8,128)(2,1)S(1)}, u32[]{:S(2)}, u32[]{:S(2)}) collective-permute-start(bf16[80,1280]{1,0:T(8,128)(2,1)S(1)} %pad_maximum_fusion.20), channel_id=1, source_target_pairs={{1,4},{3,6},{4,1},{6,3},{9,12},{11,14},{12,9},{14,11},{17,20},{19,... | collective-permute-start | bytes 614408 | tf_op jit(solution)/shard_map/ppermute | solution.py:122
  129.6 10.3 %collective-permute-start.29 = (bf16[80,2048]{1,0:T(8,128)(2,1)S(1)}, bf16[80,2048]{1,0:T(8,128)(2,1)S(1)}, u32[]{:S(2)}, u32[]{:S(2)}) collective-permute-start(bf16[80,2048]{1,0:T(8,128)(2,1)S(1)} %get-tuple-element.63), channel_id=1, source_target_pairs={{0,2},{1,3},{2,0},{3,1},{4,6},{5,7},{6,4},{7,5},{8,10},{9,11},{10,... | collective-permute-start | bytes 983048 | tf_op jit(solution)/shard_map/ppermute | solution.py:47
  141.9 2.2 %collective-permute-start.36 = (bf16[80,2048]{1,0:T(8,128)(2,1)S(1)}, bf16[80,2048]{1,0:T(8,128)(2,1)S(1)}, u32[]{:S(2)}, u32[]{:S(2)}) collective-permute-start(bf16[80,2048]{1,0:T(8,128)(2,1)S(1)} %slice.511), channel_id=1, source_target_pairs={{0,1},{1,0},{2,3},{3,2},{4,5},{5,4},{6,7},{7,6},{8,9},{9,8},{10,11... | collective-permute-start | bytes 983048 | tf_op jit(solution)/shard_map/ppermute | solution.py:47
  144.2 10.1 %collective-permute-start.37 = (bf16[80,2048]{1,0:T(8,128)(2,1)S(1)}, bf16[80,2048]{1,0:T(8,128)(2,1)S(1)}, u32[]{:S(2)}, u32[]{:S(2)}) collective-permute-start(bf16[80,2048]{1,0:T(8,128)(2,1)S(1)} %fusion.40), channel_id=1, source_target_pairs={{0,2},{1,3},{2,0},{3,1},{4,6},{5,7},{6,4},{7,5},{8,10},{9,11},{10,... | collective-permute-start | bytes 983048 | tf_op jit(solution)/shard_map/ppermute | solution.py:47
  145.0 9.4 %copy-start.3 = (bf16[160,2048]{1,0:T(8,128)(2,1)S(1)}, bf16[160,2048]{1,0:T(8,128)(2,1)}, u32[]{:S(2)}) copy-start(bf16[160,2048]{1,0:T(8,128)(2,1)} %copy-done.2) | copy-start | bytes 1966084
  154.4 3.1 %copy-start.1 = (bf16[160,2048]{1,0:T(8,128)(2,1)S(1)}, bf16[160,2048]{1,0:T(8,128)(2,1)}, u32[]{:S(2)}) copy-start(bf16[160,2048]{1,0:T(8,128)(2,1)} %param.5) | copy-start | bytes 1966084
  155.3 2.2 %collective-permute-start.38 = (bf16[160,2048]{1,0:T(8,128)(2,1)S(1)}, bf16[160,2048]{1,0:T(8,128)(2,1)S(1)}, u32[]{:S(2)}, u32[]{:S(2)}) collective-permute-start(bf16[160,2048]{1,0:T(8,128)(2,1)S(1)} %select_convert_fusion), channel_id=1, source_target_pairs={{0,1},{1,0},{2,3},{3,2},{4,5},{5,4},{6,7},{7,6},{8,9},{9,8},{10,11... | collective-permute-start | bytes 1966088 | tf_op jit(solution)/shard_map/ppermute | solution.py:47

commit v13 on v12

--- a/solution.py
+++ b/solution.py
@@ -10,31 +10,37 @@
 HALVES = 2
 PARTS = ((14, 14), (18, 10))
 EDGES = {
+    "t1.pick": ["t0.add"],
     "w.pull": ["t0.columns"],
-    "t1.add": ["t0.halves"],
-    "t1.halves": ["t0.columns"],
+    "t0.cores": ["w.pull"],
+    "t1.columns": ["t0.cores"],
     "c00.dots": ["t1.columns"],
-    "c01.dots": ["c00.dots"],
-    "c00.sum": ["c01.dots"],
-    "c00.hidden": ["c01.sum"],
-    "t1.cores": ["c00.hidden"],
-    "c11.dots": ["c10.dots"],
-    "c01.hidden": ["c11.dots"],
-    "c10.sum": ["c01.hidden"],
-    "c00.halves": ["c10.sum"],
-    "c11.sum": ["c00.halves"],
-    "c01.halves": ["c11.sum"],
-    "c00.columns": ["c01.halves"],
-    "c10.hidden": ["c00.columns"],
-    "c01.columns": ["c10.hidden"],
-    "c11.hidden": ["c01.columns"],
-    "c10.halves": ["c11.hidden"],
-    "c00.cores": ["c10.halves"],
-    "c01.cores": ["c10.halves"],
+    "t1.cores": ["c00.dots"],
+    "c01.dots": ["c00.sum"],
+    "c10.dots": ["c01.sum"],
+    "c00.hidden": ["c10.dots"],
+    "c10.sum": ["c00.halves"],
+    "c01.hidden": ["c10.sum"],
+    "c11.dots": ["c01.hidden"],
+    "c00.columns": ["c11.dots"],
+    "c01.halves": ["c00.columns"],
+    "c10.hidden": ["c01.halves"],
+    "c11.sum": ["c10.hidden"],
+    "c01.columns": ["c11.sum"],
+    "c00.cores": ["c01.columns"],
+    "c10.halves": ["c00.cores"],
+    "c11.hidden": ["c10.halves"],
+    "c00.down": ["c11.hidden"],
+    "c01.cores": ["c00.down"],
+    "c10.columns": ["c01.cores"],
+    "c01.down": ["c10.columns"],
     "c11.halves": ["c01.down"],
-    "b0.total": ["c11.halves"],
-    "c10.cores": ["b0.all"],
+    "c10.cores": ["c11.halves"],
+    "c11.columns": ["c10.down"],
+    "b0.total": ["c11.columns"],
     "c11.cores": ["b0.total"],
+    "c11.down": ["b0.all"],
+    "b1.total": ["c11.down"],
 }
 
 
@@ -105,10 +111,12 @@
     count = jnp.sum(jnp.where(rows == here, lengths[None], 0), axis=1, keepdims=True)
     places = jnp.where(slot < count, slot + first, -1)
     inside = jnp.arange(piece, dtype=jnp.int32)
-    mine = [
-        jnp.concatenate([inside + quarter * c, inside + quarter * (c ^ 2)]) + h * piece
-        for h in range(HALVES)
-    ]
+
+    def mine_of(c):
+        both = jnp.concatenate([inside + quarter * c, inside + quarter * (c ^ 2)])
+        return [both + h * piece for h in range(HALVES)]
+
+    mine = mine_of(c)
 
     devices = [(i // col_count, i % col_count) for i in range(lax.axis_size("row") * col_count)]
 
@@ -170,17 +178,15 @@
         yield
         return issued(name + ".cores", finish(ordered(name + ".cores", pair)))
 
-    picked = {}
-
-    def pick_steps():
-        own = jnp.concatenate(mine)[:, None] == places[0][None]
-        sib = jnp.concatenate(mine)[:, None] == places[1][None]
+    def pick_steps(name, h):
+        spots = ordered(name + ".pick", mine[h])
+        own = spots[:, None] == places[0][None]
+        sib = spots[:, None] == places[1][None]
         rows = dot(own.astype(jnp.bfloat16), tokens) + dot(sib.astype(jnp.bfloat16), sibling)
-        rows = rows.astype(jnp.bfloat16).reshape(HALVES, 2, piece, width)
-        picked["got"] = swap_x(rows[:, 1])
-        picked["rows"] = rows[:, 0]
-        return None
-        yield
+        rows = issued(name + ".pick", rows.astype(jnp.bfloat16))
+        got = swap_x(rows[piece:])
+        yield
+        return issued(name + ".add", ordered(name + ".add", rows[:piece]) + got)
 
     pulled = []
 
@@ -192,7 +198,7 @@
         yield
 
     def half_steps(name, h):
-        own = issued(name + ".add", ordered(name + ".add", picked["rows"][h]) + picked["got"][h])
+        own = yield from pick_steps(name, h)
         return (yield from spread_steps(name, own))
 
     def chunk_steps(name, h, i):
@@ -216,6 +222,7 @@
         gate, up = gate[:piece] + got[0], up[:piece] + got[1]
         hidden = issued(name + ".hidden", (jax.nn.silu(gate) * up).astype(jnp.bfloat16))
         whole = yield from spread_steps(name, hidden)
+        yield
         whole = ordered(name + ".down", whole)
         return issued(name + ".down", dot(whole, down_weight[part]))
 
@@ -230,7 +237,7 @@
         got = ordered(name + ".all", got)
         return issued(name + ".all", total + jnp.concatenate([got[piece:], got[:piece]], axis=0))
 
-    chains = {"p": pick_steps(), "w": pull_steps()}
+    chains = {"w": pull_steps()}
     results = {}
     for h in range(HALVES):
         chains["t" + str(h)] = half_steps("t" + str(h), h)
@@ -249,18 +256,22 @@
             advance(name)
         return results[name]
 
-    result("p")
+    for name in EDGES:
+        while name not in seen:
+            advance(name.split(".")[0])
     for h in range(HALVES):
         result("b" + str(h))
 
-    total = jnp.concatenate([results["b" + str(h)] for h in range(HALVES)])
-    mixed = []
-    for place, known in zip(places, (tokens, sibling)):
-        put = place[:, None] == jnp.concatenate(mine)[None]
-        moved = jnp.dot(put.astype(jnp.float32), total, precision=lax.Precision.HIGHEST)
-        handled = jnp.any(put, axis=1)[:, None]
-        mixed.append(jnp.where(handled, known.astype(jnp.float32) + moved, 0.0).astype(jnp.bfloat16))
-    return mixed[0] + flip(mixed[1], "col", 1)
+    totals = [results["b" + str(h)] for h in range(HALVES)]
+    theirs = [flip(total.astype(jnp.bfloat16), "col", 1) for total in totals]
+    put = places[0][:, None] == jnp.concatenate(mine)[None]
+    moved = jnp.dot(
+        put.astype(jnp.float32), jnp.concatenate(totals), precision=lax.Precision.HIGHEST
+    )
+    put = places[0][:, None] == jnp.concatenate(mine_of(c ^ 1))[None]
+    moved = moved + dot(put.astype(jnp.bfloat16), jnp.concatenate(theirs))
+    used = (places[0] >= 0)[:, None]
+    return jnp.where(used, tokens.astype(jnp.float32) + moved, 0.0).astype(jnp.bfloat16)
 
 
 def general(tokens, lengths, gate_weight, up_weight, down_weight):

time: 160 us -> 146 us (0.912)
  waiting for transfers between devices: 69.6 us -> 55.8 us
  matrix products: 28.4 us -> 25.6 us
  other arithmetic: 5.16 us -> 6.89 us
    ppermute x27 -> x29, waiting for transfers between devices: 62.1 us -> 51.8 us  [flip(): return lax.ppermute(value, axis, [(i, i ^ bit) for i in range(count)])]
    ppermute x12, starting transfers between devices: 11.3 us -> 16.1 us  [move(): return lax.ppermute(value, ('row', 'col'), pairs)]
    ppermute x27 -> x29, starting transfers between devices: 37 us -> 32.9 us  [flip(): return lax.ppermute(value, axis, [(i, i ^ bit) for i in range(count)])]
    ppermute x12, waiting for transfers between devices: 7.48 us -> 3.99 us  [move(): return lax.ppermute(value, ('row', 'col'), pairs)]
    dot_general x2 -> x1, matrix products: 2.79 us -> 0.82 us  [stationary(): jnp.dot(put.astype(jnp.float32), jnp.concatenate(totals), precision=lax.P...]
    dot_general x14 -> x17, matrix products: 25.6 us -> 24.8 us  [dot(): return jnp.dot(a, b, preferred_element_type=jnp.float32)]
  transfers between devices with their start and end apart: 39 -> 41, of which waited for: 16 -> 17; matrix products, arithmetic and copies ran while one was open for 18% -> 18% of each run, Pallas kernels for 4% -> 4%
where the time goes in v13:
time: 146 us; the launch traced here: 145 us
  waiting for transfers between devices  55.8 us (38%)
  starting transfers between devices  49 us (34%)
  matrix products  25.6 us (18%)
  other arithmetic  6.89 us (5%)
  Pallas kernels  5.99 us (4%)
    ppermute x29, waiting for transfers between devices, flip(): return lax.ppermute(value, axis, [(i, i ^ bit) for i in range(count)])  51.8 us
    ppermute x29, starting transfers between devices, flip(): return lax.ppermute(value, axis, [(i, i ^ bit) for i in range(count)])  32.9 us
    dot_general x17, matrix products, dot(): return jnp.dot(a, b, preferred_element_type=jnp.float32)  24.8 us
    ppermute x12, starting transfers between devices, move(): return lax.ppermute(value, ('row', 'col'), pairs)  16.1 us
    pallas_call x1, Pallas kernels, pull(): pl.pallas_call(functools.partial(pull_kernel, first, end), in_specs=[pl.B...  5.99 us
    ppermute x12, waiting for transfers between devices, move(): return lax.ppermute(value, ('row', 'col'), pairs)  3.99 us
  transfers between devices with their start and end apart: 41, of which 17 were waited for; matrix products, arithmetic and copies ran while one was open for 18% of the time, Pallas kernels for 4%

profile of v13, /device:TPU:0, one launch (start us, length us, event | category | flops | bytes accessed | tf_op | source)
XLA Modules:
  0.0 145.3 jit_solution(1683100664879767338)
XLA Ops:
  0.5 0.9 fusion.80
  1.5 1.4 fusion.70
  3.2 2.6 %collective-permute-start.1 = (bf16[40,2048]{1,0:T(8,128)(2,1)S(1)}, bf16[40,2048]{1,0:T(8,128)(2,1)S(1)}, u32[]{:S(2)}, u32[]{:S(2)}) collective-permute-start(bf16[40,2048]{1,0:T(8,128)(2,1)S(1)} %slice.314), channel_id=1, source_target_pairs={{0,2},{1,3},{2,0},{3,1},{4,6},{5,7},{6,4},{7,5},{8,10},{9,11},{10,... | collective-permute-start | bytes 491528 | tf_op jit(solution)/shard_map/ppermute | solution.py:53
  5.8 4.9 %collective-permute-done.1 = bf16[40,2048]{1,0:T(8,128)(2,1)S(1)} collective-permute-done((bf16[40,2048]{1,0:T(8,128)(2,1)S(1)}, bf16[40,2048]{1,0:T(8,128)(2,1)S(1)}, u32[]{:S(2)}, u32[]{:S(2)}) %collective-permute-start.1) | collective-permute-done | bytes 163872 | tf_op jit(solution)/shard_map/ppermute | solution.py:53
  10.7 2.9 %collective-permute-start.2 = (bf16[40,2048]{1,0:T(8,128)(2,1)S(1)}, bf16[40,2048]{1,0:T(8,128)(2,1)S(1)}, u32[]{:S(2)}, u32[]{:S(2)}) collective-permute-start(bf16[40,2048]{1,0:T(8,128)(2,1)S(1)} %slice_add_fusion.19), channel_id=1, source_target_pairs={{0,8},{4,12},{8,0},{12,4},{1,9},{5,13},{9,1},{13,5},{2,10},{6,14},... | collective-permute-start | bytes 491528 | tf_op jit(solution)/shard_map/ppermute | solution.py:53
  14.2 1.6 %collective-permute-start.6 = (bf16[40,2048]{1,0:T(8,128)(2,1)S(1)}, bf16[40,2048]{1,0:T(8,128)(2,1)S(1)}, u32[]{:S(2)}, u32[]{:S(2)}) collective-permute-start(bf16[40,2048]{1,0:T(8,128)(2,1)S(1)} %slice.316), channel_id=1, source_target_pairs={{0,2},{1,3},{2,0},{3,1},{4,6},{5,7},{6,4},{7,5},{8,10},{9,11},{10,... | collective-permute-start | bytes 491528 | tf_op jit(solution)/shard_map/ppermute | solution.py:53
  15.8 5.4 %collective-permute-done.2 = bf16[40,2048]{1,0:T(8,128)(2,1)S(1)} collective-permute-done((bf16[40,2048]{1,0:T(8,128)(2,1)S(1)}, bf16[40,2048]{1,0:T(8,128)(2,1)S(1)}, u32[]{:S(2)}, u32[]{:S(2)}) %collective-permute-start.2) | collective-permute-done | bytes 163872 | tf_op jit(solution)/shard_map/ppermute | solution.py:53
  21.2 1.6 %collective-permute-start.3 = (bf16[40,2048]{1,0:T(8,128)(2,1)S(1)}, bf16[40,2048]{1,0:T(8,128)(2,1)S(1)}, u32[]{:S(2)}, u32[]{:S(2)}) collective-permute-start(bf16[40,2048]{1,0:T(8,128)(2,1)S(1)} %get-tuple-element.104), channel_id=1, source_target_pairs={{0,2},{1,3},{2,0},{3,1},{4,6},{5,7},{6,4},{7,5},{8,10},{9,11},{10,... | collective-permute-start | bytes 491528 | tf_op jit(solution)/shard_map/ppermute | solution.py:53
  22.9 3.7 %collective-permute-done.3 = bf16[40,2048]{1,0:T(8,128)(2,1)S(1)} collective-permute-done((bf16[40,2048]{1,0:T(8,128)(2,1)S(1)}, bf16[40,2048]{1,0:T(8,128)(2,1)S(1)}, u32[]{:S(2)}, u32[]{:S(2)}) %collective-permute-start.3) | collective-permute-done | bytes 163872 | tf_op jit(solution)/shard_map/ppermute | solution.py:53
  26.6 1.6 %collective-permute-start.4 = (bf16[80,2048]{1,0:T(8,128)(2,1)S(1)}, bf16[80,2048]{1,0:T(8,128)(2,1)S(1)}, u32[]{:S(2)}, u32[]{:S(2)}) collective-permute-start(bf16[80,2048]{1,0:T(8,128)(2,1)S(1)} %pad_maximum_fusion.11), channel_id=1, source_target_pairs={{0,4},{1,0},{2,6},{3,2},{4,5},{5,1},{6,7},{7,3},{8,12},{9,8},{10,1... | collective-permute-start | bytes 983048 | tf_op jit(solution)/shard_map/ppermute | solution.py:130
  28.2 0.7 collective-permute-start.5
  28.9 3.5 %collective-permute-done.7 = bf16[40,2048]{1,0:T(8,128)(2,1)S(1)} collective-permute-done((bf16[40,2048]{1,0:T(8,128)(2,1)S(1)}, bf16[40,2048]{1,0:T(8,128)(2,1)S(1)}, u32[]{:S(2)}, u32[]{:S(2)}) %collective-permute-start.7) | collective-permute-done | bytes 163872 | tf_op jit(solution)/shard_map/ppermute | solution.py:53
  33.0 6.0 %shard_map.55 = (bf16[2048,1792]{1,0:T(8,128)(2,1)S(1)}, bf16[2048,1792]{1,0:T(8,128)(2,1)S(1)}) custom-call(s32[4]{0:T(128)S(1)} %copy-done, bf16[2048,3584]{1,0:T(8,128)(2,1)} %gate_ref.1, bf16[2048,3584]{1,0:T(8,128)(2,1)} %up_ref.1), custom_call_target="tpu_custom_call" | custom-call | tf_op jit(solution)/shard_map/pallas_call | solution.py:73
  39.2 1.4 fusion.93
  40.6 1.4 fusion.94
  42.3 1.0 collective-permute-start.12
  43.3 0.9 collective-permute-done.9
  44.4 0.7 pad_maximum_fusion.13
  45.2 1.4 fusion.12
  47.0 1.4 fusion.10
  48.6 0.7 collective-permute-start.13
  49.4 1.5 %collective-permute-start.10 = (bf16[2,40,1792]{2,1,0:T(8,128)(2,1)}, bf16[2,40,1792]{2,1,0:T(8,128)(2,1)}, u32[]{:S(2)}, u32[]{:S(2)}) collective-permute-start(bf16[2,40,1792]{2,1,0:T(8,128)(2,1)} %pad_maximum_fusion.13), channel_id=1, source_target_pairs={{0,2},{1,3},{2,0},{3,1},{4,6},{5,7},{6,4},{7,5},{8,10},{9,11},{10,... | collective-permute-start | bytes 860168 | tf_op jit(solution)/shard_map/ppermute | solution.py:53
  51.0 0.8 pad_maximum_fusion.14
  51.8 1.7 %fusion.4 = f32[160,2304]{1,0:T(8,128)S(1)} fusion(bf16[160,2048]{1,0:T(8,128)(2,1)S(1)} %pad_maximum_fusion.2, bf16[2048,3584]{1,0:T(8,128)(2,1)S(1)} %bitcast.110), kind=kOutput, calls=%fused_computation.4 | convolution fusion | flops 1509949440 | bytes 11567104 | tf_op jit(solution)/shard_map/dot_general | solution.py:48
  53.5 2.9 %fusion.2 = f32[160,2304]{1,0:T(8,128)S(1)} fusion(bf16[160,2048]{1,0:T(8,128)(2,1)} %copy-done.2, bf16[2048,3584]{1,0:T(8,128)(2,1)S(1)} %bitcast.108), kind=kOutput, calls=%fused_computation.2 | convolution fusion | flops 1509949440 | bytes 11567104 | tf_op jit(solution)/shard_map/dot_general | solution.py:48
  56.6 2.8 %collective-permute-start.17 = (bf16[2,80,2304]{2,1,0:T(8,128)(2,1)S(1)}, bf16[2,80,2304]{2,1,0:T(8,128)(2,1)S(1)}, u32[]{:S(2)}, u32[]{:S(2)}) collective-permute-start(bf16[2,80,2304]{2,1,0:T(8,128)(2,1)S(1)} %pad_maximum_fusion), channel_id=1, source_target_pairs={{0,1},{1,0},{2,3},{3,2},{4,5},{5,4},{6,7},{7,6},{8,9},{9,8},{10,11... | collective-permute-start | bytes 2211848 | tf_op jit(solution)/shard_map/ppermute | solution.py:53
  59.4 1.1 fusion.47
  60.5 3.3 %collective-permute-start.14 = (bf16[40,1792]{1,0:T(8,128)(2,1)S(1)}, bf16[40,1792]{1,0:T(8,128)(2,1)S(1)}, u32[]{:S(2)}, u32[]{:S(2)}) collective-permute-start(bf16[40,1792]{1,0:T(8,128)(2,1)S(1)} %fusion.47), channel_id=1, source_target_pairs={{0,8},{4,12},{8,0},{12,4},{1,9},{5,13},{9,1},{13,5},{2,10},{6,14},... | collective-permute-start | bytes 430088 | tf_op jit(solution)/shard_map/ppermute | solution.py:53
  63.8 1.5 %collective-permute-start.16 = (bf16[2,40,1792]{2,1,0:T(8,128)(2,1)S(1)}, bf16[2,40,1792]{2,1,0:T(8,128)(2,1)S(1)}, u32[]{:S(2)}, u32[]{:S(2)}) collective-permute-start(bf16[2,40,1792]{2,1,0:T(8,128)(2,1)S(1)} %copy-done.4), channel_id=1, source_target_pairs={{0,2},{1,3},{2,0},{3,1},{4,6},{5,7},{6,4},{7,5},{8,10},{9,11},{10,... | collective-permute-start | bytes 860168 | tf_op jit(solution)/shard_map/ppermute | solution.py:53
  65.3 5.6 %collective-permute-done.14 = bf16[40,1792]{1,0:T(8,128)(2,1)S(1)} collective-permute-done((bf16[40,1792]{1,0:T(8,128)(2,1)S(1)}, bf16[40,1792]{1,0:T(8,128)(2,1)S(1)}, u32[]{:S(2)}, u32[]{:S(2)}) %collective-permute-start.14) | collective-permute-done | bytes 143392 | tf_op jit(solution)/shard_map/ppermute | solution.py:53
  70.9 1.4 collective-permute-start.15
  72.5 0.8 collective-permute-start.21
  73.5 1.1 fusion.16
  74.6 1.1 fusion.18
  75.9 1.7 %collective-permute-done.15 = bf16[40,1792]{1,0:T(8,128)(2,1)S(1)} collective-permute-done((bf16[40,1792]{1,0:T(8,128)(2,1)S(1)}, bf16[40,1792]{1,0:T(8,128)(2,1)S(1)}, u32[]{:S(2)}, u32[]{:S(2)}) %collective-permute-start.15) | collective-permute-done | bytes 143392 | tf_op jit(solution)/shard_map/ppermute | solution.py:53
  77.6 2.4 %collective-permute-start.22 = (bf16[80,1792]{1,0:T(8,128)(2,1)S(1)}, bf16[80,1792]{1,0:T(8,128)(2,1)S(1)}, u32[]{:S(2)}, u32[]{:S(2)}) collective-permute-start(bf16[80,1792]{1,0:T(8,128)(2,1)S(1)} %pad_maximum_fusion.15), channel_id=1, source_target_pairs={{0,4},{1,0},{2,6},{3,2},{4,5},{5,1},{6,7},{7,3},{8,12},{9,8},{10,1... | collective-permute-start | bytes 860168 | tf_op jit(solution)/shard_map/ppermute | solution.py:130
  80.6 1.7 %collective-permute-done.18 = bf16[40,1792]{1,0:T(8,128)(2,1)S(1)} collective-permute-done((bf16[40,1792]{1,0:T(8,128)(2,1)S(1)}, bf16[40,1792]{1,0:T(8,128)(2,1)S(1)}, u32[]{:S(2)}, u32[]{:S(2)}) %collective-permute-start.18) | collective-permute-done | bytes 143392 | tf_op jit(solution)/shard_map/ppermute | solution.py:53
  82.4 1.4 collective-permute-start.19
  84.6 1.8 %collective-permute-start.24 = (bf16[2,40,1280]{2,1,0:T(8,128)(2,1)S(1)}, bf16[2,40,1280]{2,1,0:T(8,128)(2,1)S(1)}, u32[]{:S(2)}, u32[]{:S(2)}) collective-permute-start(bf16[2,40,1280]{2,1,0:T(8,128)(2,1)S(1)} %pad_maximum_fusion.17), channel_id=1, source_target_pairs={{0,2},{1,3},{2,0},{3,1},{4,6},{5,7},{6,4},{7,5},{8,10},{9,11},{10,... | collective-permute-start | bytes 614408 | tf_op jit(solution)/shard_map/ppermute | solution.py:53
  86.4 2.7 %collective-permute-done.19 = bf16[40,1792]{1,0:T(8,128)(2,1)S(1)} collective-permute-done((bf16[40,1792]{1,0:T(8,128)(2,1)S(1)}, bf16[40,1792]{1,0:T(8,128)(2,1)S(1)}, u32[]{:S(2)}, u32[]{:S(2)}) %collective-permute-start.19) | collective-permute-done | bytes 143392 | tf_op jit(solution)/shard_map/ppermute | solution.py:53
  89.1 1.0 collective-permute-start.26
  90.0 0.7 collective-permute-start.27
  90.9 4.3 %collective-permute-done.25 = bf16[40,2304]{1,0:T(8,128)(2,1)S(1)} collective-permute-done((bf16[40,2304]{1,0:T(8,128)(2,1)S(1)}, bf16[40,2304]{1,0:T(8,128)(2,1)S(1)}, u32[]{:S(2)}, u32[]{:S(2)}) %collective-permute-start.25) | collective-permute-done | bytes 184352 | tf_op jit(solution)/shard_map/ppermute | solution.py:53
  95.1 1.4 collective-permute-start.28
  96.8 4.6 %fusion.8 = f32[160,2048]{1,0:T(8,128)S(1)} fusion(bf16[160,1792]{1,0:T(8,128)(2,1)S(1)} %pad_maximum_fusion.5, bf16[3584,2048]{1,0:T(8,128)(2,1)} %param.9), kind=kOutput, calls=%fused_computation.8 | convolution fusion | flops 1174405120 | bytes 9224192 | tf_op jit(solution)/shard_map/dot_general | solution.py:48
  101.6 2.7 %collective-permute-start.32 = (bf16[80,2304]{1,0:T(8,128)(2,1)S(1)}, bf16[80,2304]{1,0:T(8,128)(2,1)S(1)}, u32[]{:S(2)}, u32[]{:S(2)}) collective-permute-start(bf16[80,2304]{1,0:T(8,128)(2,1)S(1)} %pad_maximum_fusion.10), channel_id=1, source_target_pairs={{0,4},{1,0},{2,6},{3,2},{4,5},{5,1},{6,7},{7,3},{8,12},{9,8},{10,1... | collective-permute-start | bytes 1105928 | tf_op jit(solution)/shard_map/ppermute | solution.py:130
  104.2 0.9 collective-permute-start.33
  105.2 1.5 %fusion.91 = f32[160,2048]{1,0:T(8,128)S(1)} fusion(f32[160,2048]{1,0:T(8,128)S(1)} %fusion.8, bf16[160,1792]{1,0:T(8,128)(2,1)S(1)} %pad_maximum_fusion.6, bf16[3584,2048]{1,0:T(8,128)(2,1)S(1)} %bitcast.119), kind=kOutput, calls=%fused_computation.195 | convolution fusion | flops 1174732800 | bytes 10534912 | tf_op jit(solution)/shard_map/dot_general | solution.py:48
  106.7 1.6 %collective-permute-start.31 = (bf16[40,1280]{1,0:T(8,128)(2,1)S(1)}, bf16[40,1280]{1,0:T(8,128)(2,1)S(1)}, u32[]{:S(2)}, u32[]{:S(2)}) collective-permute-start(bf16[40,1280]{1,0:T(8,128)(2,1)S(1)} %get-tuple-element.116), channel_id=1, source_target_pairs={{0,2},{1,3},{2,0},{3,1},{4,6},{5,7},{6,4},{7,5},{8,10},{9,11},{10,... | collective-permute-start | bytes 307208 | tf_op jit(solution)/shard_map/ppermute | solution.py:53
  108.4 1.2 collective-permute-start.29
  109.5 2.3 %collective-permute-done.32 = bf16[80,2304]{1,0:T(8,128)(2,1)S(1)} collective-permute-done((bf16[80,2304]{1,0:T(8,128)(2,1)S(1)}, bf16[80,2304]{1,0:T(8,128)(2,1)S(1)}, u32[]{:S(2)}, u32[]{:S(2)}) %collective-permute-start.32) | collective-permute-done | bytes 368672 | tf_op jit(solution)/shard_map/ppermute | solution.py:130
  111.9 1.7 %fusion = f32[160,2048]{1,0:T(8,128)S(1)} fusion(bf16[3584,2048]{1,0:T(8,128)(2,1)S(1)} %bitcast.119, bf16[80,2304]{1,0:T(8,128)(2,1)S(1)} %get-tuple-element.90, bf16[80,2304]{1,0:T(8,128)(2,1)S(1)} %get-tuple-element.89), kind=kOutput, calls=%fused_computation | convolution fusion | flops 1511424000 | bytes 11485184 | tf_op jit(solution)/shard_map/dot_general | solution.py:48
  113.7 3.9 %collective-permute-start.35 = (bf16[80,1280]{1,0:T(8,128)(2,1)S(1)}, bf16[80,1280]{1,0:T(8,128)(2,1)S(1)}, u32[]{:S(2)}, u32[]{:S(2)}) collective-permute-start(bf16[80,1280]{1,0:T(8,128)(2,1)S(1)} %pad_maximum_fusion.18), channel_id=1, source_target_pairs={{0,4},{1,0},{2,6},{3,2},{4,5},{5,1},{6,7},{7,3},{8,12},{9,8},{10,1... | collective-permute-start | bytes 614408 | tf_op jit(solution)/shard_map/ppermute | solution.py:130
  118.4 1.6 %collective-permute-start.34 = (bf16[80,2048]{1,0:T(8,128)(2,1)S(1)}, bf16[80,2048]{1,0:T(8,128)(2,1)S(1)}, u32[]{:S(2)}, u32[]{:S(2)}) collective-permute-start(bf16[80,2048]{1,0:T(8,128)(2,1)S(1)} %get-tuple-element.77), channel_id=1, source_target_pairs={{0,2},{1,3},{2,0},{3,1},{4,6},{5,7},{6,4},{7,5},{8,10},{9,11},{10,... | collective-permute-start | bytes 983048 | tf_op jit(solution)/shard_map/ppermute | solution.py:53
  120.0 1.7 %collective-permute-done.35 = bf16[80,1280]{1,0:T(8,128)(2,1)S(1)} collective-permute-done((bf16[80,1280]{1,0:T(8,128)(2,1)S(1)}, bf16[80,1280]{1,0:T(8,128)(2,1)S(1)}, u32[]{:S(2)}, u32[]{:S(2)}) %collective-permute-start.35) | collective-permute-done | bytes 204832 | tf_op jit(solution)/shard_map/ppermute | solution.py:130
  121.8 6.9 %collective-permute-done.34 = bf16[80,2048]{1,0:T(8,128)(2,1)S(1)} collective-permute-done((bf16[80,2048]{1,0:T(8,128)(2,1)S(1)}, bf16[80,2048]{1,0:T(8,128)(2,1)S(1)}, u32[]{:S(2)}, u32[]{:S(2)}) %collective-permute-start.34) | collective-permute-done | bytes 327712 | tf_op jit(solution)/shard_map/ppermute | solution.py:53
  128.7 0.8 fusion.85
  129.6 1.1 fusion.92
  131.0 1.4 collective-permute-done.37
  132.4 1.6 %collective-permute-start.38 = (bf16[80,2048]{1,0:T(8,128)(2,1)S(1)}, bf16[80,2048]{1,0:T(8,128)(2,1)S(1)}, u32[]{:S(2)}, u32[]{:S(2)}) collective-permute-start(bf16[80,2048]{1,0:T(8,128)(2,1)S(1)} %fusion.35), channel_id=1, source_target_pairs={{0,2},{1,3},{2,0},{3,1},{4,6},{5,7},{6,4},{7,5},{8,10},{9,11},{10,... | collective-permute-start | bytes 983048 | tf_op jit(solution)/shard_map/ppermute | solution.py:53
  134.2 8.1 %collective-permute-done.38 = bf16[80,2048]{1,0:T(8,128)(2,1)S(1)} collective-permute-done((bf16[80,2048]{1,0:T(8,128)(2,1)S(1)}, bf16[80,2048]{1,0:T(8,128)(2,1)S(1)}, u32[]{:S(2)}, u32[]{:S(2)}) %collective-permute-start.38) | collective-permute-done | bytes 327712 | tf_op jit(solution)/shard_map/ppermute | solution.py:53
  142.6 0.8 fusion.25
  143.4 0.7 collective-permute-done.40
  144.1 1.3 fusion.22
  (152 shorter events, 8.2 us)
Async XLA Ops:
  0.0 2.9 %collective-permute-start = (bf16[160,2048]{1,0:T(8,128)(2,1)}, bf16[160,2048]{1,0:T(8,128)(2,1)S(1)}, u32[]{:S(2)}, u32[]{:S(2)}) collective-permute-start(bf16[160,2048]{1,0:T(8,128)(2,1)} %param.5), channel_id=1, source_target_pairs={{0,1},{1,0},{2,3},{3,2},{4,5},{5,4},{6,7},{7,6},{8,9},{9,8},{10,11... | collective-permute-start | bytes 1966088 | tf_op jit(solution)/shard_map/ppermute | solution.py:53
  2.9 10.7 %copy-start.1 = (bf16[160,2048]{1,0:T(8,128)(2,1)S(1)}, bf16[160,2048]{1,0:T(8,128)(2,1)}, u32[]{:S(2)}) copy-start(bf16[160,2048]{1,0:T(8,128)(2,1)} %param.5) | copy-start | bytes 1966084
  3.2 7.4 %collective-permute-start.1 = (bf16[40,2048]{1,0:T(8,128)(2,1)S(1)}, bf16[40,2048]{1,0:T(8,128)(2,1)S(1)}, u32[]{:S(2)}, u32[]{:S(2)}) collective-permute-start(bf16[40,2048]{1,0:T(8,128)(2,1)S(1)} %slice.314), channel_id=1, source_target_pairs={{0,2},{1,3},{2,0},{3,1},{4,6},{5,7},{6,4},{7,5},{8,10},{9,11},{10,... | collective-permute-start | bytes 491528 | tf_op jit(solution)/shard_map/ppermute | solution.py:53
  10.7 10.5 %collective-permute-start.2 = (bf16[40,2048]{1,0:T(8,128)(2,1)S(1)}, bf16[40,2048]{1,0:T(8,128)(2,1)S(1)}, u32[]{:S(2)}, u32[]{:S(2)}) collective-permute-start(bf16[40,2048]{1,0:T(8,128)(2,1)S(1)} %slice_add_fusion.19), channel_id=1, source_target_pairs={{0,8},{4,12},{8,0},{12,4},{1,9},{5,13},{9,1},{13,5},{2,10},{6,14},... | collective-permute-start | bytes 491528 | tf_op jit(solution)/shard_map/ppermute | solution.py:53
  14.2 18.8 %copy-start = (s32[4]{0:T(128)S(1)}, s32[4]{0:T(128)}, u32[]{:S(2)}) copy-start(s32[4]{0:T(128)} %tick_ref) | copy-start | bytes 52
  14.2 8.6 %collective-permute-start.6 = (bf16[40,2048]{1,0:T(8,128)(2,1)S(1)}, bf16[40,2048]{1,0:T(8,128)(2,1)S(1)}, u32[]{:S(2)}, u32[]{:S(2)}) collective-permute-start(bf16[40,2048]{1,0:T(8,128)(2,1)S(1)} %slice.316), channel_id=1, source_target_pairs={{0,2},{1,3},{2,0},{3,1},{4,6},{5,7},{6,4},{7,5},{8,10},{9,11},{10,... | collective-permute-start | bytes 491528 | tf_op jit(solution)/shard_map/ppermute | solution.py:53
  21.2 5.4 %collective-permute-start.3 = (bf16[40,2048]{1,0:T(8,128)(2,1)S(1)}, bf16[40,2048]{1,0:T(8,128)(2,1)S(1)}, u32[]{:S(2)}, u32[]{:S(2)}) collective-permute-start(bf16[40,2048]{1,0:T(8,128)(2,1)S(1)} %get-tuple-element.104), channel_id=1, source_target_pairs={{0,2},{1,3},{2,0},{3,1},{4,6},{5,7},{6,4},{7,5},{8,10},{9,11},{10,... | collective-permute-start | bytes 491528 | tf_op jit(solution)/shard_map/ppermute | solution.py:53
  22.8 9.5 %collective-permute-start.7 = (bf16[40,2048]{1,0:T(8,128)(2,1)S(1)}, bf16[40,2048]{1,0:T(8,128)(2,1)S(1)}, u32[]{:S(2)}, u32[]{:S(2)}) collective-permute-start(bf16[40,2048]{1,0:T(8,128)(2,1)S(1)} %slice_add_fusion.18), channel_id=1, source_target_pairs={{0,8},{4,12},{8,0},{12,4},{1,9},{5,13},{9,1},{13,5},{2,10},{6,14},... | collective-permute-start | bytes 491528 | tf_op jit(solution)/shard_map/ppermute | solution.py:53
  26.6 12.4 %collective-permute-start.4 = (bf16[80,2048]{1,0:T(8,128)(2,1)S(1)}, bf16[80,2048]{1,0:T(8,128)(2,1)S(1)}, u32[]{:S(2)}, u32[]{:S(2)}) collective-permute-start(bf16[80,2048]{1,0:T(8,128)(2,1)S(1)} %pad_maximum_fusion.11), channel_id=1, source_target_pairs={{0,4},{1,0},{2,6},{3,2},{4,5},{5,1},{6,7},{7,3},{8,12},{9,8},{10,1... | collective-permute-start | bytes 983048 | tf_op jit(solution)/shard_map/ppermute | solution.py:130
  28.2 10.8 %collective-permute-start.5 = (bf16[80,2048]{1,0:T(8,128)(2,1)S(1)}, bf16[80,2048]{1,0:T(8,128)(2,1)S(1)}, u32[]{:S(2)}, u32[]{:S(2)}) collective-permute-start(bf16[80,2048]{1,0:T(8,128)(2,1)S(1)} %pad_maximum_fusion.11), channel_id=1, source_target_pairs={{1,4},{3,6},{4,1},{6,3},{9,12},{11,14},{12,9},{14,11},{17,20},{19,... | collective-permute-start | bytes 983048 | tf_op jit(solution)/shard_map/ppermute | solution.py:130
  32.4 6.8 %collective-permute-start.8 = (bf16[40,2048]{1,0:T(8,128)(2,1)S(1)}, bf16[40,2048]{1,0:T(8,128)(2,1)S(1)}, u32[]{:S(2)}, u32[]{:S(2)}) collective-permute-start(bf16[40,2048]{1,0:T(8,128)(2,1)S(1)} %get-tuple-element.100), channel_id=1, source_target_pairs={{0,2},{1,3},{2,0},{3,1},{4,6},{5,7},{6,4},{7,5},{8,10},{9,11},{10,... | collective-permute-start | bytes 491528 | tf_op jit(solution)/shard_map/ppermute | solution.py:53
  33.0 12.2 %slice-start.4 = ((s8[14680064]{0:T(1024)(128)(4,1)}), s8[4194304]{0:T(1024)(128)(4,1)S(1)}, s32[]{:S(2)}) async-start(s8[14680064]{0:T(1024)(128)(4,1)} %bitcast.109), calls=%async_computation.4 | async-start | bytes 8388608
  33.0 12.2 %slice-start.5 = ((s8[14680064]{0:T(1024)(128)(4,1)}), s8[4194304]{0:T(1024)(128)(4,1)S(1)}, s32[]{:S(2)}) async-start(s8[14680064]{0:T(1024)(128)(4,1)} %bitcast.109), calls=%async_computation.5 | async-start | bytes 8388608
  39.2 6.0 %slice-start.6 = ((s8[14680064]{0:T(1024)(128)(4,1)}), s8[4194304]{0:T(1024)(128)(4,1)S(1)}, s32[]{:S(2)}) async-start(s8[14680064]{0:T(1024)(128)(4,1)} %bitcast.109), calls=%async_computation.6 | async-start | bytes 8388608
  40.6 4.6 %slice-start.7 = ((s8[14680064]{0:T(1024)(128)(4,1)}), s8[2097152]{0:T(1024)(128)(4,1)S(1)}, s32[]{:S(2)}) async-start(s8[14680064]{0:T(1024)(128)(4,1)} %bitcast.109), calls=%async_computation.7 | async-start | bytes 4194304
  40.6 6.0 %slice-start = ((s8[14680064]{0:T(1024)(128)(4,1)}), s8[4194304]{0:T(1024)(128)(4,1)S(1)}, s32[]{:S(2)}) async-start(s8[14680064]{0:T(1024)(128)(4,1)} %bitcast.107), calls=%async_computation | async-start | bytes 8388608
  40.6 6.0 %slice-start.1 = ((s8[14680064]{0:T(1024)(128)(4,1)}), s8[4194304]{0:T(1024)(128)(4,1)S(1)}, s32[]{:S(2)}) async-start(s8[14680064]{0:T(1024)(128)(4,1)} %bitcast.107), calls=%async_computation.1 | async-start | bytes 8388608
  42.1 4.6 %slice-start.2 = ((s8[14680064]{0:T(1024)(128)(4,1)}), s8[4194304]{0:T(1024)(128)(4,1)S(1)}, s32[]{:S(2)}) async-start(s8[14680064]{0:T(1024)(128)(4,1)} %bitcast.107), calls=%async_computation.2 | async-start | bytes 8388608
  42.2 2.0 %collective-permute-start.9 = (bf16[2,80,1792]{2,1,0:T(8,128)(2,1)S(1)}, bf16[2,80,1792]{2,1,0:T(8,128)(2,1)S(1)}, u32[]{:S(2)}, u32[]{:S(2)}) collective-permute-start(bf16[2,80,1792]{2,1,0:T(8,128)(2,1)S(1)} %pad_maximum_fusion.3), channel_id=1, source_target_pairs={{0,1},{1,0},{2,3},{3,2},{4,5},{5,4},{6,7},{7,6},{8,9},{9,8},{10,11... | collective-permute-start | bytes 1720328 | tf_op jit(solution)/shard_map/ppermute | solution.py:53
  42.3 7.0 %collective-permute-start.11 = (bf16[80,2048]{1,0:T(8,128)(2,1)S(1)}, bf16[80,2048]{1,0:T(8,128)(2,1)S(1)}, u32[]{:S(2)}, u32[]{:S(2)}) collective-permute-start(bf16[80,2048]{1,0:T(8,128)(2,1)S(1)} %pad_maximum_fusion.12), channel_id=1, source_target_pairs={{0,4},{1,0},{2,6},{3,2},{4,5},{5,1},{6,7},{7,3},{8,12},{9,8},{10,1... | collective-permute-start | bytes 983048 | tf_op jit(solution)/shard_map/ppermute | solution.py:130
  42.3 6.9 %collective-permute-start.12 = (bf16[80,2048]{1,0:T(8,128)(2,1)S(1)}, bf16[80,2048]{1,0:T(8,128)(2,1)S(1)}, u32[]{:S(2)}, u32[]{:S(2)}) collective-permute-start(bf16[80,2048]{1,0:T(8,128)(2,1)S(1)} %pad_maximum_fusion.12), channel_id=1, source_target_pairs={{1,4},{3,6},{4,1},{6,3},{9,12},{11,14},{12,9},{14,11},{17,20},{19,... | collective-permute-start | bytes 983048 | tf_op jit(solution)/shard_map/ppermute | solution.py:130
  45.2 1.8 %slice-start.3 = ((s8[14680064]{0:T(1024)(128)(4,1)}), s8[2097152]{0:T(1024)(128)(4,1)S(1)}, s32[]{:S(2)}) async-start(s8[14680064]{0:T(1024)(128)(4,1)} %bitcast.107), calls=%async_computation.3 | async-start | bytes 4194304
  48.6 2.3 %collective-permute-start.13 = (bf16[2,80,1792]{2,1,0:T(8,128)(2,1)S(1)}, bf16[2,80,1792]{2,1,0:T(8,128)(2,1)S(1)}, u32[]{:S(2)}, u32[]{:S(2)}) collective-permute-start(bf16[2,80,1792]{2,1,0:T(8,128)(2,1)S(1)} %pad_maximum_fusion.4), channel_id=1, source_target_pairs={{0,1},{1,0},{2,3},{3,2},{4,5},{5,4},{6,7},{7,6},{8,9},{9,8},{10,11... | collective-permute-start | bytes 1720328 | tf_op jit(solution)/shard_map/ppermute | solution.py:53
  49.4 2.4 %copy-start.2 = (bf16[160,2048]{1,0:T(8,128)(2,1)}, bf16[160,2048]{1,0:T(8,128)(2,1)S(1)}, u32[]{:S(2)}) copy-start(bf16[160,2048]{1,0:T(8,128)(2,1)S(1)} %pad_maximum_fusion.2) | copy-start | bytes 1966084
  49.4 10.0 %collective-permute-start.10 = (bf16[2,40,1792]{2,1,0:T(8,128)(2,1)}, bf16[2,40,1792]{2,1,0:T(8,128)(2,1)}, u32[]{:S(2)}, u32[]{:S(2)}) collective-permute-start(bf16[2,40,1792]{2,1,0:T(8,128)(2,1)} %pad_maximum_fusion.13), channel_id=1, source_target_pairs={{0,2},{1,3},{2,0},{3,1},{4,6},{5,7},{6,4},{7,5},{8,10},{9,11},{10,... | collective-permute-start | bytes 860168 | tf_op jit(solution)/shard_map/ppermute | solution.py:53
  56.5 7.3 %copy-start.4 = (bf16[2,40,1792]{2,1,0:T(8,128)(2,1)S(1)}, bf16[2,40,1792]{2,1,0:T(8,128)(2,1)}, u32[]{:S(2)}) copy-start(bf16[2,40,1792]{2,1,0:T(8,128)(2,1)} %pad_maximum_fusion.14) | copy-start | bytes 860164
  56.6 15.7 %collective-permute-start.17 = (bf16[2,80,2304]{2,1,0:T(8,128)(2,1)S(1)}, bf16[2,80,2304]{2,1,0:T(8,128)(2,1)S(1)}, u32[]{:S(2)}, u32[]{:S(2)}) collective-permute-start(bf16[2,80,2304]{2,1,0:T(8,128)(2,1)S(1)} %pad_maximum_fusion), channel_id=1, source_target_pairs={{0,1},{1,0},{2,3},{3,2},{4,5},{5,4},{6,7},{7,6},{8,9},{9,8},{10,11... | collective-permute-start | bytes 2211848 | tf_op jit(solution)/shard_map/ppermute | solution.py:53
  60.5 10.4 %collective-permute-start.14 = (bf16[40,1792]{1,0:T(8,128)(2,1)S(1)}, bf16[40,1792]{1,0:T(8,128)(2,1)S(1)}, u32[]{:S(2)}, u32[]{:S(2)}) collective-permute-start(bf16[40,1792]{1,0:T(8,128)(2,1)S(1)} %fusion.47), channel_id=1, source_target_pairs={{0,8},{4,12},{8,0},{12,4},{1,9},{5,13},{9,1},{13,5},{2,10},{6,14},... | collective-permute-start | bytes 430088 | tf_op jit(solution)/shard_map/ppermute | solution.py:53
  63.8 9.6 %collective-permute-start.16 = (bf16[2,40,1792]{2,1,0:T(8,128)(2,1)S(1)}, bf16[2,40,1792]{2,1,0:T(8,128)(2,1)S(1)}, u32[]{:S(2)}, u32[]{:S(2)}) collective-permute-start(bf16[2,40,1792]{2,1,0:T(8,128)(2,1)S(1)} %copy-done.4), channel_id=1, source_target_pairs={{0,2},{1,3},{2,0},{3,1},{4,6},{5,7},{6,4},{7,5},{8,10},{9,11},{10,... | collective-permute-start | bytes 860168 | tf_op jit(solution)/shard_map/ppermute | solution.py:53
  70.9 6.7 %collective-permute-start.15 = (bf16[40,1792]{1,0:T(8,128)(2,1)S(1)}, bf16[40,1792]{1,0:T(8,128)(2,1)S(1)}, u32[]{:S(2)}, u32[]{:S(2)}) collective-permute-start(bf16[40,1792]{1,0:T(8,128)(2,1)S(1)} %get-tuple-element.112), channel_id=1, source_target_pairs={{0,2},{1,3},{2,0},{3,1},{4,6},{5,7},{6,4},{7,5},{8,10},{9,11},{10,... | collective-permute-start | bytes 430088 | tf_op jit(solution)/shard_map/ppermute | solution.py:53
  72.4 1.1 copy-start.3
  72.5 11.6 %collective-permute-start.21 = (bf16[2,40,2304]{2,1,0:T(8,128)(2,1)S(1)}, bf16[2,40,2304]{2,1,0:T(8,128)(2,1)S(1)}, u32[]{:S(2)}, u32[]{:S(2)}) collective-permute-start(bf16[2,40,2304]{2,1,0:T(8,128)(2,1)S(1)} %pad_maximum_fusion.9), channel_id=1, source_target_pairs={{0,2},{1,3},{2,0},{3,1},{4,6},{5,7},{6,4},{7,5},{8,10},{9,11},{10,... | collective-permute-start | bytes 1105928 | tf_op jit(solution)/shard_map/ppermute | solution.py:53
  73.4 8.9 %collective-permute-start.18 = (bf16[40,1792]{1,0:T(8,128)(2,1)S(1)}, bf16[40,1792]{1,0:T(8,128)(2,1)S(1)}, u32[]{:S(2)}, u32[]{:S(2)}) collective-permute-start(bf16[40,1792]{1,0:T(8,128)(2,1)S(1)} %fusion.45), channel_id=1, source_target_pairs={{0,8},{4,12},{8,0},{12,4},{1,9},{5,13},{9,1},{13,5},{2,10},{6,14},... | collective-permute-start | bytes 430088 | tf_op jit(solution)/shard_map/ppermute | solution.py:53
  74.6 30.5 %slice-start.8 = ((s8[14680064]{0:T(1024)(128)(4,1)}), s8[2097152]{0:T(1024)(128)(4,1)S(1)}, s32[]{:S(2)}) async-start(s8[14680064]{0:T(1024)(128)(4,1)} %bitcast.118), calls=%async_computation.8 | async-start | bytes 4194304
  75.7 29.4 %slice-start.9 = ((s8[14680064]{0:T(1024)(128)(4,1)}), s8[4194304]{0:T(1024)(128)(4,1)S(1)}, s32[]{:S(2)}) async-start(s8[14680064]{0:T(1024)(128)(4,1)} %bitcast.118), calls=%async_computation.9 | async-start | bytes 8388608
  75.8 8.6 %collective-permute-start.20 = (bf16[2,80,1280]{2,1,0:T(8,128)(2,1)S(1)}, bf16[2,80,1280]{2,1,0:T(8,128)(2,1)S(1)}, u32[]{:S(2)}, u32[]{:S(2)}) collective-permute-start(bf16[2,80,1280]{2,1,0:T(8,128)(2,1)S(1)} %pad_maximum_fusion.7), channel_id=1, source_target_pairs={{0,1},{1,0},{2,3},{3,2},{4,5},{5,4},{6,7},{7,6},{8,9},{9,8},{10,11... | collective-permute-start | bytes 1228808 | tf_op jit(solution)/shard_map/ppermute | solution.py:53
  77.6 12.4 %collective-permute-start.22 = (bf16[80,1792]{1,0:T(8,128)(2,1)S(1)}, bf16[80,1792]{1,0:T(8,128)(2,1)S(1)}, u32[]{:S(2)}, u32[]{:S(2)}) collective-permute-start(bf16[80,1792]{1,0:T(8,128)(2,1)S(1)} %pad_maximum_fusion.15), channel_id=1, source_target_pairs={{0,4},{1,0},{2,6},{3,2},{4,5},{5,1},{6,7},{7,3},{8,12},{9,8},{10,1... | collective-permute-start | bytes 860168 | tf_op jit(solution)/shard_map/ppermute | solution.py:130
  80.0 10.8 %collective-permute-start.23 = (bf16[80,1792]{1,0:T(8,128)(2,1)S(1)}, bf16[80,1792]{1,0:T(8,128)(2,1)S(1)}, u32[]{:S(2)}, u32[]{:S(2)}) collective-permute-start(bf16[80,1792]{1,0:T(8,128)(2,1)S(1)} %pad_maximum_fusion.15), channel_id=1, source_target_pairs={{1,4},{3,6},{4,1},{6,3},{9,12},{11,14},{12,9},{14,11},{17,20},{19,... | collective-permute-start | bytes 860168 | tf_op jit(solution)/shard_map/ppermute | solution.py:130
  82.4 6.7 %collective-permute-start.19 = (bf16[40,1792]{1,0:T(8,128)(2,1)S(1)}, bf16[40,1792]{1,0:T(8,128)(2,1)S(1)}, u32[]{:S(2)}, u32[]{:S(2)}) collective-permute-start(bf16[40,1792]{1,0:T(8,128)(2,1)S(1)} %get-tuple-element.110), channel_id=1, source_target_pairs={{0,2},{1,3},{2,0},{3,1},{4,6},{5,7},{6,4},{7,5},{8,10},{9,11},{10,... | collective-permute-start | bytes 430088 | tf_op jit(solution)/shard_map/ppermute | solution.py:53
  84.3 10.8 %collective-permute-start.25 = (bf16[40,2304]{1,0:T(8,128)(2,1)S(1)}, bf16[40,2304]{1,0:T(8,128)(2,1)S(1)}, u32[]{:S(2)}, u32[]{:S(2)}) collective-permute-start(bf16[40,2304]{1,0:T(8,128)(2,1)S(1)} %fusion.39), channel_id=1, source_target_pairs={{0,8},{4,12},{8,0},{12,4},{1,9},{5,13},{9,1},{13,5},{2,10},{6,14},... | collective-permute-start | bytes 552968 | tf_op jit(solution)/shard_map/ppermute | solution.py:53
  84.6 12.0 %collective-permute-start.24 = (bf16[2,40,1280]{2,1,0:T(8,128)(2,1)S(1)}, bf16[2,40,1280]{2,1,0:T(8,128)(2,1)S(1)}, u32[]{:S(2)}, u32[]{:S(2)}) collective-permute-start(bf16[2,40,1280]{2,1,0:T(8,128)(2,1)S(1)} %pad_maximum_fusion.17), channel_id=1, source_target_pairs={{0,2},{1,3},{2,0},{3,1},{4,6},{5,7},{6,4},{7,5},{8,10},{9,11},{10,... | collective-permute-start | bytes 614408 | tf_op jit(solution)/shard_map/ppermute | solution.py:53
  89.1 12.3 %collective-permute-start.26 = (bf16[80,1792]{1,0:T(8,128)(2,1)S(1)}, bf16[80,1792]{1,0:T(8,128)(2,1)S(1)}, u32[]{:S(2)}, u32[]{:S(2)}) collective-permute-start(bf16[80,1792]{1,0:T(8,128)(2,1)S(1)} %pad_maximum_fusion.16), channel_id=1, source_target_pairs={{0,4},{1,0},{2,6},{3,2},{4,5},{5,1},{6,7},{7,3},{8,12},{9,8},{10,1... | collective-permute-start | bytes 860168 | tf_op jit(solution)/shard_map/ppermute | solution.py:130
  90.0 11.4 %collective-permute-start.27 = (bf16[80,1792]{1,0:T(8,128)(2,1)S(1)}, bf16[80,1792]{1,0:T(8,128)(2,1)S(1)}, u32[]{:S(2)}, u32[]{:S(2)}) collective-permute-start(bf16[80,1792]{1,0:T(8,128)(2,1)S(1)} %pad_maximum_fusion.16), channel_id=1, source_target_pairs={{1,4},{3,6},{4,1},{6,3},{9,12},{11,14},{12,9},{14,11},{17,20},{19,... | collective-permute-start | bytes 860168 | tf_op jit(solution)/shard_map/ppermute | solution.py:130
  90.8 14.3 %slice-start.10 = ((s8[14680064]{0:T(1024)(128)(4,1)}), s8[4194304]{0:T(1024)(128)(4,1)S(1)}, s32[]{:S(2)}) async-start(s8[14680064]{0:T(1024)(128)(4,1)} %bitcast.118), calls=%async_computation.10 | async-start | bytes 8388608
  95.1 6.4 %collective-permute-start.28 = (bf16[40,2304]{1,0:T(8,128)(2,1)S(1)}, bf16[40,2304]{1,0:T(8,128)(2,1)S(1)}, u32[]{:S(2)}, u32[]{:S(2)}) collective-permute-start(bf16[40,2304]{1,0:T(8,128)(2,1)S(1)} %get-tuple-element.92), channel_id=1, source_target_pairs={{0,2},{1,3},{2,0},{3,1},{4,6},{5,7},{6,4},{7,5},{8,10},{9,11},{10,... | collective-permute-start | bytes 552968 | tf_op jit(solution)/shard_map/ppermute | solution.py:53
  96.7 8.5 %slice-start.11 = ((s8[14680064]{0:T(1024)(128)(4,1)}), s8[4194304]{0:T(1024)(128)(4,1)S(1)}, s32[]{:S(2)}) async-start(s8[14680064]{0:T(1024)(128)(4,1)} %bitcast.118), calls=%async_computation.11 | async-start | bytes 8388608
  96.7 10.0 %collective-permute-start.30 = (bf16[40,1280]{1,0:T(8,128)(2,1)S(1)}, bf16[40,1280]{1,0:T(8,128)(2,1)S(1)}, u32[]{:S(2)}, u32[]{:S(2)}) collective-permute-start(bf16[40,1280]{1,0:T(8,128)(2,1)S(1)} %fusion.51), channel_id=1, source_target_pairs={{0,8},{4,12},{8,0},{12,4},{1,9},{5,13},{9,1},{13,5},{2,10},{6,14},... | collective-permute-start | bytes 307208 | tf_op jit(solution)/shard_map/ppermute | solution.py:53
  101.6 10.3 %collective-permute-start.32 = (bf16[80,2304]{1,0:T(8,128)(2,1)S(1)}, bf16[80,2304]{1,0:T(8,128)(2,1)S(1)}, u32[]{:S(2)}, u32[]{:S(2)}) collective-permute-start(bf16[80,2304]{1,0:T(8,128)(2,1)S(1)} %pad_maximum_fusion.10), channel_id=1, source_target_pairs={{0,4},{1,0},{2,6},{3,2},{4,5},{5,1},{6,7},{7,3},{8,12},{9,8},{10,1... | collective-permute-start | bytes 1105928 | tf_op jit(solution)/shard_map/ppermute | solution.py:130
  104.2 7.6 %collective-permute-start.33 = (bf16[80,2304]{1,0:T(8,128)(2,1)S(1)}, bf16[80,2304]{1,0:T(8,128)(2,1)S(1)}, u32[]{:S(2)}, u32[]{:S(2)}) collective-permute-start(bf16[80,2304]{1,0:T(8,128)(2,1)S(1)} %pad_maximum_fusion.10), channel_id=1, source_target_pairs={{1,4},{3,6},{4,1},{6,3},{9,12},{11,14},{12,9},{14,11},{17,20},{19,... | collective-permute-start | bytes 1105928 | tf_op jit(solution)/shard_map/ppermute | solution.py:130
  106.7 7.0 %collective-permute-start.31 = (bf16[40,1280]{1,0:T(8,128)(2,1)S(1)}, bf16[40,1280]{1,0:T(8,128)(2,1)S(1)}, u32[]{:S(2)}, u32[]{:S(2)}) collective-permute-start(bf16[40,1280]{1,0:T(8,128)(2,1)S(1)} %get-tuple-element.116), channel_id=1, source_target_pairs={{0,2},{1,3},{2,0},{3,1},{4,6},{5,7},{6,4},{7,5},{8,10},{9,11},{10,... | collective-permute-start | bytes 307208 | tf_op jit(solution)/shard_map/ppermute | solution.py:53
  108.4 9.9 %collective-permute-start.29 = (bf16[80,2048]{1,0:T(8,128)(2,1)S(1)}, bf16[80,2048]{1,0:T(8,128)(2,1)S(1)}, u32[]{:S(2)}, u32[]{:S(2)}) collective-permute-start(bf16[80,2048]{1,0:T(8,128)(2,1)S(1)} %slice.504), channel_id=1, source_target_pairs={{0,1},{1,0},{2,3},{3,2},{4,5},{5,4},{6,7},{7,6},{8,9},{9,8},{10,11... | collective-permute-start | bytes 983048 | tf_op jit(solution)/shard_map/ppermute | solution.py:53
  113.7 8.0 %collective-permute-start.35 = (bf16[80,1280]{1,0:T(8,128)(2,1)S(1)}, bf16[80,1280]{1,0:T(8,128)(2,1)S(1)}, u32[]{:S(2)}, u32[]{:S(2)}) collective-permute-start(bf16[80,1280]{1,0:T(8,128)(2,1)S(1)} %pad_maximum_fusion.18), channel_id=1, source_target_pairs={{0,4},{1,0},{2,6},{3,2},{4,5},{5,1},{6,7},{7,3},{8,12},{9,8},{10,1... | collective-permute-start | bytes 614408 | tf_op jit(solution)/shard_map/ppermute | solution.py:130
  117.6 4.1 %collective-permute-start.36 = (bf16[80,1280]{1,0:T(8,128)(2,1)S(1)}, bf16[80,1280]{1,0:T(8,128)(2,1)S(1)}, u32[]{:S(2)}, u32[]{:S(2)}) collective-permute-start(bf16[80,1280]{1,0:T(8,128)(2,1)S(1)} %pad_maximum_fusion.18), channel_id=1, source_target_pairs={{1,4},{3,6},{4,1},{6,3},{9,12},{11,14},{12,9},{14,11},{17,20},{19,... | collective-permute-start | bytes 614408 | tf_op jit(solution)/shard_map/ppermute | solution.py:130
  118.4 10.3 %collective-permute-start.34 = (bf16[80,2048]{1,0:T(8,128)(2,1)S(1)}, bf16[80,2048]{1,0:T(8,128)(2,1)S(1)}, u32[]{:S(2)}, u32[]{:S(2)}) collective-permute-start(bf16[80,2048]{1,0:T(8,128)(2,1)S(1)} %get-tuple-element.77), channel_id=1, source_target_pairs={{0,2},{1,3},{2,0},{3,1},{4,6},{5,7},{6,4},{7,5},{8,10},{9,11},{10,... | collective-permute-start | bytes 983048 | tf_op jit(solution)/shard_map/ppermute | solution.py:53
  130.7 1.7 %collective-permute-start.37 = (bf16[80,2048]{1,0:T(8,128)(2,1)S(1)}, bf16[80,2048]{1,0:T(8,128)(2,1)S(1)}, u32[]{:S(2)}, u32[]{:S(2)}) collective-permute-start(bf16[80,2048]{1,0:T(8,128)(2,1)S(1)} %slice.503), channel_id=1, source_target_pairs={{0,1},{1,0},{2,3},{3,2},{4,5},{5,4},{6,7},{7,6},{8,9},{9,8},{10,11... | collective-permute-start | bytes 983048 | tf_op jit(solution)/shard_map/ppermute | solution.py:53
  132.4 9.8 %collective-permute-start.38 = (bf16[80,2048]{1,0:T(8,128)(2,1)S(1)}, bf16[80,2048]{1,0:T(8,128)(2,1)S(1)}, u32[]{:S(2)}, u32[]{:S(2)}) collective-permute-start(bf16[80,2048]{1,0:T(8,128)(2,1)S(1)} %fusion.35), channel_id=1, source_target_pairs={{0,2},{1,3},{2,0},{3,1},{4,6},{5,7},{6,4},{7,5},{8,10},{9,11},{10,... | collective-permute-start | bytes 983048 | tf_op jit(solution)/shard_map/ppermute | solution.py:53
  134.2 9.2 %collective-permute-start.39 = (bf16[80,2048]{1,0:T(8,128)(2,1)}, bf16[80,2048]{1,0:T(8,128)(2,1)S(1)}, u32[]{:S(2)}, u32[]{:S(2)}) collective-permute-start(bf16[80,2048]{1,0:T(8,128)(2,1)} %get-tuple-element.73), channel_id=1, source_target_pairs={{0,1},{1,0},{2,3},{3,2},{4,5},{5,4},{6,7},{7,6},{8,9},{9,8},{10,11... | collective-permute-start | bytes 983048 | tf_op jit(solution)/shard_map/ppermute | solution.py:53
  142.4 1.7 %collective-permute-start.40 = (bf16[80,2048]{1,0:T(8,128)(2,1)S(1)}, bf16[80,2048]{1,0:T(8,128)(2,1)S(1)}, u32[]{:S(2)}, u32[]{:S(2)}) collective-permute-start(bf16[80,2048]{1,0:T(8,128)(2,1)S(1)} %get-tuple-element.75), channel_id=1, source_target_pairs={{0,1},{1,0},{2,3},{3,2},{4,5},{5,4},{6,7},{7,6},{8,9},{9,8},{10,11... | collective-permute-start | bytes 983048 | tf_op jit(solution)/shard_map/ppermute | solution.py:53

commit v14 on v13

--- a/solution.py
+++ b/solution.py
@@ -8,39 +8,44 @@
 from jax.sharding import PartitionSpec as P
 
 HALVES = 2
-PARTS = ((14, 14), (18, 10))
+PIECES = (1, 1)
+PARTS = ((14, 14), (12, 10, 6))
 EDGES = {
     "t1.pick": ["t0.add"],
-    "w.pull": ["t0.columns"],
+    "t1.halves": ["t0.columns"],
+    "w.pull": ["t1.halves"],
     "t0.cores": ["w.pull"],
     "t1.columns": ["t0.cores"],
     "c00.dots": ["t1.columns"],
     "t1.cores": ["c00.dots"],
     "c01.dots": ["c00.sum"],
-    "c10.dots": ["c01.sum"],
-    "c00.hidden": ["c10.dots"],
+    "c10.dots": ["c01.dots"],
+    "c01.sum": ["c10.dots"],
+    "c00.hidden": ["c01.sum"],
     "c10.sum": ["c00.halves"],
     "c01.hidden": ["c10.sum"],
     "c11.dots": ["c01.hidden"],
     "c00.columns": ["c11.dots"],
     "c01.halves": ["c00.columns"],
-    "c10.hidden": ["c01.halves"],
+    "c12.dots": ["c01.halves"],
+    "c10.hidden": ["c12.dots"],
     "c11.sum": ["c10.hidden"],
     "c01.columns": ["c11.sum"],
     "c00.cores": ["c01.columns"],
-    "c10.halves": ["c00.cores"],
+    "c12.sum": ["c00.down"],
+    "c10.halves": ["c12.sum"],
     "c11.hidden": ["c10.halves"],
-    "c00.down": ["c11.hidden"],
-    "c01.cores": ["c00.down"],
-    "c10.columns": ["c01.cores"],
+    "c01.cores": ["c11.hidden"],
+    "c12.hidden": ["c01.cores"],
+    "c10.columns": ["c12.hidden"],
     "c01.down": ["c10.columns"],
-    "c11.halves": ["c01.down"],
-    "c10.cores": ["c11.halves"],
-    "c11.columns": ["c10.down"],
-    "b0.total": ["c11.columns"],
-    "c11.cores": ["b0.total"],
-    "c11.down": ["b0.all"],
-    "b1.total": ["c11.down"],
+    "b0.total": ["c11.halves"],
+    "c10.cores": ["b0.total"],
+    "c12.halves": ["c10.down"],
+    "c11.columns": ["c12.halves"],
+    "c12.columns": ["c11.cores"],
+    "c12.cores": ["c11.down"],
+    "b1.total": ["c12.down"],
 }
 
 
@@ -95,8 +100,7 @@
     r = lax.axis_index("row")
     x, k, zh, zl = c // 2, c % 2, r // 2, r % 2
     quarter = slots // 2
-    piece = quarter // HALVES
-    half = 2 * piece
+    pieces = [quarter * share // sum(PIECES) for share in PIECES]
     spans = []
     for sizes in PARTS:
         ends = [0]
@@ -110,11 +114,12 @@
     first = jnp.sum(jnp.where(rows < here, lengths[None], 0), axis=1, keepdims=True)
     count = jnp.sum(jnp.where(rows == here, lengths[None], 0), axis=1, keepdims=True)
     places = jnp.where(slot < count, slot + first, -1)
-    inside = jnp.arange(piece, dtype=jnp.int32)
-
     def mine_of(c):
-        both = jnp.concatenate([inside + quarter * c, inside + quarter * (c ^ 2)])
-        return [both + h * piece for h in range(HALVES)]
+        found = []
+        for h, piece in enumerate(pieces):
+            inside = jnp.arange(piece, dtype=jnp.int32) + sum(pieces[:h])
+            found.append(jnp.concatenate([inside + quarter * c, inside + quarter * (c ^ 2)]))
+        return found
 
     mine = mine_of(c)
 
@@ -179,6 +184,7 @@
         return issued(name + ".cores", finish(ordered(name + ".cores", pair)))
 
     def pick_steps(name, h):
+        piece = pieces[h]
         spots = ordered(name + ".pick", mine[h])
         own = spots[:, None] == places[0][None]
         sib = spots[:, None] == places[1][None]
@@ -204,6 +210,7 @@
     def chunk_steps(name, h, i):
         full = result("t" + str(h))
         part = slice(*spans[h][i])
+        piece, half = pieces[h], 2 * pieces[h]
         full = ordered(name + ".dots", full)
         if (h, i) == (0, 0):
             result("w")
@@ -228,6 +235,7 @@
 
     def branch_steps(name, h):
         parts = [result("c" + str(h) + str(i)) for i in range(len(spans[h]))]
+        piece, half = pieces[h], 2 * pieces[h]
         branch = issued(name + ".branch", sum(parts[1:], parts[0]))
         got = flip(branch[half:].astype(jnp.bfloat16), "col", 1)
         yield

time: 146 us -> 152 us (1.041)
  starting transfers between devices: 49 us -> 65.7 us
  waiting for transfers between devices: 55.8 us -> 41.6 us
  matrix products: 25.6 us -> 30.8 us
    ppermute x29 -> x33, waiting for transfers between devices: 51.8 us -> 34.5 us  [flip(): return lax.ppermute(value, axis, [(i, i ^ bit) for i in range(count)])]
    ppermute x12 -> x14, starting transfers between devices: 16.1 us -> 29.8 us  [move(): return lax.ppermute(value, ('row', 'col'), pairs)]
    dot_general x17 -> x20, matrix products: 24.8 us -> 29.9 us  [dot(): return jnp.dot(a, b, preferred_element_type=jnp.float32)]
    ppermute x12 -> x14, waiting for transfers between devices: 3.99 us -> 7.06 us  [move(): return lax.ppermute(value, ('row', 'col'), pairs)]
    ppermute x29 -> x33, starting transfers between devices: 32.9 us -> 35.9 us  [flip(): return lax.ppermute(value, axis, [(i, i ^ bit) for i in range(count)])]
  transfers between devices with their start and end apart: 41 -> 47, of which waited for: 17 -> 16; matrix products, arithmetic and copies ran while one was open for 18% -> 23% of each run, Pallas kernels for 4% -> 4%
where the time goes in v14:
time: 152 us
  starting transfers between devices  65.7 us (43%)
  waiting for transfers between devices  41.6 us (27%)
  matrix products  30.8 us (20%)
  other arithmetic  5.92 us (4%)
  Pallas kernels  5.84 us (4%)
    ppermute x33, starting transfers between devices, flip(): return lax.ppermute(value, axis, [(i, i ^ bit) for i in range(count)])  35.9 us
    ppermute x33, waiting for transfers between devices, flip(): return lax.ppermute(value, axis, [(i, i ^ bit) for i in range(count)])  34.5 us
    dot_general x20, matrix products, dot(): return jnp.dot(a, b, preferred_element_type=jnp.float32)  29.9 us
    ppermute x14, starting transfers between devices, move(): return lax.ppermute(value, ('row', 'col'), pairs)  29.8 us
    ppermute x14, waiting for transfers between devices, move(): return lax.ppermute(value, ('row', 'col'), pairs)  7.06 us
    pallas_call x1, Pallas kernels, pull(): pl.pallas_call(functools.partial(pull_kernel, first, end), in_specs=[pl.B...  5.84 us
  transfers between devices with their start and end apart: 47, of which 16 were waited for; matrix products, arithmetic and copies ran while one was open for 23% of the time, Pallas kernels for 4%

profile of v14, /device:TPU:0, one launch (start us, length us, event | category | flops | bytes accessed | tf_op | source)
XLA Modules:
  0.0 151.6 jit_solution(17059814714647383278)
XLA Ops:
  0.5 0.9 fusion.101
  1.5 1.4 fusion.89
  3.2 2.6 %collective-permute-start.1 = (bf16[40,2048]{1,0:T(8,128)(2,1)S(1)}, bf16[40,2048]{1,0:T(8,128)(2,1)S(1)}, u32[]{:S(2)}, u32[]{:S(2)}) collective-permute-start(bf16[40,2048]{1,0:T(8,128)(2,1)S(1)} %slice.378), channel_id=1, source_target_pairs={{0,2},{1,3},{2,0},{3,1},{4,6},{5,7},{6,4},{7,5},{8,10},{9,11},{10,... | collective-permute-start | bytes 491528 | tf_op jit(solution)/shard_map/ppermute | solution.py:58
  5.9 4.7 %collective-permute-done.1 = bf16[40,2048]{1,0:T(8,128)(2,1)S(1)} collective-permute-done((bf16[40,2048]{1,0:T(8,128)(2,1)S(1)}, bf16[40,2048]{1,0:T(8,128)(2,1)S(1)}, u32[]{:S(2)}, u32[]{:S(2)}) %collective-permute-start.1) | collective-permute-done | bytes 163872 | tf_op jit(solution)/shard_map/ppermute | solution.py:58
  10.7 2.9 %collective-permute-start.2 = (bf16[40,2048]{1,0:T(8,128)(2,1)S(1)}, bf16[40,2048]{1,0:T(8,128)(2,1)S(1)}, u32[]{:S(2)}, u32[]{:S(2)}) collective-permute-start(bf16[40,2048]{1,0:T(8,128)(2,1)S(1)} %slice_add_fusion.21), channel_id=1, source_target_pairs={{0,8},{4,12},{8,0},{12,4},{1,9},{5,13},{9,1},{13,5},{2,10},{6,14},... | collective-permute-start | bytes 491528 | tf_op jit(solution)/shard_map/ppermute | solution.py:58
  14.2 1.6 %collective-permute-start.4 = (bf16[40,2048]{1,0:T(8,128)(2,1)S(1)}, bf16[40,2048]{1,0:T(8,128)(2,1)S(1)}, u32[]{:S(2)}, u32[]{:S(2)}) collective-permute-start(bf16[40,2048]{1,0:T(8,128)(2,1)S(1)} %slice.380), channel_id=1, source_target_pairs={{0,2},{1,3},{2,0},{3,1},{4,6},{5,7},{6,4},{7,5},{8,10},{9,11},{10,... | collective-permute-start | bytes 491528 | tf_op jit(solution)/shard_map/ppermute | solution.py:58
  15.8 5.4 %collective-permute-done.2 = bf16[40,2048]{1,0:T(8,128)(2,1)S(1)} collective-permute-done((bf16[40,2048]{1,0:T(8,128)(2,1)S(1)}, bf16[40,2048]{1,0:T(8,128)(2,1)S(1)}, u32[]{:S(2)}, u32[]{:S(2)}) %collective-permute-start.2) | collective-permute-done | bytes 163872 | tf_op jit(solution)/shard_map/ppermute | solution.py:58
  21.2 1.6 %collective-permute-start.3 = (bf16[40,2048]{1,0:T(8,128)(2,1)S(1)}, bf16[40,2048]{1,0:T(8,128)(2,1)S(1)}, u32[]{:S(2)}, u32[]{:S(2)}) collective-permute-start(bf16[40,2048]{1,0:T(8,128)(2,1)S(1)} %get-tuple-element.106), channel_id=1, source_target_pairs={{0,2},{1,3},{2,0},{3,1},{4,6},{5,7},{6,4},{7,5},{8,10},{9,11},{10,... | collective-permute-start | bytes 491528 | tf_op jit(solution)/shard_map/ppermute | solution.py:58
  22.9 3.7 %collective-permute-done.3 = bf16[40,2048]{1,0:T(8,128)(2,1)S(1)} collective-permute-done((bf16[40,2048]{1,0:T(8,128)(2,1)S(1)}, bf16[40,2048]{1,0:T(8,128)(2,1)S(1)}, u32[]{:S(2)}, u32[]{:S(2)}) %collective-permute-start.3) | collective-permute-done | bytes 163872 | tf_op jit(solution)/shard_map/ppermute | solution.py:58
  26.6 0.7 collective-permute-start.7
  27.3 2.8 %collective-permute-start.6 = (bf16[80,2048]{1,0:T(8,128)(2,1)S(1)}, bf16[80,2048]{1,0:T(8,128)(2,1)S(1)}, u32[]{:S(2)}, u32[]{:S(2)}) collective-permute-start(bf16[80,2048]{1,0:T(8,128)(2,1)S(1)} %pad_maximum_fusion.8), channel_id=1, source_target_pairs={{0,4},{1,0},{2,6},{3,2},{4,5},{5,1},{6,7},{7,3},{8,12},{9,8},{10,1... | collective-permute-start | bytes 983048 | tf_op jit(solution)/shard_map/ppermute | solution.py:135
  30.1 2.2 %collective-permute-done.5 = bf16[40,2048]{1,0:T(8,128)(2,1)S(1)} collective-permute-done((bf16[40,2048]{1,0:T(8,128)(2,1)S(1)}, bf16[40,2048]{1,0:T(8,128)(2,1)S(1)}, u32[]{:S(2)}, u32[]{:S(2)}) %collective-permute-start.5) | collective-permute-done | bytes 163872 | tf_op jit(solution)/shard_map/ppermute | solution.py:58
  32.8 5.8 %shard_map.55 = (bf16[2048,1792]{1,0:T(8,128)(2,1)S(1)}, bf16[2048,1792]{1,0:T(8,128)(2,1)S(1)}) custom-call(s32[4]{0:T(128)S(1)} %copy-done, bf16[2048,3584]{1,0:T(8,128)(2,1)} %gate_ref.1, bf16[2048,3584]{1,0:T(8,128)(2,1)} %up_ref.1), custom_call_target="tpu_custom_call" | custom-call | tf_op jit(solution)/shard_map/pallas_call | solution.py:78
  38.9 0.7 collective-permute-start.13
  39.6 3.3 %collective-permute-start.12 = (bf16[80,2048]{1,0:T(8,128)(2,1)S(1)}, bf16[80,2048]{1,0:T(8,128)(2,1)S(1)}, u32[]{:S(2)}, u32[]{:S(2)}) collective-permute-start(bf16[80,2048]{1,0:T(8,128)(2,1)S(1)} %pad_maximum_fusion.9), channel_id=1, source_target_pairs={{0,4},{1,0},{2,6},{3,2},{4,5},{5,1},{6,7},{7,3},{8,12},{9,8},{10,1... | collective-permute-start | bytes 983048 | tf_op jit(solution)/shard_map/ppermute | solution.py:135
  42.8 1.4 fusion.118
  44.2 1.4 fusion.119
  45.8 3.7 %collective-permute-done.12 = bf16[80,2048]{1,0:T(8,128)(2,1)S(1)} collective-permute-done((bf16[80,2048]{1,0:T(8,128)(2,1)S(1)}, bf16[80,2048]{1,0:T(8,128)(2,1)S(1)}, u32[]{:S(2)}, u32[]{:S(2)}) %collective-permute-start.12) | collective-permute-done | bytes 327712 | tf_op jit(solution)/shard_map/ppermute | solution.py:135
  49.9 1.6 %collective-permute-start.10 = (bf16[2,40,1792]{2,1,0:T(8,128)(2,1)S(1)}, bf16[2,40,1792]{2,1,0:T(8,128)(2,1)S(1)}, u32[]{:S(2)}, u32[]{:S(2)}) collective-permute-start(bf16[2,40,1792]{2,1,0:T(8,128)(2,1)S(1)} %pad_maximum_fusion.10), channel_id=1, source_target_pairs={{0,2},{1,3},{2,0},{3,1},{4,6},{5,7},{6,4},{7,5},{8,10},{9,11},{10,... | collective-permute-start | bytes 860168 | tf_op jit(solution)/shard_map/ppermute | solution.py:58
  51.5 1.4 fusion.4
  52.9 1.4 fusion.6
  54.4 0.8 collective-permute-start.11
  55.2 1.2 fusion.10
  56.4 1.2 fusion.12
  57.7 0.9 pad_maximum_fusion.5
  59.3 3.8 %collective-permute-start.14 = (bf16[40,1792]{1,0:T(8,128)(2,1)S(1)}, bf16[40,1792]{1,0:T(8,128)(2,1)S(1)}, u32[]{:S(2)}, u32[]{:S(2)}) collective-permute-start(bf16[40,1792]{1,0:T(8,128)(2,1)S(1)} %fusion.55), channel_id=1, source_target_pairs={{0,8},{4,12},{8,0},{12,4},{1,9},{5,13},{9,1},{13,5},{2,10},{6,14},... | collective-permute-start | bytes 430088 | tf_op jit(solution)/shard_map/ppermute | solution.py:58
  63.3 1.6 %collective-permute-start.16 = (bf16[2,40,1792]{2,1,0:T(8,128)(2,1)S(1)}, bf16[2,40,1792]{2,1,0:T(8,128)(2,1)S(1)}, u32[]{:S(2)}, u32[]{:S(2)}) collective-permute-start(bf16[2,40,1792]{2,1,0:T(8,128)(2,1)S(1)} %pad_maximum_fusion.11), channel_id=1, source_target_pairs={{0,2},{1,3},{2,0},{3,1},{4,6},{5,7},{6,4},{7,5},{8,10},{9,11},{10,... | collective-permute-start | bytes 860168 | tf_op jit(solution)/shard_map/ppermute | solution.py:58
  64.8 5.3 %collective-permute-done.14 = bf16[40,1792]{1,0:T(8,128)(2,1)S(1)} collective-permute-done((bf16[40,1792]{1,0:T(8,128)(2,1)S(1)}, bf16[40,1792]{1,0:T(8,128)(2,1)S(1)}, u32[]{:S(2)}, u32[]{:S(2)}) %collective-permute-start.14) | collective-permute-done | bytes 143392 | tf_op jit(solution)/shard_map/ppermute | solution.py:58
  70.2 1.6 %collective-permute-start.15 = (bf16[40,1792]{1,0:T(8,128)(2,1)S(1)}, bf16[40,1792]{1,0:T(8,128)(2,1)S(1)}, u32[]{:S(2)}, u32[]{:S(2)}) collective-permute-start(bf16[40,1792]{1,0:T(8,128)(2,1)S(1)} %get-tuple-element.114), channel_id=1, source_target_pairs={{0,2},{1,3},{2,0},{3,1},{4,6},{5,7},{6,4},{7,5},{8,10},{9,11},{10,... | collective-permute-start | bytes 430088 | tf_op jit(solution)/shard_map/ppermute | solution.py:58
  71.8 1.3 slice_add_fusion.7
  74.0 3.5 %fusion.16 = f32[160,1280]{1,0:T(8,128)S(1)} fusion(bf16[160,2048]{1,0:T(8,128)(2,1)S(1)} %pad_maximum_fusion.1, bf16[2048,3584]{1,0:T(8,128)(2,1)} %up_ref.1), kind=kOutput, calls=%fused_computation.16 | convolution fusion | flops 838860800 | bytes 6717440 | tf_op jit(solution)/shard_map/dot_general | solution.py:53
  77.5 3.7 %fusion.18 = f32[160,1280]{1,0:T(8,128)S(1)} fusion(bf16[160,2048]{1,0:T(8,128)(2,1)S(1)} %pad_maximum_fusion.1, bf16[2048,3584]{1,0:T(8,128)(2,1)} %gate_ref.1), kind=kOutput, calls=%fused_computation.18 | convolution fusion | flops 838860800 | bytes 6717440 | tf_op jit(solution)/shard_map/dot_general | solution.py:53
  81.3 0.8 collective-permute-start.23
  82.1 5.6 %collective-permute-start.22 = (bf16[80,1792]{1,0:T(8,128)(2,1)S(1)}, bf16[80,1792]{1,0:T(8,128)(2,1)S(1)}, u32[]{:S(2)}, u32[]{:S(2)}) collective-permute-start(bf16[80,1792]{1,0:T(8,128)(2,1)S(1)} %pad_maximum_fusion.12), channel_id=1, source_target_pairs={{0,4},{1,0},{2,6},{3,2},{4,5},{5,1},{6,7},{7,3},{8,12},{9,8},{10,1... | collective-permute-start | bytes 860168 | tf_op jit(solution)/shard_map/ppermute | solution.py:135
  87.9 0.8 collective-permute-start.19
  88.7 3.0 %fusion.22 = f32[160,768]{1,0:T(8,128)S(1)} fusion(bf16[160,2048]{1,0:T(8,128)(2,1)S(1)} %pad_maximum_fusion.1, bf16[2048,3584]{1,0:T(8,128)(2,1)} %up_ref.1), kind=kOutput, calls=%fused_computation.22 | convolution fusion | flops 503316480 | bytes 4292608 | tf_op jit(solution)/shard_map/dot_general | solution.py:53
  91.7 2.7 %fusion.24 = f32[160,768]{1,0:T(8,128)S(1)} fusion(bf16[160,2048]{1,0:T(8,128)(2,1)S(1)} %pad_maximum_fusion.1, bf16[2048,3584]{1,0:T(8,128)(2,1)} %gate_ref.1), kind=kOutput, calls=%fused_computation.24 | convolution fusion | flops 503316480 | bytes 4292608 | tf_op jit(solution)/shard_map/dot_general | solution.py:53
  95.2 1.2 collective-permute-start.24
  97.1 2.7 %collective-permute-start.27 = (bf16[80,1792]{1,0:T(8,128)(2,1)S(1)}, bf16[80,1792]{1,0:T(8,128)(2,1)S(1)}, u32[]{:S(2)}, u32[]{:S(2)}) collective-permute-start(bf16[80,1792]{1,0:T(8,128)(2,1)S(1)} %pad_maximum_fusion.13), channel_id=1, source_target_pairs={{0,4},{1,0},{2,6},{3,2},{4,5},{5,1},{6,7},{7,3},{8,12},{9,8},{10,1... | collective-permute-start | bytes 860168 | tf_op jit(solution)/shard_map/ppermute | solution.py:135
  99.9 1.4 fusion.2
  101.4 1.2 collective-permute-start.30
  102.6 1.5 %collective-permute-done.25 = bf16[40,1536]{1,0:T(8,128)(2,1)S(1)} collective-permute-done((bf16[40,1536]{1,0:T(8,128)(2,1)S(1)}, bf16[40,1536]{1,0:T(8,128)(2,1)S(1)}, u32[]{:S(2)}, u32[]{:S(2)}) %collective-permute-start.25) | collective-permute-done | bytes 122912 | tf_op jit(solution)/shard_map/ppermute | solution.py:58
  104.2 1.0 collective-permute-start.29
  105.2 1.3 collective-permute-start.32
  106.9 3.7 %collective-permute-start.37 = (bf16[40,768]{1,0:T(8,128)(2,1)S(1)}, bf16[40,768]{1,0:T(8,128)(2,1)S(1)}, u32[]{:S(2)}, u32[]{:S(2)}) collective-permute-start(bf16[40,768]{1,0:T(8,128)(2,1)S(1)} %fusion.78), channel_id=1, source_target_pairs={{0,8},{4,12},{8,0},{12,4},{1,9},{5,13},{9,1},{13,5},{2,10},{6,14},... | collective-permute-start | bytes 184328 | tf_op jit(solution)/shard_map/ppermute | solution.py:58
  111.2 3.7 %collective-permute-start.34 = (bf16[80,1536]{1,0:T(8,128)(2,1)S(1)}, bf16[80,1536]{1,0:T(8,128)(2,1)S(1)}, u32[]{:S(2)}, u32[]{:S(2)}) collective-permute-start(bf16[80,1536]{1,0:T(8,128)(2,1)S(1)} %pad_maximum_fusion.16), channel_id=1, source_target_pairs={{0,4},{1,0},{2,6},{3,2},{4,5},{5,1},{6,7},{7,3},{8,12},{9,8},{10,1... | collective-permute-start | bytes 737288 | tf_op jit(solution)/shard_map/ppermute | solution.py:135
  114.9 1.4 fusion.28
  116.5 1.2 collective-permute-start.36
  118.2 1.7 %collective-permute-done.34 = bf16[80,1536]{1,0:T(8,128)(2,1)S(1)} collective-permute-done((bf16[80,1536]{1,0:T(8,128)(2,1)S(1)}, bf16[80,1536]{1,0:T(8,128)(2,1)S(1)}, u32[]{:S(2)}, u32[]{:S(2)}) %collective-permute-start.34) | collective-permute-done | bytes 245792 | tf_op jit(solution)/shard_map/ppermute | solution.py:135
  120.0 1.2 fusion.8
  121.2 0.9 collective-permute-start.40
  122.8 4.7 %collective-permute-start.38 = (bf16[80,1280]{1,0:T(8,128)(2,1)S(1)}, bf16[80,1280]{1,0:T(8,128)(2,1)S(1)}, u32[]{:S(2)}, u32[]{:S(2)}) collective-permute-start(bf16[80,1280]{1,0:T(8,128)(2,1)S(1)} %pad_maximum_fusion.18), channel_id=1, source_target_pairs={{0,4},{1,0},{2,6},{3,2},{4,5},{5,1},{6,7},{7,3},{8,12},{9,8},{10,1... | collective-permute-start | bytes 614408 | tf_op jit(solution)/shard_map/ppermute | solution.py:135
  127.6 0.9 collective-permute-start.33
  129.2 2.1 %collective-permute-start.41 = (bf16[80,768]{1,0:T(8,128)(2,1)S(1)}, bf16[80,768]{1,0:T(8,128)(2,1)S(1)}, u32[]{:S(2)}, u32[]{:S(2)}) collective-permute-start(bf16[80,768]{1,0:T(8,128)(2,1)S(1)} %pad_maximum_fusion.20), channel_id=1, source_target_pairs={{0,4},{1,0},{2,6},{3,2},{4,5},{5,1},{6,7},{7,3},{8,12},{9,8},{10,1... | collective-permute-start | bytes 368648 | tf_op jit(solution)/shard_map/ppermute | solution.py:135
  131.9 1.0 fusion.14
  132.9 1.1 collective-permute-done.41
  134.1 0.8 add_add_fusion
  134.9 2.2 %collective-permute-start.43 = (bf16[80,2048]{1,0:T(8,128)(2,1)S(1)}, bf16[80,2048]{1,0:T(8,128)(2,1)S(1)}, u32[]{:S(2)}, u32[]{:S(2)}) collective-permute-start(bf16[80,2048]{1,0:T(8,128)(2,1)S(1)} %slice.603), channel_id=1, source_target_pairs={{0,1},{1,0},{2,3},{3,2},{4,5},{5,4},{6,7},{7,6},{8,9},{9,8},{10,11... | collective-permute-start | bytes 983048 | tf_op jit(solution)/shard_map/ppermute | solution.py:58
  137.2 1.2 collective-permute-done.43
  138.5 1.0 collective-permute-start.44
  139.7 8.8 %collective-permute-done.44 = bf16[80,2048]{1,0:T(8,128)(2,1)S(1)} collective-permute-done((bf16[80,2048]{1,0:T(8,128)(2,1)S(1)}, bf16[80,2048]{1,0:T(8,128)(2,1)S(1)}, u32[]{:S(2)}, u32[]{:S(2)}) %collective-permute-start.44) | collective-permute-done | bytes 327712 | tf_op jit(solution)/shard_map/ppermute | solution.py:58
  148.8 0.8 fusion.34
  149.7 0.7 collective-permute-done.46
  150.4 1.3 fusion.31
  (176 shorter events, 11.2 us)
Async XLA Ops:
  0.0 13.6 %copy-start.1 = (bf16[160,2048]{1,0:T(8,128)(2,1)S(1)}, bf16[160,2048]{1,0:T(8,128)(2,1)}, u32[]{:S(2)}) copy-start(bf16[160,2048]{1,0:T(8,128)(2,1)} %param.5) | copy-start | bytes 1966084
  0.0 2.9 %collective-permute-start = (bf16[160,2048]{1,0:T(8,128)(2,1)}, bf16[160,2048]{1,0:T(8,128)(2,1)S(1)}, u32[]{:S(2)}, u32[]{:S(2)}) collective-permute-start(bf16[160,2048]{1,0:T(8,128)(2,1)} %param.5), channel_id=1, source_target_pairs={{0,1},{1,0},{2,3},{3,2},{4,5},{5,4},{6,7},{7,6},{8,9},{9,8},{10,11... | collective-permute-start | bytes 1966088 | tf_op jit(solution)/shard_map/ppermute | solution.py:58
  3.2 7.4 %collective-permute-start.1 = (bf16[40,2048]{1,0:T(8,128)(2,1)S(1)}, bf16[40,2048]{1,0:T(8,128)(2,1)S(1)}, u32[]{:S(2)}, u32[]{:S(2)}) collective-permute-start(bf16[40,2048]{1,0:T(8,128)(2,1)S(1)} %slice.378), channel_id=1, source_target_pairs={{0,2},{1,3},{2,0},{3,1},{4,6},{5,7},{6,4},{7,5},{8,10},{9,11},{10,... | collective-permute-start | bytes 491528 | tf_op jit(solution)/shard_map/ppermute | solution.py:58
  5.9 27.0 %copy-start = (s32[4]{0:T(128)S(1)}, s32[4]{0:T(128)}, u32[]{:S(2)}) copy-start(s32[4]{0:T(128)} %tick_ref) | copy-start | bytes 52
  10.7 10.4 %collective-permute-start.2 = (bf16[40,2048]{1,0:T(8,128)(2,1)S(1)}, bf16[40,2048]{1,0:T(8,128)(2,1)S(1)}, u32[]{:S(2)}, u32[]{:S(2)}) collective-permute-start(bf16[40,2048]{1,0:T(8,128)(2,1)S(1)} %slice_add_fusion.21), channel_id=1, source_target_pairs={{0,8},{4,12},{8,0},{12,4},{1,9},{5,13},{9,1},{13,5},{2,10},{6,14},... | collective-permute-start | bytes 491528 | tf_op jit(solution)/shard_map/ppermute | solution.py:58
  14.2 8.6 %collective-permute-start.4 = (bf16[40,2048]{1,0:T(8,128)(2,1)S(1)}, bf16[40,2048]{1,0:T(8,128)(2,1)S(1)}, u32[]{:S(2)}, u32[]{:S(2)}) collective-permute-start(bf16[40,2048]{1,0:T(8,128)(2,1)S(1)} %slice.380), channel_id=1, source_target_pairs={{0,2},{1,3},{2,0},{3,1},{4,6},{5,7},{6,4},{7,5},{8,10},{9,11},{10,... | collective-permute-start | bytes 491528 | tf_op jit(solution)/shard_map/ppermute | solution.py:58
  21.2 5.4 %collective-permute-start.3 = (bf16[40,2048]{1,0:T(8,128)(2,1)S(1)}, bf16[40,2048]{1,0:T(8,128)(2,1)S(1)}, u32[]{:S(2)}, u32[]{:S(2)}) collective-permute-start(bf16[40,2048]{1,0:T(8,128)(2,1)S(1)} %get-tuple-element.106), channel_id=1, source_target_pairs={{0,2},{1,3},{2,0},{3,1},{4,6},{5,7},{6,4},{7,5},{8,10},{9,11},{10,... | collective-permute-start | bytes 491528 | tf_op jit(solution)/shard_map/ppermute | solution.py:58
  22.8 9.5 %collective-permute-start.5 = (bf16[40,2048]{1,0:T(8,128)(2,1)S(1)}, bf16[40,2048]{1,0:T(8,128)(2,1)S(1)}, u32[]{:S(2)}, u32[]{:S(2)}) collective-permute-start(bf16[40,2048]{1,0:T(8,128)(2,1)S(1)} %slice_add_fusion.20), channel_id=1, source_target_pairs={{0,8},{4,12},{8,0},{12,4},{1,9},{5,13},{9,1},{13,5},{2,10},{6,14},... | collective-permute-start | bytes 491528 | tf_op jit(solution)/shard_map/ppermute | solution.py:58
  26.6 12.1 %collective-permute-start.7 = (bf16[80,2048]{1,0:T(8,128)(2,1)S(1)}, bf16[80,2048]{1,0:T(8,128)(2,1)S(1)}, u32[]{:S(2)}, u32[]{:S(2)}) collective-permute-start(bf16[80,2048]{1,0:T(8,128)(2,1)S(1)} %pad_maximum_fusion.8), channel_id=1, source_target_pairs={{1,4},{3,6},{4,1},{6,3},{9,12},{11,14},{12,9},{14,11},{17,20},{19,... | collective-permute-start | bytes 983048 | tf_op jit(solution)/shard_map/ppermute | solution.py:135
  27.3 11.4 %collective-permute-start.6 = (bf16[80,2048]{1,0:T(8,128)(2,1)S(1)}, bf16[80,2048]{1,0:T(8,128)(2,1)S(1)}, u32[]{:S(2)}, u32[]{:S(2)}) collective-permute-start(bf16[80,2048]{1,0:T(8,128)(2,1)S(1)} %pad_maximum_fusion.8), channel_id=1, source_target_pairs={{0,4},{1,0},{2,6},{3,2},{4,5},{5,1},{6,7},{7,3},{8,12},{9,8},{10,1... | collective-permute-start | bytes 983048 | tf_op jit(solution)/shard_map/ppermute | solution.py:135
  32.3 6.5 %collective-permute-start.8 = (bf16[40,2048]{1,0:T(8,128)(2,1)S(1)}, bf16[40,2048]{1,0:T(8,128)(2,1)S(1)}, u32[]{:S(2)}, u32[]{:S(2)}) collective-permute-start(bf16[40,2048]{1,0:T(8,128)(2,1)S(1)} %get-tuple-element.102), channel_id=1, source_target_pairs={{0,2},{1,3},{2,0},{3,1},{4,6},{5,7},{6,4},{7,5},{8,10},{9,11},{10,... | collective-permute-start | bytes 491528 | tf_op jit(solution)/shard_map/ppermute | solution.py:58
  38.9 7.0 %collective-permute-start.13 = (bf16[80,2048]{1,0:T(8,128)(2,1)S(1)}, bf16[80,2048]{1,0:T(8,128)(2,1)S(1)}, u32[]{:S(2)}, u32[]{:S(2)}) collective-permute-start(bf16[80,2048]{1,0:T(8,128)(2,1)S(1)} %pad_maximum_fusion.9), channel_id=1, source_target_pairs={{1,4},{3,6},{4,1},{6,3},{9,12},{11,14},{12,9},{14,11},{17,20},{19,... | collective-permute-start | bytes 983048 | tf_op jit(solution)/shard_map/ppermute | solution.py:135
  39.6 10.0 %collective-permute-start.12 = (bf16[80,2048]{1,0:T(8,128)(2,1)S(1)}, bf16[80,2048]{1,0:T(8,128)(2,1)S(1)}, u32[]{:S(2)}, u32[]{:S(2)}) collective-permute-start(bf16[80,2048]{1,0:T(8,128)(2,1)S(1)} %pad_maximum_fusion.9), channel_id=1, source_target_pairs={{0,4},{1,0},{2,6},{3,2},{4,5},{5,1},{6,7},{7,3},{8,12},{9,8},{10,1... | collective-permute-start | bytes 983048 | tf_op jit(solution)/shard_map/ppermute | solution.py:135
  42.8 8.7 %slice-start = ((s8[14680064]{0:T(1024)(128)(4,1)}), s8[4194304]{0:T(1024)(128)(4,1)S(1)}, s32[]{:S(2)}) async-start(s8[14680064]{0:T(1024)(128)(4,1)} %bitcast.123), calls=%async_computation | async-start | bytes 8388608
  42.8 8.7 %slice-start.1 = ((s8[14680064]{0:T(1024)(128)(4,1)}), s8[2097152]{0:T(1024)(128)(4,1)S(1)}, s32[]{:S(2)}) async-start(s8[14680064]{0:T(1024)(128)(4,1)} %bitcast.123), calls=%async_computation.1 | async-start | bytes 4194304
  44.2 7.3 %slice-start.2 = ((s8[14680064]{0:T(1024)(128)(4,1)}), s8[4194304]{0:T(1024)(128)(4,1)S(1)}, s32[]{:S(2)}) async-start(s8[14680064]{0:T(1024)(128)(4,1)} %bitcast.123), calls=%async_computation.2 | async-start | bytes 8388608
  44.2 7.3 %slice-start.3 = ((s8[14680064]{0:T(1024)(128)(4,1)}), s8[4194304]{0:T(1024)(128)(4,1)S(1)}, s32[]{:S(2)}) async-start(s8[14680064]{0:T(1024)(128)(4,1)} %bitcast.123), calls=%async_computation.3 | async-start | bytes 8388608
  44.2 8.7 %slice-start.4 = ((s8[14680064]{0:T(1024)(128)(4,1)}), s8[4194304]{0:T(1024)(128)(4,1)S(1)}, s32[]{:S(2)}) async-start(s8[14680064]{0:T(1024)(128)(4,1)} %bitcast.125), calls=%async_computation.4 | async-start | bytes 8388608
  44.2 8.7 %slice-start.5 = ((s8[14680064]{0:T(1024)(128)(4,1)}), s8[2097152]{0:T(1024)(128)(4,1)S(1)}, s32[]{:S(2)}) async-start(s8[14680064]{0:T(1024)(128)(4,1)} %bitcast.125), calls=%async_computation.5 | async-start | bytes 4194304
  45.7 7.2 %slice-start.6 = ((s8[14680064]{0:T(1024)(128)(4,1)}), s8[4194304]{0:T(1024)(128)(4,1)S(1)}, s32[]{:S(2)}) async-start(s8[14680064]{0:T(1024)(128)(4,1)} %bitcast.125), calls=%async_computation.6 | async-start | bytes 8388608
  45.7 4.0 %collective-permute-start.9 = (bf16[2,80,1792]{2,1,0:T(8,128)(2,1)S(1)}, bf16[2,80,1792]{2,1,0:T(8,128)(2,1)S(1)}, u32[]{:S(2)}, u32[]{:S(2)}) collective-permute-start(bf16[2,80,1792]{2,1,0:T(8,128)(2,1)S(1)} %pad_maximum_fusion.2), channel_id=1, source_target_pairs={{0,1},{1,0},{2,3},{3,2},{4,5},{5,4},{6,7},{7,6},{8,9},{9,8},{10,11... | collective-permute-start | bytes 1720328 | tf_op jit(solution)/shard_map/ppermute | solution.py:58
  49.9 3.0 %slice-start.7 = ((s8[14680064]{0:T(1024)(128)(4,1)}), s8[4194304]{0:T(1024)(128)(4,1)S(1)}, s32[]{:S(2)}) async-start(s8[14680064]{0:T(1024)(128)(4,1)} %bitcast.125), calls=%async_computation.7 | async-start | bytes 8388608
  49.9 9.3 %collective-permute-start.10 = (bf16[2,40,1792]{2,1,0:T(8,128)(2,1)S(1)}, bf16[2,40,1792]{2,1,0:T(8,128)(2,1)S(1)}, u32[]{:S(2)}, u32[]{:S(2)}) collective-permute-start(bf16[2,40,1792]{2,1,0:T(8,128)(2,1)S(1)} %pad_maximum_fusion.10), channel_id=1, source_target_pairs={{0,2},{1,3},{2,0},{3,1},{4,6},{5,7},{6,4},{7,5},{8,10},{9,11},{10,... | collective-permute-start | bytes 860168 | tf_op jit(solution)/shard_map/ppermute | solution.py:58
  54.4 4.2 %collective-permute-start.11 = (bf16[2,80,1792]{2,1,0:T(8,128)(2,1)S(1)}, bf16[2,80,1792]{2,1,0:T(8,128)(2,1)S(1)}, u32[]{:S(2)}, u32[]{:S(2)}) collective-permute-start(bf16[2,80,1792]{2,1,0:T(8,128)(2,1)S(1)} %pad_maximum_fusion.3), channel_id=1, source_target_pairs={{0,1},{1,0},{2,3},{3,2},{4,5},{5,4},{6,7},{7,6},{8,9},{9,8},{10,11... | collective-permute-start | bytes 1720328 | tf_op jit(solution)/shard_map/ppermute | solution.py:58
  56.4 1.2 copy-start.2
  57.6 1.7 %copy-start.3 = (f32[160,1536]{1,0:T(8,128)}, f32[160,1536]{1,0:T(8,128)S(1)}, u32[]{:S(2)}) copy-start(f32[160,1536]{1,0:T(8,128)S(1)} %fusion.12) | copy-start | bytes 2949124
  59.3 10.8 %collective-permute-start.14 = (bf16[40,1792]{1,0:T(8,128)(2,1)S(1)}, bf16[40,1792]{1,0:T(8,128)(2,1)S(1)}, u32[]{:S(2)}, u32[]{:S(2)}) collective-permute-start(bf16[40,1792]{1,0:T(8,128)(2,1)S(1)} %fusion.55), channel_id=1, source_target_pairs={{0,8},{4,12},{8,0},{12,4},{1,9},{5,13},{9,1},{13,5},{2,10},{6,14},... | collective-permute-start | bytes 430088 | tf_op jit(solution)/shard_map/ppermute | solution.py:58
  63.3 8.5 %collective-permute-start.17 = (bf16[2,80,1536]{2,1,0:T(8,128)(2,1)}, bf16[2,80,1536]{2,1,0:T(8,128)(2,1)S(1)}, u32[]{:S(2)}, u32[]{:S(2)}) collective-permute-start(bf16[2,80,1536]{2,1,0:T(8,128)(2,1)} %pad_maximum_fusion.5), channel_id=1, source_target_pairs={{0,1},{1,0},{2,3},{3,2},{4,5},{5,4},{6,7},{7,6},{8,9},{9,8},{10,11... | collective-permute-start | bytes 1474568 | tf_op jit(solution)/shard_map/ppermute | solution.py:58
  63.3 10.5 %collective-permute-start.16 = (bf16[2,40,1792]{2,1,0:T(8,128)(2,1)S(1)}, bf16[2,40,1792]{2,1,0:T(8,128)(2,1)S(1)}, u32[]{:S(2)}, u32[]{:S(2)}) collective-permute-start(bf16[2,40,1792]{2,1,0:T(8,128)(2,1)S(1)} %pad_maximum_fusion.11), channel_id=1, source_target_pairs={{0,2},{1,3},{2,0},{3,1},{4,6},{5,7},{6,4},{7,5},{8,10},{9,11},{10,... | collective-permute-start | bytes 860168 | tf_op jit(solution)/shard_map/ppermute | solution.py:58
  70.2 11.1 %collective-permute-start.15 = (bf16[40,1792]{1,0:T(8,128)(2,1)S(1)}, bf16[40,1792]{1,0:T(8,128)(2,1)S(1)}, u32[]{:S(2)}, u32[]{:S(2)}) collective-permute-start(bf16[40,1792]{1,0:T(8,128)(2,1)S(1)} %get-tuple-element.114), channel_id=1, source_target_pairs={{0,2},{1,3},{2,0},{3,1},{4,6},{5,7},{6,4},{7,5},{8,10},{9,11},{10,... | collective-permute-start | bytes 430088 | tf_op jit(solution)/shard_map/ppermute | solution.py:58
  73.2 21.3 %collective-permute-start.21 = (bf16[2,40,1536]{2,1,0:T(8,128)(2,1)S(1)}, bf16[2,40,1536]{2,1,0:T(8,128)(2,1)S(1)}, u32[]{:S(2)}, u32[]{:S(2)}) collective-permute-start(bf16[2,40,1536]{2,1,0:T(8,128)(2,1)S(1)} %pad_maximum_fusion.14), channel_id=1, source_target_pairs={{0,2},{1,3},{2,0},{3,1},{4,6},{5,7},{6,4},{7,5},{8,10},{9,11},{10,... | collective-permute-start | bytes 737288 | tf_op jit(solution)/shard_map/ppermute | solution.py:58
  73.9 14.0 %collective-permute-start.18 = (bf16[40,1792]{1,0:T(8,128)(2,1)S(1)}, bf16[40,1792]{1,0:T(8,128)(2,1)S(1)}, u32[]{:S(2)}, u32[]{:S(2)}) collective-permute-start(bf16[40,1792]{1,0:T(8,128)(2,1)S(1)} %fusion.53), channel_id=1, source_target_pairs={{0,8},{4,12},{8,0},{12,4},{1,9},{5,13},{9,1},{13,5},{2,10},{6,14},... | collective-permute-start | bytes 430088 | tf_op jit(solution)/shard_map/ppermute | solution.py:58
  77.5 22.4 %slice-start.8 = ((s8[14680064]{0:T(1024)(128)(4,1)}), s8[4194304]{0:T(1024)(128)(4,1)S(1)}, s32[]{:S(2)}) async-start(s8[14680064]{0:T(1024)(128)(4,1)} %bitcast.127), calls=%async_computation.8 | async-start | bytes 8388608
  77.5 22.4 %slice-start.9 = ((s8[14680064]{0:T(1024)(128)(4,1)}), s8[4194304]{0:T(1024)(128)(4,1)S(1)}, s32[]{:S(2)}) async-start(s8[14680064]{0:T(1024)(128)(4,1)} %bitcast.127), calls=%async_computation.9 | async-start | bytes 8388608
  81.3 15.1 %collective-permute-start.23 = (bf16[80,1792]{1,0:T(8,128)(2,1)S(1)}, bf16[80,1792]{1,0:T(8,128)(2,1)S(1)}, u32[]{:S(2)}, u32[]{:S(2)}) collective-permute-start(bf16[80,1792]{1,0:T(8,128)(2,1)S(1)} %pad_maximum_fusion.12), channel_id=1, source_target_pairs={{1,4},{3,6},{4,1},{6,3},{9,12},{11,14},{12,9},{14,11},{17,20},{19,... | collective-permute-start | bytes 860168 | tf_op jit(solution)/shard_map/ppermute | solution.py:135
  82.1 14.9 %collective-permute-start.22 = (bf16[80,1792]{1,0:T(8,128)(2,1)S(1)}, bf16[80,1792]{1,0:T(8,128)(2,1)S(1)}, u32[]{:S(2)}, u32[]{:S(2)}) collective-permute-start(bf16[80,1792]{1,0:T(8,128)(2,1)S(1)} %pad_maximum_fusion.12), channel_id=1, source_target_pairs={{0,4},{1,0},{2,6},{3,2},{4,5},{5,1},{6,7},{7,3},{8,12},{9,8},{10,1... | collective-permute-start | bytes 860168 | tf_op jit(solution)/shard_map/ppermute | solution.py:135
  87.7 7.0 %collective-permute-start.20 = (bf16[2,80,1280]{2,1,0:T(8,128)(2,1)S(1)}, bf16[2,80,1280]{2,1,0:T(8,128)(2,1)S(1)}, u32[]{:S(2)}, u32[]{:S(2)}) collective-permute-start(bf16[2,80,1280]{2,1,0:T(8,128)(2,1)S(1)} %pad_maximum_fusion.6), channel_id=1, source_target_pairs={{0,1},{1,0},{2,3},{3,2},{4,5},{5,4},{6,7},{7,6},{8,9},{9,8},{10,11... | collective-permute-start | bytes 1228808 | tf_op jit(solution)/shard_map/ppermute | solution.py:58
  87.9 12.0 %slice-start.10 = ((s8[14680064]{0:T(1024)(128)(4,1)}), s8[4194304]{0:T(1024)(128)(4,1)S(1)}, s32[]{:S(2)}) async-start(s8[14680064]{0:T(1024)(128)(4,1)} %bitcast.127), calls=%async_computation.10 | async-start | bytes 8388608
  87.9 7.3 %collective-permute-start.19 = (bf16[40,1792]{1,0:T(8,128)(2,1)S(1)}, bf16[40,1792]{1,0:T(8,128)(2,1)S(1)}, u32[]{:S(2)}, u32[]{:S(2)}) collective-permute-start(bf16[40,1792]{1,0:T(8,128)(2,1)S(1)} %get-tuple-element.112), channel_id=1, source_target_pairs={{0,2},{1,3},{2,0},{3,1},{4,6},{5,7},{6,4},{7,5},{8,10},{9,11},{10,... | collective-permute-start | bytes 430088 | tf_op jit(solution)/shard_map/ppermute | solution.py:58
  91.7 8.2 %slice-start.11 = ((s8[14680064]{0:T(1024)(128)(4,1)}), s8[2097152]{0:T(1024)(128)(4,1)S(1)}, s32[]{:S(2)}) async-start(s8[14680064]{0:T(1024)(128)(4,1)} %bitcast.127), calls=%async_computation.11 | async-start | bytes 4194304
  94.5 6.8 %collective-permute-start.26 = (bf16[2,80,768]{2,1,0:T(8,128)(2,1)S(1)}, bf16[2,80,768]{2,1,0:T(8,128)(2,1)S(1)}, u32[]{:S(2)}, u32[]{:S(2)}) collective-permute-start(bf16[2,80,768]{2,1,0:T(8,128)(2,1)S(1)} %pad_maximum_fusion.15), channel_id=1, source_target_pairs={{0,1},{1,0},{2,3},{3,2},{4,5},{5,4},{6,7},{7,6},{8,9},{9,8},{10,11... | collective-permute-start | bytes 737288 | tf_op jit(solution)/shard_map/ppermute | solution.py:58
  94.7 9.4 %collective-permute-start.25 = (bf16[40,1536]{1,0:T(8,128)(2,1)S(1)}, bf16[40,1536]{1,0:T(8,128)(2,1)S(1)}, u32[]{:S(2)}, u32[]{:S(2)}) collective-permute-start(bf16[40,1536]{1,0:T(8,128)(2,1)S(1)} %fusion.59), channel_id=1, source_target_pairs={{0,8},{4,12},{8,0},{12,4},{1,9},{5,13},{9,1},{13,5},{2,10},{6,14},... | collective-permute-start | bytes 368648 | tf_op jit(solution)/shard_map/ppermute | solution.py:58
  95.2 9.9 %collective-permute-start.24 = (bf16[2,40,1280]{2,1,0:T(8,128)(2,1)S(1)}, bf16[2,40,1280]{2,1,0:T(8,128)(2,1)S(1)}, u32[]{:S(2)}, u32[]{:S(2)}) collective-permute-start(bf16[2,40,1280]{2,1,0:T(8,128)(2,1)S(1)} %pad_maximum_fusion.17), channel_id=1, source_target_pairs={{0,2},{1,3},{2,0},{3,1},{4,6},{5,7},{6,4},{7,5},{8,10},{9,11},{10,... | collective-permute-start | bytes 614408 | tf_op jit(solution)/shard_map/ppermute | solution.py:58
  96.4 10.1 %collective-permute-start.28 = (bf16[80,1792]{1,0:T(8,128)(2,1)S(1)}, bf16[80,1792]{1,0:T(8,128)(2,1)S(1)}, u32[]{:S(2)}, u32[]{:S(2)}) collective-permute-start(bf16[80,1792]{1,0:T(8,128)(2,1)S(1)} %pad_maximum_fusion.13), channel_id=1, source_target_pairs={{1,4},{3,6},{4,1},{6,3},{9,12},{11,14},{12,9},{14,11},{17,20},{19,... | collective-permute-start | bytes 860168 | tf_op jit(solution)/shard_map/ppermute | solution.py:135
  97.1 9.4 %collective-permute-start.27 = (bf16[80,1792]{1,0:T(8,128)(2,1)S(1)}, bf16[80,1792]{1,0:T(8,128)(2,1)S(1)}, u32[]{:S(2)}, u32[]{:S(2)}) collective-permute-start(bf16[80,1792]{1,0:T(8,128)(2,1)S(1)} %pad_maximum_fusion.13), channel_id=1, source_target_pairs={{0,4},{1,0},{2,6},{3,2},{4,5},{5,1},{6,7},{7,3},{8,12},{9,8},{10,1... | collective-permute-start | bytes 860168 | tf_op jit(solution)/shard_map/ppermute | solution.py:135
  101.4 5.4 %collective-permute-start.30 = (bf16[2,40,768]{2,1,0:T(8,128)(2,1)S(1)}, bf16[2,40,768]{2,1,0:T(8,128)(2,1)S(1)}, u32[]{:S(2)}, u32[]{:S(2)}) collective-permute-start(bf16[2,40,768]{2,1,0:T(8,128)(2,1)S(1)} %pad_maximum_fusion.19), channel_id=1, source_target_pairs={{0,2},{1,3},{2,0},{3,1},{4,6},{5,7},{6,4},{7,5},{8,10},{9,11},{10,... | collective-permute-start | bytes 368648 | tf_op jit(solution)/shard_map/ppermute | solution.py:58
  104.2 6.4 %collective-permute-start.29 = (bf16[40,1536]{1,0:T(8,128)(2,1)S(1)}, bf16[40,1536]{1,0:T(8,128)(2,1)S(1)}, u32[]{:S(2)}, u32[]{:S(2)}) collective-permute-start(bf16[40,1536]{1,0:T(8,128)(2,1)S(1)} %get-tuple-element.118), channel_id=1, source_target_pairs={{0,2},{1,3},{2,0},{3,1},{4,6},{5,7},{6,4},{7,5},{8,10},{9,11},{10,... | collective-permute-start | bytes 368648 | tf_op jit(solution)/shard_map/ppermute | solution.py:58
  105.2 11.3 %collective-permute-start.32 = (bf16[40,1280]{1,0:T(8,128)(2,1)S(1)}, bf16[40,1280]{1,0:T(8,128)(2,1)S(1)}, u32[]{:S(2)}, u32[]{:S(2)}) collective-permute-start(bf16[40,1280]{1,0:T(8,128)(2,1)S(1)} %fusion.66), channel_id=1, source_target_pairs={{0,8},{4,12},{8,0},{12,4},{1,9},{5,13},{9,1},{13,5},{2,10},{6,14},... | collective-permute-start | bytes 307208 | tf_op jit(solution)/shard_map/ppermute | solution.py:58
  106.9 14.3 %collective-permute-start.37 = (bf16[40,768]{1,0:T(8,128)(2,1)S(1)}, bf16[40,768]{1,0:T(8,128)(2,1)S(1)}, u32[]{:S(2)}, u32[]{:S(2)}) collective-permute-start(bf16[40,768]{1,0:T(8,128)(2,1)S(1)} %fusion.78), channel_id=1, source_target_pairs={{0,8},{4,12},{8,0},{12,4},{1,9},{5,13},{9,1},{13,5},{2,10},{6,14},... | collective-permute-start | bytes 184328 | tf_op jit(solution)/shard_map/ppermute | solution.py:58
  110.6 7.6 %collective-permute-start.35 = (bf16[80,1536]{1,0:T(8,128)(2,1)S(1)}, bf16[80,1536]{1,0:T(8,128)(2,1)S(1)}, u32[]{:S(2)}, u32[]{:S(2)}) collective-permute-start(bf16[80,1536]{1,0:T(8,128)(2,1)S(1)} %pad_maximum_fusion.16), channel_id=1, source_target_pairs={{1,4},{3,6},{4,1},{6,3},{9,12},{11,14},{12,9},{14,11},{17,20},{19,... | collective-permute-start | bytes 737288 | tf_op jit(solution)/shard_map/ppermute | solution.py:135
  111.2 8.7 %collective-permute-start.34 = (bf16[80,1536]{1,0:T(8,128)(2,1)S(1)}, bf16[80,1536]{1,0:T(8,128)(2,1)S(1)}, u32[]{:S(2)}, u32[]{:S(2)}) collective-permute-start(bf16[80,1536]{1,0:T(8,128)(2,1)S(1)} %pad_maximum_fusion.16), channel_id=1, source_target_pairs={{0,4},{1,0},{2,6},{3,2},{4,5},{5,1},{6,7},{7,3},{8,12},{9,8},{10,1... | collective-permute-start | bytes 737288 | tf_op jit(solution)/shard_map/ppermute | solution.py:135
  116.4 1.7 %collective-permute-start.31 = (bf16[80,2048]{1,0:T(8,128)(2,1)S(1)}, bf16[80,2048]{1,0:T(8,128)(2,1)S(1)}, u32[]{:S(2)}, u32[]{:S(2)}) collective-permute-start(bf16[80,2048]{1,0:T(8,128)(2,1)S(1)} %slice.604), channel_id=1, source_target_pairs={{0,1},{1,0},{2,3},{3,2},{4,5},{5,4},{6,7},{7,6},{8,9},{9,8},{10,11... | collective-permute-start | bytes 983048 | tf_op jit(solution)/shard_map/ppermute | solution.py:58
  116.5 5.6 %collective-permute-start.36 = (bf16[40,1280]{1,0:T(8,128)(2,1)S(1)}, bf16[40,1280]{1,0:T(8,128)(2,1)S(1)}, u32[]{:S(2)}, u32[]{:S(2)}) collective-permute-start(bf16[40,1280]{1,0:T(8,128)(2,1)S(1)} %get-tuple-element.124), channel_id=1, source_target_pairs={{0,2},{1,3},{2,0},{3,1},{4,6},{5,7},{6,4},{7,5},{8,10},{9,11},{10,... | collective-permute-start | bytes 307208 | tf_op jit(solution)/shard_map/ppermute | solution.py:58
  121.2 7.3 %collective-permute-start.40 = (bf16[40,768]{1,0:T(8,128)(2,1)S(1)}, bf16[40,768]{1,0:T(8,128)(2,1)S(1)}, u32[]{:S(2)}, u32[]{:S(2)}) collective-permute-start(bf16[40,768]{1,0:T(8,128)(2,1)S(1)} %get-tuple-element.128), channel_id=1, source_target_pairs={{0,2},{1,3},{2,0},{3,1},{4,6},{5,7},{6,4},{7,5},{8,10},{9,11},{10,... | collective-permute-start | bytes 184328 | tf_op jit(solution)/shard_map/ppermute | solution.py:58
  122.2 9.2 %collective-permute-start.39 = (bf16[80,1280]{1,0:T(8,128)(2,1)S(1)}, bf16[80,1280]{1,0:T(8,128)(2,1)S(1)}, u32[]{:S(2)}, u32[]{:S(2)}) collective-permute-start(bf16[80,1280]{1,0:T(8,128)(2,1)S(1)} %pad_maximum_fusion.18), channel_id=1, source_target_pairs={{1,4},{3,6},{4,1},{6,3},{9,12},{11,14},{12,9},{14,11},{17,20},{19,... | collective-permute-start | bytes 614408 | tf_op jit(solution)/shard_map/ppermute | solution.py:135
  122.8 8.9 %collective-permute-start.38 = (bf16[80,1280]{1,0:T(8,128)(2,1)S(1)}, bf16[80,1280]{1,0:T(8,128)(2,1)S(1)}, u32[]{:S(2)}, u32[]{:S(2)}) collective-permute-start(bf16[80,1280]{1,0:T(8,128)(2,1)S(1)} %pad_maximum_fusion.18), channel_id=1, source_target_pairs={{0,4},{1,0},{2,6},{3,2},{4,5},{5,1},{6,7},{7,3},{8,12},{9,8},{10,1... | collective-permute-start | bytes 614408 | tf_op jit(solution)/shard_map/ppermute | solution.py:135
  127.6 9.5 %collective-permute-start.33 = (bf16[80,2048]{1,0:T(8,128)(2,1)S(1)}, bf16[80,2048]{1,0:T(8,128)(2,1)S(1)}, u32[]{:S(2)}, u32[]{:S(2)}) collective-permute-start(bf16[80,2048]{1,0:T(8,128)(2,1)S(1)} %get-tuple-element.85), channel_id=1, source_target_pairs={{0,2},{1,3},{2,0},{3,1},{4,6},{5,7},{6,4},{7,5},{8,10},{9,11},{10,... | collective-permute-start | bytes 983048 | tf_op jit(solution)/shard_map/ppermute | solution.py:58
  128.5 4.4 %collective-permute-start.42 = (bf16[80,768]{1,0:T(8,128)(2,1)S(1)}, bf16[80,768]{1,0:T(8,128)(2,1)S(1)}, u32[]{:S(2)}, u32[]{:S(2)}) collective-permute-start(bf16[80,768]{1,0:T(8,128)(2,1)S(1)} %pad_maximum_fusion.20), channel_id=1, source_target_pairs={{1,4},{3,6},{4,1},{6,3},{9,12},{11,14},{12,9},{14,11},{17,20},{19,... | collective-permute-start | bytes 368648 | tf_op jit(solution)/shard_map/ppermute | solution.py:135
  129.2 4.9 %collective-permute-start.41 = (bf16[80,768]{1,0:T(8,128)(2,1)S(1)}, bf16[80,768]{1,0:T(8,128)(2,1)S(1)}, u32[]{:S(2)}, u32[]{:S(2)}) collective-permute-start(bf16[80,768]{1,0:T(8,128)(2,1)S(1)} %pad_maximum_fusion.20), channel_id=1, source_target_pairs={{0,4},{1,0},{2,6},{3,2},{4,5},{5,1},{6,7},{7,3},{8,12},{9,8},{10,1... | collective-permute-start | bytes 368648 | tf_op jit(solution)/shard_map/ppermute | solution.py:135
  134.9 3.4 %collective-permute-start.43 = (bf16[80,2048]{1,0:T(8,128)(2,1)S(1)}, bf16[80,2048]{1,0:T(8,128)(2,1)S(1)}, u32[]{:S(2)}, u32[]{:S(2)}) collective-permute-start(bf16[80,2048]{1,0:T(8,128)(2,1)S(1)} %slice.603), channel_id=1, source_target_pairs={{0,1},{1,0},{2,3},{3,2},{4,5},{5,4},{6,7},{7,6},{8,9},{9,8},{10,11... | collective-permute-start | bytes 983048 | tf_op jit(solution)/shard_map/ppermute | solution.py:58
  138.5 10.1 %collective-permute-start.44 = (bf16[80,2048]{1,0:T(8,128)(2,1)S(1)}, bf16[80,2048]{1,0:T(8,128)(2,1)S(1)}, u32[]{:S(2)}, u32[]{:S(2)}) collective-permute-start(bf16[80,2048]{1,0:T(8,128)(2,1)S(1)} %fusion.47), channel_id=1, source_target_pairs={{0,2},{1,3},{2,0},{3,1},{4,6},{5,7},{6,4},{7,5},{8,10},{9,11},{10,... | collective-permute-start | bytes 983048 | tf_op jit(solution)/shard_map/ppermute | solution.py:58
  139.5 10.1 %collective-permute-start.45 = (bf16[80,2048]{1,0:T(8,128)(2,1)S(1)}, bf16[80,2048]{1,0:T(8,128)(2,1)S(1)}, u32[]{:S(2)}, u32[]{:S(2)}) collective-permute-start(bf16[80,2048]{1,0:T(8,128)(2,1)S(1)} %get-tuple-element.81), channel_id=1, source_target_pairs={{0,1},{1,0},{2,3},{3,2},{4,5},{5,4},{6,7},{7,6},{8,9},{9,8},{10,11... | collective-permute-start | bytes 983048 | tf_op jit(solution)/shard_map/ppermute | solution.py:58
  148.7 1.7 %collective-permute-start.46 = (bf16[80,2048]{1,0:T(8,128)(2,1)S(1)}, bf16[80,2048]{1,0:T(8,128)(2,1)S(1)}, u32[]{:S(2)}, u32[]{:S(2)}) collective-permute-start(bf16[80,2048]{1,0:T(8,128)(2,1)S(1)} %get-tuple-element.83), channel_id=1, source_target_pairs={{0,1},{1,0},{2,3},{3,2},{4,5},{5,4},{6,7},{7,6},{8,9},{9,8},{10,11... | collective-permute-start | bytes 983048 | tf_op jit(solution)/shard_map/ppermute | solution.py:58

commit v15 on v13

--- a/solution.py
+++ b/solution.py
@@ -8,15 +8,19 @@
 from jax.sharding import PartitionSpec as P
 
 HALVES = 2
+PIECES = (1, 1)
 PARTS = ((14, 14), (18, 10))
 EDGES = {
-    "t1.pick": ["t0.add"],
+    "t1.pick": ["t0.pick"],
+    "t0.add": ["t1.pick"],
+    "t1.add": ["t0.add"],
     "w.pull": ["t0.columns"],
     "t0.cores": ["w.pull"],
     "t1.columns": ["t0.cores"],
     "c00.dots": ["t1.columns"],
-    "t1.cores": ["c00.dots"],
-    "c01.dots": ["c00.sum"],
+    "c01.dots": ["c00.dots"],
+    "t1.cores": ["c01.dots"],
+    "c01.sum": ["c00.sum"],
     "c10.dots": ["c01.sum"],
     "c00.hidden": ["c10.dots"],
     "c10.sum": ["c00.halves"],
@@ -25,22 +29,18 @@
     "c00.columns": ["c11.dots"],
     "c01.halves": ["c00.columns"],
     "c10.hidden": ["c01.halves"],
-    "c11.sum": ["c10.hidden"],
-    "c01.columns": ["c11.sum"],
-    "c00.cores": ["c01.columns"],
-    "c10.halves": ["c00.cores"],
+    "c01.columns": ["c10.hidden"],
+    "c11.sum": ["c01.columns"],
+    "c00.cores": ["c11.sum"],
     "c11.hidden": ["c10.halves"],
     "c00.down": ["c11.hidden"],
     "c01.cores": ["c00.down"],
-    "c10.columns": ["c01.cores"],
-    "c01.down": ["c10.columns"],
-    "c11.halves": ["c01.down"],
-    "c10.cores": ["c11.halves"],
+    "c11.halves": ["c10.columns"],
+    "c01.down": ["c11.halves"],
     "c11.columns": ["c10.down"],
     "b0.total": ["c11.columns"],
     "c11.cores": ["b0.total"],
-    "c11.down": ["b0.all"],
-    "b1.total": ["c11.down"],
+    "b1.total": ["b0.all"],
 }
 
 
@@ -95,8 +95,7 @@
     r = lax.axis_index("row")
     x, k, zh, zl = c // 2, c % 2, r // 2, r % 2
     quarter = slots // 2
-    piece = quarter // HALVES
-    half = 2 * piece
+    pieces = [quarter * share // sum(PIECES) for share in PIECES]
     spans = []
     for sizes in PARTS:
         ends = [0]
@@ -110,11 +109,12 @@
     first = jnp.sum(jnp.where(rows < here, lengths[None], 0), axis=1, keepdims=True)
     count = jnp.sum(jnp.where(rows == here, lengths[None], 0), axis=1, keepdims=True)
     places = jnp.where(slot < count, slot + first, -1)
-    inside = jnp.arange(piece, dtype=jnp.int32)
-
     def mine_of(c):
-        both = jnp.concatenate([inside + quarter * c, inside + quarter * (c ^ 2)])
-        return [both + h * piece for h in range(HALVES)]
+        found = []
+        for h, piece in enumerate(pieces):
+            inside = jnp.arange(piece, dtype=jnp.int32) + sum(pieces[:h])
+            found.append(jnp.concatenate([inside + quarter * c, inside + quarter * (c ^ 2)]))
+        return found
 
     mine = mine_of(c)
 
@@ -179,6 +179,7 @@
         return issued(name + ".cores", finish(ordered(name + ".cores", pair)))
 
     def pick_steps(name, h):
+        piece = pieces[h]
         spots = ordered(name + ".pick", mine[h])
         own = spots[:, None] == places[0][None]
         sib = spots[:, None] == places[1][None]
@@ -204,6 +205,7 @@
     def chunk_steps(name, h, i):
         full = result("t" + str(h))
         part = slice(*spans[h][i])
+        piece, half = pieces[h], 2 * pieces[h]
         full = ordered(name + ".dots", full)
         if (h, i) == (0, 0):
             result("w")
@@ -228,6 +230,7 @@
 
     def branch_steps(name, h):
         parts = [result("c" + str(h) + str(i)) for i in range(len(spans[h]))]
+        piece, half = pieces[h], 2 * pieces[h]
         branch = issued(name + ".branch", sum(parts[1:], parts[0]))
         got = flip(branch[half:].astype(jnp.bfloat16), "col", 1)
         yield

time: 146 us -> 156 us (1.068)
  local copies, waits for them, and re-layouts: 1.03 us -> 5.83 us
  starting transfers between devices: 49 us -> 53.7 us
  other arithmetic: 6.89 us -> 10.4 us
  waiting for transfers between devices: 55.8 us -> 52.4 us
    ppermute x12, starting transfers between devices: 16.1 us -> 23.4 us  [move(): return lax.ppermute(value, ('row', 'col'), pairs)]
    ppermute x29, waiting for transfers between devices: 51.8 us -> 45.9 us  [flip(): return lax.ppermute(value, axis, [(i, i ^ bit) for i in range(count)])]
    unnamed x34, local copies, waits for them, and re-layouts: 0.48 us -> 5.26 us
    ppermute x29, starting transfers between devices: 32.9 us -> 30.3 us  [flip(): return lax.ppermute(value, axis, [(i, i ^ bit) for i in range(count)])]
    ppermute x12, waiting for transfers between devices: 3.99 us -> 6.53 us  [move(): return lax.ppermute(value, ('row', 'col'), pairs)]
  transfers between devices with their start and end apart: 41 -> 41, of which waited for: 17 -> 16; matrix products, arithmetic and copies ran while one was open for 18% -> 23% of each run, Pallas kernels for 4% -> 4%
where the time goes in v15:
time: 156 us
  starting transfers between devices  53.7 us (34%)
  waiting for transfers between devices  52.4 us (34%)
  matrix products  26.9 us (17%)
  other arithmetic  10.4 us (7%)
  Pallas kernels  5.84 us (4%)
  local copies, waits for them, and re-layouts  5.83 us (4%)
    ppermute x29, waiting for transfers between devices, flip(): return lax.ppermute(value, axis, [(i, i ^ bit) for i in range(count)])  45.9 us
    ppermute x29, starting transfers between devices, flip(): return lax.ppermute(value, axis, [(i, i ^ bit) for i in range(count)])  30.3 us
    dot_general x17, matrix products, dot(): return jnp.dot(a, b, preferred_element_type=jnp.float32)  26.1 us
    ppermute x12, starting transfers between devices, move(): return lax.ppermute(value, ('row', 'col'), pairs)  23.4 us
    ppermute x12, waiting for transfers between devices, move(): return lax.ppermute(value, ('row', 'col'), pairs)  6.53 us
    pallas_call x1, Pallas kernels, pull(): pl.pallas_call(functools.partial(pull_kernel, first, end), in_specs=[pl.B...  5.84 us
    unnamed x34, local copies, waits for them, and re-layouts  5.26 us
  transfers between devices with their start and end apart: 41, of which 16 were waited for; matrix products, arithmetic and copies ran while one was open for 23% of the time, Pallas kernels for 4%

profile of v15, /device:TPU:0, one launch (start us, length us, event | category | flops | bytes accessed | tf_op | source)
XLA Modules:
  0.0 156.0 jit_solution(3862938431897774592)
XLA Ops:
  0.5 0.9 fusion.89
  1.6 1.4 fusion.79
  3.3 2.6 %collective-permute-start.1 = (bf16[40,2048]{1,0:T(8,128)(2,1)S(1)}, bf16[40,2048]{1,0:T(8,128)(2,1)S(1)}, u32[]{:S(2)}, u32[]{:S(2)}) collective-permute-start(bf16[40,2048]{1,0:T(8,128)(2,1)S(1)} %get-tuple-element.103), channel_id=1, source_target_pairs={{0,2},{1,3},{2,0},{3,1},{4,6},{5,7},{6,4},{7,5},{8,10},{9,11},{10,... | collective-permute-start | bytes 491528 | tf_op jit(solution)/shard_map/ppermute | solution.py:53
  6.5 4.2 %collective-permute-done.1 = bf16[40,2048]{1,0:T(8,128)(2,1)S(1)} collective-permute-done((bf16[40,2048]{1,0:T(8,128)(2,1)S(1)}, bf16[40,2048]{1,0:T(8,128)(2,1)S(1)}, u32[]{:S(2)}, u32[]{:S(2)}) %collective-permute-start.1) | collective-permute-done | bytes 163872 | tf_op jit(solution)/shard_map/ppermute | solution.py:53
  10.8 2.9 %collective-permute-start.2 = (bf16[40,2048]{1,0:T(8,128)(2,1)S(1)}, bf16[40,2048]{1,0:T(8,128)(2,1)S(1)}, u32[]{:S(2)}, u32[]{:S(2)}) collective-permute-start(bf16[40,2048]{1,0:T(8,128)(2,1)S(1)} %add.182), channel_id=1, source_target_pairs={{0,8},{4,12},{8,0},{12,4},{1,9},{5,13},{9,1},{13,5},{2,10},{6,14},... | collective-permute-start | bytes 491528 | tf_op jit(solution)/shard_map/ppermute | solution.py:53
  13.7 1.6 collective-permute-start.6
  15.3 6.0 %collective-permute-done.2 = bf16[40,2048]{1,0:T(8,128)(2,1)S(1)} collective-permute-done((bf16[40,2048]{1,0:T(8,128)(2,1)S(1)}, bf16[40,2048]{1,0:T(8,128)(2,1)S(1)}, u32[]{:S(2)}, u32[]{:S(2)}) %collective-permute-start.2) | collective-permute-done | bytes 163872 | tf_op jit(solution)/shard_map/ppermute | solution.py:53
  21.3 1.6 %collective-permute-start.3 = (bf16[40,2048]{1,0:T(8,128)(2,1)S(1)}, bf16[40,2048]{1,0:T(8,128)(2,1)S(1)}, u32[]{:S(2)}, u32[]{:S(2)}) collective-permute-start(bf16[40,2048]{1,0:T(8,128)(2,1)S(1)} %get-tuple-element.100), channel_id=1, source_target_pairs={{0,2},{1,3},{2,0},{3,1},{4,6},{5,7},{6,4},{7,5},{8,10},{9,11},{10,... | collective-permute-start | bytes 491528 | tf_op jit(solution)/shard_map/ppermute | solution.py:53
  23.0 3.7 %collective-permute-done.3 = bf16[40,2048]{1,0:T(8,128)(2,1)S(1)} collective-permute-done((bf16[40,2048]{1,0:T(8,128)(2,1)S(1)}, bf16[40,2048]{1,0:T(8,128)(2,1)S(1)}, u32[]{:S(2)}, u32[]{:S(2)}) %collective-permute-start.3) | collective-permute-done | bytes 163872 | tf_op jit(solution)/shard_map/ppermute | solution.py:53
  27.4 2.8 %collective-permute-start.4 = (bf16[80,2048]{1,0:T(8,128)(2,1)S(1)}, bf16[80,2048]{1,0:T(8,128)(2,1)S(1)}, u32[]{:S(2)}, u32[]{:S(2)}) collective-permute-start(bf16[80,2048]{1,0:T(8,128)(2,1)S(1)} %pad_maximum_fusion.10), channel_id=1, source_target_pairs={{0,4},{1,0},{2,6},{3,2},{4,5},{5,1},{6,7},{7,3},{8,12},{9,8},{10,1... | collective-permute-start | bytes 983048 | tf_op jit(solution)/shard_map/ppermute | solution.py:130
  30.2 2.2 %collective-permute-done.7 = bf16[40,2048]{1,0:T(8,128)(2,1)S(1)} collective-permute-done((bf16[40,2048]{1,0:T(8,128)(2,1)S(1)}, bf16[40,2048]{1,0:T(8,128)(2,1)S(1)}, u32[]{:S(2)}, u32[]{:S(2)}) %collective-permute-start.7) | collective-permute-done | bytes 163872 | tf_op jit(solution)/shard_map/ppermute | solution.py:53
  33.0 5.8 %shard_map.55 = (bf16[2048,1792]{1,0:T(8,128)(2,1)S(1)}, bf16[2048,1792]{1,0:T(8,128)(2,1)S(1)}) custom-call(s32[4]{0:T(128)S(1)} %copy-done, bf16[2048,3584]{1,0:T(8,128)(2,1)} %gate_ref.1, bf16[2048,3584]{1,0:T(8,128)(2,1)} %up_ref.1), custom_call_target="tpu_custom_call" | custom-call | tf_op jit(solution)/shard_map/pallas_call | solution.py:73
  39.7 3.4 %collective-permute-start.11 = (bf16[80,2048]{1,0:T(8,128)(2,1)S(1)}, bf16[80,2048]{1,0:T(8,128)(2,1)S(1)}, u32[]{:S(2)}, u32[]{:S(2)}) collective-permute-start(bf16[80,2048]{1,0:T(8,128)(2,1)S(1)} %pad_maximum_fusion.11), channel_id=1, source_target_pairs={{0,4},{1,0},{2,6},{3,2},{4,5},{5,1},{6,7},{7,3},{8,12},{9,8},{10,1... | collective-permute-start | bytes 983048 | tf_op jit(solution)/shard_map/ppermute | solution.py:130
  43.2 1.4 fusion.107
  44.6 1.4 fusion.108
  46.3 3.6 %slice-done.2 = s8[4194304]{0:T(1024)(128)(4,1)S(1)} async-done(((s8[14680064]{0:T(1024)(128)(4,1)}), s8[4194304]{0:T(1024)(128)(4,1)S(1)}, s32[]{:S(2)}) %slice-start.2) | async-done | bytes 4194328
  49.8 1.2 slice-done.3
  51.0 1.4 fusion.10
  52.8 1.4 fusion.12
  54.6 0.9 pad_maximum_fusion.2
  55.7 0.7 pad_maximum_fusion.12
  56.4 0.9 collective-permute-start.10
  57.5 0.8 pad_maximum_fusion.13
  58.3 1.7 %fusion.2 = f32[160,2304]{1,0:T(8,128)S(1)} fusion(bf16[160,2048]{1,0:T(8,128)(2,1)S(1)} %copy-done.3, bf16[2048,3584]{1,0:T(8,128)(2,1)S(1)} %bitcast.103), kind=kOutput, calls=%fused_computation.2 | convolution fusion | flops 1509949440 | bytes 11567104 | tf_op jit(solution)/shard_map/dot_general | solution.py:48
  60.0 1.7 %fusion.4 = f32[160,2304]{1,0:T(8,128)S(1)} fusion(bf16[160,2048]{1,0:T(8,128)(2,1)S(1)} %copy-done.3, bf16[2048,3584]{1,0:T(8,128)(2,1)S(1)} %bitcast.105), kind=kOutput, calls=%fused_computation.4 | convolution fusion | flops 1509949440 | bytes 11567104 | tf_op jit(solution)/shard_map/dot_general | solution.py:48
  61.8 1.1 pad_maximum_fusion
  63.0 3.0 %collective-permute-done.10 = bf16[2,40,1792]{2,1,0:T(8,128)(2,1)} collective-permute-done((bf16[2,40,1792]{2,1,0:T(8,128)(2,1)}, bf16[2,40,1792]{2,1,0:T(8,128)(2,1)}, u32[]{:S(2)}, u32[]{:S(2)}) %collective-permute-start.10) | collective-permute-done | bytes 286752 | tf_op jit(solution)/shard_map/ppermute | solution.py:53
  65.9 1.1 fusion.56
  67.1 2.8 %collective-permute-start.14 = (bf16[40,1792]{1,0:T(8,128)(2,1)S(1)}, bf16[40,1792]{1,0:T(8,128)(2,1)}, u32[]{:S(2)}, u32[]{:S(2)}) collective-permute-start(bf16[40,1792]{1,0:T(8,128)(2,1)S(1)} %fusion.56), channel_id=1, source_target_pairs={{0,8},{4,12},{8,0},{12,4},{1,9},{5,13},{9,1},{13,5},{2,10},{6,14},... | collective-permute-start | bytes 430088 | tf_op jit(solution)/shard_map/ppermute | solution.py:53
  69.9 1.5 collective-permute-start.16
  71.4 5.2 %collective-permute-done.14 = bf16[40,1792]{1,0:T(8,128)(2,1)} collective-permute-done((bf16[40,1792]{1,0:T(8,128)(2,1)S(1)}, bf16[40,1792]{1,0:T(8,128)(2,1)}, u32[]{:S(2)}, u32[]{:S(2)}) %collective-permute-start.14) | collective-permute-done | bytes 143392 | tf_op jit(solution)/shard_map/ppermute | solution.py:53
  76.6 0.9 broadcast_select_fusion.21
  77.5 1.5 collective-permute-start.15
  79.0 1.5 slice_add_fusion.1
  81.5 4.0 %fusion.16 = f32[160,1280]{1,0:T(8,128)S(1)} fusion(bf16[160,2048]{1,0:T(8,128)(2,1)S(1)} %copy-done.4, bf16[2048,3584]{1,0:T(8,128)(2,1)} %up_ref.1), kind=kOutput, calls=%fused_computation.16 | convolution fusion | flops 838860800 | bytes 6717440 | tf_op jit(solution)/shard_map/dot_general | solution.py:48
  85.6 3.7 %fusion.18 = f32[160,1280]{1,0:T(8,128)S(1)} fusion(bf16[160,2048]{1,0:T(8,128)(2,1)S(1)} %copy-done.4, bf16[2048,3584]{1,0:T(8,128)(2,1)} %gate_ref.1), kind=kOutput, calls=%fused_computation.18 | convolution fusion | flops 838860800 | bytes 6717440 | tf_op jit(solution)/shard_map/dot_general | solution.py:48
  90.1 4.5 %collective-permute-start.22 = (bf16[80,1792]{1,0:T(8,128)(2,1)S(1)}, bf16[80,1792]{1,0:T(8,128)(2,1)S(1)}, u32[]{:S(2)}, u32[]{:S(2)}) collective-permute-start(bf16[80,1792]{1,0:T(8,128)(2,1)S(1)} %pad_maximum_fusion.14), channel_id=1, source_target_pairs={{0,4},{1,0},{2,6},{3,2},{4,5},{5,1},{6,7},{7,3},{8,12},{9,8},{10,1... | collective-permute-start | bytes 860168 | tf_op jit(solution)/shard_map/ppermute | solution.py:130
  94.8 1.6 collective-permute-start.20
  96.5 0.9 collective-permute-start.25
  97.4 3.5 %collective-permute-done.20 = bf16[40,1792]{1,0:T(8,128)(2,1)S(1)} collective-permute-done((bf16[40,1792]{1,0:T(8,128)(2,1)S(1)}, bf16[40,1792]{1,0:T(8,128)(2,1)S(1)}, u32[]{:S(2)}, u32[]{:S(2)}) %collective-permute-start.20) | collective-permute-done | bytes 143392 | tf_op jit(solution)/shard_map/ppermute | solution.py:53
  101.6 2.6 %collective-permute-start.26 = (bf16[80,1792]{1,0:T(8,128)(2,1)S(1)}, bf16[80,1792]{1,0:T(8,128)(2,1)S(1)}, u32[]{:S(2)}, u32[]{:S(2)}) collective-permute-start(bf16[80,1792]{1,0:T(8,128)(2,1)S(1)} %pad_maximum_fusion.15), channel_id=1, source_target_pairs={{0,4},{1,0},{2,6},{3,2},{4,5},{5,1},{6,7},{7,3},{8,12},{9,8},{10,1... | collective-permute-start | bytes 860168 | tf_op jit(solution)/shard_map/ppermute | solution.py:130
  104.4 1.6 collective-permute-start.24
  106.1 2.1 %collective-permute-done.25 = bf16[40,2304]{1,0:T(8,128)(2,1)S(1)} collective-permute-done((bf16[40,2304]{1,0:T(8,128)(2,1)S(1)}, bf16[40,2304]{1,0:T(8,128)(2,1)S(1)}, u32[]{:S(2)}, u32[]{:S(2)}) %collective-permute-start.25) | collective-permute-done | bytes 184352 | tf_op jit(solution)/shard_map/ppermute | solution.py:53
  108.8 3.6 %collective-permute-done.24 = bf16[2,40,1280]{2,1,0:T(8,128)(2,1)S(1)} collective-permute-done((bf16[2,40,1280]{2,1,0:T(8,128)(2,1)S(1)}, bf16[2,40,1280]{2,1,0:T(8,128)(2,1)S(1)}, u32[]{:S(2)}, u32[]{:S(2)}) %collective-permute-start.24) | collective-permute-done | bytes 204832 | tf_op jit(solution)/shard_map/ppermute | solution.py:53
  112.5 0.8 collective-permute-start.28
  113.3 1.4 fusion.8
  114.8 0.7 collective-permute-done.29
  115.5 0.7 collective-permute-start.33
  116.2 2.2 %collective-permute-start.32 = (bf16[80,2304]{1,0:T(8,128)(2,1)S(1)}, bf16[80,2304]{1,0:T(8,128)(2,1)S(1)}, u32[]{:S(2)}, u32[]{:S(2)}) collective-permute-start(bf16[80,2304]{1,0:T(8,128)(2,1)S(1)} %pad_maximum_fusion.9), channel_id=1, source_target_pairs={{0,4},{1,0},{2,6},{3,2},{4,5},{5,1},{6,7},{7,3},{8,12},{9,8},{10,1... | collective-permute-start | bytes 1105928 | tf_op jit(solution)/shard_map/ppermute | solution.py:130
  119.1 2.1 %collective-permute-start.31 = (bf16[40,1280]{1,0:T(8,128)(2,1)S(1)}, bf16[40,1280]{1,0:T(8,128)(2,1)S(1)}, u32[]{:S(2)}, u32[]{:S(2)}) collective-permute-start(bf16[40,1280]{1,0:T(8,128)(2,1)S(1)} %get-tuple-element.116), channel_id=1, source_target_pairs={{0,2},{1,3},{2,0},{3,1},{4,6},{5,7},{6,4},{7,5},{8,10},{9,11},{10,... | collective-permute-start | bytes 307208 | tf_op jit(solution)/shard_map/ppermute | solution.py:53
  121.2 1.5 fusion.25
  122.8 3.9 %collective-permute-done.32 = bf16[80,2304]{1,0:T(8,128)(2,1)S(1)} collective-permute-done((bf16[80,2304]{1,0:T(8,128)(2,1)S(1)}, bf16[80,2304]{1,0:T(8,128)(2,1)S(1)}, u32[]{:S(2)}, u32[]{:S(2)}) %collective-permute-start.32) | collective-permute-done | bytes 368672 | tf_op jit(solution)/shard_map/ppermute | solution.py:130
  126.9 1.7 %fusion = f32[160,2048]{1,0:T(8,128)S(1)} fusion(bf16[3584,2048]{1,0:T(8,128)(2,1)S(1)} %bitcast.114, bf16[80,2304]{1,0:T(8,128)(2,1)S(1)} %get-tuple-element.86, bf16[80,2304]{1,0:T(8,128)(2,1)S(1)} %get-tuple-element.85), kind=kOutput, calls=%fused_computation | convolution fusion | flops 1511424000 | bytes 11485184 | tf_op jit(solution)/shard_map/dot_general | solution.py:48
  129.4 3.8 %collective-permute-start.35 = (bf16[80,1280]{1,0:T(8,128)(2,1)S(1)}, bf16[80,1280]{1,0:T(8,128)(2,1)S(1)}, u32[]{:S(2)}, u32[]{:S(2)}) collective-permute-start(bf16[80,1280]{1,0:T(8,128)(2,1)S(1)} %pad_maximum_fusion.17), channel_id=1, source_target_pairs={{0,4},{1,0},{2,6},{3,2},{4,5},{5,1},{6,7},{7,3},{8,12},{9,8},{10,1... | collective-permute-start | bytes 614408 | tf_op jit(solution)/shard_map/ppermute | solution.py:130
  133.3 2.1 %collective-permute-start.34 = (bf16[80,2048]{1,0:T(8,128)(2,1)S(1)}, bf16[80,2048]{1,0:T(8,128)(2,1)S(1)}, u32[]{:S(2)}, u32[]{:S(2)}) collective-permute-start(bf16[80,2048]{1,0:T(8,128)(2,1)S(1)} %get-tuple-element.75), channel_id=1, source_target_pairs={{0,2},{1,3},{2,0},{3,1},{4,6},{5,7},{6,4},{7,5},{8,10},{9,11},{10,... | collective-permute-start | bytes 983048 | tf_op jit(solution)/shard_map/ppermute | solution.py:53
  135.4 2.6 %collective-permute-done.35 = bf16[80,1280]{1,0:T(8,128)(2,1)S(1)} collective-permute-done((bf16[80,1280]{1,0:T(8,128)(2,1)S(1)}, bf16[80,1280]{1,0:T(8,128)(2,1)S(1)}, u32[]{:S(2)}, u32[]{:S(2)}) %collective-permute-start.35) | collective-permute-done | bytes 204832 | tf_op jit(solution)/shard_map/ppermute | solution.py:130
  138.0 1.1 fusion.22
  139.2 1.2 collective-permute-start.37
  140.4 3.0 %collective-permute-done.34 = bf16[80,2048]{1,0:T(8,128)(2,1)S(1)} collective-permute-done((bf16[80,2048]{1,0:T(8,128)(2,1)S(1)}, bf16[80,2048]{1,0:T(8,128)(2,1)S(1)}, u32[]{:S(2)}, u32[]{:S(2)}) %collective-permute-start.34) | collective-permute-done | bytes 327712 | tf_op jit(solution)/shard_map/ppermute | solution.py:53
  143.6 1.8 %collective-permute-start.38 = (bf16[80,2048]{1,0:T(8,128)(2,1)S(1)}, bf16[80,2048]{1,0:T(8,128)(2,1)S(1)}, u32[]{:S(2)}, u32[]{:S(2)}) collective-permute-start(bf16[80,2048]{1,0:T(8,128)(2,1)S(1)} %fusion.41), channel_id=1, source_target_pairs={{0,2},{1,3},{2,0},{3,1},{4,6},{5,7},{6,4},{7,5},{8,10},{9,11},{10,... | collective-permute-start | bytes 983048 | tf_op jit(solution)/shard_map/ppermute | solution.py:53
  145.5 7.4 %collective-permute-done.38 = bf16[80,2048]{1,0:T(8,128)(2,1)S(1)} collective-permute-done((bf16[80,2048]{1,0:T(8,128)(2,1)S(1)}, bf16[80,2048]{1,0:T(8,128)(2,1)S(1)}, u32[]{:S(2)}, u32[]{:S(2)}) %collective-permute-start.38) | collective-permute-done | bytes 327712 | tf_op jit(solution)/shard_map/ppermute | solution.py:53
  153.2 0.8 fusion.31
  154.0 0.7 collective-permute-done.40
  154.7 1.3 fusion.28
  (153 shorter events, 11.7 us)
Async XLA Ops:
  0.0 3.0 %collective-permute-start = (bf16[160,2048]{1,0:T(8,128)(2,1)}, bf16[160,2048]{1,0:T(8,128)(2,1)S(1)}, u32[]{:S(2)}, u32[]{:S(2)}) collective-permute-start(bf16[160,2048]{1,0:T(8,128)(2,1)} %param.5), channel_id=1, source_target_pairs={{0,1},{1,0},{2,3},{3,2},{4,5},{5,4},{6,7},{7,6},{8,9},{9,8},{10,11... | collective-permute-start | bytes 1966088 | tf_op jit(solution)/shard_map/ppermute | solution.py:53
  3.0 2.9 %copy-start.1 = (bf16[160,2048]{1,0:T(8,128)(2,1)S(1)}, bf16[160,2048]{1,0:T(8,128)(2,1)}, u32[]{:S(2)}) copy-start(bf16[160,2048]{1,0:T(8,128)(2,1)} %param.5) | copy-start | bytes 1966084
  3.3 7.4 %collective-permute-start.1 = (bf16[40,2048]{1,0:T(8,128)(2,1)S(1)}, bf16[40,2048]{1,0:T(8,128)(2,1)S(1)}, u32[]{:S(2)}, u32[]{:S(2)}) collective-permute-start(bf16[40,2048]{1,0:T(8,128)(2,1)S(1)} %get-tuple-element.103), channel_id=1, source_target_pairs={{0,2},{1,3},{2,0},{3,1},{4,6},{5,7},{6,4},{7,5},{8,10},{9,11},{10,... | collective-permute-start | bytes 491528 | tf_op jit(solution)/shard_map/ppermute | solution.py:53
  10.8 22.2 %copy-start = (s32[4]{0:T(128)S(1)}, s32[4]{0:T(128)}, u32[]{:S(2)}) copy-start(s32[4]{0:T(128)} %tick_ref) | copy-start | bytes 52
  10.8 10.5 %collective-permute-start.2 = (bf16[40,2048]{1,0:T(8,128)(2,1)S(1)}, bf16[40,2048]{1,0:T(8,128)(2,1)S(1)}, u32[]{:S(2)}, u32[]{:S(2)}) collective-permute-start(bf16[40,2048]{1,0:T(8,128)(2,1)S(1)} %add.182), channel_id=1, source_target_pairs={{0,8},{4,12},{8,0},{12,4},{1,9},{5,13},{9,1},{13,5},{2,10},{6,14},... | collective-permute-start | bytes 491528 | tf_op jit(solution)/shard_map/ppermute | solution.py:53
  13.7 9.2 %collective-permute-start.6 = (bf16[40,2048]{1,0:T(8,128)(2,1)S(1)}, bf16[40,2048]{1,0:T(8,128)(2,1)S(1)}, u32[]{:S(2)}, u32[]{:S(2)}) collective-permute-start(bf16[40,2048]{1,0:T(8,128)(2,1)S(1)} %get-tuple-element.101), channel_id=1, source_target_pairs={{0,2},{1,3},{2,0},{3,1},{4,6},{5,7},{6,4},{7,5},{8,10},{9,11},{10,... | collective-permute-start | bytes 491528 | tf_op jit(solution)/shard_map/ppermute | solution.py:53
  21.3 5.4 %collective-permute-start.3 = (bf16[40,2048]{1,0:T(8,128)(2,1)S(1)}, bf16[40,2048]{1,0:T(8,128)(2,1)S(1)}, u32[]{:S(2)}, u32[]{:S(2)}) collective-permute-start(bf16[40,2048]{1,0:T(8,128)(2,1)S(1)} %get-tuple-element.100), channel_id=1, source_target_pairs={{0,2},{1,3},{2,0},{3,1},{4,6},{5,7},{6,4},{7,5},{8,10},{9,11},{10,... | collective-permute-start | bytes 491528 | tf_op jit(solution)/shard_map/ppermute | solution.py:53
  23.0 9.5 %collective-permute-start.7 = (bf16[40,2048]{1,0:T(8,128)(2,1)S(1)}, bf16[40,2048]{1,0:T(8,128)(2,1)S(1)}, u32[]{:S(2)}, u32[]{:S(2)}) collective-permute-start(bf16[40,2048]{1,0:T(8,128)(2,1)S(1)} %add.183), channel_id=1, source_target_pairs={{0,8},{4,12},{8,0},{12,4},{1,9},{5,13},{9,1},{13,5},{2,10},{6,14},... | collective-permute-start | bytes 491528 | tf_op jit(solution)/shard_map/ppermute | solution.py:53
  26.7 12.1 %collective-permute-start.5 = (bf16[80,2048]{1,0:T(8,128)(2,1)S(1)}, bf16[80,2048]{1,0:T(8,128)(2,1)S(1)}, u32[]{:S(2)}, u32[]{:S(2)}) collective-permute-start(bf16[80,2048]{1,0:T(8,128)(2,1)S(1)} %pad_maximum_fusion.10), channel_id=1, source_target_pairs={{1,4},{3,6},{4,1},{6,3},{9,12},{11,14},{12,9},{14,11},{17,20},{19,... | collective-permute-start | bytes 983048 | tf_op jit(solution)/shard_map/ppermute | solution.py:130
  27.4 11.5 %collective-permute-start.4 = (bf16[80,2048]{1,0:T(8,128)(2,1)S(1)}, bf16[80,2048]{1,0:T(8,128)(2,1)S(1)}, u32[]{:S(2)}, u32[]{:S(2)}) collective-permute-start(bf16[80,2048]{1,0:T(8,128)(2,1)S(1)} %pad_maximum_fusion.10), channel_id=1, source_target_pairs={{0,4},{1,0},{2,6},{3,2},{4,5},{5,1},{6,7},{7,3},{8,12},{9,8},{10,1... | collective-permute-start | bytes 983048 | tf_op jit(solution)/shard_map/ppermute | solution.py:130
  32.5 6.5 %collective-permute-start.8 = (bf16[40,2048]{1,0:T(8,128)(2,1)S(1)}, bf16[40,2048]{1,0:T(8,128)(2,1)S(1)}, u32[]{:S(2)}, u32[]{:S(2)}) collective-permute-start(bf16[40,2048]{1,0:T(8,128)(2,1)S(1)} %get-tuple-element.96), channel_id=1, source_target_pairs={{0,2},{1,3},{2,0},{3,1},{4,6},{5,7},{6,4},{7,5},{8,10},{9,11},{10,... | collective-permute-start | bytes 491528 | tf_op jit(solution)/shard_map/ppermute | solution.py:53
  39.0 15.4 %collective-permute-start.12 = (bf16[80,2048]{1,0:T(8,128)(2,1)S(1)}, bf16[80,2048]{1,0:T(8,128)(2,1)S(1)}, u32[]{:S(2)}, u32[]{:S(2)}) collective-permute-start(bf16[80,2048]{1,0:T(8,128)(2,1)S(1)} %pad_maximum_fusion.11), channel_id=1, source_target_pairs={{1,4},{3,6},{4,1},{6,3},{9,12},{11,14},{12,9},{14,11},{17,20},{19,... | collective-permute-start | bytes 983048 | tf_op jit(solution)/shard_map/ppermute | solution.py:130
  39.7 14.8 %collective-permute-start.11 = (bf16[80,2048]{1,0:T(8,128)(2,1)S(1)}, bf16[80,2048]{1,0:T(8,128)(2,1)S(1)}, u32[]{:S(2)}, u32[]{:S(2)}) collective-permute-start(bf16[80,2048]{1,0:T(8,128)(2,1)S(1)} %pad_maximum_fusion.11), channel_id=1, source_target_pairs={{0,4},{1,0},{2,6},{3,2},{4,5},{5,1},{6,7},{7,3},{8,12},{9,8},{10,1... | collective-permute-start | bytes 983048 | tf_op jit(solution)/shard_map/ppermute | solution.py:130
  43.2 3.1 %slice-start = ((s8[14680064]{0:T(1024)(128)(4,1)}), s8[4194304]{0:T(1024)(128)(4,1)S(1)}, s32[]{:S(2)}) async-start(s8[14680064]{0:T(1024)(128)(4,1)} %bitcast.102), calls=%async_computation | async-start | bytes 8388608
  43.2 3.1 %slice-start.1 = ((s8[14680064]{0:T(1024)(128)(4,1)}), s8[2097152]{0:T(1024)(128)(4,1)S(1)}, s32[]{:S(2)}) async-start(s8[14680064]{0:T(1024)(128)(4,1)} %bitcast.102), calls=%async_computation.1 | async-start | bytes 4194304
  43.2 9.3 %slice-start.4 = ((s8[14680064]{0:T(1024)(128)(4,1)}), s8[4194304]{0:T(1024)(128)(4,1)S(1)}, s32[]{:S(2)}) async-start(s8[14680064]{0:T(1024)(128)(4,1)} %bitcast.104), calls=%async_computation.4 | async-start | bytes 8388608
  43.2 9.3 %slice-start.5 = ((s8[14680064]{0:T(1024)(128)(4,1)}), s8[4194304]{0:T(1024)(128)(4,1)S(1)}, s32[]{:S(2)}) async-start(s8[14680064]{0:T(1024)(128)(4,1)} %bitcast.104), calls=%async_computation.5 | async-start | bytes 8388608
  44.6 5.3 %slice-start.2 = ((s8[14680064]{0:T(1024)(128)(4,1)}), s8[4194304]{0:T(1024)(128)(4,1)S(1)}, s32[]{:S(2)}) async-start(s8[14680064]{0:T(1024)(128)(4,1)} %bitcast.102), calls=%async_computation.2 | async-start | bytes 8388608
  44.6 6.5 %slice-start.3 = ((s8[14680064]{0:T(1024)(128)(4,1)}), s8[4194304]{0:T(1024)(128)(4,1)S(1)}, s32[]{:S(2)}) async-start(s8[14680064]{0:T(1024)(128)(4,1)} %bitcast.102), calls=%async_computation.3 | async-start | bytes 8388608
  44.6 7.9 %slice-start.6 = ((s8[14680064]{0:T(1024)(128)(4,1)}), s8[4194304]{0:T(1024)(128)(4,1)S(1)}, s32[]{:S(2)}) async-start(s8[14680064]{0:T(1024)(128)(4,1)} %bitcast.104), calls=%async_computation.6 | async-start | bytes 8388608
  46.1 6.8 %slice-start.7 = ((s8[14680064]{0:T(1024)(128)(4,1)}), s8[2097152]{0:T(1024)(128)(4,1)S(1)}, s32[]{:S(2)}) async-start(s8[14680064]{0:T(1024)(128)(4,1)} %bitcast.104), calls=%async_computation.7 | async-start | bytes 4194304
  46.2 9.3 %collective-permute-start.9 = (bf16[2,80,1792]{2,1,0:T(8,128)(2,1)S(1)}, bf16[2,80,1792]{2,1,0:T(8,128)(2,1)S(1)}, u32[]{:S(2)}, u32[]{:S(2)}) collective-permute-start(bf16[2,80,1792]{2,1,0:T(8,128)(2,1)S(1)} %pad_maximum_fusion.3), channel_id=1, source_target_pairs={{0,1},{1,0},{2,3},{3,2},{4,5},{5,4},{6,7},{7,6},{8,9},{9,8},{10,11... | collective-permute-start | bytes 1720328 | tf_op jit(solution)/shard_map/ppermute | solution.py:53
  54.4 2.9 %collective-permute-start.13 = (bf16[2,80,1792]{2,1,0:T(8,128)(2,1)S(1)}, bf16[2,80,1792]{2,1,0:T(8,128)(2,1)S(1)}, u32[]{:S(2)}, u32[]{:S(2)}) collective-permute-start(bf16[2,80,1792]{2,1,0:T(8,128)(2,1)S(1)} %pad_maximum_fusion.4), channel_id=1, source_target_pairs={{0,1},{1,0},{2,3},{3,2},{4,5},{5,4},{6,7},{7,6},{8,9},{9,8},{10,11... | collective-permute-start | bytes 1720328 | tf_op jit(solution)/shard_map/ppermute | solution.py:53
  56.4 1.8 %copy-start.3 = (bf16[160,2048]{1,0:T(8,128)(2,1)S(1)}, bf16[160,2048]{1,0:T(8,128)(2,1)}, u32[]{:S(2)}) copy-start(bf16[160,2048]{1,0:T(8,128)(2,1)} %pad_maximum_fusion.2) | copy-start | bytes 1966084
  56.4 9.5 %collective-permute-start.10 = (bf16[2,40,1792]{2,1,0:T(8,128)(2,1)}, bf16[2,40,1792]{2,1,0:T(8,128)(2,1)}, u32[]{:S(2)}, u32[]{:S(2)}) collective-permute-start(bf16[2,40,1792]{2,1,0:T(8,128)(2,1)} %pad_maximum_fusion.12), channel_id=1, source_target_pairs={{0,2},{1,3},{2,0},{3,1},{4,6},{5,7},{6,4},{7,5},{8,10},{9,11},{10,... | collective-permute-start | bytes 860168 | tf_op jit(solution)/shard_map/ppermute | solution.py:53
  61.7 5.3 %copy-start.2 = (f32[160,2304]{1,0:T(8,128)}, f32[160,2304]{1,0:T(8,128)S(1)}, u32[]{:S(2)}) copy-start(f32[160,2304]{1,0:T(8,128)S(1)} %fusion.4) | copy-start | bytes 4423684
  62.9 16.1 %collective-permute-start.17 = (bf16[2,80,2304]{2,1,0:T(8,128)(2,1)}, bf16[2,80,2304]{2,1,0:T(8,128)(2,1)}, u32[]{:S(2)}, u32[]{:S(2)}) collective-permute-start(bf16[2,80,2304]{2,1,0:T(8,128)(2,1)} %pad_maximum_fusion), channel_id=1, source_target_pairs={{0,1},{1,0},{2,3},{3,2},{4,5},{5,4},{6,7},{7,6},{8,9},{9,8},{10,11... | collective-permute-start | bytes 2211848 | tf_op jit(solution)/shard_map/ppermute | solution.py:53
  67.1 9.5 %collective-permute-start.14 = (bf16[40,1792]{1,0:T(8,128)(2,1)S(1)}, bf16[40,1792]{1,0:T(8,128)(2,1)}, u32[]{:S(2)}, u32[]{:S(2)}) collective-permute-start(bf16[40,1792]{1,0:T(8,128)(2,1)S(1)} %fusion.56), channel_id=1, source_target_pairs={{0,8},{4,12},{8,0},{12,4},{1,9},{5,13},{9,1},{13,5},{2,10},{6,14},... | collective-permute-start | bytes 430088 | tf_op jit(solution)/shard_map/ppermute | solution.py:53
  69.9 10.7 %collective-permute-start.16 = (bf16[2,40,1792]{2,1,0:T(8,128)(2,1)}, bf16[2,40,1792]{2,1,0:T(8,128)(2,1)S(1)}, u32[]{:S(2)}, u32[]{:S(2)}) collective-permute-start(bf16[2,40,1792]{2,1,0:T(8,128)(2,1)} %pad_maximum_fusion.13), channel_id=1, source_target_pairs={{0,2},{1,3},{2,0},{3,1},{4,6},{5,7},{6,4},{7,5},{8,10},{9,11},{10,... | collective-permute-start | bytes 860168 | tf_op jit(solution)/shard_map/ppermute | solution.py:53
  77.5 11.9 %collective-permute-start.15 = (bf16[40,1792]{1,0:T(8,128)(2,1)S(1)}, bf16[40,1792]{1,0:T(8,128)(2,1)S(1)}, u32[]{:S(2)}, u32[]{:S(2)}) collective-permute-start(bf16[40,1792]{1,0:T(8,128)(2,1)S(1)} %get-tuple-element.112), channel_id=1, source_target_pairs={{0,2},{1,3},{2,0},{3,1},{4,6},{5,7},{6,4},{7,5},{8,10},{9,11},{10,... | collective-permute-start | bytes 430088 | tf_op jit(solution)/shard_map/ppermute | solution.py:53
  80.4 1.1 copy-start.4
  80.5 32.8 %slice-start.8 = ((s8[14680064]{0:T(1024)(128)(4,1)}), s8[4194304]{0:T(1024)(128)(4,1)S(1)}, s32[]{:S(2)}) async-start(s8[14680064]{0:T(1024)(128)(4,1)} %bitcast.113), calls=%async_computation.8 | async-start | bytes 8388608
  80.7 32.5 %slice-start.9 = ((s8[14680064]{0:T(1024)(128)(4,1)}), s8[4194304]{0:T(1024)(128)(4,1)S(1)}, s32[]{:S(2)}) async-start(s8[14680064]{0:T(1024)(128)(4,1)} %bitcast.113), calls=%async_computation.9 | async-start | bytes 8388608
  80.7 14.0 %collective-permute-start.19 = (bf16[40,1792]{1,0:T(8,128)(2,1)S(1)}, bf16[40,1792]{1,0:T(8,128)(2,1)S(1)}, u32[]{:S(2)}, u32[]{:S(2)}) collective-permute-start(bf16[40,1792]{1,0:T(8,128)(2,1)S(1)} %fusion.54), channel_id=1, source_target_pairs={{0,8},{4,12},{8,0},{12,4},{1,9},{5,13},{9,1},{13,5},{2,10},{6,14},... | collective-permute-start | bytes 430088 | tf_op jit(solution)/shard_map/ppermute | solution.py:53
  80.8 15.6 %collective-permute-start.21 = (bf16[2,40,2304]{2,1,0:T(8,128)(2,1)S(1)}, bf16[2,40,2304]{2,1,0:T(8,128)(2,1)S(1)}, u32[]{:S(2)}, u32[]{:S(2)}) collective-permute-start(bf16[2,40,2304]{2,1,0:T(8,128)(2,1)S(1)} %pad_maximum_fusion.8), channel_id=1, source_target_pairs={{0,2},{1,3},{2,0},{3,1},{4,6},{5,7},{6,4},{7,5},{8,10},{9,11},{10,... | collective-permute-start | bytes 1105928 | tf_op jit(solution)/shard_map/ppermute | solution.py:53
  85.6 27.7 %slice-start.10 = ((s8[14680064]{0:T(1024)(128)(4,1)}), s8[4194304]{0:T(1024)(128)(4,1)S(1)}, s32[]{:S(2)}) async-start(s8[14680064]{0:T(1024)(128)(4,1)} %bitcast.113), calls=%async_computation.10 | async-start | bytes 8388608
  89.4 14.9 %collective-permute-start.23 = (bf16[80,1792]{1,0:T(8,128)(2,1)S(1)}, bf16[80,1792]{1,0:T(8,128)(2,1)S(1)}, u32[]{:S(2)}, u32[]{:S(2)}) collective-permute-start(bf16[80,1792]{1,0:T(8,128)(2,1)S(1)} %pad_maximum_fusion.14), channel_id=1, source_target_pairs={{1,4},{3,6},{4,1},{6,3},{9,12},{11,14},{12,9},{14,11},{17,20},{19,... | collective-permute-start | bytes 860168 | tf_op jit(solution)/shard_map/ppermute | solution.py:130
  90.1 15.8 %collective-permute-start.22 = (bf16[80,1792]{1,0:T(8,128)(2,1)S(1)}, bf16[80,1792]{1,0:T(8,128)(2,1)S(1)}, u32[]{:S(2)}, u32[]{:S(2)}) collective-permute-start(bf16[80,1792]{1,0:T(8,128)(2,1)S(1)} %pad_maximum_fusion.14), channel_id=1, source_target_pairs={{0,4},{1,0},{2,6},{3,2},{4,5},{5,1},{6,7},{7,3},{8,12},{9,8},{10,1... | collective-permute-start | bytes 860168 | tf_op jit(solution)/shard_map/ppermute | solution.py:130
  94.6 7.0 %collective-permute-start.18 = (bf16[2,80,1280]{2,1,0:T(8,128)(2,1)S(1)}, bf16[2,80,1280]{2,1,0:T(8,128)(2,1)S(1)}, u32[]{:S(2)}, u32[]{:S(2)}) collective-permute-start(bf16[2,80,1280]{2,1,0:T(8,128)(2,1)S(1)} %pad_maximum_fusion.7), channel_id=1, source_target_pairs={{0,1},{1,0},{2,3},{3,2},{4,5},{5,4},{6,7},{7,6},{8,9},{9,8},{10,11... | collective-permute-start | bytes 1228808 | tf_op jit(solution)/shard_map/ppermute | solution.py:53
  94.8 18.4 %slice-start.11 = ((s8[14680064]{0:T(1024)(128)(4,1)}), s8[2097152]{0:T(1024)(128)(4,1)S(1)}, s32[]{:S(2)}) async-start(s8[14680064]{0:T(1024)(128)(4,1)} %bitcast.113), calls=%async_computation.11 | async-start | bytes 4194304
  94.8 6.1 %collective-permute-start.20 = (bf16[40,1792]{1,0:T(8,128)(2,1)S(1)}, bf16[40,1792]{1,0:T(8,128)(2,1)S(1)}, u32[]{:S(2)}, u32[]{:S(2)}) collective-permute-start(bf16[40,1792]{1,0:T(8,128)(2,1)S(1)} %get-tuple-element.110), channel_id=1, source_target_pairs={{0,2},{1,3},{2,0},{3,1},{4,6},{5,7},{6,4},{7,5},{8,10},{9,11},{10,... | collective-permute-start | bytes 430088 | tf_op jit(solution)/shard_map/ppermute | solution.py:53
  96.5 11.7 %collective-permute-start.25 = (bf16[40,2304]{1,0:T(8,128)(2,1)S(1)}, bf16[40,2304]{1,0:T(8,128)(2,1)S(1)}, u32[]{:S(2)}, u32[]{:S(2)}) collective-permute-start(bf16[40,2304]{1,0:T(8,128)(2,1)S(1)} %fusion.48), channel_id=1, source_target_pairs={{0,8},{4,12},{8,0},{12,4},{1,9},{5,13},{9,1},{13,5},{2,10},{6,14},... | collective-permute-start | bytes 552968 | tf_op jit(solution)/shard_map/ppermute | solution.py:53
  100.9 13.8 %collective-permute-start.27 = (bf16[80,1792]{1,0:T(8,128)(2,1)S(1)}, bf16[80,1792]{1,0:T(8,128)(2,1)S(1)}, u32[]{:S(2)}, u32[]{:S(2)}) collective-permute-start(bf16[80,1792]{1,0:T(8,128)(2,1)S(1)} %pad_maximum_fusion.15), channel_id=1, source_target_pairs={{1,4},{3,6},{4,1},{6,3},{9,12},{11,14},{12,9},{14,11},{17,20},{19,... | collective-permute-start | bytes 860168 | tf_op jit(solution)/shard_map/ppermute | solution.py:130
  101.6 13.1 %collective-permute-start.26 = (bf16[80,1792]{1,0:T(8,128)(2,1)S(1)}, bf16[80,1792]{1,0:T(8,128)(2,1)S(1)}, u32[]{:S(2)}, u32[]{:S(2)}) collective-permute-start(bf16[80,1792]{1,0:T(8,128)(2,1)S(1)} %pad_maximum_fusion.15), channel_id=1, source_target_pairs={{0,4},{1,0},{2,6},{3,2},{4,5},{5,1},{6,7},{7,3},{8,12},{9,8},{10,1... | collective-permute-start | bytes 860168 | tf_op jit(solution)/shard_map/ppermute | solution.py:130
  104.4 8.0 %collective-permute-start.24 = (bf16[2,40,1280]{2,1,0:T(8,128)(2,1)S(1)}, bf16[2,40,1280]{2,1,0:T(8,128)(2,1)S(1)}, u32[]{:S(2)}, u32[]{:S(2)}) collective-permute-start(bf16[2,40,1280]{2,1,0:T(8,128)(2,1)S(1)} %pad_maximum_fusion.16), channel_id=1, source_target_pairs={{0,2},{1,3},{2,0},{3,1},{4,6},{5,7},{6,4},{7,5},{8,10},{9,11},{10,... | collective-permute-start | bytes 614408 | tf_op jit(solution)/shard_map/ppermute | solution.py:53
  108.2 7.3 %collective-permute-start.29 = (bf16[40,2304]{1,0:T(8,128)(2,1)S(1)}, bf16[40,2304]{1,0:T(8,128)(2,1)S(1)}, u32[]{:S(2)}, u32[]{:S(2)}) collective-permute-start(bf16[40,2304]{1,0:T(8,128)(2,1)S(1)} %get-tuple-element.88), channel_id=1, source_target_pairs={{0,2},{1,3},{2,0},{3,1},{4,6},{5,7},{6,4},{7,5},{8,10},{9,11},{10,... | collective-permute-start | bytes 552968 | tf_op jit(solution)/shard_map/ppermute | solution.py:53
  112.5 6.6 %collective-permute-start.28 = (bf16[40,1280]{1,0:T(8,128)(2,1)S(1)}, bf16[40,1280]{1,0:T(8,128)(2,1)S(1)}, u32[]{:S(2)}, u32[]{:S(2)}) collective-permute-start(bf16[40,1280]{1,0:T(8,128)(2,1)S(1)} %fusion.60), channel_id=1, source_target_pairs={{0,8},{4,12},{8,0},{12,4},{1,9},{5,13},{9,1},{13,5},{2,10},{6,14},... | collective-permute-start | bytes 307208 | tf_op jit(solution)/shard_map/ppermute | solution.py:53
  115.5 7.3 %collective-permute-start.33 = (bf16[80,2304]{1,0:T(8,128)(2,1)S(1)}, bf16[80,2304]{1,0:T(8,128)(2,1)S(1)}, u32[]{:S(2)}, u32[]{:S(2)}) collective-permute-start(bf16[80,2304]{1,0:T(8,128)(2,1)S(1)} %pad_maximum_fusion.9), channel_id=1, source_target_pairs={{1,4},{3,6},{4,1},{6,3},{9,12},{11,14},{12,9},{14,11},{17,20},{19,... | collective-permute-start | bytes 1105928 | tf_op jit(solution)/shard_map/ppermute | solution.py:130
  116.2 10.5 %collective-permute-start.32 = (bf16[80,2304]{1,0:T(8,128)(2,1)S(1)}, bf16[80,2304]{1,0:T(8,128)(2,1)S(1)}, u32[]{:S(2)}, u32[]{:S(2)}) collective-permute-start(bf16[80,2304]{1,0:T(8,128)(2,1)S(1)} %pad_maximum_fusion.9), channel_id=1, source_target_pairs={{0,4},{1,0},{2,6},{3,2},{4,5},{5,1},{6,7},{7,3},{8,12},{9,8},{10,1... | collective-permute-start | bytes 1105928 | tf_op jit(solution)/shard_map/ppermute | solution.py:130
  119.1 9.5 %collective-permute-start.31 = (bf16[40,1280]{1,0:T(8,128)(2,1)S(1)}, bf16[40,1280]{1,0:T(8,128)(2,1)S(1)}, u32[]{:S(2)}, u32[]{:S(2)}) collective-permute-start(bf16[40,1280]{1,0:T(8,128)(2,1)S(1)} %get-tuple-element.116), channel_id=1, source_target_pairs={{0,2},{1,3},{2,0},{3,1},{4,6},{5,7},{6,4},{7,5},{8,10},{9,11},{10,... | collective-permute-start | bytes 307208 | tf_op jit(solution)/shard_map/ppermute | solution.py:53
  122.7 10.5 %collective-permute-start.30 = (bf16[80,2048]{1,0:T(8,128)(2,1)S(1)}, bf16[80,2048]{1,0:T(8,128)(2,1)S(1)}, u32[]{:S(2)}, u32[]{:S(2)}) collective-permute-start(bf16[80,2048]{1,0:T(8,128)(2,1)S(1)} %slice.500), channel_id=1, source_target_pairs={{0,1},{1,0},{2,3},{3,2},{4,5},{5,4},{6,7},{7,6},{8,9},{9,8},{10,11... | collective-permute-start | bytes 983048 | tf_op jit(solution)/shard_map/ppermute | solution.py:53
  128.7 6.7 %collective-permute-start.36 = (bf16[80,1280]{1,0:T(8,128)(2,1)S(1)}, bf16[80,1280]{1,0:T(8,128)(2,1)S(1)}, u32[]{:S(2)}, u32[]{:S(2)}) collective-permute-start(bf16[80,1280]{1,0:T(8,128)(2,1)S(1)} %pad_maximum_fusion.17), channel_id=1, source_target_pairs={{1,4},{3,6},{4,1},{6,3},{9,12},{11,14},{12,9},{14,11},{17,20},{19,... | collective-permute-start | bytes 614408 | tf_op jit(solution)/shard_map/ppermute | solution.py:130
  129.4 8.6 %collective-permute-start.35 = (bf16[80,1280]{1,0:T(8,128)(2,1)S(1)}, bf16[80,1280]{1,0:T(8,128)(2,1)S(1)}, u32[]{:S(2)}, u32[]{:S(2)}) collective-permute-start(bf16[80,1280]{1,0:T(8,128)(2,1)S(1)} %pad_maximum_fusion.17), channel_id=1, source_target_pairs={{0,4},{1,0},{2,6},{3,2},{4,5},{5,1},{6,7},{7,3},{8,12},{9,8},{10,1... | collective-permute-start | bytes 614408 | tf_op jit(solution)/shard_map/ppermute | solution.py:130
  133.3 10.1 %collective-permute-start.34 = (bf16[80,2048]{1,0:T(8,128)(2,1)S(1)}, bf16[80,2048]{1,0:T(8,128)(2,1)S(1)}, u32[]{:S(2)}, u32[]{:S(2)}) collective-permute-start(bf16[80,2048]{1,0:T(8,128)(2,1)S(1)} %get-tuple-element.75), channel_id=1, source_target_pairs={{0,2},{1,3},{2,0},{3,1},{4,6},{5,7},{6,4},{7,5},{8,10},{9,11},{10,... | collective-permute-start | bytes 983048 | tf_op jit(solution)/shard_map/ppermute | solution.py:53
  139.2 4.3 %collective-permute-start.37 = (bf16[80,2048]{1,0:T(8,128)(2,1)S(1)}, bf16[80,2048]{1,0:T(8,128)(2,1)S(1)}, u32[]{:S(2)}, u32[]{:S(2)}) collective-permute-start(bf16[80,2048]{1,0:T(8,128)(2,1)S(1)} %slice.499), channel_id=1, source_target_pairs={{0,1},{1,0},{2,3},{3,2},{4,5},{5,4},{6,7},{7,6},{8,9},{9,8},{10,11... | collective-permute-start | bytes 983048 | tf_op jit(solution)/shard_map/ppermute | solution.py:53
  143.6 9.3 %collective-permute-start.38 = (bf16[80,2048]{1,0:T(8,128)(2,1)S(1)}, bf16[80,2048]{1,0:T(8,128)(2,1)S(1)}, u32[]{:S(2)}, u32[]{:S(2)}) collective-permute-start(bf16[80,2048]{1,0:T(8,128)(2,1)S(1)} %fusion.41), channel_id=1, source_target_pairs={{0,2},{1,3},{2,0},{3,1},{4,6},{5,7},{6,4},{7,5},{8,10},{9,11},{10,... | collective-permute-start | bytes 983048 | tf_op jit(solution)/shard_map/ppermute | solution.py:53
  145.4 8.6 %collective-permute-start.39 = (bf16[80,2048]{1,0:T(8,128)(2,1)S(1)}, bf16[80,2048]{1,0:T(8,128)(2,1)S(1)}, u32[]{:S(2)}, u32[]{:S(2)}) collective-permute-start(bf16[80,2048]{1,0:T(8,128)(2,1)S(1)} %get-tuple-element.71), channel_id=1, source_target_pairs={{0,1},{1,0},{2,3},{3,2},{4,5},{5,4},{6,7},{7,6},{8,9},{9,8},{10,11... | collective-permute-start | bytes 983048 | tf_op jit(solution)/shard_map/ppermute | solution.py:53
  153.0 1.7 %collective-permute-start.40 = (bf16[80,2048]{1,0:T(8,128)(2,1)S(1)}, bf16[80,2048]{1,0:T(8,128)(2,1)S(1)}, u32[]{:S(2)}, u32[]{:S(2)}) collective-permute-start(bf16[80,2048]{1,0:T(8,128)(2,1)S(1)} %get-tuple-element.73), channel_id=1, source_target_pairs={{0,1},{1,0},{2,3},{3,2},{4,5},{5,4},{6,7},{7,6},{8,9},{9,8},{10,11... | collective-permute-start | bytes 983048 | tf_op jit(solution)/shard_map/ppermute | solution.py:53

commit v16 on v13

--- a/solution.py
+++ b/solution.py
@@ -39,7 +39,7 @@
     "c11.columns": ["c10.down"],
     "b0.total": ["c11.columns"],
     "c11.cores": ["b0.total"],
-    "c11.down": ["b0.all"],
+    "c11.down": ["b0.total"],
     "b1.total": ["c11.down"],
 }
 

time: 146 us -> 147 us (level)
  matrix products: 25.6 us -> 33.7 us
  waiting for transfers between devices: 55.8 us -> 53.2 us
  starting transfers between devices: 49 us -> 46.5 us
  other arithmetic: 6.89 us -> 4.98 us
    dot_general x17, matrix products: 24.8 us -> 32.8 us  [dot(): return jnp.dot(a, b, preferred_element_type=jnp.float32)]
    ppermute x29, waiting for transfers between devices: 51.8 us -> 48.5 us  [flip(): return lax.ppermute(value, axis, [(i, i ^ bit) for i in range(count)])]
    ppermute x29, starting transfers between devices: 32.9 us -> 31 us  [flip(): return lax.ppermute(value, axis, [(i, i ^ bit) for i in range(count)])]
  transfers between devices with their start and end apart: 41 -> 41, of which waited for: 17 -> 15; matrix products, arithmetic and copies ran while one was open for 18% -> 24% of each run, Pallas kernels for 4% -> 4%
where the time goes in v16:
time: 147 us
  waiting for transfers between devices  53.2 us (36%)
  starting transfers between devices  46.5 us (32%)
  matrix products  33.7 us (23%)
  Pallas kernels  5.84 us (4%)
  other arithmetic  4.98 us (3%)
  local copies, waits for them, and re-layouts  1.63 us (1%)
    ppermute x29, waiting for transfers between devices, flip(): return lax.ppermute(value, axis, [(i, i ^ bit) for i in range(count)])  48.5 us
    dot_general x17, matrix products, dot(): return jnp.dot(a, b, preferred_element_type=jnp.float32)  32.8 us
    ppermute x29, starting transfers between devices, flip(): return lax.ppermute(value, axis, [(i, i ^ bit) for i in range(count)])  31 us
    ppermute x12, starting transfers between devices, move(): return lax.ppermute(value, ('row', 'col'), pairs)  15.5 us
    pallas_call x1, Pallas kernels, pull(): pl.pallas_call(functools.partial(pull_kernel, first, end), in_specs=[pl.B...  5.84 us
    ppermute x12, waiting for transfers between devices, move(): return lax.ppermute(value, ('row', 'col'), pairs)  4.69 us
  transfers between devices with their start and end apart: 41, of which 15 were waited for; matrix products, arithmetic and copies ran while one was open for 24% of the time, Pallas kernels for 4%

profile of v16, /device:TPU:0, one launch (start us, length us, event | category | flops | bytes accessed | tf_op | source)
XLA Modules:
  0.0 146.8 jit_solution(3755340344505617823)
XLA Ops:
  0.5 0.9 fusion.80
  1.5 1.4 fusion.70
  3.2 2.6 %collective-permute-start.1 = (bf16[40,2048]{1,0:T(8,128)(2,1)S(1)}, bf16[40,2048]{1,0:T(8,128)(2,1)S(1)}, u32[]{:S(2)}, u32[]{:S(2)}) collective-permute-start(bf16[40,2048]{1,0:T(8,128)(2,1)S(1)} %slice.314), channel_id=1, source_target_pairs={{0,2},{1,3},{2,0},{3,1},{4,6},{5,7},{6,4},{7,5},{8,10},{9,11},{10,... | collective-permute-start | bytes 491528 | tf_op jit(solution)/shard_map/ppermute | solution.py:53
  5.8 4.9 %collective-permute-done.1 = bf16[40,2048]{1,0:T(8,128)(2,1)S(1)} collective-permute-done((bf16[40,2048]{1,0:T(8,128)(2,1)S(1)}, bf16[40,2048]{1,0:T(8,128)(2,1)S(1)}, u32[]{:S(2)}, u32[]{:S(2)}) %collective-permute-start.1) | collective-permute-done | bytes 163872 | tf_op jit(solution)/shard_map/ppermute | solution.py:53
  10.7 2.9 %collective-permute-start.2 = (bf16[40,2048]{1,0:T(8,128)(2,1)S(1)}, bf16[40,2048]{1,0:T(8,128)(2,1)S(1)}, u32[]{:S(2)}, u32[]{:S(2)}) collective-permute-start(bf16[40,2048]{1,0:T(8,128)(2,1)S(1)} %slice_add_fusion.19), channel_id=1, source_target_pairs={{0,8},{4,12},{8,0},{12,4},{1,9},{5,13},{9,1},{13,5},{2,10},{6,14},... | collective-permute-start | bytes 491528 | tf_op jit(solution)/shard_map/ppermute | solution.py:53
  14.2 1.6 %collective-permute-start.6 = (bf16[40,2048]{1,0:T(8,128)(2,1)S(1)}, bf16[40,2048]{1,0:T(8,128)(2,1)S(1)}, u32[]{:S(2)}, u32[]{:S(2)}) collective-permute-start(bf16[40,2048]{1,0:T(8,128)(2,1)S(1)} %slice.316), channel_id=1, source_target_pairs={{0,2},{1,3},{2,0},{3,1},{4,6},{5,7},{6,4},{7,5},{8,10},{9,11},{10,... | collective-permute-start | bytes 491528 | tf_op jit(solution)/shard_map/ppermute | solution.py:53
  15.8 5.4 %collective-permute-done.2 = bf16[40,2048]{1,0:T(8,128)(2,1)S(1)} collective-permute-done((bf16[40,2048]{1,0:T(8,128)(2,1)S(1)}, bf16[40,2048]{1,0:T(8,128)(2,1)S(1)}, u32[]{:S(2)}, u32[]{:S(2)}) %collective-permute-start.2) | collective-permute-done | bytes 163872 | tf_op jit(solution)/shard_map/ppermute | solution.py:53
  21.2 1.6 %collective-permute-start.3 = (bf16[40,2048]{1,0:T(8,128)(2,1)S(1)}, bf16[40,2048]{1,0:T(8,128)(2,1)S(1)}, u32[]{:S(2)}, u32[]{:S(2)}) collective-permute-start(bf16[40,2048]{1,0:T(8,128)(2,1)S(1)} %get-tuple-element.104), channel_id=1, source_target_pairs={{0,2},{1,3},{2,0},{3,1},{4,6},{5,7},{6,4},{7,5},{8,10},{9,11},{10,... | collective-permute-start | bytes 491528 | tf_op jit(solution)/shard_map/ppermute | solution.py:53
  22.9 3.7 %collective-permute-done.3 = bf16[40,2048]{1,0:T(8,128)(2,1)S(1)} collective-permute-done((bf16[40,2048]{1,0:T(8,128)(2,1)S(1)}, bf16[40,2048]{1,0:T(8,128)(2,1)S(1)}, u32[]{:S(2)}, u32[]{:S(2)}) %collective-permute-start.3) | collective-permute-done | bytes 163872 | tf_op jit(solution)/shard_map/ppermute | solution.py:53
  26.6 1.6 %collective-permute-start.4 = (bf16[80,2048]{1,0:T(8,128)(2,1)S(1)}, bf16[80,2048]{1,0:T(8,128)(2,1)S(1)}, u32[]{:S(2)}, u32[]{:S(2)}) collective-permute-start(bf16[80,2048]{1,0:T(8,128)(2,1)S(1)} %pad_maximum_fusion.11), channel_id=1, source_target_pairs={{0,4},{1,0},{2,6},{3,2},{4,5},{5,1},{6,7},{7,3},{8,12},{9,8},{10,1... | collective-permute-start | bytes 983048 | tf_op jit(solution)/shard_map/ppermute | solution.py:130
  28.2 0.7 collective-permute-start.5
  28.9 3.5 %collective-permute-done.7 = bf16[40,2048]{1,0:T(8,128)(2,1)S(1)} collective-permute-done((bf16[40,2048]{1,0:T(8,128)(2,1)S(1)}, bf16[40,2048]{1,0:T(8,128)(2,1)S(1)}, u32[]{:S(2)}, u32[]{:S(2)}) %collective-permute-start.7) | collective-permute-done | bytes 163872 | tf_op jit(solution)/shard_map/ppermute | solution.py:53
  32.4 0.6 collective-permute-start.8
  33.0 5.8 %shard_map.55 = (bf16[2048,1792]{1,0:T(8,128)(2,1)S(1)}, bf16[2048,1792]{1,0:T(8,128)(2,1)S(1)}) custom-call(s32[4]{0:T(128)S(1)} %copy-done, bf16[2048,3584]{1,0:T(8,128)(2,1)} %gate_ref.1, bf16[2048,3584]{1,0:T(8,128)(2,1)} %up_ref.1), custom_call_target="tpu_custom_call" | custom-call | tf_op jit(solution)/shard_map/pallas_call | solution.py:73
  39.0 1.4 fusion.93
  40.4 1.4 fusion.94
  41.8 1.0 copy-done.2
  43.1 0.9 collective-permute-start.12
  44.0 1.1 collective-permute-done.9
  45.1 1.3 slice_add_fusion.7
  46.5 4.5 %fusion.12 = f32[160,1792]{1,0:T(8,128)S(1)} fusion(bf16[160,2048]{1,0:T(8,128)(2,1)S(1)} %pad_maximum_fusion.1, bf16[2048,3584]{1,0:T(8,128)(2,1)} %gate_ref.1), kind=kOutput, calls=%fused_computation.12 | convolution fusion | flops 1174405120 | bytes 9142272 | tf_op jit(solution)/shard_map/dot_general | solution.py:48
  51.0 4.6 %fusion.10 = f32[160,1792]{1,0:T(8,128)S(1)} fusion(bf16[160,2048]{1,0:T(8,128)(2,1)S(1)} %pad_maximum_fusion.1, bf16[2048,3584]{1,0:T(8,128)(2,1)} %up_ref.1), kind=kOutput, calls=%fused_computation.10 | convolution fusion | flops 1174405120 | bytes 9142272 | tf_op jit(solution)/shard_map/dot_general | solution.py:48
  55.8 0.7 collective-permute-start.13
  56.6 1.6 %collective-permute-start.10 = (bf16[2,40,1792]{2,1,0:T(8,128)(2,1)S(1)}, bf16[2,40,1792]{2,1,0:T(8,128)(2,1)S(1)}, u32[]{:S(2)}, u32[]{:S(2)}) collective-permute-start(bf16[2,40,1792]{2,1,0:T(8,128)(2,1)S(1)} %pad_maximum_fusion.13), channel_id=1, source_target_pairs={{0,2},{1,3},{2,0},{3,1},{4,6},{5,7},{6,4},{7,5},{8,10},{9,11},{10,... | collective-permute-start | bytes 860168 | tf_op jit(solution)/shard_map/ppermute | solution.py:53
  58.3 5.5 %fusion.4 = f32[160,2304]{1,0:T(8,128)S(1)} fusion(bf16[160,2048]{1,0:T(8,128)(2,1)S(1)} %pad_maximum_fusion.2, bf16[2048,3584]{1,0:T(8,128)(2,1)} %gate_ref.1), kind=kOutput, calls=%fused_computation.4 | convolution fusion | flops 1509949440 | bytes 11567104 | tf_op jit(solution)/shard_map/dot_general | solution.py:48
  63.9 1.7 %fusion.2 = f32[160,2304]{1,0:T(8,128)S(1)} fusion(bf16[160,2048]{1,0:T(8,128)(2,1)S(1)} %pad_maximum_fusion.2, bf16[2048,3584]{1,0:T(8,128)(2,1)S(1)} %bitcast.108), kind=kOutput, calls=%fused_computation.2 | convolution fusion | flops 1509949440 | bytes 11567104 | tf_op jit(solution)/shard_map/dot_general | solution.py:48
  66.3 3.4 %collective-permute-start.14 = (bf16[40,1792]{1,0:T(8,128)(2,1)S(1)}, bf16[40,1792]{1,0:T(8,128)(2,1)S(1)}, u32[]{:S(2)}, u32[]{:S(2)}) collective-permute-start(bf16[40,1792]{1,0:T(8,128)(2,1)S(1)} %fusion.47), channel_id=1, source_target_pairs={{0,8},{4,12},{8,0},{12,4},{1,9},{5,13},{9,1},{13,5},{2,10},{6,14},... | collective-permute-start | bytes 430088 | tf_op jit(solution)/shard_map/ppermute | solution.py:53
  69.9 1.5 %collective-permute-start.16 = (bf16[2,40,1792]{2,1,0:T(8,128)(2,1)S(1)}, bf16[2,40,1792]{2,1,0:T(8,128)(2,1)S(1)}, u32[]{:S(2)}, u32[]{:S(2)}) collective-permute-start(bf16[2,40,1792]{2,1,0:T(8,128)(2,1)S(1)} %pad_maximum_fusion.14), channel_id=1, source_target_pairs={{0,2},{1,3},{2,0},{3,1},{4,6},{5,7},{6,4},{7,5},{8,10},{9,11},{10,... | collective-permute-start | bytes 860168 | tf_op jit(solution)/shard_map/ppermute | solution.py:53
  71.4 5.6 %collective-permute-done.14 = bf16[40,1792]{1,0:T(8,128)(2,1)S(1)} collective-permute-done((bf16[40,1792]{1,0:T(8,128)(2,1)S(1)}, bf16[40,1792]{1,0:T(8,128)(2,1)S(1)}, u32[]{:S(2)}, u32[]{:S(2)}) %collective-permute-start.14) | collective-permute-done | bytes 143392 | tf_op jit(solution)/shard_map/ppermute | solution.py:53
  77.0 1.5 collective-permute-start.15
  78.7 0.7 collective-permute-start.21
  79.6 1.0 fusion.16
  80.7 3.7 %fusion.18 = f32[160,1280]{1,0:T(8,128)S(1)} fusion(bf16[160,2048]{1,0:T(8,128)(2,1)S(1)} %pad_maximum_fusion.2, bf16[2048,3584]{1,0:T(8,128)(2,1)} %gate_ref.1), kind=kOutput, calls=%fused_computation.18 | convolution fusion | flops 838860800 | bytes 6717440 | tf_op jit(solution)/shard_map/dot_general | solution.py:48
  84.6 3.2 %collective-permute-start.22 = (bf16[80,1792]{1,0:T(8,128)(2,1)S(1)}, bf16[80,1792]{1,0:T(8,128)(2,1)S(1)}, u32[]{:S(2)}, u32[]{:S(2)}) collective-permute-start(bf16[80,1792]{1,0:T(8,128)(2,1)S(1)} %pad_maximum_fusion.15), channel_id=1, source_target_pairs={{0,4},{1,0},{2,6},{3,2},{4,5},{5,1},{6,7},{7,3},{8,12},{9,8},{10,1... | collective-permute-start | bytes 860168 | tf_op jit(solution)/shard_map/ppermute | solution.py:130
  87.8 0.7 collective-permute-start.23
  88.5 1.3 collective-permute-start.19
  89.8 0.6 collective-permute-done.21
  90.7 1.4 collective-permute-start.24
  92.1 2.3 %collective-permute-done.19 = bf16[40,1792]{1,0:T(8,128)(2,1)S(1)} collective-permute-done((bf16[40,1792]{1,0:T(8,128)(2,1)S(1)}, bf16[40,1792]{1,0:T(8,128)(2,1)S(1)}, u32[]{:S(2)}, u32[]{:S(2)}) %collective-permute-start.19) | collective-permute-done | bytes 143392 | tf_op jit(solution)/shard_map/ppermute | solution.py:53
  94.4 1.9 %collective-permute-start.26 = (bf16[80,1792]{1,0:T(8,128)(2,1)S(1)}, bf16[80,1792]{1,0:T(8,128)(2,1)S(1)}, u32[]{:S(2)}, u32[]{:S(2)}) collective-permute-start(bf16[80,1792]{1,0:T(8,128)(2,1)S(1)} %pad_maximum_fusion.16), channel_id=1, source_target_pairs={{0,4},{1,0},{2,6},{3,2},{4,5},{5,1},{6,7},{7,3},{8,12},{9,8},{10,1... | collective-permute-start | bytes 860168 | tf_op jit(solution)/shard_map/ppermute | solution.py:130
  96.2 0.7 collective-permute-start.27
  97.0 4.7 %collective-permute-done.25 = bf16[40,2304]{1,0:T(8,128)(2,1)S(1)} collective-permute-done((bf16[40,2304]{1,0:T(8,128)(2,1)S(1)}, bf16[40,2304]{1,0:T(8,128)(2,1)S(1)}, u32[]{:S(2)}, u32[]{:S(2)}) %collective-permute-start.25) | collective-permute-done | bytes 184352 | tf_op jit(solution)/shard_map/ppermute | solution.py:53
  101.8 0.9 collective-permute-start.28
  102.9 1.4 fusion.8
  104.4 4.1 %collective-permute-done.28 = bf16[40,2304]{1,0:T(8,128)(2,1)S(1)} collective-permute-done((bf16[40,2304]{1,0:T(8,128)(2,1)S(1)}, bf16[40,2304]{1,0:T(8,128)(2,1)S(1)}, u32[]{:S(2)}, u32[]{:S(2)}) %collective-permute-start.28) | collective-permute-done | bytes 184352 | tf_op jit(solution)/shard_map/ppermute | solution.py:53
  108.5 0.7 collective-permute-start.32
  109.3 0.7 collective-permute-start.33
  109.9 1.4 fusion.91
  111.4 1.5 %collective-permute-start.31 = (bf16[40,1280]{1,0:T(8,128)(2,1)S(1)}, bf16[40,1280]{1,0:T(8,128)(2,1)S(1)}, u32[]{:S(2)}, u32[]{:S(2)}) collective-permute-start(bf16[40,1280]{1,0:T(8,128)(2,1)S(1)} %get-tuple-element.116), channel_id=1, source_target_pairs={{0,2},{1,3},{2,0},{3,1},{4,6},{5,7},{6,4},{7,5},{8,10},{9,11},{10,... | collective-permute-start | bytes 307208 | tf_op jit(solution)/shard_map/ppermute | solution.py:53
  112.9 1.1 collective-permute-start.29
  114.1 2.8 %collective-permute-done.32 = bf16[80,2304]{1,0:T(8,128)(2,1)S(1)} collective-permute-done((bf16[80,2304]{1,0:T(8,128)(2,1)S(1)}, bf16[80,2304]{1,0:T(8,128)(2,1)S(1)}, u32[]{:S(2)}, u32[]{:S(2)}) %collective-permute-start.32) | collective-permute-done | bytes 368672 | tf_op jit(solution)/shard_map/ppermute | solution.py:130
  116.9 1.7 %fusion = f32[160,2048]{1,0:T(8,128)S(1)} fusion(bf16[3584,2048]{1,0:T(8,128)(2,1)S(1)} %bitcast.117, bf16[80,2304]{1,0:T(8,128)(2,1)S(1)} %get-tuple-element.90, bf16[80,2304]{1,0:T(8,128)(2,1)S(1)} %get-tuple-element.89), kind=kOutput, calls=%fused_computation | convolution fusion | flops 1511424000 | bytes 11485184 | tf_op jit(solution)/shard_map/dot_general | solution.py:48
  118.7 3.9 %collective-permute-start.35 = (bf16[80,1280]{1,0:T(8,128)(2,1)S(1)}, bf16[80,1280]{1,0:T(8,128)(2,1)S(1)}, u32[]{:S(2)}, u32[]{:S(2)}) collective-permute-start(bf16[80,1280]{1,0:T(8,128)(2,1)S(1)} %pad_maximum_fusion.18), channel_id=1, source_target_pairs={{0,4},{1,0},{2,6},{3,2},{4,5},{5,1},{6,7},{7,3},{8,12},{9,8},{10,1... | collective-permute-start | bytes 614408 | tf_op jit(solution)/shard_map/ppermute | solution.py:130
  122.7 0.7 collective-permute-start.36
  123.4 1.5 %collective-permute-start.34 = (bf16[80,2048]{1,0:T(8,128)(2,1)S(1)}, bf16[80,2048]{1,0:T(8,128)(2,1)S(1)}, u32[]{:S(2)}, u32[]{:S(2)}) collective-permute-start(bf16[80,2048]{1,0:T(8,128)(2,1)S(1)} %get-tuple-element.77), channel_id=1, source_target_pairs={{0,2},{1,3},{2,0},{3,1},{4,6},{5,7},{6,4},{7,5},{8,10},{9,11},{10,... | collective-permute-start | bytes 983048 | tf_op jit(solution)/shard_map/ppermute | solution.py:53
  124.9 1.9 %collective-permute-done.35 = bf16[80,1280]{1,0:T(8,128)(2,1)S(1)} collective-permute-done((bf16[80,1280]{1,0:T(8,128)(2,1)S(1)}, bf16[80,1280]{1,0:T(8,128)(2,1)S(1)}, u32[]{:S(2)}, u32[]{:S(2)}) %collective-permute-start.35) | collective-permute-done | bytes 204832 | tf_op jit(solution)/shard_map/ppermute | solution.py:130
  126.8 1.1 fusion.92
  127.9 2.0 %collective-permute-start.37 = (bf16[80,2048]{1,0:T(8,128)(2,1)S(1)}, bf16[80,2048]{1,0:T(8,128)(2,1)S(1)}, u32[]{:S(2)}, u32[]{:S(2)}) collective-permute-start(bf16[80,2048]{1,0:T(8,128)(2,1)S(1)} %slice.503), channel_id=1, source_target_pairs={{0,1},{1,0},{2,3},{3,2},{4,5},{5,4},{6,7},{7,6},{8,9},{9,8},{10,11... | collective-permute-start | bytes 983048 | tf_op jit(solution)/shard_map/ppermute | solution.py:53
  129.9 3.8 %collective-permute-done.34 = bf16[80,2048]{1,0:T(8,128)(2,1)S(1)} collective-permute-done((bf16[80,2048]{1,0:T(8,128)(2,1)S(1)}, bf16[80,2048]{1,0:T(8,128)(2,1)S(1)}, u32[]{:S(2)}, u32[]{:S(2)}) %collective-permute-start.34) | collective-permute-done | bytes 327712 | tf_op jit(solution)/shard_map/ppermute | solution.py:53
  133.9 1.5 %collective-permute-start.38 = (bf16[80,2048]{1,0:T(8,128)(2,1)S(1)}, bf16[80,2048]{1,0:T(8,128)(2,1)S(1)}, u32[]{:S(2)}, u32[]{:S(2)}) collective-permute-start(bf16[80,2048]{1,0:T(8,128)(2,1)S(1)} %fusion.35), channel_id=1, source_target_pairs={{0,2},{1,3},{2,0},{3,1},{4,6},{5,7},{6,4},{7,5},{8,10},{9,11},{10,... | collective-permute-start | bytes 983048 | tf_op jit(solution)/shard_map/ppermute | solution.py:53
  135.5 8.2 %collective-permute-done.38 = bf16[80,2048]{1,0:T(8,128)(2,1)S(1)} collective-permute-done((bf16[80,2048]{1,0:T(8,128)(2,1)S(1)}, bf16[80,2048]{1,0:T(8,128)(2,1)S(1)}, u32[]{:S(2)}, u32[]{:S(2)}) %collective-permute-start.38) | collective-permute-done | bytes 327712 | tf_op jit(solution)/shard_map/ppermute | solution.py:53
  144.0 0.8 fusion.25
  144.8 0.7 collective-permute-done.40
  145.5 1.3 fusion.22
  (139 shorter events, 5.8 us)
Async XLA Ops:
  0.0 2.9 %collective-permute-start = (bf16[160,2048]{1,0:T(8,128)(2,1)}, bf16[160,2048]{1,0:T(8,128)(2,1)S(1)}, u32[]{:S(2)}, u32[]{:S(2)}) collective-permute-start(bf16[160,2048]{1,0:T(8,128)(2,1)} %param.5), channel_id=1, source_target_pairs={{0,1},{1,0},{2,3},{3,2},{4,5},{5,4},{6,7},{7,6},{8,9},{9,8},{10,11... | collective-permute-start | bytes 1966088 | tf_op jit(solution)/shard_map/ppermute | solution.py:53
  2.9 10.7 %copy-start.1 = (bf16[160,2048]{1,0:T(8,128)(2,1)S(1)}, bf16[160,2048]{1,0:T(8,128)(2,1)}, u32[]{:S(2)}) copy-start(bf16[160,2048]{1,0:T(8,128)(2,1)} %param.5) | copy-start | bytes 1966084
  3.2 7.4 %collective-permute-start.1 = (bf16[40,2048]{1,0:T(8,128)(2,1)S(1)}, bf16[40,2048]{1,0:T(8,128)(2,1)S(1)}, u32[]{:S(2)}, u32[]{:S(2)}) collective-permute-start(bf16[40,2048]{1,0:T(8,128)(2,1)S(1)} %slice.314), channel_id=1, source_target_pairs={{0,2},{1,3},{2,0},{3,1},{4,6},{5,7},{6,4},{7,5},{8,10},{9,11},{10,... | collective-permute-start | bytes 491528 | tf_op jit(solution)/shard_map/ppermute | solution.py:53
  10.7 10.5 %collective-permute-start.2 = (bf16[40,2048]{1,0:T(8,128)(2,1)S(1)}, bf16[40,2048]{1,0:T(8,128)(2,1)S(1)}, u32[]{:S(2)}, u32[]{:S(2)}) collective-permute-start(bf16[40,2048]{1,0:T(8,128)(2,1)S(1)} %slice_add_fusion.19), channel_id=1, source_target_pairs={{0,8},{4,12},{8,0},{12,4},{1,9},{5,13},{9,1},{13,5},{2,10},{6,14},... | collective-permute-start | bytes 491528 | tf_op jit(solution)/shard_map/ppermute | solution.py:53
  14.2 18.8 %copy-start = (s32[4]{0:T(128)S(1)}, s32[4]{0:T(128)}, u32[]{:S(2)}) copy-start(s32[4]{0:T(128)} %tick_ref) | copy-start | bytes 52
  14.2 8.6 %collective-permute-start.6 = (bf16[40,2048]{1,0:T(8,128)(2,1)S(1)}, bf16[40,2048]{1,0:T(8,128)(2,1)S(1)}, u32[]{:S(2)}, u32[]{:S(2)}) collective-permute-start(bf16[40,2048]{1,0:T(8,128)(2,1)S(1)} %slice.316), channel_id=1, source_target_pairs={{0,2},{1,3},{2,0},{3,1},{4,6},{5,7},{6,4},{7,5},{8,10},{9,11},{10,... | collective-permute-start | bytes 491528 | tf_op jit(solution)/shard_map/ppermute | solution.py:53
  21.2 5.4 %collective-permute-start.3 = (bf16[40,2048]{1,0:T(8,128)(2,1)S(1)}, bf16[40,2048]{1,0:T(8,128)(2,1)S(1)}, u32[]{:S(2)}, u32[]{:S(2)}) collective-permute-start(bf16[40,2048]{1,0:T(8,128)(2,1)S(1)} %get-tuple-element.104), channel_id=1, source_target_pairs={{0,2},{1,3},{2,0},{3,1},{4,6},{5,7},{6,4},{7,5},{8,10},{9,11},{10,... | collective-permute-start | bytes 491528 | tf_op jit(solution)/shard_map/ppermute | solution.py:53
  22.8 9.5 %collective-permute-start.7 = (bf16[40,2048]{1,0:T(8,128)(2,1)S(1)}, bf16[40,2048]{1,0:T(8,128)(2,1)S(1)}, u32[]{:S(2)}, u32[]{:S(2)}) collective-permute-start(bf16[40,2048]{1,0:T(8,128)(2,1)S(1)} %slice_add_fusion.18), channel_id=1, source_target_pairs={{0,8},{4,12},{8,0},{12,4},{1,9},{5,13},{9,1},{13,5},{2,10},{6,14},... | collective-permute-start | bytes 491528 | tf_op jit(solution)/shard_map/ppermute | solution.py:53
  26.6 12.2 %collective-permute-start.4 = (bf16[80,2048]{1,0:T(8,128)(2,1)S(1)}, bf16[80,2048]{1,0:T(8,128)(2,1)S(1)}, u32[]{:S(2)}, u32[]{:S(2)}) collective-permute-start(bf16[80,2048]{1,0:T(8,128)(2,1)S(1)} %pad_maximum_fusion.11), channel_id=1, source_target_pairs={{0,4},{1,0},{2,6},{3,2},{4,5},{5,1},{6,7},{7,3},{8,12},{9,8},{10,1... | collective-permute-start | bytes 983048 | tf_op jit(solution)/shard_map/ppermute | solution.py:130
  28.2 10.7 %collective-permute-start.5 = (bf16[80,2048]{1,0:T(8,128)(2,1)S(1)}, bf16[80,2048]{1,0:T(8,128)(2,1)S(1)}, u32[]{:S(2)}, u32[]{:S(2)}) collective-permute-start(bf16[80,2048]{1,0:T(8,128)(2,1)S(1)} %pad_maximum_fusion.11), channel_id=1, source_target_pairs={{1,4},{3,6},{4,1},{6,3},{9,12},{11,14},{12,9},{14,11},{17,20},{19,... | collective-permute-start | bytes 983048 | tf_op jit(solution)/shard_map/ppermute | solution.py:130
  32.4 6.6 %collective-permute-start.8 = (bf16[40,2048]{1,0:T(8,128)(2,1)S(1)}, bf16[40,2048]{1,0:T(8,128)(2,1)S(1)}, u32[]{:S(2)}, u32[]{:S(2)}) collective-permute-start(bf16[40,2048]{1,0:T(8,128)(2,1)S(1)} %get-tuple-element.100), channel_id=1, source_target_pairs={{0,2},{1,3},{2,0},{3,1},{4,6},{5,7},{6,4},{7,5},{8,10},{9,11},{10,... | collective-permute-start | bytes 491528 | tf_op jit(solution)/shard_map/ppermute | solution.py:53
  41.8 1.0 copy-start.2
  42.9 2.2 %collective-permute-start.9 = (bf16[2,80,1792]{2,1,0:T(8,128)(2,1)S(1)}, bf16[2,80,1792]{2,1,0:T(8,128)(2,1)}, u32[]{:S(2)}, u32[]{:S(2)}) collective-permute-start(bf16[2,80,1792]{2,1,0:T(8,128)(2,1)S(1)} %pad_maximum_fusion.3), channel_id=1, source_target_pairs={{0,1},{1,0},{2,3},{3,2},{4,5},{5,4},{6,7},{7,6},{8,9},{9,8},{10,11... | collective-permute-start | bytes 1720328 | tf_op jit(solution)/shard_map/ppermute | solution.py:53
  43.0 13.4 %collective-permute-start.11 = (bf16[80,2048]{1,0:T(8,128)(2,1)S(1)}, bf16[80,2048]{1,0:T(8,128)(2,1)S(1)}, u32[]{:S(2)}, u32[]{:S(2)}) collective-permute-start(bf16[80,2048]{1,0:T(8,128)(2,1)S(1)} %pad_maximum_fusion.12), channel_id=1, source_target_pairs={{0,4},{1,0},{2,6},{3,2},{4,5},{5,1},{6,7},{7,3},{8,12},{9,8},{10,1... | collective-permute-start | bytes 983048 | tf_op jit(solution)/shard_map/ppermute | solution.py:130
  43.1 13.3 %collective-permute-start.12 = (bf16[80,2048]{1,0:T(8,128)(2,1)S(1)}, bf16[80,2048]{1,0:T(8,128)(2,1)S(1)}, u32[]{:S(2)}, u32[]{:S(2)}) collective-permute-start(bf16[80,2048]{1,0:T(8,128)(2,1)S(1)} %pad_maximum_fusion.12), channel_id=1, source_target_pairs={{1,4},{3,6},{4,1},{6,3},{9,12},{11,14},{12,9},{14,11},{17,20},{19,... | collective-permute-start | bytes 983048 | tf_op jit(solution)/shard_map/ppermute | solution.py:130
  51.0 12.9 %slice-start = ((s8[14680064]{0:T(1024)(128)(4,1)}), s8[4194304]{0:T(1024)(128)(4,1)S(1)}, s32[]{:S(2)}) async-start(s8[14680064]{0:T(1024)(128)(4,1)} %bitcast.107), calls=%async_computation | async-start | bytes 8388608
  51.0 12.9 %slice-start.1 = ((s8[14680064]{0:T(1024)(128)(4,1)}), s8[4194304]{0:T(1024)(128)(4,1)S(1)}, s32[]{:S(2)}) async-start(s8[14680064]{0:T(1024)(128)(4,1)} %bitcast.107), calls=%async_computation.1 | async-start | bytes 8388608
  55.8 2.4 %collective-permute-start.13 = (bf16[2,80,1792]{2,1,0:T(8,128)(2,1)S(1)}, bf16[2,80,1792]{2,1,0:T(8,128)(2,1)S(1)}, u32[]{:S(2)}, u32[]{:S(2)}) collective-permute-start(bf16[2,80,1792]{2,1,0:T(8,128)(2,1)S(1)} %pad_maximum_fusion.4), channel_id=1, source_target_pairs={{0,1},{1,0},{2,3},{3,2},{4,5},{5,4},{6,7},{7,6},{8,9},{9,8},{10,11... | collective-permute-start | bytes 1720328 | tf_op jit(solution)/shard_map/ppermute | solution.py:53
  56.6 7.3 %slice-start.2 = ((s8[14680064]{0:T(1024)(128)(4,1)}), s8[4194304]{0:T(1024)(128)(4,1)S(1)}, s32[]{:S(2)}) async-start(s8[14680064]{0:T(1024)(128)(4,1)} %bitcast.107), calls=%async_computation.2 | async-start | bytes 8388608
  56.6 9.6 %collective-permute-start.10 = (bf16[2,40,1792]{2,1,0:T(8,128)(2,1)S(1)}, bf16[2,40,1792]{2,1,0:T(8,128)(2,1)S(1)}, u32[]{:S(2)}, u32[]{:S(2)}) collective-permute-start(bf16[2,40,1792]{2,1,0:T(8,128)(2,1)S(1)} %pad_maximum_fusion.13), channel_id=1, source_target_pairs={{0,2},{1,3},{2,0},{3,1},{4,6},{5,7},{6,4},{7,5},{8,10},{9,11},{10,... | collective-permute-start | bytes 860168 | tf_op jit(solution)/shard_map/ppermute | solution.py:53
  58.3 5.6 %slice-start.3 = ((s8[14680064]{0:T(1024)(128)(4,1)}), s8[2097152]{0:T(1024)(128)(4,1)S(1)}, s32[]{:S(2)}) async-start(s8[14680064]{0:T(1024)(128)(4,1)} %bitcast.107), calls=%async_computation.3 | async-start | bytes 4194304
  65.8 12.6 %collective-permute-start.17 = (bf16[2,80,2304]{2,1,0:T(8,128)(2,1)S(1)}, bf16[2,80,2304]{2,1,0:T(8,128)(2,1)S(1)}, u32[]{:S(2)}, u32[]{:S(2)}) collective-permute-start(bf16[2,80,2304]{2,1,0:T(8,128)(2,1)S(1)} %pad_maximum_fusion), channel_id=1, source_target_pairs={{0,1},{1,0},{2,3},{3,2},{4,5},{5,4},{6,7},{7,6},{8,9},{9,8},{10,11... | collective-permute-start | bytes 2211848 | tf_op jit(solution)/shard_map/ppermute | solution.py:53
  66.3 10.6 %collective-permute-start.14 = (bf16[40,1792]{1,0:T(8,128)(2,1)S(1)}, bf16[40,1792]{1,0:T(8,128)(2,1)S(1)}, u32[]{:S(2)}, u32[]{:S(2)}) collective-permute-start(bf16[40,1792]{1,0:T(8,128)(2,1)S(1)} %fusion.47), channel_id=1, source_target_pairs={{0,8},{4,12},{8,0},{12,4},{1,9},{5,13},{9,1},{13,5},{2,10},{6,14},... | collective-permute-start | bytes 430088 | tf_op jit(solution)/shard_map/ppermute | solution.py:53
  69.9 9.5 %collective-permute-start.16 = (bf16[2,40,1792]{2,1,0:T(8,128)(2,1)S(1)}, bf16[2,40,1792]{2,1,0:T(8,128)(2,1)S(1)}, u32[]{:S(2)}, u32[]{:S(2)}) collective-permute-start(bf16[2,40,1792]{2,1,0:T(8,128)(2,1)S(1)} %pad_maximum_fusion.14), channel_id=1, source_target_pairs={{0,2},{1,3},{2,0},{3,1},{4,6},{5,7},{6,4},{7,5},{8,10},{9,11},{10,... | collective-permute-start | bytes 860168 | tf_op jit(solution)/shard_map/ppermute | solution.py:53
  77.0 7.6 %collective-permute-start.15 = (bf16[40,1792]{1,0:T(8,128)(2,1)S(1)}, bf16[40,1792]{1,0:T(8,128)(2,1)S(1)}, u32[]{:S(2)}, u32[]{:S(2)}) collective-permute-start(bf16[40,1792]{1,0:T(8,128)(2,1)S(1)} %get-tuple-element.112), channel_id=1, source_target_pairs={{0,2},{1,3},{2,0},{3,1},{4,6},{5,7},{6,4},{7,5},{8,10},{9,11},{10,... | collective-permute-start | bytes 430088 | tf_op jit(solution)/shard_map/ppermute | solution.py:53
  78.6 24.2 %slice-start.4 = ((s8[14680064]{0:T(1024)(128)(4,1)}), s8[2097152]{0:T(1024)(128)(4,1)S(1)}, s32[]{:S(2)}) async-start(s8[14680064]{0:T(1024)(128)(4,1)} %bitcast.116), calls=%async_computation.4 | async-start | bytes 4194304
  78.7 11.6 %collective-permute-start.21 = (bf16[2,40,2304]{2,1,0:T(8,128)(2,1)S(1)}, bf16[2,40,2304]{2,1,0:T(8,128)(2,1)S(1)}, u32[]{:S(2)}, u32[]{:S(2)}) collective-permute-start(bf16[2,40,2304]{2,1,0:T(8,128)(2,1)S(1)} %pad_maximum_fusion.9), channel_id=1, source_target_pairs={{0,2},{1,3},{2,0},{3,1},{4,6},{5,7},{6,4},{7,5},{8,10},{9,11},{10,... | collective-permute-start | bytes 1105928 | tf_op jit(solution)/shard_map/ppermute | solution.py:53
  79.5 23.3 %slice-start.5 = ((s8[14680064]{0:T(1024)(128)(4,1)}), s8[4194304]{0:T(1024)(128)(4,1)S(1)}, s32[]{:S(2)}) async-start(s8[14680064]{0:T(1024)(128)(4,1)} %bitcast.116), calls=%async_computation.5 | async-start | bytes 8388608
  79.6 8.9 %collective-permute-start.18 = (bf16[40,1792]{1,0:T(8,128)(2,1)S(1)}, bf16[40,1792]{1,0:T(8,128)(2,1)S(1)}, u32[]{:S(2)}, u32[]{:S(2)}) collective-permute-start(bf16[40,1792]{1,0:T(8,128)(2,1)S(1)} %fusion.45), channel_id=1, source_target_pairs={{0,8},{4,12},{8,0},{12,4},{1,9},{5,13},{9,1},{13,5},{2,10},{6,14},... | collective-permute-start | bytes 430088 | tf_op jit(solution)/shard_map/ppermute | solution.py:53
  80.7 22.2 %slice-start.6 = ((s8[14680064]{0:T(1024)(128)(4,1)}), s8[4194304]{0:T(1024)(128)(4,1)S(1)}, s32[]{:S(2)}) async-start(s8[14680064]{0:T(1024)(128)(4,1)} %bitcast.116), calls=%async_computation.6 | async-start | bytes 8388608
  84.5 6.1 %collective-permute-start.20 = (bf16[2,80,1280]{2,1,0:T(8,128)(2,1)S(1)}, bf16[2,80,1280]{2,1,0:T(8,128)(2,1)S(1)}, u32[]{:S(2)}, u32[]{:S(2)}) collective-permute-start(bf16[2,80,1280]{2,1,0:T(8,128)(2,1)S(1)} %pad_maximum_fusion.7), channel_id=1, source_target_pairs={{0,1},{1,0},{2,3},{3,2},{4,5},{5,4},{6,7},{7,6},{8,9},{9,8},{10,11... | collective-permute-start | bytes 1228808 | tf_op jit(solution)/shard_map/ppermute | solution.py:53
  84.6 11.6 %collective-permute-start.22 = (bf16[80,1792]{1,0:T(8,128)(2,1)S(1)}, bf16[80,1792]{1,0:T(8,128)(2,1)S(1)}, u32[]{:S(2)}, u32[]{:S(2)}) collective-permute-start(bf16[80,1792]{1,0:T(8,128)(2,1)S(1)} %pad_maximum_fusion.15), channel_id=1, source_target_pairs={{0,4},{1,0},{2,6},{3,2},{4,5},{5,1},{6,7},{7,3},{8,12},{9,8},{10,1... | collective-permute-start | bytes 860168 | tf_op jit(solution)/shard_map/ppermute | solution.py:130
  87.8 9.2 %collective-permute-start.23 = (bf16[80,1792]{1,0:T(8,128)(2,1)S(1)}, bf16[80,1792]{1,0:T(8,128)(2,1)S(1)}, u32[]{:S(2)}, u32[]{:S(2)}) collective-permute-start(bf16[80,1792]{1,0:T(8,128)(2,1)S(1)} %pad_maximum_fusion.15), channel_id=1, source_target_pairs={{1,4},{3,6},{4,1},{6,3},{9,12},{11,14},{12,9},{14,11},{17,20},{19,... | collective-permute-start | bytes 860168 | tf_op jit(solution)/shard_map/ppermute | solution.py:130
  88.5 14.4 %slice-start.7 = ((s8[14680064]{0:T(1024)(128)(4,1)}), s8[4194304]{0:T(1024)(128)(4,1)S(1)}, s32[]{:S(2)}) async-start(s8[14680064]{0:T(1024)(128)(4,1)} %bitcast.116), calls=%async_computation.7 | async-start | bytes 8388608
  88.5 5.9 %collective-permute-start.19 = (bf16[40,1792]{1,0:T(8,128)(2,1)S(1)}, bf16[40,1792]{1,0:T(8,128)(2,1)S(1)}, u32[]{:S(2)}, u32[]{:S(2)}) collective-permute-start(bf16[40,1792]{1,0:T(8,128)(2,1)S(1)} %get-tuple-element.110), channel_id=1, source_target_pairs={{0,2},{1,3},{2,0},{3,1},{4,6},{5,7},{6,4},{7,5},{8,10},{9,11},{10,... | collective-permute-start | bytes 430088 | tf_op jit(solution)/shard_map/ppermute | solution.py:53
  90.5 11.3 %collective-permute-start.25 = (bf16[40,2304]{1,0:T(8,128)(2,1)S(1)}, bf16[40,2304]{1,0:T(8,128)(2,1)S(1)}, u32[]{:S(2)}, u32[]{:S(2)}) collective-permute-start(bf16[40,2304]{1,0:T(8,128)(2,1)S(1)} %fusion.39), channel_id=1, source_target_pairs={{0,8},{4,12},{8,0},{12,4},{1,9},{5,13},{9,1},{13,5},{2,10},{6,14},... | collective-permute-start | bytes 552968 | tf_op jit(solution)/shard_map/ppermute | solution.py:53
  90.7 12.0 %collective-permute-start.24 = (bf16[2,40,1280]{2,1,0:T(8,128)(2,1)S(1)}, bf16[2,40,1280]{2,1,0:T(8,128)(2,1)S(1)}, u32[]{:S(2)}, u32[]{:S(2)}) collective-permute-start(bf16[2,40,1280]{2,1,0:T(8,128)(2,1)S(1)} %pad_maximum_fusion.17), channel_id=1, source_target_pairs={{0,2},{1,3},{2,0},{3,1},{4,6},{5,7},{6,4},{7,5},{8,10},{9,11},{10,... | collective-permute-start | bytes 614408 | tf_op jit(solution)/shard_map/ppermute | solution.py:53
  94.4 9.9 %collective-permute-start.26 = (bf16[80,1792]{1,0:T(8,128)(2,1)S(1)}, bf16[80,1792]{1,0:T(8,128)(2,1)S(1)}, u32[]{:S(2)}, u32[]{:S(2)}) collective-permute-start(bf16[80,1792]{1,0:T(8,128)(2,1)S(1)} %pad_maximum_fusion.16), channel_id=1, source_target_pairs={{0,4},{1,0},{2,6},{3,2},{4,5},{5,1},{6,7},{7,3},{8,12},{9,8},{10,1... | collective-permute-start | bytes 860168 | tf_op jit(solution)/shard_map/ppermute | solution.py:130
  96.2 8.1 %collective-permute-start.27 = (bf16[80,1792]{1,0:T(8,128)(2,1)S(1)}, bf16[80,1792]{1,0:T(8,128)(2,1)S(1)}, u32[]{:S(2)}, u32[]{:S(2)}) collective-permute-start(bf16[80,1792]{1,0:T(8,128)(2,1)S(1)} %pad_maximum_fusion.16), channel_id=1, source_target_pairs={{1,4},{3,6},{4,1},{6,3},{9,12},{11,14},{12,9},{14,11},{17,20},{19,... | collective-permute-start | bytes 860168 | tf_op jit(solution)/shard_map/ppermute | solution.py:130
  101.8 6.7 %collective-permute-start.28 = (bf16[40,2304]{1,0:T(8,128)(2,1)S(1)}, bf16[40,2304]{1,0:T(8,128)(2,1)S(1)}, u32[]{:S(2)}, u32[]{:S(2)}) collective-permute-start(bf16[40,2304]{1,0:T(8,128)(2,1)S(1)} %get-tuple-element.92), channel_id=1, source_target_pairs={{0,2},{1,3},{2,0},{3,1},{4,6},{5,7},{6,4},{7,5},{8,10},{9,11},{10,... | collective-permute-start | bytes 552968 | tf_op jit(solution)/shard_map/ppermute | solution.py:53
  102.8 8.6 %collective-permute-start.30 = (bf16[40,1280]{1,0:T(8,128)(2,1)S(1)}, bf16[40,1280]{1,0:T(8,128)(2,1)S(1)}, u32[]{:S(2)}, u32[]{:S(2)}) collective-permute-start(bf16[40,1280]{1,0:T(8,128)(2,1)S(1)} %fusion.51), channel_id=1, source_target_pairs={{0,8},{4,12},{8,0},{12,4},{1,9},{5,13},{9,1},{13,5},{2,10},{6,14},... | collective-permute-start | bytes 307208 | tf_op jit(solution)/shard_map/ppermute | solution.py:53
  108.5 8.3 %collective-permute-start.32 = (bf16[80,2304]{1,0:T(8,128)(2,1)S(1)}, bf16[80,2304]{1,0:T(8,128)(2,1)S(1)}, u32[]{:S(2)}, u32[]{:S(2)}) collective-permute-start(bf16[80,2304]{1,0:T(8,128)(2,1)S(1)} %pad_maximum_fusion.10), channel_id=1, source_target_pairs={{0,4},{1,0},{2,6},{3,2},{4,5},{5,1},{6,7},{7,3},{8,12},{9,8},{10,1... | collective-permute-start | bytes 1105928 | tf_op jit(solution)/shard_map/ppermute | solution.py:130
  109.3 7.6 %collective-permute-start.33 = (bf16[80,2304]{1,0:T(8,128)(2,1)S(1)}, bf16[80,2304]{1,0:T(8,128)(2,1)S(1)}, u32[]{:S(2)}, u32[]{:S(2)}) collective-permute-start(bf16[80,2304]{1,0:T(8,128)(2,1)S(1)} %pad_maximum_fusion.10), channel_id=1, source_target_pairs={{1,4},{3,6},{4,1},{6,3},{9,12},{11,14},{12,9},{14,11},{17,20},{19,... | collective-permute-start | bytes 1105928 | tf_op jit(solution)/shard_map/ppermute | solution.py:130
  111.4 7.3 %collective-permute-start.31 = (bf16[40,1280]{1,0:T(8,128)(2,1)S(1)}, bf16[40,1280]{1,0:T(8,128)(2,1)S(1)}, u32[]{:S(2)}, u32[]{:S(2)}) collective-permute-start(bf16[40,1280]{1,0:T(8,128)(2,1)S(1)} %get-tuple-element.116), channel_id=1, source_target_pairs={{0,2},{1,3},{2,0},{3,1},{4,6},{5,7},{6,4},{7,5},{8,10},{9,11},{10,... | collective-permute-start | bytes 307208 | tf_op jit(solution)/shard_map/ppermute | solution.py:53
  112.9 10.4 %collective-permute-start.29 = (bf16[80,2048]{1,0:T(8,128)(2,1)S(1)}, bf16[80,2048]{1,0:T(8,128)(2,1)S(1)}, u32[]{:S(2)}, u32[]{:S(2)}) collective-permute-start(bf16[80,2048]{1,0:T(8,128)(2,1)S(1)} %slice.504), channel_id=1, source_target_pairs={{0,1},{1,0},{2,3},{3,2},{4,5},{5,4},{6,7},{7,6},{8,9},{9,8},{10,11... | collective-permute-start | bytes 983048 | tf_op jit(solution)/shard_map/ppermute | solution.py:53
  118.7 8.0 %collective-permute-start.35 = (bf16[80,1280]{1,0:T(8,128)(2,1)S(1)}, bf16[80,1280]{1,0:T(8,128)(2,1)S(1)}, u32[]{:S(2)}, u32[]{:S(2)}) collective-permute-start(bf16[80,1280]{1,0:T(8,128)(2,1)S(1)} %pad_maximum_fusion.18), channel_id=1, source_target_pairs={{0,4},{1,0},{2,6},{3,2},{4,5},{5,1},{6,7},{7,3},{8,12},{9,8},{10,1... | collective-permute-start | bytes 614408 | tf_op jit(solution)/shard_map/ppermute | solution.py:130
  122.7 4.1 %collective-permute-start.36 = (bf16[80,1280]{1,0:T(8,128)(2,1)S(1)}, bf16[80,1280]{1,0:T(8,128)(2,1)S(1)}, u32[]{:S(2)}, u32[]{:S(2)}) collective-permute-start(bf16[80,1280]{1,0:T(8,128)(2,1)S(1)} %pad_maximum_fusion.18), channel_id=1, source_target_pairs={{1,4},{3,6},{4,1},{6,3},{9,12},{11,14},{12,9},{14,11},{17,20},{19,... | collective-permute-start | bytes 614408 | tf_op jit(solution)/shard_map/ppermute | solution.py:130
  123.4 10.3 %collective-permute-start.34 = (bf16[80,2048]{1,0:T(8,128)(2,1)S(1)}, bf16[80,2048]{1,0:T(8,128)(2,1)S(1)}, u32[]{:S(2)}, u32[]{:S(2)}) collective-permute-start(bf16[80,2048]{1,0:T(8,128)(2,1)S(1)} %get-tuple-element.77), channel_id=1, source_target_pairs={{0,2},{1,3},{2,0},{3,1},{4,6},{5,7},{6,4},{7,5},{8,10},{9,11},{10,... | collective-permute-start | bytes 983048 | tf_op jit(solution)/shard_map/ppermute | solution.py:53
  127.9 5.8 %collective-permute-start.37 = (bf16[80,2048]{1,0:T(8,128)(2,1)S(1)}, bf16[80,2048]{1,0:T(8,128)(2,1)S(1)}, u32[]{:S(2)}, u32[]{:S(2)}) collective-permute-start(bf16[80,2048]{1,0:T(8,128)(2,1)S(1)} %slice.503), channel_id=1, source_target_pairs={{0,1},{1,0},{2,3},{3,2},{4,5},{5,4},{6,7},{7,6},{8,9},{9,8},{10,11... | collective-permute-start | bytes 983048 | tf_op jit(solution)/shard_map/ppermute | solution.py:53
  133.9 9.8 %collective-permute-start.38 = (bf16[80,2048]{1,0:T(8,128)(2,1)S(1)}, bf16[80,2048]{1,0:T(8,128)(2,1)S(1)}, u32[]{:S(2)}, u32[]{:S(2)}) collective-permute-start(bf16[80,2048]{1,0:T(8,128)(2,1)S(1)} %fusion.35), channel_id=1, source_target_pairs={{0,2},{1,3},{2,0},{3,1},{4,6},{5,7},{6,4},{7,5},{8,10},{9,11},{10,... | collective-permute-start | bytes 983048 | tf_op jit(solution)/shard_map/ppermute | solution.py:53
  135.4 9.4 %collective-permute-start.39 = (bf16[80,2048]{1,0:T(8,128)(2,1)S(1)}, bf16[80,2048]{1,0:T(8,128)(2,1)S(1)}, u32[]{:S(2)}, u32[]{:S(2)}) collective-permute-start(bf16[80,2048]{1,0:T(8,128)(2,1)S(1)} %get-tuple-element.73), channel_id=1, source_target_pairs={{0,1},{1,0},{2,3},{3,2},{4,5},{5,4},{6,7},{7,6},{8,9},{9,8},{10,11... | collective-permute-start | bytes 983048 | tf_op jit(solution)/shard_map/ppermute | solution.py:53
  143.8 1.7 %collective-permute-start.40 = (bf16[80,2048]{1,0:T(8,128)(2,1)S(1)}, bf16[80,2048]{1,0:T(8,128)(2,1)S(1)}, u32[]{:S(2)}, u32[]{:S(2)}) collective-permute-start(bf16[80,2048]{1,0:T(8,128)(2,1)S(1)} %get-tuple-element.75), channel_id=1, source_target_pairs={{0,1},{1,0},{2,3},{3,2},{4,5},{5,4},{6,7},{7,6},{8,9},{9,8},{10,11... | collective-permute-start | bytes 983048 | tf_op jit(solution)/shard_map/ppermute | solution.py:53

commit v17 on v16

--- a/solution.py
+++ b/solution.py
@@ -8,7 +8,7 @@
 from jax.sharding import PartitionSpec as P
 
 HALVES = 2
-PARTS = ((14, 14), (18, 10))
+PARTS = ((12, 16), (18, 10))
 EDGES = {
     "t1.pick": ["t0.add"],
     "w.pull": ["t0.columns"],

time: 147 us -> 152 us (1.034)
  other arithmetic: 4.98 us -> 9.1 us
  starting transfers between devices: 46.5 us -> 43.7 us
  waiting for transfers between devices: 53.2 us -> 55.9 us
  local copies, waits for them, and re-layouts: 1.63 us -> 4.3 us
    ppermute x29, waiting for transfers between devices: 48.5 us -> 50.9 us  [flip(): return lax.ppermute(value, axis, [(i, i ^ bit) for i in range(count)])]
    ppermute x12, starting transfers between devices: 15.5 us -> 14 us  [move(): return lax.ppermute(value, ('row', 'col'), pairs)]
  transfers between devices with their start and end apart: 41 -> 41, of which waited for: 15 -> 16; matrix products, arithmetic and copies ran while one was open for 24% -> 25% of each run, Pallas kernels for 4% -> 3%
where the time goes in v17:
time: 152 us
  waiting for transfers between devices  55.9 us (37%)
  starting transfers between devices  43.7 us (29%)
  matrix products  32.3 us (21%)
  other arithmetic  9.1 us (6%)
  Pallas kernels  5.26 us (3%)
  local copies, waits for them, and re-layouts  4.3 us (3%)
    ppermute x29, waiting for transfers between devices, flip(): return lax.ppermute(value, axis, [(i, i ^ bit) for i in range(count)])  50.9 us
    dot_general x17, matrix products, dot(): return jnp.dot(a, b, preferred_element_type=jnp.float32)  31.5 us
    ppermute x29, starting transfers between devices, flip(): return lax.ppermute(value, axis, [(i, i ^ bit) for i in range(count)])  29.8 us
    ppermute x12, starting transfers between devices, move(): return lax.ppermute(value, ('row', 'col'), pairs)  14 us
    pallas_call x1, Pallas kernels, pull(): pl.pallas_call(functools.partial(pull_kernel, first, end), in_specs=[pl.B...  5.26 us
    ppermute x12, waiting for transfers between devices, move(): return lax.ppermute(value, ('row', 'col'), pairs)  5.04 us
  transfers between devices with their start and end apart: 41, of which 16 were waited for; matrix products, arithmetic and copies ran while one was open for 25% of the time, Pallas kernels for 3%

profile of v17, /device:TPU:0, one launch (start us, length us, event | category | flops | bytes accessed | tf_op | source)
XLA Modules:
  0.0 151.7 jit_solution(11170095124878039341)
XLA Ops:
  0.5 0.9 fusion.80
  1.5 1.4 fusion.70
  3.2 2.6 %collective-permute-start.1 = (bf16[40,2048]{1,0:T(8,128)(2,1)S(1)}, bf16[40,2048]{1,0:T(8,128)(2,1)S(1)}, u32[]{:S(2)}, u32[]{:S(2)}) collective-permute-start(bf16[40,2048]{1,0:T(8,128)(2,1)S(1)} %slice.314), channel_id=1, source_target_pairs={{0,2},{1,3},{2,0},{3,1},{4,6},{5,7},{6,4},{7,5},{8,10},{9,11},{10,... | collective-permute-start | bytes 491528 | tf_op jit(solution)/shard_map/ppermute | solution.py:53
  5.8 4.9 %collective-permute-done.1 = bf16[40,2048]{1,0:T(8,128)(2,1)S(1)} collective-permute-done((bf16[40,2048]{1,0:T(8,128)(2,1)S(1)}, bf16[40,2048]{1,0:T(8,128)(2,1)S(1)}, u32[]{:S(2)}, u32[]{:S(2)}) %collective-permute-start.1) | collective-permute-done | bytes 163872 | tf_op jit(solution)/shard_map/ppermute | solution.py:53
  10.7 2.9 %collective-permute-start.2 = (bf16[40,2048]{1,0:T(8,128)(2,1)S(1)}, bf16[40,2048]{1,0:T(8,128)(2,1)S(1)}, u32[]{:S(2)}, u32[]{:S(2)}) collective-permute-start(bf16[40,2048]{1,0:T(8,128)(2,1)S(1)} %slice_add_fusion.19), channel_id=1, source_target_pairs={{0,8},{4,12},{8,0},{12,4},{1,9},{5,13},{9,1},{13,5},{2,10},{6,14},... | collective-permute-start | bytes 491528 | tf_op jit(solution)/shard_map/ppermute | solution.py:53
  14.2 1.6 %collective-permute-start.6 = (bf16[40,2048]{1,0:T(8,128)(2,1)S(1)}, bf16[40,2048]{1,0:T(8,128)(2,1)S(1)}, u32[]{:S(2)}, u32[]{:S(2)}) collective-permute-start(bf16[40,2048]{1,0:T(8,128)(2,1)S(1)} %slice.316), channel_id=1, source_target_pairs={{0,2},{1,3},{2,0},{3,1},{4,6},{5,7},{6,4},{7,5},{8,10},{9,11},{10,... | collective-permute-start | bytes 491528 | tf_op jit(solution)/shard_map/ppermute | solution.py:53
  15.8 5.4 %collective-permute-done.2 = bf16[40,2048]{1,0:T(8,128)(2,1)S(1)} collective-permute-done((bf16[40,2048]{1,0:T(8,128)(2,1)S(1)}, bf16[40,2048]{1,0:T(8,128)(2,1)S(1)}, u32[]{:S(2)}, u32[]{:S(2)}) %collective-permute-start.2) | collective-permute-done | bytes 163872 | tf_op jit(solution)/shard_map/ppermute | solution.py:53
  21.2 1.6 %collective-permute-start.3 = (bf16[40,2048]{1,0:T(8,128)(2,1)S(1)}, bf16[40,2048]{1,0:T(8,128)(2,1)S(1)}, u32[]{:S(2)}, u32[]{:S(2)}) collective-permute-start(bf16[40,2048]{1,0:T(8,128)(2,1)S(1)} %get-tuple-element.108), channel_id=1, source_target_pairs={{0,2},{1,3},{2,0},{3,1},{4,6},{5,7},{6,4},{7,5},{8,10},{9,11},{10,... | collective-permute-start | bytes 491528 | tf_op jit(solution)/shard_map/ppermute | solution.py:53
  22.9 3.7 %collective-permute-done.3 = bf16[40,2048]{1,0:T(8,128)(2,1)S(1)} collective-permute-done((bf16[40,2048]{1,0:T(8,128)(2,1)S(1)}, bf16[40,2048]{1,0:T(8,128)(2,1)S(1)}, u32[]{:S(2)}, u32[]{:S(2)}) %collective-permute-start.3) | collective-permute-done | bytes 163872 | tf_op jit(solution)/shard_map/ppermute | solution.py:53
  26.6 1.6 %collective-permute-start.4 = (bf16[80,2048]{1,0:T(8,128)(2,1)S(1)}, bf16[80,2048]{1,0:T(8,128)(2,1)S(1)}, u32[]{:S(2)}, u32[]{:S(2)}) collective-permute-start(bf16[80,2048]{1,0:T(8,128)(2,1)S(1)} %pad_maximum_fusion.11), channel_id=1, source_target_pairs={{0,4},{1,0},{2,6},{3,2},{4,5},{5,1},{6,7},{7,3},{8,12},{9,8},{10,1... | collective-permute-start | bytes 983048 | tf_op jit(solution)/shard_map/ppermute | solution.py:130
  28.9 3.5 %collective-permute-done.7 = bf16[40,2048]{1,0:T(8,128)(2,1)S(1)} collective-permute-done((bf16[40,2048]{1,0:T(8,128)(2,1)S(1)}, bf16[40,2048]{1,0:T(8,128)(2,1)S(1)}, u32[]{:S(2)}, u32[]{:S(2)}) %collective-permute-start.7) | collective-permute-done | bytes 163872 | tf_op jit(solution)/shard_map/ppermute | solution.py:53
  33.0 5.3 %shard_map.55 = (bf16[2048,1536]{1,0:T(8,128)(2,1)S(1)}, bf16[2048,1536]{1,0:T(8,128)(2,1)S(1)}) custom-call(s32[4]{0:T(128)S(1)} %copy-done, bf16[2048,3584]{1,0:T(8,128)(2,1)} %gate_ref.1, bf16[2048,3584]{1,0:T(8,128)(2,1)} %up_ref.1), custom_call_target="tpu_custom_call" | custom-call | tf_op jit(solution)/shard_map/pallas_call | solution.py:73
  38.4 0.7 pad_maximum_fusion.12
  39.1 1.2 fusion.93
  40.4 1.2 fusion.94
  41.6 0.9 copy-done.3
  42.5 0.8 pad_maximum_fusion.5
  43.9 0.8 collective-permute-start.12
  44.8 0.8 collective-permute-done.9
  45.5 1.5 slice_add_fusion.7
  47.1 0.7 pad_maximum_fusion.15
  47.8 5.4 %fusion.10 = f32[160,2048]{1,0:T(8,128)S(1)} fusion(bf16[160,2048]{1,0:T(8,128)(2,1)S(1)} %pad_maximum_fusion.1, bf16[2048,3584]{1,0:T(8,128)(2,1)} %gate_ref.1), kind=kOutput, calls=%fused_computation.10 | convolution fusion | flops 1342177280 | bytes 10354688 | tf_op jit(solution)/shard_map/dot_general | solution.py:48
  53.2 5.1 %fusion.8 = f32[160,2048]{1,0:T(8,128)S(1)} fusion(bf16[160,2048]{1,0:T(8,128)(2,1)S(1)} %pad_maximum_fusion.1, bf16[2048,3584]{1,0:T(8,128)(2,1)} %up_ref.1), kind=kOutput, calls=%fused_computation.8 | convolution fusion | flops 1342177280 | bytes 10354688 | tf_op jit(solution)/shard_map/dot_general | solution.py:48
  58.5 1.1 collective-permute-start.13
  60.1 1.6 %collective-permute-start.10 = (bf16[2,40,1536]{2,1,0:T(8,128)(2,1)}, bf16[2,40,1536]{2,1,0:T(8,128)(2,1)}, u32[]{:S(2)}, u32[]{:S(2)}) collective-permute-start(bf16[2,40,1536]{2,1,0:T(8,128)(2,1)} %pad_maximum_fusion.15), channel_id=1, source_target_pairs={{0,2},{1,3},{2,0},{3,1},{4,6},{5,7},{6,4},{7,5},{8,10},{9,11},{10,... | collective-permute-start | bytes 737288 | tf_op jit(solution)/shard_map/ppermute | solution.py:53
  61.9 0.8 pad_maximum_fusion.13
  62.7 2.8 %fusion.4 = f32[160,2304]{1,0:T(8,128)} fusion(bf16[160,2048]{1,0:T(8,128)(2,1)S(1)} %pad_maximum_fusion.2, bf16[2048,3584]{1,0:T(8,128)(2,1)S(1)} %bitcast.110), kind=kOutput, calls=%fused_computation.4 | convolution fusion | flops 1509949440 | bytes 11567104 | tf_op jit(solution)/shard_map/dot_general | solution.py:48
  65.5 1.7 %fusion.2 = f32[160,2304]{1,0:T(8,128)S(1)} fusion(bf16[160,2048]{1,0:T(8,128)(2,1)S(1)} %pad_maximum_fusion.2, bf16[2048,3584]{1,0:T(8,128)(2,1)S(1)} %bitcast.108), kind=kOutput, calls=%fused_computation.2 | convolution fusion | flops 1509949440 | bytes 11567104 | tf_op jit(solution)/shard_map/dot_general | solution.py:48
  67.3 1.1 copy-done.6
  68.5 1.3 fusion.36
  69.9 0.9 collective-permute-start.17
  70.7 1.1 fusion.47
  71.8 3.4 %collective-permute-start.14 = (bf16[40,1536]{1,0:T(8,128)(2,1)S(1)}, bf16[40,1536]{1,0:T(8,128)(2,1)S(1)}, u32[]{:S(2)}, u32[]{:S(2)}) collective-permute-start(bf16[40,1536]{1,0:T(8,128)(2,1)S(1)} %fusion.47), channel_id=1, source_target_pairs={{0,8},{4,12},{8,0},{12,4},{1,9},{5,13},{9,1},{13,5},{2,10},{6,14},... | collective-permute-start | bytes 368648 | tf_op jit(solution)/shard_map/ppermute | solution.py:53
  76.1 5.4 %collective-permute-done.14 = bf16[40,1536]{1,0:T(8,128)(2,1)S(1)} collective-permute-done((bf16[40,1536]{1,0:T(8,128)(2,1)S(1)}, bf16[40,1536]{1,0:T(8,128)(2,1)S(1)}, u32[]{:S(2)}, u32[]{:S(2)}) %collective-permute-start.14) | collective-permute-done | bytes 122912 | tf_op jit(solution)/shard_map/ppermute | solution.py:53
  81.5 0.9 collective-permute-start.15
  82.7 1.2 collective-permute-start.21
  83.9 1.9 %collective-permute-done.16 = bf16[2,40,2048]{2,1,0:T(8,128)(2,1)S(1)} collective-permute-done((bf16[2,40,2048]{2,1,0:T(8,128)(2,1)S(1)}, bf16[2,40,2048]{2,1,0:T(8,128)(2,1)S(1)}, u32[]{:S(2)}, u32[]{:S(2)}) %collective-permute-start.16) | collective-permute-done | bytes 327712 | tf_op jit(solution)/shard_map/ppermute | solution.py:53
  86.2 1.1 fusion.16
  87.3 1.0 fusion.18
  88.5 1.2 collective-permute-start.22
  90.4 4.2 %collective-permute-done.18 = bf16[40,2048]{1,0:T(8,128)(2,1)S(1)} collective-permute-done((bf16[40,2048]{1,0:T(8,128)(2,1)S(1)}, bf16[40,2048]{1,0:T(8,128)(2,1)S(1)}, u32[]{:S(2)}, u32[]{:S(2)}) %collective-permute-start.18) | collective-permute-done | bytes 163872 | tf_op jit(solution)/shard_map/ppermute | solution.py:53
  94.7 0.9 collective-permute-start.19
  96.1 1.2 collective-permute-start.24
  97.3 4.6 %collective-permute-done.19 = bf16[40,2048]{1,0:T(8,128)(2,1)S(1)} collective-permute-done((bf16[40,2048]{1,0:T(8,128)(2,1)S(1)}, bf16[40,2048]{1,0:T(8,128)(2,1)S(1)}, u32[]{:S(2)}, u32[]{:S(2)}) %collective-permute-start.19) | collective-permute-done | bytes 163872 | tf_op jit(solution)/shard_map/ppermute | solution.py:53
  102.0 1.0 collective-permute-start.27
  103.1 3.1 %collective-permute-done.25 = bf16[40,2304]{1,0:T(8,128)(2,1)S(1)} collective-permute-done((bf16[40,2304]{1,0:T(8,128)(2,1)S(1)}, bf16[40,2304]{1,0:T(8,128)(2,1)S(1)}, u32[]{:S(2)}, u32[]{:S(2)}) %collective-permute-start.25) | collective-permute-done | bytes 184352 | tf_op jit(solution)/shard_map/ppermute | solution.py:53
  106.3 1.0 collective-permute-start.28
  107.5 4.1 %fusion.12 = f32[160,2048]{1,0:T(8,128)S(1)} fusion(bf16[160,1536]{1,0:T(8,128)(2,1)S(1)} %pad_maximum_fusion.6, bf16[3584,2048]{1,0:T(8,128)(2,1)} %param.9), kind=kOutput, calls=%fused_computation.12 | convolution fusion | flops 1006632960 | bytes 8093696 | tf_op jit(solution)/shard_map/dot_general | solution.py:48
  111.9 2.1 %collective-permute-start.32 = (bf16[80,2304]{1,0:T(8,128)(2,1)S(1)}, bf16[80,2304]{1,0:T(8,128)(2,1)S(1)}, u32[]{:S(2)}, u32[]{:S(2)}) collective-permute-start(bf16[80,2304]{1,0:T(8,128)(2,1)S(1)} %pad_maximum_fusion.10), channel_id=1, source_target_pairs={{0,4},{1,0},{2,6},{3,2},{4,5},{5,1},{6,7},{7,3},{8,12},{9,8},{10,1... | collective-permute-start | bytes 1105928 | tf_op jit(solution)/shard_map/ppermute | solution.py:130
  114.8 1.6 %fusion.91 = f32[160,2048]{1,0:T(8,128)S(1)} fusion(f32[160,2048]{1,0:T(8,128)S(1)} %fusion.12, bf16[160,2048]{1,0:T(8,128)(2,1)S(1)} %pad_maximum_fusion.4, bf16[3584,2048]{1,0:T(8,128)(2,1)S(1)} %bitcast.119), kind=kOutput, calls=%fused_computation.195 | convolution fusion | flops 1342504960 | bytes 11665408 | tf_op jit(solution)/shard_map/dot_general | solution.py:48
  116.4 1.2 collective-permute-start.31
  117.6 1.2 collective-permute-start.29
  118.8 2.9 %collective-permute-done.32 = bf16[80,2304]{1,0:T(8,128)(2,1)S(1)} collective-permute-done((bf16[80,2304]{1,0:T(8,128)(2,1)S(1)}, bf16[80,2304]{1,0:T(8,128)(2,1)S(1)}, u32[]{:S(2)}, u32[]{:S(2)}) %collective-permute-start.32) | collective-permute-done | bytes 368672 | tf_op jit(solution)/shard_map/ppermute | solution.py:130
  121.7 1.8 %fusion = f32[160,2048]{1,0:T(8,128)S(1)} fusion(bf16[3584,2048]{1,0:T(8,128)(2,1)S(1)} %bitcast.119, bf16[80,2304]{1,0:T(8,128)(2,1)S(1)} %get-tuple-element.90, bf16[80,2304]{1,0:T(8,128)(2,1)S(1)} %get-tuple-element.89), kind=kOutput, calls=%fused_computation | convolution fusion | flops 1511424000 | bytes 11485184 | tf_op jit(solution)/shard_map/dot_general | solution.py:48
  123.6 3.9 %collective-permute-start.35 = (bf16[80,1280]{1,0:T(8,128)(2,1)S(1)}, bf16[80,1280]{1,0:T(8,128)(2,1)S(1)}, u32[]{:S(2)}, u32[]{:S(2)}) collective-permute-start(bf16[80,1280]{1,0:T(8,128)(2,1)S(1)} %pad_maximum_fusion.18), channel_id=1, source_target_pairs={{0,4},{1,0},{2,6},{3,2},{4,5},{5,1},{6,7},{7,3},{8,12},{9,8},{10,1... | collective-permute-start | bytes 614408 | tf_op jit(solution)/shard_map/ppermute | solution.py:130
  128.3 1.2 collective-permute-start.34
  129.4 2.2 %collective-permute-done.35 = bf16[80,1280]{1,0:T(8,128)(2,1)S(1)} collective-permute-done((bf16[80,1280]{1,0:T(8,128)(2,1)S(1)}, bf16[80,1280]{1,0:T(8,128)(2,1)S(1)}, u32[]{:S(2)}, u32[]{:S(2)}) %collective-permute-start.35) | collective-permute-done | bytes 204832 | tf_op jit(solution)/shard_map/ppermute | solution.py:130
  131.7 1.1 fusion.92
  132.8 1.7 %collective-permute-start.37 = (bf16[80,2048]{1,0:T(8,128)(2,1)S(1)}, bf16[80,2048]{1,0:T(8,128)(2,1)S(1)}, u32[]{:S(2)}, u32[]{:S(2)}) collective-permute-start(bf16[80,2048]{1,0:T(8,128)(2,1)S(1)} %slice.503), channel_id=1, source_target_pairs={{0,1},{1,0},{2,3},{3,2},{4,5},{5,4},{6,7},{7,6},{8,9},{9,8},{10,11... | collective-permute-start | bytes 983048 | tf_op jit(solution)/shard_map/ppermute | solution.py:53
  134.5 4.1 %collective-permute-done.34 = bf16[80,2048]{1,0:T(8,128)(2,1)S(1)} collective-permute-done((bf16[80,2048]{1,0:T(8,128)(2,1)S(1)}, bf16[80,2048]{1,0:T(8,128)(2,1)S(1)}, u32[]{:S(2)}, u32[]{:S(2)}) %collective-permute-start.34) | collective-permute-done | bytes 327712 | tf_op jit(solution)/shard_map/ppermute | solution.py:53
  138.7 1.2 collective-permute-start.38
  140.0 8.5 %collective-permute-done.38 = bf16[80,2048]{1,0:T(8,128)(2,1)S(1)} collective-permute-done((bf16[80,2048]{1,0:T(8,128)(2,1)S(1)}, bf16[80,2048]{1,0:T(8,128)(2,1)S(1)}, u32[]{:S(2)}, u32[]{:S(2)}) %collective-permute-start.38) | collective-permute-done | bytes 327712 | tf_op jit(solution)/shard_map/ppermute | solution.py:53
  148.9 0.8 fusion.25
  150.4 1.3 fusion.22
  (160 shorter events, 11.3 us)
Async XLA Ops:
  0.0 2.9 %collective-permute-start = (bf16[160,2048]{1,0:T(8,128)(2,1)}, bf16[160,2048]{1,0:T(8,128)(2,1)S(1)}, u32[]{:S(2)}, u32[]{:S(2)}) collective-permute-start(bf16[160,2048]{1,0:T(8,128)(2,1)} %param.5), channel_id=1, source_target_pairs={{0,1},{1,0},{2,3},{3,2},{4,5},{5,4},{6,7},{7,6},{8,9},{9,8},{10,11... | collective-permute-start | bytes 1966088 | tf_op jit(solution)/shard_map/ppermute | solution.py:53
  2.9 10.7 %copy-start.1 = (bf16[160,2048]{1,0:T(8,128)(2,1)S(1)}, bf16[160,2048]{1,0:T(8,128)(2,1)}, u32[]{:S(2)}) copy-start(bf16[160,2048]{1,0:T(8,128)(2,1)} %param.5) | copy-start | bytes 1966084
  3.2 7.4 %collective-permute-start.1 = (bf16[40,2048]{1,0:T(8,128)(2,1)S(1)}, bf16[40,2048]{1,0:T(8,128)(2,1)S(1)}, u32[]{:S(2)}, u32[]{:S(2)}) collective-permute-start(bf16[40,2048]{1,0:T(8,128)(2,1)S(1)} %slice.314), channel_id=1, source_target_pairs={{0,2},{1,3},{2,0},{3,1},{4,6},{5,7},{6,4},{7,5},{8,10},{9,11},{10,... | collective-permute-start | bytes 491528 | tf_op jit(solution)/shard_map/ppermute | solution.py:53
  10.7 10.5 %collective-permute-start.2 = (bf16[40,2048]{1,0:T(8,128)(2,1)S(1)}, bf16[40,2048]{1,0:T(8,128)(2,1)S(1)}, u32[]{:S(2)}, u32[]{:S(2)}) collective-permute-start(bf16[40,2048]{1,0:T(8,128)(2,1)S(1)} %slice_add_fusion.19), channel_id=1, source_target_pairs={{0,8},{4,12},{8,0},{12,4},{1,9},{5,13},{9,1},{13,5},{2,10},{6,14},... | collective-permute-start | bytes 491528 | tf_op jit(solution)/shard_map/ppermute | solution.py:53
  14.2 18.8 %copy-start = (s32[4]{0:T(128)S(1)}, s32[4]{0:T(128)}, u32[]{:S(2)}) copy-start(s32[4]{0:T(128)} %tick_ref) | copy-start | bytes 52
  14.2 8.6 %collective-permute-start.6 = (bf16[40,2048]{1,0:T(8,128)(2,1)S(1)}, bf16[40,2048]{1,0:T(8,128)(2,1)S(1)}, u32[]{:S(2)}, u32[]{:S(2)}) collective-permute-start(bf16[40,2048]{1,0:T(8,128)(2,1)S(1)} %slice.316), channel_id=1, source_target_pairs={{0,2},{1,3},{2,0},{3,1},{4,6},{5,7},{6,4},{7,5},{8,10},{9,11},{10,... | collective-permute-start | bytes 491528 | tf_op jit(solution)/shard_map/ppermute | solution.py:53
  21.2 5.4 %collective-permute-start.3 = (bf16[40,2048]{1,0:T(8,128)(2,1)S(1)}, bf16[40,2048]{1,0:T(8,128)(2,1)S(1)}, u32[]{:S(2)}, u32[]{:S(2)}) collective-permute-start(bf16[40,2048]{1,0:T(8,128)(2,1)S(1)} %get-tuple-element.108), channel_id=1, source_target_pairs={{0,2},{1,3},{2,0},{3,1},{4,6},{5,7},{6,4},{7,5},{8,10},{9,11},{10,... | collective-permute-start | bytes 491528 | tf_op jit(solution)/shard_map/ppermute | solution.py:53
  22.8 9.5 %collective-permute-start.7 = (bf16[40,2048]{1,0:T(8,128)(2,1)S(1)}, bf16[40,2048]{1,0:T(8,128)(2,1)S(1)}, u32[]{:S(2)}, u32[]{:S(2)}) collective-permute-start(bf16[40,2048]{1,0:T(8,128)(2,1)S(1)} %slice_add_fusion.18), channel_id=1, source_target_pairs={{0,8},{4,12},{8,0},{12,4},{1,9},{5,13},{9,1},{13,5},{2,10},{6,14},... | collective-permute-start | bytes 491528 | tf_op jit(solution)/shard_map/ppermute | solution.py:53
  26.6 11.6 %collective-permute-start.4 = (bf16[80,2048]{1,0:T(8,128)(2,1)S(1)}, bf16[80,2048]{1,0:T(8,128)(2,1)S(1)}, u32[]{:S(2)}, u32[]{:S(2)}) collective-permute-start(bf16[80,2048]{1,0:T(8,128)(2,1)S(1)} %pad_maximum_fusion.11), channel_id=1, source_target_pairs={{0,4},{1,0},{2,6},{3,2},{4,5},{5,1},{6,7},{7,3},{8,12},{9,8},{10,1... | collective-permute-start | bytes 983048 | tf_op jit(solution)/shard_map/ppermute | solution.py:130
  28.2 10.1 %collective-permute-start.5 = (bf16[80,2048]{1,0:T(8,128)(2,1)S(1)}, bf16[80,2048]{1,0:T(8,128)(2,1)S(1)}, u32[]{:S(2)}, u32[]{:S(2)}) collective-permute-start(bf16[80,2048]{1,0:T(8,128)(2,1)S(1)} %pad_maximum_fusion.11), channel_id=1, source_target_pairs={{1,4},{3,6},{4,1},{6,3},{9,12},{11,14},{12,9},{14,11},{17,20},{19,... | collective-permute-start | bytes 983048 | tf_op jit(solution)/shard_map/ppermute | solution.py:130
  32.4 6.0 %collective-permute-start.8 = (bf16[40,2048]{1,0:T(8,128)(2,1)S(1)}, bf16[40,2048]{1,0:T(8,128)(2,1)S(1)}, u32[]{:S(2)}, u32[]{:S(2)}) collective-permute-start(bf16[40,2048]{1,0:T(8,128)(2,1)S(1)} %get-tuple-element.104), channel_id=1, source_target_pairs={{0,2},{1,3},{2,0},{3,1},{4,6},{5,7},{6,4},{7,5},{8,10},{9,11},{10,... | collective-permute-start | bytes 491528 | tf_op jit(solution)/shard_map/ppermute | solution.py:53
  40.3 1.3 copy-start.2
  40.3 22.3 %slice-start.4 = ((s8[14680064]{0:T(1024)(128)(4,1)}), s8[2097152]{0:T(1024)(128)(4,1)S(1)}, s32[]{:S(2)}) async-start(s8[14680064]{0:T(1024)(128)(4,1)} %bitcast.109), calls=%async_computation.4 | async-start | bytes 4194304
  41.6 1.0 copy-start.3
  43.3 2.2 %collective-permute-start.9 = (bf16[2,80,1536]{2,1,0:T(8,128)(2,1)}, bf16[2,80,1536]{2,1,0:T(8,128)(2,1)}, u32[]{:S(2)}, u32[]{:S(2)}) collective-permute-start(bf16[2,80,1536]{2,1,0:T(8,128)(2,1)} %pad_maximum_fusion.5), channel_id=1, source_target_pairs={{0,1},{1,0},{2,3},{3,2},{4,5},{5,4},{6,7},{7,6},{8,9},{9,8},{10,11... | collective-permute-start | bytes 1474568 | tf_op jit(solution)/shard_map/ppermute | solution.py:53
  43.3 16.3 %collective-permute-start.11 = (bf16[80,2048]{1,0:T(8,128)(2,1)}, bf16[80,2048]{1,0:T(8,128)(2,1)S(1)}, u32[]{:S(2)}, u32[]{:S(2)}) collective-permute-start(bf16[80,2048]{1,0:T(8,128)(2,1)} %pad_maximum_fusion.12), channel_id=1, source_target_pairs={{0,4},{1,0},{2,6},{3,2},{4,5},{5,1},{6,7},{7,3},{8,12},{9,8},{10,1... | collective-permute-start | bytes 983048 | tf_op jit(solution)/shard_map/ppermute | solution.py:130
  43.9 15.7 %collective-permute-start.12 = (bf16[80,2048]{1,0:T(8,128)(2,1)}, bf16[80,2048]{1,0:T(8,128)(2,1)S(1)}, u32[]{:S(2)}, u32[]{:S(2)}) collective-permute-start(bf16[80,2048]{1,0:T(8,128)(2,1)} %pad_maximum_fusion.12), channel_id=1, source_target_pairs={{1,4},{3,6},{4,1},{6,3},{9,12},{11,14},{12,9},{14,11},{17,20},{19,... | collective-permute-start | bytes 983048 | tf_op jit(solution)/shard_map/ppermute | solution.py:130
  47.0 15.7 %slice-start.5 = ((s8[14680064]{0:T(1024)(128)(4,1)}), s8[4194304]{0:T(1024)(128)(4,1)S(1)}, s32[]{:S(2)}) async-start(s8[14680064]{0:T(1024)(128)(4,1)} %bitcast.109), calls=%async_computation.5 | async-start | bytes 8388608
  47.8 14.9 %slice-start.6 = ((s8[14680064]{0:T(1024)(128)(4,1)}), s8[4194304]{0:T(1024)(128)(4,1)S(1)}, s32[]{:S(2)}) async-start(s8[14680064]{0:T(1024)(128)(4,1)} %bitcast.109), calls=%async_computation.6 | async-start | bytes 8388608
  53.2 9.5 %slice-start.7 = ((s8[14680064]{0:T(1024)(128)(4,1)}), s8[4194304]{0:T(1024)(128)(4,1)S(1)}, s32[]{:S(2)}) async-start(s8[14680064]{0:T(1024)(128)(4,1)} %bitcast.109), calls=%async_computation.7 | async-start | bytes 8388608
  53.2 12.3 %slice-start = ((s8[14680064]{0:T(1024)(128)(4,1)}), s8[4194304]{0:T(1024)(128)(4,1)S(1)}, s32[]{:S(2)}) async-start(s8[14680064]{0:T(1024)(128)(4,1)} %bitcast.107), calls=%async_computation | async-start | bytes 8388608
  53.2 12.3 %slice-start.1 = ((s8[14680064]{0:T(1024)(128)(4,1)}), s8[4194304]{0:T(1024)(128)(4,1)S(1)}, s32[]{:S(2)}) async-start(s8[14680064]{0:T(1024)(128)(4,1)} %bitcast.107), calls=%async_computation.1 | async-start | bytes 8388608
  58.3 1.7 %copy-start.4 = (bf16[80,2048]{1,0:T(8,128)(2,1)S(1)}, bf16[80,2048]{1,0:T(8,128)(2,1)}, u32[]{:S(2)}) copy-start(bf16[80,2048]{1,0:T(8,128)(2,1)} %pad_maximum_fusion.12) | copy-start | bytes 983044
  58.5 3.2 %collective-permute-start.13 = (bf16[2,80,2048]{2,1,0:T(8,128)(2,1)S(1)}, bf16[2,80,2048]{2,1,0:T(8,128)(2,1)S(1)}, u32[]{:S(2)}, u32[]{:S(2)}) collective-permute-start(bf16[2,80,2048]{2,1,0:T(8,128)(2,1)S(1)} %pad_maximum_fusion.3), channel_id=1, source_target_pairs={{0,1},{1,0},{2,3},{3,2},{4,5},{5,4},{6,7},{7,6},{8,9},{9,8},{10,11... | collective-permute-start | bytes 1966088 | tf_op jit(solution)/shard_map/ppermute | solution.py:53
  60.1 5.4 %slice-start.2 = ((s8[14680064]{0:T(1024)(128)(4,1)}), s8[4194304]{0:T(1024)(128)(4,1)S(1)}, s32[]{:S(2)}) async-start(s8[14680064]{0:T(1024)(128)(4,1)} %bitcast.107), calls=%async_computation.2 | async-start | bytes 8388608
  60.1 10.6 %collective-permute-start.10 = (bf16[2,40,1536]{2,1,0:T(8,128)(2,1)}, bf16[2,40,1536]{2,1,0:T(8,128)(2,1)}, u32[]{:S(2)}, u32[]{:S(2)}) collective-permute-start(bf16[2,40,1536]{2,1,0:T(8,128)(2,1)} %pad_maximum_fusion.15), channel_id=1, source_target_pairs={{0,2},{1,3},{2,0},{3,1},{4,6},{5,7},{6,4},{7,5},{8,10},{9,11},{10,... | collective-permute-start | bytes 737288 | tf_op jit(solution)/shard_map/ppermute | solution.py:53
  62.7 2.8 %slice-start.3 = ((s8[14680064]{0:T(1024)(128)(4,1)}), s8[2097152]{0:T(1024)(128)(4,1)S(1)}, s32[]{:S(2)}) async-start(s8[14680064]{0:T(1024)(128)(4,1)} %bitcast.107), calls=%async_computation.3 | async-start | bytes 4194304
  67.3 1.1 copy-start.6
  68.5 6.9 %copy-start.8 = (bf16[2,40,2048]{2,1,0:T(8,128)(2,1)S(1)}, bf16[2,40,2048]{2,1,0:T(8,128)(2,1)}, u32[]{:S(2)}) copy-start(bf16[2,40,2048]{2,1,0:T(8,128)(2,1)} %pad_maximum_fusion.13) | copy-start | bytes 983044
  68.5 14.0 %copy-start.7 = (f32[160,2304]{1,0:T(8,128)S(1)}, f32[160,2304]{1,0:T(8,128)}, u32[]{:S(2)}) copy-start(f32[160,2304]{1,0:T(8,128)} %copy-done.6) | copy-start | bytes 4423684
  69.8 12.7 %copy-start.5 = (f32[160,2304]{1,0:T(8,128)S(1)}, f32[160,2304]{1,0:T(8,128)}, u32[]{:S(2)}) copy-start(f32[160,2304]{1,0:T(8,128)} %fusion.4) | copy-start | bytes 4423684
  69.9 12.6 %collective-permute-start.17 = (bf16[2,80,2304]{2,1,0:T(8,128)(2,1)S(1)}, bf16[2,80,2304]{2,1,0:T(8,128)(2,1)S(1)}, u32[]{:S(2)}, u32[]{:S(2)}) collective-permute-start(bf16[2,80,2304]{2,1,0:T(8,128)(2,1)S(1)} %pad_maximum_fusion), channel_id=1, source_target_pairs={{0,1},{1,0},{2,3},{3,2},{4,5},{5,4},{6,7},{7,6},{8,9},{9,8},{10,11... | collective-permute-start | bytes 2211848 | tf_op jit(solution)/shard_map/ppermute | solution.py:53
  71.8 9.7 %collective-permute-start.14 = (bf16[40,1536]{1,0:T(8,128)(2,1)S(1)}, bf16[40,1536]{1,0:T(8,128)(2,1)S(1)}, u32[]{:S(2)}, u32[]{:S(2)}) collective-permute-start(bf16[40,1536]{1,0:T(8,128)(2,1)S(1)} %fusion.47), channel_id=1, source_target_pairs={{0,8},{4,12},{8,0},{12,4},{1,9},{5,13},{9,1},{13,5},{2,10},{6,14},... | collective-permute-start | bytes 368648 | tf_op jit(solution)/shard_map/ppermute | solution.py:53
  75.4 10.4 %collective-permute-start.16 = (bf16[2,40,2048]{2,1,0:T(8,128)(2,1)S(1)}, bf16[2,40,2048]{2,1,0:T(8,128)(2,1)S(1)}, u32[]{:S(2)}, u32[]{:S(2)}) collective-permute-start(bf16[2,40,2048]{2,1,0:T(8,128)(2,1)S(1)} %copy-done.8), channel_id=1, source_target_pairs={{0,2},{1,3},{2,0},{3,1},{4,6},{5,7},{6,4},{7,5},{8,10},{9,11},{10,... | collective-permute-start | bytes 983048 | tf_op jit(solution)/shard_map/ppermute | solution.py:53
  81.5 7.0 %collective-permute-start.15 = (bf16[40,1536]{1,0:T(8,128)(2,1)S(1)}, bf16[40,1536]{1,0:T(8,128)(2,1)S(1)}, u32[]{:S(2)}, u32[]{:S(2)}) collective-permute-start(bf16[40,1536]{1,0:T(8,128)(2,1)S(1)} %get-tuple-element.112), channel_id=1, source_target_pairs={{0,2},{1,3},{2,0},{3,1},{4,6},{5,7},{6,4},{7,5},{8,10},{9,11},{10,... | collective-permute-start | bytes 368648 | tf_op jit(solution)/shard_map/ppermute | solution.py:53
  82.7 12.9 %collective-permute-start.21 = (bf16[2,40,2304]{2,1,0:T(8,128)(2,1)S(1)}, bf16[2,40,2304]{2,1,0:T(8,128)(2,1)S(1)}, u32[]{:S(2)}, u32[]{:S(2)}) collective-permute-start(bf16[2,40,2304]{2,1,0:T(8,128)(2,1)S(1)} %pad_maximum_fusion.9), channel_id=1, source_target_pairs={{0,2},{1,3},{2,0},{3,1},{4,6},{5,7},{6,4},{7,5},{8,10},{9,11},{10,... | collective-permute-start | bytes 1105928 | tf_op jit(solution)/shard_map/ppermute | solution.py:53
  85.9 8.7 %collective-permute-start.18 = (bf16[40,2048]{1,0:T(8,128)(2,1)S(1)}, bf16[40,2048]{1,0:T(8,128)(2,1)S(1)}, u32[]{:S(2)}, u32[]{:S(2)}) collective-permute-start(bf16[40,2048]{1,0:T(8,128)(2,1)S(1)} %fusion.43), channel_id=1, source_target_pairs={{0,8},{4,12},{8,0},{12,4},{1,9},{5,13},{9,1},{13,5},{2,10},{6,14},... | collective-permute-start | bytes 491528 | tf_op jit(solution)/shard_map/ppermute | solution.py:53
  87.3 27.4 %slice-start.8 = ((s8[14680064]{0:T(1024)(128)(4,1)}), s8[4194304]{0:T(1024)(128)(4,1)S(1)}, s32[]{:S(2)}) async-start(s8[14680064]{0:T(1024)(128)(4,1)} %bitcast.118), calls=%async_computation.8 | async-start | bytes 8388608
  87.3 27.4 %slice-start.9 = ((s8[14680064]{0:T(1024)(128)(4,1)}), s8[4194304]{0:T(1024)(128)(4,1)S(1)}, s32[]{:S(2)}) async-start(s8[14680064]{0:T(1024)(128)(4,1)} %bitcast.118), calls=%async_computation.9 | async-start | bytes 8388608
  88.4 7.5 %collective-permute-start.20 = (bf16[2,80,1280]{2,1,0:T(8,128)(2,1)S(1)}, bf16[2,80,1280]{2,1,0:T(8,128)(2,1)S(1)}, u32[]{:S(2)}, u32[]{:S(2)}) collective-permute-start(bf16[2,80,1280]{2,1,0:T(8,128)(2,1)S(1)} %pad_maximum_fusion.7), channel_id=1, source_target_pairs={{0,1},{1,0},{2,3},{3,2},{4,5},{5,4},{6,7},{7,6},{8,9},{9,8},{10,11... | collective-permute-start | bytes 1228808 | tf_op jit(solution)/shard_map/ppermute | solution.py:53
  88.5 13.4 %collective-permute-start.22 = (bf16[80,1536]{1,0:T(8,128)(2,1)S(1)}, bf16[80,1536]{1,0:T(8,128)(2,1)S(1)}, u32[]{:S(2)}, u32[]{:S(2)}) collective-permute-start(bf16[80,1536]{1,0:T(8,128)(2,1)S(1)} %pad_maximum_fusion.16), channel_id=1, source_target_pairs={{0,4},{1,0},{2,6},{3,2},{4,5},{5,1},{6,7},{7,3},{8,12},{9,8},{10,1... | collective-permute-start | bytes 737288 | tf_op jit(solution)/shard_map/ppermute | solution.py:130
  89.7 13.3 %collective-permute-start.23 = (bf16[80,1536]{1,0:T(8,128)(2,1)S(1)}, bf16[80,1536]{1,0:T(8,128)(2,1)S(1)}, u32[]{:S(2)}, u32[]{:S(2)}) collective-permute-start(bf16[80,1536]{1,0:T(8,128)(2,1)S(1)} %pad_maximum_fusion.16), channel_id=1, source_target_pairs={{1,4},{3,6},{4,1},{6,3},{9,12},{11,14},{12,9},{14,11},{17,20},{19,... | collective-permute-start | bytes 737288 | tf_op jit(solution)/shard_map/ppermute | solution.py:130
  94.7 7.2 %collective-permute-start.19 = (bf16[40,2048]{1,0:T(8,128)(2,1)S(1)}, bf16[40,2048]{1,0:T(8,128)(2,1)S(1)}, u32[]{:S(2)}, u32[]{:S(2)}) collective-permute-start(bf16[40,2048]{1,0:T(8,128)(2,1)S(1)} %get-tuple-element.100), channel_id=1, source_target_pairs={{0,2},{1,3},{2,0},{3,1},{4,6},{5,7},{6,4},{7,5},{8,10},{9,11},{10,... | collective-permute-start | bytes 491528 | tf_op jit(solution)/shard_map/ppermute | solution.py:53
  95.7 10.5 %collective-permute-start.25 = (bf16[40,2304]{1,0:T(8,128)(2,1)S(1)}, bf16[40,2304]{1,0:T(8,128)(2,1)S(1)}, u32[]{:S(2)}, u32[]{:S(2)}) collective-permute-start(bf16[40,2304]{1,0:T(8,128)(2,1)S(1)} %fusion.39), channel_id=1, source_target_pairs={{0,8},{4,12},{8,0},{12,4},{1,9},{5,13},{9,1},{13,5},{2,10},{6,14},... | collective-permute-start | bytes 552968 | tf_op jit(solution)/shard_map/ppermute | solution.py:53
  96.1 11.2 %collective-permute-start.24 = (bf16[2,40,1280]{2,1,0:T(8,128)(2,1)S(1)}, bf16[2,40,1280]{2,1,0:T(8,128)(2,1)S(1)}, u32[]{:S(2)}, u32[]{:S(2)}) collective-permute-start(bf16[2,40,1280]{2,1,0:T(8,128)(2,1)S(1)} %pad_maximum_fusion.17), channel_id=1, source_target_pairs={{0,2},{1,3},{2,0},{3,1},{4,6},{5,7},{6,4},{7,5},{8,10},{9,11},{10,... | collective-permute-start | bytes 614408 | tf_op jit(solution)/shard_map/ppermute | solution.py:53
  101.9 12.9 %slice-start.10 = ((s8[14680064]{0:T(1024)(128)(4,1)}), s8[4194304]{0:T(1024)(128)(4,1)S(1)}, s32[]{:S(2)}) async-start(s8[14680064]{0:T(1024)(128)(4,1)} %bitcast.118), calls=%async_computation.10 | async-start | bytes 8388608
  101.9 9.7 %collective-permute-start.26 = (bf16[80,2048]{1,0:T(8,128)(2,1)S(1)}, bf16[80,2048]{1,0:T(8,128)(2,1)S(1)}, u32[]{:S(2)}, u32[]{:S(2)}) collective-permute-start(bf16[80,2048]{1,0:T(8,128)(2,1)S(1)} %pad_maximum_fusion.14), channel_id=1, source_target_pairs={{0,4},{1,0},{2,6},{3,2},{4,5},{5,1},{6,7},{7,3},{8,12},{9,8},{10,1... | collective-permute-start | bytes 983048 | tf_op jit(solution)/shard_map/ppermute | solution.py:130
  102.0 9.6 %collective-permute-start.27 = (bf16[80,2048]{1,0:T(8,128)(2,1)S(1)}, bf16[80,2048]{1,0:T(8,128)(2,1)S(1)}, u32[]{:S(2)}, u32[]{:S(2)}) collective-permute-start(bf16[80,2048]{1,0:T(8,128)(2,1)S(1)} %pad_maximum_fusion.14), channel_id=1, source_target_pairs={{1,4},{3,6},{4,1},{6,3},{9,12},{11,14},{12,9},{14,11},{17,20},{19,... | collective-permute-start | bytes 983048 | tf_op jit(solution)/shard_map/ppermute | solution.py:130
  106.3 5.6 %collective-permute-start.28 = (bf16[40,2304]{1,0:T(8,128)(2,1)S(1)}, bf16[40,2304]{1,0:T(8,128)(2,1)S(1)}, u32[]{:S(2)}, u32[]{:S(2)}) collective-permute-start(bf16[40,2304]{1,0:T(8,128)(2,1)S(1)} %get-tuple-element.92), channel_id=1, source_target_pairs={{0,2},{1,3},{2,0},{3,1},{4,6},{5,7},{6,4},{7,5},{8,10},{9,11},{10,... | collective-permute-start | bytes 552968 | tf_op jit(solution)/shard_map/ppermute | solution.py:53
  107.4 7.4 %slice-start.11 = ((s8[14680064]{0:T(1024)(128)(4,1)}), s8[2097152]{0:T(1024)(128)(4,1)S(1)}, s32[]{:S(2)}) async-start(s8[14680064]{0:T(1024)(128)(4,1)} %bitcast.118), calls=%async_computation.11 | async-start | bytes 4194304
  107.4 9.0 %collective-permute-start.30 = (bf16[40,1280]{1,0:T(8,128)(2,1)S(1)}, bf16[40,1280]{1,0:T(8,128)(2,1)S(1)}, u32[]{:S(2)}, u32[]{:S(2)}) collective-permute-start(bf16[40,1280]{1,0:T(8,128)(2,1)S(1)} %fusion.51), channel_id=1, source_target_pairs={{0,8},{4,12},{8,0},{12,4},{1,9},{5,13},{9,1},{13,5},{2,10},{6,14},... | collective-permute-start | bytes 307208 | tf_op jit(solution)/shard_map/ppermute | solution.py:53
  111.9 9.7 %collective-permute-start.32 = (bf16[80,2304]{1,0:T(8,128)(2,1)S(1)}, bf16[80,2304]{1,0:T(8,128)(2,1)S(1)}, u32[]{:S(2)}, u32[]{:S(2)}) collective-permute-start(bf16[80,2304]{1,0:T(8,128)(2,1)S(1)} %pad_maximum_fusion.10), channel_id=1, source_target_pairs={{0,4},{1,0},{2,6},{3,2},{4,5},{5,1},{6,7},{7,3},{8,12},{9,8},{10,1... | collective-permute-start | bytes 1105928 | tf_op jit(solution)/shard_map/ppermute | solution.py:130
  114.0 7.6 %collective-permute-start.33 = (bf16[80,2304]{1,0:T(8,128)(2,1)S(1)}, bf16[80,2304]{1,0:T(8,128)(2,1)S(1)}, u32[]{:S(2)}, u32[]{:S(2)}) collective-permute-start(bf16[80,2304]{1,0:T(8,128)(2,1)S(1)} %pad_maximum_fusion.10), channel_id=1, source_target_pairs={{1,4},{3,6},{4,1},{6,3},{9,12},{11,14},{12,9},{14,11},{17,20},{19,... | collective-permute-start | bytes 1105928 | tf_op jit(solution)/shard_map/ppermute | solution.py:130
  116.4 7.1 %collective-permute-start.31 = (bf16[40,1280]{1,0:T(8,128)(2,1)S(1)}, bf16[40,1280]{1,0:T(8,128)(2,1)S(1)}, u32[]{:S(2)}, u32[]{:S(2)}) collective-permute-start(bf16[40,1280]{1,0:T(8,128)(2,1)S(1)} %get-tuple-element.116), channel_id=1, source_target_pairs={{0,2},{1,3},{2,0},{3,1},{4,6},{5,7},{6,4},{7,5},{8,10},{9,11},{10,... | collective-permute-start | bytes 307208 | tf_op jit(solution)/shard_map/ppermute | solution.py:53
  117.6 10.5 %collective-permute-start.29 = (bf16[80,2048]{1,0:T(8,128)(2,1)S(1)}, bf16[80,2048]{1,0:T(8,128)(2,1)S(1)}, u32[]{:S(2)}, u32[]{:S(2)}) collective-permute-start(bf16[80,2048]{1,0:T(8,128)(2,1)S(1)} %slice.504), channel_id=1, source_target_pairs={{0,1},{1,0},{2,3},{3,2},{4,5},{5,4},{6,7},{7,6},{8,9},{9,8},{10,11... | collective-permute-start | bytes 983048 | tf_op jit(solution)/shard_map/ppermute | solution.py:53
  123.6 8.0 %collective-permute-start.35 = (bf16[80,1280]{1,0:T(8,128)(2,1)S(1)}, bf16[80,1280]{1,0:T(8,128)(2,1)S(1)}, u32[]{:S(2)}, u32[]{:S(2)}) collective-permute-start(bf16[80,1280]{1,0:T(8,128)(2,1)S(1)} %pad_maximum_fusion.18), channel_id=1, source_target_pairs={{0,4},{1,0},{2,6},{3,2},{4,5},{5,1},{6,7},{7,3},{8,12},{9,8},{10,1... | collective-permute-start | bytes 614408 | tf_op jit(solution)/shard_map/ppermute | solution.py:130
  127.5 4.1 %collective-permute-start.36 = (bf16[80,1280]{1,0:T(8,128)(2,1)S(1)}, bf16[80,1280]{1,0:T(8,128)(2,1)S(1)}, u32[]{:S(2)}, u32[]{:S(2)}) collective-permute-start(bf16[80,1280]{1,0:T(8,128)(2,1)S(1)} %pad_maximum_fusion.18), channel_id=1, source_target_pairs={{1,4},{3,6},{4,1},{6,3},{9,12},{11,14},{12,9},{14,11},{17,20},{19,... | collective-permute-start | bytes 614408 | tf_op jit(solution)/shard_map/ppermute | solution.py:130
  128.3 10.3 %collective-permute-start.34 = (bf16[80,2048]{1,0:T(8,128)(2,1)S(1)}, bf16[80,2048]{1,0:T(8,128)(2,1)S(1)}, u32[]{:S(2)}, u32[]{:S(2)}) collective-permute-start(bf16[80,2048]{1,0:T(8,128)(2,1)S(1)} %get-tuple-element.77), channel_id=1, source_target_pairs={{0,2},{1,3},{2,0},{3,1},{4,6},{5,7},{6,4},{7,5},{8,10},{9,11},{10,... | collective-permute-start | bytes 983048 | tf_op jit(solution)/shard_map/ppermute | solution.py:53
  132.8 5.8 %collective-permute-start.37 = (bf16[80,2048]{1,0:T(8,128)(2,1)S(1)}, bf16[80,2048]{1,0:T(8,128)(2,1)S(1)}, u32[]{:S(2)}, u32[]{:S(2)}) collective-permute-start(bf16[80,2048]{1,0:T(8,128)(2,1)S(1)} %slice.503), channel_id=1, source_target_pairs={{0,1},{1,0},{2,3},{3,2},{4,5},{5,4},{6,7},{7,6},{8,9},{9,8},{10,11... | collective-permute-start | bytes 983048 | tf_op jit(solution)/shard_map/ppermute | solution.py:53
  138.7 9.8 %collective-permute-start.38 = (bf16[80,2048]{1,0:T(8,128)(2,1)S(1)}, bf16[80,2048]{1,0:T(8,128)(2,1)S(1)}, u32[]{:S(2)}, u32[]{:S(2)}) collective-permute-start(bf16[80,2048]{1,0:T(8,128)(2,1)S(1)} %fusion.35), channel_id=1, source_target_pairs={{0,2},{1,3},{2,0},{3,1},{4,6},{5,7},{6,4},{7,5},{8,10},{9,11},{10,... | collective-permute-start | bytes 983048 | tf_op jit(solution)/shard_map/ppermute | solution.py:53
  140.0 9.7 %collective-permute-start.39 = (bf16[80,2048]{1,0:T(8,128)(2,1)S(1)}, bf16[80,2048]{1,0:T(8,128)(2,1)S(1)}, u32[]{:S(2)}, u32[]{:S(2)}) collective-permute-start(bf16[80,2048]{1,0:T(8,128)(2,1)S(1)} %get-tuple-element.73), channel_id=1, source_target_pairs={{0,1},{1,0},{2,3},{3,2},{4,5},{5,4},{6,7},{7,6},{8,9},{9,8},{10,11... | collective-permute-start | bytes 983048 | tf_op jit(solution)/shard_map/ppermute | solution.py:53
  148.7 1.7 %collective-permute-start.40 = (bf16[80,2048]{1,0:T(8,128)(2,1)S(1)}, bf16[80,2048]{1,0:T(8,128)(2,1)S(1)}, u32[]{:S(2)}, u32[]{:S(2)}) collective-permute-start(bf16[80,2048]{1,0:T(8,128)(2,1)S(1)} %get-tuple-element.75), channel_id=1, source_target_pairs={{0,1},{1,0},{2,3},{3,2},{4,5},{5,4},{6,7},{7,6},{8,9},{9,8},{10,11... | collective-permute-start | bytes 983048 | tf_op jit(solution)/shard_map/ppermute | solution.py:53

commit v18 on v16

--- a/solution.py
+++ b/solution.py
@@ -18,11 +18,11 @@
     "t1.cores": ["c00.dots"],
     "c01.dots": ["c00.sum"],
     "c10.dots": ["c01.sum"],
-    "c00.hidden": ["c10.dots"],
+    "c00.hidden": ["c11.dots"],
     "c10.sum": ["c00.halves"],
     "c01.hidden": ["c10.sum"],
-    "c11.dots": ["c01.hidden"],
-    "c00.columns": ["c11.dots"],
+    "c11.dots": ["c10.dots"],
+    "c00.columns": ["c01.hidden"],
     "c01.halves": ["c00.columns"],
     "c10.hidden": ["c01.halves"],
     "c11.sum": ["c10.hidden"],

time: 147 us -> 151 us (1.027)
  waiting for transfers between devices: 53.2 us -> 60.2 us
  starting transfers between devices: 46.5 us -> 42 us
    ppermute x29, waiting for transfers between devices: 48.5 us -> 55.8 us  [flip(): return lax.ppermute(value, axis, [(i, i ^ bit) for i in range(count)])]
    ppermute x12, starting transfers between devices: 15.5 us -> 11.3 us  [move(): return lax.ppermute(value, ('row', 'col'), pairs)]
  transfers between devices with their start and end apart: 41 -> 41, of which waited for: 15 -> 17; matrix products, arithmetic and copies ran while one was open for 24% -> 23% of each run, Pallas kernels for 4% -> 4%
where the time goes in v18:
time: 151 us; the launch traced here: 150 us
  waiting for transfers between devices  60.2 us (40%)
  starting transfers between devices  42 us (28%)
  matrix products  33.9 us (22%)
  Pallas kernels  5.84 us (4%)
  other arithmetic  5 us (3%)
  local copies, waits for them, and re-layouts  1.63 us (1%)
    ppermute x29, waiting for transfers between devices, flip(): return lax.ppermute(value, axis, [(i, i ^ bit) for i in range(count)])  55.8 us
    dot_general x17, matrix products, dot(): return jnp.dot(a, b, preferred_element_type=jnp.float32)  33.1 us
    ppermute x29, starting transfers between devices, flip(): return lax.ppermute(value, axis, [(i, i ^ bit) for i in range(count)])  30.7 us
    ppermute x12, starting transfers between devices, move(): return lax.ppermute(value, ('row', 'col'), pairs)  11.3 us
    pallas_call x1, Pallas kernels, pull(): pl.pallas_call(functools.partial(pull_kernel, first, end), in_specs=[pl.B...  5.84 us
    ppermute x12, waiting for transfers between devices, move(): return lax.ppermute(value, ('row', 'col'), pairs)  4.31 us
  transfers between devices with their start and end apart: 41, of which 17 were waited for; matrix products, arithmetic and copies ran while one was open for 23% of the time, Pallas kernels for 4%

profile of v18, /device:TPU:0, one launch (start us, length us, event | category | flops | bytes accessed | tf_op | source)
XLA Modules:
  0.0 149.5 jit_solution(891529477845674066)
XLA Ops:
  0.5 0.9 fusion.80
  1.5 1.4 fusion.70
  3.2 2.6 %collective-permute-start.1 = (bf16[40,2048]{1,0:T(8,128)(2,1)S(1)}, bf16[40,2048]{1,0:T(8,128)(2,1)S(1)}, u32[]{:S(2)}, u32[]{:S(2)}) collective-permute-start(bf16[40,2048]{1,0:T(8,128)(2,1)S(1)} %slice.314), channel_id=1, source_target_pairs={{0,2},{1,3},{2,0},{3,1},{4,6},{5,7},{6,4},{7,5},{8,10},{9,11},{10,... | collective-permute-start | bytes 491528 | tf_op jit(solution)/shard_map/ppermute | solution.py:53
  5.8 4.9 %collective-permute-done.1 = bf16[40,2048]{1,0:T(8,128)(2,1)S(1)} collective-permute-done((bf16[40,2048]{1,0:T(8,128)(2,1)S(1)}, bf16[40,2048]{1,0:T(8,128)(2,1)S(1)}, u32[]{:S(2)}, u32[]{:S(2)}) %collective-permute-start.1) | collective-permute-done | bytes 163872 | tf_op jit(solution)/shard_map/ppermute | solution.py:53
  10.7 2.9 %collective-permute-start.2 = (bf16[40,2048]{1,0:T(8,128)(2,1)S(1)}, bf16[40,2048]{1,0:T(8,128)(2,1)S(1)}, u32[]{:S(2)}, u32[]{:S(2)}) collective-permute-start(bf16[40,2048]{1,0:T(8,128)(2,1)S(1)} %slice_add_fusion.19), channel_id=1, source_target_pairs={{0,8},{4,12},{8,0},{12,4},{1,9},{5,13},{9,1},{13,5},{2,10},{6,14},... | collective-permute-start | bytes 491528 | tf_op jit(solution)/shard_map/ppermute | solution.py:53
  14.2 1.6 %collective-permute-start.6 = (bf16[40,2048]{1,0:T(8,128)(2,1)S(1)}, bf16[40,2048]{1,0:T(8,128)(2,1)S(1)}, u32[]{:S(2)}, u32[]{:S(2)}) collective-permute-start(bf16[40,2048]{1,0:T(8,128)(2,1)S(1)} %slice.316), channel_id=1, source_target_pairs={{0,2},{1,3},{2,0},{3,1},{4,6},{5,7},{6,4},{7,5},{8,10},{9,11},{10,... | collective-permute-start | bytes 491528 | tf_op jit(solution)/shard_map/ppermute | solution.py:53
  15.8 5.4 %collective-permute-done.2 = bf16[40,2048]{1,0:T(8,128)(2,1)S(1)} collective-permute-done((bf16[40,2048]{1,0:T(8,128)(2,1)S(1)}, bf16[40,2048]{1,0:T(8,128)(2,1)S(1)}, u32[]{:S(2)}, u32[]{:S(2)}) %collective-permute-start.2) | collective-permute-done | bytes 163872 | tf_op jit(solution)/shard_map/ppermute | solution.py:53
  21.2 1.6 %collective-permute-start.3 = (bf16[40,2048]{1,0:T(8,128)(2,1)S(1)}, bf16[40,2048]{1,0:T(8,128)(2,1)S(1)}, u32[]{:S(2)}, u32[]{:S(2)}) collective-permute-start(bf16[40,2048]{1,0:T(8,128)(2,1)S(1)} %get-tuple-element.104), channel_id=1, source_target_pairs={{0,2},{1,3},{2,0},{3,1},{4,6},{5,7},{6,4},{7,5},{8,10},{9,11},{10,... | collective-permute-start | bytes 491528 | tf_op jit(solution)/shard_map/ppermute | solution.py:53
  22.9 3.7 %collective-permute-done.3 = bf16[40,2048]{1,0:T(8,128)(2,1)S(1)} collective-permute-done((bf16[40,2048]{1,0:T(8,128)(2,1)S(1)}, bf16[40,2048]{1,0:T(8,128)(2,1)S(1)}, u32[]{:S(2)}, u32[]{:S(2)}) %collective-permute-start.3) | collective-permute-done | bytes 163872 | tf_op jit(solution)/shard_map/ppermute | solution.py:53
  26.6 1.6 %collective-permute-start.4 = (bf16[80,2048]{1,0:T(8,128)(2,1)S(1)}, bf16[80,2048]{1,0:T(8,128)(2,1)S(1)}, u32[]{:S(2)}, u32[]{:S(2)}) collective-permute-start(bf16[80,2048]{1,0:T(8,128)(2,1)S(1)} %pad_maximum_fusion.11), channel_id=1, source_target_pairs={{0,4},{1,0},{2,6},{3,2},{4,5},{5,1},{6,7},{7,3},{8,12},{9,8},{10,1... | collective-permute-start | bytes 983048 | tf_op jit(solution)/shard_map/ppermute | solution.py:130
  28.2 0.7 collective-permute-start.5
  28.9 3.5 %collective-permute-done.7 = bf16[40,2048]{1,0:T(8,128)(2,1)S(1)} collective-permute-done((bf16[40,2048]{1,0:T(8,128)(2,1)S(1)}, bf16[40,2048]{1,0:T(8,128)(2,1)S(1)}, u32[]{:S(2)}, u32[]{:S(2)}) %collective-permute-start.7) | collective-permute-done | bytes 163872 | tf_op jit(solution)/shard_map/ppermute | solution.py:53
  32.4 0.6 collective-permute-start.8
  33.0 5.8 %shard_map.55 = (bf16[2048,1792]{1,0:T(8,128)(2,1)S(1)}, bf16[2048,1792]{1,0:T(8,128)(2,1)S(1)}) custom-call(s32[4]{0:T(128)S(1)} %copy-done, bf16[2048,3584]{1,0:T(8,128)(2,1)} %gate_ref.1, bf16[2048,3584]{1,0:T(8,128)(2,1)} %up_ref.1), custom_call_target="tpu_custom_call" | custom-call | tf_op jit(solution)/shard_map/pallas_call | solution.py:73
  39.0 1.4 fusion.93
  40.4 1.4 fusion.94
  41.8 1.0 copy-done.2
  43.2 0.9 collective-permute-start.12
  44.0 1.1 collective-permute-done.9
  45.2 1.4 slice_add_fusion.7
  46.6 4.5 %fusion.12 = f32[160,1792]{1,0:T(8,128)S(1)} fusion(bf16[160,2048]{1,0:T(8,128)(2,1)S(1)} %pad_maximum_fusion.1, bf16[2048,3584]{1,0:T(8,128)(2,1)} %gate_ref.1), kind=kOutput, calls=%fused_computation.12 | convolution fusion | flops 1174405120 | bytes 9142272 | tf_op jit(solution)/shard_map/dot_general | solution.py:48
  51.1 4.6 %fusion.10 = f32[160,1792]{1,0:T(8,128)S(1)} fusion(bf16[160,2048]{1,0:T(8,128)(2,1)S(1)} %pad_maximum_fusion.1, bf16[2048,3584]{1,0:T(8,128)(2,1)} %up_ref.1), kind=kOutput, calls=%fused_computation.10 | convolution fusion | flops 1174405120 | bytes 9142272 | tf_op jit(solution)/shard_map/dot_general | solution.py:48
  55.9 0.7 collective-permute-start.13
  56.7 1.6 %collective-permute-start.10 = (bf16[2,40,1792]{2,1,0:T(8,128)(2,1)S(1)}, bf16[2,40,1792]{2,1,0:T(8,128)(2,1)S(1)}, u32[]{:S(2)}, u32[]{:S(2)}) collective-permute-start(bf16[2,40,1792]{2,1,0:T(8,128)(2,1)S(1)} %pad_maximum_fusion.13), channel_id=1, source_target_pairs={{0,2},{1,3},{2,0},{3,1},{4,6},{5,7},{6,4},{7,5},{8,10},{9,11},{10,... | collective-permute-start | bytes 860168 | tf_op jit(solution)/shard_map/ppermute | solution.py:53
  58.5 5.5 %fusion.4 = f32[160,2304]{1,0:T(8,128)S(1)} fusion(bf16[160,2048]{1,0:T(8,128)(2,1)S(1)} %pad_maximum_fusion.2, bf16[2048,3584]{1,0:T(8,128)(2,1)} %gate_ref.1), kind=kOutput, calls=%fused_computation.4 | convolution fusion | flops 1509949440 | bytes 11567104 | tf_op jit(solution)/shard_map/dot_general | solution.py:48
  64.0 1.7 %fusion.2 = f32[160,2304]{1,0:T(8,128)S(1)} fusion(bf16[160,2048]{1,0:T(8,128)(2,1)S(1)} %pad_maximum_fusion.2, bf16[2048,3584]{1,0:T(8,128)(2,1)S(1)} %bitcast.108), kind=kOutput, calls=%fused_computation.2 | convolution fusion | flops 1509949440 | bytes 11567104 | tf_op jit(solution)/shard_map/dot_general | solution.py:48
  66.3 1.0 fusion.16
  67.3 3.7 %fusion.18 = f32[160,1280]{1,0:T(8,128)S(1)} fusion(bf16[160,2048]{1,0:T(8,128)(2,1)S(1)} %pad_maximum_fusion.2, bf16[2048,3584]{1,0:T(8,128)(2,1)} %gate_ref.1), kind=kOutput, calls=%fused_computation.18 | convolution fusion | flops 838860800 | bytes 6717440 | tf_op jit(solution)/shard_map/dot_general | solution.py:48
  71.2 3.4 %collective-permute-start.14 = (bf16[40,1792]{1,0:T(8,128)(2,1)S(1)}, bf16[40,1792]{1,0:T(8,128)(2,1)S(1)}, u32[]{:S(2)}, u32[]{:S(2)}) collective-permute-start(bf16[40,1792]{1,0:T(8,128)(2,1)S(1)} %fusion.47), channel_id=1, source_target_pairs={{0,8},{4,12},{8,0},{12,4},{1,9},{5,13},{9,1},{13,5},{2,10},{6,14},... | collective-permute-start | bytes 430088 | tf_op jit(solution)/shard_map/ppermute | solution.py:53
  74.8 1.5 collective-permute-start.16
  76.3 5.6 %collective-permute-done.14 = bf16[40,1792]{1,0:T(8,128)(2,1)S(1)} collective-permute-done((bf16[40,1792]{1,0:T(8,128)(2,1)S(1)}, bf16[40,1792]{1,0:T(8,128)(2,1)S(1)}, u32[]{:S(2)}, u32[]{:S(2)}) %collective-permute-start.14) | collective-permute-done | bytes 143392 | tf_op jit(solution)/shard_map/ppermute | solution.py:53
  81.9 1.5 collective-permute-start.15
  83.7 0.7 collective-permute-start.21
  84.5 4.1 %collective-permute-done.15 = bf16[40,1792]{1,0:T(8,128)(2,1)S(1)} collective-permute-done((bf16[40,1792]{1,0:T(8,128)(2,1)S(1)}, bf16[40,1792]{1,0:T(8,128)(2,1)S(1)}, u32[]{:S(2)}, u32[]{:S(2)}) %collective-permute-start.15) | collective-permute-done | bytes 143392 | tf_op jit(solution)/shard_map/ppermute | solution.py:53
  88.7 0.8 collective-permute-start.23
  89.6 3.6 %collective-permute-done.18 = bf16[40,1792]{1,0:T(8,128)(2,1)S(1)} collective-permute-done((bf16[40,1792]{1,0:T(8,128)(2,1)S(1)}, bf16[40,1792]{1,0:T(8,128)(2,1)S(1)}, u32[]{:S(2)}, u32[]{:S(2)}) %collective-permute-start.18) | collective-permute-done | bytes 143392 | tf_op jit(solution)/shard_map/ppermute | solution.py:53
  93.2 1.3 collective-permute-start.19
  94.4 0.8 collective-permute-done.21
  95.6 1.4 collective-permute-start.24
  97.0 2.6 %collective-permute-done.19 = bf16[40,1792]{1,0:T(8,128)(2,1)S(1)} collective-permute-done((bf16[40,1792]{1,0:T(8,128)(2,1)S(1)}, bf16[40,1792]{1,0:T(8,128)(2,1)S(1)}, u32[]{:S(2)}, u32[]{:S(2)}) %collective-permute-start.19) | collective-permute-done | bytes 143392 | tf_op jit(solution)/shard_map/ppermute | solution.py:53
  99.6 0.6 collective-permute-start.26
  100.3 0.7 collective-permute-start.27
  101.0 4.6 %collective-permute-done.25 = bf16[40,2304]{1,0:T(8,128)(2,1)S(1)} collective-permute-done((bf16[40,2304]{1,0:T(8,128)(2,1)S(1)}, bf16[40,2304]{1,0:T(8,128)(2,1)S(1)}, u32[]{:S(2)}, u32[]{:S(2)}) %collective-permute-start.25) | collective-permute-done | bytes 184352 | tf_op jit(solution)/shard_map/ppermute | solution.py:53
  105.7 1.3 collective-permute-start.28
  107.1 1.4 fusion.8
  108.7 3.0 %collective-permute-done.28 = bf16[40,2304]{1,0:T(8,128)(2,1)S(1)} collective-permute-done((bf16[40,2304]{1,0:T(8,128)(2,1)S(1)}, bf16[40,2304]{1,0:T(8,128)(2,1)S(1)}, u32[]{:S(2)}, u32[]{:S(2)}) %collective-permute-start.28) | collective-permute-done | bytes 184352 | tf_op jit(solution)/shard_map/ppermute | solution.py:53
  112.0 0.7 collective-permute-start.33
  112.7 1.5 fusion.91
  114.2 1.2 collective-permute-start.31
  115.5 1.5 %collective-permute-start.29 = (bf16[80,2048]{1,0:T(8,128)(2,1)S(1)}, bf16[80,2048]{1,0:T(8,128)(2,1)S(1)}, u32[]{:S(2)}, u32[]{:S(2)}) collective-permute-start(bf16[80,2048]{1,0:T(8,128)(2,1)S(1)} %slice.504), channel_id=1, source_target_pairs={{0,1},{1,0},{2,3},{3,2},{4,5},{5,4},{6,7},{7,6},{8,9},{9,8},{10,11... | collective-permute-start | bytes 983048 | tf_op jit(solution)/shard_map/ppermute | solution.py:53
  117.0 2.2 %collective-permute-done.32 = bf16[80,2304]{1,0:T(8,128)(2,1)S(1)} collective-permute-done((bf16[80,2304]{1,0:T(8,128)(2,1)S(1)}, bf16[80,2304]{1,0:T(8,128)(2,1)S(1)}, u32[]{:S(2)}, u32[]{:S(2)}) %collective-permute-start.32) | collective-permute-done | bytes 368672 | tf_op jit(solution)/shard_map/ppermute | solution.py:130
  119.3 1.8 %fusion = f32[160,2048]{1,0:T(8,128)S(1)} fusion(bf16[3584,2048]{1,0:T(8,128)(2,1)S(1)} %bitcast.117, bf16[80,2304]{1,0:T(8,128)(2,1)S(1)} %get-tuple-element.90, bf16[80,2304]{1,0:T(8,128)(2,1)S(1)} %get-tuple-element.89), kind=kOutput, calls=%fused_computation | convolution fusion | flops 1511424000 | bytes 11485184 | tf_op jit(solution)/shard_map/dot_general | solution.py:48
  121.0 4.3 %collective-permute-start.35 = (bf16[80,1280]{1,0:T(8,128)(2,1)S(1)}, bf16[80,1280]{1,0:T(8,128)(2,1)S(1)}, u32[]{:S(2)}, u32[]{:S(2)}) collective-permute-start(bf16[80,1280]{1,0:T(8,128)(2,1)S(1)} %pad_maximum_fusion.18), channel_id=1, source_target_pairs={{0,4},{1,0},{2,6},{3,2},{4,5},{5,1},{6,7},{7,3},{8,12},{9,8},{10,1... | collective-permute-start | bytes 614408 | tf_op jit(solution)/shard_map/ppermute | solution.py:130
  125.4 0.7 collective-permute-start.36
  126.1 1.2 collective-permute-start.34
  127.4 2.1 %collective-permute-done.35 = bf16[80,1280]{1,0:T(8,128)(2,1)S(1)} collective-permute-done((bf16[80,1280]{1,0:T(8,128)(2,1)S(1)}, bf16[80,1280]{1,0:T(8,128)(2,1)S(1)}, u32[]{:S(2)}, u32[]{:S(2)}) %collective-permute-start.35) | collective-permute-done | bytes 204832 | tf_op jit(solution)/shard_map/ppermute | solution.py:130
  129.5 1.2 fusion.92
  130.8 1.7 %collective-permute-start.37 = (bf16[80,2048]{1,0:T(8,128)(2,1)S(1)}, bf16[80,2048]{1,0:T(8,128)(2,1)S(1)}, u32[]{:S(2)}, u32[]{:S(2)}) collective-permute-start(bf16[80,2048]{1,0:T(8,128)(2,1)S(1)} %slice.503), channel_id=1, source_target_pairs={{0,1},{1,0},{2,3},{3,2},{4,5},{5,4},{6,7},{7,6},{8,9},{9,8},{10,11... | collective-permute-start | bytes 983048 | tf_op jit(solution)/shard_map/ppermute | solution.py:53
  132.5 4.0 %collective-permute-done.34 = bf16[80,2048]{1,0:T(8,128)(2,1)S(1)} collective-permute-done((bf16[80,2048]{1,0:T(8,128)(2,1)S(1)}, bf16[80,2048]{1,0:T(8,128)(2,1)S(1)}, u32[]{:S(2)}, u32[]{:S(2)}) %collective-permute-start.34) | collective-permute-done | bytes 327712 | tf_op jit(solution)/shard_map/ppermute | solution.py:53
  136.6 1.2 collective-permute-start.38
  138.0 8.4 %collective-permute-done.38 = bf16[80,2048]{1,0:T(8,128)(2,1)S(1)} collective-permute-done((bf16[80,2048]{1,0:T(8,128)(2,1)S(1)}, bf16[80,2048]{1,0:T(8,128)(2,1)S(1)}, u32[]{:S(2)}, u32[]{:S(2)}) %collective-permute-start.38) | collective-permute-done | bytes 327712 | tf_op jit(solution)/shard_map/ppermute | solution.py:53
  146.7 0.8 fusion.25
  147.5 0.7 collective-permute-done.40
  148.2 1.3 fusion.22
  (139 shorter events, 6.0 us)
Async XLA Ops:
  0.0 2.9 %collective-permute-start = (bf16[160,2048]{1,0:T(8,128)(2,1)}, bf16[160,2048]{1,0:T(8,128)(2,1)S(1)}, u32[]{:S(2)}, u32[]{:S(2)}) collective-permute-start(bf16[160,2048]{1,0:T(8,128)(2,1)} %param.5), channel_id=1, source_target_pairs={{0,1},{1,0},{2,3},{3,2},{4,5},{5,4},{6,7},{7,6},{8,9},{9,8},{10,11... | collective-permute-start | bytes 1966088 | tf_op jit(solution)/shard_map/ppermute | solution.py:53
  2.9 10.7 %copy-start.1 = (bf16[160,2048]{1,0:T(8,128)(2,1)S(1)}, bf16[160,2048]{1,0:T(8,128)(2,1)}, u32[]{:S(2)}) copy-start(bf16[160,2048]{1,0:T(8,128)(2,1)} %param.5) | copy-start | bytes 1966084
  3.2 7.4 %collective-permute-start.1 = (bf16[40,2048]{1,0:T(8,128)(2,1)S(1)}, bf16[40,2048]{1,0:T(8,128)(2,1)S(1)}, u32[]{:S(2)}, u32[]{:S(2)}) collective-permute-start(bf16[40,2048]{1,0:T(8,128)(2,1)S(1)} %slice.314), channel_id=1, source_target_pairs={{0,2},{1,3},{2,0},{3,1},{4,6},{5,7},{6,4},{7,5},{8,10},{9,11},{10,... | collective-permute-start | bytes 491528 | tf_op jit(solution)/shard_map/ppermute | solution.py:53
  10.7 10.5 %collective-permute-start.2 = (bf16[40,2048]{1,0:T(8,128)(2,1)S(1)}, bf16[40,2048]{1,0:T(8,128)(2,1)S(1)}, u32[]{:S(2)}, u32[]{:S(2)}) collective-permute-start(bf16[40,2048]{1,0:T(8,128)(2,1)S(1)} %slice_add_fusion.19), channel_id=1, source_target_pairs={{0,8},{4,12},{8,0},{12,4},{1,9},{5,13},{9,1},{13,5},{2,10},{6,14},... | collective-permute-start | bytes 491528 | tf_op jit(solution)/shard_map/ppermute | solution.py:53
  14.2 18.8 %copy-start = (s32[4]{0:T(128)S(1)}, s32[4]{0:T(128)}, u32[]{:S(2)}) copy-start(s32[4]{0:T(128)} %tick_ref) | copy-start | bytes 52
  14.2 8.6 %collective-permute-start.6 = (bf16[40,2048]{1,0:T(8,128)(2,1)S(1)}, bf16[40,2048]{1,0:T(8,128)(2,1)S(1)}, u32[]{:S(2)}, u32[]{:S(2)}) collective-permute-start(bf16[40,2048]{1,0:T(8,128)(2,1)S(1)} %slice.316), channel_id=1, source_target_pairs={{0,2},{1,3},{2,0},{3,1},{4,6},{5,7},{6,4},{7,5},{8,10},{9,11},{10,... | collective-permute-start | bytes 491528 | tf_op jit(solution)/shard_map/ppermute | solution.py:53
  21.2 5.4 %collective-permute-start.3 = (bf16[40,2048]{1,0:T(8,128)(2,1)S(1)}, bf16[40,2048]{1,0:T(8,128)(2,1)S(1)}, u32[]{:S(2)}, u32[]{:S(2)}) collective-permute-start(bf16[40,2048]{1,0:T(8,128)(2,1)S(1)} %get-tuple-element.104), channel_id=1, source_target_pairs={{0,2},{1,3},{2,0},{3,1},{4,6},{5,7},{6,4},{7,5},{8,10},{9,11},{10,... | collective-permute-start | bytes 491528 | tf_op jit(solution)/shard_map/ppermute | solution.py:53
  22.8 9.5 %collective-permute-start.7 = (bf16[40,2048]{1,0:T(8,128)(2,1)S(1)}, bf16[40,2048]{1,0:T(8,128)(2,1)S(1)}, u32[]{:S(2)}, u32[]{:S(2)}) collective-permute-start(bf16[40,2048]{1,0:T(8,128)(2,1)S(1)} %slice_add_fusion.18), channel_id=1, source_target_pairs={{0,8},{4,12},{8,0},{12,4},{1,9},{5,13},{9,1},{13,5},{2,10},{6,14},... | collective-permute-start | bytes 491528 | tf_op jit(solution)/shard_map/ppermute | solution.py:53
  26.6 12.2 %collective-permute-start.4 = (bf16[80,2048]{1,0:T(8,128)(2,1)S(1)}, bf16[80,2048]{1,0:T(8,128)(2,1)S(1)}, u32[]{:S(2)}, u32[]{:S(2)}) collective-permute-start(bf16[80,2048]{1,0:T(8,128)(2,1)S(1)} %pad_maximum_fusion.11), channel_id=1, source_target_pairs={{0,4},{1,0},{2,6},{3,2},{4,5},{5,1},{6,7},{7,3},{8,12},{9,8},{10,1... | collective-permute-start | bytes 983048 | tf_op jit(solution)/shard_map/ppermute | solution.py:130
  28.2 10.7 %collective-permute-start.5 = (bf16[80,2048]{1,0:T(8,128)(2,1)S(1)}, bf16[80,2048]{1,0:T(8,128)(2,1)S(1)}, u32[]{:S(2)}, u32[]{:S(2)}) collective-permute-start(bf16[80,2048]{1,0:T(8,128)(2,1)S(1)} %pad_maximum_fusion.11), channel_id=1, source_target_pairs={{1,4},{3,6},{4,1},{6,3},{9,12},{11,14},{12,9},{14,11},{17,20},{19,... | collective-permute-start | bytes 983048 | tf_op jit(solution)/shard_map/ppermute | solution.py:130
  32.4 6.6 %collective-permute-start.8 = (bf16[40,2048]{1,0:T(8,128)(2,1)S(1)}, bf16[40,2048]{1,0:T(8,128)(2,1)S(1)}, u32[]{:S(2)}, u32[]{:S(2)}) collective-permute-start(bf16[40,2048]{1,0:T(8,128)(2,1)S(1)} %get-tuple-element.100), channel_id=1, source_target_pairs={{0,2},{1,3},{2,0},{3,1},{4,6},{5,7},{6,4},{7,5},{8,10},{9,11},{10,... | collective-permute-start | bytes 491528 | tf_op jit(solution)/shard_map/ppermute | solution.py:53
  41.8 1.0 copy-start.2
  43.0 2.2 %collective-permute-start.9 = (bf16[2,80,1792]{2,1,0:T(8,128)(2,1)S(1)}, bf16[2,80,1792]{2,1,0:T(8,128)(2,1)}, u32[]{:S(2)}, u32[]{:S(2)}) collective-permute-start(bf16[2,80,1792]{2,1,0:T(8,128)(2,1)S(1)} %pad_maximum_fusion.3), channel_id=1, source_target_pairs={{0,1},{1,0},{2,3},{3,2},{4,5},{5,4},{6,7},{7,6},{8,9},{9,8},{10,11... | collective-permute-start | bytes 1720328 | tf_op jit(solution)/shard_map/ppermute | solution.py:53
  43.1 13.4 %collective-permute-start.11 = (bf16[80,2048]{1,0:T(8,128)(2,1)S(1)}, bf16[80,2048]{1,0:T(8,128)(2,1)S(1)}, u32[]{:S(2)}, u32[]{:S(2)}) collective-permute-start(bf16[80,2048]{1,0:T(8,128)(2,1)S(1)} %pad_maximum_fusion.12), channel_id=1, source_target_pairs={{0,4},{1,0},{2,6},{3,2},{4,5},{5,1},{6,7},{7,3},{8,12},{9,8},{10,1... | collective-permute-start | bytes 983048 | tf_op jit(solution)/shard_map/ppermute | solution.py:130
  43.2 13.4 %collective-permute-start.12 = (bf16[80,2048]{1,0:T(8,128)(2,1)S(1)}, bf16[80,2048]{1,0:T(8,128)(2,1)S(1)}, u32[]{:S(2)}, u32[]{:S(2)}) collective-permute-start(bf16[80,2048]{1,0:T(8,128)(2,1)S(1)} %pad_maximum_fusion.12), channel_id=1, source_target_pairs={{1,4},{3,6},{4,1},{6,3},{9,12},{11,14},{12,9},{14,11},{17,20},{19,... | collective-permute-start | bytes 983048 | tf_op jit(solution)/shard_map/ppermute | solution.py:130
  51.1 12.9 %slice-start = ((s8[14680064]{0:T(1024)(128)(4,1)}), s8[4194304]{0:T(1024)(128)(4,1)S(1)}, s32[]{:S(2)}) async-start(s8[14680064]{0:T(1024)(128)(4,1)} %bitcast.107), calls=%async_computation | async-start | bytes 8388608
  51.1 12.9 %slice-start.1 = ((s8[14680064]{0:T(1024)(128)(4,1)}), s8[4194304]{0:T(1024)(128)(4,1)S(1)}, s32[]{:S(2)}) async-start(s8[14680064]{0:T(1024)(128)(4,1)} %bitcast.107), calls=%async_computation.1 | async-start | bytes 8388608
  55.9 2.4 %collective-permute-start.13 = (bf16[2,80,1792]{2,1,0:T(8,128)(2,1)S(1)}, bf16[2,80,1792]{2,1,0:T(8,128)(2,1)S(1)}, u32[]{:S(2)}, u32[]{:S(2)}) collective-permute-start(bf16[2,80,1792]{2,1,0:T(8,128)(2,1)S(1)} %pad_maximum_fusion.4), channel_id=1, source_target_pairs={{0,1},{1,0},{2,3},{3,2},{4,5},{5,4},{6,7},{7,6},{8,9},{9,8},{10,11... | collective-permute-start | bytes 1720328 | tf_op jit(solution)/shard_map/ppermute | solution.py:53
  56.7 7.4 %slice-start.2 = ((s8[14680064]{0:T(1024)(128)(4,1)}), s8[4194304]{0:T(1024)(128)(4,1)S(1)}, s32[]{:S(2)}) async-start(s8[14680064]{0:T(1024)(128)(4,1)} %bitcast.107), calls=%async_computation.2 | async-start | bytes 8388608
  56.7 14.4 %collective-permute-start.10 = (bf16[2,40,1792]{2,1,0:T(8,128)(2,1)S(1)}, bf16[2,40,1792]{2,1,0:T(8,128)(2,1)S(1)}, u32[]{:S(2)}, u32[]{:S(2)}) collective-permute-start(bf16[2,40,1792]{2,1,0:T(8,128)(2,1)S(1)} %pad_maximum_fusion.13), channel_id=1, source_target_pairs={{0,2},{1,3},{2,0},{3,1},{4,6},{5,7},{6,4},{7,5},{8,10},{9,11},{10,... | collective-permute-start | bytes 860168 | tf_op jit(solution)/shard_map/ppermute | solution.py:53
  58.4 5.6 %slice-start.3 = ((s8[14680064]{0:T(1024)(128)(4,1)}), s8[2097152]{0:T(1024)(128)(4,1)S(1)}, s32[]{:S(2)}) async-start(s8[14680064]{0:T(1024)(128)(4,1)} %bitcast.107), calls=%async_computation.3 | async-start | bytes 4194304
  65.9 17.5 %collective-permute-start.17 = (bf16[2,80,2304]{2,1,0:T(8,128)(2,1)S(1)}, bf16[2,80,2304]{2,1,0:T(8,128)(2,1)S(1)}, u32[]{:S(2)}, u32[]{:S(2)}) collective-permute-start(bf16[2,80,2304]{2,1,0:T(8,128)(2,1)S(1)} %pad_maximum_fusion), channel_id=1, source_target_pairs={{0,1},{1,0},{2,3},{3,2},{4,5},{5,4},{6,7},{7,6},{8,9},{9,8},{10,11... | collective-permute-start | bytes 2211848 | tf_op jit(solution)/shard_map/ppermute | solution.py:53
  66.3 40.8 %slice-start.4 = ((s8[14680064]{0:T(1024)(128)(4,1)}), s8[2097152]{0:T(1024)(128)(4,1)S(1)}, s32[]{:S(2)}) async-start(s8[14680064]{0:T(1024)(128)(4,1)} %bitcast.116), calls=%async_computation.4 | async-start | bytes 4194304
  67.3 39.8 %slice-start.5 = ((s8[14680064]{0:T(1024)(128)(4,1)}), s8[4194304]{0:T(1024)(128)(4,1)S(1)}, s32[]{:S(2)}) async-start(s8[14680064]{0:T(1024)(128)(4,1)} %bitcast.116), calls=%async_computation.5 | async-start | bytes 8388608
  71.0 36.1 %slice-start.6 = ((s8[14680064]{0:T(1024)(128)(4,1)}), s8[4194304]{0:T(1024)(128)(4,1)S(1)}, s32[]{:S(2)}) async-start(s8[14680064]{0:T(1024)(128)(4,1)} %bitcast.116), calls=%async_computation.6 | async-start | bytes 8388608
  71.2 10.6 %collective-permute-start.14 = (bf16[40,1792]{1,0:T(8,128)(2,1)S(1)}, bf16[40,1792]{1,0:T(8,128)(2,1)S(1)}, u32[]{:S(2)}, u32[]{:S(2)}) collective-permute-start(bf16[40,1792]{1,0:T(8,128)(2,1)S(1)} %fusion.47), channel_id=1, source_target_pairs={{0,8},{4,12},{8,0},{12,4},{1,9},{5,13},{9,1},{13,5},{2,10},{6,14},... | collective-permute-start | bytes 430088 | tf_op jit(solution)/shard_map/ppermute | solution.py:53
  74.8 9.5 %collective-permute-start.16 = (bf16[2,40,1792]{2,1,0:T(8,128)(2,1)S(1)}, bf16[2,40,1792]{2,1,0:T(8,128)(2,1)S(1)}, u32[]{:S(2)}, u32[]{:S(2)}) collective-permute-start(bf16[2,40,1792]{2,1,0:T(8,128)(2,1)S(1)} %pad_maximum_fusion.14), channel_id=1, source_target_pairs={{0,2},{1,3},{2,0},{3,1},{4,6},{5,7},{6,4},{7,5},{8,10},{9,11},{10,... | collective-permute-start | bytes 860168 | tf_op jit(solution)/shard_map/ppermute | solution.py:53
  76.3 19.2 %collective-permute-start.20 = (bf16[2,80,1280]{2,1,0:T(8,128)(2,1)S(1)}, bf16[2,80,1280]{2,1,0:T(8,128)(2,1)S(1)}, u32[]{:S(2)}, u32[]{:S(2)}) collective-permute-start(bf16[2,80,1280]{2,1,0:T(8,128)(2,1)S(1)} %pad_maximum_fusion.7), channel_id=1, source_target_pairs={{0,1},{1,0},{2,3},{3,2},{4,5},{5,4},{6,7},{7,6},{8,9},{9,8},{10,11... | collective-permute-start | bytes 1228808 | tf_op jit(solution)/shard_map/ppermute | solution.py:53
  81.9 6.7 %collective-permute-start.15 = (bf16[40,1792]{1,0:T(8,128)(2,1)S(1)}, bf16[40,1792]{1,0:T(8,128)(2,1)S(1)}, u32[]{:S(2)}, u32[]{:S(2)}) collective-permute-start(bf16[40,1792]{1,0:T(8,128)(2,1)S(1)} %get-tuple-element.112), channel_id=1, source_target_pairs={{0,2},{1,3},{2,0},{3,1},{4,6},{5,7},{6,4},{7,5},{8,10},{9,11},{10,... | collective-permute-start | bytes 430088 | tf_op jit(solution)/shard_map/ppermute | solution.py:53
  83.7 11.6 %collective-permute-start.21 = (bf16[2,40,2304]{2,1,0:T(8,128)(2,1)S(1)}, bf16[2,40,2304]{2,1,0:T(8,128)(2,1)S(1)}, u32[]{:S(2)}, u32[]{:S(2)}) collective-permute-start(bf16[2,40,2304]{2,1,0:T(8,128)(2,1)S(1)} %pad_maximum_fusion.9), channel_id=1, source_target_pairs={{0,2},{1,3},{2,0},{3,1},{4,6},{5,7},{6,4},{7,5},{8,10},{9,11},{10,... | collective-permute-start | bytes 1105928 | tf_op jit(solution)/shard_map/ppermute | solution.py:53
  84.4 8.7 %collective-permute-start.18 = (bf16[40,1792]{1,0:T(8,128)(2,1)S(1)}, bf16[40,1792]{1,0:T(8,128)(2,1)S(1)}, u32[]{:S(2)}, u32[]{:S(2)}) collective-permute-start(bf16[40,1792]{1,0:T(8,128)(2,1)S(1)} %fusion.45), channel_id=1, source_target_pairs={{0,8},{4,12},{8,0},{12,4},{1,9},{5,13},{9,1},{13,5},{2,10},{6,14},... | collective-permute-start | bytes 430088 | tf_op jit(solution)/shard_map/ppermute | solution.py:53
  88.7 18.5 %slice-start.7 = ((s8[14680064]{0:T(1024)(128)(4,1)}), s8[4194304]{0:T(1024)(128)(4,1)S(1)}, s32[]{:S(2)}) async-start(s8[14680064]{0:T(1024)(128)(4,1)} %bitcast.116), calls=%async_computation.7 | async-start | bytes 8388608
  88.7 11.6 %collective-permute-start.22 = (bf16[80,1792]{1,0:T(8,128)(2,1)S(1)}, bf16[80,1792]{1,0:T(8,128)(2,1)S(1)}, u32[]{:S(2)}, u32[]{:S(2)}) collective-permute-start(bf16[80,1792]{1,0:T(8,128)(2,1)S(1)} %pad_maximum_fusion.15), channel_id=1, source_target_pairs={{0,4},{1,0},{2,6},{3,2},{4,5},{5,1},{6,7},{7,3},{8,12},{9,8},{10,1... | collective-permute-start | bytes 860168 | tf_op jit(solution)/shard_map/ppermute | solution.py:130
  88.7 12.2 %collective-permute-start.23 = (bf16[80,1792]{1,0:T(8,128)(2,1)S(1)}, bf16[80,1792]{1,0:T(8,128)(2,1)S(1)}, u32[]{:S(2)}, u32[]{:S(2)}) collective-permute-start(bf16[80,1792]{1,0:T(8,128)(2,1)S(1)} %pad_maximum_fusion.15), channel_id=1, source_target_pairs={{1,4},{3,6},{4,1},{6,3},{9,12},{11,14},{12,9},{14,11},{17,20},{19,... | collective-permute-start | bytes 860168 | tf_op jit(solution)/shard_map/ppermute | solution.py:130
  93.2 6.4 %collective-permute-start.19 = (bf16[40,1792]{1,0:T(8,128)(2,1)S(1)}, bf16[40,1792]{1,0:T(8,128)(2,1)S(1)}, u32[]{:S(2)}, u32[]{:S(2)}) collective-permute-start(bf16[40,1792]{1,0:T(8,128)(2,1)S(1)} %get-tuple-element.110), channel_id=1, source_target_pairs={{0,2},{1,3},{2,0},{3,1},{4,6},{5,7},{6,4},{7,5},{8,10},{9,11},{10,... | collective-permute-start | bytes 430088 | tf_op jit(solution)/shard_map/ppermute | solution.py:53
  95.4 10.2 %collective-permute-start.25 = (bf16[40,2304]{1,0:T(8,128)(2,1)S(1)}, bf16[40,2304]{1,0:T(8,128)(2,1)S(1)}, u32[]{:S(2)}, u32[]{:S(2)}) collective-permute-start(bf16[40,2304]{1,0:T(8,128)(2,1)S(1)} %fusion.39), channel_id=1, source_target_pairs={{0,8},{4,12},{8,0},{12,4},{1,9},{5,13},{9,1},{13,5},{2,10},{6,14},... | collective-permute-start | bytes 552968 | tf_op jit(solution)/shard_map/ppermute | solution.py:53
  95.6 11.3 %collective-permute-start.24 = (bf16[2,40,1280]{2,1,0:T(8,128)(2,1)S(1)}, bf16[2,40,1280]{2,1,0:T(8,128)(2,1)S(1)}, u32[]{:S(2)}, u32[]{:S(2)}) collective-permute-start(bf16[2,40,1280]{2,1,0:T(8,128)(2,1)S(1)} %pad_maximum_fusion.17), channel_id=1, source_target_pairs={{0,2},{1,3},{2,0},{3,1},{4,6},{5,7},{6,4},{7,5},{8,10},{9,11},{10,... | collective-permute-start | bytes 614408 | tf_op jit(solution)/shard_map/ppermute | solution.py:53
  99.6 8.9 %collective-permute-start.26 = (bf16[80,1792]{1,0:T(8,128)(2,1)S(1)}, bf16[80,1792]{1,0:T(8,128)(2,1)S(1)}, u32[]{:S(2)}, u32[]{:S(2)}) collective-permute-start(bf16[80,1792]{1,0:T(8,128)(2,1)S(1)} %pad_maximum_fusion.16), channel_id=1, source_target_pairs={{0,4},{1,0},{2,6},{3,2},{4,5},{5,1},{6,7},{7,3},{8,12},{9,8},{10,1... | collective-permute-start | bytes 860168 | tf_op jit(solution)/shard_map/ppermute | solution.py:130
  100.3 8.3 %collective-permute-start.27 = (bf16[80,1792]{1,0:T(8,128)(2,1)S(1)}, bf16[80,1792]{1,0:T(8,128)(2,1)S(1)}, u32[]{:S(2)}, u32[]{:S(2)}) collective-permute-start(bf16[80,1792]{1,0:T(8,128)(2,1)S(1)} %pad_maximum_fusion.16), channel_id=1, source_target_pairs={{1,4},{3,6},{4,1},{6,3},{9,12},{11,14},{12,9},{14,11},{17,20},{19,... | collective-permute-start | bytes 860168 | tf_op jit(solution)/shard_map/ppermute | solution.py:130
  105.7 6.0 %collective-permute-start.28 = (bf16[40,2304]{1,0:T(8,128)(2,1)S(1)}, bf16[40,2304]{1,0:T(8,128)(2,1)S(1)}, u32[]{:S(2)}, u32[]{:S(2)}) collective-permute-start(bf16[40,2304]{1,0:T(8,128)(2,1)S(1)} %get-tuple-element.92), channel_id=1, source_target_pairs={{0,2},{1,3},{2,0},{3,1},{4,6},{5,7},{6,4},{7,5},{8,10},{9,11},{10,... | collective-permute-start | bytes 552968 | tf_op jit(solution)/shard_map/ppermute | solution.py:53
  107.0 7.1 %collective-permute-start.30 = (bf16[40,1280]{1,0:T(8,128)(2,1)S(1)}, bf16[40,1280]{1,0:T(8,128)(2,1)S(1)}, u32[]{:S(2)}, u32[]{:S(2)}) collective-permute-start(bf16[40,1280]{1,0:T(8,128)(2,1)S(1)} %fusion.51), channel_id=1, source_target_pairs={{0,8},{4,12},{8,0},{12,4},{1,9},{5,13},{9,1},{13,5},{2,10},{6,14},... | collective-permute-start | bytes 307208 | tf_op jit(solution)/shard_map/ppermute | solution.py:53
  111.7 7.5 %collective-permute-start.32 = (bf16[80,2304]{1,0:T(8,128)(2,1)S(1)}, bf16[80,2304]{1,0:T(8,128)(2,1)S(1)}, u32[]{:S(2)}, u32[]{:S(2)}) collective-permute-start(bf16[80,2304]{1,0:T(8,128)(2,1)S(1)} %pad_maximum_fusion.10), channel_id=1, source_target_pairs={{0,4},{1,0},{2,6},{3,2},{4,5},{5,1},{6,7},{7,3},{8,12},{9,8},{10,1... | collective-permute-start | bytes 1105928 | tf_op jit(solution)/shard_map/ppermute | solution.py:130
  112.0 7.2 %collective-permute-start.33 = (bf16[80,2304]{1,0:T(8,128)(2,1)S(1)}, bf16[80,2304]{1,0:T(8,128)(2,1)S(1)}, u32[]{:S(2)}, u32[]{:S(2)}) collective-permute-start(bf16[80,2304]{1,0:T(8,128)(2,1)S(1)} %pad_maximum_fusion.10), channel_id=1, source_target_pairs={{1,4},{3,6},{4,1},{6,3},{9,12},{11,14},{12,9},{14,11},{17,20},{19,... | collective-permute-start | bytes 1105928 | tf_op jit(solution)/shard_map/ppermute | solution.py:130
  114.2 6.8 %collective-permute-start.31 = (bf16[40,1280]{1,0:T(8,128)(2,1)S(1)}, bf16[40,1280]{1,0:T(8,128)(2,1)S(1)}, u32[]{:S(2)}, u32[]{:S(2)}) collective-permute-start(bf16[40,1280]{1,0:T(8,128)(2,1)S(1)} %get-tuple-element.116), channel_id=1, source_target_pairs={{0,2},{1,3},{2,0},{3,1},{4,6},{5,7},{6,4},{7,5},{8,10},{9,11},{10,... | collective-permute-start | bytes 307208 | tf_op jit(solution)/shard_map/ppermute | solution.py:53
  115.5 10.6 %collective-permute-start.29 = (bf16[80,2048]{1,0:T(8,128)(2,1)S(1)}, bf16[80,2048]{1,0:T(8,128)(2,1)S(1)}, u32[]{:S(2)}, u32[]{:S(2)}) collective-permute-start(bf16[80,2048]{1,0:T(8,128)(2,1)S(1)} %slice.504), channel_id=1, source_target_pairs={{0,1},{1,0},{2,3},{3,2},{4,5},{5,4},{6,7},{7,6},{8,9},{9,8},{10,11... | collective-permute-start | bytes 983048 | tf_op jit(solution)/shard_map/ppermute | solution.py:53
  121.0 8.4 %collective-permute-start.35 = (bf16[80,1280]{1,0:T(8,128)(2,1)S(1)}, bf16[80,1280]{1,0:T(8,128)(2,1)S(1)}, u32[]{:S(2)}, u32[]{:S(2)}) collective-permute-start(bf16[80,1280]{1,0:T(8,128)(2,1)S(1)} %pad_maximum_fusion.18), channel_id=1, source_target_pairs={{0,4},{1,0},{2,6},{3,2},{4,5},{5,1},{6,7},{7,3},{8,12},{9,8},{10,1... | collective-permute-start | bytes 614408 | tf_op jit(solution)/shard_map/ppermute | solution.py:130
  125.4 4.1 %collective-permute-start.36 = (bf16[80,1280]{1,0:T(8,128)(2,1)S(1)}, bf16[80,1280]{1,0:T(8,128)(2,1)S(1)}, u32[]{:S(2)}, u32[]{:S(2)}) collective-permute-start(bf16[80,1280]{1,0:T(8,128)(2,1)S(1)} %pad_maximum_fusion.18), channel_id=1, source_target_pairs={{1,4},{3,6},{4,1},{6,3},{9,12},{11,14},{12,9},{14,11},{17,20},{19,... | collective-permute-start | bytes 614408 | tf_op jit(solution)/shard_map/ppermute | solution.py:130
  126.1 10.3 %collective-permute-start.34 = (bf16[80,2048]{1,0:T(8,128)(2,1)S(1)}, bf16[80,2048]{1,0:T(8,128)(2,1)S(1)}, u32[]{:S(2)}, u32[]{:S(2)}) collective-permute-start(bf16[80,2048]{1,0:T(8,128)(2,1)S(1)} %get-tuple-element.77), channel_id=1, source_target_pairs={{0,2},{1,3},{2,0},{3,1},{4,6},{5,7},{6,4},{7,5},{8,10},{9,11},{10,... | collective-permute-start | bytes 983048 | tf_op jit(solution)/shard_map/ppermute | solution.py:53
  130.8 5.7 %collective-permute-start.37 = (bf16[80,2048]{1,0:T(8,128)(2,1)S(1)}, bf16[80,2048]{1,0:T(8,128)(2,1)S(1)}, u32[]{:S(2)}, u32[]{:S(2)}) collective-permute-start(bf16[80,2048]{1,0:T(8,128)(2,1)S(1)} %slice.503), channel_id=1, source_target_pairs={{0,1},{1,0},{2,3},{3,2},{4,5},{5,4},{6,7},{7,6},{8,9},{9,8},{10,11... | collective-permute-start | bytes 983048 | tf_op jit(solution)/shard_map/ppermute | solution.py:53
  136.6 9.8 %collective-permute-start.38 = (bf16[80,2048]{1,0:T(8,128)(2,1)S(1)}, bf16[80,2048]{1,0:T(8,128)(2,1)S(1)}, u32[]{:S(2)}, u32[]{:S(2)}) collective-permute-start(bf16[80,2048]{1,0:T(8,128)(2,1)S(1)} %fusion.35), channel_id=1, source_target_pairs={{0,2},{1,3},{2,0},{3,1},{4,6},{5,7},{6,4},{7,5},{8,10},{9,11},{10,... | collective-permute-start | bytes 983048 | tf_op jit(solution)/shard_map/ppermute | solution.py:53
  137.9 9.6 %collective-permute-start.39 = (bf16[80,2048]{1,0:T(8,128)(2,1)S(1)}, bf16[80,2048]{1,0:T(8,128)(2,1)S(1)}, u32[]{:S(2)}, u32[]{:S(2)}) collective-permute-start(bf16[80,2048]{1,0:T(8,128)(2,1)S(1)} %get-tuple-element.73), channel_id=1, source_target_pairs={{0,1},{1,0},{2,3},{3,2},{4,5},{5,4},{6,7},{7,6},{8,9},{9,8},{10,11... | collective-permute-start | bytes 983048 | tf_op jit(solution)/shard_map/ppermute | solution.py:53
  146.5 1.7 %collective-permute-start.40 = (bf16[80,2048]{1,0:T(8,128)(2,1)S(1)}, bf16[80,2048]{1,0:T(8,128)(2,1)S(1)}, u32[]{:S(2)}, u32[]{:S(2)}) collective-permute-start(bf16[80,2048]{1,0:T(8,128)(2,1)S(1)} %get-tuple-element.75), channel_id=1, source_target_pairs={{0,1},{1,0},{2,3},{3,2},{4,5},{5,4},{6,7},{7,6},{8,9},{9,8},{10,11... | collective-permute-start | bytes 983048 | tf_op jit(solution)/shard_map/ppermute | solution.py:53

commit v19 on v18

--- a/solution.py
+++ b/solution.py
@@ -41,6 +41,8 @@
     "c11.cores": ["b0.total"],
     "c11.down": ["b0.total"],
     "b1.total": ["c11.down"],
+    "d.pull": ["c00.hidden"],
+    "c00.halves": ["d.pull"],
 }
 
 
@@ -53,12 +55,14 @@
     return lax.ppermute(value, axis, [(i, i ^ bit) for i in range(count)])
 
 
-def pull_kernel(first, end, tick_ref, gate_ref, up_ref, gate_here, up_here, sems):
+def pull_kernel(first, end, tick_ref, *refs):
     del tick_ref
+    *refs, sems = refs
+    count = len(refs) // 2
     columns = pl.ds(first, end - first)
     copies = [
         pltpu.make_async_copy(source.at[:, columns], here, sems.at[i])
-        for i, (source, here) in enumerate(((gate_ref, gate_here), (up_ref, up_here)))
+        for i, (source, here) in enumerate(zip(refs[:count], refs[count:]))
     ]
     for copy in copies:
         copy.start()
@@ -66,25 +70,20 @@
         copy.wait()
 
 
-def pull(gate_weight, up_weight, first, end, tick):
+def pull(weights, first, end, tick):
     far = pl.BlockSpec(memory_space=pltpu.HBM)
     near = pl.BlockSpec(memory_space=pltpu.VMEM)
-    here = pltpu.VMEM((gate_weight.shape[0], end - first), gate_weight.dtype)
+    here = [pltpu.VMEM((weight.shape[0], end - first), weight.dtype) for weight in weights]
+    size = sum(2 * weight.shape[0] * (end - first) for weight in weights)
     return pl.pallas_call(
         functools.partial(pull_kernel, first, end),
-        in_specs=[pl.BlockSpec(memory_space=pltpu.SMEM), far, far],
-        out_specs=[near, near],
-        out_shape=[here, here],
-        scratch_shapes=[pltpu.SemaphoreType.DMA((2,))],
-        compiler_params=pltpu.CompilerParams(
-            vmem_limit_bytes=4 * gate_weight.shape[0] * (end - first) + 2**20
-        ),
+        in_specs=[pl.BlockSpec(memory_space=pltpu.SMEM)] + [far] * len(weights),
+        out_specs=[near] * len(weights),
+        out_shape=here,
+        scratch_shapes=[pltpu.SemaphoreType.DMA((len(weights),))],
+        compiler_params=pltpu.CompilerParams(vmem_limit_bytes=size + 2**20),
         cost_estimate=pl.CostEstimate(flops=0, bytes_accessed=0, transcendentals=0),
-    )(
-        tick,
-        pltpu.with_memory_space_constraint(gate_weight, pltpu.HBM),
-        pltpu.with_memory_space_constraint(up_weight, pltpu.HBM),
-    )
+    )(tick, *[pltpu.with_memory_space_constraint(weight, pltpu.HBM) for weight in weights])
 
 
 def stationary(tokens, lengths, gate_weight, up_weight, down_weight):
@@ -188,12 +187,12 @@
         yield
         return issued(name + ".add", ordered(name + ".add", rows[:piece]) + got)
 
-    pulled = []
-
-    def pull_steps():
-        tick = ordered("w.pull", lengths)
-        pulled.extend(pull(gate_weight, up_weight, *spans[0][0], tick))
-        issued("w.pull", pulled[0])
+    pulled = {}
+
+    def pull_steps(name, weights, first, end):
+        tick = ordered(name + ".pull", lengths)
+        pulled[name] = pull(weights, first, end, tick)
+        issued(name + ".pull", pulled[name][0])
         return None
         yield
 
@@ -207,7 +206,7 @@
         full = ordered(name + ".dots", full)
         if (h, i) == (0, 0):
             result("w")
-            gate, up = dot(full, pulled[0]), dot(full, pulled[1])
+            gate, up = (dot(full, weight) for weight in pulled["w"])
         else:
             gate, up = dot(full, gate_weight[:, part]), dot(full, up_weight[:, part])
         send = issued(name + ".dots", jnp.stack([gate[half:], up[half:]]).astype(jnp.bfloat16))
@@ -223,8 +222,9 @@
         hidden = issued(name + ".hidden", (jax.nn.silu(gate) * up).astype(jnp.bfloat16))
         whole = yield from spread_steps(name, hidden)
         yield
+        result("d")
         whole = ordered(name + ".down", whole)
-        return issued(name + ".down", dot(whole, down_weight[part]))
+        return issued(name + ".down", dot(whole, pulled["d"][0][part]))
 
     def branch_steps(name, h):
         parts = [result("c" + str(h) + str(i)) for i in range(len(spans[h]))]
@@ -237,7 +237,10 @@
         got = ordered(name + ".all", got)
         return issued(name + ".all", total + jnp.concatenate([got[piece:], got[:piece]], axis=0))
 
-    chains = {"w": pull_steps()}
+    chains = {
+        "w": pull_steps("w", (gate_weight, up_weight), *spans[0][0]),
+        "d": pull_steps("d", (down_weight,), 0, down_weight.shape[1]),
+    }
     results = {}
     for h in range(HALVES):
         chains["t" + str(h)] = half_steps("t" + str(h), h)

time: 151 us -> 152 us (level)
  Pallas kernels: 5.84 us -> 11.6 us
  starting transfers between devices: 42 us -> 36.9 us
    pallas_call x1 -> x2, Pallas kernels: 5.84 us -> 11.6 us  [pull(): pl.pallas_call(functools.partial(pull_kernel, first, end), in_specs=[pl.B...]
    ppermute x29, starting transfers between devices: 30.7 us -> 26 us  [flip(): return lax.ppermute(value, axis, [(i, i ^ bit) for i in range(count)])]
  transfers between devices with their start and end apart: 41 -> 41, of which waited for: 17 -> 16; matrix products, arithmetic and copies ran while one was open for 23% -> 23% of each run, Pallas kernels for 4% -> 8%
where the time goes in v19:
time: 152 us; the launch traced here: 151 us
  waiting for transfers between devices  61.7 us (41%)
  starting transfers between devices  36.9 us (24%)
  matrix products  33.7 us (22%)
  Pallas kernels  11.6 us (8%)
  other arithmetic  5.07 us (3%)
  local copies, waits for them, and re-layouts  1.62 us (1%)
    ppermute x29, waiting for transfers between devices, flip(): return lax.ppermute(value, axis, [(i, i ^ bit) for i in range(count)])  56 us
    dot_general x17, matrix products, dot(): return jnp.dot(a, b, preferred_element_type=jnp.float32)  32.9 us
    ppermute x29, starting transfers between devices, flip(): return lax.ppermute(value, axis, [(i, i ^ bit) for i in range(count)])  26 us
    pallas_call x2, Pallas kernels, pull(): pl.pallas_call(functools.partial(pull_kernel, first, end), in_specs=[pl.B...  11.6 us
    ppermute x12, starting transfers between devices, move(): return lax.ppermute(value, ('row', 'col'), pairs)  10.9 us
    ppermute x12, waiting for transfers between devices, move(): return lax.ppermute(value, ('row', 'col'), pairs)  5.68 us
  transfers between devices with their start and end apart: 41, of which 16 were waited for; matrix products, arithmetic and copies ran while one was open for 23% of the time, Pallas kernels for 8%

profile of v19, /device:TPU:0, one launch (start us, length us, event | category | flops | bytes accessed | tf_op | source)
XLA Modules:
  0.0 151.4 jit_solution(4166216403054648486)
XLA Ops:
  0.0 0.5 collective-permute-start
  0.5 0.9 fusion.80
  1.5 1.4 fusion.70
  3.2 2.6 %collective-permute-start.1 = (bf16[40,2048]{1,0:T(8,128)(2,1)S(1)}, bf16[40,2048]{1,0:T(8,128)(2,1)S(1)}, u32[]{:S(2)}, u32[]{:S(2)}) collective-permute-start(bf16[40,2048]{1,0:T(8,128)(2,1)S(1)} %slice.314), channel_id=1, source_target_pairs={{0,2},{1,3},{2,0},{3,1},{4,6},{5,7},{6,4},{7,5},{8,10},{9,11},{10,... | collective-permute-start | bytes 491528 | tf_op jit(solution)/shard_map/ppermute | solution.py:55
  5.8 4.9 %collective-permute-done.1 = bf16[40,2048]{1,0:T(8,128)(2,1)S(1)} collective-permute-done((bf16[40,2048]{1,0:T(8,128)(2,1)S(1)}, bf16[40,2048]{1,0:T(8,128)(2,1)S(1)}, u32[]{:S(2)}, u32[]{:S(2)}) %collective-permute-start.1) | collective-permute-done | bytes 163872 | tf_op jit(solution)/shard_map/ppermute | solution.py:55
  10.7 2.9 %collective-permute-start.2 = (bf16[40,2048]{1,0:T(8,128)(2,1)S(1)}, bf16[40,2048]{1,0:T(8,128)(2,1)S(1)}, u32[]{:S(2)}, u32[]{:S(2)}) collective-permute-start(bf16[40,2048]{1,0:T(8,128)(2,1)S(1)} %slice_add_fusion.19), channel_id=1, source_target_pairs={{0,8},{4,12},{8,0},{12,4},{1,9},{5,13},{9,1},{13,5},{2,10},{6,14},... | collective-permute-start | bytes 491528 | tf_op jit(solution)/shard_map/ppermute | solution.py:55
  14.2 1.6 %collective-permute-start.6 = (bf16[40,2048]{1,0:T(8,128)(2,1)S(1)}, bf16[40,2048]{1,0:T(8,128)(2,1)S(1)}, u32[]{:S(2)}, u32[]{:S(2)}) collective-permute-start(bf16[40,2048]{1,0:T(8,128)(2,1)S(1)} %slice.316), channel_id=1, source_target_pairs={{0,2},{1,3},{2,0},{3,1},{4,6},{5,7},{6,4},{7,5},{8,10},{9,11},{10,... | collective-permute-start | bytes 491528 | tf_op jit(solution)/shard_map/ppermute | solution.py:55
  15.8 5.4 %collective-permute-done.2 = bf16[40,2048]{1,0:T(8,128)(2,1)S(1)} collective-permute-done((bf16[40,2048]{1,0:T(8,128)(2,1)S(1)}, bf16[40,2048]{1,0:T(8,128)(2,1)S(1)}, u32[]{:S(2)}, u32[]{:S(2)}) %collective-permute-start.2) | collective-permute-done | bytes 163872 | tf_op jit(solution)/shard_map/ppermute | solution.py:55
  21.2 1.6 %collective-permute-start.3 = (bf16[40,2048]{1,0:T(8,128)(2,1)S(1)}, bf16[40,2048]{1,0:T(8,128)(2,1)S(1)}, u32[]{:S(2)}, u32[]{:S(2)}) collective-permute-start(bf16[40,2048]{1,0:T(8,128)(2,1)S(1)} %get-tuple-element.108), channel_id=1, source_target_pairs={{0,2},{1,3},{2,0},{3,1},{4,6},{5,7},{6,4},{7,5},{8,10},{9,11},{10,... | collective-permute-start | bytes 491528 | tf_op jit(solution)/shard_map/ppermute | solution.py:55
  22.9 3.7 %collective-permute-done.3 = bf16[40,2048]{1,0:T(8,128)(2,1)S(1)} collective-permute-done((bf16[40,2048]{1,0:T(8,128)(2,1)S(1)}, bf16[40,2048]{1,0:T(8,128)(2,1)S(1)}, u32[]{:S(2)}, u32[]{:S(2)}) %collective-permute-start.3) | collective-permute-done | bytes 163872 | tf_op jit(solution)/shard_map/ppermute | solution.py:55
  26.6 1.6 %collective-permute-start.4 = (bf16[80,2048]{1,0:T(8,128)(2,1)S(1)}, bf16[80,2048]{1,0:T(8,128)(2,1)S(1)}, u32[]{:S(2)}, u32[]{:S(2)}) collective-permute-start(bf16[80,2048]{1,0:T(8,128)(2,1)S(1)} %pad_maximum_fusion.11), channel_id=1, source_target_pairs={{0,4},{1,0},{2,6},{3,2},{4,5},{5,1},{6,7},{7,3},{8,12},{9,8},{10,1... | collective-permute-start | bytes 983048 | tf_op jit(solution)/shard_map/ppermute | solution.py:129
  28.2 0.7 collective-permute-start.5
  28.9 3.5 %collective-permute-done.7 = bf16[40,2048]{1,0:T(8,128)(2,1)S(1)} collective-permute-done((bf16[40,2048]{1,0:T(8,128)(2,1)S(1)}, bf16[40,2048]{1,0:T(8,128)(2,1)S(1)}, u32[]{:S(2)}, u32[]{:S(2)}) %collective-permute-start.7) | collective-permute-done | bytes 163872 | tf_op jit(solution)/shard_map/ppermute | solution.py:55
  32.4 0.6 collective-permute-start.8
  33.0 5.8 %shard_map.55 = (bf16[2048,1792]{1,0:T(8,128)(2,1)S(1)}, bf16[2048,1792]{1,0:T(8,128)(2,1)S(1)}) custom-call(s32[4]{0:T(128)S(1)} %copy-done, bf16[2048,3584]{1,0:T(8,128)(2,1)} %refs_0_.2, bf16[2048,3584]{1,0:T(8,128)(2,1)} %refs_1_.1), custom_call_target="tpu_custom_call" | custom-call | tf_op jit(solution)/shard_map/pallas_call | solution.py:78
  39.0 1.4 fusion.93
  40.4 1.4 fusion.94
  41.9 1.0 copy-done.2
  43.2 0.9 collective-permute-start.12
  44.1 1.1 collective-permute-done.9
  45.2 1.3 slice_add_fusion.7
  46.7 4.6 %fusion.12 = f32[160,1792]{1,0:T(8,128)S(1)} fusion(bf16[160,2048]{1,0:T(8,128)(2,1)S(1)} %pad_maximum_fusion.1, bf16[2048,3584]{1,0:T(8,128)(2,1)} %refs_0_.2), kind=kOutput, calls=%fused_computation.12 | convolution fusion | flops 1174405120 | bytes 9142272 | tf_op jit(solution)/shard_map/dot_general | solution.py:50
  51.3 4.6 %fusion.10 = f32[160,1792]{1,0:T(8,128)S(1)} fusion(bf16[160,2048]{1,0:T(8,128)(2,1)S(1)} %pad_maximum_fusion.1, bf16[2048,3584]{1,0:T(8,128)(2,1)} %refs_1_.1), kind=kOutput, calls=%fused_computation.10 | convolution fusion | flops 1174405120 | bytes 9142272 | tf_op jit(solution)/shard_map/dot_general | solution.py:50
  56.1 0.7 collective-permute-start.13
  56.9 1.6 %collective-permute-start.10 = (bf16[2,40,1792]{2,1,0:T(8,128)(2,1)S(1)}, bf16[2,40,1792]{2,1,0:T(8,128)(2,1)S(1)}, u32[]{:S(2)}, u32[]{:S(2)}) collective-permute-start(bf16[2,40,1792]{2,1,0:T(8,128)(2,1)S(1)} %pad_maximum_fusion.13), channel_id=1, source_target_pairs={{0,2},{1,3},{2,0},{3,1},{4,6},{5,7},{6,4},{7,5},{8,10},{9,11},{10,... | collective-permute-start | bytes 860168 | tf_op jit(solution)/shard_map/ppermute | solution.py:55
  58.7 1.7 %fusion.4 = f32[160,2304]{1,0:T(8,128)S(1)} fusion(bf16[160,2048]{1,0:T(8,128)(2,1)S(1)} %pad_maximum_fusion.2, bf16[2048,3584]{1,0:T(8,128)(2,1)S(1)} %bitcast.108), kind=kOutput, calls=%fused_computation.4 | convolution fusion | flops 1509949440 | bytes 11567104 | tf_op jit(solution)/shard_map/dot_general | solution.py:50
  60.4 5.4 %fusion.2 = f32[160,2304]{1,0:T(8,128)S(1)} fusion(bf16[160,2048]{1,0:T(8,128)(2,1)S(1)} %pad_maximum_fusion.2, bf16[2048,3584]{1,0:T(8,128)(2,1)} %refs_1_.1), kind=kOutput, calls=%fused_computation.2 | convolution fusion | flops 1509949440 | bytes 11567104 | tf_op jit(solution)/shard_map/dot_general | solution.py:50
  66.0 1.0 fusion.18
  67.1 3.5 %fusion.16 = f32[160,1280]{1,0:T(8,128)S(1)} fusion(bf16[160,2048]{1,0:T(8,128)(2,1)S(1)} %pad_maximum_fusion.2, bf16[2048,3584]{1,0:T(8,128)(2,1)} %refs_1_.1), kind=kOutput, calls=%fused_computation.16 | convolution fusion | flops 838860800 | bytes 6717440 | tf_op jit(solution)/shard_map/dot_general | solution.py:50
  70.6 0.4 collective-permute-start.17
  71.2 3.4 %collective-permute-start.14 = (bf16[40,1792]{1,0:T(8,128)(2,1)S(1)}, bf16[40,1792]{1,0:T(8,128)(2,1)S(1)}, u32[]{:S(2)}, u32[]{:S(2)}) collective-permute-start(bf16[40,1792]{1,0:T(8,128)(2,1)S(1)} %fusion.47), channel_id=1, source_target_pairs={{0,8},{4,12},{8,0},{12,4},{1,9},{5,13},{9,1},{13,5},{2,10},{6,14},... | collective-permute-start | bytes 430088 | tf_op jit(solution)/shard_map/ppermute | solution.py:55
  74.8 1.5 collective-permute-start.16
  76.3 5.7 %shard_map.56 = bf16[3584,2048]{1,0:T(8,128)(2,1)S(1)} custom-call(s32[4]{0:T(128)S(1)} %copy-done, bf16[3584,2048]{1,0:T(8,128)(2,1)} %refs_0_.3), custom_call_target="tpu_custom_call" | custom-call | tf_op jit(solution)/shard_map/pallas_call | solution.py:78
  82.1 1.3 collective-permute-start.15
  83.6 0.9 collective-permute-start.21
  84.7 4.0 %collective-permute-done.15 = bf16[40,1792]{1,0:T(8,128)(2,1)S(1)} collective-permute-done((bf16[40,1792]{1,0:T(8,128)(2,1)S(1)}, bf16[40,1792]{1,0:T(8,128)(2,1)S(1)}, u32[]{:S(2)}, u32[]{:S(2)}) %collective-permute-start.15) | collective-permute-done | bytes 143392 | tf_op jit(solution)/shard_map/ppermute | solution.py:55
  88.8 0.7 collective-permute-start.23
  89.5 4.3 %collective-permute-done.18 = bf16[40,1792]{1,0:T(8,128)(2,1)S(1)} collective-permute-done((bf16[40,1792]{1,0:T(8,128)(2,1)S(1)}, bf16[40,1792]{1,0:T(8,128)(2,1)S(1)}, u32[]{:S(2)}, u32[]{:S(2)}) %collective-permute-start.18) | collective-permute-done | bytes 143392 | tf_op jit(solution)/shard_map/ppermute | solution.py:55
  93.8 0.9 collective-permute-start.19
  94.7 1.5 collective-permute-done.21
  96.6 0.6 collective-permute-start.24
  97.2 2.8 %collective-permute-done.19 = bf16[40,1792]{1,0:T(8,128)(2,1)S(1)} collective-permute-done((bf16[40,1792]{1,0:T(8,128)(2,1)S(1)}, bf16[40,1792]{1,0:T(8,128)(2,1)S(1)}, u32[]{:S(2)}, u32[]{:S(2)}) %collective-permute-start.19) | collective-permute-done | bytes 143392 | tf_op jit(solution)/shard_map/ppermute | solution.py:55
  100.1 0.7 collective-permute-start.27
  100.9 6.2 %collective-permute-done.25 = bf16[40,2304]{1,0:T(8,128)(2,1)S(1)} collective-permute-done((bf16[40,2304]{1,0:T(8,128)(2,1)S(1)}, bf16[40,2304]{1,0:T(8,128)(2,1)S(1)}, u32[]{:S(2)}, u32[]{:S(2)}) %collective-permute-start.25) | collective-permute-done | bytes 184352 | tf_op jit(solution)/shard_map/ppermute | solution.py:55
  107.7 1.4 fusion.8
  109.1 4.6 %collective-permute-done.28 = bf16[40,2304]{1,0:T(8,128)(2,1)S(1)} collective-permute-done((bf16[40,2304]{1,0:T(8,128)(2,1)S(1)}, bf16[40,2304]{1,0:T(8,128)(2,1)S(1)}, u32[]{:S(2)}, u32[]{:S(2)}) %collective-permute-start.28) | collective-permute-done | bytes 184352 | tf_op jit(solution)/shard_map/ppermute | solution.py:55
  113.8 0.9 collective-permute-start.33
  114.8 1.4 fusion.91
  116.2 0.4 collective-permute-start.31
  116.6 1.5 collective-permute-start.29
  118.1 2.7 %collective-permute-done.32 = bf16[80,2304]{1,0:T(8,128)(2,1)S(1)} collective-permute-done((bf16[80,2304]{1,0:T(8,128)(2,1)S(1)}, bf16[80,2304]{1,0:T(8,128)(2,1)S(1)}, u32[]{:S(2)}, u32[]{:S(2)}) %collective-permute-start.32) | collective-permute-done | bytes 368672 | tf_op jit(solution)/shard_map/ppermute | solution.py:129
  120.9 1.8 %fusion = f32[160,2048]{1,0:T(8,128)S(1)} fusion(bf16[3584,2048]{1,0:T(8,128)(2,1)S(1)} %shard_map.56, bf16[80,2304]{1,0:T(8,128)(2,1)S(1)} %get-tuple-element.94, bf16[80,2304]{1,0:T(8,128)(2,1)S(1)} %get-tuple-element.93), kind=kOutput, calls=%fused_computation | convolution fusion | flops 1511424000 | bytes 11485184 | tf_op jit(solution)/shard_map/dot_general | solution.py:50
  122.7 4.5 %collective-permute-start.35 = (bf16[80,1280]{1,0:T(8,128)(2,1)S(1)}, bf16[80,1280]{1,0:T(8,128)(2,1)S(1)}, u32[]{:S(2)}, u32[]{:S(2)}) collective-permute-start(bf16[80,1280]{1,0:T(8,128)(2,1)S(1)} %pad_maximum_fusion.18), channel_id=1, source_target_pairs={{0,4},{1,0},{2,6},{3,2},{4,5},{5,1},{6,7},{7,3},{8,12},{9,8},{10,1... | collective-permute-start | bytes 614408 | tf_op jit(solution)/shard_map/ppermute | solution.py:129
  127.2 0.7 collective-permute-start.36
  128.0 0.4 collective-permute-start.34
  128.4 3.0 %collective-permute-done.35 = bf16[80,1280]{1,0:T(8,128)(2,1)S(1)} collective-permute-done((bf16[80,1280]{1,0:T(8,128)(2,1)S(1)}, bf16[80,1280]{1,0:T(8,128)(2,1)S(1)}, u32[]{:S(2)}, u32[]{:S(2)}) %collective-permute-start.35) | collective-permute-done | bytes 204832 | tf_op jit(solution)/shard_map/ppermute | solution.py:129
  131.4 1.1 fusion.92
  132.6 1.7 %collective-permute-start.37 = (bf16[80,2048]{1,0:T(8,128)(2,1)S(1)}, bf16[80,2048]{1,0:T(8,128)(2,1)S(1)}, u32[]{:S(2)}, u32[]{:S(2)}) collective-permute-start(bf16[80,2048]{1,0:T(8,128)(2,1)S(1)} %slice.507), channel_id=1, source_target_pairs={{0,1},{1,0},{2,3},{3,2},{4,5},{5,4},{6,7},{7,6},{8,9},{9,8},{10,11... | collective-permute-start | bytes 983048 | tf_op jit(solution)/shard_map/ppermute | solution.py:55
  134.3 4.0 %collective-permute-done.34 = bf16[80,2048]{1,0:T(8,128)(2,1)S(1)} collective-permute-done((bf16[80,2048]{1,0:T(8,128)(2,1)S(1)}, bf16[80,2048]{1,0:T(8,128)(2,1)S(1)}, u32[]{:S(2)}, u32[]{:S(2)}) %collective-permute-start.34) | collective-permute-done | bytes 327712 | tf_op jit(solution)/shard_map/ppermute | solution.py:55
  138.5 0.4 collective-permute-start.38
  139.0 9.3 %collective-permute-done.38 = bf16[80,2048]{1,0:T(8,128)(2,1)S(1)} collective-permute-done((bf16[80,2048]{1,0:T(8,128)(2,1)S(1)}, bf16[80,2048]{1,0:T(8,128)(2,1)S(1)}, u32[]{:S(2)}, u32[]{:S(2)}) %collective-permute-start.38) | collective-permute-done | bytes 327712 | tf_op jit(solution)/shard_map/ppermute | solution.py:55
  148.6 0.8 fusion.25
  149.5 0.7 collective-permute-done.40
  150.2 1.3 fusion.22
  (131 shorter events, 5.5 us)
Async XLA Ops:
  0.0 2.9 %collective-permute-start = (bf16[160,2048]{1,0:T(8,128)(2,1)}, bf16[160,2048]{1,0:T(8,128)(2,1)S(1)}, u32[]{:S(2)}, u32[]{:S(2)}) collective-permute-start(bf16[160,2048]{1,0:T(8,128)(2,1)} %param.5), channel_id=1, source_target_pairs={{0,1},{1,0},{2,3},{3,2},{4,5},{5,4},{6,7},{7,6},{8,9},{9,8},{10,11... | collective-permute-start | bytes 1966088 | tf_op jit(solution)/shard_map/ppermute | solution.py:55
  2.9 10.7 %copy-start.1 = (bf16[160,2048]{1,0:T(8,128)(2,1)S(1)}, bf16[160,2048]{1,0:T(8,128)(2,1)}, u32[]{:S(2)}) copy-start(bf16[160,2048]{1,0:T(8,128)(2,1)} %param.5) | copy-start | bytes 1966084
  3.2 7.4 %collective-permute-start.1 = (bf16[40,2048]{1,0:T(8,128)(2,1)S(1)}, bf16[40,2048]{1,0:T(8,128)(2,1)S(1)}, u32[]{:S(2)}, u32[]{:S(2)}) collective-permute-start(bf16[40,2048]{1,0:T(8,128)(2,1)S(1)} %slice.314), channel_id=1, source_target_pairs={{0,2},{1,3},{2,0},{3,1},{4,6},{5,7},{6,4},{7,5},{8,10},{9,11},{10,... | collective-permute-start | bytes 491528 | tf_op jit(solution)/shard_map/ppermute | solution.py:55
  10.7 10.5 %collective-permute-start.2 = (bf16[40,2048]{1,0:T(8,128)(2,1)S(1)}, bf16[40,2048]{1,0:T(8,128)(2,1)S(1)}, u32[]{:S(2)}, u32[]{:S(2)}) collective-permute-start(bf16[40,2048]{1,0:T(8,128)(2,1)S(1)} %slice_add_fusion.19), channel_id=1, source_target_pairs={{0,8},{4,12},{8,0},{12,4},{1,9},{5,13},{9,1},{13,5},{2,10},{6,14},... | collective-permute-start | bytes 491528 | tf_op jit(solution)/shard_map/ppermute | solution.py:55
  14.2 18.8 %copy-start = (s32[4]{0:T(128)S(1)}, s32[4]{0:T(128)}, u32[]{:S(2)}) copy-start(s32[4]{0:T(128)} %tick_ref.1) | copy-start | bytes 52
  14.2 8.6 %collective-permute-start.6 = (bf16[40,2048]{1,0:T(8,128)(2,1)S(1)}, bf16[40,2048]{1,0:T(8,128)(2,1)S(1)}, u32[]{:S(2)}, u32[]{:S(2)}) collective-permute-start(bf16[40,2048]{1,0:T(8,128)(2,1)S(1)} %slice.316), channel_id=1, source_target_pairs={{0,2},{1,3},{2,0},{3,1},{4,6},{5,7},{6,4},{7,5},{8,10},{9,11},{10,... | collective-permute-start | bytes 491528 | tf_op jit(solution)/shard_map/ppermute | solution.py:55
  21.2 5.4 %collective-permute-start.3 = (bf16[40,2048]{1,0:T(8,128)(2,1)S(1)}, bf16[40,2048]{1,0:T(8,128)(2,1)S(1)}, u32[]{:S(2)}, u32[]{:S(2)}) collective-permute-start(bf16[40,2048]{1,0:T(8,128)(2,1)S(1)} %get-tuple-element.108), channel_id=1, source_target_pairs={{0,2},{1,3},{2,0},{3,1},{4,6},{5,7},{6,4},{7,5},{8,10},{9,11},{10,... | collective-permute-start | bytes 491528 | tf_op jit(solution)/shard_map/ppermute | solution.py:55
  22.8 9.5 %collective-permute-start.7 = (bf16[40,2048]{1,0:T(8,128)(2,1)S(1)}, bf16[40,2048]{1,0:T(8,128)(2,1)S(1)}, u32[]{:S(2)}, u32[]{:S(2)}) collective-permute-start(bf16[40,2048]{1,0:T(8,128)(2,1)S(1)} %slice_add_fusion.18), channel_id=1, source_target_pairs={{0,8},{4,12},{8,0},{12,4},{1,9},{5,13},{9,1},{13,5},{2,10},{6,14},... | collective-permute-start | bytes 491528 | tf_op jit(solution)/shard_map/ppermute | solution.py:55
  26.6 12.2 %collective-permute-start.4 = (bf16[80,2048]{1,0:T(8,128)(2,1)S(1)}, bf16[80,2048]{1,0:T(8,128)(2,1)S(1)}, u32[]{:S(2)}, u32[]{:S(2)}) collective-permute-start(bf16[80,2048]{1,0:T(8,128)(2,1)S(1)} %pad_maximum_fusion.11), channel_id=1, source_target_pairs={{0,4},{1,0},{2,6},{3,2},{4,5},{5,1},{6,7},{7,3},{8,12},{9,8},{10,1... | collective-permute-start | bytes 983048 | tf_op jit(solution)/shard_map/ppermute | solution.py:129
  28.2 10.6 %collective-permute-start.5 = (bf16[80,2048]{1,0:T(8,128)(2,1)S(1)}, bf16[80,2048]{1,0:T(8,128)(2,1)S(1)}, u32[]{:S(2)}, u32[]{:S(2)}) collective-permute-start(bf16[80,2048]{1,0:T(8,128)(2,1)S(1)} %pad_maximum_fusion.11), channel_id=1, source_target_pairs={{1,4},{3,6},{4,1},{6,3},{9,12},{11,14},{12,9},{14,11},{17,20},{19,... | collective-permute-start | bytes 983048 | tf_op jit(solution)/shard_map/ppermute | solution.py:129
  32.4 6.6 %collective-permute-start.8 = (bf16[40,2048]{1,0:T(8,128)(2,1)S(1)}, bf16[40,2048]{1,0:T(8,128)(2,1)S(1)}, u32[]{:S(2)}, u32[]{:S(2)}) collective-permute-start(bf16[40,2048]{1,0:T(8,128)(2,1)S(1)} %get-tuple-element.104), channel_id=1, source_target_pairs={{0,2},{1,3},{2,0},{3,1},{4,6},{5,7},{6,4},{7,5},{8,10},{9,11},{10,... | collective-permute-start | bytes 491528 | tf_op jit(solution)/shard_map/ppermute | solution.py:55
  41.8 1.0 copy-start.2
  43.0 2.2 %collective-permute-start.9 = (bf16[2,80,1792]{2,1,0:T(8,128)(2,1)S(1)}, bf16[2,80,1792]{2,1,0:T(8,128)(2,1)}, u32[]{:S(2)}, u32[]{:S(2)}) collective-permute-start(bf16[2,80,1792]{2,1,0:T(8,128)(2,1)S(1)} %pad_maximum_fusion.3), channel_id=1, source_target_pairs={{0,1},{1,0},{2,3},{3,2},{4,5},{5,4},{6,7},{7,6},{8,9},{9,8},{10,11... | collective-permute-start | bytes 1720328 | tf_op jit(solution)/shard_map/ppermute | solution.py:55
  43.1 13.6 %collective-permute-start.11 = (bf16[80,2048]{1,0:T(8,128)(2,1)S(1)}, bf16[80,2048]{1,0:T(8,128)(2,1)S(1)}, u32[]{:S(2)}, u32[]{:S(2)}) collective-permute-start(bf16[80,2048]{1,0:T(8,128)(2,1)S(1)} %pad_maximum_fusion.12), channel_id=1, source_target_pairs={{0,4},{1,0},{2,6},{3,2},{4,5},{5,1},{6,7},{7,3},{8,12},{9,8},{10,1... | collective-permute-start | bytes 983048 | tf_op jit(solution)/shard_map/ppermute | solution.py:129
  43.2 13.5 %collective-permute-start.12 = (bf16[80,2048]{1,0:T(8,128)(2,1)S(1)}, bf16[80,2048]{1,0:T(8,128)(2,1)S(1)}, u32[]{:S(2)}, u32[]{:S(2)}) collective-permute-start(bf16[80,2048]{1,0:T(8,128)(2,1)S(1)} %pad_maximum_fusion.12), channel_id=1, source_target_pairs={{1,4},{3,6},{4,1},{6,3},{9,12},{11,14},{12,9},{14,11},{17,20},{19,... | collective-permute-start | bytes 983048 | tf_op jit(solution)/shard_map/ppermute | solution.py:129
  46.6 12.0 %slice-start = ((s8[14680064]{0:T(1024)(128)(4,1)}), s8[4194304]{0:T(1024)(128)(4,1)S(1)}, s32[]{:S(2)}) async-start(s8[14680064]{0:T(1024)(128)(4,1)} %bitcast.107), calls=%async_computation | async-start | bytes 8388608
  46.7 12.0 %slice-start.1 = ((s8[14680064]{0:T(1024)(128)(4,1)}), s8[4194304]{0:T(1024)(128)(4,1)S(1)}, s32[]{:S(2)}) async-start(s8[14680064]{0:T(1024)(128)(4,1)} %bitcast.107), calls=%async_computation.1 | async-start | bytes 8388608
  51.3 7.4 %slice-start.2 = ((s8[14680064]{0:T(1024)(128)(4,1)}), s8[4194304]{0:T(1024)(128)(4,1)S(1)}, s32[]{:S(2)}) async-start(s8[14680064]{0:T(1024)(128)(4,1)} %bitcast.107), calls=%async_computation.2 | async-start | bytes 8388608
  56.0 2.7 %slice-start.3 = ((s8[14680064]{0:T(1024)(128)(4,1)}), s8[2097152]{0:T(1024)(128)(4,1)S(1)}, s32[]{:S(2)}) async-start(s8[14680064]{0:T(1024)(128)(4,1)} %bitcast.107), calls=%async_computation.3 | async-start | bytes 4194304
  56.1 2.4 %collective-permute-start.13 = (bf16[2,80,1792]{2,1,0:T(8,128)(2,1)S(1)}, bf16[2,80,1792]{2,1,0:T(8,128)(2,1)S(1)}, u32[]{:S(2)}, u32[]{:S(2)}) collective-permute-start(bf16[2,80,1792]{2,1,0:T(8,128)(2,1)S(1)} %pad_maximum_fusion.4), channel_id=1, source_target_pairs={{0,1},{1,0},{2,3},{3,2},{4,5},{5,4},{6,7},{7,6},{8,9},{9,8},{10,11... | collective-permute-start | bytes 1720328 | tf_op jit(solution)/shard_map/ppermute | solution.py:55
  56.9 14.2 %collective-permute-start.10 = (bf16[2,40,1792]{2,1,0:T(8,128)(2,1)S(1)}, bf16[2,40,1792]{2,1,0:T(8,128)(2,1)S(1)}, u32[]{:S(2)}, u32[]{:S(2)}) collective-permute-start(bf16[2,40,1792]{2,1,0:T(8,128)(2,1)S(1)} %pad_maximum_fusion.13), channel_id=1, source_target_pairs={{0,2},{1,3},{2,0},{3,1},{4,6},{5,7},{6,4},{7,5},{8,10},{9,11},{10,... | collective-permute-start | bytes 860168 | tf_op jit(solution)/shard_map/ppermute | solution.py:55
  70.6 12.8 %collective-permute-start.17 = (bf16[2,80,2304]{2,1,0:T(8,128)(2,1)S(1)}, bf16[2,80,2304]{2,1,0:T(8,128)(2,1)S(1)}, u32[]{:S(2)}, u32[]{:S(2)}) collective-permute-start(bf16[2,80,2304]{2,1,0:T(8,128)(2,1)S(1)} %pad_maximum_fusion), channel_id=1, source_target_pairs={{0,1},{1,0},{2,3},{3,2},{4,5},{5,4},{6,7},{7,6},{8,9},{9,8},{10,11... | collective-permute-start | bytes 2211848 | tf_op jit(solution)/shard_map/ppermute | solution.py:55
  71.2 10.8 %collective-permute-start.14 = (bf16[40,1792]{1,0:T(8,128)(2,1)S(1)}, bf16[40,1792]{1,0:T(8,128)(2,1)S(1)}, u32[]{:S(2)}, u32[]{:S(2)}) collective-permute-start(bf16[40,1792]{1,0:T(8,128)(2,1)S(1)} %fusion.47), channel_id=1, source_target_pairs={{0,8},{4,12},{8,0},{12,4},{1,9},{5,13},{9,1},{13,5},{2,10},{6,14},... | collective-permute-start | bytes 430088 | tf_op jit(solution)/shard_map/ppermute | solution.py:55
  74.8 9.7 %collective-permute-start.16 = (bf16[2,40,1792]{2,1,0:T(8,128)(2,1)S(1)}, bf16[2,40,1792]{2,1,0:T(8,128)(2,1)S(1)}, u32[]{:S(2)}, u32[]{:S(2)}) collective-permute-start(bf16[2,40,1792]{2,1,0:T(8,128)(2,1)S(1)} %pad_maximum_fusion.14), channel_id=1, source_target_pairs={{0,2},{1,3},{2,0},{3,1},{4,6},{5,7},{6,4},{7,5},{8,10},{9,11},{10,... | collective-permute-start | bytes 860168 | tf_op jit(solution)/shard_map/ppermute | solution.py:55
  76.3 20.1 %collective-permute-start.20 = (bf16[2,80,1280]{2,1,0:T(8,128)(2,1)S(1)}, bf16[2,80,1280]{2,1,0:T(8,128)(2,1)S(1)}, u32[]{:S(2)}, u32[]{:S(2)}) collective-permute-start(bf16[2,80,1280]{2,1,0:T(8,128)(2,1)S(1)} %pad_maximum_fusion.7), channel_id=1, source_target_pairs={{0,1},{1,0},{2,3},{3,2},{4,5},{5,4},{6,7},{7,6},{8,9},{9,8},{10,11... | collective-permute-start | bytes 1228808 | tf_op jit(solution)/shard_map/ppermute | solution.py:55
  82.1 6.6 %collective-permute-start.15 = (bf16[40,1792]{1,0:T(8,128)(2,1)S(1)}, bf16[40,1792]{1,0:T(8,128)(2,1)S(1)}, u32[]{:S(2)}, u32[]{:S(2)}) collective-permute-start(bf16[40,1792]{1,0:T(8,128)(2,1)S(1)} %get-tuple-element.116), channel_id=1, source_target_pairs={{0,2},{1,3},{2,0},{3,1},{4,6},{5,7},{6,4},{7,5},{8,10},{9,11},{10,... | collective-permute-start | bytes 430088 | tf_op jit(solution)/shard_map/ppermute | solution.py:55
  83.6 12.6 %collective-permute-start.21 = (bf16[2,40,2304]{2,1,0:T(8,128)(2,1)S(1)}, bf16[2,40,2304]{2,1,0:T(8,128)(2,1)S(1)}, u32[]{:S(2)}, u32[]{:S(2)}) collective-permute-start(bf16[2,40,2304]{2,1,0:T(8,128)(2,1)S(1)} %pad_maximum_fusion.9), channel_id=1, source_target_pairs={{0,2},{1,3},{2,0},{3,1},{4,6},{5,7},{6,4},{7,5},{8,10},{9,11},{10,... | collective-permute-start | bytes 1105928 | tf_op jit(solution)/shard_map/ppermute | solution.py:55
  84.6 9.2 %collective-permute-start.18 = (bf16[40,1792]{1,0:T(8,128)(2,1)S(1)}, bf16[40,1792]{1,0:T(8,128)(2,1)S(1)}, u32[]{:S(2)}, u32[]{:S(2)}) collective-permute-start(bf16[40,1792]{1,0:T(8,128)(2,1)S(1)} %fusion.45), channel_id=1, source_target_pairs={{0,8},{4,12},{8,0},{12,4},{1,9},{5,13},{9,1},{13,5},{2,10},{6,14},... | collective-permute-start | bytes 430088 | tf_op jit(solution)/shard_map/ppermute | solution.py:55
  88.7 11.4 %collective-permute-start.22 = (bf16[80,1792]{1,0:T(8,128)(2,1)S(1)}, bf16[80,1792]{1,0:T(8,128)(2,1)S(1)}, u32[]{:S(2)}, u32[]{:S(2)}) collective-permute-start(bf16[80,1792]{1,0:T(8,128)(2,1)S(1)} %pad_maximum_fusion.15), channel_id=1, source_target_pairs={{0,4},{1,0},{2,6},{3,2},{4,5},{5,1},{6,7},{7,3},{8,12},{9,8},{10,1... | collective-permute-start | bytes 860168 | tf_op jit(solution)/shard_map/ppermute | solution.py:129
  88.8 12.0 %collective-permute-start.23 = (bf16[80,1792]{1,0:T(8,128)(2,1)S(1)}, bf16[80,1792]{1,0:T(8,128)(2,1)S(1)}, u32[]{:S(2)}, u32[]{:S(2)}) collective-permute-start(bf16[80,1792]{1,0:T(8,128)(2,1)S(1)} %pad_maximum_fusion.15), channel_id=1, source_target_pairs={{1,4},{3,6},{4,1},{6,3},{9,12},{11,14},{12,9},{14,11},{17,20},{19,... | collective-permute-start | bytes 860168 | tf_op jit(solution)/shard_map/ppermute | solution.py:129
  93.8 6.2 %collective-permute-start.19 = (bf16[40,1792]{1,0:T(8,128)(2,1)S(1)}, bf16[40,1792]{1,0:T(8,128)(2,1)S(1)}, u32[]{:S(2)}, u32[]{:S(2)}) collective-permute-start(bf16[40,1792]{1,0:T(8,128)(2,1)S(1)} %get-tuple-element.114), channel_id=1, source_target_pairs={{0,2},{1,3},{2,0},{3,1},{4,6},{5,7},{6,4},{7,5},{8,10},{9,11},{10,... | collective-permute-start | bytes 430088 | tf_op jit(solution)/shard_map/ppermute | solution.py:55
  96.3 10.8 %collective-permute-start.25 = (bf16[40,2304]{1,0:T(8,128)(2,1)S(1)}, bf16[40,2304]{1,0:T(8,128)(2,1)S(1)}, u32[]{:S(2)}, u32[]{:S(2)}) collective-permute-start(bf16[40,2304]{1,0:T(8,128)(2,1)S(1)} %fusion.39), channel_id=1, source_target_pairs={{0,8},{4,12},{8,0},{12,4},{1,9},{5,13},{9,1},{13,5},{2,10},{6,14},... | collective-permute-start | bytes 552968 | tf_op jit(solution)/shard_map/ppermute | solution.py:55
  96.6 10.9 %collective-permute-start.24 = (bf16[2,40,1280]{2,1,0:T(8,128)(2,1)S(1)}, bf16[2,40,1280]{2,1,0:T(8,128)(2,1)S(1)}, u32[]{:S(2)}, u32[]{:S(2)}) collective-permute-start(bf16[2,40,1280]{2,1,0:T(8,128)(2,1)S(1)} %pad_maximum_fusion.17), channel_id=1, source_target_pairs={{0,2},{1,3},{2,0},{3,1},{4,6},{5,7},{6,4},{7,5},{8,10},{9,11},{10,... | collective-permute-start | bytes 614408 | tf_op jit(solution)/shard_map/ppermute | solution.py:55
  100.0 9.0 %collective-permute-start.26 = (bf16[80,1792]{1,0:T(8,128)(2,1)S(1)}, bf16[80,1792]{1,0:T(8,128)(2,1)S(1)}, u32[]{:S(2)}, u32[]{:S(2)}) collective-permute-start(bf16[80,1792]{1,0:T(8,128)(2,1)S(1)} %pad_maximum_fusion.16), channel_id=1, source_target_pairs={{0,4},{1,0},{2,6},{3,2},{4,5},{5,1},{6,7},{7,3},{8,12},{9,8},{10,1... | collective-permute-start | bytes 860168 | tf_op jit(solution)/shard_map/ppermute | solution.py:129
  100.1 8.9 %collective-permute-start.27 = (bf16[80,1792]{1,0:T(8,128)(2,1)S(1)}, bf16[80,1792]{1,0:T(8,128)(2,1)S(1)}, u32[]{:S(2)}, u32[]{:S(2)}) collective-permute-start(bf16[80,1792]{1,0:T(8,128)(2,1)S(1)} %pad_maximum_fusion.16), channel_id=1, source_target_pairs={{1,4},{3,6},{4,1},{6,3},{9,12},{11,14},{12,9},{14,11},{17,20},{19,... | collective-permute-start | bytes 860168 | tf_op jit(solution)/shard_map/ppermute | solution.py:129
  107.2 6.6 %collective-permute-start.28 = (bf16[40,2304]{1,0:T(8,128)(2,1)S(1)}, bf16[40,2304]{1,0:T(8,128)(2,1)S(1)}, u32[]{:S(2)}, u32[]{:S(2)}) collective-permute-start(bf16[40,2304]{1,0:T(8,128)(2,1)S(1)} %get-tuple-element.96), channel_id=1, source_target_pairs={{0,2},{1,3},{2,0},{3,1},{4,6},{5,7},{6,4},{7,5},{8,10},{9,11},{10,... | collective-permute-start | bytes 552968 | tf_op jit(solution)/shard_map/ppermute | solution.py:55
  107.6 8.6 %collective-permute-start.30 = (bf16[40,1280]{1,0:T(8,128)(2,1)S(1)}, bf16[40,1280]{1,0:T(8,128)(2,1)S(1)}, u32[]{:S(2)}, u32[]{:S(2)}) collective-permute-start(bf16[40,1280]{1,0:T(8,128)(2,1)S(1)} %fusion.51), channel_id=1, source_target_pairs={{0,8},{4,12},{8,0},{12,4},{1,9},{5,13},{9,1},{13,5},{2,10},{6,14},... | collective-permute-start | bytes 307208 | tf_op jit(solution)/shard_map/ppermute | solution.py:55
  113.8 7.1 %collective-permute-start.32 = (bf16[80,2304]{1,0:T(8,128)(2,1)S(1)}, bf16[80,2304]{1,0:T(8,128)(2,1)S(1)}, u32[]{:S(2)}, u32[]{:S(2)}) collective-permute-start(bf16[80,2304]{1,0:T(8,128)(2,1)S(1)} %pad_maximum_fusion.10), channel_id=1, source_target_pairs={{0,4},{1,0},{2,6},{3,2},{4,5},{5,1},{6,7},{7,3},{8,12},{9,8},{10,1... | collective-permute-start | bytes 1105928 | tf_op jit(solution)/shard_map/ppermute | solution.py:129
  113.8 7.0 %collective-permute-start.33 = (bf16[80,2304]{1,0:T(8,128)(2,1)S(1)}, bf16[80,2304]{1,0:T(8,128)(2,1)S(1)}, u32[]{:S(2)}, u32[]{:S(2)}) collective-permute-start(bf16[80,2304]{1,0:T(8,128)(2,1)S(1)} %pad_maximum_fusion.10), channel_id=1, source_target_pairs={{1,4},{3,6},{4,1},{6,3},{9,12},{11,14},{12,9},{14,11},{17,20},{19,... | collective-permute-start | bytes 1105928 | tf_op jit(solution)/shard_map/ppermute | solution.py:129
  116.2 6.5 %collective-permute-start.31 = (bf16[40,1280]{1,0:T(8,128)(2,1)S(1)}, bf16[40,1280]{1,0:T(8,128)(2,1)S(1)}, u32[]{:S(2)}, u32[]{:S(2)}) collective-permute-start(bf16[40,1280]{1,0:T(8,128)(2,1)S(1)} %get-tuple-element.120), channel_id=1, source_target_pairs={{0,2},{1,3},{2,0},{3,1},{4,6},{5,7},{6,4},{7,5},{8,10},{9,11},{10,... | collective-permute-start | bytes 307208 | tf_op jit(solution)/shard_map/ppermute | solution.py:55
  116.6 11.3 %collective-permute-start.29 = (bf16[80,2048]{1,0:T(8,128)(2,1)S(1)}, bf16[80,2048]{1,0:T(8,128)(2,1)S(1)}, u32[]{:S(2)}, u32[]{:S(2)}) collective-permute-start(bf16[80,2048]{1,0:T(8,128)(2,1)S(1)} %slice.508), channel_id=1, source_target_pairs={{0,1},{1,0},{2,3},{3,2},{4,5},{5,4},{6,7},{7,6},{8,9},{9,8},{10,11... | collective-permute-start | bytes 983048 | tf_op jit(solution)/shard_map/ppermute | solution.py:55
  122.7 8.6 %collective-permute-start.35 = (bf16[80,1280]{1,0:T(8,128)(2,1)S(1)}, bf16[80,1280]{1,0:T(8,128)(2,1)S(1)}, u32[]{:S(2)}, u32[]{:S(2)}) collective-permute-start(bf16[80,1280]{1,0:T(8,128)(2,1)S(1)} %pad_maximum_fusion.18), channel_id=1, source_target_pairs={{0,4},{1,0},{2,6},{3,2},{4,5},{5,1},{6,7},{7,3},{8,12},{9,8},{10,1... | collective-permute-start | bytes 614408 | tf_op jit(solution)/shard_map/ppermute | solution.py:129
  127.2 4.1 %collective-permute-start.36 = (bf16[80,1280]{1,0:T(8,128)(2,1)S(1)}, bf16[80,1280]{1,0:T(8,128)(2,1)S(1)}, u32[]{:S(2)}, u32[]{:S(2)}) collective-permute-start(bf16[80,1280]{1,0:T(8,128)(2,1)S(1)} %pad_maximum_fusion.18), channel_id=1, source_target_pairs={{1,4},{3,6},{4,1},{6,3},{9,12},{11,14},{12,9},{14,11},{17,20},{19,... | collective-permute-start | bytes 614408 | tf_op jit(solution)/shard_map/ppermute | solution.py:129
  128.0 10.3 %collective-permute-start.34 = (bf16[80,2048]{1,0:T(8,128)(2,1)S(1)}, bf16[80,2048]{1,0:T(8,128)(2,1)S(1)}, u32[]{:S(2)}, u32[]{:S(2)}) collective-permute-start(bf16[80,2048]{1,0:T(8,128)(2,1)S(1)} %get-tuple-element.81), channel_id=1, source_target_pairs={{0,2},{1,3},{2,0},{3,1},{4,6},{5,7},{6,4},{7,5},{8,10},{9,11},{10,... | collective-permute-start | bytes 983048 | tf_op jit(solution)/shard_map/ppermute | solution.py:55
  132.6 5.8 %collective-permute-start.37 = (bf16[80,2048]{1,0:T(8,128)(2,1)S(1)}, bf16[80,2048]{1,0:T(8,128)(2,1)S(1)}, u32[]{:S(2)}, u32[]{:S(2)}) collective-permute-start(bf16[80,2048]{1,0:T(8,128)(2,1)S(1)} %slice.507), channel_id=1, source_target_pairs={{0,1},{1,0},{2,3},{3,2},{4,5},{5,4},{6,7},{7,6},{8,9},{9,8},{10,11... | collective-permute-start | bytes 983048 | tf_op jit(solution)/shard_map/ppermute | solution.py:55
  138.5 9.8 %collective-permute-start.38 = (bf16[80,2048]{1,0:T(8,128)(2,1)S(1)}, bf16[80,2048]{1,0:T(8,128)(2,1)S(1)}, u32[]{:S(2)}, u32[]{:S(2)}) collective-permute-start(bf16[80,2048]{1,0:T(8,128)(2,1)S(1)} %fusion.35), channel_id=1, source_target_pairs={{0,2},{1,3},{2,0},{3,1},{4,6},{5,7},{6,4},{7,5},{8,10},{9,11},{10,... | collective-permute-start | bytes 983048 | tf_op jit(solution)/shard_map/ppermute | solution.py:55
  138.9 10.5 %collective-permute-start.39 = (bf16[80,2048]{1,0:T(8,128)(2,1)S(1)}, bf16[80,2048]{1,0:T(8,128)(2,1)S(1)}, u32[]{:S(2)}, u32[]{:S(2)}) collective-permute-start(bf16[80,2048]{1,0:T(8,128)(2,1)S(1)} %get-tuple-element.77), channel_id=1, source_target_pairs={{0,1},{1,0},{2,3},{3,2},{4,5},{5,4},{6,7},{7,6},{8,9},{9,8},{10,11... | collective-permute-start | bytes 983048 | tf_op jit(solution)/shard_map/ppermute | solution.py:55
  148.5 1.7 %collective-permute-start.40 = (bf16[80,2048]{1,0:T(8,128)(2,1)S(1)}, bf16[80,2048]{1,0:T(8,128)(2,1)S(1)}, u32[]{:S(2)}, u32[]{:S(2)}) collective-permute-start(bf16[80,2048]{1,0:T(8,128)(2,1)S(1)} %get-tuple-element.79), channel_id=1, source_target_pairs={{0,1},{1,0},{2,3},{3,2},{4,5},{5,4},{6,7},{7,6},{8,9},{9,8},{10,11... | collective-permute-start | bytes 983048 | tf_op jit(solution)/shard_map/ppermute | solution.py:55

commit v20 on v16

--- a/solution.py
+++ b/solution.py
@@ -35,11 +35,9 @@
     "c10.columns": ["c01.cores"],
     "c01.down": ["c10.columns"],
     "c11.halves": ["c01.down"],
-    "c10.cores": ["c11.halves"],
+    "c10.cores": ["b0.total"],
     "c11.columns": ["c10.down"],
-    "b0.total": ["c11.columns"],
-    "c11.cores": ["b0.total"],
-    "c11.down": ["b0.total"],
+    "b0.total": ["c11.halves"],
     "b1.total": ["c11.down"],
 }
 

time: 147 us -> 147 us (level)
  no operation moved by 1% of the time
where the time goes in v20:
time: 147 us
  waiting for transfers between devices  52.9 us (36%)
  starting transfers between devices  46.4 us (32%)
  matrix products  33.8 us (23%)
  Pallas kernels  5.84 us (4%)
  other arithmetic  5.03 us (3%)
  local copies, waits for them, and re-layouts  1.63 us (1%)
    ppermute x29, waiting for transfers between devices, flip(): return lax.ppermute(value, axis, [(i, i ^ bit) for i in range(count)])  48.5 us
    dot_general x17, matrix products, dot(): return jnp.dot(a, b, preferred_element_type=jnp.float32)  33 us
    ppermute x29, starting transfers between devices, flip(): return lax.ppermute(value, axis, [(i, i ^ bit) for i in range(count)])  31 us
    ppermute x12, starting transfers between devices, move(): return lax.ppermute(value, ('row', 'col'), pairs)  15.5 us
    pallas_call x1, Pallas kernels, pull(): pl.pallas_call(functools.partial(pull_kernel, first, end), in_specs=[pl.B...  5.84 us
    ppermute x12, waiting for transfers between devices, move(): return lax.ppermute(value, ('row', 'col'), pairs)  4.34 us
  transfers between devices with their start and end apart: 41, of which 15 were waited for; matrix products, arithmetic and copies ran while one was open for 24% of the time, Pallas kernels for 4%

profile of v20, /device:TPU:0, one launch (start us, length us, event | category | flops | bytes accessed | tf_op | source)
XLA Modules:
  0.0 146.6 jit_solution(10590750231447727340)
XLA Ops:
  0.5 0.9 fusion.83
  1.5 1.4 fusion.73
  3.2 2.6 %collective-permute-start.1 = (bf16[40,2048]{1,0:T(8,128)(2,1)S(1)}, bf16[40,2048]{1,0:T(8,128)(2,1)S(1)}, u32[]{:S(2)}, u32[]{:S(2)}) collective-permute-start(bf16[40,2048]{1,0:T(8,128)(2,1)S(1)} %slice.314), channel_id=1, source_target_pairs={{0,2},{1,3},{2,0},{3,1},{4,6},{5,7},{6,4},{7,5},{8,10},{9,11},{10,... | collective-permute-start | bytes 491528 | tf_op jit(solution)/shard_map/ppermute | solution.py:51
  5.8 4.9 %collective-permute-done.1 = bf16[40,2048]{1,0:T(8,128)(2,1)S(1)} collective-permute-done((bf16[40,2048]{1,0:T(8,128)(2,1)S(1)}, bf16[40,2048]{1,0:T(8,128)(2,1)S(1)}, u32[]{:S(2)}, u32[]{:S(2)}) %collective-permute-start.1) | collective-permute-done | bytes 163872 | tf_op jit(solution)/shard_map/ppermute | solution.py:51
  10.7 2.9 %collective-permute-start.2 = (bf16[40,2048]{1,0:T(8,128)(2,1)S(1)}, bf16[40,2048]{1,0:T(8,128)(2,1)S(1)}, u32[]{:S(2)}, u32[]{:S(2)}) collective-permute-start(bf16[40,2048]{1,0:T(8,128)(2,1)S(1)} %slice_add_fusion.19), channel_id=1, source_target_pairs={{0,8},{4,12},{8,0},{12,4},{1,9},{5,13},{9,1},{13,5},{2,10},{6,14},... | collective-permute-start | bytes 491528 | tf_op jit(solution)/shard_map/ppermute | solution.py:51
  14.2 1.6 %collective-permute-start.6 = (bf16[40,2048]{1,0:T(8,128)(2,1)S(1)}, bf16[40,2048]{1,0:T(8,128)(2,1)S(1)}, u32[]{:S(2)}, u32[]{:S(2)}) collective-permute-start(bf16[40,2048]{1,0:T(8,128)(2,1)S(1)} %slice.316), channel_id=1, source_target_pairs={{0,2},{1,3},{2,0},{3,1},{4,6},{5,7},{6,4},{7,5},{8,10},{9,11},{10,... | collective-permute-start | bytes 491528 | tf_op jit(solution)/shard_map/ppermute | solution.py:51
  15.8 5.4 %collective-permute-done.2 = bf16[40,2048]{1,0:T(8,128)(2,1)S(1)} collective-permute-done((bf16[40,2048]{1,0:T(8,128)(2,1)S(1)}, bf16[40,2048]{1,0:T(8,128)(2,1)S(1)}, u32[]{:S(2)}, u32[]{:S(2)}) %collective-permute-start.2) | collective-permute-done | bytes 163872 | tf_op jit(solution)/shard_map/ppermute | solution.py:51
  21.2 1.6 %collective-permute-start.3 = (bf16[40,2048]{1,0:T(8,128)(2,1)S(1)}, bf16[40,2048]{1,0:T(8,128)(2,1)S(1)}, u32[]{:S(2)}, u32[]{:S(2)}) collective-permute-start(bf16[40,2048]{1,0:T(8,128)(2,1)S(1)} %get-tuple-element.100), channel_id=1, source_target_pairs={{0,2},{1,3},{2,0},{3,1},{4,6},{5,7},{6,4},{7,5},{8,10},{9,11},{10,... | collective-permute-start | bytes 491528 | tf_op jit(solution)/shard_map/ppermute | solution.py:51
  22.9 3.7 %collective-permute-done.3 = bf16[40,2048]{1,0:T(8,128)(2,1)S(1)} collective-permute-done((bf16[40,2048]{1,0:T(8,128)(2,1)S(1)}, bf16[40,2048]{1,0:T(8,128)(2,1)S(1)}, u32[]{:S(2)}, u32[]{:S(2)}) %collective-permute-start.3) | collective-permute-done | bytes 163872 | tf_op jit(solution)/shard_map/ppermute | solution.py:51
  26.6 1.6 %collective-permute-start.4 = (bf16[80,2048]{1,0:T(8,128)(2,1)S(1)}, bf16[80,2048]{1,0:T(8,128)(2,1)S(1)}, u32[]{:S(2)}, u32[]{:S(2)}) collective-permute-start(bf16[80,2048]{1,0:T(8,128)(2,1)S(1)} %pad_maximum_fusion.10), channel_id=1, source_target_pairs={{0,4},{1,0},{2,6},{3,2},{4,5},{5,1},{6,7},{7,3},{8,12},{9,8},{10,1... | collective-permute-start | bytes 983048 | tf_op jit(solution)/shard_map/ppermute | solution.py:128
  28.2 0.7 collective-permute-start.5
  28.9 3.5 %collective-permute-done.7 = bf16[40,2048]{1,0:T(8,128)(2,1)S(1)} collective-permute-done((bf16[40,2048]{1,0:T(8,128)(2,1)S(1)}, bf16[40,2048]{1,0:T(8,128)(2,1)S(1)}, u32[]{:S(2)}, u32[]{:S(2)}) %collective-permute-start.7) | collective-permute-done | bytes 163872 | tf_op jit(solution)/shard_map/ppermute | solution.py:51
  32.4 0.6 collective-permute-start.8
  33.0 5.8 %shard_map.55 = (bf16[2048,1792]{1,0:T(8,128)(2,1)S(1)}, bf16[2048,1792]{1,0:T(8,128)(2,1)S(1)}) custom-call(s32[4]{0:T(128)S(1)} %copy-done, bf16[2048,3584]{1,0:T(8,128)(2,1)} %gate_ref.1, bf16[2048,3584]{1,0:T(8,128)(2,1)} %up_ref.1), custom_call_target="tpu_custom_call" | custom-call | tf_op jit(solution)/shard_map/pallas_call | solution.py:71
  39.0 1.4 fusion.97
  40.4 1.4 fusion.98
  41.8 1.0 copy-done.2
  43.2 0.9 collective-permute-start.12
  44.0 1.1 collective-permute-done.9
  45.2 1.3 slice_add_fusion.7
  46.6 4.5 %fusion.12 = f32[160,1792]{1,0:T(8,128)S(1)} fusion(bf16[160,2048]{1,0:T(8,128)(2,1)S(1)} %pad_maximum_fusion.1, bf16[2048,3584]{1,0:T(8,128)(2,1)} %gate_ref.1), kind=kOutput, calls=%fused_computation.12 | convolution fusion | flops 1174405120 | bytes 9142272 | tf_op jit(solution)/shard_map/dot_general | solution.py:46
  51.1 4.6 %fusion.10 = f32[160,1792]{1,0:T(8,128)S(1)} fusion(bf16[160,2048]{1,0:T(8,128)(2,1)S(1)} %pad_maximum_fusion.1, bf16[2048,3584]{1,0:T(8,128)(2,1)} %up_ref.1), kind=kOutput, calls=%fused_computation.10 | convolution fusion | flops 1174405120 | bytes 9142272 | tf_op jit(solution)/shard_map/dot_general | solution.py:46
  55.8 0.7 collective-permute-start.13
  56.7 1.5 %collective-permute-start.10 = (bf16[2,40,1792]{2,1,0:T(8,128)(2,1)S(1)}, bf16[2,40,1792]{2,1,0:T(8,128)(2,1)S(1)}, u32[]{:S(2)}, u32[]{:S(2)}) collective-permute-start(bf16[2,40,1792]{2,1,0:T(8,128)(2,1)S(1)} %pad_maximum_fusion.12), channel_id=1, source_target_pairs={{0,2},{1,3},{2,0},{3,1},{4,6},{5,7},{6,4},{7,5},{8,10},{9,11},{10,... | collective-permute-start | bytes 860168 | tf_op jit(solution)/shard_map/ppermute | solution.py:51
  58.4 5.5 %fusion.4 = f32[160,2304]{1,0:T(8,128)S(1)} fusion(bf16[160,2048]{1,0:T(8,128)(2,1)S(1)} %pad_maximum_fusion.2, bf16[2048,3584]{1,0:T(8,128)(2,1)} %gate_ref.1), kind=kOutput, calls=%fused_computation.4 | convolution fusion | flops 1509949440 | bytes 11567104 | tf_op jit(solution)/shard_map/dot_general | solution.py:46
  64.0 1.7 %fusion.2 = f32[160,2304]{1,0:T(8,128)S(1)} fusion(bf16[160,2048]{1,0:T(8,128)(2,1)S(1)} %pad_maximum_fusion.2, bf16[2048,3584]{1,0:T(8,128)(2,1)S(1)} %bitcast.107), kind=kOutput, calls=%fused_computation.2 | convolution fusion | flops 1509949440 | bytes 11567104 | tf_op jit(solution)/shard_map/dot_general | solution.py:46
  66.3 3.4 %collective-permute-start.14 = (bf16[40,1792]{1,0:T(8,128)(2,1)S(1)}, bf16[40,1792]{1,0:T(8,128)(2,1)S(1)}, u32[]{:S(2)}, u32[]{:S(2)}) collective-permute-start(bf16[40,1792]{1,0:T(8,128)(2,1)S(1)} %fusion.50), channel_id=1, source_target_pairs={{0,8},{4,12},{8,0},{12,4},{1,9},{5,13},{9,1},{13,5},{2,10},{6,14},... | collective-permute-start | bytes 430088 | tf_op jit(solution)/shard_map/ppermute | solution.py:51
  69.8 1.5 %collective-permute-start.16 = (bf16[2,40,1792]{2,1,0:T(8,128)(2,1)S(1)}, bf16[2,40,1792]{2,1,0:T(8,128)(2,1)S(1)}, u32[]{:S(2)}, u32[]{:S(2)}) collective-permute-start(bf16[2,40,1792]{2,1,0:T(8,128)(2,1)S(1)} %pad_maximum_fusion.13), channel_id=1, source_target_pairs={{0,2},{1,3},{2,0},{3,1},{4,6},{5,7},{6,4},{7,5},{8,10},{9,11},{10,... | collective-permute-start | bytes 860168 | tf_op jit(solution)/shard_map/ppermute | solution.py:51
  71.3 5.6 %collective-permute-done.14 = bf16[40,1792]{1,0:T(8,128)(2,1)S(1)} collective-permute-done((bf16[40,1792]{1,0:T(8,128)(2,1)S(1)}, bf16[40,1792]{1,0:T(8,128)(2,1)S(1)}, u32[]{:S(2)}, u32[]{:S(2)}) %collective-permute-start.14) | collective-permute-done | bytes 143392 | tf_op jit(solution)/shard_map/ppermute | solution.py:51
  77.0 1.4 collective-permute-start.15
  78.7 0.7 collective-permute-start.21
  79.6 1.0 fusion.16
  80.7 3.7 %fusion.18 = f32[160,1280]{1,0:T(8,128)S(1)} fusion(bf16[160,2048]{1,0:T(8,128)(2,1)S(1)} %pad_maximum_fusion.2, bf16[2048,3584]{1,0:T(8,128)(2,1)} %gate_ref.1), kind=kOutput, calls=%fused_computation.18 | convolution fusion | flops 838860800 | bytes 6717440 | tf_op jit(solution)/shard_map/dot_general | solution.py:46
  84.5 3.1 %collective-permute-start.22 = (bf16[80,1792]{1,0:T(8,128)(2,1)S(1)}, bf16[80,1792]{1,0:T(8,128)(2,1)S(1)}, u32[]{:S(2)}, u32[]{:S(2)}) collective-permute-start(bf16[80,1792]{1,0:T(8,128)(2,1)S(1)} %pad_maximum_fusion.14), channel_id=1, source_target_pairs={{0,4},{1,0},{2,6},{3,2},{4,5},{5,1},{6,7},{7,3},{8,12},{9,8},{10,1... | collective-permute-start | bytes 860168 | tf_op jit(solution)/shard_map/ppermute | solution.py:128
  87.7 0.7 collective-permute-start.23
  88.4 1.3 collective-permute-start.19
  89.7 0.7 collective-permute-done.21
  90.7 1.3 collective-permute-start.24
  92.1 2.2 %collective-permute-done.19 = bf16[40,1792]{1,0:T(8,128)(2,1)S(1)} collective-permute-done((bf16[40,1792]{1,0:T(8,128)(2,1)S(1)}, bf16[40,1792]{1,0:T(8,128)(2,1)S(1)}, u32[]{:S(2)}, u32[]{:S(2)}) %collective-permute-start.19) | collective-permute-done | bytes 143392 | tf_op jit(solution)/shard_map/ppermute | solution.py:51
  94.3 1.8 %collective-permute-start.26 = (bf16[80,1792]{1,0:T(8,128)(2,1)S(1)}, bf16[80,1792]{1,0:T(8,128)(2,1)S(1)}, u32[]{:S(2)}, u32[]{:S(2)}) collective-permute-start(bf16[80,1792]{1,0:T(8,128)(2,1)S(1)} %pad_maximum_fusion.15), channel_id=1, source_target_pairs={{0,4},{1,0},{2,6},{3,2},{4,5},{5,1},{6,7},{7,3},{8,12},{9,8},{10,1... | collective-permute-start | bytes 860168 | tf_op jit(solution)/shard_map/ppermute | solution.py:128
  96.1 0.7 collective-permute-start.27
  96.9 4.8 %collective-permute-done.25 = bf16[40,2304]{1,0:T(8,128)(2,1)S(1)} collective-permute-done((bf16[40,2304]{1,0:T(8,128)(2,1)S(1)}, bf16[40,2304]{1,0:T(8,128)(2,1)S(1)}, u32[]{:S(2)}, u32[]{:S(2)}) %collective-permute-start.25) | collective-permute-done | bytes 184352 | tf_op jit(solution)/shard_map/ppermute | solution.py:51
  101.7 0.9 collective-permute-start.28
  102.8 1.4 fusion.8
  104.4 4.0 %collective-permute-done.28 = bf16[40,2304]{1,0:T(8,128)(2,1)S(1)} collective-permute-done((bf16[40,2304]{1,0:T(8,128)(2,1)S(1)}, bf16[40,2304]{1,0:T(8,128)(2,1)S(1)}, u32[]{:S(2)}, u32[]{:S(2)}) %collective-permute-start.28) | collective-permute-done | bytes 184352 | tf_op jit(solution)/shard_map/ppermute | solution.py:51
  108.4 0.8 collective-permute-start.32
  109.2 0.7 collective-permute-start.33
  109.9 1.5 %fusion.95 = f32[160,2048]{1,0:T(8,128)S(1)} fusion(f32[160,2048]{1,0:T(8,128)S(1)} %fusion.8, bf16[160,1792]{1,0:T(8,128)(2,1)S(1)} %pad_maximum_fusion.6, bf16[3584,2048]{1,0:T(8,128)(2,1)S(1)} %bitcast.116), kind=kOutput, calls=%fused_computation.198 | convolution fusion | flops 1174732800 | bytes 10534912 | tf_op jit(solution)/shard_map/dot_general | solution.py:46
  111.4 1.4 collective-permute-start.29
  112.9 1.4 collective-permute-start.34
  114.5 2.3 %collective-permute-done.32 = bf16[80,2304]{1,0:T(8,128)(2,1)S(1)} collective-permute-done((bf16[80,2304]{1,0:T(8,128)(2,1)S(1)}, bf16[80,2304]{1,0:T(8,128)(2,1)S(1)}, u32[]{:S(2)}, u32[]{:S(2)}) %collective-permute-start.32) | collective-permute-done | bytes 368672 | tf_op jit(solution)/shard_map/ppermute | solution.py:128
  116.9 1.7 %fusion = f32[160,2048]{1,0:T(8,128)S(1)} fusion(bf16[3584,2048]{1,0:T(8,128)(2,1)S(1)} %bitcast.116, bf16[80,2304]{1,0:T(8,128)(2,1)S(1)} %get-tuple-element.86, bf16[80,2304]{1,0:T(8,128)(2,1)S(1)} %get-tuple-element.85), kind=kOutput, calls=%fused_computation | convolution fusion | flops 1511424000 | bytes 11485184 | tf_op jit(solution)/shard_map/dot_general | solution.py:46
  118.7 3.9 %collective-permute-start.35 = (bf16[80,1280]{1,0:T(8,128)(2,1)S(1)}, bf16[80,1280]{1,0:T(8,128)(2,1)S(1)}, u32[]{:S(2)}, u32[]{:S(2)}) collective-permute-start(bf16[80,1280]{1,0:T(8,128)(2,1)S(1)} %pad_maximum_fusion.17), channel_id=1, source_target_pairs={{0,4},{1,0},{2,6},{3,2},{4,5},{5,1},{6,7},{7,3},{8,12},{9,8},{10,1... | collective-permute-start | bytes 614408 | tf_op jit(solution)/shard_map/ppermute | solution.py:128
  122.6 0.7 collective-permute-start.36
  123.3 1.4 collective-permute-start.31
  124.7 2.0 %collective-permute-done.35 = bf16[80,1280]{1,0:T(8,128)(2,1)S(1)} collective-permute-done((bf16[80,1280]{1,0:T(8,128)(2,1)S(1)}, bf16[80,1280]{1,0:T(8,128)(2,1)S(1)}, u32[]{:S(2)}, u32[]{:S(2)}) %collective-permute-start.35) | collective-permute-done | bytes 204832 | tf_op jit(solution)/shard_map/ppermute | solution.py:128
  126.8 1.1 fusion.96
  127.9 1.9 %collective-permute-start.37 = (bf16[80,2048]{1,0:T(8,128)(2,1)S(1)}, bf16[80,2048]{1,0:T(8,128)(2,1)S(1)}, u32[]{:S(2)}, u32[]{:S(2)}) collective-permute-start(bf16[80,2048]{1,0:T(8,128)(2,1)S(1)} %slice.503), channel_id=1, source_target_pairs={{0,1},{1,0},{2,3},{3,2},{4,5},{5,4},{6,7},{7,6},{8,9},{9,8},{10,11... | collective-permute-start | bytes 983048 | tf_op jit(solution)/shard_map/ppermute | solution.py:51
  129.9 3.7 %collective-permute-done.31 = bf16[80,2048]{1,0:T(8,128)(2,1)S(1)} collective-permute-done((bf16[80,2048]{1,0:T(8,128)(2,1)S(1)}, bf16[80,2048]{1,0:T(8,128)(2,1)S(1)}, u32[]{:S(2)}, u32[]{:S(2)}) %collective-permute-start.31) | collective-permute-done | bytes 327712 | tf_op jit(solution)/shard_map/ppermute | solution.py:51
  133.7 1.4 collective-permute-start.38
  135.3 8.2 %collective-permute-done.38 = bf16[80,2048]{1,0:T(8,128)(2,1)S(1)} collective-permute-done((bf16[80,2048]{1,0:T(8,128)(2,1)S(1)}, bf16[80,2048]{1,0:T(8,128)(2,1)S(1)}, u32[]{:S(2)}, u32[]{:S(2)}) %collective-permute-start.38) | collective-permute-done | bytes 327712 | tf_op jit(solution)/shard_map/ppermute | solution.py:51
  143.8 0.8 fusion.25
  144.7 0.7 collective-permute-done.40
  145.4 1.3 fusion.22
  (138 shorter events, 5.8 us)
Async XLA Ops:
  0.0 2.9 %collective-permute-start = (bf16[160,2048]{1,0:T(8,128)(2,1)}, bf16[160,2048]{1,0:T(8,128)(2,1)S(1)}, u32[]{:S(2)}, u32[]{:S(2)}) collective-permute-start(bf16[160,2048]{1,0:T(8,128)(2,1)} %param.5), channel_id=1, source_target_pairs={{0,1},{1,0},{2,3},{3,2},{4,5},{5,4},{6,7},{7,6},{8,9},{9,8},{10,11... | collective-permute-start | bytes 1966088 | tf_op jit(solution)/shard_map/ppermute | solution.py:51
  2.9 10.7 %copy-start.1 = (bf16[160,2048]{1,0:T(8,128)(2,1)S(1)}, bf16[160,2048]{1,0:T(8,128)(2,1)}, u32[]{:S(2)}) copy-start(bf16[160,2048]{1,0:T(8,128)(2,1)} %param.5) | copy-start | bytes 1966084
  3.2 7.4 %collective-permute-start.1 = (bf16[40,2048]{1,0:T(8,128)(2,1)S(1)}, bf16[40,2048]{1,0:T(8,128)(2,1)S(1)}, u32[]{:S(2)}, u32[]{:S(2)}) collective-permute-start(bf16[40,2048]{1,0:T(8,128)(2,1)S(1)} %slice.314), channel_id=1, source_target_pairs={{0,2},{1,3},{2,0},{3,1},{4,6},{5,7},{6,4},{7,5},{8,10},{9,11},{10,... | collective-permute-start | bytes 491528 | tf_op jit(solution)/shard_map/ppermute | solution.py:51
  10.7 10.5 %collective-permute-start.2 = (bf16[40,2048]{1,0:T(8,128)(2,1)S(1)}, bf16[40,2048]{1,0:T(8,128)(2,1)S(1)}, u32[]{:S(2)}, u32[]{:S(2)}) collective-permute-start(bf16[40,2048]{1,0:T(8,128)(2,1)S(1)} %slice_add_fusion.19), channel_id=1, source_target_pairs={{0,8},{4,12},{8,0},{12,4},{1,9},{5,13},{9,1},{13,5},{2,10},{6,14},... | collective-permute-start | bytes 491528 | tf_op jit(solution)/shard_map/ppermute | solution.py:51
  14.2 18.8 %copy-start = (s32[4]{0:T(128)S(1)}, s32[4]{0:T(128)}, u32[]{:S(2)}) copy-start(s32[4]{0:T(128)} %tick_ref) | copy-start | bytes 52
  14.2 8.6 %collective-permute-start.6 = (bf16[40,2048]{1,0:T(8,128)(2,1)S(1)}, bf16[40,2048]{1,0:T(8,128)(2,1)S(1)}, u32[]{:S(2)}, u32[]{:S(2)}) collective-permute-start(bf16[40,2048]{1,0:T(8,128)(2,1)S(1)} %slice.316), channel_id=1, source_target_pairs={{0,2},{1,3},{2,0},{3,1},{4,6},{5,7},{6,4},{7,5},{8,10},{9,11},{10,... | collective-permute-start | bytes 491528 | tf_op jit(solution)/shard_map/ppermute | solution.py:51
  21.2 5.4 %collective-permute-start.3 = (bf16[40,2048]{1,0:T(8,128)(2,1)S(1)}, bf16[40,2048]{1,0:T(8,128)(2,1)S(1)}, u32[]{:S(2)}, u32[]{:S(2)}) collective-permute-start(bf16[40,2048]{1,0:T(8,128)(2,1)S(1)} %get-tuple-element.100), channel_id=1, source_target_pairs={{0,2},{1,3},{2,0},{3,1},{4,6},{5,7},{6,4},{7,5},{8,10},{9,11},{10,... | collective-permute-start | bytes 491528 | tf_op jit(solution)/shard_map/ppermute | solution.py:51
  22.8 9.5 %collective-permute-start.7 = (bf16[40,2048]{1,0:T(8,128)(2,1)S(1)}, bf16[40,2048]{1,0:T(8,128)(2,1)S(1)}, u32[]{:S(2)}, u32[]{:S(2)}) collective-permute-start(bf16[40,2048]{1,0:T(8,128)(2,1)S(1)} %slice_add_fusion.18), channel_id=1, source_target_pairs={{0,8},{4,12},{8,0},{12,4},{1,9},{5,13},{9,1},{13,5},{2,10},{6,14},... | collective-permute-start | bytes 491528 | tf_op jit(solution)/shard_map/ppermute | solution.py:51
  26.6 12.2 %collective-permute-start.4 = (bf16[80,2048]{1,0:T(8,128)(2,1)S(1)}, bf16[80,2048]{1,0:T(8,128)(2,1)S(1)}, u32[]{:S(2)}, u32[]{:S(2)}) collective-permute-start(bf16[80,2048]{1,0:T(8,128)(2,1)S(1)} %pad_maximum_fusion.10), channel_id=1, source_target_pairs={{0,4},{1,0},{2,6},{3,2},{4,5},{5,1},{6,7},{7,3},{8,12},{9,8},{10,1... | collective-permute-start | bytes 983048 | tf_op jit(solution)/shard_map/ppermute | solution.py:128
  28.2 10.7 %collective-permute-start.5 = (bf16[80,2048]{1,0:T(8,128)(2,1)S(1)}, bf16[80,2048]{1,0:T(8,128)(2,1)S(1)}, u32[]{:S(2)}, u32[]{:S(2)}) collective-permute-start(bf16[80,2048]{1,0:T(8,128)(2,1)S(1)} %pad_maximum_fusion.10), channel_id=1, source_target_pairs={{1,4},{3,6},{4,1},{6,3},{9,12},{11,14},{12,9},{14,11},{17,20},{19,... | collective-permute-start | bytes 983048 | tf_op jit(solution)/shard_map/ppermute | solution.py:128
  32.4 6.6 %collective-permute-start.8 = (bf16[40,2048]{1,0:T(8,128)(2,1)S(1)}, bf16[40,2048]{1,0:T(8,128)(2,1)S(1)}, u32[]{:S(2)}, u32[]{:S(2)}) collective-permute-start(bf16[40,2048]{1,0:T(8,128)(2,1)S(1)} %get-tuple-element.96), channel_id=1, source_target_pairs={{0,2},{1,3},{2,0},{3,1},{4,6},{5,7},{6,4},{7,5},{8,10},{9,11},{10,... | collective-permute-start | bytes 491528 | tf_op jit(solution)/shard_map/ppermute | solution.py:51
  41.8 1.0 copy-start.2
  43.0 2.2 %collective-permute-start.9 = (bf16[2,80,1792]{2,1,0:T(8,128)(2,1)S(1)}, bf16[2,80,1792]{2,1,0:T(8,128)(2,1)}, u32[]{:S(2)}, u32[]{:S(2)}) collective-permute-start(bf16[2,80,1792]{2,1,0:T(8,128)(2,1)S(1)} %pad_maximum_fusion.3), channel_id=1, source_target_pairs={{0,1},{1,0},{2,3},{3,2},{4,5},{5,4},{6,7},{7,6},{8,9},{9,8},{10,11... | collective-permute-start | bytes 1720328 | tf_op jit(solution)/shard_map/ppermute | solution.py:51
  43.1 13.4 %collective-permute-start.11 = (bf16[80,2048]{1,0:T(8,128)(2,1)S(1)}, bf16[80,2048]{1,0:T(8,128)(2,1)S(1)}, u32[]{:S(2)}, u32[]{:S(2)}) collective-permute-start(bf16[80,2048]{1,0:T(8,128)(2,1)S(1)} %pad_maximum_fusion.11), channel_id=1, source_target_pairs={{0,4},{1,0},{2,6},{3,2},{4,5},{5,1},{6,7},{7,3},{8,12},{9,8},{10,1... | collective-permute-start | bytes 983048 | tf_op jit(solution)/shard_map/ppermute | solution.py:128
  43.2 13.4 %collective-permute-start.12 = (bf16[80,2048]{1,0:T(8,128)(2,1)S(1)}, bf16[80,2048]{1,0:T(8,128)(2,1)S(1)}, u32[]{:S(2)}, u32[]{:S(2)}) collective-permute-start(bf16[80,2048]{1,0:T(8,128)(2,1)S(1)} %pad_maximum_fusion.11), channel_id=1, source_target_pairs={{1,4},{3,6},{4,1},{6,3},{9,12},{11,14},{12,9},{14,11},{17,20},{19,... | collective-permute-start | bytes 983048 | tf_op jit(solution)/shard_map/ppermute | solution.py:128
  51.1 12.9 %slice-start = ((s8[14680064]{0:T(1024)(128)(4,1)}), s8[4194304]{0:T(1024)(128)(4,1)S(1)}, s32[]{:S(2)}) async-start(s8[14680064]{0:T(1024)(128)(4,1)} %bitcast.106), calls=%async_computation | async-start | bytes 8388608
  51.1 12.9 %slice-start.1 = ((s8[14680064]{0:T(1024)(128)(4,1)}), s8[4194304]{0:T(1024)(128)(4,1)S(1)}, s32[]{:S(2)}) async-start(s8[14680064]{0:T(1024)(128)(4,1)} %bitcast.106), calls=%async_computation.1 | async-start | bytes 8388608
  55.8 2.4 %collective-permute-start.13 = (bf16[2,80,1792]{2,1,0:T(8,128)(2,1)S(1)}, bf16[2,80,1792]{2,1,0:T(8,128)(2,1)S(1)}, u32[]{:S(2)}, u32[]{:S(2)}) collective-permute-start(bf16[2,80,1792]{2,1,0:T(8,128)(2,1)S(1)} %pad_maximum_fusion.4), channel_id=1, source_target_pairs={{0,1},{1,0},{2,3},{3,2},{4,5},{5,4},{6,7},{7,6},{8,9},{9,8},{10,11... | collective-permute-start | bytes 1720328 | tf_op jit(solution)/shard_map/ppermute | solution.py:51
  56.7 7.3 %slice-start.2 = ((s8[14680064]{0:T(1024)(128)(4,1)}), s8[4194304]{0:T(1024)(128)(4,1)S(1)}, s32[]{:S(2)}) async-start(s8[14680064]{0:T(1024)(128)(4,1)} %bitcast.106), calls=%async_computation.2 | async-start | bytes 8388608
  56.7 9.5 %collective-permute-start.10 = (bf16[2,40,1792]{2,1,0:T(8,128)(2,1)S(1)}, bf16[2,40,1792]{2,1,0:T(8,128)(2,1)S(1)}, u32[]{:S(2)}, u32[]{:S(2)}) collective-permute-start(bf16[2,40,1792]{2,1,0:T(8,128)(2,1)S(1)} %pad_maximum_fusion.12), channel_id=1, source_target_pairs={{0,2},{1,3},{2,0},{3,1},{4,6},{5,7},{6,4},{7,5},{8,10},{9,11},{10,... | collective-permute-start | bytes 860168 | tf_op jit(solution)/shard_map/ppermute | solution.py:51
  58.4 5.6 %slice-start.3 = ((s8[14680064]{0:T(1024)(128)(4,1)}), s8[2097152]{0:T(1024)(128)(4,1)S(1)}, s32[]{:S(2)}) async-start(s8[14680064]{0:T(1024)(128)(4,1)} %bitcast.106), calls=%async_computation.3 | async-start | bytes 4194304
  65.9 12.5 %collective-permute-start.17 = (bf16[2,80,2304]{2,1,0:T(8,128)(2,1)S(1)}, bf16[2,80,2304]{2,1,0:T(8,128)(2,1)S(1)}, u32[]{:S(2)}, u32[]{:S(2)}) collective-permute-start(bf16[2,80,2304]{2,1,0:T(8,128)(2,1)S(1)} %pad_maximum_fusion), channel_id=1, source_target_pairs={{0,1},{1,0},{2,3},{3,2},{4,5},{5,4},{6,7},{7,6},{8,9},{9,8},{10,11... | collective-permute-start | bytes 2211848 | tf_op jit(solution)/shard_map/ppermute | solution.py:51
  66.3 10.6 %collective-permute-start.14 = (bf16[40,1792]{1,0:T(8,128)(2,1)S(1)}, bf16[40,1792]{1,0:T(8,128)(2,1)S(1)}, u32[]{:S(2)}, u32[]{:S(2)}) collective-permute-start(bf16[40,1792]{1,0:T(8,128)(2,1)S(1)} %fusion.50), channel_id=1, source_target_pairs={{0,8},{4,12},{8,0},{12,4},{1,9},{5,13},{9,1},{13,5},{2,10},{6,14},... | collective-permute-start | bytes 430088 | tf_op jit(solution)/shard_map/ppermute | solution.py:51
  69.8 9.6 %collective-permute-start.16 = (bf16[2,40,1792]{2,1,0:T(8,128)(2,1)S(1)}, bf16[2,40,1792]{2,1,0:T(8,128)(2,1)S(1)}, u32[]{:S(2)}, u32[]{:S(2)}) collective-permute-start(bf16[2,40,1792]{2,1,0:T(8,128)(2,1)S(1)} %pad_maximum_fusion.13), channel_id=1, source_target_pairs={{0,2},{1,3},{2,0},{3,1},{4,6},{5,7},{6,4},{7,5},{8,10},{9,11},{10,... | collective-permute-start | bytes 860168 | tf_op jit(solution)/shard_map/ppermute | solution.py:51
  77.0 7.5 %collective-permute-start.15 = (bf16[40,1792]{1,0:T(8,128)(2,1)S(1)}, bf16[40,1792]{1,0:T(8,128)(2,1)S(1)}, u32[]{:S(2)}, u32[]{:S(2)}) collective-permute-start(bf16[40,1792]{1,0:T(8,128)(2,1)S(1)} %get-tuple-element.108), channel_id=1, source_target_pairs={{0,2},{1,3},{2,0},{3,1},{4,6},{5,7},{6,4},{7,5},{8,10},{9,11},{10,... | collective-permute-start | bytes 430088 | tf_op jit(solution)/shard_map/ppermute | solution.py:51
  78.6 24.2 %slice-start.4 = ((s8[14680064]{0:T(1024)(128)(4,1)}), s8[2097152]{0:T(1024)(128)(4,1)S(1)}, s32[]{:S(2)}) async-start(s8[14680064]{0:T(1024)(128)(4,1)} %bitcast.115), calls=%async_computation.4 | async-start | bytes 4194304
  78.7 11.7 %collective-permute-start.21 = (bf16[2,40,2304]{2,1,0:T(8,128)(2,1)S(1)}, bf16[2,40,2304]{2,1,0:T(8,128)(2,1)S(1)}, u32[]{:S(2)}, u32[]{:S(2)}) collective-permute-start(bf16[2,40,2304]{2,1,0:T(8,128)(2,1)S(1)} %pad_maximum_fusion.8), channel_id=1, source_target_pairs={{0,2},{1,3},{2,0},{3,1},{4,6},{5,7},{6,4},{7,5},{8,10},{9,11},{10,... | collective-permute-start | bytes 1105928 | tf_op jit(solution)/shard_map/ppermute | solution.py:51
  79.5 23.3 %slice-start.5 = ((s8[14680064]{0:T(1024)(128)(4,1)}), s8[4194304]{0:T(1024)(128)(4,1)S(1)}, s32[]{:S(2)}) async-start(s8[14680064]{0:T(1024)(128)(4,1)} %bitcast.115), calls=%async_computation.5 | async-start | bytes 8388608
  79.5 8.8 %collective-permute-start.18 = (bf16[40,1792]{1,0:T(8,128)(2,1)S(1)}, bf16[40,1792]{1,0:T(8,128)(2,1)S(1)}, u32[]{:S(2)}, u32[]{:S(2)}) collective-permute-start(bf16[40,1792]{1,0:T(8,128)(2,1)S(1)} %fusion.48), channel_id=1, source_target_pairs={{0,8},{4,12},{8,0},{12,4},{1,9},{5,13},{9,1},{13,5},{2,10},{6,14},... | collective-permute-start | bytes 430088 | tf_op jit(solution)/shard_map/ppermute | solution.py:51
  80.6 22.2 %slice-start.6 = ((s8[14680064]{0:T(1024)(128)(4,1)}), s8[4194304]{0:T(1024)(128)(4,1)S(1)}, s32[]{:S(2)}) async-start(s8[14680064]{0:T(1024)(128)(4,1)} %bitcast.115), calls=%async_computation.6 | async-start | bytes 8388608
  84.4 6.1 %collective-permute-start.20 = (bf16[2,80,1280]{2,1,0:T(8,128)(2,1)S(1)}, bf16[2,80,1280]{2,1,0:T(8,128)(2,1)S(1)}, u32[]{:S(2)}, u32[]{:S(2)}) collective-permute-start(bf16[2,80,1280]{2,1,0:T(8,128)(2,1)S(1)} %pad_maximum_fusion.7), channel_id=1, source_target_pairs={{0,1},{1,0},{2,3},{3,2},{4,5},{5,4},{6,7},{7,6},{8,9},{9,8},{10,11... | collective-permute-start | bytes 1228808 | tf_op jit(solution)/shard_map/ppermute | solution.py:51
  84.5 11.5 %collective-permute-start.22 = (bf16[80,1792]{1,0:T(8,128)(2,1)S(1)}, bf16[80,1792]{1,0:T(8,128)(2,1)S(1)}, u32[]{:S(2)}, u32[]{:S(2)}) collective-permute-start(bf16[80,1792]{1,0:T(8,128)(2,1)S(1)} %pad_maximum_fusion.14), channel_id=1, source_target_pairs={{0,4},{1,0},{2,6},{3,2},{4,5},{5,1},{6,7},{7,3},{8,12},{9,8},{10,1... | collective-permute-start | bytes 860168 | tf_op jit(solution)/shard_map/ppermute | solution.py:128
  87.7 9.1 %collective-permute-start.23 = (bf16[80,1792]{1,0:T(8,128)(2,1)S(1)}, bf16[80,1792]{1,0:T(8,128)(2,1)S(1)}, u32[]{:S(2)}, u32[]{:S(2)}) collective-permute-start(bf16[80,1792]{1,0:T(8,128)(2,1)S(1)} %pad_maximum_fusion.14), channel_id=1, source_target_pairs={{1,4},{3,6},{4,1},{6,3},{9,12},{11,14},{12,9},{14,11},{17,20},{19,... | collective-permute-start | bytes 860168 | tf_op jit(solution)/shard_map/ppermute | solution.py:128
  88.4 14.4 %slice-start.7 = ((s8[14680064]{0:T(1024)(128)(4,1)}), s8[4194304]{0:T(1024)(128)(4,1)S(1)}, s32[]{:S(2)}) async-start(s8[14680064]{0:T(1024)(128)(4,1)} %bitcast.115), calls=%async_computation.7 | async-start | bytes 8388608
  88.4 5.9 %collective-permute-start.19 = (bf16[40,1792]{1,0:T(8,128)(2,1)S(1)}, bf16[40,1792]{1,0:T(8,128)(2,1)S(1)}, u32[]{:S(2)}, u32[]{:S(2)}) collective-permute-start(bf16[40,1792]{1,0:T(8,128)(2,1)S(1)} %get-tuple-element.106), channel_id=1, source_target_pairs={{0,2},{1,3},{2,0},{3,1},{4,6},{5,7},{6,4},{7,5},{8,10},{9,11},{10,... | collective-permute-start | bytes 430088 | tf_op jit(solution)/shard_map/ppermute | solution.py:51
  90.5 11.2 %collective-permute-start.25 = (bf16[40,2304]{1,0:T(8,128)(2,1)S(1)}, bf16[40,2304]{1,0:T(8,128)(2,1)S(1)}, u32[]{:S(2)}, u32[]{:S(2)}) collective-permute-start(bf16[40,2304]{1,0:T(8,128)(2,1)S(1)} %fusion.42), channel_id=1, source_target_pairs={{0,8},{4,12},{8,0},{12,4},{1,9},{5,13},{9,1},{13,5},{2,10},{6,14},... | collective-permute-start | bytes 552968 | tf_op jit(solution)/shard_map/ppermute | solution.py:51
  90.7 11.9 %collective-permute-start.24 = (bf16[2,40,1280]{2,1,0:T(8,128)(2,1)S(1)}, bf16[2,40,1280]{2,1,0:T(8,128)(2,1)S(1)}, u32[]{:S(2)}, u32[]{:S(2)}) collective-permute-start(bf16[2,40,1280]{2,1,0:T(8,128)(2,1)S(1)} %pad_maximum_fusion.16), channel_id=1, source_target_pairs={{0,2},{1,3},{2,0},{3,1},{4,6},{5,7},{6,4},{7,5},{8,10},{9,11},{10,... | collective-permute-start | bytes 614408 | tf_op jit(solution)/shard_map/ppermute | solution.py:51
  94.3 9.9 %collective-permute-start.26 = (bf16[80,1792]{1,0:T(8,128)(2,1)S(1)}, bf16[80,1792]{1,0:T(8,128)(2,1)S(1)}, u32[]{:S(2)}, u32[]{:S(2)}) collective-permute-start(bf16[80,1792]{1,0:T(8,128)(2,1)S(1)} %pad_maximum_fusion.15), channel_id=1, source_target_pairs={{0,4},{1,0},{2,6},{3,2},{4,5},{5,1},{6,7},{7,3},{8,12},{9,8},{10,1... | collective-permute-start | bytes 860168 | tf_op jit(solution)/shard_map/ppermute | solution.py:128
  96.1 8.2 %collective-permute-start.27 = (bf16[80,1792]{1,0:T(8,128)(2,1)S(1)}, bf16[80,1792]{1,0:T(8,128)(2,1)S(1)}, u32[]{:S(2)}, u32[]{:S(2)}) collective-permute-start(bf16[80,1792]{1,0:T(8,128)(2,1)S(1)} %pad_maximum_fusion.15), channel_id=1, source_target_pairs={{1,4},{3,6},{4,1},{6,3},{9,12},{11,14},{12,9},{14,11},{17,20},{19,... | collective-permute-start | bytes 860168 | tf_op jit(solution)/shard_map/ppermute | solution.py:128
  101.7 6.6 %collective-permute-start.28 = (bf16[40,2304]{1,0:T(8,128)(2,1)S(1)}, bf16[40,2304]{1,0:T(8,128)(2,1)S(1)}, u32[]{:S(2)}, u32[]{:S(2)}) collective-permute-start(bf16[40,2304]{1,0:T(8,128)(2,1)S(1)} %get-tuple-element.88), channel_id=1, source_target_pairs={{0,2},{1,3},{2,0},{3,1},{4,6},{5,7},{6,4},{7,5},{8,10},{9,11},{10,... | collective-permute-start | bytes 552968 | tf_op jit(solution)/shard_map/ppermute | solution.py:51
  102.7 10.2 %collective-permute-start.30 = (bf16[40,1280]{1,0:T(8,128)(2,1)S(1)}, bf16[40,1280]{1,0:T(8,128)(2,1)S(1)}, u32[]{:S(2)}, u32[]{:S(2)}) collective-permute-start(bf16[40,1280]{1,0:T(8,128)(2,1)S(1)} %fusion.54), channel_id=1, source_target_pairs={{0,8},{4,12},{8,0},{12,4},{1,9},{5,13},{9,1},{13,5},{2,10},{6,14},... | collective-permute-start | bytes 307208 | tf_op jit(solution)/shard_map/ppermute | solution.py:51
  108.4 8.4 %collective-permute-start.32 = (bf16[80,2304]{1,0:T(8,128)(2,1)S(1)}, bf16[80,2304]{1,0:T(8,128)(2,1)S(1)}, u32[]{:S(2)}, u32[]{:S(2)}) collective-permute-start(bf16[80,2304]{1,0:T(8,128)(2,1)S(1)} %pad_maximum_fusion.9), channel_id=1, source_target_pairs={{0,4},{1,0},{2,6},{3,2},{4,5},{5,1},{6,7},{7,3},{8,12},{9,8},{10,1... | collective-permute-start | bytes 1105928 | tf_op jit(solution)/shard_map/ppermute | solution.py:128
  109.2 7.6 %collective-permute-start.33 = (bf16[80,2304]{1,0:T(8,128)(2,1)S(1)}, bf16[80,2304]{1,0:T(8,128)(2,1)S(1)}, u32[]{:S(2)}, u32[]{:S(2)}) collective-permute-start(bf16[80,2304]{1,0:T(8,128)(2,1)S(1)} %pad_maximum_fusion.9), channel_id=1, source_target_pairs={{1,4},{3,6},{4,1},{6,3},{9,12},{11,14},{12,9},{14,11},{17,20},{19,... | collective-permute-start | bytes 1105928 | tf_op jit(solution)/shard_map/ppermute | solution.py:128
  111.4 2.9 %collective-permute-start.29 = (bf16[80,2048]{1,0:T(8,128)(2,1)S(1)}, bf16[80,2048]{1,0:T(8,128)(2,1)S(1)}, u32[]{:S(2)}, u32[]{:S(2)}) collective-permute-start(bf16[80,2048]{1,0:T(8,128)(2,1)S(1)} %slice.504), channel_id=1, source_target_pairs={{0,1},{1,0},{2,3},{3,2},{4,5},{5,4},{6,7},{7,6},{8,9},{9,8},{10,11... | collective-permute-start | bytes 983048 | tf_op jit(solution)/shard_map/ppermute | solution.py:51
  112.9 5.7 %collective-permute-start.34 = (bf16[40,1280]{1,0:T(8,128)(2,1)S(1)}, bf16[40,1280]{1,0:T(8,128)(2,1)S(1)}, u32[]{:S(2)}, u32[]{:S(2)}) collective-permute-start(bf16[40,1280]{1,0:T(8,128)(2,1)S(1)} %get-tuple-element.112), channel_id=1, source_target_pairs={{0,2},{1,3},{2,0},{3,1},{4,6},{5,7},{6,4},{7,5},{8,10},{9,11},{10,... | collective-permute-start | bytes 307208 | tf_op jit(solution)/shard_map/ppermute | solution.py:51
  118.7 8.0 %collective-permute-start.35 = (bf16[80,1280]{1,0:T(8,128)(2,1)S(1)}, bf16[80,1280]{1,0:T(8,128)(2,1)S(1)}, u32[]{:S(2)}, u32[]{:S(2)}) collective-permute-start(bf16[80,1280]{1,0:T(8,128)(2,1)S(1)} %pad_maximum_fusion.17), channel_id=1, source_target_pairs={{0,4},{1,0},{2,6},{3,2},{4,5},{5,1},{6,7},{7,3},{8,12},{9,8},{10,1... | collective-permute-start | bytes 614408 | tf_op jit(solution)/shard_map/ppermute | solution.py:128
  122.6 4.1 %collective-permute-start.36 = (bf16[80,1280]{1,0:T(8,128)(2,1)S(1)}, bf16[80,1280]{1,0:T(8,128)(2,1)S(1)}, u32[]{:S(2)}, u32[]{:S(2)}) collective-permute-start(bf16[80,1280]{1,0:T(8,128)(2,1)S(1)} %pad_maximum_fusion.17), channel_id=1, source_target_pairs={{1,4},{3,6},{4,1},{6,3},{9,12},{11,14},{12,9},{14,11},{17,20},{19,... | collective-permute-start | bytes 614408 | tf_op jit(solution)/shard_map/ppermute | solution.py:128
  123.3 10.3 %collective-permute-start.31 = (bf16[80,2048]{1,0:T(8,128)(2,1)S(1)}, bf16[80,2048]{1,0:T(8,128)(2,1)S(1)}, u32[]{:S(2)}, u32[]{:S(2)}) collective-permute-start(bf16[80,2048]{1,0:T(8,128)(2,1)S(1)} %get-tuple-element.73), channel_id=1, source_target_pairs={{0,2},{1,3},{2,0},{3,1},{4,6},{5,7},{6,4},{7,5},{8,10},{9,11},{10,... | collective-permute-start | bytes 983048 | tf_op jit(solution)/shard_map/ppermute | solution.py:51
  127.9 5.7 %collective-permute-start.37 = (bf16[80,2048]{1,0:T(8,128)(2,1)S(1)}, bf16[80,2048]{1,0:T(8,128)(2,1)S(1)}, u32[]{:S(2)}, u32[]{:S(2)}) collective-permute-start(bf16[80,2048]{1,0:T(8,128)(2,1)S(1)} %slice.503), channel_id=1, source_target_pairs={{0,1},{1,0},{2,3},{3,2},{4,5},{5,4},{6,7},{7,6},{8,9},{9,8},{10,11... | collective-permute-start | bytes 983048 | tf_op jit(solution)/shard_map/ppermute | solution.py:51
  133.7 9.8 %collective-permute-start.38 = (bf16[80,2048]{1,0:T(8,128)(2,1)S(1)}, bf16[80,2048]{1,0:T(8,128)(2,1)S(1)}, u32[]{:S(2)}, u32[]{:S(2)}) collective-permute-start(bf16[80,2048]{1,0:T(8,128)(2,1)S(1)} %fusion.35), channel_id=1, source_target_pairs={{0,2},{1,3},{2,0},{3,1},{4,6},{5,7},{6,4},{7,5},{8,10},{9,11},{10,... | collective-permute-start | bytes 983048 | tf_op jit(solution)/shard_map/ppermute | solution.py:51
  135.2 9.4 %collective-permute-start.39 = (bf16[80,2048]{1,0:T(8,128)(2,1)S(1)}, bf16[80,2048]{1,0:T(8,128)(2,1)S(1)}, u32[]{:S(2)}, u32[]{:S(2)}) collective-permute-start(bf16[80,2048]{1,0:T(8,128)(2,1)S(1)} %get-tuple-element.69), channel_id=1, source_target_pairs={{0,1},{1,0},{2,3},{3,2},{4,5},{5,4},{6,7},{7,6},{8,9},{9,8},{10,11... | collective-permute-start | bytes 983048 | tf_op jit(solution)/shard_map/ppermute | solution.py:51
  143.7 1.7 %collective-permute-start.40 = (bf16[80,2048]{1,0:T(8,128)(2,1)S(1)}, bf16[80,2048]{1,0:T(8,128)(2,1)S(1)}, u32[]{:S(2)}, u32[]{:S(2)}) collective-permute-start(bf16[80,2048]{1,0:T(8,128)(2,1)S(1)} %get-tuple-element.71), channel_id=1, source_target_pairs={{0,1},{1,0},{2,3},{3,2},{4,5},{5,4},{6,7},{7,6},{8,9},{9,8},{10,11... | collective-permute-start | bytes 983048 | tf_op jit(solution)/shard_map/ppermute | solution.py:51

commit v21 on v20

--- a/solution.py
+++ b/solution.py
@@ -38,6 +38,8 @@
     "c10.cores": ["b0.total"],
     "c11.columns": ["c10.down"],
     "b0.total": ["c11.halves"],
+    "c11.cores": ["b0.all"],
+    "c11.down": ["b0.all"],
     "b1.total": ["c11.down"],
 }
 

time: 147 us -> 139 us (0.946)
  matrix products: 33.8 us -> 25.6 us
  waiting for transfers between devices: 52.9 us -> 48.1 us
  starting transfers between devices: 46.4 us -> 50.4 us
  other arithmetic: 5.03 us -> 6.89 us
    dot_general x17, matrix products: 33 us -> 24.8 us  [dot(): return jnp.dot(a, b, preferred_element_type=jnp.float32)]
    ppermute x29, starting transfers between devices: 31 us -> 34.2 us  [flip(): return lax.ppermute(value, axis, [(i, i ^ bit) for i in range(count)])]
    ppermute x12, waiting for transfers between devices: 4.34 us -> 1.53 us  [move(): return lax.ppermute(value, ('row', 'col'), pairs)]
    ppermute x29, waiting for transfers between devices: 48.5 us -> 46.6 us  [flip(): return lax.ppermute(value, axis, [(i, i ^ bit) for i in range(count)])]
  transfers between devices with their start and end apart: 41 -> 41, of which waited for: 15 -> 17; matrix products, arithmetic and copies ran while one was open for 24% -> 20% of each run, Pallas kernels for 4% -> 4%
where the time goes in v21:
time: 139 us
  starting transfers between devices  50.4 us (36%)
  waiting for transfers between devices  48.1 us (35%)
  matrix products  25.6 us (18%)
  other arithmetic  6.89 us (5%)
  Pallas kernels  5.99 us (4%)
    ppermute x29, waiting for transfers between devices, flip(): return lax.ppermute(value, axis, [(i, i ^ bit) for i in range(count)])  46.6 us
    ppermute x29, starting transfers between devices, flip(): return lax.ppermute(value, axis, [(i, i ^ bit) for i in range(count)])  34.2 us
    dot_general x17, matrix products, dot(): return jnp.dot(a, b, preferred_element_type=jnp.float32)  24.8 us
    ppermute x12, starting transfers between devices, move(): return lax.ppermute(value, ('row', 'col'), pairs)  16.1 us
    pallas_call x1, Pallas kernels, pull(): pl.pallas_call(functools.partial(pull_kernel, first, end), in_specs=[pl.B...  5.99 us
  transfers between devices with their start and end apart: 41, of which 17 were waited for; matrix products, arithmetic and copies ran while one was open for 20% of the time, Pallas kernels for 4%

profile of v21, /device:TPU:0, one launch (start us, length us, event | category | flops | bytes accessed | tf_op | source)
XLA Modules:
  0.0 138.9 jit_solution(272803706334679392)
XLA Ops:
  0.5 0.9 fusion.80
  1.5 1.4 fusion.70
  3.2 2.6 %collective-permute-start.1 = (bf16[40,2048]{1,0:T(8,128)(2,1)S(1)}, bf16[40,2048]{1,0:T(8,128)(2,1)S(1)}, u32[]{:S(2)}, u32[]{:S(2)}) collective-permute-start(bf16[40,2048]{1,0:T(8,128)(2,1)S(1)} %slice.314), channel_id=1, source_target_pairs={{0,2},{1,3},{2,0},{3,1},{4,6},{5,7},{6,4},{7,5},{8,10},{9,11},{10,... | collective-permute-start | bytes 491528 | tf_op jit(solution)/shard_map/ppermute | solution.py:53
  5.8 4.9 %collective-permute-done.1 = bf16[40,2048]{1,0:T(8,128)(2,1)S(1)} collective-permute-done((bf16[40,2048]{1,0:T(8,128)(2,1)S(1)}, bf16[40,2048]{1,0:T(8,128)(2,1)S(1)}, u32[]{:S(2)}, u32[]{:S(2)}) %collective-permute-start.1) | collective-permute-done | bytes 163872 | tf_op jit(solution)/shard_map/ppermute | solution.py:53
  10.7 2.9 %collective-permute-start.2 = (bf16[40,2048]{1,0:T(8,128)(2,1)S(1)}, bf16[40,2048]{1,0:T(8,128)(2,1)S(1)}, u32[]{:S(2)}, u32[]{:S(2)}) collective-permute-start(bf16[40,2048]{1,0:T(8,128)(2,1)S(1)} %slice_add_fusion.19), channel_id=1, source_target_pairs={{0,8},{4,12},{8,0},{12,4},{1,9},{5,13},{9,1},{13,5},{2,10},{6,14},... | collective-permute-start | bytes 491528 | tf_op jit(solution)/shard_map/ppermute | solution.py:53
  14.2 1.6 %collective-permute-start.6 = (bf16[40,2048]{1,0:T(8,128)(2,1)S(1)}, bf16[40,2048]{1,0:T(8,128)(2,1)S(1)}, u32[]{:S(2)}, u32[]{:S(2)}) collective-permute-start(bf16[40,2048]{1,0:T(8,128)(2,1)S(1)} %slice.316), channel_id=1, source_target_pairs={{0,2},{1,3},{2,0},{3,1},{4,6},{5,7},{6,4},{7,5},{8,10},{9,11},{10,... | collective-permute-start | bytes 491528 | tf_op jit(solution)/shard_map/ppermute | solution.py:53
  15.8 5.4 %collective-permute-done.2 = bf16[40,2048]{1,0:T(8,128)(2,1)S(1)} collective-permute-done((bf16[40,2048]{1,0:T(8,128)(2,1)S(1)}, bf16[40,2048]{1,0:T(8,128)(2,1)S(1)}, u32[]{:S(2)}, u32[]{:S(2)}) %collective-permute-start.2) | collective-permute-done | bytes 163872 | tf_op jit(solution)/shard_map/ppermute | solution.py:53
  21.2 1.6 %collective-permute-start.3 = (bf16[40,2048]{1,0:T(8,128)(2,1)S(1)}, bf16[40,2048]{1,0:T(8,128)(2,1)S(1)}, u32[]{:S(2)}, u32[]{:S(2)}) collective-permute-start(bf16[40,2048]{1,0:T(8,128)(2,1)S(1)} %get-tuple-element.104), channel_id=1, source_target_pairs={{0,2},{1,3},{2,0},{3,1},{4,6},{5,7},{6,4},{7,5},{8,10},{9,11},{10,... | collective-permute-start | bytes 491528 | tf_op jit(solution)/shard_map/ppermute | solution.py:53
  22.9 3.7 %collective-permute-done.3 = bf16[40,2048]{1,0:T(8,128)(2,1)S(1)} collective-permute-done((bf16[40,2048]{1,0:T(8,128)(2,1)S(1)}, bf16[40,2048]{1,0:T(8,128)(2,1)S(1)}, u32[]{:S(2)}, u32[]{:S(2)}) %collective-permute-start.3) | collective-permute-done | bytes 163872 | tf_op jit(solution)/shard_map/ppermute | solution.py:53
  26.6 1.6 %collective-permute-start.4 = (bf16[80,2048]{1,0:T(8,128)(2,1)S(1)}, bf16[80,2048]{1,0:T(8,128)(2,1)S(1)}, u32[]{:S(2)}, u32[]{:S(2)}) collective-permute-start(bf16[80,2048]{1,0:T(8,128)(2,1)S(1)} %pad_maximum_fusion.11), channel_id=1, source_target_pairs={{0,4},{1,0},{2,6},{3,2},{4,5},{5,1},{6,7},{7,3},{8,12},{9,8},{10,1... | collective-permute-start | bytes 983048 | tf_op jit(solution)/shard_map/ppermute | solution.py:130
  28.2 0.7 collective-permute-start.5
  28.9 3.5 %collective-permute-done.7 = bf16[40,2048]{1,0:T(8,128)(2,1)S(1)} collective-permute-done((bf16[40,2048]{1,0:T(8,128)(2,1)S(1)}, bf16[40,2048]{1,0:T(8,128)(2,1)S(1)}, u32[]{:S(2)}, u32[]{:S(2)}) %collective-permute-start.7) | collective-permute-done | bytes 163872 | tf_op jit(solution)/shard_map/ppermute | solution.py:53
  33.0 6.0 %shard_map.55 = (bf16[2048,1792]{1,0:T(8,128)(2,1)S(1)}, bf16[2048,1792]{1,0:T(8,128)(2,1)S(1)}) custom-call(s32[4]{0:T(128)S(1)} %copy-done, bf16[2048,3584]{1,0:T(8,128)(2,1)} %gate_ref.1, bf16[2048,3584]{1,0:T(8,128)(2,1)} %up_ref.1), custom_call_target="tpu_custom_call" | custom-call | tf_op jit(solution)/shard_map/pallas_call | solution.py:73
  39.2 1.4 %fusion.93 = f32[160,1792]{1,0:T(8,128)S(1)} fusion(bf16[160,2048]{1,0:T(8,128)(2,1)S(1)} %pad_maximum_fusion.1, bf16[2048,1792]{1,0:T(8,128)(2,1)S(1)} %get-tuple-element.39), kind=kOutput, calls=%fused_computation.197 | convolution fusion | flops 1174405120 | bytes 9142272 | tf_op jit(solution)/shard_map/dot_general | solution.py:48
  40.6 1.4 %fusion.94 = f32[160,1792]{1,0:T(8,128)S(1)} fusion(bf16[160,2048]{1,0:T(8,128)(2,1)S(1)} %pad_maximum_fusion.1, bf16[2048,1792]{1,0:T(8,128)(2,1)S(1)} %get-tuple-element.44), kind=kOutput, calls=%fused_computation.198 | convolution fusion | flops 1174405120 | bytes 9142272 | tf_op jit(solution)/shard_map/dot_general | solution.py:48
  42.3 1.0 collective-permute-start.12
  43.3 0.9 collective-permute-done.9
  44.4 0.7 pad_maximum_fusion.13
  45.2 1.4 %fusion.12 = f32[160,1792]{1,0:T(8,128)S(1)} fusion(bf16[160,2048]{1,0:T(8,128)(2,1)S(1)} %pad_maximum_fusion.1, bf16[2048,3584]{1,0:T(8,128)(2,1)S(1)} %bitcast.110), kind=kOutput, calls=%fused_computation.12 | convolution fusion | flops 1174405120 | bytes 9142272 | tf_op jit(solution)/shard_map/dot_general | solution.py:48
  47.0 1.4 %fusion.10 = f32[160,1792]{1,0:T(8,128)S(1)} fusion(bf16[160,2048]{1,0:T(8,128)(2,1)S(1)} %pad_maximum_fusion.1, bf16[2048,3584]{1,0:T(8,128)(2,1)S(1)} %bitcast.108), kind=kOutput, calls=%fused_computation.10 | convolution fusion | flops 1174405120 | bytes 9142272 | tf_op jit(solution)/shard_map/dot_general | solution.py:48
  48.6 0.7 collective-permute-start.13
  49.4 1.5 %collective-permute-start.10 = (bf16[2,40,1792]{2,1,0:T(8,128)(2,1)}, bf16[2,40,1792]{2,1,0:T(8,128)(2,1)}, u32[]{:S(2)}, u32[]{:S(2)}) collective-permute-start(bf16[2,40,1792]{2,1,0:T(8,128)(2,1)} %pad_maximum_fusion.13), channel_id=1, source_target_pairs={{0,2},{1,3},{2,0},{3,1},{4,6},{5,7},{6,4},{7,5},{8,10},{9,11},{10,... | collective-permute-start | bytes 860168 | tf_op jit(solution)/shard_map/ppermute | solution.py:53
  51.0 0.8 pad_maximum_fusion.14
  51.8 1.7 %fusion.4 = f32[160,2304]{1,0:T(8,128)S(1)} fusion(bf16[160,2048]{1,0:T(8,128)(2,1)S(1)} %pad_maximum_fusion.2, bf16[2048,3584]{1,0:T(8,128)(2,1)S(1)} %bitcast.110), kind=kOutput, calls=%fused_computation.4 | convolution fusion | flops 1509949440 | bytes 11567104 | tf_op jit(solution)/shard_map/dot_general | solution.py:48
  53.5 2.9 %fusion.2 = f32[160,2304]{1,0:T(8,128)S(1)} fusion(bf16[160,2048]{1,0:T(8,128)(2,1)} %copy-done.2, bf16[2048,3584]{1,0:T(8,128)(2,1)S(1)} %bitcast.108), kind=kOutput, calls=%fused_computation.2 | convolution fusion | flops 1509949440 | bytes 11567104 | tf_op jit(solution)/shard_map/dot_general | solution.py:48
  56.6 2.8 %collective-permute-start.17 = (bf16[2,80,2304]{2,1,0:T(8,128)(2,1)S(1)}, bf16[2,80,2304]{2,1,0:T(8,128)(2,1)S(1)}, u32[]{:S(2)}, u32[]{:S(2)}) collective-permute-start(bf16[2,80,2304]{2,1,0:T(8,128)(2,1)S(1)} %pad_maximum_fusion), channel_id=1, source_target_pairs={{0,1},{1,0},{2,3},{3,2},{4,5},{5,4},{6,7},{7,6},{8,9},{9,8},{10,11... | collective-permute-start | bytes 2211848 | tf_op jit(solution)/shard_map/ppermute | solution.py:53
  59.4 1.1 fusion.47
  60.5 3.3 %collective-permute-start.14 = (bf16[40,1792]{1,0:T(8,128)(2,1)S(1)}, bf16[40,1792]{1,0:T(8,128)(2,1)S(1)}, u32[]{:S(2)}, u32[]{:S(2)}) collective-permute-start(bf16[40,1792]{1,0:T(8,128)(2,1)S(1)} %fusion.47), channel_id=1, source_target_pairs={{0,8},{4,12},{8,0},{12,4},{1,9},{5,13},{9,1},{13,5},{2,10},{6,14},... | collective-permute-start | bytes 430088 | tf_op jit(solution)/shard_map/ppermute | solution.py:53
  63.8 1.5 %collective-permute-start.16 = (bf16[2,40,1792]{2,1,0:T(8,128)(2,1)S(1)}, bf16[2,40,1792]{2,1,0:T(8,128)(2,1)S(1)}, u32[]{:S(2)}, u32[]{:S(2)}) collective-permute-start(bf16[2,40,1792]{2,1,0:T(8,128)(2,1)S(1)} %copy-done.4), channel_id=1, source_target_pairs={{0,2},{1,3},{2,0},{3,1},{4,6},{5,7},{6,4},{7,5},{8,10},{9,11},{10,... | collective-permute-start | bytes 860168 | tf_op jit(solution)/shard_map/ppermute | solution.py:53
  65.3 5.6 %collective-permute-done.14 = bf16[40,1792]{1,0:T(8,128)(2,1)S(1)} collective-permute-done((bf16[40,1792]{1,0:T(8,128)(2,1)S(1)}, bf16[40,1792]{1,0:T(8,128)(2,1)S(1)}, u32[]{:S(2)}, u32[]{:S(2)}) %collective-permute-start.14) | collective-permute-done | bytes 143392 | tf_op jit(solution)/shard_map/ppermute | solution.py:53
  70.9 1.4 %collective-permute-start.15 = (bf16[40,1792]{1,0:T(8,128)(2,1)S(1)}, bf16[40,1792]{1,0:T(8,128)(2,1)S(1)}, u32[]{:S(2)}, u32[]{:S(2)}) collective-permute-start(bf16[40,1792]{1,0:T(8,128)(2,1)S(1)} %get-tuple-element.112), channel_id=1, source_target_pairs={{0,2},{1,3},{2,0},{3,1},{4,6},{5,7},{6,4},{7,5},{8,10},{9,11},{10,... | collective-permute-start | bytes 430088 | tf_op jit(solution)/shard_map/ppermute | solution.py:53
  72.5 0.8 collective-permute-start.21
  73.5 1.1 fusion.16
  74.6 1.1 fusion.18
  75.9 1.7 %collective-permute-done.15 = bf16[40,1792]{1,0:T(8,128)(2,1)S(1)} collective-permute-done((bf16[40,1792]{1,0:T(8,128)(2,1)S(1)}, bf16[40,1792]{1,0:T(8,128)(2,1)S(1)}, u32[]{:S(2)}, u32[]{:S(2)}) %collective-permute-start.15) | collective-permute-done | bytes 143392 | tf_op jit(solution)/shard_map/ppermute | solution.py:53
  77.6 2.4 %collective-permute-start.22 = (bf16[80,1792]{1,0:T(8,128)(2,1)S(1)}, bf16[80,1792]{1,0:T(8,128)(2,1)S(1)}, u32[]{:S(2)}, u32[]{:S(2)}) collective-permute-start(bf16[80,1792]{1,0:T(8,128)(2,1)S(1)} %pad_maximum_fusion.15), channel_id=1, source_target_pairs={{0,4},{1,0},{2,6},{3,2},{4,5},{5,1},{6,7},{7,3},{8,12},{9,8},{10,1... | collective-permute-start | bytes 860168 | tf_op jit(solution)/shard_map/ppermute | solution.py:130
  80.6 1.7 %collective-permute-done.18 = bf16[40,1792]{1,0:T(8,128)(2,1)S(1)} collective-permute-done((bf16[40,1792]{1,0:T(8,128)(2,1)S(1)}, bf16[40,1792]{1,0:T(8,128)(2,1)S(1)}, u32[]{:S(2)}, u32[]{:S(2)}) %collective-permute-start.18) | collective-permute-done | bytes 143392 | tf_op jit(solution)/shard_map/ppermute | solution.py:53
  82.4 1.4 collective-permute-start.19
  84.6 1.8 %collective-permute-start.24 = (bf16[2,40,1280]{2,1,0:T(8,128)(2,1)S(1)}, bf16[2,40,1280]{2,1,0:T(8,128)(2,1)S(1)}, u32[]{:S(2)}, u32[]{:S(2)}) collective-permute-start(bf16[2,40,1280]{2,1,0:T(8,128)(2,1)S(1)} %pad_maximum_fusion.17), channel_id=1, source_target_pairs={{0,2},{1,3},{2,0},{3,1},{4,6},{5,7},{6,4},{7,5},{8,10},{9,11},{10,... | collective-permute-start | bytes 614408 | tf_op jit(solution)/shard_map/ppermute | solution.py:53
  86.4 2.7 %collective-permute-done.19 = bf16[40,1792]{1,0:T(8,128)(2,1)S(1)} collective-permute-done((bf16[40,1792]{1,0:T(8,128)(2,1)S(1)}, bf16[40,1792]{1,0:T(8,128)(2,1)S(1)}, u32[]{:S(2)}, u32[]{:S(2)}) %collective-permute-start.19) | collective-permute-done | bytes 143392 | tf_op jit(solution)/shard_map/ppermute | solution.py:53
  89.1 1.0 collective-permute-start.26
  90.9 4.3 %collective-permute-done.25 = bf16[40,2304]{1,0:T(8,128)(2,1)S(1)} collective-permute-done((bf16[40,2304]{1,0:T(8,128)(2,1)S(1)}, bf16[40,2304]{1,0:T(8,128)(2,1)S(1)}, u32[]{:S(2)}, u32[]{:S(2)}) %collective-permute-start.25) | collective-permute-done | bytes 184352 | tf_op jit(solution)/shard_map/ppermute | solution.py:53
  95.2 1.4 %collective-permute-start.28 = (bf16[40,2304]{1,0:T(8,128)(2,1)S(1)}, bf16[40,2304]{1,0:T(8,128)(2,1)S(1)}, u32[]{:S(2)}, u32[]{:S(2)}) collective-permute-start(bf16[40,2304]{1,0:T(8,128)(2,1)S(1)} %get-tuple-element.92), channel_id=1, source_target_pairs={{0,2},{1,3},{2,0},{3,1},{4,6},{5,7},{6,4},{7,5},{8,10},{9,11},{10,... | collective-permute-start | bytes 552968 | tf_op jit(solution)/shard_map/ppermute | solution.py:53
  96.8 4.6 %fusion.8 = f32[160,2048]{1,0:T(8,128)S(1)} fusion(bf16[160,1792]{1,0:T(8,128)(2,1)S(1)} %pad_maximum_fusion.5, bf16[3584,2048]{1,0:T(8,128)(2,1)} %param.9), kind=kOutput, calls=%fused_computation.8 | convolution fusion | flops 1174405120 | bytes 9224192 | tf_op jit(solution)/shard_map/dot_general | solution.py:48
  101.6 2.7 %collective-permute-start.32 = (bf16[80,2304]{1,0:T(8,128)(2,1)S(1)}, bf16[80,2304]{1,0:T(8,128)(2,1)S(1)}, u32[]{:S(2)}, u32[]{:S(2)}) collective-permute-start(bf16[80,2304]{1,0:T(8,128)(2,1)S(1)} %pad_maximum_fusion.10), channel_id=1, source_target_pairs={{0,4},{1,0},{2,6},{3,2},{4,5},{5,1},{6,7},{7,3},{8,12},{9,8},{10,1... | collective-permute-start | bytes 1105928 | tf_op jit(solution)/shard_map/ppermute | solution.py:130
  104.2 0.9 collective-permute-start.33
  105.2 1.5 %fusion.91 = f32[160,2048]{1,0:T(8,128)S(1)} fusion(f32[160,2048]{1,0:T(8,128)S(1)} %fusion.8, bf16[160,1792]{1,0:T(8,128)(2,1)S(1)} %pad_maximum_fusion.6, bf16[3584,2048]{1,0:T(8,128)(2,1)S(1)} %bitcast.119), kind=kOutput, calls=%fused_computation.195 | convolution fusion | flops 1174732800 | bytes 10534912 | tf_op jit(solution)/shard_map/dot_general | solution.py:48
  106.7 1.4 %collective-permute-start.29 = (bf16[80,2048]{1,0:T(8,128)(2,1)S(1)}, bf16[80,2048]{1,0:T(8,128)(2,1)S(1)}, u32[]{:S(2)}, u32[]{:S(2)}) collective-permute-start(bf16[80,2048]{1,0:T(8,128)(2,1)S(1)} %slice.504), channel_id=1, source_target_pairs={{0,1},{1,0},{2,3},{3,2},{4,5},{5,4},{6,7},{7,6},{8,9},{9,8},{10,11... | collective-permute-start | bytes 983048 | tf_op jit(solution)/shard_map/ppermute | solution.py:53
  108.2 1.6 %collective-permute-start.34 = (bf16[40,1280]{1,0:T(8,128)(2,1)S(1)}, bf16[40,1280]{1,0:T(8,128)(2,1)S(1)}, u32[]{:S(2)}, u32[]{:S(2)}) collective-permute-start(bf16[40,1280]{1,0:T(8,128)(2,1)S(1)} %get-tuple-element.116), channel_id=1, source_target_pairs={{0,2},{1,3},{2,0},{3,1},{4,6},{5,7},{6,4},{7,5},{8,10},{9,11},{10,... | collective-permute-start | bytes 307208 | tf_op jit(solution)/shard_map/ppermute | solution.py:53
  109.9 1.2 collective-permute-start.31
  111.1 0.7 collective-permute-done.32
  111.9 1.7 %fusion = f32[160,2048]{1,0:T(8,128)S(1)} fusion(bf16[3584,2048]{1,0:T(8,128)(2,1)S(1)} %bitcast.119, bf16[80,2304]{1,0:T(8,128)(2,1)S(1)} %get-tuple-element.90, bf16[80,2304]{1,0:T(8,128)(2,1)S(1)} %get-tuple-element.89), kind=kOutput, calls=%fused_computation | convolution fusion | flops 1511424000 | bytes 11485184 | tf_op jit(solution)/shard_map/dot_general | solution.py:48
  113.7 3.9 %collective-permute-start.35 = (bf16[80,1280]{1,0:T(8,128)(2,1)S(1)}, bf16[80,1280]{1,0:T(8,128)(2,1)S(1)}, u32[]{:S(2)}, u32[]{:S(2)}) collective-permute-start(bf16[80,1280]{1,0:T(8,128)(2,1)S(1)} %pad_maximum_fusion.18), channel_id=1, source_target_pairs={{0,4},{1,0},{2,6},{3,2},{4,5},{5,1},{6,7},{7,3},{8,12},{9,8},{10,1... | collective-permute-start | bytes 614408 | tf_op jit(solution)/shard_map/ppermute | solution.py:130
  118.3 1.8 %collective-permute-done.31 = bf16[80,2048]{1,0:T(8,128)(2,1)S(1)} collective-permute-done((bf16[80,2048]{1,0:T(8,128)(2,1)S(1)}, bf16[80,2048]{1,0:T(8,128)(2,1)S(1)}, u32[]{:S(2)}, u32[]{:S(2)}) %collective-permute-start.31) | collective-permute-done | bytes 327712 | tf_op jit(solution)/shard_map/ppermute | solution.py:53
  120.1 0.8 fusion.85
  120.9 0.8 collective-permute-done.35
  121.8 1.1 fusion.92
  122.9 1.6 %collective-permute-start.37 = (bf16[80,2048]{1,0:T(8,128)(2,1)S(1)}, bf16[80,2048]{1,0:T(8,128)(2,1)S(1)}, u32[]{:S(2)}, u32[]{:S(2)}) collective-permute-start(bf16[80,2048]{1,0:T(8,128)(2,1)S(1)} %slice.503), channel_id=1, source_target_pairs={{0,1},{1,0},{2,3},{3,2},{4,5},{5,4},{6,7},{7,6},{8,9},{9,8},{10,11... | collective-permute-start | bytes 983048 | tf_op jit(solution)/shard_map/ppermute | solution.py:53
  124.5 1.2 collective-permute-done.37
  125.8 1.7 %collective-permute-start.38 = (bf16[80,2048]{1,0:T(8,128)(2,1)S(1)}, bf16[80,2048]{1,0:T(8,128)(2,1)S(1)}, u32[]{:S(2)}, u32[]{:S(2)}) collective-permute-start(bf16[80,2048]{1,0:T(8,128)(2,1)S(1)} %fusion.35), channel_id=1, source_target_pairs={{0,2},{1,3},{2,0},{3,1},{4,6},{5,7},{6,4},{7,5},{8,10},{9,11},{10,... | collective-permute-start | bytes 983048 | tf_op jit(solution)/shard_map/ppermute | solution.py:53
  127.6 8.2 %collective-permute-done.38 = bf16[80,2048]{1,0:T(8,128)(2,1)S(1)} collective-permute-done((bf16[80,2048]{1,0:T(8,128)(2,1)S(1)}, bf16[80,2048]{1,0:T(8,128)(2,1)S(1)}, u32[]{:S(2)}, u32[]{:S(2)}) %collective-permute-start.38) | collective-permute-done | bytes 327712 | tf_op jit(solution)/shard_map/ppermute | solution.py:53
  136.1 0.8 fusion.25
  137.0 0.7 collective-permute-done.40
  137.7 1.3 fusion.22
  (152 shorter events, 8.7 us)
Async XLA Ops:
  0.0 2.9 %collective-permute-start = (bf16[160,2048]{1,0:T(8,128)(2,1)}, bf16[160,2048]{1,0:T(8,128)(2,1)S(1)}, u32[]{:S(2)}, u32[]{:S(2)}) collective-permute-start(bf16[160,2048]{1,0:T(8,128)(2,1)} %param.5), channel_id=1, source_target_pairs={{0,1},{1,0},{2,3},{3,2},{4,5},{5,4},{6,7},{7,6},{8,9},{9,8},{10,11... | collective-permute-start | bytes 1966088 | tf_op jit(solution)/shard_map/ppermute | solution.py:53
  2.9 10.7 %copy-start.1 = (bf16[160,2048]{1,0:T(8,128)(2,1)S(1)}, bf16[160,2048]{1,0:T(8,128)(2,1)}, u32[]{:S(2)}) copy-start(bf16[160,2048]{1,0:T(8,128)(2,1)} %param.5) | copy-start | bytes 1966084
  3.2 7.4 %collective-permute-start.1 = (bf16[40,2048]{1,0:T(8,128)(2,1)S(1)}, bf16[40,2048]{1,0:T(8,128)(2,1)S(1)}, u32[]{:S(2)}, u32[]{:S(2)}) collective-permute-start(bf16[40,2048]{1,0:T(8,128)(2,1)S(1)} %slice.314), channel_id=1, source_target_pairs={{0,2},{1,3},{2,0},{3,1},{4,6},{5,7},{6,4},{7,5},{8,10},{9,11},{10,... | collective-permute-start | bytes 491528 | tf_op jit(solution)/shard_map/ppermute | solution.py:53
  10.7 10.5 %collective-permute-start.2 = (bf16[40,2048]{1,0:T(8,128)(2,1)S(1)}, bf16[40,2048]{1,0:T(8,128)(2,1)S(1)}, u32[]{:S(2)}, u32[]{:S(2)}) collective-permute-start(bf16[40,2048]{1,0:T(8,128)(2,1)S(1)} %slice_add_fusion.19), channel_id=1, source_target_pairs={{0,8},{4,12},{8,0},{12,4},{1,9},{5,13},{9,1},{13,5},{2,10},{6,14},... | collective-permute-start | bytes 491528 | tf_op jit(solution)/shard_map/ppermute | solution.py:53
  14.2 18.8 %copy-start = (s32[4]{0:T(128)S(1)}, s32[4]{0:T(128)}, u32[]{:S(2)}) copy-start(s32[4]{0:T(128)} %tick_ref) | copy-start | bytes 52
  14.2 8.6 %collective-permute-start.6 = (bf16[40,2048]{1,0:T(8,128)(2,1)S(1)}, bf16[40,2048]{1,0:T(8,128)(2,1)S(1)}, u32[]{:S(2)}, u32[]{:S(2)}) collective-permute-start(bf16[40,2048]{1,0:T(8,128)(2,1)S(1)} %slice.316), channel_id=1, source_target_pairs={{0,2},{1,3},{2,0},{3,1},{4,6},{5,7},{6,4},{7,5},{8,10},{9,11},{10,... | collective-permute-start | bytes 491528 | tf_op jit(solution)/shard_map/ppermute | solution.py:53
  21.2 5.4 %collective-permute-start.3 = (bf16[40,2048]{1,0:T(8,128)(2,1)S(1)}, bf16[40,2048]{1,0:T(8,128)(2,1)S(1)}, u32[]{:S(2)}, u32[]{:S(2)}) collective-permute-start(bf16[40,2048]{1,0:T(8,128)(2,1)S(1)} %get-tuple-element.104), channel_id=1, source_target_pairs={{0,2},{1,3},{2,0},{3,1},{4,6},{5,7},{6,4},{7,5},{8,10},{9,11},{10,... | collective-permute-start | bytes 491528 | tf_op jit(solution)/shard_map/ppermute | solution.py:53
  22.8 9.5 %collective-permute-start.7 = (bf16[40,2048]{1,0:T(8,128)(2,1)S(1)}, bf16[40,2048]{1,0:T(8,128)(2,1)S(1)}, u32[]{:S(2)}, u32[]{:S(2)}) collective-permute-start(bf16[40,2048]{1,0:T(8,128)(2,1)S(1)} %slice_add_fusion.18), channel_id=1, source_target_pairs={{0,8},{4,12},{8,0},{12,4},{1,9},{5,13},{9,1},{13,5},{2,10},{6,14},... | collective-permute-start | bytes 491528 | tf_op jit(solution)/shard_map/ppermute | solution.py:53
  26.6 12.4 %collective-permute-start.4 = (bf16[80,2048]{1,0:T(8,128)(2,1)S(1)}, bf16[80,2048]{1,0:T(8,128)(2,1)S(1)}, u32[]{:S(2)}, u32[]{:S(2)}) collective-permute-start(bf16[80,2048]{1,0:T(8,128)(2,1)S(1)} %pad_maximum_fusion.11), channel_id=1, source_target_pairs={{0,4},{1,0},{2,6},{3,2},{4,5},{5,1},{6,7},{7,3},{8,12},{9,8},{10,1... | collective-permute-start | bytes 983048 | tf_op jit(solution)/shard_map/ppermute | solution.py:130
  28.2 10.8 %collective-permute-start.5 = (bf16[80,2048]{1,0:T(8,128)(2,1)S(1)}, bf16[80,2048]{1,0:T(8,128)(2,1)S(1)}, u32[]{:S(2)}, u32[]{:S(2)}) collective-permute-start(bf16[80,2048]{1,0:T(8,128)(2,1)S(1)} %pad_maximum_fusion.11), channel_id=1, source_target_pairs={{1,4},{3,6},{4,1},{6,3},{9,12},{11,14},{12,9},{14,11},{17,20},{19,... | collective-permute-start | bytes 983048 | tf_op jit(solution)/shard_map/ppermute | solution.py:130
  32.4 6.8 %collective-permute-start.8 = (bf16[40,2048]{1,0:T(8,128)(2,1)S(1)}, bf16[40,2048]{1,0:T(8,128)(2,1)S(1)}, u32[]{:S(2)}, u32[]{:S(2)}) collective-permute-start(bf16[40,2048]{1,0:T(8,128)(2,1)S(1)} %get-tuple-element.100), channel_id=1, source_target_pairs={{0,2},{1,3},{2,0},{3,1},{4,6},{5,7},{6,4},{7,5},{8,10},{9,11},{10,... | collective-permute-start | bytes 491528 | tf_op jit(solution)/shard_map/ppermute | solution.py:53
  33.0 12.2 %slice-start.4 = ((s8[14680064]{0:T(1024)(128)(4,1)}), s8[4194304]{0:T(1024)(128)(4,1)S(1)}, s32[]{:S(2)}) async-start(s8[14680064]{0:T(1024)(128)(4,1)} %bitcast.109), calls=%async_computation.4 | async-start | bytes 8388608
  33.0 12.2 %slice-start.5 = ((s8[14680064]{0:T(1024)(128)(4,1)}), s8[4194304]{0:T(1024)(128)(4,1)S(1)}, s32[]{:S(2)}) async-start(s8[14680064]{0:T(1024)(128)(4,1)} %bitcast.109), calls=%async_computation.5 | async-start | bytes 8388608
  39.2 6.0 %slice-start.6 = ((s8[14680064]{0:T(1024)(128)(4,1)}), s8[4194304]{0:T(1024)(128)(4,1)S(1)}, s32[]{:S(2)}) async-start(s8[14680064]{0:T(1024)(128)(4,1)} %bitcast.109), calls=%async_computation.6 | async-start | bytes 8388608
  40.6 4.6 %slice-start.7 = ((s8[14680064]{0:T(1024)(128)(4,1)}), s8[2097152]{0:T(1024)(128)(4,1)S(1)}, s32[]{:S(2)}) async-start(s8[14680064]{0:T(1024)(128)(4,1)} %bitcast.109), calls=%async_computation.7 | async-start | bytes 4194304
  40.6 6.0 %slice-start = ((s8[14680064]{0:T(1024)(128)(4,1)}), s8[4194304]{0:T(1024)(128)(4,1)S(1)}, s32[]{:S(2)}) async-start(s8[14680064]{0:T(1024)(128)(4,1)} %bitcast.107), calls=%async_computation | async-start | bytes 8388608
  40.6 6.0 %slice-start.1 = ((s8[14680064]{0:T(1024)(128)(4,1)}), s8[4194304]{0:T(1024)(128)(4,1)S(1)}, s32[]{:S(2)}) async-start(s8[14680064]{0:T(1024)(128)(4,1)} %bitcast.107), calls=%async_computation.1 | async-start | bytes 8388608
  42.1 4.6 %slice-start.2 = ((s8[14680064]{0:T(1024)(128)(4,1)}), s8[4194304]{0:T(1024)(128)(4,1)S(1)}, s32[]{:S(2)}) async-start(s8[14680064]{0:T(1024)(128)(4,1)} %bitcast.107), calls=%async_computation.2 | async-start | bytes 8388608
  42.2 2.0 %collective-permute-start.9 = (bf16[2,80,1792]{2,1,0:T(8,128)(2,1)S(1)}, bf16[2,80,1792]{2,1,0:T(8,128)(2,1)S(1)}, u32[]{:S(2)}, u32[]{:S(2)}) collective-permute-start(bf16[2,80,1792]{2,1,0:T(8,128)(2,1)S(1)} %pad_maximum_fusion.3), channel_id=1, source_target_pairs={{0,1},{1,0},{2,3},{3,2},{4,5},{5,4},{6,7},{7,6},{8,9},{9,8},{10,11... | collective-permute-start | bytes 1720328 | tf_op jit(solution)/shard_map/ppermute | solution.py:53
  42.3 7.0 %collective-permute-start.11 = (bf16[80,2048]{1,0:T(8,128)(2,1)S(1)}, bf16[80,2048]{1,0:T(8,128)(2,1)S(1)}, u32[]{:S(2)}, u32[]{:S(2)}) collective-permute-start(bf16[80,2048]{1,0:T(8,128)(2,1)S(1)} %pad_maximum_fusion.12), channel_id=1, source_target_pairs={{0,4},{1,0},{2,6},{3,2},{4,5},{5,1},{6,7},{7,3},{8,12},{9,8},{10,1... | collective-permute-start | bytes 983048 | tf_op jit(solution)/shard_map/ppermute | solution.py:130
  42.3 6.9 %collective-permute-start.12 = (bf16[80,2048]{1,0:T(8,128)(2,1)S(1)}, bf16[80,2048]{1,0:T(8,128)(2,1)S(1)}, u32[]{:S(2)}, u32[]{:S(2)}) collective-permute-start(bf16[80,2048]{1,0:T(8,128)(2,1)S(1)} %pad_maximum_fusion.12), channel_id=1, source_target_pairs={{1,4},{3,6},{4,1},{6,3},{9,12},{11,14},{12,9},{14,11},{17,20},{19,... | collective-permute-start | bytes 983048 | tf_op jit(solution)/shard_map/ppermute | solution.py:130
  45.2 1.8 %slice-start.3 = ((s8[14680064]{0:T(1024)(128)(4,1)}), s8[2097152]{0:T(1024)(128)(4,1)S(1)}, s32[]{:S(2)}) async-start(s8[14680064]{0:T(1024)(128)(4,1)} %bitcast.107), calls=%async_computation.3 | async-start | bytes 4194304
  48.6 2.3 %collective-permute-start.13 = (bf16[2,80,1792]{2,1,0:T(8,128)(2,1)S(1)}, bf16[2,80,1792]{2,1,0:T(8,128)(2,1)S(1)}, u32[]{:S(2)}, u32[]{:S(2)}) collective-permute-start(bf16[2,80,1792]{2,1,0:T(8,128)(2,1)S(1)} %pad_maximum_fusion.4), channel_id=1, source_target_pairs={{0,1},{1,0},{2,3},{3,2},{4,5},{5,4},{6,7},{7,6},{8,9},{9,8},{10,11... | collective-permute-start | bytes 1720328 | tf_op jit(solution)/shard_map/ppermute | solution.py:53
  49.4 2.4 %copy-start.2 = (bf16[160,2048]{1,0:T(8,128)(2,1)}, bf16[160,2048]{1,0:T(8,128)(2,1)S(1)}, u32[]{:S(2)}) copy-start(bf16[160,2048]{1,0:T(8,128)(2,1)S(1)} %pad_maximum_fusion.2) | copy-start | bytes 1966084
  49.4 10.0 %collective-permute-start.10 = (bf16[2,40,1792]{2,1,0:T(8,128)(2,1)}, bf16[2,40,1792]{2,1,0:T(8,128)(2,1)}, u32[]{:S(2)}, u32[]{:S(2)}) collective-permute-start(bf16[2,40,1792]{2,1,0:T(8,128)(2,1)} %pad_maximum_fusion.13), channel_id=1, source_target_pairs={{0,2},{1,3},{2,0},{3,1},{4,6},{5,7},{6,4},{7,5},{8,10},{9,11},{10,... | collective-permute-start | bytes 860168 | tf_op jit(solution)/shard_map/ppermute | solution.py:53
  56.5 7.3 %copy-start.4 = (bf16[2,40,1792]{2,1,0:T(8,128)(2,1)S(1)}, bf16[2,40,1792]{2,1,0:T(8,128)(2,1)}, u32[]{:S(2)}) copy-start(bf16[2,40,1792]{2,1,0:T(8,128)(2,1)} %pad_maximum_fusion.14) | copy-start | bytes 860164
  56.6 15.7 %collective-permute-start.17 = (bf16[2,80,2304]{2,1,0:T(8,128)(2,1)S(1)}, bf16[2,80,2304]{2,1,0:T(8,128)(2,1)S(1)}, u32[]{:S(2)}, u32[]{:S(2)}) collective-permute-start(bf16[2,80,2304]{2,1,0:T(8,128)(2,1)S(1)} %pad_maximum_fusion), channel_id=1, source_target_pairs={{0,1},{1,0},{2,3},{3,2},{4,5},{5,4},{6,7},{7,6},{8,9},{9,8},{10,11... | collective-permute-start | bytes 2211848 | tf_op jit(solution)/shard_map/ppermute | solution.py:53
  60.5 10.4 %collective-permute-start.14 = (bf16[40,1792]{1,0:T(8,128)(2,1)S(1)}, bf16[40,1792]{1,0:T(8,128)(2,1)S(1)}, u32[]{:S(2)}, u32[]{:S(2)}) collective-permute-start(bf16[40,1792]{1,0:T(8,128)(2,1)S(1)} %fusion.47), channel_id=1, source_target_pairs={{0,8},{4,12},{8,0},{12,4},{1,9},{5,13},{9,1},{13,5},{2,10},{6,14},... | collective-permute-start | bytes 430088 | tf_op jit(solution)/shard_map/ppermute | solution.py:53
  63.8 9.6 %collective-permute-start.16 = (bf16[2,40,1792]{2,1,0:T(8,128)(2,1)S(1)}, bf16[2,40,1792]{2,1,0:T(8,128)(2,1)S(1)}, u32[]{:S(2)}, u32[]{:S(2)}) collective-permute-start(bf16[2,40,1792]{2,1,0:T(8,128)(2,1)S(1)} %copy-done.4), channel_id=1, source_target_pairs={{0,2},{1,3},{2,0},{3,1},{4,6},{5,7},{6,4},{7,5},{8,10},{9,11},{10,... | collective-permute-start | bytes 860168 | tf_op jit(solution)/shard_map/ppermute | solution.py:53
  70.9 6.7 %collective-permute-start.15 = (bf16[40,1792]{1,0:T(8,128)(2,1)S(1)}, bf16[40,1792]{1,0:T(8,128)(2,1)S(1)}, u32[]{:S(2)}, u32[]{:S(2)}) collective-permute-start(bf16[40,1792]{1,0:T(8,128)(2,1)S(1)} %get-tuple-element.112), channel_id=1, source_target_pairs={{0,2},{1,3},{2,0},{3,1},{4,6},{5,7},{6,4},{7,5},{8,10},{9,11},{10,... | collective-permute-start | bytes 430088 | tf_op jit(solution)/shard_map/ppermute | solution.py:53
  72.4 1.1 copy-start.3
  72.5 11.6 %collective-permute-start.21 = (bf16[2,40,2304]{2,1,0:T(8,128)(2,1)S(1)}, bf16[2,40,2304]{2,1,0:T(8,128)(2,1)S(1)}, u32[]{:S(2)}, u32[]{:S(2)}) collective-permute-start(bf16[2,40,2304]{2,1,0:T(8,128)(2,1)S(1)} %pad_maximum_fusion.9), channel_id=1, source_target_pairs={{0,2},{1,3},{2,0},{3,1},{4,6},{5,7},{6,4},{7,5},{8,10},{9,11},{10,... | collective-permute-start | bytes 1105928 | tf_op jit(solution)/shard_map/ppermute | solution.py:53
  73.4 8.9 %collective-permute-start.18 = (bf16[40,1792]{1,0:T(8,128)(2,1)S(1)}, bf16[40,1792]{1,0:T(8,128)(2,1)S(1)}, u32[]{:S(2)}, u32[]{:S(2)}) collective-permute-start(bf16[40,1792]{1,0:T(8,128)(2,1)S(1)} %fusion.45), channel_id=1, source_target_pairs={{0,8},{4,12},{8,0},{12,4},{1,9},{5,13},{9,1},{13,5},{2,10},{6,14},... | collective-permute-start | bytes 430088 | tf_op jit(solution)/shard_map/ppermute | solution.py:53
  74.6 30.5 %slice-start.8 = ((s8[14680064]{0:T(1024)(128)(4,1)}), s8[2097152]{0:T(1024)(128)(4,1)S(1)}, s32[]{:S(2)}) async-start(s8[14680064]{0:T(1024)(128)(4,1)} %bitcast.118), calls=%async_computation.8 | async-start | bytes 4194304
  75.7 29.5 %slice-start.9 = ((s8[14680064]{0:T(1024)(128)(4,1)}), s8[4194304]{0:T(1024)(128)(4,1)S(1)}, s32[]{:S(2)}) async-start(s8[14680064]{0:T(1024)(128)(4,1)} %bitcast.118), calls=%async_computation.9 | async-start | bytes 8388608
  75.8 8.6 %collective-permute-start.20 = (bf16[2,80,1280]{2,1,0:T(8,128)(2,1)S(1)}, bf16[2,80,1280]{2,1,0:T(8,128)(2,1)S(1)}, u32[]{:S(2)}, u32[]{:S(2)}) collective-permute-start(bf16[2,80,1280]{2,1,0:T(8,128)(2,1)S(1)} %pad_maximum_fusion.7), channel_id=1, source_target_pairs={{0,1},{1,0},{2,3},{3,2},{4,5},{5,4},{6,7},{7,6},{8,9},{9,8},{10,11... | collective-permute-start | bytes 1228808 | tf_op jit(solution)/shard_map/ppermute | solution.py:53
  77.6 12.4 %collective-permute-start.22 = (bf16[80,1792]{1,0:T(8,128)(2,1)S(1)}, bf16[80,1792]{1,0:T(8,128)(2,1)S(1)}, u32[]{:S(2)}, u32[]{:S(2)}) collective-permute-start(bf16[80,1792]{1,0:T(8,128)(2,1)S(1)} %pad_maximum_fusion.15), channel_id=1, source_target_pairs={{0,4},{1,0},{2,6},{3,2},{4,5},{5,1},{6,7},{7,3},{8,12},{9,8},{10,1... | collective-permute-start | bytes 860168 | tf_op jit(solution)/shard_map/ppermute | solution.py:130
  80.0 10.8 %collective-permute-start.23 = (bf16[80,1792]{1,0:T(8,128)(2,1)S(1)}, bf16[80,1792]{1,0:T(8,128)(2,1)S(1)}, u32[]{:S(2)}, u32[]{:S(2)}) collective-permute-start(bf16[80,1792]{1,0:T(8,128)(2,1)S(1)} %pad_maximum_fusion.15), channel_id=1, source_target_pairs={{1,4},{3,6},{4,1},{6,3},{9,12},{11,14},{12,9},{14,11},{17,20},{19,... | collective-permute-start | bytes 860168 | tf_op jit(solution)/shard_map/ppermute | solution.py:130
  82.4 6.7 %collective-permute-start.19 = (bf16[40,1792]{1,0:T(8,128)(2,1)S(1)}, bf16[40,1792]{1,0:T(8,128)(2,1)S(1)}, u32[]{:S(2)}, u32[]{:S(2)}) collective-permute-start(bf16[40,1792]{1,0:T(8,128)(2,1)S(1)} %get-tuple-element.110), channel_id=1, source_target_pairs={{0,2},{1,3},{2,0},{3,1},{4,6},{5,7},{6,4},{7,5},{8,10},{9,11},{10,... | collective-permute-start | bytes 430088 | tf_op jit(solution)/shard_map/ppermute | solution.py:53
  84.3 10.8 %collective-permute-start.25 = (bf16[40,2304]{1,0:T(8,128)(2,1)S(1)}, bf16[40,2304]{1,0:T(8,128)(2,1)S(1)}, u32[]{:S(2)}, u32[]{:S(2)}) collective-permute-start(bf16[40,2304]{1,0:T(8,128)(2,1)S(1)} %fusion.39), channel_id=1, source_target_pairs={{0,8},{4,12},{8,0},{12,4},{1,9},{5,13},{9,1},{13,5},{2,10},{6,14},... | collective-permute-start | bytes 552968 | tf_op jit(solution)/shard_map/ppermute | solution.py:53
  84.6 12.0 %collective-permute-start.24 = (bf16[2,40,1280]{2,1,0:T(8,128)(2,1)S(1)}, bf16[2,40,1280]{2,1,0:T(8,128)(2,1)S(1)}, u32[]{:S(2)}, u32[]{:S(2)}) collective-permute-start(bf16[2,40,1280]{2,1,0:T(8,128)(2,1)S(1)} %pad_maximum_fusion.17), channel_id=1, source_target_pairs={{0,2},{1,3},{2,0},{3,1},{4,6},{5,7},{6,4},{7,5},{8,10},{9,11},{10,... | collective-permute-start | bytes 614408 | tf_op jit(solution)/shard_map/ppermute | solution.py:53
  89.1 12.3 %collective-permute-start.26 = (bf16[80,1792]{1,0:T(8,128)(2,1)S(1)}, bf16[80,1792]{1,0:T(8,128)(2,1)S(1)}, u32[]{:S(2)}, u32[]{:S(2)}) collective-permute-start(bf16[80,1792]{1,0:T(8,128)(2,1)S(1)} %pad_maximum_fusion.16), channel_id=1, source_target_pairs={{0,4},{1,0},{2,6},{3,2},{4,5},{5,1},{6,7},{7,3},{8,12},{9,8},{10,1... | collective-permute-start | bytes 860168 | tf_op jit(solution)/shard_map/ppermute | solution.py:130
  90.0 11.4 %collective-permute-start.27 = (bf16[80,1792]{1,0:T(8,128)(2,1)S(1)}, bf16[80,1792]{1,0:T(8,128)(2,1)S(1)}, u32[]{:S(2)}, u32[]{:S(2)}) collective-permute-start(bf16[80,1792]{1,0:T(8,128)(2,1)S(1)} %pad_maximum_fusion.16), channel_id=1, source_target_pairs={{1,4},{3,6},{4,1},{6,3},{9,12},{11,14},{12,9},{14,11},{17,20},{19,... | collective-permute-start | bytes 860168 | tf_op jit(solution)/shard_map/ppermute | solution.py:130
  90.8 14.4 %slice-start.10 = ((s8[14680064]{0:T(1024)(128)(4,1)}), s8[4194304]{0:T(1024)(128)(4,1)S(1)}, s32[]{:S(2)}) async-start(s8[14680064]{0:T(1024)(128)(4,1)} %bitcast.118), calls=%async_computation.10 | async-start | bytes 8388608
  95.2 6.4 %collective-permute-start.28 = (bf16[40,2304]{1,0:T(8,128)(2,1)S(1)}, bf16[40,2304]{1,0:T(8,128)(2,1)S(1)}, u32[]{:S(2)}, u32[]{:S(2)}) collective-permute-start(bf16[40,2304]{1,0:T(8,128)(2,1)S(1)} %get-tuple-element.92), channel_id=1, source_target_pairs={{0,2},{1,3},{2,0},{3,1},{4,6},{5,7},{6,4},{7,5},{8,10},{9,11},{10,... | collective-permute-start | bytes 552968 | tf_op jit(solution)/shard_map/ppermute | solution.py:53
  96.7 8.5 %slice-start.11 = ((s8[14680064]{0:T(1024)(128)(4,1)}), s8[4194304]{0:T(1024)(128)(4,1)S(1)}, s32[]{:S(2)}) async-start(s8[14680064]{0:T(1024)(128)(4,1)} %bitcast.118), calls=%async_computation.11 | async-start | bytes 8388608
  96.7 11.4 %collective-permute-start.30 = (bf16[40,1280]{1,0:T(8,128)(2,1)S(1)}, bf16[40,1280]{1,0:T(8,128)(2,1)S(1)}, u32[]{:S(2)}, u32[]{:S(2)}) collective-permute-start(bf16[40,1280]{1,0:T(8,128)(2,1)S(1)} %fusion.51), channel_id=1, source_target_pairs={{0,8},{4,12},{8,0},{12,4},{1,9},{5,13},{9,1},{13,5},{2,10},{6,14},... | collective-permute-start | bytes 307208 | tf_op jit(solution)/shard_map/ppermute | solution.py:53
  101.6 10.3 %collective-permute-start.32 = (bf16[80,2304]{1,0:T(8,128)(2,1)S(1)}, bf16[80,2304]{1,0:T(8,128)(2,1)S(1)}, u32[]{:S(2)}, u32[]{:S(2)}) collective-permute-start(bf16[80,2304]{1,0:T(8,128)(2,1)S(1)} %pad_maximum_fusion.10), channel_id=1, source_target_pairs={{0,4},{1,0},{2,6},{3,2},{4,5},{5,1},{6,7},{7,3},{8,12},{9,8},{10,1... | collective-permute-start | bytes 1105928 | tf_op jit(solution)/shard_map/ppermute | solution.py:130
  104.2 7.6 %collective-permute-start.33 = (bf16[80,2304]{1,0:T(8,128)(2,1)S(1)}, bf16[80,2304]{1,0:T(8,128)(2,1)S(1)}, u32[]{:S(2)}, u32[]{:S(2)}) collective-permute-start(bf16[80,2304]{1,0:T(8,128)(2,1)S(1)} %pad_maximum_fusion.10), channel_id=1, source_target_pairs={{1,4},{3,6},{4,1},{6,3},{9,12},{11,14},{12,9},{14,11},{17,20},{19,... | collective-permute-start | bytes 1105928 | tf_op jit(solution)/shard_map/ppermute | solution.py:130
  106.7 3.1 %collective-permute-start.29 = (bf16[80,2048]{1,0:T(8,128)(2,1)S(1)}, bf16[80,2048]{1,0:T(8,128)(2,1)S(1)}, u32[]{:S(2)}, u32[]{:S(2)}) collective-permute-start(bf16[80,2048]{1,0:T(8,128)(2,1)S(1)} %slice.504), channel_id=1, source_target_pairs={{0,1},{1,0},{2,3},{3,2},{4,5},{5,4},{6,7},{7,6},{8,9},{9,8},{10,11... | collective-permute-start | bytes 983048 | tf_op jit(solution)/shard_map/ppermute | solution.py:53
  108.2 5.5 %collective-permute-start.34 = (bf16[40,1280]{1,0:T(8,128)(2,1)S(1)}, bf16[40,1280]{1,0:T(8,128)(2,1)S(1)}, u32[]{:S(2)}, u32[]{:S(2)}) collective-permute-start(bf16[40,1280]{1,0:T(8,128)(2,1)S(1)} %get-tuple-element.116), channel_id=1, source_target_pairs={{0,2},{1,3},{2,0},{3,1},{4,6},{5,7},{6,4},{7,5},{8,10},{9,11},{10,... | collective-permute-start | bytes 307208 | tf_op jit(solution)/shard_map/ppermute | solution.py:53
  109.9 10.2 %collective-permute-start.31 = (bf16[80,2048]{1,0:T(8,128)(2,1)S(1)}, bf16[80,2048]{1,0:T(8,128)(2,1)S(1)}, u32[]{:S(2)}, u32[]{:S(2)}) collective-permute-start(bf16[80,2048]{1,0:T(8,128)(2,1)S(1)} %get-tuple-element.77), channel_id=1, source_target_pairs={{0,2},{1,3},{2,0},{3,1},{4,6},{5,7},{6,4},{7,5},{8,10},{9,11},{10,... | collective-permute-start | bytes 983048 | tf_op jit(solution)/shard_map/ppermute | solution.py:53
  113.7 8.0 %collective-permute-start.35 = (bf16[80,1280]{1,0:T(8,128)(2,1)S(1)}, bf16[80,1280]{1,0:T(8,128)(2,1)S(1)}, u32[]{:S(2)}, u32[]{:S(2)}) collective-permute-start(bf16[80,1280]{1,0:T(8,128)(2,1)S(1)} %pad_maximum_fusion.18), channel_id=1, source_target_pairs={{0,4},{1,0},{2,6},{3,2},{4,5},{5,1},{6,7},{7,3},{8,12},{9,8},{10,1... | collective-permute-start | bytes 614408 | tf_op jit(solution)/shard_map/ppermute | solution.py:130
  117.6 4.1 %collective-permute-start.36 = (bf16[80,1280]{1,0:T(8,128)(2,1)S(1)}, bf16[80,1280]{1,0:T(8,128)(2,1)S(1)}, u32[]{:S(2)}, u32[]{:S(2)}) collective-permute-start(bf16[80,1280]{1,0:T(8,128)(2,1)S(1)} %pad_maximum_fusion.18), channel_id=1, source_target_pairs={{1,4},{3,6},{4,1},{6,3},{9,12},{11,14},{12,9},{14,11},{17,20},{19,... | collective-permute-start | bytes 614408 | tf_op jit(solution)/shard_map/ppermute | solution.py:130
  122.9 2.8 %collective-permute-start.37 = (bf16[80,2048]{1,0:T(8,128)(2,1)S(1)}, bf16[80,2048]{1,0:T(8,128)(2,1)S(1)}, u32[]{:S(2)}, u32[]{:S(2)}) collective-permute-start(bf16[80,2048]{1,0:T(8,128)(2,1)S(1)} %slice.503), channel_id=1, source_target_pairs={{0,1},{1,0},{2,3},{3,2},{4,5},{5,4},{6,7},{7,6},{8,9},{9,8},{10,11... | collective-permute-start | bytes 983048 | tf_op jit(solution)/shard_map/ppermute | solution.py:53
  125.8 10.1 %collective-permute-start.38 = (bf16[80,2048]{1,0:T(8,128)(2,1)S(1)}, bf16[80,2048]{1,0:T(8,128)(2,1)S(1)}, u32[]{:S(2)}, u32[]{:S(2)}) collective-permute-start(bf16[80,2048]{1,0:T(8,128)(2,1)S(1)} %fusion.35), channel_id=1, source_target_pairs={{0,2},{1,3},{2,0},{3,1},{4,6},{5,7},{6,4},{7,5},{8,10},{9,11},{10,... | collective-permute-start | bytes 983048 | tf_op jit(solution)/shard_map/ppermute | solution.py:53
  127.5 9.4 %collective-permute-start.39 = (bf16[80,2048]{1,0:T(8,128)(2,1)}, bf16[80,2048]{1,0:T(8,128)(2,1)S(1)}, u32[]{:S(2)}, u32[]{:S(2)}) collective-permute-start(bf16[80,2048]{1,0:T(8,128)(2,1)} %get-tuple-element.73), channel_id=1, source_target_pairs={{0,1},{1,0},{2,3},{3,2},{4,5},{5,4},{6,7},{7,6},{8,9},{9,8},{10,11... | collective-permute-start | bytes 983048 | tf_op jit(solution)/shard_map/ppermute | solution.py:53
  136.0 1.7 %collective-permute-start.40 = (bf16[80,2048]{1,0:T(8,128)(2,1)S(1)}, bf16[80,2048]{1,0:T(8,128)(2,1)S(1)}, u32[]{:S(2)}, u32[]{:S(2)}) collective-permute-start(bf16[80,2048]{1,0:T(8,128)(2,1)S(1)} %get-tuple-element.75), channel_id=1, source_target_pairs={{0,1},{1,0},{2,3},{3,2},{4,5},{5,4},{6,7},{7,6},{8,9},{9,8},{10,11... | collective-permute-start | bytes 983048 | tf_op jit(solution)/shard_map/ppermute | solution.py:53

commit v22 on v21

--- a/solution.py
+++ b/solution.py
@@ -8,7 +8,7 @@
 from jax.sharding import PartitionSpec as P
 
 HALVES = 2
-PARTS = ((14, 14), (18, 10))
+PARTS = ((13, 15), (18, 10))
 EDGES = {
     "t1.pick": ["t0.add"],
     "w.pull": ["t0.columns"],

time: 139 us -> 140 us (level); the launches traced: 139 us -> 138 us
  no operation moved by 1% of the time
where the time goes in v22:
time: 140 us; the launch traced here: 138 us
  starting transfers between devices  49.9 us (36%)
  waiting for transfers between devices  48 us (34%)
  matrix products  25.9 us (18%)
  other arithmetic  7.04 us (5%)
  Pallas kernels  5.71 us (4%)
    ppermute x29, waiting for transfers between devices, flip(): return lax.ppermute(value, axis, [(i, i ^ bit) for i in range(count)])  46.4 us
    ppermute x29, starting transfers between devices, flip(): return lax.ppermute(value, axis, [(i, i ^ bit) for i in range(count)])  34.4 us
    dot_general x17, matrix products, dot(): return jnp.dot(a, b, preferred_element_type=jnp.float32)  25.1 us
    ppermute x12, starting transfers between devices, move(): return lax.ppermute(value, ('row', 'col'), pairs)  15.5 us
    pallas_call x1, Pallas kernels, pull(): pl.pallas_call(functools.partial(pull_kernel, first, end), in_specs=[pl.B...  5.71 us
  transfers between devices with their start and end apart: 41, of which 17 were waited for; matrix products, arithmetic and copies ran while one was open for 20% of the time, Pallas kernels for 4%

profile of v22, /device:TPU:0, one launch (start us, length us, event | category | flops | bytes accessed | tf_op | source)
XLA Modules:
  0.0 138.5 jit_solution(6309623476906211459)
XLA Ops:
  0.5 0.9 fusion.80
  1.5 1.4 fusion.70
  3.2 2.6 %collective-permute-start.1 = (bf16[40,2048]{1,0:T(8,128)(2,1)S(1)}, bf16[40,2048]{1,0:T(8,128)(2,1)S(1)}, u32[]{:S(2)}, u32[]{:S(2)}) collective-permute-start(bf16[40,2048]{1,0:T(8,128)(2,1)S(1)} %slice.314), channel_id=1, source_target_pairs={{0,2},{1,3},{2,0},{3,1},{4,6},{5,7},{6,4},{7,5},{8,10},{9,11},{10,... | collective-permute-start | bytes 491528 | tf_op jit(solution)/shard_map/ppermute | solution.py:53
  5.8 4.9 %collective-permute-done.1 = bf16[40,2048]{1,0:T(8,128)(2,1)S(1)} collective-permute-done((bf16[40,2048]{1,0:T(8,128)(2,1)S(1)}, bf16[40,2048]{1,0:T(8,128)(2,1)S(1)}, u32[]{:S(2)}, u32[]{:S(2)}) %collective-permute-start.1) | collective-permute-done | bytes 163872 | tf_op jit(solution)/shard_map/ppermute | solution.py:53
  10.7 2.9 %collective-permute-start.2 = (bf16[40,2048]{1,0:T(8,128)(2,1)S(1)}, bf16[40,2048]{1,0:T(8,128)(2,1)S(1)}, u32[]{:S(2)}, u32[]{:S(2)}) collective-permute-start(bf16[40,2048]{1,0:T(8,128)(2,1)S(1)} %slice_add_fusion.19), channel_id=1, source_target_pairs={{0,8},{4,12},{8,0},{12,4},{1,9},{5,13},{9,1},{13,5},{2,10},{6,14},... | collective-permute-start | bytes 491528 | tf_op jit(solution)/shard_map/ppermute | solution.py:53
  14.2 1.6 %collective-permute-start.6 = (bf16[40,2048]{1,0:T(8,128)(2,1)S(1)}, bf16[40,2048]{1,0:T(8,128)(2,1)S(1)}, u32[]{:S(2)}, u32[]{:S(2)}) collective-permute-start(bf16[40,2048]{1,0:T(8,128)(2,1)S(1)} %slice.316), channel_id=1, source_target_pairs={{0,2},{1,3},{2,0},{3,1},{4,6},{5,7},{6,4},{7,5},{8,10},{9,11},{10,... | collective-permute-start | bytes 491528 | tf_op jit(solution)/shard_map/ppermute | solution.py:53
  15.8 5.4 %collective-permute-done.2 = bf16[40,2048]{1,0:T(8,128)(2,1)S(1)} collective-permute-done((bf16[40,2048]{1,0:T(8,128)(2,1)S(1)}, bf16[40,2048]{1,0:T(8,128)(2,1)S(1)}, u32[]{:S(2)}, u32[]{:S(2)}) %collective-permute-start.2) | collective-permute-done | bytes 163872 | tf_op jit(solution)/shard_map/ppermute | solution.py:53
  21.2 1.6 %collective-permute-start.3 = (bf16[40,2048]{1,0:T(8,128)(2,1)S(1)}, bf16[40,2048]{1,0:T(8,128)(2,1)S(1)}, u32[]{:S(2)}, u32[]{:S(2)}) collective-permute-start(bf16[40,2048]{1,0:T(8,128)(2,1)S(1)} %get-tuple-element.104), channel_id=1, source_target_pairs={{0,2},{1,3},{2,0},{3,1},{4,6},{5,7},{6,4},{7,5},{8,10},{9,11},{10,... | collective-permute-start | bytes 491528 | tf_op jit(solution)/shard_map/ppermute | solution.py:53
  22.9 3.7 %collective-permute-done.3 = bf16[40,2048]{1,0:T(8,128)(2,1)S(1)} collective-permute-done((bf16[40,2048]{1,0:T(8,128)(2,1)S(1)}, bf16[40,2048]{1,0:T(8,128)(2,1)S(1)}, u32[]{:S(2)}, u32[]{:S(2)}) %collective-permute-start.3) | collective-permute-done | bytes 163872 | tf_op jit(solution)/shard_map/ppermute | solution.py:53
  26.6 1.6 %collective-permute-start.4 = (bf16[80,2048]{1,0:T(8,128)(2,1)S(1)}, bf16[80,2048]{1,0:T(8,128)(2,1)S(1)}, u32[]{:S(2)}, u32[]{:S(2)}) collective-permute-start(bf16[80,2048]{1,0:T(8,128)(2,1)S(1)} %pad_maximum_fusion.11), channel_id=1, source_target_pairs={{0,4},{1,0},{2,6},{3,2},{4,5},{5,1},{6,7},{7,3},{8,12},{9,8},{10,1... | collective-permute-start | bytes 983048 | tf_op jit(solution)/shard_map/ppermute | solution.py:130
  28.2 0.7 collective-permute-start.5
  28.9 3.5 %collective-permute-done.7 = bf16[40,2048]{1,0:T(8,128)(2,1)S(1)} collective-permute-done((bf16[40,2048]{1,0:T(8,128)(2,1)S(1)}, bf16[40,2048]{1,0:T(8,128)(2,1)S(1)}, u32[]{:S(2)}, u32[]{:S(2)}) %collective-permute-start.7) | collective-permute-done | bytes 163872 | tf_op jit(solution)/shard_map/ppermute | solution.py:53
  33.0 5.7 %shard_map.55 = (bf16[2048,1664]{1,0:T(8,128)(2,1)S(1)}, bf16[2048,1664]{1,0:T(8,128)(2,1)S(1)}) custom-call(s32[4]{0:T(128)S(1)} %copy-done, bf16[2048,3584]{1,0:T(8,128)(2,1)} %gate_ref.1, bf16[2048,3584]{1,0:T(8,128)(2,1)} %up_ref.1), custom_call_target="tpu_custom_call" | custom-call | tf_op jit(solution)/shard_map/pallas_call | solution.py:73
  38.9 1.4 %fusion.93 = f32[160,1664]{1,0:T(8,128)S(1)} fusion(bf16[160,2048]{1,0:T(8,128)(2,1)S(1)} %pad_maximum_fusion.1, bf16[2048,1664]{1,0:T(8,128)(2,1)S(1)} %get-tuple-element.39), kind=kOutput, calls=%fused_computation.197 | convolution fusion | flops 1090519040 | bytes 8536064 | tf_op jit(solution)/shard_map/dot_general | solution.py:48
  40.4 1.4 %fusion.94 = f32[160,1664]{1,0:T(8,128)S(1)} fusion(bf16[160,2048]{1,0:T(8,128)(2,1)S(1)} %pad_maximum_fusion.1, bf16[2048,1664]{1,0:T(8,128)(2,1)S(1)} %get-tuple-element.44), kind=kOutput, calls=%fused_computation.198 | convolution fusion | flops 1090519040 | bytes 8536064 | tf_op jit(solution)/shard_map/dot_general | solution.py:48
  42.1 1.0 collective-permute-start.12
  43.1 0.8 collective-permute-done.9
  44.1 0.7 pad_maximum_fusion.15
  44.8 1.6 %fusion.10 = f32[160,1920]{1,0:T(8,128)S(1)} fusion(bf16[160,2048]{1,0:T(8,128)(2,1)S(1)} %pad_maximum_fusion.1, bf16[2048,3584]{1,0:T(8,128)(2,1)S(1)} %bitcast.110), kind=kOutput, calls=%fused_computation.10 | convolution fusion | flops 1258291200 | bytes 9748480 | tf_op jit(solution)/shard_map/dot_general | solution.py:48
  46.7 1.6 %fusion.8 = f32[160,1920]{1,0:T(8,128)S(1)} fusion(bf16[160,2048]{1,0:T(8,128)(2,1)S(1)} %pad_maximum_fusion.1, bf16[2048,3584]{1,0:T(8,128)(2,1)S(1)} %bitcast.108), kind=kOutput, calls=%fused_computation.8 | convolution fusion | flops 1258291200 | bytes 9748480 | tf_op jit(solution)/shard_map/dot_general | solution.py:48
  48.4 1.0 collective-permute-start.13
  49.6 1.6 %collective-permute-start.10 = (bf16[2,40,1664]{2,1,0:T(8,128)(2,1)}, bf16[2,40,1664]{2,1,0:T(8,128)(2,1)}, u32[]{:S(2)}, u32[]{:S(2)}) collective-permute-start(bf16[2,40,1664]{2,1,0:T(8,128)(2,1)} %pad_maximum_fusion.15), channel_id=1, source_target_pairs={{0,2},{1,3},{2,0},{3,1},{4,6},{5,7},{6,4},{7,5},{8,10},{9,11},{10,... | collective-permute-start | bytes 798728 | tf_op jit(solution)/shard_map/ppermute | solution.py:53
  51.3 0.8 pad_maximum_fusion.13
  52.1 1.7 %fusion.4 = f32[160,2304]{1,0:T(8,128)S(1)} fusion(bf16[160,2048]{1,0:T(8,128)(2,1)S(1)} %pad_maximum_fusion.2, bf16[2048,3584]{1,0:T(8,128)(2,1)S(1)} %bitcast.110), kind=kOutput, calls=%fused_computation.4 | convolution fusion | flops 1509949440 | bytes 11567104 | tf_op jit(solution)/shard_map/dot_general | solution.py:48
  53.8 2.9 %fusion.2 = f32[160,2304]{1,0:T(8,128)S(1)} fusion(bf16[160,2048]{1,0:T(8,128)(2,1)} %copy-done.2, bf16[2048,3584]{1,0:T(8,128)(2,1)S(1)} %bitcast.108), kind=kOutput, calls=%fused_computation.2 | convolution fusion | flops 1509949440 | bytes 11567104 | tf_op jit(solution)/shard_map/dot_general | solution.py:48
  56.9 2.3 %collective-permute-start.17 = (bf16[2,80,2304]{2,1,0:T(8,128)(2,1)S(1)}, bf16[2,80,2304]{2,1,0:T(8,128)(2,1)S(1)}, u32[]{:S(2)}, u32[]{:S(2)}) collective-permute-start(bf16[2,80,2304]{2,1,0:T(8,128)(2,1)S(1)} %pad_maximum_fusion), channel_id=1, source_target_pairs={{0,1},{1,0},{2,3},{3,2},{4,5},{5,4},{6,7},{7,6},{8,9},{9,8},{10,11... | collective-permute-start | bytes 2211848 | tf_op jit(solution)/shard_map/ppermute | solution.py:53
  59.2 1.1 fusion.47
  60.3 3.4 %collective-permute-start.14 = (bf16[40,1664]{1,0:T(8,128)(2,1)S(1)}, bf16[40,1664]{1,0:T(8,128)(2,1)S(1)}, u32[]{:S(2)}, u32[]{:S(2)}) collective-permute-start(bf16[40,1664]{1,0:T(8,128)(2,1)S(1)} %fusion.47), channel_id=1, source_target_pairs={{0,8},{4,12},{8,0},{12,4},{1,9},{5,13},{9,1},{13,5},{2,10},{6,14},... | collective-permute-start | bytes 399368 | tf_op jit(solution)/shard_map/ppermute | solution.py:53
  63.7 1.5 %collective-permute-start.16 = (bf16[2,40,1920]{2,1,0:T(8,128)(2,1)S(1)}, bf16[2,40,1920]{2,1,0:T(8,128)(2,1)S(1)}, u32[]{:S(2)}, u32[]{:S(2)}) collective-permute-start(bf16[2,40,1920]{2,1,0:T(8,128)(2,1)S(1)} %copy-done.4), channel_id=1, source_target_pairs={{0,2},{1,3},{2,0},{3,1},{4,6},{5,7},{6,4},{7,5},{8,10},{9,11},{10,... | collective-permute-start | bytes 921608 | tf_op jit(solution)/shard_map/ppermute | solution.py:53
  65.2 5.1 %collective-permute-done.14 = bf16[40,1664]{1,0:T(8,128)(2,1)S(1)} collective-permute-done((bf16[40,1664]{1,0:T(8,128)(2,1)S(1)}, bf16[40,1664]{1,0:T(8,128)(2,1)S(1)}, u32[]{:S(2)}, u32[]{:S(2)}) %collective-permute-start.14) | collective-permute-done | bytes 133152 | tf_op jit(solution)/shard_map/ppermute | solution.py:53
  70.3 1.6 %collective-permute-start.15 = (bf16[40,1664]{1,0:T(8,128)(2,1)S(1)}, bf16[40,1664]{1,0:T(8,128)(2,1)S(1)}, u32[]{:S(2)}, u32[]{:S(2)}) collective-permute-start(bf16[40,1664]{1,0:T(8,128)(2,1)S(1)} %get-tuple-element.112), channel_id=1, source_target_pairs={{0,2},{1,3},{2,0},{3,1},{4,6},{5,7},{6,4},{7,5},{8,10},{9,11},{10,... | collective-permute-start | bytes 399368 | tf_op jit(solution)/shard_map/ppermute | solution.py:53
  72.9 0.9 collective-permute-start.18
  73.8 1.1 fusion.16
  74.9 1.1 fusion.18
  76.7 2.8 %collective-permute-start.22 = (bf16[80,1664]{1,0:T(8,128)(2,1)S(1)}, bf16[80,1664]{1,0:T(8,128)(2,1)S(1)}, u32[]{:S(2)}, u32[]{:S(2)}) collective-permute-start(bf16[80,1664]{1,0:T(8,128)(2,1)S(1)} %pad_maximum_fusion.16), channel_id=1, source_target_pairs={{0,4},{1,0},{2,6},{3,2},{4,5},{5,1},{6,7},{7,3},{8,12},{9,8},{10,1... | collective-permute-start | bytes 798728 | tf_op jit(solution)/shard_map/ppermute | solution.py:130
  79.5 0.7 collective-permute-start.23
  80.2 2.2 %collective-permute-done.18 = bf16[40,1920]{1,0:T(8,128)(2,1)S(1)} collective-permute-done((bf16[40,1920]{1,0:T(8,128)(2,1)S(1)}, bf16[40,1920]{1,0:T(8,128)(2,1)S(1)}, u32[]{:S(2)}, u32[]{:S(2)}) %collective-permute-start.18) | collective-permute-done | bytes 153632 | tf_op jit(solution)/shard_map/ppermute | solution.py:53
  82.4 1.5 %collective-permute-start.19 = (bf16[40,1920]{1,0:T(8,128)(2,1)S(1)}, bf16[40,1920]{1,0:T(8,128)(2,1)S(1)}, u32[]{:S(2)}, u32[]{:S(2)}) collective-permute-start(bf16[40,1920]{1,0:T(8,128)(2,1)S(1)} %get-tuple-element.108), channel_id=1, source_target_pairs={{0,2},{1,3},{2,0},{3,1},{4,6},{5,7},{6,4},{7,5},{8,10},{9,11},{10,... | collective-permute-start | bytes 460808 | tf_op jit(solution)/shard_map/ppermute | solution.py:53
  84.3 1.4 collective-permute-start.24
  85.7 3.6 %collective-permute-done.19 = bf16[40,1920]{1,0:T(8,128)(2,1)S(1)} collective-permute-done((bf16[40,1920]{1,0:T(8,128)(2,1)S(1)}, bf16[40,1920]{1,0:T(8,128)(2,1)S(1)}, u32[]{:S(2)}, u32[]{:S(2)}) %collective-permute-start.19) | collective-permute-done | bytes 153632 | tf_op jit(solution)/shard_map/ppermute | solution.py:53
  89.5 1.0 collective-permute-start.27
  90.6 4.6 %collective-permute-done.25 = bf16[40,2304]{1,0:T(8,128)(2,1)S(1)} collective-permute-done((bf16[40,2304]{1,0:T(8,128)(2,1)S(1)}, bf16[40,2304]{1,0:T(8,128)(2,1)S(1)}, u32[]{:S(2)}, u32[]{:S(2)}) %collective-permute-start.25) | collective-permute-done | bytes 184352 | tf_op jit(solution)/shard_map/ppermute | solution.py:53
  95.3 0.9 collective-permute-start.28
  96.4 4.4 %fusion.12 = f32[160,2048]{1,0:T(8,128)S(1)} fusion(bf16[160,1664]{1,0:T(8,128)(2,1)S(1)} %pad_maximum_fusion.6, bf16[3584,2048]{1,0:T(8,128)(2,1)} %param.9), kind=kOutput, calls=%fused_computation.12 | convolution fusion | flops 1090519040 | bytes 8658944 | tf_op jit(solution)/shard_map/dot_general | solution.py:48
  101.4 2.3 %collective-permute-start.32 = (bf16[80,2304]{1,0:T(8,128)(2,1)S(1)}, bf16[80,2304]{1,0:T(8,128)(2,1)S(1)}, u32[]{:S(2)}, u32[]{:S(2)}) collective-permute-start(bf16[80,2304]{1,0:T(8,128)(2,1)S(1)} %pad_maximum_fusion.10), channel_id=1, source_target_pairs={{0,4},{1,0},{2,6},{3,2},{4,5},{5,1},{6,7},{7,3},{8,12},{9,8},{10,1... | collective-permute-start | bytes 1105928 | tf_op jit(solution)/shard_map/ppermute | solution.py:130
  103.7 0.7 collective-permute-start.33
  104.4 1.6 %fusion.91 = f32[160,2048]{1,0:T(8,128)S(1)} fusion(f32[160,2048]{1,0:T(8,128)S(1)} %fusion.12, bf16[160,1920]{1,0:T(8,128)(2,1)S(1)} %pad_maximum_fusion.4, bf16[3584,2048]{1,0:T(8,128)(2,1)S(1)} %bitcast.119), kind=kOutput, calls=%fused_computation.195 | convolution fusion | flops 1258618880 | bytes 11100160 | tf_op jit(solution)/shard_map/dot_general | solution.py:48
  106.1 1.4 %collective-permute-start.29 = (bf16[80,2048]{1,0:T(8,128)(2,1)S(1)}, bf16[80,2048]{1,0:T(8,128)(2,1)S(1)}, u32[]{:S(2)}, u32[]{:S(2)}) collective-permute-start(bf16[80,2048]{1,0:T(8,128)(2,1)S(1)} %slice.504), channel_id=1, source_target_pairs={{0,1},{1,0},{2,3},{3,2},{4,5},{5,4},{6,7},{7,6},{8,9},{9,8},{10,11... | collective-permute-start | bytes 983048 | tf_op jit(solution)/shard_map/ppermute | solution.py:53
  107.6 1.7 %collective-permute-start.34 = (bf16[40,1280]{1,0:T(8,128)(2,1)S(1)}, bf16[40,1280]{1,0:T(8,128)(2,1)S(1)}, u32[]{:S(2)}, u32[]{:S(2)}) collective-permute-start(bf16[40,1280]{1,0:T(8,128)(2,1)S(1)} %get-tuple-element.116), channel_id=1, source_target_pairs={{0,2},{1,3},{2,0},{3,1},{4,6},{5,7},{6,4},{7,5},{8,10},{9,11},{10,... | collective-permute-start | bytes 307208 | tf_op jit(solution)/shard_map/ppermute | solution.py:53
  109.4 1.2 collective-permute-start.31
  110.6 0.7 collective-permute-done.32
  111.4 1.7 %fusion = f32[160,2048]{1,0:T(8,128)S(1)} fusion(bf16[3584,2048]{1,0:T(8,128)(2,1)S(1)} %bitcast.119, bf16[80,2304]{1,0:T(8,128)(2,1)S(1)} %get-tuple-element.90, bf16[80,2304]{1,0:T(8,128)(2,1)S(1)} %get-tuple-element.89), kind=kOutput, calls=%fused_computation | convolution fusion | flops 1511424000 | bytes 11485184 | tf_op jit(solution)/shard_map/dot_general | solution.py:48
  113.2 3.9 %collective-permute-start.35 = (bf16[80,1280]{1,0:T(8,128)(2,1)S(1)}, bf16[80,1280]{1,0:T(8,128)(2,1)S(1)}, u32[]{:S(2)}, u32[]{:S(2)}) collective-permute-start(bf16[80,1280]{1,0:T(8,128)(2,1)S(1)} %pad_maximum_fusion.18), channel_id=1, source_target_pairs={{0,4},{1,0},{2,6},{3,2},{4,5},{5,1},{6,7},{7,3},{8,12},{9,8},{10,1... | collective-permute-start | bytes 614408 | tf_op jit(solution)/shard_map/ppermute | solution.py:130
  117.8 1.7 %collective-permute-done.31 = bf16[80,2048]{1,0:T(8,128)(2,1)S(1)} collective-permute-done((bf16[80,2048]{1,0:T(8,128)(2,1)S(1)}, bf16[80,2048]{1,0:T(8,128)(2,1)S(1)}, u32[]{:S(2)}, u32[]{:S(2)}) %collective-permute-start.31) | collective-permute-done | bytes 327712 | tf_op jit(solution)/shard_map/ppermute | solution.py:53
  119.5 0.8 fusion.85
  120.3 0.9 collective-permute-done.35
  121.3 1.1 fusion.92
  122.4 1.6 %collective-permute-start.37 = (bf16[80,2048]{1,0:T(8,128)(2,1)S(1)}, bf16[80,2048]{1,0:T(8,128)(2,1)S(1)}, u32[]{:S(2)}, u32[]{:S(2)}) collective-permute-start(bf16[80,2048]{1,0:T(8,128)(2,1)S(1)} %slice.503), channel_id=1, source_target_pairs={{0,1},{1,0},{2,3},{3,2},{4,5},{5,4},{6,7},{7,6},{8,9},{9,8},{10,11... | collective-permute-start | bytes 983048 | tf_op jit(solution)/shard_map/ppermute | solution.py:53
  124.0 1.2 collective-permute-done.37
  125.3 1.7 %collective-permute-start.38 = (bf16[80,2048]{1,0:T(8,128)(2,1)S(1)}, bf16[80,2048]{1,0:T(8,128)(2,1)S(1)}, u32[]{:S(2)}, u32[]{:S(2)}) collective-permute-start(bf16[80,2048]{1,0:T(8,128)(2,1)S(1)} %fusion.35), channel_id=1, source_target_pairs={{0,2},{1,3},{2,0},{3,1},{4,6},{5,7},{6,4},{7,5},{8,10},{9,11},{10,... | collective-permute-start | bytes 983048 | tf_op jit(solution)/shard_map/ppermute | solution.py:53
  127.2 8.2 %collective-permute-done.38 = bf16[80,2048]{1,0:T(8,128)(2,1)S(1)} collective-permute-done((bf16[80,2048]{1,0:T(8,128)(2,1)S(1)}, bf16[80,2048]{1,0:T(8,128)(2,1)S(1)}, u32[]{:S(2)}, u32[]{:S(2)}) %collective-permute-start.38) | collective-permute-done | bytes 327712 | tf_op jit(solution)/shard_map/ppermute | solution.py:53
  135.6 0.8 fusion.25
  136.5 0.7 collective-permute-done.40
  137.2 1.3 fusion.22
  (152 shorter events, 8.5 us)
Async XLA Ops:
  0.0 2.9 %collective-permute-start = (bf16[160,2048]{1,0:T(8,128)(2,1)}, bf16[160,2048]{1,0:T(8,128)(2,1)S(1)}, u32[]{:S(2)}, u32[]{:S(2)}) collective-permute-start(bf16[160,2048]{1,0:T(8,128)(2,1)} %param.5), channel_id=1, source_target_pairs={{0,1},{1,0},{2,3},{3,2},{4,5},{5,4},{6,7},{7,6},{8,9},{9,8},{10,11... | collective-permute-start | bytes 1966088 | tf_op jit(solution)/shard_map/ppermute | solution.py:53
  2.9 10.7 %copy-start.1 = (bf16[160,2048]{1,0:T(8,128)(2,1)S(1)}, bf16[160,2048]{1,0:T(8,128)(2,1)}, u32[]{:S(2)}) copy-start(bf16[160,2048]{1,0:T(8,128)(2,1)} %param.5) | copy-start | bytes 1966084
  3.2 7.4 %collective-permute-start.1 = (bf16[40,2048]{1,0:T(8,128)(2,1)S(1)}, bf16[40,2048]{1,0:T(8,128)(2,1)S(1)}, u32[]{:S(2)}, u32[]{:S(2)}) collective-permute-start(bf16[40,2048]{1,0:T(8,128)(2,1)S(1)} %slice.314), channel_id=1, source_target_pairs={{0,2},{1,3},{2,0},{3,1},{4,6},{5,7},{6,4},{7,5},{8,10},{9,11},{10,... | collective-permute-start | bytes 491528 | tf_op jit(solution)/shard_map/ppermute | solution.py:53
  10.7 10.5 %collective-permute-start.2 = (bf16[40,2048]{1,0:T(8,128)(2,1)S(1)}, bf16[40,2048]{1,0:T(8,128)(2,1)S(1)}, u32[]{:S(2)}, u32[]{:S(2)}) collective-permute-start(bf16[40,2048]{1,0:T(8,128)(2,1)S(1)} %slice_add_fusion.19), channel_id=1, source_target_pairs={{0,8},{4,12},{8,0},{12,4},{1,9},{5,13},{9,1},{13,5},{2,10},{6,14},... | collective-permute-start | bytes 491528 | tf_op jit(solution)/shard_map/ppermute | solution.py:53
  14.2 18.8 %copy-start = (s32[4]{0:T(128)S(1)}, s32[4]{0:T(128)}, u32[]{:S(2)}) copy-start(s32[4]{0:T(128)} %tick_ref) | copy-start | bytes 52
  14.2 8.6 %collective-permute-start.6 = (bf16[40,2048]{1,0:T(8,128)(2,1)S(1)}, bf16[40,2048]{1,0:T(8,128)(2,1)S(1)}, u32[]{:S(2)}, u32[]{:S(2)}) collective-permute-start(bf16[40,2048]{1,0:T(8,128)(2,1)S(1)} %slice.316), channel_id=1, source_target_pairs={{0,2},{1,3},{2,0},{3,1},{4,6},{5,7},{6,4},{7,5},{8,10},{9,11},{10,... | collective-permute-start | bytes 491528 | tf_op jit(solution)/shard_map/ppermute | solution.py:53
  21.2 5.4 %collective-permute-start.3 = (bf16[40,2048]{1,0:T(8,128)(2,1)S(1)}, bf16[40,2048]{1,0:T(8,128)(2,1)S(1)}, u32[]{:S(2)}, u32[]{:S(2)}) collective-permute-start(bf16[40,2048]{1,0:T(8,128)(2,1)S(1)} %get-tuple-element.104), channel_id=1, source_target_pairs={{0,2},{1,3},{2,0},{3,1},{4,6},{5,7},{6,4},{7,5},{8,10},{9,11},{10,... | collective-permute-start | bytes 491528 | tf_op jit(solution)/shard_map/ppermute | solution.py:53
  22.8 9.5 %collective-permute-start.7 = (bf16[40,2048]{1,0:T(8,128)(2,1)S(1)}, bf16[40,2048]{1,0:T(8,128)(2,1)S(1)}, u32[]{:S(2)}, u32[]{:S(2)}) collective-permute-start(bf16[40,2048]{1,0:T(8,128)(2,1)S(1)} %slice_add_fusion.18), channel_id=1, source_target_pairs={{0,8},{4,12},{8,0},{12,4},{1,9},{5,13},{9,1},{13,5},{2,10},{6,14},... | collective-permute-start | bytes 491528 | tf_op jit(solution)/shard_map/ppermute | solution.py:53
  26.6 12.1 %collective-permute-start.4 = (bf16[80,2048]{1,0:T(8,128)(2,1)S(1)}, bf16[80,2048]{1,0:T(8,128)(2,1)S(1)}, u32[]{:S(2)}, u32[]{:S(2)}) collective-permute-start(bf16[80,2048]{1,0:T(8,128)(2,1)S(1)} %pad_maximum_fusion.11), channel_id=1, source_target_pairs={{0,4},{1,0},{2,6},{3,2},{4,5},{5,1},{6,7},{7,3},{8,12},{9,8},{10,1... | collective-permute-start | bytes 983048 | tf_op jit(solution)/shard_map/ppermute | solution.py:130
  28.2 10.5 %collective-permute-start.5 = (bf16[80,2048]{1,0:T(8,128)(2,1)S(1)}, bf16[80,2048]{1,0:T(8,128)(2,1)S(1)}, u32[]{:S(2)}, u32[]{:S(2)}) collective-permute-start(bf16[80,2048]{1,0:T(8,128)(2,1)S(1)} %pad_maximum_fusion.11), channel_id=1, source_target_pairs={{1,4},{3,6},{4,1},{6,3},{9,12},{11,14},{12,9},{14,11},{17,20},{19,... | collective-permute-start | bytes 983048 | tf_op jit(solution)/shard_map/ppermute | solution.py:130
  32.4 6.5 %collective-permute-start.8 = (bf16[40,2048]{1,0:T(8,128)(2,1)S(1)}, bf16[40,2048]{1,0:T(8,128)(2,1)S(1)}, u32[]{:S(2)}, u32[]{:S(2)}) collective-permute-start(bf16[40,2048]{1,0:T(8,128)(2,1)S(1)} %get-tuple-element.100), channel_id=1, source_target_pairs={{0,2},{1,3},{2,0},{3,1},{4,6},{5,7},{6,4},{7,5},{8,10},{9,11},{10,... | collective-permute-start | bytes 491528 | tf_op jit(solution)/shard_map/ppermute | solution.py:53
  33.0 11.8 %slice-start.4 = ((s8[14680064]{0:T(1024)(128)(4,1)}), s8[4194304]{0:T(1024)(128)(4,1)S(1)}, s32[]{:S(2)}) async-start(s8[14680064]{0:T(1024)(128)(4,1)} %bitcast.109), calls=%async_computation.4 | async-start | bytes 8388608
  33.0 11.8 %slice-start.5 = ((s8[14680064]{0:T(1024)(128)(4,1)}), s8[4194304]{0:T(1024)(128)(4,1)S(1)}, s32[]{:S(2)}) async-start(s8[14680064]{0:T(1024)(128)(4,1)} %bitcast.109), calls=%async_computation.5 | async-start | bytes 8388608
  38.9 5.9 %slice-start.6 = ((s8[14680064]{0:T(1024)(128)(4,1)}), s8[4194304]{0:T(1024)(128)(4,1)S(1)}, s32[]{:S(2)}) async-start(s8[14680064]{0:T(1024)(128)(4,1)} %bitcast.109), calls=%async_computation.6 | async-start | bytes 8388608
  40.3 4.5 %slice-start.7 = ((s8[14680064]{0:T(1024)(128)(4,1)}), s8[2097152]{0:T(1024)(128)(4,1)S(1)}, s32[]{:S(2)}) async-start(s8[14680064]{0:T(1024)(128)(4,1)} %bitcast.109), calls=%async_computation.7 | async-start | bytes 4194304
  40.3 6.1 %slice-start = ((s8[14680064]{0:T(1024)(128)(4,1)}), s8[4194304]{0:T(1024)(128)(4,1)S(1)}, s32[]{:S(2)}) async-start(s8[14680064]{0:T(1024)(128)(4,1)} %bitcast.107), calls=%async_computation | async-start | bytes 8388608
  40.3 6.1 %slice-start.1 = ((s8[14680064]{0:T(1024)(128)(4,1)}), s8[4194304]{0:T(1024)(128)(4,1)S(1)}, s32[]{:S(2)}) async-start(s8[14680064]{0:T(1024)(128)(4,1)} %bitcast.107), calls=%async_computation.1 | async-start | bytes 8388608
  41.8 4.6 %slice-start.2 = ((s8[14680064]{0:T(1024)(128)(4,1)}), s8[4194304]{0:T(1024)(128)(4,1)S(1)}, s32[]{:S(2)}) async-start(s8[14680064]{0:T(1024)(128)(4,1)} %bitcast.107), calls=%async_computation.2 | async-start | bytes 8388608
  41.9 2.0 %collective-permute-start.9 = (bf16[2,80,1664]{2,1,0:T(8,128)(2,1)S(1)}, bf16[2,80,1664]{2,1,0:T(8,128)(2,1)S(1)}, u32[]{:S(2)}, u32[]{:S(2)}) collective-permute-start(bf16[2,80,1664]{2,1,0:T(8,128)(2,1)S(1)} %pad_maximum_fusion.5), channel_id=1, source_target_pairs={{0,1},{1,0},{2,3},{3,2},{4,5},{5,4},{6,7},{7,6},{8,9},{9,8},{10,11... | collective-permute-start | bytes 1597448 | tf_op jit(solution)/shard_map/ppermute | solution.py:53
  42.0 7.4 %collective-permute-start.11 = (bf16[80,2048]{1,0:T(8,128)(2,1)S(1)}, bf16[80,2048]{1,0:T(8,128)(2,1)S(1)}, u32[]{:S(2)}, u32[]{:S(2)}) collective-permute-start(bf16[80,2048]{1,0:T(8,128)(2,1)S(1)} %pad_maximum_fusion.12), channel_id=1, source_target_pairs={{0,4},{1,0},{2,6},{3,2},{4,5},{5,1},{6,7},{7,3},{8,12},{9,8},{10,1... | collective-permute-start | bytes 983048 | tf_op jit(solution)/shard_map/ppermute | solution.py:130
  42.1 7.3 %collective-permute-start.12 = (bf16[80,2048]{1,0:T(8,128)(2,1)S(1)}, bf16[80,2048]{1,0:T(8,128)(2,1)S(1)}, u32[]{:S(2)}, u32[]{:S(2)}) collective-permute-start(bf16[80,2048]{1,0:T(8,128)(2,1)S(1)} %pad_maximum_fusion.12), channel_id=1, source_target_pairs={{1,4},{3,6},{4,1},{6,3},{9,12},{11,14},{12,9},{14,11},{17,20},{19,... | collective-permute-start | bytes 983048 | tf_op jit(solution)/shard_map/ppermute | solution.py:130
  44.8 1.8 %slice-start.3 = ((s8[14680064]{0:T(1024)(128)(4,1)}), s8[2097152]{0:T(1024)(128)(4,1)S(1)}, s32[]{:S(2)}) async-start(s8[14680064]{0:T(1024)(128)(4,1)} %bitcast.107), calls=%async_computation.3 | async-start | bytes 4194304
  48.4 2.7 %collective-permute-start.13 = (bf16[2,80,1920]{2,1,0:T(8,128)(2,1)S(1)}, bf16[2,80,1920]{2,1,0:T(8,128)(2,1)S(1)}, u32[]{:S(2)}, u32[]{:S(2)}) collective-permute-start(bf16[2,80,1920]{2,1,0:T(8,128)(2,1)S(1)} %pad_maximum_fusion.3), channel_id=1, source_target_pairs={{0,1},{1,0},{2,3},{3,2},{4,5},{5,4},{6,7},{7,6},{8,9},{9,8},{10,11... | collective-permute-start | bytes 1843208 | tf_op jit(solution)/shard_map/ppermute | solution.py:53
  49.6 2.5 %copy-start.2 = (bf16[160,2048]{1,0:T(8,128)(2,1)}, bf16[160,2048]{1,0:T(8,128)(2,1)S(1)}, u32[]{:S(2)}) copy-start(bf16[160,2048]{1,0:T(8,128)(2,1)S(1)} %pad_maximum_fusion.2) | copy-start | bytes 1966084
  49.6 9.6 %collective-permute-start.10 = (bf16[2,40,1664]{2,1,0:T(8,128)(2,1)}, bf16[2,40,1664]{2,1,0:T(8,128)(2,1)}, u32[]{:S(2)}, u32[]{:S(2)}) collective-permute-start(bf16[2,40,1664]{2,1,0:T(8,128)(2,1)} %pad_maximum_fusion.15), channel_id=1, source_target_pairs={{0,2},{1,3},{2,0},{3,1},{4,6},{5,7},{6,4},{7,5},{8,10},{9,11},{10,... | collective-permute-start | bytes 798728 | tf_op jit(solution)/shard_map/ppermute | solution.py:53
  56.8 6.9 %copy-start.4 = (bf16[2,40,1920]{2,1,0:T(8,128)(2,1)S(1)}, bf16[2,40,1920]{2,1,0:T(8,128)(2,1)}, u32[]{:S(2)}) copy-start(bf16[2,40,1920]{2,1,0:T(8,128)(2,1)} %pad_maximum_fusion.13) | copy-start | bytes 921604
  56.9 15.0 %collective-permute-start.17 = (bf16[2,80,2304]{2,1,0:T(8,128)(2,1)S(1)}, bf16[2,80,2304]{2,1,0:T(8,128)(2,1)S(1)}, u32[]{:S(2)}, u32[]{:S(2)}) collective-permute-start(bf16[2,80,2304]{2,1,0:T(8,128)(2,1)S(1)} %pad_maximum_fusion), channel_id=1, source_target_pairs={{0,1},{1,0},{2,3},{3,2},{4,5},{5,4},{6,7},{7,6},{8,9},{9,8},{10,11... | collective-permute-start | bytes 2211848 | tf_op jit(solution)/shard_map/ppermute | solution.py:53
  60.3 10.0 %collective-permute-start.14 = (bf16[40,1664]{1,0:T(8,128)(2,1)S(1)}, bf16[40,1664]{1,0:T(8,128)(2,1)S(1)}, u32[]{:S(2)}, u32[]{:S(2)}) collective-permute-start(bf16[40,1664]{1,0:T(8,128)(2,1)S(1)} %fusion.47), channel_id=1, source_target_pairs={{0,8},{4,12},{8,0},{12,4},{1,9},{5,13},{9,1},{13,5},{2,10},{6,14},... | collective-permute-start | bytes 399368 | tf_op jit(solution)/shard_map/ppermute | solution.py:53
  63.7 9.1 %collective-permute-start.16 = (bf16[2,40,1920]{2,1,0:T(8,128)(2,1)S(1)}, bf16[2,40,1920]{2,1,0:T(8,128)(2,1)S(1)}, u32[]{:S(2)}, u32[]{:S(2)}) collective-permute-start(bf16[2,40,1920]{2,1,0:T(8,128)(2,1)S(1)} %copy-done.4), channel_id=1, source_target_pairs={{0,2},{1,3},{2,0},{3,1},{4,6},{5,7},{6,4},{7,5},{8,10},{9,11},{10,... | collective-permute-start | bytes 921608 | tf_op jit(solution)/shard_map/ppermute | solution.py:53
  70.3 6.4 %collective-permute-start.15 = (bf16[40,1664]{1,0:T(8,128)(2,1)S(1)}, bf16[40,1664]{1,0:T(8,128)(2,1)S(1)}, u32[]{:S(2)}, u32[]{:S(2)}) collective-permute-start(bf16[40,1664]{1,0:T(8,128)(2,1)S(1)} %get-tuple-element.112), channel_id=1, source_target_pairs={{0,2},{1,3},{2,0},{3,1},{4,6},{5,7},{6,4},{7,5},{8,10},{9,11},{10,... | collective-permute-start | bytes 399368 | tf_op jit(solution)/shard_map/ppermute | solution.py:53
  72.1 1.7 %copy-start.3 = (bf16[160,2048]{1,0:T(8,128)(2,1)S(1)}, bf16[160,2048]{1,0:T(8,128)(2,1)}, u32[]{:S(2)}) copy-start(bf16[160,2048]{1,0:T(8,128)(2,1)} %copy-done.2) | copy-start | bytes 1966084
  72.2 11.7 %collective-permute-start.21 = (bf16[2,40,2304]{2,1,0:T(8,128)(2,1)S(1)}, bf16[2,40,2304]{2,1,0:T(8,128)(2,1)S(1)}, u32[]{:S(2)}, u32[]{:S(2)}) collective-permute-start(bf16[2,40,2304]{2,1,0:T(8,128)(2,1)S(1)} %pad_maximum_fusion.9), channel_id=1, source_target_pairs={{0,2},{1,3},{2,0},{3,1},{4,6},{5,7},{6,4},{7,5},{8,10},{9,11},{10,... | collective-permute-start | bytes 1105928 | tf_op jit(solution)/shard_map/ppermute | solution.py:53
  72.9 9.5 %collective-permute-start.18 = (bf16[40,1920]{1,0:T(8,128)(2,1)S(1)}, bf16[40,1920]{1,0:T(8,128)(2,1)S(1)}, u32[]{:S(2)}, u32[]{:S(2)}) collective-permute-start(bf16[40,1920]{1,0:T(8,128)(2,1)S(1)} %fusion.43), channel_id=1, source_target_pairs={{0,8},{4,12},{8,0},{12,4},{1,9},{5,13},{9,1},{13,5},{2,10},{6,14},... | collective-permute-start | bytes 460808 | tf_op jit(solution)/shard_map/ppermute | solution.py:53
  74.9 29.5 %slice-start.8 = ((s8[14680064]{0:T(1024)(128)(4,1)}), s8[2097152]{0:T(1024)(128)(4,1)S(1)}, s32[]{:S(2)}) async-start(s8[14680064]{0:T(1024)(128)(4,1)} %bitcast.118), calls=%async_computation.8 | async-start | bytes 4194304
  76.0 28.4 %slice-start.9 = ((s8[14680064]{0:T(1024)(128)(4,1)}), s8[4194304]{0:T(1024)(128)(4,1)S(1)}, s32[]{:S(2)}) async-start(s8[14680064]{0:T(1024)(128)(4,1)} %bitcast.118), calls=%async_computation.9 | async-start | bytes 8388608
  76.1 8.1 %collective-permute-start.20 = (bf16[2,80,1280]{2,1,0:T(8,128)(2,1)S(1)}, bf16[2,80,1280]{2,1,0:T(8,128)(2,1)S(1)}, u32[]{:S(2)}, u32[]{:S(2)}) collective-permute-start(bf16[2,80,1280]{2,1,0:T(8,128)(2,1)S(1)} %pad_maximum_fusion.7), channel_id=1, source_target_pairs={{0,1},{1,0},{2,3},{3,2},{4,5},{5,4},{6,7},{7,6},{8,9},{9,8},{10,11... | collective-permute-start | bytes 1228808 | tf_op jit(solution)/shard_map/ppermute | solution.py:53
  76.7 12.7 %collective-permute-start.22 = (bf16[80,1664]{1,0:T(8,128)(2,1)S(1)}, bf16[80,1664]{1,0:T(8,128)(2,1)S(1)}, u32[]{:S(2)}, u32[]{:S(2)}) collective-permute-start(bf16[80,1664]{1,0:T(8,128)(2,1)S(1)} %pad_maximum_fusion.16), channel_id=1, source_target_pairs={{0,4},{1,0},{2,6},{3,2},{4,5},{5,1},{6,7},{7,3},{8,12},{9,8},{10,1... | collective-permute-start | bytes 798728 | tf_op jit(solution)/shard_map/ppermute | solution.py:130
  79.5 11.0 %collective-permute-start.23 = (bf16[80,1664]{1,0:T(8,128)(2,1)S(1)}, bf16[80,1664]{1,0:T(8,128)(2,1)S(1)}, u32[]{:S(2)}, u32[]{:S(2)}) collective-permute-start(bf16[80,1664]{1,0:T(8,128)(2,1)S(1)} %pad_maximum_fusion.16), channel_id=1, source_target_pairs={{1,4},{3,6},{4,1},{6,3},{9,12},{11,14},{12,9},{14,11},{17,20},{19,... | collective-permute-start | bytes 798728 | tf_op jit(solution)/shard_map/ppermute | solution.py:130
  82.4 6.9 %collective-permute-start.19 = (bf16[40,1920]{1,0:T(8,128)(2,1)S(1)}, bf16[40,1920]{1,0:T(8,128)(2,1)S(1)}, u32[]{:S(2)}, u32[]{:S(2)}) collective-permute-start(bf16[40,1920]{1,0:T(8,128)(2,1)S(1)} %get-tuple-element.108), channel_id=1, source_target_pairs={{0,2},{1,3},{2,0},{3,1},{4,6},{5,7},{6,4},{7,5},{8,10},{9,11},{10,... | collective-permute-start | bytes 460808 | tf_op jit(solution)/shard_map/ppermute | solution.py:53
  84.1 11.2 %collective-permute-start.25 = (bf16[40,2304]{1,0:T(8,128)(2,1)S(1)}, bf16[40,2304]{1,0:T(8,128)(2,1)S(1)}, u32[]{:S(2)}, u32[]{:S(2)}) collective-permute-start(bf16[40,2304]{1,0:T(8,128)(2,1)S(1)} %fusion.39), channel_id=1, source_target_pairs={{0,8},{4,12},{8,0},{12,4},{1,9},{5,13},{9,1},{13,5},{2,10},{6,14},... | collective-permute-start | bytes 552968 | tf_op jit(solution)/shard_map/ppermute | solution.py:53
  84.3 11.9 %collective-permute-start.24 = (bf16[2,40,1280]{2,1,0:T(8,128)(2,1)S(1)}, bf16[2,40,1280]{2,1,0:T(8,128)(2,1)S(1)}, u32[]{:S(2)}, u32[]{:S(2)}) collective-permute-start(bf16[2,40,1280]{2,1,0:T(8,128)(2,1)S(1)} %pad_maximum_fusion.17), channel_id=1, source_target_pairs={{0,2},{1,3},{2,0},{3,1},{4,6},{5,7},{6,4},{7,5},{8,10},{9,11},{10,... | collective-permute-start | bytes 614408 | tf_op jit(solution)/shard_map/ppermute | solution.py:53
  89.4 15.1 %slice-start.10 = ((s8[14680064]{0:T(1024)(128)(4,1)}), s8[4194304]{0:T(1024)(128)(4,1)S(1)}, s32[]{:S(2)}) async-start(s8[14680064]{0:T(1024)(128)(4,1)} %bitcast.118), calls=%async_computation.10 | async-start | bytes 8388608
  89.4 11.5 %collective-permute-start.26 = (bf16[80,1920]{1,0:T(8,128)(2,1)S(1)}, bf16[80,1920]{1,0:T(8,128)(2,1)S(1)}, u32[]{:S(2)}, u32[]{:S(2)}) collective-permute-start(bf16[80,1920]{1,0:T(8,128)(2,1)S(1)} %pad_maximum_fusion.14), channel_id=1, source_target_pairs={{0,4},{1,0},{2,6},{3,2},{4,5},{5,1},{6,7},{7,3},{8,12},{9,8},{10,1... | collective-permute-start | bytes 921608 | tf_op jit(solution)/shard_map/ppermute | solution.py:130
  89.5 11.4 %collective-permute-start.27 = (bf16[80,1920]{1,0:T(8,128)(2,1)S(1)}, bf16[80,1920]{1,0:T(8,128)(2,1)S(1)}, u32[]{:S(2)}, u32[]{:S(2)}) collective-permute-start(bf16[80,1920]{1,0:T(8,128)(2,1)S(1)} %pad_maximum_fusion.14), channel_id=1, source_target_pairs={{1,4},{3,6},{4,1},{6,3},{9,12},{11,14},{12,9},{14,11},{17,20},{19,... | collective-permute-start | bytes 921608 | tf_op jit(solution)/shard_map/ppermute | solution.py:130
  95.3 6.1 %collective-permute-start.28 = (bf16[40,2304]{1,0:T(8,128)(2,1)S(1)}, bf16[40,2304]{1,0:T(8,128)(2,1)S(1)}, u32[]{:S(2)}, u32[]{:S(2)}) collective-permute-start(bf16[40,2304]{1,0:T(8,128)(2,1)S(1)} %get-tuple-element.92), channel_id=1, source_target_pairs={{0,2},{1,3},{2,0},{3,1},{4,6},{5,7},{6,4},{7,5},{8,10},{9,11},{10,... | collective-permute-start | bytes 552968 | tf_op jit(solution)/shard_map/ppermute | solution.py:53
  96.3 8.1 %slice-start.11 = ((s8[14680064]{0:T(1024)(128)(4,1)}), s8[4194304]{0:T(1024)(128)(4,1)S(1)}, s32[]{:S(2)}) async-start(s8[14680064]{0:T(1024)(128)(4,1)} %bitcast.118), calls=%async_computation.11 | async-start | bytes 8388608
  96.3 11.3 %collective-permute-start.30 = (bf16[40,1280]{1,0:T(8,128)(2,1)S(1)}, bf16[40,1280]{1,0:T(8,128)(2,1)S(1)}, u32[]{:S(2)}, u32[]{:S(2)}) collective-permute-start(bf16[40,1280]{1,0:T(8,128)(2,1)S(1)} %fusion.51), channel_id=1, source_target_pairs={{0,8},{4,12},{8,0},{12,4},{1,9},{5,13},{9,1},{13,5},{2,10},{6,14},... | collective-permute-start | bytes 307208 | tf_op jit(solution)/shard_map/ppermute | solution.py:53
  101.4 9.9 %collective-permute-start.32 = (bf16[80,2304]{1,0:T(8,128)(2,1)S(1)}, bf16[80,2304]{1,0:T(8,128)(2,1)S(1)}, u32[]{:S(2)}, u32[]{:S(2)}) collective-permute-start(bf16[80,2304]{1,0:T(8,128)(2,1)S(1)} %pad_maximum_fusion.10), channel_id=1, source_target_pairs={{0,4},{1,0},{2,6},{3,2},{4,5},{5,1},{6,7},{7,3},{8,12},{9,8},{10,1... | collective-permute-start | bytes 1105928 | tf_op jit(solution)/shard_map/ppermute | solution.py:130
  103.7 7.6 %collective-permute-start.33 = (bf16[80,2304]{1,0:T(8,128)(2,1)S(1)}, bf16[80,2304]{1,0:T(8,128)(2,1)S(1)}, u32[]{:S(2)}, u32[]{:S(2)}) collective-permute-start(bf16[80,2304]{1,0:T(8,128)(2,1)S(1)} %pad_maximum_fusion.10), channel_id=1, source_target_pairs={{1,4},{3,6},{4,1},{6,3},{9,12},{11,14},{12,9},{14,11},{17,20},{19,... | collective-permute-start | bytes 1105928 | tf_op jit(solution)/shard_map/ppermute | solution.py:130
  106.1 3.2 %collective-permute-start.29 = (bf16[80,2048]{1,0:T(8,128)(2,1)S(1)}, bf16[80,2048]{1,0:T(8,128)(2,1)S(1)}, u32[]{:S(2)}, u32[]{:S(2)}) collective-permute-start(bf16[80,2048]{1,0:T(8,128)(2,1)S(1)} %slice.504), channel_id=1, source_target_pairs={{0,1},{1,0},{2,3},{3,2},{4,5},{5,4},{6,7},{7,6},{8,9},{9,8},{10,11... | collective-permute-start | bytes 983048 | tf_op jit(solution)/shard_map/ppermute | solution.py:53
  107.6 5.6 %collective-permute-start.34 = (bf16[40,1280]{1,0:T(8,128)(2,1)S(1)}, bf16[40,1280]{1,0:T(8,128)(2,1)S(1)}, u32[]{:S(2)}, u32[]{:S(2)}) collective-permute-start(bf16[40,1280]{1,0:T(8,128)(2,1)S(1)} %get-tuple-element.116), channel_id=1, source_target_pairs={{0,2},{1,3},{2,0},{3,1},{4,6},{5,7},{6,4},{7,5},{8,10},{9,11},{10,... | collective-permute-start | bytes 307208 | tf_op jit(solution)/shard_map/ppermute | solution.py:53
  109.4 10.1 %collective-permute-start.31 = (bf16[80,2048]{1,0:T(8,128)(2,1)S(1)}, bf16[80,2048]{1,0:T(8,128)(2,1)S(1)}, u32[]{:S(2)}, u32[]{:S(2)}) collective-permute-start(bf16[80,2048]{1,0:T(8,128)(2,1)S(1)} %get-tuple-element.77), channel_id=1, source_target_pairs={{0,2},{1,3},{2,0},{3,1},{4,6},{5,7},{6,4},{7,5},{8,10},{9,11},{10,... | collective-permute-start | bytes 983048 | tf_op jit(solution)/shard_map/ppermute | solution.py:53
  113.2 8.0 %collective-permute-start.35 = (bf16[80,1280]{1,0:T(8,128)(2,1)S(1)}, bf16[80,1280]{1,0:T(8,128)(2,1)S(1)}, u32[]{:S(2)}, u32[]{:S(2)}) collective-permute-start(bf16[80,1280]{1,0:T(8,128)(2,1)S(1)} %pad_maximum_fusion.18), channel_id=1, source_target_pairs={{0,4},{1,0},{2,6},{3,2},{4,5},{5,1},{6,7},{7,3},{8,12},{9,8},{10,1... | collective-permute-start | bytes 614408 | tf_op jit(solution)/shard_map/ppermute | solution.py:130
  117.1 4.1 %collective-permute-start.36 = (bf16[80,1280]{1,0:T(8,128)(2,1)S(1)}, bf16[80,1280]{1,0:T(8,128)(2,1)S(1)}, u32[]{:S(2)}, u32[]{:S(2)}) collective-permute-start(bf16[80,1280]{1,0:T(8,128)(2,1)S(1)} %pad_maximum_fusion.18), channel_id=1, source_target_pairs={{1,4},{3,6},{4,1},{6,3},{9,12},{11,14},{12,9},{14,11},{17,20},{19,... | collective-permute-start | bytes 614408 | tf_op jit(solution)/shard_map/ppermute | solution.py:130
  122.4 2.8 %collective-permute-start.37 = (bf16[80,2048]{1,0:T(8,128)(2,1)S(1)}, bf16[80,2048]{1,0:T(8,128)(2,1)S(1)}, u32[]{:S(2)}, u32[]{:S(2)}) collective-permute-start(bf16[80,2048]{1,0:T(8,128)(2,1)S(1)} %slice.503), channel_id=1, source_target_pairs={{0,1},{1,0},{2,3},{3,2},{4,5},{5,4},{6,7},{7,6},{8,9},{9,8},{10,11... | collective-permute-start | bytes 983048 | tf_op jit(solution)/shard_map/ppermute | solution.py:53
  125.3 10.1 %collective-permute-start.38 = (bf16[80,2048]{1,0:T(8,128)(2,1)S(1)}, bf16[80,2048]{1,0:T(8,128)(2,1)S(1)}, u32[]{:S(2)}, u32[]{:S(2)}) collective-permute-start(bf16[80,2048]{1,0:T(8,128)(2,1)S(1)} %fusion.35), channel_id=1, source_target_pairs={{0,2},{1,3},{2,0},{3,1},{4,6},{5,7},{6,4},{7,5},{8,10},{9,11},{10,... | collective-permute-start | bytes 983048 | tf_op jit(solution)/shard_map/ppermute | solution.py:53
  127.1 9.4 %collective-permute-start.39 = (bf16[80,2048]{1,0:T(8,128)(2,1)}, bf16[80,2048]{1,0:T(8,128)(2,1)S(1)}, u32[]{:S(2)}, u32[]{:S(2)}) collective-permute-start(bf16[80,2048]{1,0:T(8,128)(2,1)} %get-tuple-element.73), channel_id=1, source_target_pairs={{0,1},{1,0},{2,3},{3,2},{4,5},{5,4},{6,7},{7,6},{8,9},{9,8},{10,11... | collective-permute-start | bytes 983048 | tf_op jit(solution)/shard_map/ppermute | solution.py:53
  135.5 1.7 %collective-permute-start.40 = (bf16[80,2048]{1,0:T(8,128)(2,1)S(1)}, bf16[80,2048]{1,0:T(8,128)(2,1)S(1)}, u32[]{:S(2)}, u32[]{:S(2)}) collective-permute-start(bf16[80,2048]{1,0:T(8,128)(2,1)S(1)} %get-tuple-element.75), channel_id=1, source_target_pairs={{0,1},{1,0},{2,3},{3,2},{4,5},{5,4},{6,7},{7,6},{8,9},{9,8},{10,11... | collective-permute-start | bytes 983048 | tf_op jit(solution)/shard_map/ppermute | solution.py:53

commit v23 on v22

--- a/solution.py
+++ b/solution.py
@@ -15,7 +15,6 @@
     "t0.cores": ["w.pull"],
     "t1.columns": ["t0.cores"],
     "c00.dots": ["t1.columns"],
-    "t1.cores": ["c00.dots"],
     "c01.dots": ["c00.sum"],
     "c10.dots": ["c01.sum"],
     "c00.hidden": ["c10.dots"],
@@ -35,11 +34,9 @@
     "c10.columns": ["c01.cores"],
     "c01.down": ["c10.columns"],
     "c11.halves": ["c01.down"],
-    "c10.cores": ["b0.total"],
+    "b0.total": ["c11.halves"],
     "c11.columns": ["c10.down"],
-    "b0.total": ["c11.halves"],
     "c11.cores": ["b0.all"],
-    "c11.down": ["b0.all"],
     "b1.total": ["c11.down"],
 }
 

time: 140 us -> 147 us (1.050)
  starting transfers between devices: 49.9 us -> 59.4 us
    ppermute x12, starting transfers between devices: 15.5 us -> 25.9 us  [move(): return lax.ppermute(value, ('row', 'col'), pairs)]
    ppermute x29, waiting for transfers between devices: 46.4 us -> 39.3 us  [flip(): return lax.ppermute(value, axis, [(i, i ^ bit) for i in range(count)])]
    ppermute x12, waiting for transfers between devices: 1.59 us -> 7.71 us  [move(): return lax.ppermute(value, ('row', 'col'), pairs)]
  transfers between devices with their start and end apart: 41 -> 41, of which waited for: 17 -> 18; matrix products, arithmetic and copies ran while one was open for 20% -> 18% of each run, Pallas kernels for 4% -> 4%
where the time goes in v23:
time: 147 us
  starting transfers between devices  59.4 us (40%)
  waiting for transfers between devices  47 us (32%)
  matrix products  25.9 us (18%)
  other arithmetic  6.36 us (4%)
  Pallas kernels  5.57 us (4%)
    ppermute x29, waiting for transfers between devices, flip(): return lax.ppermute(value, axis, [(i, i ^ bit) for i in range(count)])  39.3 us
    ppermute x29, starting transfers between devices, flip(): return lax.ppermute(value, axis, [(i, i ^ bit) for i in range(count)])  33.4 us
    ppermute x12, starting transfers between devices, move(): return lax.ppermute(value, ('row', 'col'), pairs)  25.9 us
    dot_general x17, matrix products, dot(): return jnp.dot(a, b, preferred_element_type=jnp.float32)  25.1 us
    ppermute x12, waiting for transfers between devices, move(): return lax.ppermute(value, ('row', 'col'), pairs)  7.71 us
    pallas_call x1, Pallas kernels, pull(): pl.pallas_call(functools.partial(pull_kernel, first, end), in_specs=[pl.B...  5.57 us
  transfers between devices with their start and end apart: 41, of which 18 were waited for; matrix products, arithmetic and copies ran while one was open for 18% of the time, Pallas kernels for 4%

profile of v23, /device:TPU:0, one launch (start us, length us, event | category | flops | bytes accessed | tf_op | source)
XLA Modules:
  0.0 146.5 jit_solution(3082022888841483450)
XLA Ops:
  0.5 0.9 fusion.84
  1.5 1.4 fusion.74
  3.2 2.6 %collective-permute-start.1 = (bf16[40,2048]{1,0:T(8,128)(2,1)S(1)}, bf16[40,2048]{1,0:T(8,128)(2,1)S(1)}, u32[]{:S(2)}, u32[]{:S(2)}) collective-permute-start(bf16[40,2048]{1,0:T(8,128)(2,1)S(1)} %slice.314), channel_id=1, source_target_pairs={{0,2},{1,3},{2,0},{3,1},{4,6},{5,7},{6,4},{7,5},{8,10},{9,11},{10,... | collective-permute-start | bytes 491528 | tf_op jit(solution)/shard_map/ppermute | solution.py:50
  5.8 4.9 %collective-permute-done.1 = bf16[40,2048]{1,0:T(8,128)(2,1)S(1)} collective-permute-done((bf16[40,2048]{1,0:T(8,128)(2,1)S(1)}, bf16[40,2048]{1,0:T(8,128)(2,1)S(1)}, u32[]{:S(2)}, u32[]{:S(2)}) %collective-permute-start.1) | collective-permute-done | bytes 163872 | tf_op jit(solution)/shard_map/ppermute | solution.py:50
  10.7 2.9 %collective-permute-start.2 = (bf16[40,2048]{1,0:T(8,128)(2,1)S(1)}, bf16[40,2048]{1,0:T(8,128)(2,1)S(1)}, u32[]{:S(2)}, u32[]{:S(2)}) collective-permute-start(bf16[40,2048]{1,0:T(8,128)(2,1)S(1)} %slice_add_fusion.19), channel_id=1, source_target_pairs={{0,8},{4,12},{8,0},{12,4},{1,9},{5,13},{9,1},{13,5},{2,10},{6,14},... | collective-permute-start | bytes 491528 | tf_op jit(solution)/shard_map/ppermute | solution.py:50
  14.2 1.6 %collective-permute-start.6 = (bf16[40,2048]{1,0:T(8,128)(2,1)S(1)}, bf16[40,2048]{1,0:T(8,128)(2,1)S(1)}, u32[]{:S(2)}, u32[]{:S(2)}) collective-permute-start(bf16[40,2048]{1,0:T(8,128)(2,1)S(1)} %slice.316), channel_id=1, source_target_pairs={{0,2},{1,3},{2,0},{3,1},{4,6},{5,7},{6,4},{7,5},{8,10},{9,11},{10,... | collective-permute-start | bytes 491528 | tf_op jit(solution)/shard_map/ppermute | solution.py:50
  15.8 5.4 %collective-permute-done.2 = bf16[40,2048]{1,0:T(8,128)(2,1)S(1)} collective-permute-done((bf16[40,2048]{1,0:T(8,128)(2,1)S(1)}, bf16[40,2048]{1,0:T(8,128)(2,1)S(1)}, u32[]{:S(2)}, u32[]{:S(2)}) %collective-permute-start.2) | collective-permute-done | bytes 163872 | tf_op jit(solution)/shard_map/ppermute | solution.py:50
  21.2 1.6 %collective-permute-start.3 = (bf16[40,2048]{1,0:T(8,128)(2,1)S(1)}, bf16[40,2048]{1,0:T(8,128)(2,1)S(1)}, u32[]{:S(2)}, u32[]{:S(2)}) collective-permute-start(bf16[40,2048]{1,0:T(8,128)(2,1)S(1)} %get-tuple-element.96), channel_id=1, source_target_pairs={{0,2},{1,3},{2,0},{3,1},{4,6},{5,7},{6,4},{7,5},{8,10},{9,11},{10,... | collective-permute-start | bytes 491528 | tf_op jit(solution)/shard_map/ppermute | solution.py:50
  22.9 3.7 %collective-permute-done.3 = bf16[40,2048]{1,0:T(8,128)(2,1)S(1)} collective-permute-done((bf16[40,2048]{1,0:T(8,128)(2,1)S(1)}, bf16[40,2048]{1,0:T(8,128)(2,1)S(1)}, u32[]{:S(2)}, u32[]{:S(2)}) %collective-permute-start.3) | collective-permute-done | bytes 163872 | tf_op jit(solution)/shard_map/ppermute | solution.py:50
  27.3 2.8 %collective-permute-start.4 = (bf16[80,2048]{1,0:T(8,128)(2,1)S(1)}, bf16[80,2048]{1,0:T(8,128)(2,1)S(1)}, u32[]{:S(2)}, u32[]{:S(2)}) collective-permute-start(bf16[80,2048]{1,0:T(8,128)(2,1)S(1)} %pad_maximum_fusion.10), channel_id=1, source_target_pairs={{0,4},{1,0},{2,6},{3,2},{4,5},{5,1},{6,7},{7,3},{8,12},{9,8},{10,1... | collective-permute-start | bytes 983048 | tf_op jit(solution)/shard_map/ppermute | solution.py:127
  30.1 2.2 %collective-permute-done.7 = bf16[40,2048]{1,0:T(8,128)(2,1)S(1)} collective-permute-done((bf16[40,2048]{1,0:T(8,128)(2,1)S(1)}, bf16[40,2048]{1,0:T(8,128)(2,1)S(1)}, u32[]{:S(2)}, u32[]{:S(2)}) %collective-permute-start.7) | collective-permute-done | bytes 163872 | tf_op jit(solution)/shard_map/ppermute | solution.py:50
  32.9 5.6 %shard_map.55 = (bf16[2048,1664]{1,0:T(8,128)(2,1)S(1)}, bf16[2048,1664]{1,0:T(8,128)(2,1)S(1)}) custom-call(s32[4]{0:T(128)S(1)} %copy-done, bf16[2048,3584]{1,0:T(8,128)(2,1)} %gate_ref.1, bf16[2048,3584]{1,0:T(8,128)(2,1)} %up_ref.1), custom_call_target="tpu_custom_call" | custom-call | tf_op jit(solution)/shard_map/pallas_call | solution.py:70
  38.7 1.4 fusion.97
  40.1 1.4 fusion.98
  42.3 0.8 collective-permute-start.12
  43.2 3.4 %collective-permute-start.11 = (bf16[80,2048]{1,0:T(8,128)(2,1)S(1)}, bf16[80,2048]{1,0:T(8,128)(2,1)S(1)}, u32[]{:S(2)}, u32[]{:S(2)}) collective-permute-start(bf16[80,2048]{1,0:T(8,128)(2,1)S(1)} %pad_maximum_fusion.11), channel_id=1, source_target_pairs={{0,4},{1,0},{2,6},{3,2},{4,5},{5,1},{6,7},{7,3},{8,12},{9,8},{10,1... | collective-permute-start | bytes 983048 | tf_op jit(solution)/shard_map/ppermute | solution.py:127
  46.7 0.7 pad_maximum_fusion.14
  47.5 1.6 %fusion.8 = f32[160,1920]{1,0:T(8,128)S(1)} fusion(bf16[160,2048]{1,0:T(8,128)(2,1)S(1)} %pad_maximum_fusion.1, bf16[2048,3584]{1,0:T(8,128)(2,1)S(1)} %bitcast.107), kind=kOutput, calls=%fused_computation.8 | convolution fusion | flops 1258291200 | bytes 9748480 | tf_op jit(solution)/shard_map/dot_general | solution.py:45
  49.1 1.6 %fusion.10 = f32[160,1920]{1,0:T(8,128)S(1)} fusion(bf16[160,2048]{1,0:T(8,128)(2,1)S(1)} %pad_maximum_fusion.1, bf16[2048,3584]{1,0:T(8,128)(2,1)S(1)} %bitcast.109), kind=kOutput, calls=%fused_computation.10 | convolution fusion | flops 1258291200 | bytes 9748480 | tf_op jit(solution)/shard_map/dot_general | solution.py:45
  51.0 2.2 %collective-permute-done.11 = bf16[80,2048]{1,0:T(8,128)(2,1)S(1)} collective-permute-done((bf16[80,2048]{1,0:T(8,128)(2,1)S(1)}, bf16[80,2048]{1,0:T(8,128)(2,1)S(1)}, u32[]{:S(2)}, u32[]{:S(2)}) %collective-permute-start.11) | collective-permute-done | bytes 327712 | tf_op jit(solution)/shard_map/ppermute | solution.py:127
  53.4 1.6 %collective-permute-start.10 = (bf16[2,40,1664]{2,1,0:T(8,128)(2,1)}, bf16[2,40,1664]{2,1,0:T(8,128)(2,1)}, u32[]{:S(2)}, u32[]{:S(2)}) collective-permute-start(bf16[2,40,1664]{2,1,0:T(8,128)(2,1)} %pad_maximum_fusion.14), channel_id=1, source_target_pairs={{0,2},{1,3},{2,0},{3,1},{4,6},{5,7},{6,4},{7,5},{8,10},{9,11},{10,... | collective-permute-start | bytes 798728 | tf_op jit(solution)/shard_map/ppermute | solution.py:50
  55.1 0.8 pad_maximum_fusion.12
  55.9 1.7 %fusion.2 = f32[160,2304]{1,0:T(8,128)S(1)} fusion(bf16[160,2048]{1,0:T(8,128)(2,1)S(1)} %pad_maximum_fusion.2, bf16[2048,3584]{1,0:T(8,128)(2,1)S(1)} %bitcast.107), kind=kOutput, calls=%fused_computation.2 | convolution fusion | flops 1509949440 | bytes 11567104 | tf_op jit(solution)/shard_map/dot_general | solution.py:45
  57.6 2.9 %fusion.4 = f32[160,2304]{1,0:T(8,128)S(1)} fusion(bf16[160,2048]{1,0:T(8,128)(2,1)} %copy-done.2, bf16[2048,3584]{1,0:T(8,128)(2,1)S(1)} %bitcast.109), kind=kOutput, calls=%fused_computation.4 | convolution fusion | flops 1509949440 | bytes 11567104 | tf_op jit(solution)/shard_map/dot_general | solution.py:45
  60.7 1.3 collective-permute-start.17
  62.5 1.1 fusion.51
  63.6 3.8 %collective-permute-start.14 = (bf16[40,1664]{1,0:T(8,128)(2,1)S(1)}, bf16[40,1664]{1,0:T(8,128)(2,1)S(1)}, u32[]{:S(2)}, u32[]{:S(2)}) collective-permute-start(bf16[40,1664]{1,0:T(8,128)(2,1)S(1)} %fusion.51), channel_id=1, source_target_pairs={{0,8},{4,12},{8,0},{12,4},{1,9},{5,13},{9,1},{13,5},{2,10},{6,14},... | collective-permute-start | bytes 399368 | tf_op jit(solution)/shard_map/ppermute | solution.py:50
  67.4 1.5 %collective-permute-start.16 = (bf16[2,40,1920]{2,1,0:T(8,128)(2,1)S(1)}, bf16[2,40,1920]{2,1,0:T(8,128)(2,1)S(1)}, u32[]{:S(2)}, u32[]{:S(2)}) collective-permute-start(bf16[2,40,1920]{2,1,0:T(8,128)(2,1)S(1)} %copy-done.4), channel_id=1, source_target_pairs={{0,2},{1,3},{2,0},{3,1},{4,6},{5,7},{6,4},{7,5},{8,10},{9,11},{10,... | collective-permute-start | bytes 921608 | tf_op jit(solution)/shard_map/ppermute | solution.py:50
  68.9 5.1 %collective-permute-done.14 = bf16[40,1664]{1,0:T(8,128)(2,1)S(1)} collective-permute-done((bf16[40,1664]{1,0:T(8,128)(2,1)S(1)}, bf16[40,1664]{1,0:T(8,128)(2,1)S(1)}, u32[]{:S(2)}, u32[]{:S(2)}) %collective-permute-start.14) | collective-permute-done | bytes 133152 | tf_op jit(solution)/shard_map/ppermute | solution.py:50
  74.0 0.8 collective-permute-start.15
  75.1 1.2 collective-permute-done.16
  76.5 1.1 collective-permute-start.18
  77.5 1.8 %collective-permute-start.21 = (bf16[2,40,2304]{2,1,0:T(8,128)(2,1)S(1)}, bf16[2,40,2304]{2,1,0:T(8,128)(2,1)S(1)}, u32[]{:S(2)}, u32[]{:S(2)}) collective-permute-start(bf16[2,40,2304]{2,1,0:T(8,128)(2,1)S(1)} %pad_maximum_fusion.8), channel_id=1, source_target_pairs={{0,2},{1,3},{2,0},{3,1},{4,6},{5,7},{6,4},{7,5},{8,10},{9,11},{10,... | collective-permute-start | bytes 1105928 | tf_op jit(solution)/shard_map/ppermute | solution.py:50
  79.3 1.0 fusion.16
  80.4 1.0 fusion.18
  81.6 0.8 collective-permute-start.23
  82.4 2.1 %collective-permute-start.22 = (bf16[80,1664]{1,0:T(8,128)(2,1)S(1)}, bf16[80,1664]{1,0:T(8,128)(2,1)S(1)}, u32[]{:S(2)}, u32[]{:S(2)}) collective-permute-start(bf16[80,1664]{1,0:T(8,128)(2,1)S(1)} %pad_maximum_fusion.15), channel_id=1, source_target_pairs={{0,4},{1,0},{2,6},{3,2},{4,5},{5,1},{6,7},{7,3},{8,12},{9,8},{10,1... | collective-permute-start | bytes 798728 | tf_op jit(solution)/shard_map/ppermute | solution.py:127
  85.5 0.9 collective-permute-start.19
  86.4 0.8 collective-permute-done.21
  87.4 1.4 collective-permute-start.25
  88.9 1.6 %collective-permute-start.24 = (bf16[2,40,1280]{2,1,0:T(8,128)(2,1)S(1)}, bf16[2,40,1280]{2,1,0:T(8,128)(2,1)S(1)}, u32[]{:S(2)}, u32[]{:S(2)}) collective-permute-start(bf16[2,40,1280]{2,1,0:T(8,128)(2,1)S(1)} %pad_maximum_fusion.16), channel_id=1, source_target_pairs={{0,2},{1,3},{2,0},{3,1},{4,6},{5,7},{6,4},{7,5},{8,10},{9,11},{10,... | collective-permute-start | bytes 614408 | tf_op jit(solution)/shard_map/ppermute | solution.py:50
  90.5 1.1 collective-permute-done.19
  91.6 0.8 collective-permute-start.27
  92.4 3.0 %collective-permute-start.26 = (bf16[80,1920]{1,0:T(8,128)(2,1)S(1)}, bf16[80,1920]{1,0:T(8,128)(2,1)S(1)}, u32[]{:S(2)}, u32[]{:S(2)}) collective-permute-start(bf16[80,1920]{1,0:T(8,128)(2,1)S(1)} %pad_maximum_fusion.13), channel_id=1, source_target_pairs={{0,4},{1,0},{2,6},{3,2},{4,5},{5,1},{6,7},{7,3},{8,12},{9,8},{10,1... | collective-permute-start | bytes 921608 | tf_op jit(solution)/shard_map/ppermute | solution.py:127
  95.5 2.4 %collective-permute-done.25 = bf16[40,2304]{1,0:T(8,128)(2,1)S(1)} collective-permute-done((bf16[40,2304]{1,0:T(8,128)(2,1)S(1)}, bf16[40,2304]{1,0:T(8,128)(2,1)S(1)}, u32[]{:S(2)}, u32[]{:S(2)}) %collective-permute-start.25) | collective-permute-done | bytes 184352 | tf_op jit(solution)/shard_map/ppermute | solution.py:50
  98.0 1.7 %collective-permute-start.28 = (bf16[40,2304]{1,0:T(8,128)(2,1)S(1)}, bf16[40,2304]{1,0:T(8,128)(2,1)S(1)}, u32[]{:S(2)}, u32[]{:S(2)}) collective-permute-start(bf16[40,2304]{1,0:T(8,128)(2,1)S(1)} %get-tuple-element.84), channel_id=1, source_target_pairs={{0,2},{1,3},{2,0},{3,1},{4,6},{5,7},{6,4},{7,5},{8,10},{9,11},{10,... | collective-permute-start | bytes 552968 | tf_op jit(solution)/shard_map/ppermute | solution.py:50
  99.8 4.4 %fusion.12 = f32[160,2048]{1,0:T(8,128)S(1)} fusion(bf16[160,1664]{1,0:T(8,128)(2,1)S(1)} %pad_maximum_fusion.6, bf16[3584,2048]{1,0:T(8,128)(2,1)} %param.9), kind=kOutput, calls=%fused_computation.12 | convolution fusion | flops 1090519040 | bytes 8658944 | tf_op jit(solution)/shard_map/dot_general | solution.py:45
  105.1 4.8 %collective-permute-start.32 = (bf16[80,2304]{1,0:T(8,128)(2,1)S(1)}, bf16[80,2304]{1,0:T(8,128)(2,1)S(1)}, u32[]{:S(2)}, u32[]{:S(2)}) collective-permute-start(bf16[80,2304]{1,0:T(8,128)(2,1)S(1)} %pad_maximum_fusion.9), channel_id=1, source_target_pairs={{0,4},{1,0},{2,6},{3,2},{4,5},{5,1},{6,7},{7,3},{8,12},{9,8},{10,1... | collective-permute-start | bytes 1105928 | tf_op jit(solution)/shard_map/ppermute | solution.py:127
  110.0 1.6 %fusion.95 = f32[160,2048]{1,0:T(8,128)S(1)} fusion(f32[160,2048]{1,0:T(8,128)S(1)} %fusion.12, bf16[160,1920]{1,0:T(8,128)(2,1)S(1)} %pad_maximum_fusion.4, bf16[3584,2048]{1,0:T(8,128)(2,1)S(1)} %bitcast.118), kind=kOutput, calls=%fused_computation.198 | convolution fusion | flops 1258618880 | bytes 11100160 | tf_op jit(solution)/shard_map/dot_general | solution.py:45
  111.8 0.8 collective-permute-start.34
  112.6 0.8 collective-permute-done.29
  113.4 0.8 collective-permute-start.31
  114.2 2.4 %collective-permute-done.32 = bf16[80,2304]{1,0:T(8,128)(2,1)S(1)} collective-permute-done((bf16[80,2304]{1,0:T(8,128)(2,1)S(1)}, bf16[80,2304]{1,0:T(8,128)(2,1)S(1)}, u32[]{:S(2)}, u32[]{:S(2)}) %collective-permute-start.32) | collective-permute-done | bytes 368672 | tf_op jit(solution)/shard_map/ppermute | solution.py:127
  116.8 1.7 %fusion = f32[160,2048]{1,0:T(8,128)S(1)} fusion(bf16[3584,2048]{1,0:T(8,128)(2,1)S(1)} %bitcast.118, bf16[80,2304]{1,0:T(8,128)(2,1)S(1)} %get-tuple-element.82, bf16[80,2304]{1,0:T(8,128)(2,1)S(1)} %get-tuple-element.81), kind=kOutput, calls=%fused_computation | convolution fusion | flops 1511424000 | bytes 11485184 | tf_op jit(solution)/shard_map/dot_general | solution.py:45
  119.3 5.3 %collective-permute-start.35 = (bf16[80,1280]{1,0:T(8,128)(2,1)S(1)}, bf16[80,1280]{1,0:T(8,128)(2,1)S(1)}, u32[]{:S(2)}, u32[]{:S(2)}) collective-permute-start(bf16[80,1280]{1,0:T(8,128)(2,1)S(1)} %pad_maximum_fusion.17), channel_id=1, source_target_pairs={{0,4},{1,0},{2,6},{3,2},{4,5},{5,1},{6,7},{7,3},{8,12},{9,8},{10,1... | collective-permute-start | bytes 614408 | tf_op jit(solution)/shard_map/ppermute | solution.py:127
  124.8 3.1 %collective-permute-done.35 = bf16[80,1280]{1,0:T(8,128)(2,1)S(1)} collective-permute-done((bf16[80,1280]{1,0:T(8,128)(2,1)S(1)}, bf16[80,1280]{1,0:T(8,128)(2,1)S(1)}, u32[]{:S(2)}, u32[]{:S(2)}) %collective-permute-start.35) | collective-permute-done | bytes 204832 | tf_op jit(solution)/shard_map/ppermute | solution.py:127
  127.9 1.0 fusion.96
  129.0 0.8 slice.507
  129.7 2.1 %collective-permute-start.37 = (bf16[80,2048]{1,0:T(8,128)(2,1)}, bf16[80,2048]{1,0:T(8,128)(2,1)S(1)}, u32[]{:S(2)}, u32[]{:S(2)}) collective-permute-start(bf16[80,2048]{1,0:T(8,128)(2,1)} %slice.507), channel_id=1, source_target_pairs={{0,1},{1,0},{2,3},{3,2},{4,5},{5,4},{6,7},{7,6},{8,9},{9,8},{10,11... | collective-permute-start | bytes 983048 | tf_op jit(solution)/shard_map/ppermute | solution.py:50
  131.9 1.4 collective-permute-done.37
  133.3 1.5 %collective-permute-start.38 = (bf16[80,2048]{1,0:T(8,128)(2,1)S(1)}, bf16[80,2048]{1,0:T(8,128)(2,1)S(1)}, u32[]{:S(2)}, u32[]{:S(2)}) collective-permute-start(bf16[80,2048]{1,0:T(8,128)(2,1)S(1)} %fusion.36), channel_id=1, source_target_pairs={{0,2},{1,3},{2,0},{3,1},{4,6},{5,7},{6,4},{7,5},{8,10},{9,11},{10,... | collective-permute-start | bytes 983048 | tf_op jit(solution)/shard_map/ppermute | solution.py:50
  135.0 8.4 %collective-permute-done.38 = bf16[80,2048]{1,0:T(8,128)(2,1)S(1)} collective-permute-done((bf16[80,2048]{1,0:T(8,128)(2,1)S(1)}, bf16[80,2048]{1,0:T(8,128)(2,1)S(1)}, u32[]{:S(2)}, u32[]{:S(2)}) %collective-permute-start.38) | collective-permute-done | bytes 327712 | tf_op jit(solution)/shard_map/ppermute | solution.py:50
  143.7 0.8 fusion.25
  145.2 1.3 fusion.22
  (151 shorter events, 10.8 us)
Async XLA Ops:
  0.0 2.9 %collective-permute-start = (bf16[160,2048]{1,0:T(8,128)(2,1)}, bf16[160,2048]{1,0:T(8,128)(2,1)S(1)}, u32[]{:S(2)}, u32[]{:S(2)}) collective-permute-start(bf16[160,2048]{1,0:T(8,128)(2,1)} %param.5), channel_id=1, source_target_pairs={{0,1},{1,0},{2,3},{3,2},{4,5},{5,4},{6,7},{7,6},{8,9},{9,8},{10,11... | collective-permute-start | bytes 1966088 | tf_op jit(solution)/shard_map/ppermute | solution.py:50
  2.9 10.7 %copy-start.1 = (bf16[160,2048]{1,0:T(8,128)(2,1)S(1)}, bf16[160,2048]{1,0:T(8,128)(2,1)}, u32[]{:S(2)}) copy-start(bf16[160,2048]{1,0:T(8,128)(2,1)} %param.5) | copy-start | bytes 1966084
  3.2 7.4 %collective-permute-start.1 = (bf16[40,2048]{1,0:T(8,128)(2,1)S(1)}, bf16[40,2048]{1,0:T(8,128)(2,1)S(1)}, u32[]{:S(2)}, u32[]{:S(2)}) collective-permute-start(bf16[40,2048]{1,0:T(8,128)(2,1)S(1)} %slice.314), channel_id=1, source_target_pairs={{0,2},{1,3},{2,0},{3,1},{4,6},{5,7},{6,4},{7,5},{8,10},{9,11},{10,... | collective-permute-start | bytes 491528 | tf_op jit(solution)/shard_map/ppermute | solution.py:50
  10.7 10.5 %collective-permute-start.2 = (bf16[40,2048]{1,0:T(8,128)(2,1)S(1)}, bf16[40,2048]{1,0:T(8,128)(2,1)S(1)}, u32[]{:S(2)}, u32[]{:S(2)}) collective-permute-start(bf16[40,2048]{1,0:T(8,128)(2,1)S(1)} %slice_add_fusion.19), channel_id=1, source_target_pairs={{0,8},{4,12},{8,0},{12,4},{1,9},{5,13},{9,1},{13,5},{2,10},{6,14},... | collective-permute-start | bytes 491528 | tf_op jit(solution)/shard_map/ppermute | solution.py:50
  14.2 18.7 %copy-start = (s32[4]{0:T(128)S(1)}, s32[4]{0:T(128)}, u32[]{:S(2)}) copy-start(s32[4]{0:T(128)} %tick_ref) | copy-start | bytes 52
  14.2 8.6 %collective-permute-start.6 = (bf16[40,2048]{1,0:T(8,128)(2,1)S(1)}, bf16[40,2048]{1,0:T(8,128)(2,1)S(1)}, u32[]{:S(2)}, u32[]{:S(2)}) collective-permute-start(bf16[40,2048]{1,0:T(8,128)(2,1)S(1)} %slice.316), channel_id=1, source_target_pairs={{0,2},{1,3},{2,0},{3,1},{4,6},{5,7},{6,4},{7,5},{8,10},{9,11},{10,... | collective-permute-start | bytes 491528 | tf_op jit(solution)/shard_map/ppermute | solution.py:50
  21.2 5.4 %collective-permute-start.3 = (bf16[40,2048]{1,0:T(8,128)(2,1)S(1)}, bf16[40,2048]{1,0:T(8,128)(2,1)S(1)}, u32[]{:S(2)}, u32[]{:S(2)}) collective-permute-start(bf16[40,2048]{1,0:T(8,128)(2,1)S(1)} %get-tuple-element.96), channel_id=1, source_target_pairs={{0,2},{1,3},{2,0},{3,1},{4,6},{5,7},{6,4},{7,5},{8,10},{9,11},{10,... | collective-permute-start | bytes 491528 | tf_op jit(solution)/shard_map/ppermute | solution.py:50
  22.8 9.5 %collective-permute-start.7 = (bf16[40,2048]{1,0:T(8,128)(2,1)S(1)}, bf16[40,2048]{1,0:T(8,128)(2,1)S(1)}, u32[]{:S(2)}, u32[]{:S(2)}) collective-permute-start(bf16[40,2048]{1,0:T(8,128)(2,1)S(1)} %slice_add_fusion.18), channel_id=1, source_target_pairs={{0,8},{4,12},{8,0},{12,4},{1,9},{5,13},{9,1},{13,5},{2,10},{6,14},... | collective-permute-start | bytes 491528 | tf_op jit(solution)/shard_map/ppermute | solution.py:50
  26.6 11.8 %collective-permute-start.5 = (bf16[80,2048]{1,0:T(8,128)(2,1)S(1)}, bf16[80,2048]{1,0:T(8,128)(2,1)S(1)}, u32[]{:S(2)}, u32[]{:S(2)}) collective-permute-start(bf16[80,2048]{1,0:T(8,128)(2,1)S(1)} %pad_maximum_fusion.10), channel_id=1, source_target_pairs={{1,4},{3,6},{4,1},{6,3},{9,12},{11,14},{12,9},{14,11},{17,20},{19,... | collective-permute-start | bytes 983048 | tf_op jit(solution)/shard_map/ppermute | solution.py:127
  27.3 11.2 %collective-permute-start.4 = (bf16[80,2048]{1,0:T(8,128)(2,1)S(1)}, bf16[80,2048]{1,0:T(8,128)(2,1)S(1)}, u32[]{:S(2)}, u32[]{:S(2)}) collective-permute-start(bf16[80,2048]{1,0:T(8,128)(2,1)S(1)} %pad_maximum_fusion.10), channel_id=1, source_target_pairs={{0,4},{1,0},{2,6},{3,2},{4,5},{5,1},{6,7},{7,3},{8,12},{9,8},{10,1... | collective-permute-start | bytes 983048 | tf_op jit(solution)/shard_map/ppermute | solution.py:127
  32.3 6.3 %collective-permute-start.8 = (bf16[40,2048]{1,0:T(8,128)(2,1)S(1)}, bf16[40,2048]{1,0:T(8,128)(2,1)S(1)}, u32[]{:S(2)}, u32[]{:S(2)}) collective-permute-start(bf16[40,2048]{1,0:T(8,128)(2,1)S(1)} %get-tuple-element.92), channel_id=1, source_target_pairs={{0,2},{1,3},{2,0},{3,1},{4,6},{5,7},{6,4},{7,5},{8,10},{9,11},{10,... | collective-permute-start | bytes 491528 | tf_op jit(solution)/shard_map/ppermute | solution.py:50
  38.6 8.9 %slice-start = ((s8[14680064]{0:T(1024)(128)(4,1)}), s8[4194304]{0:T(1024)(128)(4,1)S(1)}, s32[]{:S(2)}) async-start(s8[14680064]{0:T(1024)(128)(4,1)} %bitcast.106), calls=%async_computation | async-start | bytes 8388608
  38.6 8.8 %slice-start.1 = ((s8[14680064]{0:T(1024)(128)(4,1)}), s8[2097152]{0:T(1024)(128)(4,1)S(1)}, s32[]{:S(2)}) async-start(s8[14680064]{0:T(1024)(128)(4,1)} %bitcast.106), calls=%async_computation.1 | async-start | bytes 4194304
  38.6 10.4 %slice-start.4 = ((s8[14680064]{0:T(1024)(128)(4,1)}), s8[4194304]{0:T(1024)(128)(4,1)S(1)}, s32[]{:S(2)}) async-start(s8[14680064]{0:T(1024)(128)(4,1)} %bitcast.108), calls=%async_computation.4 | async-start | bytes 8388608
  38.7 10.4 %slice-start.5 = ((s8[14680064]{0:T(1024)(128)(4,1)}), s8[4194304]{0:T(1024)(128)(4,1)S(1)}, s32[]{:S(2)}) async-start(s8[14680064]{0:T(1024)(128)(4,1)} %bitcast.108), calls=%async_computation.5 | async-start | bytes 8388608
  40.1 7.4 %slice-start.2 = ((s8[14680064]{0:T(1024)(128)(4,1)}), s8[4194304]{0:T(1024)(128)(4,1)S(1)}, s32[]{:S(2)}) async-start(s8[14680064]{0:T(1024)(128)(4,1)} %bitcast.106), calls=%async_computation.2 | async-start | bytes 8388608
  40.1 7.4 %slice-start.3 = ((s8[14680064]{0:T(1024)(128)(4,1)}), s8[4194304]{0:T(1024)(128)(4,1)S(1)}, s32[]{:S(2)}) async-start(s8[14680064]{0:T(1024)(128)(4,1)} %bitcast.106), calls=%async_computation.3 | async-start | bytes 8388608
  40.1 9.0 %slice-start.6 = ((s8[14680064]{0:T(1024)(128)(4,1)}), s8[4194304]{0:T(1024)(128)(4,1)S(1)}, s32[]{:S(2)}) async-start(s8[14680064]{0:T(1024)(128)(4,1)} %bitcast.108), calls=%async_computation.6 | async-start | bytes 8388608
  41.7 4.9 %collective-permute-start.9 = (bf16[2,80,1664]{2,1,0:T(8,128)(2,1)S(1)}, bf16[2,80,1664]{2,1,0:T(8,128)(2,1)S(1)}, u32[]{:S(2)}, u32[]{:S(2)}) collective-permute-start(bf16[2,80,1664]{2,1,0:T(8,128)(2,1)S(1)} %pad_maximum_fusion.5), channel_id=1, source_target_pairs={{0,1},{1,0},{2,3},{3,2},{4,5},{5,4},{6,7},{7,6},{8,9},{9,8},{10,11... | collective-permute-start | bytes 1597448 | tf_op jit(solution)/shard_map/ppermute | solution.py:50
  42.3 8.6 %collective-permute-start.12 = (bf16[80,2048]{1,0:T(8,128)(2,1)S(1)}, bf16[80,2048]{1,0:T(8,128)(2,1)S(1)}, u32[]{:S(2)}, u32[]{:S(2)}) collective-permute-start(bf16[80,2048]{1,0:T(8,128)(2,1)S(1)} %pad_maximum_fusion.11), channel_id=1, source_target_pairs={{1,4},{3,6},{4,1},{6,3},{9,12},{11,14},{12,9},{14,11},{17,20},{19,... | collective-permute-start | bytes 983048 | tf_op jit(solution)/shard_map/ppermute | solution.py:127
  43.2 10.0 %collective-permute-start.11 = (bf16[80,2048]{1,0:T(8,128)(2,1)S(1)}, bf16[80,2048]{1,0:T(8,128)(2,1)S(1)}, u32[]{:S(2)}, u32[]{:S(2)}) collective-permute-start(bf16[80,2048]{1,0:T(8,128)(2,1)S(1)} %pad_maximum_fusion.11), channel_id=1, source_target_pairs={{0,4},{1,0},{2,6},{3,2},{4,5},{5,1},{6,7},{7,3},{8,12},{9,8},{10,1... | collective-permute-start | bytes 983048 | tf_op jit(solution)/shard_map/ppermute | solution.py:127
  47.5 1.6 %slice-start.7 = ((s8[14680064]{0:T(1024)(128)(4,1)}), s8[2097152]{0:T(1024)(128)(4,1)S(1)}, s32[]{:S(2)}) async-start(s8[14680064]{0:T(1024)(128)(4,1)} %bitcast.108), calls=%async_computation.7 | async-start | bytes 4194304
  50.9 4.0 %collective-permute-start.13 = (bf16[2,80,1920]{2,1,0:T(8,128)(2,1)S(1)}, bf16[2,80,1920]{2,1,0:T(8,128)(2,1)S(1)}, u32[]{:S(2)}, u32[]{:S(2)}) collective-permute-start(bf16[2,80,1920]{2,1,0:T(8,128)(2,1)S(1)} %pad_maximum_fusion.3), channel_id=1, source_target_pairs={{0,1},{1,0},{2,3},{3,2},{4,5},{5,4},{6,7},{7,6},{8,9},{9,8},{10,11... | collective-permute-start | bytes 1843208 | tf_op jit(solution)/shard_map/ppermute | solution.py:50
  53.4 2.5 %copy-start.2 = (bf16[160,2048]{1,0:T(8,128)(2,1)}, bf16[160,2048]{1,0:T(8,128)(2,1)S(1)}, u32[]{:S(2)}) copy-start(bf16[160,2048]{1,0:T(8,128)(2,1)S(1)} %pad_maximum_fusion.2) | copy-start | bytes 1966084
  53.4 9.2 %collective-permute-start.10 = (bf16[2,40,1664]{2,1,0:T(8,128)(2,1)}, bf16[2,40,1664]{2,1,0:T(8,128)(2,1)}, u32[]{:S(2)}, u32[]{:S(2)}) collective-permute-start(bf16[2,40,1664]{2,1,0:T(8,128)(2,1)} %pad_maximum_fusion.14), channel_id=1, source_target_pairs={{0,2},{1,3},{2,0},{3,1},{4,6},{5,7},{6,4},{7,5},{8,10},{9,11},{10,... | collective-permute-start | bytes 798728 | tf_op jit(solution)/shard_map/ppermute | solution.py:50
  60.5 6.9 %copy-start.4 = (bf16[2,40,1920]{2,1,0:T(8,128)(2,1)S(1)}, bf16[2,40,1920]{2,1,0:T(8,128)(2,1)}, u32[]{:S(2)}) copy-start(bf16[2,40,1920]{2,1,0:T(8,128)(2,1)} %pad_maximum_fusion.12) | copy-start | bytes 921604
  60.7 14.2 %collective-permute-start.17 = (bf16[2,80,2304]{2,1,0:T(8,128)(2,1)S(1)}, bf16[2,80,2304]{2,1,0:T(8,128)(2,1)S(1)}, u32[]{:S(2)}, u32[]{:S(2)}) collective-permute-start(bf16[2,80,2304]{2,1,0:T(8,128)(2,1)S(1)} %pad_maximum_fusion), channel_id=1, source_target_pairs={{0,1},{1,0},{2,3},{3,2},{4,5},{5,4},{6,7},{7,6},{8,9},{9,8},{10,11... | collective-permute-start | bytes 2211848 | tf_op jit(solution)/shard_map/ppermute | solution.py:50
  63.6 10.4 %collective-permute-start.14 = (bf16[40,1664]{1,0:T(8,128)(2,1)S(1)}, bf16[40,1664]{1,0:T(8,128)(2,1)S(1)}, u32[]{:S(2)}, u32[]{:S(2)}) collective-permute-start(bf16[40,1664]{1,0:T(8,128)(2,1)S(1)} %fusion.51), channel_id=1, source_target_pairs={{0,8},{4,12},{8,0},{12,4},{1,9},{5,13},{9,1},{13,5},{2,10},{6,14},... | collective-permute-start | bytes 399368 | tf_op jit(solution)/shard_map/ppermute | solution.py:50
  67.4 8.9 %collective-permute-start.16 = (bf16[2,40,1920]{2,1,0:T(8,128)(2,1)S(1)}, bf16[2,40,1920]{2,1,0:T(8,128)(2,1)S(1)}, u32[]{:S(2)}, u32[]{:S(2)}) collective-permute-start(bf16[2,40,1920]{2,1,0:T(8,128)(2,1)S(1)} %copy-done.4), channel_id=1, source_target_pairs={{0,2},{1,3},{2,0},{3,1},{4,6},{5,7},{6,4},{7,5},{8,10},{9,11},{10,... | collective-permute-start | bytes 921608 | tf_op jit(solution)/shard_map/ppermute | solution.py:50
  74.0 7.5 %collective-permute-start.15 = (bf16[40,1664]{1,0:T(8,128)(2,1)S(1)}, bf16[40,1664]{1,0:T(8,128)(2,1)S(1)}, u32[]{:S(2)}, u32[]{:S(2)}) collective-permute-start(bf16[40,1664]{1,0:T(8,128)(2,1)S(1)} %get-tuple-element.104), channel_id=1, source_target_pairs={{0,2},{1,3},{2,0},{3,1},{4,6},{5,7},{6,4},{7,5},{8,10},{9,11},{10,... | collective-permute-start | bytes 399368 | tf_op jit(solution)/shard_map/ppermute | solution.py:50
  75.0 4.3 %copy-start.3 = (bf16[160,2048]{1,0:T(8,128)(2,1)S(1)}, bf16[160,2048]{1,0:T(8,128)(2,1)}, u32[]{:S(2)}) copy-start(bf16[160,2048]{1,0:T(8,128)(2,1)} %copy-done.2) | copy-start | bytes 1966084
  76.5 9.0 %collective-permute-start.18 = (bf16[40,1920]{1,0:T(8,128)(2,1)S(1)}, bf16[40,1920]{1,0:T(8,128)(2,1)S(1)}, u32[]{:S(2)}, u32[]{:S(2)}) collective-permute-start(bf16[40,1920]{1,0:T(8,128)(2,1)S(1)} %fusion.47), channel_id=1, source_target_pairs={{0,8},{4,12},{8,0},{12,4},{1,9},{5,13},{9,1},{13,5},{2,10},{6,14},... | collective-permute-start | bytes 460808 | tf_op jit(solution)/shard_map/ppermute | solution.py:50
  77.5 9.7 %collective-permute-start.21 = (bf16[2,40,2304]{2,1,0:T(8,128)(2,1)S(1)}, bf16[2,40,2304]{2,1,0:T(8,128)(2,1)S(1)}, u32[]{:S(2)}, u32[]{:S(2)}) collective-permute-start(bf16[2,40,2304]{2,1,0:T(8,128)(2,1)S(1)} %pad_maximum_fusion.8), channel_id=1, source_target_pairs={{0,2},{1,3},{2,0},{3,1},{4,6},{5,7},{6,4},{7,5},{8,10},{9,11},{10,... | collective-permute-start | bytes 1105928 | tf_op jit(solution)/shard_map/ppermute | solution.py:50
  80.4 29.5 %slice-start.8 = ((s8[14680064]{0:T(1024)(128)(4,1)}), s8[2097152]{0:T(1024)(128)(4,1)S(1)}, s32[]{:S(2)}) async-start(s8[14680064]{0:T(1024)(128)(4,1)} %bitcast.117), calls=%async_computation.8 | async-start | bytes 4194304
  81.4 28.5 %slice-start.9 = ((s8[14680064]{0:T(1024)(128)(4,1)}), s8[4194304]{0:T(1024)(128)(4,1)S(1)}, s32[]{:S(2)}) async-start(s8[14680064]{0:T(1024)(128)(4,1)} %bitcast.117), calls=%async_computation.9 | async-start | bytes 8388608
  81.6 10.8 %collective-permute-start.23 = (bf16[80,1664]{1,0:T(8,128)(2,1)S(1)}, bf16[80,1664]{1,0:T(8,128)(2,1)S(1)}, u32[]{:S(2)}, u32[]{:S(2)}) collective-permute-start(bf16[80,1664]{1,0:T(8,128)(2,1)S(1)} %pad_maximum_fusion.15), channel_id=1, source_target_pairs={{1,4},{3,6},{4,1},{6,3},{9,12},{11,14},{12,9},{14,11},{17,20},{19,... | collective-permute-start | bytes 798728 | tf_op jit(solution)/shard_map/ppermute | solution.py:127
  82.4 12.9 %collective-permute-start.22 = (bf16[80,1664]{1,0:T(8,128)(2,1)S(1)}, bf16[80,1664]{1,0:T(8,128)(2,1)S(1)}, u32[]{:S(2)}, u32[]{:S(2)}) collective-permute-start(bf16[80,1664]{1,0:T(8,128)(2,1)S(1)} %pad_maximum_fusion.15), channel_id=1, source_target_pairs={{0,4},{1,0},{2,6},{3,2},{4,5},{5,1},{6,7},{7,3},{8,12},{9,8},{10,1... | collective-permute-start | bytes 798728 | tf_op jit(solution)/shard_map/ppermute | solution.py:127
  84.6 4.2 %collective-permute-start.20 = (bf16[2,80,1280]{2,1,0:T(8,128)(2,1)S(1)}, bf16[2,80,1280]{2,1,0:T(8,128)(2,1)S(1)}, u32[]{:S(2)}, u32[]{:S(2)}) collective-permute-start(bf16[2,80,1280]{2,1,0:T(8,128)(2,1)S(1)} %pad_maximum_fusion.7), channel_id=1, source_target_pairs={{0,1},{1,0},{2,3},{3,2},{4,5},{5,4},{6,7},{7,6},{8,9},{9,8},{10,11... | collective-permute-start | bytes 1228808 | tf_op jit(solution)/shard_map/ppermute | solution.py:50
  85.5 6.0 %collective-permute-start.19 = (bf16[40,1920]{1,0:T(8,128)(2,1)S(1)}, bf16[40,1920]{1,0:T(8,128)(2,1)S(1)}, u32[]{:S(2)}, u32[]{:S(2)}) collective-permute-start(bf16[40,1920]{1,0:T(8,128)(2,1)S(1)} %get-tuple-element.100), channel_id=1, source_target_pairs={{0,2},{1,3},{2,0},{3,1},{4,6},{5,7},{6,4},{7,5},{8,10},{9,11},{10,... | collective-permute-start | bytes 460808 | tf_op jit(solution)/shard_map/ppermute | solution.py:50
  87.4 10.6 %collective-permute-start.25 = (bf16[40,2304]{1,0:T(8,128)(2,1)S(1)}, bf16[40,2304]{1,0:T(8,128)(2,1)S(1)}, u32[]{:S(2)}, u32[]{:S(2)}) collective-permute-start(bf16[40,2304]{1,0:T(8,128)(2,1)S(1)} %fusion.43), channel_id=1, source_target_pairs={{0,8},{4,12},{8,0},{12,4},{1,9},{5,13},{9,1},{13,5},{2,10},{6,14},... | collective-permute-start | bytes 552968 | tf_op jit(solution)/shard_map/ppermute | solution.py:50
  88.9 10.7 %collective-permute-start.24 = (bf16[2,40,1280]{2,1,0:T(8,128)(2,1)S(1)}, bf16[2,40,1280]{2,1,0:T(8,128)(2,1)S(1)}, u32[]{:S(2)}, u32[]{:S(2)}) collective-permute-start(bf16[2,40,1280]{2,1,0:T(8,128)(2,1)S(1)} %pad_maximum_fusion.16), channel_id=1, source_target_pairs={{0,2},{1,3},{2,0},{3,1},{4,6},{5,7},{6,4},{7,5},{8,10},{9,11},{10,... | collective-permute-start | bytes 614408 | tf_op jit(solution)/shard_map/ppermute | solution.py:50
  91.5 18.4 %slice-start.10 = ((s8[14680064]{0:T(1024)(128)(4,1)}), s8[4194304]{0:T(1024)(128)(4,1)S(1)}, s32[]{:S(2)}) async-start(s8[14680064]{0:T(1024)(128)(4,1)} %bitcast.117), calls=%async_computation.10 | async-start | bytes 8388608
  91.6 12.7 %collective-permute-start.27 = (bf16[80,1920]{1,0:T(8,128)(2,1)S(1)}, bf16[80,1920]{1,0:T(8,128)(2,1)S(1)}, u32[]{:S(2)}, u32[]{:S(2)}) collective-permute-start(bf16[80,1920]{1,0:T(8,128)(2,1)S(1)} %pad_maximum_fusion.13), channel_id=1, source_target_pairs={{1,4},{3,6},{4,1},{6,3},{9,12},{11,14},{12,9},{14,11},{17,20},{19,... | collective-permute-start | bytes 921608 | tf_op jit(solution)/shard_map/ppermute | solution.py:127
  92.4 11.9 %collective-permute-start.26 = (bf16[80,1920]{1,0:T(8,128)(2,1)S(1)}, bf16[80,1920]{1,0:T(8,128)(2,1)S(1)}, u32[]{:S(2)}, u32[]{:S(2)}) collective-permute-start(bf16[80,1920]{1,0:T(8,128)(2,1)S(1)} %pad_maximum_fusion.13), channel_id=1, source_target_pairs={{0,4},{1,0},{2,6},{3,2},{4,5},{5,1},{6,7},{7,3},{8,12},{9,8},{10,1... | collective-permute-start | bytes 921608 | tf_op jit(solution)/shard_map/ppermute | solution.py:127
  98.0 6.4 %collective-permute-start.28 = (bf16[40,2304]{1,0:T(8,128)(2,1)S(1)}, bf16[40,2304]{1,0:T(8,128)(2,1)S(1)}, u32[]{:S(2)}, u32[]{:S(2)}) collective-permute-start(bf16[40,2304]{1,0:T(8,128)(2,1)S(1)} %get-tuple-element.84), channel_id=1, source_target_pairs={{0,2},{1,3},{2,0},{3,1},{4,6},{5,7},{6,4},{7,5},{8,10},{9,11},{10,... | collective-permute-start | bytes 552968 | tf_op jit(solution)/shard_map/ppermute | solution.py:50
  99.7 10.2 %slice-start.11 = ((s8[14680064]{0:T(1024)(128)(4,1)}), s8[4194304]{0:T(1024)(128)(4,1)S(1)}, s32[]{:S(2)}) async-start(s8[14680064]{0:T(1024)(128)(4,1)} %bitcast.117), calls=%async_computation.11 | async-start | bytes 8388608
  99.7 11.9 %collective-permute-start.30 = (bf16[40,1280]{1,0:T(8,128)(2,1)S(1)}, bf16[40,1280]{1,0:T(8,128)(2,1)S(1)}, u32[]{:S(2)}, u32[]{:S(2)}) collective-permute-start(bf16[40,1280]{1,0:T(8,128)(2,1)S(1)} %fusion.55), channel_id=1, source_target_pairs={{0,8},{4,12},{8,0},{12,4},{1,9},{5,13},{9,1},{13,5},{2,10},{6,14},... | collective-permute-start | bytes 307208 | tf_op jit(solution)/shard_map/ppermute | solution.py:50
  104.4 9.8 %collective-permute-start.33 = (bf16[80,2304]{1,0:T(8,128)(2,1)S(1)}, bf16[80,2304]{1,0:T(8,128)(2,1)S(1)}, u32[]{:S(2)}, u32[]{:S(2)}) collective-permute-start(bf16[80,2304]{1,0:T(8,128)(2,1)S(1)} %pad_maximum_fusion.9), channel_id=1, source_target_pairs={{1,4},{3,6},{4,1},{6,3},{9,12},{11,14},{12,9},{14,11},{17,20},{19,... | collective-permute-start | bytes 1105928 | tf_op jit(solution)/shard_map/ppermute | solution.py:127
  105.1 11.5 %collective-permute-start.32 = (bf16[80,2304]{1,0:T(8,128)(2,1)S(1)}, bf16[80,2304]{1,0:T(8,128)(2,1)S(1)}, u32[]{:S(2)}, u32[]{:S(2)}) collective-permute-start(bf16[80,2304]{1,0:T(8,128)(2,1)S(1)} %pad_maximum_fusion.9), channel_id=1, source_target_pairs={{0,4},{1,0},{2,6},{3,2},{4,5},{5,1},{6,7},{7,3},{8,12},{9,8},{10,1... | collective-permute-start | bytes 1105928 | tf_op jit(solution)/shard_map/ppermute | solution.py:127
  111.7 1.7 %collective-permute-start.29 = (bf16[80,2048]{1,0:T(8,128)(2,1)S(1)}, bf16[80,2048]{1,0:T(8,128)(2,1)S(1)}, u32[]{:S(2)}, u32[]{:S(2)}) collective-permute-start(bf16[80,2048]{1,0:T(8,128)(2,1)S(1)} %slice.508), channel_id=1, source_target_pairs={{0,1},{1,0},{2,3},{3,2},{4,5},{5,4},{6,7},{7,6},{8,9},{9,8},{10,11... | collective-permute-start | bytes 983048 | tf_op jit(solution)/shard_map/ppermute | solution.py:50
  111.8 6.8 %collective-permute-start.34 = (bf16[40,1280]{1,0:T(8,128)(2,1)S(1)}, bf16[40,1280]{1,0:T(8,128)(2,1)S(1)}, u32[]{:S(2)}, u32[]{:S(2)}) collective-permute-start(bf16[40,1280]{1,0:T(8,128)(2,1)S(1)} %get-tuple-element.108), channel_id=1, source_target_pairs={{0,2},{1,3},{2,0},{3,1},{4,6},{5,7},{6,4},{7,5},{8,10},{9,11},{10,... | collective-permute-start | bytes 307208 | tf_op jit(solution)/shard_map/ppermute | solution.py:50
  113.4 11.2 %collective-permute-start.31 = (bf16[80,2048]{1,0:T(8,128)(2,1)S(1)}, bf16[80,2048]{1,0:T(8,128)(2,1)S(1)}, u32[]{:S(2)}, u32[]{:S(2)}) collective-permute-start(bf16[80,2048]{1,0:T(8,128)(2,1)S(1)} %fusion.35), channel_id=1, source_target_pairs={{0,2},{1,3},{2,0},{3,1},{4,6},{5,7},{6,4},{7,5},{8,10},{9,11},{10,... | collective-permute-start | bytes 983048 | tf_op jit(solution)/shard_map/ppermute | solution.py:50
  118.6 6.2 %collective-permute-start.36 = (bf16[80,1280]{1,0:T(8,128)(2,1)S(1)}, bf16[80,1280]{1,0:T(8,128)(2,1)S(1)}, u32[]{:S(2)}, u32[]{:S(2)}) collective-permute-start(bf16[80,1280]{1,0:T(8,128)(2,1)S(1)} %pad_maximum_fusion.17), channel_id=1, source_target_pairs={{1,4},{3,6},{4,1},{6,3},{9,12},{11,14},{12,9},{14,11},{17,20},{19,... | collective-permute-start | bytes 614408 | tf_op jit(solution)/shard_map/ppermute | solution.py:127
  119.3 8.6 %collective-permute-start.35 = (bf16[80,1280]{1,0:T(8,128)(2,1)S(1)}, bf16[80,1280]{1,0:T(8,128)(2,1)S(1)}, u32[]{:S(2)}, u32[]{:S(2)}) collective-permute-start(bf16[80,1280]{1,0:T(8,128)(2,1)S(1)} %pad_maximum_fusion.17), channel_id=1, source_target_pairs={{0,4},{1,0},{2,6},{3,2},{4,5},{5,1},{6,7},{7,3},{8,12},{9,8},{10,1... | collective-permute-start | bytes 614408 | tf_op jit(solution)/shard_map/ppermute | solution.py:127
  129.7 3.6 %collective-permute-start.37 = (bf16[80,2048]{1,0:T(8,128)(2,1)}, bf16[80,2048]{1,0:T(8,128)(2,1)S(1)}, u32[]{:S(2)}, u32[]{:S(2)}) collective-permute-start(bf16[80,2048]{1,0:T(8,128)(2,1)} %slice.507), channel_id=1, source_target_pairs={{0,1},{1,0},{2,3},{3,2},{4,5},{5,4},{6,7},{7,6},{8,9},{9,8},{10,11... | collective-permute-start | bytes 983048 | tf_op jit(solution)/shard_map/ppermute | solution.py:50
  133.3 10.1 %collective-permute-start.38 = (bf16[80,2048]{1,0:T(8,128)(2,1)S(1)}, bf16[80,2048]{1,0:T(8,128)(2,1)S(1)}, u32[]{:S(2)}, u32[]{:S(2)}) collective-permute-start(bf16[80,2048]{1,0:T(8,128)(2,1)S(1)} %fusion.36), channel_id=1, source_target_pairs={{0,2},{1,3},{2,0},{3,1},{4,6},{5,7},{6,4},{7,5},{8,10},{9,11},{10,... | collective-permute-start | bytes 983048 | tf_op jit(solution)/shard_map/ppermute | solution.py:50
  134.9 9.6 %collective-permute-start.39 = (bf16[80,2048]{1,0:T(8,128)(2,1)S(1)}, bf16[80,2048]{1,0:T(8,128)(2,1)S(1)}, u32[]{:S(2)}, u32[]{:S(2)}) collective-permute-start(bf16[80,2048]{1,0:T(8,128)(2,1)S(1)} %get-tuple-element.67), channel_id=1, source_target_pairs={{0,1},{1,0},{2,3},{3,2},{4,5},{5,4},{6,7},{7,6},{8,9},{9,8},{10,11... | collective-permute-start | bytes 983048 | tf_op jit(solution)/shard_map/ppermute | solution.py:50
  143.6 1.7 %collective-permute-start.40 = (bf16[80,2048]{1,0:T(8,128)(2,1)S(1)}, bf16[80,2048]{1,0:T(8,128)(2,1)S(1)}, u32[]{:S(2)}, u32[]{:S(2)}) collective-permute-start(bf16[80,2048]{1,0:T(8,128)(2,1)S(1)} %get-tuple-element.69), channel_id=1, source_target_pairs={{0,1},{1,0},{2,3},{3,2},{4,5},{5,4},{6,7},{7,6},{8,9},{9,8},{10,11... | collective-permute-start | bytes 983048 | tf_op jit(solution)/shard_map/ppermute | solution.py:50
